TPU v7x, 128 devices: a whole 4x4x4 slice. The times are simulated.
128 devices in a mesh: rows: 32 (over y, z, core), probe: 4 (over x).
Axes of the slice: x: 4, y: 4, z: 4, core: 2. Of those that a mesh axis runs over, the one named last changes fastest.
Arguments:
- states: bfloat16 [32768, 256], P('rows'), may hold values from -1 to 1
- offsets: int32 [32], P('rows'), may hold values from 0 to 512, as said below
- right_side: float32 [16384, 64], P('rows', 'probe'), may hold values from -6 to 6
Outputs:
- solution_field: float32 [16384, 64], P('rows', 'probe')
- residual: float32 [16384, 64], P('rows', 'probe')
Inputs may be any that keep to these rules, and one draw needn't show every extreme that they name: `offsets`: each window of 512 states lies inside its block; some block starts at 0 and some at 512.
All inputs are finite; a program needn't handle non-finite values.
Results may differ from a plain program's by a relative error of at most 0.0056.
Values may be sent and summed in bfloat16 or wider, within the bound.
No kernel may reach another device: no remote copies, remote signals or barrier semaphores. Data moves between devices by JAX's collectives and lax.ppermute only.
A program may use at most 64 MiB of HBM per device.

v0:
```python
import math

import jax
import jax.numpy as jnp
from jax import lax
from jax.sharding import PartitionSpec as P

ITERS = 2


noise_level = 1.0
kernel_rate = 0.5


def squared_norms(features):
    return jnp.sum(features.astype(jnp.float32) ** 2, axis=1)


def kernel_product(own_points, own_norms, features, feature_norms, panel):
    count = features.shape[0]
    block_rows = math.gcd(count, 2048)
    block_count = count // block_rows
    feature_blocks = features.reshape(block_count, block_rows, features.shape[1])
    norm_blocks = feature_norms.reshape(block_count, block_rows)
    panel_blocks = panel.reshape(block_count, block_rows, panel.shape[1])

    def accumulate(total, inputs):
        block_features, block_norms, block_panel = inputs
        cross = lax.dot_general(
            own_points, block_features, (((1,), (1,)), ((), ())), preferred_element_type=jnp.float32
        )
        dist = own_norms[:, None] + block_norms[None, :] - 2.0 * cross
        kern = jnp.exp(-kernel_rate * dist).astype(jnp.bfloat16)
        return (total + jnp.dot(kern, block_panel, preferred_element_type=jnp.float32), None)

    start_total = jnp.zeros((own_points.shape[0], panel.shape[1]), jnp.float32)
    total, unused = lax.scan(accumulate, start_total, (feature_blocks, norm_blocks, panel_blocks))
    return total


def curvature_sum(direction, image):
    return lax.psum(jnp.sum(direction * image, axis=0), "rows")


def on_device(states, offsets, right_side):
    own_rows = right_side.shape[0]
    own_points = lax.dynamic_slice_in_dim(states, offsets[0], own_rows, 0)
    own_norms = squared_norms(own_points)
    gathered = lax.all_gather(own_points, "rows", axis=0, tiled=True)
    gathered_norms = squared_norms(gathered)
    solution_field = jnp.zeros_like(right_side)
    residual = right_side
    direction = right_side
    norm_now = lax.psum(jnp.sum(residual * residual, axis=0), "rows")
    for iteration in range(ITERS):
        image = kernel_product(
            own_points,
            own_norms,
            gathered,
            gathered_norms,
            lax.all_gather(direction.astype(jnp.bfloat16), "rows", axis=0, tiled=True),
        )
        image = image + noise_level * direction
        alpha = norm_now / curvature_sum(direction, image)
        solution_field = solution_field + alpha * direction
        residual = residual - alpha * image
        if iteration + 1 < ITERS:
            norm_next = lax.psum(jnp.sum(residual * residual, axis=0), "rows")
            direction = residual + norm_next / norm_now * direction
            norm_now = norm_next
    return (solution_field, residual)


def solution(mesh):
    in_specs = (P("rows", None), P("rows"), P("rows", "probe"))
    out_specs = (P("rows", "probe"), P("rows", "probe"))
    return jax.shard_map(
        on_device, mesh=mesh, in_specs=in_specs, out_specs=out_specs, check_vma=False
    )
```

profile of v0, /device:TPU:0, one launch (start us, length us, event | category | flops | bytes accessed | tf_op | source)
XLA Modules:
  0.0 338.1 jit_solution(6070814377201917271)
XLA Ops:
  7.9 1.8 multiply_reduce_fusion.1
  9.7 0.8 convert_element_type.20
  10.4 26.4 %all_gather.10 = bf16[16384,16]{0,1:T(8,128)(2,1)S(1)} all-gather(bf16[512,16]{0,1:T(8,128)(2,1)S(1)} %convert_element_type.20), channel_id=1, replica_groups=mesh['rows'=32,'probe'=4] {'rows'}, dimensions={0}, use_global_device_ids=true | all-gather | bytes 540672 | tf_op jit(solution)/shard_map/all_gather | solution.py:61
  36.9 29.0 %all-gather.2.cloned.1.call-done = bf16[16384,256]{1,0:T(8,128)(2,1)} async-done(((bf16[512,256]{1,0:T(8,128)(2,1)}), bf16[16384,256]{1,0:T(8,128)(2,1)}) %all-gather.2.cloned.1.call-update) | async-done | bytes 8388624 | tf_op jit(solution)/shard_map/all_gather | solution.py:49
  65.9 5.2 %multiply_reduce_fusion = f32[16384]{0:T(1024)S(1)} fusion(bf16[16384,256]{1,0:T(8,128)(2,1)} %all-gather.2.cloned.1.call-done), kind=kLoop, calls=%fused_computation.28 | loop fusion | flops 12566528 | bytes 8454144 | tf_op jit(solution)/shard_map/reduce_sum | solution.py:16
  71.2 21.7 %while.22 = (s32[]{:T(128)}, f32[512,16]{0,1:T(8,128)S(1)}, f32[512]{0:T(512)S(1)}, f32[8,2048]{1,0:T(8,128)S(1)}, bf16[8,2048,256]{2,1,0:T(8,128)(2,1)}, /*inde...) while((s32[]{:T(128)}, f32[512,16]{0,1:T(8,128)S(1)}, ...), condition=%wide.region_5.6_spmd.clone, body=%wide.region_4.5_spmd.clone.sunk | while | flops 575684608 | bytes 1469547 | solution.py:37
  71.2 2.7 fusion.44
  73.9 2.7 fusion.44
  76.7 2.7 fusion.44
  79.4 2.7 fusion.44
  82.1 2.7 fusion.44
  84.8 2.7 fusion.44
  87.5 2.7 fusion.44
  90.2 2.7 fusion.44
  92.9 0.1 multiply_reduce_fusion.4
  93.0 65.5 %all-reduce = (f32[16]{0:T(128)S(1)}, f32[16]{0:T(128)S(1)}) all-reduce(f32[16]{0:T(128)S(1)} %get-tuple-element.148, f32[16]{0:T(128)S(1)} %get-tuple-element.147), channel_id=1, replica_groups=mesh['rows'=32,'probe'=4] {'rows'}, use_global_device_ids=true, to_apply=%region_1.0 | all-reduce | flops 32 | bytes 256 | tf_op jit(solution)/shard_map/psum | solution.py:54
  158.5 0.2 multiply_reduce_fusion.3
  158.7 62.7 %psum.30 = f32[16]{0:T(128)S(1)} all-reduce(f32[16]{0:T(128)S(1)} %multiply_reduce_fusion.3), channel_id=1, replica_groups=mesh['rows'=32,'probe'=4] {'rows'}, use_global_device_ids=true, to_apply=%region_9.10 | all-reduce | flops 16 | bytes 128 | tf_op jit(solution)/shard_map/psum | solution.py:68
  221.4 0.1 fusion.30
  221.5 21.8 %all_gather.11 = bf16[16384,16]{0,1:T(8,128)(2,1)S(1)} all-gather(bf16[512,16]{0,1:T(8,128)(2,1)S(1)} %get-tuple-element.181), channel_id=1, replica_groups=mesh['rows'=32,'probe'=4] {'rows'}, dimensions={0}, use_global_device_ids=true | all-gather | bytes 540672 | tf_op jit(solution)/shard_map/all_gather | solution.py:61
  243.3 21.7 %while.23 = (s32[]{:T(128)}, f32[512,16]{0,1:T(8,128)S(1)}, f32[512]{0:T(512)S(1)}, f32[8,2048]{1,0:T(8,128)S(1)}, bf16[8,2048,256]{2,1,0:T(8,128)(2,1)}, /*inde...) while((s32[]{:T(128)}, f32[512,16]{0,1:T(8,128)S(1)}, ...), condition=%wide.region_11.12_spmd.clone, body=%wide.region_10.11_spmd.clone.sunk | while | flops 575684608 | bytes 1469547 | solution.py:37
  243.4 2.7 fusion.48
  246.1 2.7 fusion.48
  248.8 2.7 fusion.48
  251.5 2.7 fusion.48
  254.2 2.7 fusion.48
  257.0 2.7 fusion.48
  259.7 2.7 fusion.48
  262.4 2.7 fusion.48
  265.1 0.1 multiply_reduce_fusion.2
  265.2 65.3 %psum.31 = f32[16]{0:T(128)S(1)} all-reduce(f32[16]{0:T(128)S(1)} %get-tuple-element.179), channel_id=1, replica_groups=mesh['rows'=32,'probe'=4] {'rows'}, use_global_device_ids=true, to_apply=%region_13.14 | all-reduce | flops 16 | bytes 128 | tf_op jit(solution)/shard_map/psum | solution.py:42
  330.5 0.7 multiply_subtract_fusion
  (30 shorter events, 0.6 us)
Async XLA Ops:
  7.2 58.8 %all-gather.2.cloned.1.call-start = ((), (), s32[]{:S(2)}) async-start(), calls=%async_computation | async-start | bytes 8650752 | tf_op jit(solution)/shard_map/all_gather | solution.py:49
  36.9 34.3 %copy-start = (bf16[512,256]{1,0:T(8,128)(2,1)S(1)}, bf16[512,256]{1,0:T(8,128)(2,1)}, u32[]{:S(2)}) copy-start(bf16[512,256]{1,0:T(8,128)(2,1)} %get-tuple-element.306) | copy-start | bytes 786436
  71.2 21.7 %copy-start.1 = (f32[512,16]{0,1:T(8,128)S(1)}, f32[512,16]{0,1:T(8,128)}, u32[]{:S(2)}) copy-start(f32[512,16]{0,1:T(8,128)} %param.9) | copy-start | bytes 98308
Sparse Core Ops, SparseCore 0:
  10.3 55.6 all-gather.1
where the time goes:
time: 339 us; the launch traced here: 338 us
  blocking collectives  242 us (71%)
  matrix products  42.8 us (13%)
  waiting for transfers between devices  29.1 us (9%)
  between operations  14.8 us (4%)
  other arithmetic  9.01 us (3%)
    psum x1, blocking collectives, on_device(): norm_now = lax.psum(jnp.sum(residual * residual, axis=0), 'rows')  65.5 us
    psum x1, blocking collectives, curvature_sum(): return lax.psum(jnp.sum(direction * image, axis=0), 'rows')  65.3 us
    psum x1, blocking collectives, on_device(): norm_next = lax.psum(jnp.sum(residual * residual, axis=0), 'rows')  62.7 us
    all_gather x2, blocking collectives, on_device(): lax.all_gather(direction.astype(jnp.bfloat16), 'rows', axis=0, tiled=True)  48.2 us
    dot_general x16, matrix products, accumulate(): jnp.dot(kern, block_panel, preferred_element_type=jnp.float32)  42.8 us
    all_gather x1, waiting for transfers between devices, on_device(): gathered = lax.all_gather(own_points, 'rows', axis=0, tiled=True)  29 us
    reduce_sum x2, other arithmetic, squared_norms(): return jnp.sum(features.astype(jnp.float32) ** 2, axis=1)  6.97 us
  transfers between devices with their start and end apart: 1, of which 1 were waited for; matrix products, arithmetic and copies ran while one was open for 0% of the time, Pallas kernels for 0%

commit v1 on v0

v1 whole, which is shorter than its diff:
```python
import functools

import jax
import jax.numpy as jnp
from jax import lax
from jax.experimental import pallas as pl
from jax.experimental.pallas import tpu as pltpu
from jax.sharding import Mesh
from jax.sharding import PartitionSpec as P

NY, NZ, NC, NX = 4, 4, 2, 4
LANES = 128

noise_level = 1.0
kernel_rate = 0.5


def shift(value, axis, size, step):
    return lax.ppermute(value, axis, [(i, (i + step) % size) for i in range(size)])


def others(value, axis, size):
    return [shift(value, axis, size, k) for k in range(1, size)]


def prepare_kernel(points_ref, side_ref, out_ref):
    probes = side_ref.shape[1]
    out_ref[:probes, :] = side_ref[...].T
    squares = points_ref[...].astype(jnp.float32) ** 2
    norms = jnp.sum(squares, axis=1, keepdims=True)
    out_ref[probes:, :] = jnp.broadcast_to(norms, (norms.shape[0], 8)).T


def prepare(points, side):
    rows, probes = side.shape
    return pl.pallas_call(
        prepare_kernel,
        out_shape=jax.ShapeDtypeStruct((probes + 8, rows), jnp.float32),
        name="prepare",
    )(points, side)


def tile_kernel(probes, chunk, row_ref, col_ref, field_ref, tile_ref, image_ref, half_ref):
    @pl.when(pl.program_id(0) == 0)
    def _():
        image_ref[...] = jnp.zeros_like(image_ref)
        squares = row_ref[...].astype(jnp.float32) ** 2
        half_ref[...] = -kernel_rate * jnp.sum(squares, axis=1, keepdims=True)

    field = field_ref[:probes, :].astype(jnp.bfloat16)
    col_half = -kernel_rate * field_ref[probes : probes + 1, :]
    for i in range(row_ref.shape[0] // chunk):
        rows = pl.ds(i * chunk, chunk)
        cross = lax.dot_general(
            row_ref[rows, :], col_ref[...], (((1,), (1,)), ((), ())), preferred_element_type=jnp.float32
        )
        kern = jnp.exp(2.0 * kernel_rate * cross + half_ref[rows, :] + col_half).astype(jnp.bfloat16)
        tile_ref[rows, :] = kern
        image_ref[:, rows] += lax.dot_general(
            field, kern, (((1,), (1,)), ((), ())), preferred_element_type=jnp.float32
        )


def build_tile(row_points, col_points, col_field, probes):
    rows, features = row_points.shape
    cols = col_points.shape[0]
    chunk, block = 256, 512
    height = col_field.shape[0]
    return pl.pallas_call(
        functools.partial(tile_kernel, probes, chunk),
        grid=(cols // block,),
        in_specs=[
            pl.BlockSpec((rows, features), lambda j: (0, 0)),
            pl.BlockSpec((block, features), lambda j: (j, 0)),
            pl.BlockSpec((height, block), lambda j: (0, j)),
        ],
        out_specs=[
            pl.BlockSpec((rows, block), lambda j: (0, j)),
            pl.BlockSpec((probes, rows), lambda j: (0, 0)),
        ],
        out_shape=[
            jax.ShapeDtypeStruct((rows, cols), jnp.bfloat16),
            jax.ShapeDtypeStruct((probes, rows), jnp.float32),
        ],
        scratch_shapes=[pltpu.VMEM((rows, 1), jnp.float32)],
        compiler_params=pltpu.CompilerParams(vmem_limit_bytes=24 << 20),
        cost_estimate=pl.CostEstimate(
            flops=2 * rows * cols * (features + 256), bytes_accessed=24 << 20, transcendentals=rows * cols
        ),
        name="build_tile",
    )(row_points, col_points, col_field)


def second_kernel(own, tile_ref, side_r, image_r, side_c, image_c, sums_ref, part_ref, own_ref, out_sums):
    sums = sums_ref[...]
    rr, curve, square = sums[:, 0:1], sums[:, 1:2], sums[:, 2:3]
    alpha = rr / curve
    rr_next = rr - 2.0 * alpha * curve + alpha * alpha * square
    beta = rr_next / rr
    res_r = side_r[...] - alpha * image_r[...]
    dir_r = res_r + beta * side_r[...]
    narrow = dir_r.astype(jnp.bfloat16)
    total = jnp.zeros_like(alpha)
    block = 1024
    for j in range(tile_ref.shape[1] // block):
        cols = pl.ds(j * block, block)
        part = jnp.dot(narrow, tile_ref[:, cols], preferred_element_type=jnp.float32)
        part_ref[:, cols] = part
        res_c = side_c[:, cols] - alpha * image_c[:, cols]
        dir_c = res_c + beta * side_c[:, cols]
        total = total + jnp.sum(part * dir_c, axis=1, keepdims=True)
    own_res, own_dir = res_r[:, :own], dir_r[:, :own]
    own_ref[0] = own_res
    own_ref[1] = own_dir
    own_ref[2] = alpha * side_r[:, :own]
    total = total + noise_level * jnp.sum(own_dir * own_dir, axis=1, keepdims=True)
    rr_own = jnp.sum(own_res * own_res, axis=1, keepdims=True)
    lane = lax.broadcasted_iota(jnp.int32, out_sums.shape, 1)
    out_sums[...] = jnp.where(lane == 0, total, jnp.where(lane == 1, rr_own, 0.0))


def second_product(tile, side_r, image_r, side_c, image_c, sums, own):
    rows, cols = tile.shape
    probes = side_r.shape[0]
    return pl.pallas_call(
        functools.partial(second_kernel, own),
        out_shape=[
            jax.ShapeDtypeStruct((probes, cols), jnp.float32),
            jax.ShapeDtypeStruct((3, probes, own), jnp.float32),
            jax.ShapeDtypeStruct((probes, LANES), jnp.float32),
        ],
        compiler_params=pltpu.CompilerParams(vmem_limit_bytes=24 << 20),
        cost_estimate=pl.CostEstimate(flops=2 * rows * cols * 256, bytes_accessed=20 << 20, transcendentals=0),
        name="second_product",
    )(tile, side_r, image_r, side_c, image_c, sums)


def on_device(states, offsets, right_side):
    own, probes = right_side.shape
    points = lax.dynamic_slice_in_dim(states, offsets[0], own, 0)
    with jax.named_scope("fetch_points"):
        row_points = jnp.concatenate([points] + others(points, "z", NZ), axis=0)
        col_points = jnp.concatenate([points] + others(points, "y", NY), axis=0)
        packed = prepare(points, right_side)
        side = packed[:probes]
        side_r = jnp.concatenate([side] + others(side, "z", NZ), axis=1)
        packed_c = jnp.concatenate([packed] + others(packed, "y", NY), axis=1)
        col_points = jnp.concatenate([col_points, shift(col_points, "c", NC, 1)], axis=0)
        packed_c = jnp.concatenate([packed_c, shift(packed_c, "c", NC, 1)], axis=1)
        side_c = packed_c[:probes]

    tile, part = build_tile(row_points, col_points, packed_c, probes)

    with jax.named_scope("sum_over_z"):
        image_r = part + noise_level * side_r
        for s, other in enumerate(others(part, "z", NZ), 1):
            image_r = image_r + jnp.concatenate([other[:, (NZ - s) * own :], other[:, : (NZ - s) * own]], axis=1)
        sums = jnp.stack(
            [jnp.sum(side_r * side_r, axis=1), jnp.sum(side_r * image_r, axis=1), jnp.sum(image_r * image_r, axis=1)],
            axis=1,
        )
        sums = jnp.pad(sums, ((0, 0), (0, LANES - 3)))

    with jax.named_scope("gather_image"):
        message = jnp.concatenate([image_r[:, :own], sums], axis=1)
        pair = jnp.stack([message, shift(message, "c", NC, 1)])
        every = jnp.stack([pair] + others(pair, "y", NY), axis=1)
        image_c = every[:, :, :, :own].transpose(2, 0, 1, 3).reshape(probes, -1)
        sums = jnp.sum(every[:, :, :, own:], axis=(0, 1))

    part, held, sums = second_product(tile, side_r, image_r, side_c, image_c, sums, own)

    with jax.named_scope("sum_over_yc"):
        half = NY * own
        message = jnp.concatenate([part[:, half:], sums], axis=1)
        message = shift(message, "c", NC, 1)
        mine = part[:, :half] + message[:, :half]
        sums = sums + message[:, half:]
        image = mine[:, :own]
        total = sums
        for m in range(1, NY):
            message = jnp.concatenate([mine[:, m * own : (m + 1) * own], sums], axis=1)
            message = shift(message, "y", NY, -m)
            image = image + message[:, :own]
            total = total + message[:, own:]

    with jax.named_scope("sum_sums_over_z"):
        for other in others(total, "z", NZ):
            total = total + other

    alpha = total[:, 1:2] / total[:, 0:1]
    residual, direction, field = held[0], held[1], held[2]
    image = image + noise_level * direction
    field = field + alpha * direction
    residual = residual - alpha * image
    return field.T, residual.T


def solution(mesh):
    fine = Mesh(mesh.devices.reshape(NY, NZ, NC, NX), ("y", "z", "c", "x"))
    rows = ("y", "z", "c")
    in_specs = (P(rows, None), P(rows), P(rows, "x"))
    out_specs = (P(rows, "x"), P(rows, "x"))
    return jax.shard_map(on_device, mesh=fine, in_specs=in_specs, out_specs=out_specs, check_vma=False)
```

time: 339 us -> 103 us (0.30)
  blocking collectives: 242 us -> 0 us
  starting transfers between devices: 0.04 us -> 43.3 us
  matrix products: 42.8 us -> 0 us
  Pallas kernels: 0 us -> 16.4 us
  local copies, waits for them, and re-layouts: 0.54 us -> 15.7 us
  between operations: 14.8 us -> 1.6 us
  other arithmetic: 9.01 us -> 2.53 us
  waiting for transfers between devices: 29.1 us -> 23.5 us
    psum x3 -> x0, blocking collectives: 193 us -> none  [the longest x1 65.5 us: on_device(): norm_now = lax.psum(jnp.sum(residual * residual, axis=0), 'rows')]
    all_gather x2 -> x0, blocking collectives: 48.2 us -> none  [on_device(): lax.all_gather(direction.astype(jnp.bfloat16), 'rows', axis=0, tiled=True)]
    ppermute x0 -> x28, starting transfers between devices: none -> 43.3 us  [shift(): lax.ppermute(value, axis, [(i, (i + step) % size) for i in range(size)])]
    dot_general x16 -> x0, matrix products: 42.8 us -> none  [accumulate(): jnp.dot(kern, block_panel, preferred_element_type=jnp.float32)]
    all_gather x1 -> x0, waiting for transfers between devices: 29 us -> none  [on_device(): gathered = lax.all_gather(own_points, 'rows', axis=0, tiled=True)]
    ppermute x0 -> x28, waiting for transfers between devices: none -> 23.5 us  [shift(): lax.ppermute(value, axis, [(i, (i + step) % size) for i in range(size)])]
    pallas_call x0 -> x3, Pallas kernels: none -> 16.4 us  [the longest x1 12 us: build_tile(): pl.pallas_call(functools.partial(tile_kernel, probes, chunk), grid=(cols...]
    unnamed x4 -> x17, local copies, waits for them, and re-layouts: 0.01 us -> 15.1 us
  transfers between devices with their start and end apart: 1 -> 28, of which waited for: 1 -> 16; matrix products, arithmetic and copies ran while one was open for 0% -> 4% of each run, Pallas kernels for 0% -> 2%
where the time goes in v1:
time: 103 us
  starting transfers between devices  43.3 us (42%)
  waiting for transfers between devices  23.5 us (23%)
  Pallas kernels  16.4 us (16%)
  local copies, waits for them, and re-layouts  15.7 us (15%)
  other arithmetic  2.53 us (2%)
  between operations  1.6 us (2%)
    ppermute x28, starting transfers between devices, shift(): lax.ppermute(value, axis, [(i, (i + step) % size) for i in range(size)])  43.3 us
    ppermute x28, waiting for transfers between devices, shift(): lax.ppermute(value, axis, [(i, (i + step) % size) for i in range(size)])  23.5 us
    unnamed x17, local copies, waits for them, and re-layouts  15.1 us
    pallas_call x1, Pallas kernels, build_tile(): pl.pallas_call(functools.partial(tile_kernel, probes, chunk), grid=(cols...  12 us
    pallas_call x1, Pallas kernels, second_product(): pl.pallas_call(functools.partial(second_kernel, own), out_shape=[jax.Shap...  2.48 us
  transfers between devices with their start and end apart: 28, of which 16 were waited for; matrix products, arithmetic and copies ran while one was open for 4% of the time, Pallas kernels for 2%

profile of v1, /device:TPU:0, one launch (start us, length us, event | category | flops | bytes accessed | tf_op | source)
XLA Modules:
  0.0 103.0 jit_solution(16922818070139638379)
XLA Ops:
  2.3 1.7 %collective-permute-start.3 = (bf16[512,256]{1,0:T(8,128)(2,1)S(1)}, bf16[512,256]{1,0:T(8,128)(2,1)S(1)}, u32[]{:S(2)}, u32[]{:S(2)}) collective-permute-start(bf16[512,256]{1,0:T(8,128)(2,1)S(1)} %get-tuple-element.17.points_ref), channel_id=1, source_target_pairs={{0,32},{32,64},{64,96},{96,0},{1,33},{33,65},{65,97},{97,1},{2,34}... | collective-permute-start | bytes 786440 | tf_op jit(solution)/shard_map/fetch_points/ppermute | solution.py:19
  4.0 2.9 %collective-permute-start.4 = (bf16[512,256]{1,0:T(8,128)(2,1)S(1)}, bf16[512,256]{1,0:T(8,128)(2,1)S(1)}, u32[]{:S(2)}, u32[]{:S(2)}) collective-permute-start(bf16[512,256]{1,0:T(8,128)(2,1)S(1)} %get-tuple-element.17.points_ref), channel_id=1, source_target_pairs={{0,64},{32,96},{64,0},{96,32},{1,65},{33,97},{65,1},{97,33},{2,66}... | collective-permute-start | bytes 786440 | tf_op jit(solution)/shard_map/fetch_points/ppermute | solution.py:19
  6.9 1.3 %collective-permute-start.5 = (bf16[512,256]{1,0:T(8,128)(2,1)S(1)}, bf16[512,256]{1,0:T(8,128)(2,1)S(1)}, u32[]{:S(2)}, u32[]{:S(2)}) collective-permute-start(bf16[512,256]{1,0:T(8,128)(2,1)S(1)} %get-tuple-element.17.points_ref), channel_id=1, source_target_pairs={{0,96},{32,0},{64,32},{96,64},{1,97},{33,1},{65,33},{97,65},{2,98}... | collective-permute-start | bytes 786440 | tf_op jit(solution)/shard_map/fetch_points/ppermute | solution.py:19
  8.3 1.9 %collective-permute-start = (bf16[512,256]{1,0:T(8,128)(2,1)S(1)}, bf16[512,256]{1,0:T(8,128)(2,1)}, u32[]{:S(2)}, u32[]{:S(2)}) collective-permute-start(bf16[512,256]{1,0:T(8,128)(2,1)S(1)} %get-tuple-element.17.points_ref), channel_id=1, source_target_pairs={{0,8},{8,16},{16,24},{24,0},{1,9},{9,17},{17,25},{25,1},{2,10},{10... | collective-permute-start | bytes 786440 | tf_op jit(solution)/shard_map/fetch_points/ppermute | solution.py:19
  10.2 3.6 %collective-permute-start.1 = (bf16[512,256]{1,0:T(8,128)(2,1)S(1)}, bf16[512,256]{1,0:T(8,128)(2,1)}, u32[]{:S(2)}, u32[]{:S(2)}) collective-permute-start(bf16[512,256]{1,0:T(8,128)(2,1)S(1)} %get-tuple-element.17.points_ref), channel_id=1, source_target_pairs={{0,16},{8,24},{16,0},{24,8},{1,17},{9,25},{17,1},{25,9},{2,18},{10... | collective-permute-start | bytes 786440 | tf_op jit(solution)/shard_map/fetch_points/ppermute | solution.py:19
  13.8 2.0 %collective-permute-start.2 = (bf16[512,256]{1,0:T(8,128)(2,1)S(1)}, bf16[512,256]{1,0:T(8,128)(2,1)}, u32[]{:S(2)}, u32[]{:S(2)}) collective-permute-start(bf16[512,256]{1,0:T(8,128)(2,1)S(1)} %get-tuple-element.17.points_ref), channel_id=1, source_target_pairs={{0,24},{8,0},{16,8},{24,16},{1,25},{9,1},{17,9},{25,17},{2,26},{10... | collective-permute-start | bytes 786440 | tf_op jit(solution)/shard_map/fetch_points/ppermute | solution.py:19
  15.8 1.6 %copy.15.side_ref = f32[512,16]{1,0:T(8,128)} copy(f32[512,16]{0,1:T(8,128)} %param.5) | data formatting | bytes 65536 | tf_op args[2]
  17.4 1.9 %prepare.1 = f32[24,512]{1,0:T(8,128)} custom-call(bf16[512,256]{1,0:T(8,128)(2,1)} %copy-done.2, f32[512,16]{1,0:T(8,128)} %copy.15.side_ref), custom_call_target="tpu_custom_call" | custom-call | tf_op jit(solution)/shard_map/fetch_points/prepare/pallas_call | solution.py:36
  20.2 1.4 %collective-permute-start.7 = (f32[24,512]{1,0:T(8,128)}, f32[24,512]{1,0:T(8,128)S(1)}, u32[]{:S(2)}, u32[]{:S(2)}) collective-permute-start(f32[24,512]{1,0:T(8,128)} %prepare.1), channel_id=1, source_target_pairs={{0,32},{32,64},{64,96},{96,0},{1,33},{33,65},{65,97},{97,1},{2,34}... | collective-permute-start | bytes 147464 | tf_op jit(solution)/shard_map/fetch_points/ppermute | solution.py:19
  21.7 6.2 %collective-permute-start.8 = (f32[24,512]{1,0:T(8,128)}, f32[24,512]{1,0:T(8,128)S(1)}, u32[]{:S(2)}, u32[]{:S(2)}) collective-permute-start(f32[24,512]{1,0:T(8,128)} %prepare.1), channel_id=1, source_target_pairs={{0,64},{32,96},{64,0},{96,32},{1,65},{33,97},{65,1},{97,33},{2,66}... | collective-permute-start | bytes 147464 | tf_op jit(solution)/shard_map/fetch_points/ppermute | solution.py:19
  27.9 2.5 %collective-permute-start.9 = (f32[24,512]{1,0:T(8,128)}, f32[24,512]{1,0:T(8,128)S(1)}, u32[]{:S(2)}, u32[]{:S(2)}) collective-permute-start(f32[24,512]{1,0:T(8,128)} %prepare.1), channel_id=1, source_target_pairs={{0,96},{32,0},{64,32},{96,64},{1,97},{33,1},{65,33},{97,65},{2,98}... | collective-permute-start | bytes 147464 | tf_op jit(solution)/shard_map/fetch_points/ppermute | solution.py:19
  30.4 1.3 %fusion.3 = (bf16[2048,256]{1,0:T(8,128)(2,1)S(1)}, bf16[2048,256]{1,0:T(8,128)(2,1)S(1)}) fusion(bf16[512,256]{1,0:T(8,128)(2,1)} %copy-done.2, bf16[512,256]{1,0:T(8,128)(2,1)S(1)} %collective-permute-done.5, bf16[512,256]{1,0:T(8,128)(2,1)S(1)} %collective-permute-done.4, bf16[512,256]{1,0:T(8,128)(2,1)S(1)} %collective-permute-done.3, ...), kind=kLoop, calls=%fused_computation.5 | loop fusion | flops 7864320 | bytes 3932160 | tf_op jit(solution)/shard_map/fetch_points/concatenate | solution.py:143
  32.6 2.1 %collective-permute-done.10 = f32[24,2048]{1,0:T(8,128)S(1)} collective-permute-done((f32[24,2048]{1,0:T(8,128)S(1)}, f32[24,2048]{1,0:T(8,128)S(1)}, u32[]{:S(2)}, u32[]{:S(2)}) %collective-permute-start.10) | collective-permute-done | bytes 196640 | tf_op jit(solution)/shard_map/fetch_points/ppermute | solution.py:19
  34.9 12.0 %build_tile.1 = (bf16[2048,4096]{1,0:T(8,128)(2,1)S(1)}, f32[16,2048]{1,0:T(8,128)S(1)}) custom-call(bf16[2048,256]{1,0:T(8,128)(2,1)S(1)} %get-tuple-element.19.row_ref, bf16[4096,256]{1,0:T(8,128)(2,1)S(1)} %constant_dynamic-update-slice_fusion.col_ref, f32[24,4096]{1,0:T(8,128)S(1)} %constant_dynamic-update-slice_fusion.5.field_ref), custom_call_target="tpu_custom_call" | custom-call | flops 8589934592 | bytes 25165824 | tf_op jit(solution)/shard_map/build_tile/pallas_call | solution.py:69
  47.0 5.7 %copy-done = bf16[2048,4096]{1,0:T(8,128)(2,1)} copy-done((bf16[2048,4096]{1,0:T(8,128)(2,1)}, bf16[2048,4096]{1,0:T(8,128)(2,1)S(1)}, u32[]{:S(2)}) %copy-start) | copy-done | bytes 16777240
  52.7 1.3 %collective-permute-start.11 = (f32[16,512]{1,0:T(8,128)S(1)}, f32[16,512]{1,0:T(8,128)S(1)}, u32[]{:S(2)}, u32[]{:S(2)}) collective-permute-start(f32[16,512]{1,0:T(8,128)S(1)} %slice.120), channel_id=1, source_target_pairs={{0,8},{8,16},{16,24},{24,0},{1,9},{9,17},{17,25},{25,1},{2,10},{10... | collective-permute-start | bytes 98312 | tf_op jit(solution)/shard_map/fetch_points/ppermute | solution.py:19
  54.0 2.3 %collective-permute-start.12 = (f32[16,512]{1,0:T(8,128)S(1)}, f32[16,512]{1,0:T(8,128)S(1)}, u32[]{:S(2)}, u32[]{:S(2)}) collective-permute-start(f32[16,512]{1,0:T(8,128)S(1)} %slice.120), channel_id=1, source_target_pairs={{0,16},{8,24},{16,0},{24,8},{1,17},{9,25},{17,1},{25,9},{2,18},{10... | collective-permute-start | bytes 98312 | tf_op jit(solution)/shard_map/fetch_points/ppermute | solution.py:19
  56.2 2.6 %collective-permute-start.13 = (f32[16,512]{1,0:T(8,128)S(1)}, f32[16,512]{1,0:T(8,128)S(1)}, u32[]{:S(2)}, u32[]{:S(2)}) collective-permute-start(f32[16,512]{1,0:T(8,128)S(1)} %slice.120), channel_id=1, source_target_pairs={{0,24},{8,0},{16,8},{24,16},{1,25},{9,1},{17,9},{25,17},{2,26},{10... | collective-permute-start | bytes 98312 | tf_op jit(solution)/shard_map/fetch_points/ppermute | solution.py:19
  58.9 1.7 %collective-permute-done.15 = f32[16,2048]{1,0:T(8,128)S(1)} collective-permute-done((f32[16,2048]{1,0:T(8,128)S(1)}, f32[16,2048]{1,0:T(8,128)S(1)}, u32[]{:S(2)}, u32[]{:S(2)}) %collective-permute-start.15) | collective-permute-done | bytes 131104 | tf_op jit(solution)/shard_map/sum_over_z/ppermute | solution.py:19
  60.6 1.5 %collective-permute-start.16 = (f32[16,2048]{1,0:T(8,128)S(1)}, f32[16,2048]{1,0:T(8,128)S(1)}, u32[]{:S(2)}, u32[]{:S(2)}) collective-permute-start(f32[16,2048]{1,0:T(8,128)S(1)} %get-tuple-element.8), channel_id=1, source_target_pairs={{0,24},{8,0},{16,8},{24,16},{1,25},{9,1},{17,9},{25,17},{2,26},{10... | collective-permute-start | bytes 393224 | tf_op jit(solution)/shard_map/sum_over_z/ppermute | solution.py:19
  62.1 2.9 %collective-permute-done.14 = f32[16,2048]{1,0:T(8,128)S(1)} collective-permute-done((f32[16,2048]{1,0:T(8,128)S(1)}, f32[16,2048]{1,0:T(8,128)S(1)}, u32[]{:S(2)}, u32[]{:S(2)}) %collective-permute-start.14) | collective-permute-done | bytes 131104 | tf_op jit(solution)/shard_map/sum_over_z/ppermute | solution.py:19
  67.6 3.8 %collective-permute-start.19 = (f32[2,16,640]{2,1,0:T(8,128)S(1)}, f32[2,16,640]{2,1,0:T(8,128)S(1)}, u32[]{:S(2)}, u32[]{:S(2)}) collective-permute-start(f32[2,16,640]{2,1,0:T(8,128)S(1)} %get-tuple-element.29), channel_id=1, source_target_pairs={{0,64},{32,96},{64,0},{96,32},{1,65},{33,97},{65,1},{97,33},{2,66}... | collective-permute-start | bytes 245768 | tf_op jit(solution)/shard_map/gather_image/ppermute | solution.py:19
  71.5 1.5 %collective-permute-done.18 = f32[2,16,640]{2,1,0:T(8,128)S(1)} collective-permute-done((f32[2,16,640]{2,1,0:T(8,128)S(1)}, f32[2,16,640]{2,1,0:T(8,128)S(1)}, u32[]{:S(2)}, u32[]{:S(2)}) %collective-permute-start.18) | collective-permute-done | bytes 81952 | tf_op jit(solution)/shard_map/gather_image/ppermute | solution.py:19
  73.0 2.7 %collective-permute-done.19 = f32[2,16,640]{2,1,0:T(8,128)S(1)} collective-permute-done((f32[2,16,640]{2,1,0:T(8,128)S(1)}, f32[2,16,640]{2,1,0:T(8,128)S(1)}, u32[]{:S(2)}, u32[]{:S(2)}) %collective-permute-start.19) | collective-permute-done | bytes 81952 | tf_op jit(solution)/shard_map/gather_image/ppermute | solution.py:19
  76.3 5.8 %copy-done.1 = bf16[2048,4096]{1,0:T(8,128)(2,1)S(1)} copy-done((bf16[2048,4096]{1,0:T(8,128)(2,1)S(1)}, bf16[2048,4096]{1,0:T(8,128)(2,1)}, u32[]{:S(2)}) %copy-start.1) | copy-done | bytes 16777240
  82.1 2.5 %second_product.1 = (f32[16,4096]{1,0:T(8,128)S(1)}, f32[3,16,512]{2,1,0:T(8,128)S(1)}, f32[16,128]{1,0:T(8,128)S(1)}) custom-call(bf16[2048,4096]{1,0:T(8,128)(2,1)S(1)} %copy-done.1, f32[16,2048]{1,0:T(8,128)S(1)} %get-tuple-element.23.side_r, f32[16,2048]{1,0:T(8,128)S(1)} %get-tuple-element.15.image_r, f32[16,4096]{1,0:T(8,128)S(1)} %slice.127.side_c, ...), custom_call_target="tpu_custom_call" | custom-call | flops 4294967296 | bytes 20971520 | tf_op jit(solution)/shard_map/second_product/pallas_call | solution.py:125
  84.7 1.3 %collective-permute-done.21 = f32[16,2176]{1,0:T(8,128)S(1)} collective-permute-done((f32[16,2176]{1,0:T(8,128)S(1)}, f32[16,2176]{1,0:T(8,128)S(1)}, u32[]{:S(2)}, u32[]{:S(2)}) %collective-permute-start.21) | collective-permute-done | bytes 139296 | tf_op jit(solution)/shard_map/sum_over_yc/ppermute | solution.py:19
  86.1 2.2 %collective-permute-start.22 = (f32[16,640]{1,0:T(8,128)S(1)}, f32[16,640]{1,0:T(8,128)S(1)}, u32[]{:S(2)}, u32[]{:S(2)}) collective-permute-start(f32[16,640]{1,0:T(8,128)S(1)} %get-tuple-element.32), channel_id=1, source_target_pairs={{0,96},{32,0},{64,32},{96,64},{1,97},{33,1},{65,33},{97,65},{2,98}... | collective-permute-start | bytes 122888 | tf_op jit(solution)/shard_map/sum_over_yc/ppermute | solution.py:19
  89.3 1.3 %collective-permute-done.22 = f32[16,640]{1,0:T(8,128)S(1)} collective-permute-done((f32[16,640]{1,0:T(8,128)S(1)}, f32[16,640]{1,0:T(8,128)S(1)}, u32[]{:S(2)}, u32[]{:S(2)}) %collective-permute-start.22) | collective-permute-done | bytes 40992 | tf_op jit(solution)/shard_map/sum_over_yc/ppermute | solution.py:19
  90.5 3.3 %collective-permute-done.23 = f32[16,640]{1,0:T(8,128)S(1)} collective-permute-done((f32[16,640]{1,0:T(8,128)S(1)}, f32[16,640]{1,0:T(8,128)S(1)}, u32[]{:S(2)}, u32[]{:S(2)}) %collective-permute-start.23) | collective-permute-done | bytes 40992 | tf_op jit(solution)/shard_map/sum_over_yc/ppermute | solution.py:19
  94.2 4.2 %collective-permute-start.26 = (f32[16,128]{1,0:T(8,128)S(1)}, f32[16,128]{1,0:T(8,128)S(1)}, u32[]{:S(2)}, u32[]{:S(2)}) collective-permute-start(f32[16,128]{1,0:T(8,128)S(1)} %slice_add_fusion.4), channel_id=1, source_target_pairs={{0,16},{8,24},{16,0},{24,8},{1,17},{9,25},{17,1},{25,9},{2,18},{10... | collective-permute-start | bytes 24584 | tf_op jit(solution)/shard_map/sum_sums_over_z/ppermute | solution.py:19
  100.1 1.9 %collective-permute-done.27 = f32[16,128]{1,0:T(8,128)S(1)} collective-permute-done((f32[16,128]{1,0:T(8,128)S(1)}, f32[16,128]{1,0:T(8,128)S(1)}, u32[]{:S(2)}, u32[]{:S(2)}) %collective-permute-start.27) | collective-permute-done | bytes 8224 | tf_op jit(solution)/shard_map/sum_sums_over_z/ppermute | solution.py:19
  (76 shorter events, 10.1 us)
Async XLA Ops:
  2.3 15.1 %copy-start.2 = (bf16[512,256]{1,0:T(8,128)(2,1)}, bf16[512,256]{1,0:T(8,128)(2,1)S(1)}, u32[]{:S(2)}) copy-start(bf16[512,256]{1,0:T(8,128)(2,1)S(1)} %get-tuple-element.17.points_ref) | copy-start | bytes 786436
  2.3 11.5 %collective-permute-start.3 = (bf16[512,256]{1,0:T(8,128)(2,1)S(1)}, bf16[512,256]{1,0:T(8,128)(2,1)S(1)}, u32[]{:S(2)}, u32[]{:S(2)}) collective-permute-start(bf16[512,256]{1,0:T(8,128)(2,1)S(1)} %get-tuple-element.17.points_ref), channel_id=1, source_target_pairs={{0,32},{32,64},{64,96},{96,0},{1,33},{33,65},{65,97},{97,1},{2,34}... | collective-permute-start | bytes 786440 | tf_op jit(solution)/shard_map/fetch_points/ppermute | solution.py:19
  4.0 16.2 %collective-permute-start.4 = (bf16[512,256]{1,0:T(8,128)(2,1)S(1)}, bf16[512,256]{1,0:T(8,128)(2,1)S(1)}, u32[]{:S(2)}, u32[]{:S(2)}) collective-permute-start(bf16[512,256]{1,0:T(8,128)(2,1)S(1)} %get-tuple-element.17.points_ref), channel_id=1, source_target_pairs={{0,64},{32,96},{64,0},{96,32},{1,65},{33,97},{65,1},{97,33},{2,66}... | collective-permute-start | bytes 786440 | tf_op jit(solution)/shard_map/fetch_points/ppermute | solution.py:19
  6.9 14.7 %collective-permute-start.5 = (bf16[512,256]{1,0:T(8,128)(2,1)S(1)}, bf16[512,256]{1,0:T(8,128)(2,1)S(1)}, u32[]{:S(2)}, u32[]{:S(2)}) collective-permute-start(bf16[512,256]{1,0:T(8,128)(2,1)S(1)} %get-tuple-element.17.points_ref), channel_id=1, source_target_pairs={{0,96},{32,0},{64,32},{96,64},{1,97},{33,1},{65,33},{97,65},{2,98}... | collective-permute-start | bytes 786440 | tf_op jit(solution)/shard_map/fetch_points/ppermute | solution.py:19
  8.3 19.6 %collective-permute-start = (bf16[512,256]{1,0:T(8,128)(2,1)S(1)}, bf16[512,256]{1,0:T(8,128)(2,1)}, u32[]{:S(2)}, u32[]{:S(2)}) collective-permute-start(bf16[512,256]{1,0:T(8,128)(2,1)S(1)} %get-tuple-element.17.points_ref), channel_id=1, source_target_pairs={{0,8},{8,16},{16,24},{24,0},{1,9},{9,17},{17,25},{25,1},{2,10},{10... | collective-permute-start | bytes 786440 | tf_op jit(solution)/shard_map/fetch_points/ppermute | solution.py:19
  10.2 20.2 %collective-permute-start.1 = (bf16[512,256]{1,0:T(8,128)(2,1)S(1)}, bf16[512,256]{1,0:T(8,128)(2,1)}, u32[]{:S(2)}, u32[]{:S(2)}) collective-permute-start(bf16[512,256]{1,0:T(8,128)(2,1)S(1)} %get-tuple-element.17.points_ref), channel_id=1, source_target_pairs={{0,16},{8,24},{16,0},{24,8},{1,17},{9,25},{17,1},{25,9},{2,18},{10... | collective-permute-start | bytes 786440 | tf_op jit(solution)/shard_map/fetch_points/ppermute | solution.py:19
  13.8 16.6 %collective-permute-start.2 = (bf16[512,256]{1,0:T(8,128)(2,1)S(1)}, bf16[512,256]{1,0:T(8,128)(2,1)}, u32[]{:S(2)}, u32[]{:S(2)}) collective-permute-start(bf16[512,256]{1,0:T(8,128)(2,1)S(1)} %get-tuple-element.17.points_ref), channel_id=1, source_target_pairs={{0,24},{8,0},{16,8},{24,16},{1,25},{9,1},{17,9},{25,17},{2,26},{10... | collective-permute-start | bytes 786440 | tf_op jit(solution)/shard_map/fetch_points/ppermute | solution.py:19
  19.3 13.1 %copy-start.3 = (f32[24,512]{1,0:T(8,128)S(1)}, f32[24,512]{1,0:T(8,128)}, u32[]{:S(2)}) copy-start(f32[24,512]{1,0:T(8,128)} %prepare.1) | copy-start | bytes 147460
  20.2 11.6 %collective-permute-start.7 = (f32[24,512]{1,0:T(8,128)}, f32[24,512]{1,0:T(8,128)S(1)}, u32[]{:S(2)}, u32[]{:S(2)}) collective-permute-start(f32[24,512]{1,0:T(8,128)} %prepare.1), channel_id=1, source_target_pairs={{0,32},{32,64},{64,96},{96,0},{1,33},{33,65},{65,97},{97,1},{2,34}... | collective-permute-start | bytes 147464 | tf_op jit(solution)/shard_map/fetch_points/ppermute | solution.py:19
  21.7 10.2 %collective-permute-start.8 = (f32[24,512]{1,0:T(8,128)}, f32[24,512]{1,0:T(8,128)S(1)}, u32[]{:S(2)}, u32[]{:S(2)}) collective-permute-start(f32[24,512]{1,0:T(8,128)} %prepare.1), channel_id=1, source_target_pairs={{0,64},{32,96},{64,0},{96,32},{1,65},{33,97},{65,1},{97,33},{2,66}... | collective-permute-start | bytes 147464 | tf_op jit(solution)/shard_map/fetch_points/ppermute | solution.py:19
  27.9 4.6 %collective-permute-start.9 = (f32[24,512]{1,0:T(8,128)}, f32[24,512]{1,0:T(8,128)S(1)}, u32[]{:S(2)}, u32[]{:S(2)}) collective-permute-start(f32[24,512]{1,0:T(8,128)} %prepare.1), channel_id=1, source_target_pairs={{0,96},{32,0},{64,32},{96,64},{1,97},{33,1},{65,33},{97,65},{2,98}... | collective-permute-start | bytes 147464 | tf_op jit(solution)/shard_map/fetch_points/ppermute | solution.py:19
  31.7 3.1 %collective-permute-start.6 = (bf16[2048,256]{1,0:T(8,128)(2,1)S(1)}, bf16[2048,256]{1,0:T(8,128)(2,1)S(1)}, u32[]{:S(2)}, u32[]{:S(2)}) collective-permute-start(bf16[2048,256]{1,0:T(8,128)(2,1)S(1)} %get-tuple-element.18), channel_id=1, source_target_pairs={{0,4},{4,0},{1,5},{5,1},{2,6},{6,2},{3,7},{7,3},{8,12},{12,8},{9,1... | collective-permute-start | bytes 3145736 | tf_op jit(solution)/shard_map/fetch_points/ppermute | solution.py:19
  32.5 2.3 %collective-permute-start.10 = (f32[24,2048]{1,0:T(8,128)S(1)}, f32[24,2048]{1,0:T(8,128)S(1)}, u32[]{:S(2)}, u32[]{:S(2)}) collective-permute-start(f32[24,2048]{1,0:T(8,128)S(1)} %pad_maximum_fusion.3), channel_id=1, source_target_pairs={{0,4},{4,0},{1,5},{5,1},{2,6},{6,2},{3,7},{7,3},{8,12},{12,8},{9,1... | collective-permute-start | bytes 589832 | tf_op jit(solution)/shard_map/fetch_points/ppermute | solution.py:19
  47.0 5.7 %copy-start = (bf16[2048,4096]{1,0:T(8,128)(2,1)}, bf16[2048,4096]{1,0:T(8,128)(2,1)S(1)}, u32[]{:S(2)}) copy-start(bf16[2048,4096]{1,0:T(8,128)(2,1)S(1)} %get-tuple-element.7.tile_ref) | copy-start | bytes 50331652
  52.7 7.9 %collective-permute-start.15 = (f32[16,2048]{1,0:T(8,128)S(1)}, f32[16,2048]{1,0:T(8,128)S(1)}, u32[]{:S(2)}, u32[]{:S(2)}) collective-permute-start(f32[16,2048]{1,0:T(8,128)S(1)} %get-tuple-element.8), channel_id=1, source_target_pairs={{0,16},{8,24},{16,0},{24,8},{1,17},{9,25},{17,1},{25,9},{2,18},{10... | collective-permute-start | bytes 393224 | tf_op jit(solution)/shard_map/sum_over_z/ppermute | solution.py:19
  52.7 12.9 %collective-permute-start.11 = (f32[16,512]{1,0:T(8,128)S(1)}, f32[16,512]{1,0:T(8,128)S(1)}, u32[]{:S(2)}, u32[]{:S(2)}) collective-permute-start(f32[16,512]{1,0:T(8,128)S(1)} %slice.120), channel_id=1, source_target_pairs={{0,8},{8,16},{16,24},{24,0},{1,9},{9,17},{17,25},{25,1},{2,10},{10... | collective-permute-start | bytes 98312 | tf_op jit(solution)/shard_map/fetch_points/ppermute | solution.py:19
  54.0 11.6 %collective-permute-start.12 = (f32[16,512]{1,0:T(8,128)S(1)}, f32[16,512]{1,0:T(8,128)S(1)}, u32[]{:S(2)}, u32[]{:S(2)}) collective-permute-start(f32[16,512]{1,0:T(8,128)S(1)} %slice.120), channel_id=1, source_target_pairs={{0,16},{8,24},{16,0},{24,8},{1,17},{9,25},{17,1},{25,9},{2,18},{10... | collective-permute-start | bytes 98312 | tf_op jit(solution)/shard_map/fetch_points/ppermute | solution.py:19
  56.2 9.4 %collective-permute-start.13 = (f32[16,512]{1,0:T(8,128)S(1)}, f32[16,512]{1,0:T(8,128)S(1)}, u32[]{:S(2)}, u32[]{:S(2)}) collective-permute-start(f32[16,512]{1,0:T(8,128)S(1)} %slice.120), channel_id=1, source_target_pairs={{0,24},{8,0},{16,8},{24,16},{1,25},{9,1},{17,9},{25,17},{2,26},{10... | collective-permute-start | bytes 98312 | tf_op jit(solution)/shard_map/fetch_points/ppermute | solution.py:19
  58.9 6.2 %collective-permute-start.14 = (f32[16,2048]{1,0:T(8,128)S(1)}, f32[16,2048]{1,0:T(8,128)S(1)}, u32[]{:S(2)}, u32[]{:S(2)}) collective-permute-start(f32[16,2048]{1,0:T(8,128)S(1)} %get-tuple-element.8), channel_id=1, source_target_pairs={{0,8},{8,16},{16,24},{24,0},{1,9},{9,17},{17,25},{25,1},{2,10},{10... | collective-permute-start | bytes 393224 | tf_op jit(solution)/shard_map/sum_over_z/ppermute | solution.py:19
  60.6 5.0 %collective-permute-start.16 = (f32[16,2048]{1,0:T(8,128)S(1)}, f32[16,2048]{1,0:T(8,128)S(1)}, u32[]{:S(2)}, u32[]{:S(2)}) collective-permute-start(f32[16,2048]{1,0:T(8,128)S(1)} %get-tuple-element.8), channel_id=1, source_target_pairs={{0,24},{8,0},{16,8},{24,16},{1,25},{9,1},{17,9},{25,17},{2,26},{10... | collective-permute-start | bytes 393224 | tf_op jit(solution)/shard_map/sum_over_z/ppermute | solution.py:19
  65.9 1.3 %collective-permute-start.17 = (f32[16,640]{1,0:T(8,128)S(1)}, f32[16,640]{1,0:T(8,128)S(1)}, u32[]{:S(2)}, u32[]{:S(2)}) collective-permute-start(f32[16,640]{1,0:T(8,128)S(1)} %get-tuple-element.31), channel_id=1, source_target_pairs={{0,4},{4,0},{1,5},{5,1},{2,6},{6,2},{3,7},{7,3},{8,12},{12,8},{9,1... | collective-permute-start | bytes 122888 | tf_op jit(solution)/shard_map/gather_image/ppermute | solution.py:19
  67.2 5.8 %collective-permute-start.18 = (f32[2,16,640]{2,1,0:T(8,128)S(1)}, f32[2,16,640]{2,1,0:T(8,128)S(1)}, u32[]{:S(2)}, u32[]{:S(2)}) collective-permute-start(f32[2,16,640]{2,1,0:T(8,128)S(1)} %get-tuple-element.29), channel_id=1, source_target_pairs={{0,32},{32,64},{64,96},{96,0},{1,33},{33,65},{65,97},{97,1},{2,34}... | collective-permute-start | bytes 245768 | tf_op jit(solution)/shard_map/gather_image/ppermute | solution.py:19
  67.6 8.1 %collective-permute-start.19 = (f32[2,16,640]{2,1,0:T(8,128)S(1)}, f32[2,16,640]{2,1,0:T(8,128)S(1)}, u32[]{:S(2)}, u32[]{:S(2)}) collective-permute-start(f32[2,16,640]{2,1,0:T(8,128)S(1)} %get-tuple-element.29), channel_id=1, source_target_pairs={{0,64},{32,96},{64,0},{96,32},{1,65},{33,97},{65,1},{97,33},{2,66}... | collective-permute-start | bytes 245768 | tf_op jit(solution)/shard_map/gather_image/ppermute | solution.py:19
  71.4 4.4 %collective-permute-start.20 = (f32[2,16,640]{2,1,0:T(8,128)S(1)}, f32[2,16,640]{2,1,0:T(8,128)S(1)}, u32[]{:S(2)}, u32[]{:S(2)}) collective-permute-start(f32[2,16,640]{2,1,0:T(8,128)S(1)} %get-tuple-element.29), channel_id=1, source_target_pairs={{0,96},{32,0},{64,32},{96,64},{1,97},{33,1},{65,33},{97,65},{2,98}... | collective-permute-start | bytes 245768 | tf_op jit(solution)/shard_map/gather_image/ppermute | solution.py:19
  76.3 5.8 %copy-start.1 = (bf16[2048,4096]{1,0:T(8,128)(2,1)S(1)}, bf16[2048,4096]{1,0:T(8,128)(2,1)}, u32[]{:S(2)}) copy-start(bf16[2048,4096]{1,0:T(8,128)(2,1)} %copy-done) | copy-start | bytes 50331652
  84.6 1.4 %collective-permute-start.21 = (f32[16,2176]{1,0:T(8,128)S(1)}, f32[16,2176]{1,0:T(8,128)S(1)}, u32[]{:S(2)}, u32[]{:S(2)}) collective-permute-start(f32[16,2176]{1,0:T(8,128)S(1)} %pad_maximum_fusion.4), channel_id=1, source_target_pairs={{0,4},{4,0},{1,5},{5,1},{2,6},{6,2},{3,7},{7,3},{8,12},{12,8},{9,1... | collective-permute-start | bytes 417800 | tf_op jit(solution)/shard_map/sum_over_yc/ppermute | solution.py:19
  86.1 4.4 %collective-permute-start.22 = (f32[16,640]{1,0:T(8,128)S(1)}, f32[16,640]{1,0:T(8,128)S(1)}, u32[]{:S(2)}, u32[]{:S(2)}) collective-permute-start(f32[16,640]{1,0:T(8,128)S(1)} %get-tuple-element.32), channel_id=1, source_target_pairs={{0,96},{32,0},{64,32},{96,64},{1,97},{33,1},{65,33},{97,65},{2,98}... | collective-permute-start | bytes 122888 | tf_op jit(solution)/shard_map/sum_over_yc/ppermute | solution.py:19
  88.3 5.6 %collective-permute-start.23 = (f32[16,640]{1,0:T(8,128)S(1)}, f32[16,640]{1,0:T(8,128)S(1)}, u32[]{:S(2)}, u32[]{:S(2)}) collective-permute-start(f32[16,640]{1,0:T(8,128)S(1)} %get-tuple-element.33), channel_id=1, source_target_pairs={{0,64},{32,96},{64,0},{96,32},{1,65},{33,97},{65,1},{97,33},{2,66}... | collective-permute-start | bytes 122888 | tf_op jit(solution)/shard_map/sum_over_yc/ppermute | solution.py:19
  88.6 5.7 %collective-permute-start.24 = (f32[16,640]{1,0:T(8,128)S(1)}, f32[16,640]{1,0:T(8,128)S(1)}, u32[]{:S(2)}, u32[]{:S(2)}) collective-permute-start(f32[16,640]{1,0:T(8,128)S(1)} %get-tuple-element.34), channel_id=1, source_target_pairs={{0,32},{32,64},{64,96},{96,0},{1,33},{33,65},{65,97},{97,1},{2,34}... | collective-permute-start | bytes 122888 | tf_op jit(solution)/shard_map/sum_over_yc/ppermute | solution.py:19
  94.2 4.9 %collective-permute-start.25 = (f32[16,128]{1,0:T(8,128)S(1)}, f32[16,128]{1,0:T(8,128)S(1)}, u32[]{:S(2)}, u32[]{:S(2)}) collective-permute-start(f32[16,128]{1,0:T(8,128)S(1)} %slice_add_fusion.4), channel_id=1, source_target_pairs={{0,8},{8,16},{16,24},{24,0},{1,9},{9,17},{17,25},{25,1},{2,10},{10... | collective-permute-start | bytes 24584 | tf_op jit(solution)/shard_map/sum_sums_over_z/ppermute | solution.py:19
  94.2 5.9 %collective-permute-start.26 = (f32[16,128]{1,0:T(8,128)S(1)}, f32[16,128]{1,0:T(8,128)S(1)}, u32[]{:S(2)}, u32[]{:S(2)}) collective-permute-start(f32[16,128]{1,0:T(8,128)S(1)} %slice_add_fusion.4), channel_id=1, source_target_pairs={{0,16},{8,24},{16,0},{24,8},{1,17},{9,25},{17,1},{25,9},{2,18},{10... | collective-permute-start | bytes 24584 | tf_op jit(solution)/shard_map/sum_sums_over_z/ppermute | solution.py:19
  98.4 3.7 %collective-permute-start.27 = (f32[16,128]{1,0:T(8,128)S(1)}, f32[16,128]{1,0:T(8,128)S(1)}, u32[]{:S(2)}, u32[]{:S(2)}) collective-permute-start(f32[16,128]{1,0:T(8,128)S(1)} %slice_add_fusion.4), channel_id=1, source_target_pairs={{0,24},{8,0},{16,8},{24,16},{1,25},{9,1},{17,9},{25,17},{2,26},{10... | collective-permute-start | bytes 24584 | tf_op jit(solution)/shard_map/sum_sums_over_z/ppermute | solution.py:19

commit v2 on v1

v2 whole, which is shorter than its diff:
```python
import functools

import jax
import jax.numpy as jnp
from jax import lax
from jax.experimental import pallas as pl
from jax.experimental.pallas import tpu as pltpu
from jax.sharding import Mesh
from jax.sharding import PartitionSpec as P

NY, NZ, NC, NX = 4, 4, 2, 4
LANES = 128
CHUNK = 256
ROWS = (0, 1, 3, 2)
COLS = ((0, 0), (1, 0), (0, 1), (0, 3), (1, 1), (1, 3), (0, 2), (1, 2))

noise_level = 1.0
kernel_rate = 0.5


def shift(value, axis, size, step):
    return lax.ppermute(value, axis, [(i, (i + step) % size) for i in range(size)])


def split_rows(value):
    high = value.astype(jnp.bfloat16).astype(jnp.float32)
    middle = (value - high).astype(jnp.bfloat16).astype(jnp.float32)
    return high, middle, value - high - middle


def pack_kernel(points_ref, side_ref, out_ref):
    own, width = points_ref.shape
    probes = side_ref.shape[0]
    out_ref[:own, :] = points_ref[...]
    norms = jnp.sum(points_ref[...].astype(jnp.float32) ** 2, axis=1, keepdims=True)
    norms = jnp.broadcast_to(norms, (own, LANES)).T[:16, :]
    high, middle, low = split_rows(norms)
    row = lax.broadcasted_iota(jnp.int32, norms.shape, 0)
    norms = jnp.where(row == 0, high, jnp.where(row == 1, middle, jnp.where(row == 2, low, 0.0)))
    high, middle, _ = split_rows(side_ref[...])
    at = own
    for part in (high, middle, norms):
        for j in range(own // width):
            out_ref[at : at + probes, :] = part[:, j * width : (j + 1) * width].astype(jnp.bfloat16)
            at += probes


def pack(points, side):
    own, width = points.shape
    extra = side.shape[0] * 3 * own // width
    return pl.pallas_call(
        pack_kernel,
        out_shape=jax.ShapeDtypeStruct((own + extra, width), jnp.bfloat16),
        name="pack",
    )(points, side)


def unpack_rows(message, probes, own, term):
    width = message.shape[1]
    count = own // width
    at = own + term * count * probes
    return jnp.concatenate([message[at + j * probes : at + (j + 1) * probes] for j in range(count)], axis=1)


def tile_kernel(counts, probes, *refs):
    rows_count, cols_count, known_halves, prior_count, has_side = counts
    refs = list(refs)
    row_refs = [refs.pop(0) for _ in range(rows_count)]
    col_refs = [refs.pop(0) for _ in range(cols_count)]
    half_refs = [refs.pop(0) for _ in range(known_halves)]
    prior_refs = [refs.pop(0) for _ in range(prior_count)]
    side_ref = refs.pop(0) if has_side else None
    tile_ref, image_ref = refs.pop(0), refs.pop(0)
    own = row_refs[0].shape[0]
    if known_halves:
        pieces = []
        for half_ref in half_refs:
            pieces += [half_ref[j * own : (j + 1) * own, :] for j in range(half_ref.shape[0] // own)]
        halves = pieces
    else:
        new_ref = refs.pop(0)
        halves = []
        for i, row_ref in enumerate(row_refs):
            squares = row_ref[...].astype(jnp.float32) ** 2
            halves.append(-kernel_rate * jnp.sum(squares, axis=1, keepdims=True))
            new_ref[i * own : (i + 1) * own, :] = halves[-1]
    if prior_count:
        at = 0
        for prior_ref in prior_refs:
            image_ref[:, at : at + prior_ref.shape[1]] = prior_ref[...]
            at += prior_ref.shape[1]
    else:
        image_ref[...] = jnp.zeros_like(image_ref)
        if has_side:
            image_ref[:, :own] = noise_level * side_ref[...]
    for j, col_ref in enumerate(col_refs):
        field = unpack_rows(col_ref, probes, own, 0)
        norms = unpack_rows(col_ref, probes, own, 2).astype(jnp.float32)
        col_half = -kernel_rate * (norms[0:1] + norms[1:2] + norms[2:3])
        for i, row_ref in enumerate(row_refs):
            for k in range(own // CHUNK):
                part = slice(k * CHUNK, (k + 1) * CHUNK)
                place = slice(i * own + k * CHUNK, i * own + (k + 1) * CHUNK)
                cross = lax.dot_general(
                    row_ref[part, :], col_ref[:own, :], (((1,), (1,)), ((), ())), preferred_element_type=jnp.float32
                )
                kern = jnp.exp(2.0 * kernel_rate * cross + halves[i][part, :] + col_half).astype(jnp.bfloat16)
                tile_ref[place, j * own : (j + 1) * own] = kern
                image_ref[:, place] += lax.dot_general(
                    field, kern, (((1,), (1,)), ((), ())), preferred_element_type=jnp.float32
                )


def build(rows, cols, probes, halves=(), prior=(), side=None):
    own, features = rows[0].shape
    height, width = len(rows) * own, len(cols) * own
    counts = (len(rows), len(cols), len(halves), len(prior), side is not None)
    out_shape = [
        pltpu.VMEM((height, width), jnp.bfloat16),
        jax.ShapeDtypeStruct((probes, height), jnp.float32),
    ]
    if not halves:
        out_shape.append(jax.ShapeDtypeStruct((height, 1), jnp.float32))
    args = [*rows, *cols, *halves, *prior] + ([] if side is None else [side])
    return pl.pallas_call(
        functools.partial(tile_kernel, counts, probes),
        out_shape=out_shape,
        compiler_params=pltpu.CompilerParams(vmem_limit_bytes=16 << 20),
        cost_estimate=pl.CostEstimate(
            flops=2 * height * width * (features + 256), bytes_accessed=1 << 20, transcendentals=height * width
        ),
        name="build_tile",
    )(*args)


def second_kernel(own, tiles, image_r, side_r, image_c, side_c, sums_ref, mine_ref, other_ref, own_ref):
    sums = sums_ref[...]
    rr, curve, square = sums[:, 0:1], sums[:, 1:2], sums[:, 2:3]
    alpha = rr / curve
    rr_next = rr - 2.0 * alpha * curve + alpha * alpha * square
    beta = rr_next / rr
    res_r = side_r[...] - alpha * image_r[...]
    dir_r = res_r + beta * side_r[...]
    narrow = dir_r.astype(jnp.bfloat16)
    total = jnp.zeros_like(alpha)
    for j, (h, m) in enumerate(COLS):
        part = 0.0
        for tile_ref, top, left in tiles:
            at = j * own - left
            if 0 <= at < tile_ref.shape[1]:
                part = part + jnp.dot(
                    narrow[:, top : top + tile_ref.shape[0]],
                    tile_ref[:, at : at + own],
                    preferred_element_type=jnp.float32,
                )
        cols = slice(j * own, (j + 1) * own)
        dir_c = (side_c[:, cols] - alpha * image_c[:, cols]) + beta * side_c[:, cols]
        total = total + jnp.sum(part * dir_c, axis=1, keepdims=True)
        (other_ref if h else mine_ref)[:, m * own : (m + 1) * own] = part
    own_res, own_dir = res_r[:, :own], dir_r[:, :own]
    own_ref[0] = own_res
    own_ref[1] = own_dir
    own_ref[2] = alpha * side_r[:, :own]
    total = total + noise_level * jnp.sum(own_dir * own_dir, axis=1, keepdims=True)
    rr_own = jnp.sum(own_res * own_res, axis=1, keepdims=True)
    lane = lax.broadcasted_iota(jnp.int32, (total.shape[0], LANES), 1)
    out_sums = jnp.where(lane == 0, total, jnp.where(lane == 1, rr_own, 0.0))
    mine_ref[:, NY * own :] = out_sums
    other_ref[:, NY * own :] = out_sums


def second_product(tiles, image_r, side_r, image_c, side_c, sums, own):
    probes, rows = side_r.shape
    cols = side_c.shape[1]
    places = [(top, left) for _, top, left in tiles]

    def kernel(*refs):
        held = [(ref, top, left) for ref, (top, left) in zip(refs, places)]
        second_kernel(own, held, *refs[len(places) :])

    return pl.pallas_call(
        kernel,
        in_specs=[pl.BlockSpec(memory_space=pltpu.VMEM)] * (len(tiles) + 5),
        out_shape=[
            jax.ShapeDtypeStruct((probes, cols // NC + LANES), jnp.float32),
            jax.ShapeDtypeStruct((probes, cols // NC + LANES), jnp.float32),
            jax.ShapeDtypeStruct((3, probes, own), jnp.float32),
        ],
        compiler_params=pltpu.CompilerParams(vmem_limit_bytes=16 << 20),
        cost_estimate=pl.CostEstimate(flops=2 * rows * cols * 256, bytes_accessed=1 << 20, transcendentals=0),
        name="second_product",
    )(*[tile for tile, _, _ in tiles], image_r, side_r, image_c, side_c, sums)


def on_device(states, offsets, right_side):
    own, probes = right_side.shape
    side = right_side.T
    points = lax.dynamic_slice_in_dim(states, offsets[0], own, 0)
    with jax.named_scope("fetch_points"):
        row = {0: points}
        for k in (1, 3, 2):
            row[k] = shift(points, "z", NZ, k)
        message = pack(points, side)
        col = {(0, 0): message, (1, 0): shift(message, "c", NC, 1)}
        for m in (1, 3, 2):
            col[0, m] = shift(message, "y", NY, m)
        for m in (1, 3, 2):
            col[1, m] = shift(col[0, m], "c", NC, 1)
        near = [row[k] for k in ROWS[:3]]
        col = [col[at] for at in COLS]

    with jax.named_scope("build_tiles"):
        tile_a, image, half = build(near, col[:2], probes, side=side)
        tile_b, image = build(near, col[2:4], probes, [half], [image])
        tile_c, image = build(near, col[4:6], probes, [half], [image])
        tile_d, image_far, half_far = build([row[2]], col[:6], probes)
        tile_e, image = build(near + [row[2]], col[6:], probes, [half, half_far], [image, image_far])
        far = 3 * own
        tiles = [
            (tile_a, 0, 0),
            (tile_b, 0, 2 * own),
            (tile_c, 0, 4 * own),
            (tile_d, far, 0),
            (tile_e, 0, 6 * own),
        ]
        side_c = [unpack_rows(one, probes, own, 0) + unpack_rows(one, probes, own, 1).astype(jnp.float32) for one in col]
        side_c = jnp.concatenate(side_c, axis=1)

    with jax.named_scope("sum_over_z"):
        message = jnp.concatenate([image, side], axis=1)
        every = {0: message}
        for s in (1, 3, 2):
            every[s] = shift(message, "z", NZ, s)
        pieces = []
        for p in ROWS:
            piece = 0.0
            for s in range(NZ):
                at = ROWS.index((p - s) % NZ) * own
                piece = piece + every[s][:, at : at + own]
            pieces.append(piece)
        image_r = jnp.concatenate(pieces, axis=1)
        side_r = jnp.concatenate([every[p][:, NZ * own :] for p in ROWS], axis=1)
        sums = jnp.stack(
            [jnp.sum(side_r * side_r, axis=1), jnp.sum(side_r * image_r, axis=1), jnp.sum(image_r * image_r, axis=1)],
            axis=1,
        )
        sums = jnp.pad(sums, ((0, 0), (0, LANES - 3)))

    with jax.named_scope("gather_image"):
        message = jnp.concatenate([image_r[:, :own], sums], axis=1)
        pair = jnp.concatenate([message, shift(message, "c", NC, 1)], axis=0)
        every = {0: pair}
        for m in (1, 3, 2):
            every[m] = shift(pair, "y", NY, m)
        image_c = jnp.concatenate([every[m][h * probes : (h + 1) * probes, :own] for h, m in COLS], axis=1)
        sums = sum(every[m][h * probes : (h + 1) * probes, own:] for h, m in COLS)

    mine, other, held = second_product(tiles, image_r, side_r, image_c, side_c, sums, own)

    with jax.named_scope("sum_over_yc"):
        mine = mine + shift(other, "c", NC, 1)
        image = mine[:, :own]
        sums = mine[:, NY * own :]
        total = sums
        for m in (1, 3, 2):
            message = jnp.concatenate([mine[:, m * own : (m + 1) * own], sums], axis=1)
            message = shift(message, "y", NY, -m)
            image = image + message[:, :own]
            total = total + message[:, own:]

    with jax.named_scope("sum_sums_over_z"):
        sums = total
        for k in (1, 3, 2):
            total = total + shift(sums, "z", NZ, k)

    alpha = total[:, 1:2] / total[:, 0:1]
    residual, direction, field = held[0], held[1], held[2]
    image = image + noise_level * direction
    field = field + alpha * direction
    residual = residual - alpha * image
    return field.T, residual.T


def solution(mesh):
    fine = Mesh(mesh.devices.reshape(NY, NZ, NC, NX), ("y", "z", "c", "x"))
    rows = ("y", "z", "c")
    in_specs = (P(rows, None), P(rows), P(rows, "x"))
    out_specs = (P(rows, "x"), P(rows, "x"))
    return jax.shard_map(on_device, mesh=fine, in_specs=in_specs, out_specs=out_specs, check_vma=False)
```

time: 103 us -> 114 us (1.11)
  waiting for transfers between devices: 23.5 us -> 48.7 us
  starting transfers between devices: 43.3 us -> 24.8 us
  local copies, waits for them, and re-layouts: 15.7 us -> 22.6 us
  Pallas kernels: 16.4 us -> 14.7 us
  other arithmetic: 2.53 us -> 1.27 us
    ppermute x28 -> x24, waiting for transfers between devices: 23.5 us -> 48.7 us  [shift(): lax.ppermute(value, axis, [(i, (i + step) % size) for i in range(size)])]
    ppermute x28 -> x24, starting transfers between devices: 43.3 us -> 24.8 us  [shift(): lax.ppermute(value, axis, [(i, (i + step) % size) for i in range(size)])]
    unnamed x17 -> x42, local copies, waits for them, and re-layouts: 15.1 us -> 21.6 us
    pallas_call x3 -> x7, Pallas kernels: 16.4 us -> 14.7 us  [the longest x5 10.3 us: build(): pl.pallas_call(functools.partial(tile_kernel, counts, probes), out_shape=...]
    concatenate x3 -> x4, other arithmetic: 1.35 us -> 0.03 us  [the longest x1 0.01 us: on_device(): message = jnp.concatenate([image, side], axis=1)]
  transfers between devices with their start and end apart: 28 -> 24, of which waited for: 16 -> 13; matrix products, arithmetic and copies ran while one was open for 4% -> 1% of each run, Pallas kernels for 2% -> 9%
where the time goes in v2:
time: 114 us
  waiting for transfers between devices  48.7 us (43%)
  starting transfers between devices  24.8 us (22%)
  local copies, waits for them, and re-layouts  22.6 us (20%)
  Pallas kernels  14.7 us (13%)
  between operations  1.63 us (1%)
  other arithmetic  1.27 us (1%)
    ppermute x24, waiting for transfers between devices, shift(): lax.ppermute(value, axis, [(i, (i + step) % size) for i in range(size)])  48.7 us
    ppermute x24, starting transfers between devices, shift(): lax.ppermute(value, axis, [(i, (i + step) % size) for i in range(size)])  24.8 us
    unnamed x42, local copies, waits for them, and re-layouts  21.6 us
    pallas_call x5, Pallas kernels, build(): pl.pallas_call(functools.partial(tile_kernel, counts, probes), out_shape=...  10.3 us
    pallas_call x1, Pallas kernels, second_product(): pl.pallas_call(kernel, in_specs=[pl.BlockSpec(memory_space=pltpu.VMEM)] *...  2.48 us
  transfers between devices with their start and end apart: 24, of which 13 were waited for; matrix products, arithmetic and copies ran while one was open for 1% of the time, Pallas kernels for 9%

profile of v2, /device:TPU:0, one launch (start us, length us, event | category | flops | bytes accessed | tf_op | source)
XLA Modules:
  0.0 113.6 jit_solution(8830796046560098865)
XLA Ops:
  1.8 4.0 %collective-permute-start.7 = (bf16[512,256]{1,0:T(8,128)(2,1)S(1)}, bf16[512,256]{1,0:T(8,128)(2,1)S(1)}, u32[]{:S(2)}, u32[]{:S(2)}) collective-permute-start(bf16[512,256]{1,0:T(8,128)(2,1)S(1)} %constant_dynamic-slice_fusion.points_ref.refs_0_), channel_id=1, source_target_pairs={{0,16},{8,24},{16,0},{24,8},{1,17},{9,25},{17,1},{25,9},{2,18},{10... | collective-permute-start | bytes 786440 | tf_op jit(solution)/shard_map/fetch_points/ppermute | solution.py:22
  7.8 1.9 %pack.1.refs_3_.refs_1_ = bf16[608,256]{1,0:T(8,128)(2,1)} custom-call(bf16[512,256]{1,0:T(8,128)(2,1)} %copy-done.11, f32[16,512]{1,0:T(8,128)} %bitcast.23), custom_call_target="tpu_custom_call" | custom-call | tf_op jit(solution)/shard_map/fetch_points/pack/pallas_call | solution.py:51
  9.7 3.2 %collective-permute-start.8 = (bf16[608,256]{1,0:T(8,128)(2,1)}, bf16[608,256]{1,0:T(8,128)(2,1)S(1)}, u32[]{:S(2)}, u32[]{:S(2)}) collective-permute-start(bf16[608,256]{1,0:T(8,128)(2,1)} %pack.1.refs_3_.refs_1_), channel_id=1, source_target_pairs={{0,64},{32,96},{64,0},{96,32},{1,65},{33,97},{65,1},{97,33},{2,66}... | collective-permute-start | bytes 933896 | tf_op jit(solution)/shard_map/fetch_points/ppermute | solution.py:22
  14.7 4.9 %collective-permute-done.8.refs_4_ = bf16[608,256]{1,0:T(8,128)(2,1)S(1)} collective-permute-done((bf16[608,256]{1,0:T(8,128)(2,1)}, bf16[608,256]{1,0:T(8,128)(2,1)S(1)}, u32[]{:S(2)}, u32[]{:S(2)}) %collective-permute-start.8) | collective-permute-done | bytes 311328 | tf_op jit(solution)/shard_map/fetch_points/ppermute | solution.py:22
  19.7 7.0 %collective-permute-done.4.refs_4_ = bf16[608,256]{1,0:T(8,128)(2,1)S(1)} collective-permute-done((bf16[608,256]{1,0:T(8,128)(2,1)}, bf16[608,256]{1,0:T(8,128)(2,1)S(1)}, u32[]{:S(2)}, u32[]{:S(2)}) %collective-permute-start.4) | collective-permute-done | bytes 311328 | tf_op jit(solution)/shard_map/fetch_points/ppermute | solution.py:22
  28.0 9.1 %collective-permute-done.3.refs_3_ = bf16[608,256]{1,0:T(8,128)(2,1)S(1)} collective-permute-done((bf16[608,256]{1,0:T(8,128)(2,1)}, bf16[608,256]{1,0:T(8,128)(2,1)S(1)}, u32[]{:S(2)}, u32[]{:S(2)}) %collective-permute-start.3) | collective-permute-done | bytes 311328 | tf_op jit(solution)/shard_map/fetch_points/ppermute | solution.py:22
  40.3 2.0 %build_tile.5 = (bf16[1536,1024]{1,0:T(8,128)(2,1)S(1)}, f32[16,1536]{1,0:T(8,128)S(1)}, f32[1536,1]{1,0:T(8,128)S(1)}) custom-call(bf16[512,256]{1,0:T(8,128)(2,1)S(1)} %copy-done.12, bf16[512,256]{1,0:T(8,128)(2,1)S(1)} %collective-permute-done.refs_1_, bf16[512,256]{1,0:T(8,128)(2,1)S(1)} %collective-permute-done.1.refs_2_, ...), custom_call_target="tpu_custom_call" | custom-call | flops 1610612736 | bytes 1048576 | tf_op jit(solution)/shard_map/build_tiles/build_tile/pallas_call | solution.py:125
  42.4 1.6 %copy-done.3 = bf16[1536,1024]{1,0:T(8,128)(2,1)} copy-done((bf16[1536,1024]{1,0:T(8,128)(2,1)}, bf16[1536,1024]{1,0:T(8,128)(2,1)S(1)}, u32[]{:S(2)}) %copy-start.3) | copy-done | bytes 3145752
  44.0 1.9 %build_tile.6 = (bf16[1536,1024]{1,0:T(8,128)(2,1)S(1)}, f32[16,1536]{1,0:T(8,128)S(1)}) custom-call(bf16[512,256]{1,0:T(8,128)(2,1)S(1)} %copy-done.12, bf16[512,256]{1,0:T(8,128)(2,1)S(1)} %collective-permute-done.refs_1_, bf16[512,256]{1,0:T(8,128)(2,1)S(1)} %collective-permute-done.1.refs_2_, bf16[608,256]{1,0:T(8,128)(2,1)S(1)} %collective-permute-done.3.refs_3_, ...), custom_call_target="tpu_custom_call" | custom-call | flops 1610612736 | bytes 1048576 | tf_op jit(solution)/shard_map/build_tiles/build_tile/pallas_call | solution.py:125
  45.9 1.8 %copy-done.5 = bf16[1536,1024]{1,0:T(8,128)(2,1)} copy-done((bf16[1536,1024]{1,0:T(8,128)(2,1)}, bf16[1536,1024]{1,0:T(8,128)(2,1)S(1)}, u32[]{:S(2)}) %copy-start.5) | copy-done | bytes 3145752
  47.7 2.0 %build_tile.8 = (bf16[512,3072]{1,0:T(8,128)(2,1)S(1)}, f32[16,512]{1,0:T(8,128)S(1)}, f32[512,1]{1,0:T(8,128)S(1)}) custom-call(bf16[512,256]{1,0:T(8,128)(2,1)S(1)} %collective-permute-done.7.refs_0_.refs_3_, bf16[608,256]{1,0:T(8,128)(2,1)S(1)} %copy-done.15, bf16[608,256]{1,0:T(8,128)(2,1)S(1)} %collective-permute-done.2.refs_4_.refs_2_, ...), custom_call_target="tpu_custom_call" | custom-call | flops 1610612736 | bytes 1048576 | tf_op jit(solution)/shard_map/build_tiles/build_tile/pallas_call | solution.py:125
  49.8 1.8 %copy-done.7 = bf16[512,3072]{1,0:T(8,128)(2,1)} copy-done((bf16[512,3072]{1,0:T(8,128)(2,1)}, bf16[512,3072]{1,0:T(8,128)(2,1)S(1)}, u32[]{:S(2)}) %copy-start.7) | copy-done | bytes 3145752
  51.5 1.9 %build_tile.7 = (bf16[1536,1024]{1,0:T(8,128)(2,1)S(1)}, f32[16,1536]{1,0:T(8,128)S(1)}) custom-call(bf16[512,256]{1,0:T(8,128)(2,1)S(1)} %copy-done.13, bf16[512,256]{1,0:T(8,128)(2,1)S(1)} %collective-permute-done.refs_1_, bf16[512,256]{1,0:T(8,128)(2,1)S(1)} %collective-permute-done.1.refs_2_, ...), custom_call_target="tpu_custom_call" | custom-call | flops 1610612736 | bytes 1048576 | tf_op jit(solution)/shard_map/build_tiles/build_tile/pallas_call | solution.py:125
  53.4 1.6 %copy-done.9 = bf16[1536,1024]{1,0:T(8,128)(2,1)} copy-done((bf16[1536,1024]{1,0:T(8,128)(2,1)}, bf16[1536,1024]{1,0:T(8,128)(2,1)S(1)}, u32[]{:S(2)}) %copy-start.9) | copy-done | bytes 3145752
  55.1 2.5 %build_tile.9 = (bf16[2048,1024]{1,0:T(8,128)(2,1)S(1)}, f32[16,2048]{1,0:T(8,128)S(1)}) custom-call(bf16[512,256]{1,0:T(8,128)(2,1)S(1)} %copy-done.13, bf16[512,256]{1,0:T(8,128)(2,1)S(1)} %collective-permute-done.refs_1_, bf16[512,256]{1,0:T(8,128)(2,1)S(1)} %collective-permute-done.1.refs_2_, ...), custom_call_target="tpu_custom_call" | custom-call | flops 2147483648 | bytes 1048576 | tf_op jit(solution)/shard_map/build_tiles/build_tile/pallas_call | solution.py:125
  57.5 2.0 %copy-done.1 = bf16[2048,1024]{1,0:T(8,128)(2,1)} copy-done((bf16[2048,1024]{1,0:T(8,128)(2,1)}, bf16[2048,1024]{1,0:T(8,128)(2,1)S(1)}, u32[]{:S(2)}) %copy-start.1) | copy-done | bytes 4194328
  59.5 2.0 %collective-permute-start.12 = (f32[16,2560]{1,0:T(8,128)S(1)}, f32[16,2560]{1,0:T(8,128)S(1)}, u32[]{:S(2)}, u32[]{:S(2)}) collective-permute-start(f32[16,2560]{1,0:T(8,128)S(1)} %pad_maximum_fusion), channel_id=1, source_target_pairs={{0,24},{8,0},{16,8},{24,16},{1,25},{9,1},{17,9},{25,17},{2,26},{10... | collective-permute-start | bytes 491528 | tf_op jit(solution)/shard_map/sum_over_z/ppermute | solution.py:22
  62.8 6.2 %collective-permute-done.12 = f32[16,2560]{1,0:T(8,128)S(1)} collective-permute-done((f32[16,2560]{1,0:T(8,128)S(1)}, f32[16,2560]{1,0:T(8,128)S(1)}, u32[]{:S(2)}, u32[]{:S(2)}) %collective-permute-start.12) | collective-permute-done | bytes 163872 | tf_op jit(solution)/shard_map/sum_over_z/ppermute | solution.py:22
  70.1 2.5 %collective-permute-done.10 = f32[16,2560]{1,0:T(8,128)S(1)} collective-permute-done((f32[16,2560]{1,0:T(8,128)S(1)}, f32[16,2560]{1,0:T(8,128)S(1)}, u32[]{:S(2)}, u32[]{:S(2)}) %collective-permute-start.10) | collective-permute-done | bytes 163872 | tf_op jit(solution)/shard_map/sum_over_z/ppermute | solution.py:22
  75.1 2.1 %collective-permute-start.15 = (f32[32,640]{1,0:T(8,128)S(1)}, f32[32,640]{1,0:T(8,128)S(1)}, u32[]{:S(2)}, u32[]{:S(2)}) collective-permute-start(f32[32,640]{1,0:T(8,128)S(1)} %pad_maximum_fusion.3), channel_id=1, source_target_pairs={{0,96},{32,0},{64,32},{96,64},{1,97},{33,1},{65,33},{97,65},{2,98}... | collective-permute-start | bytes 245768 | tf_op jit(solution)/shard_map/gather_image/ppermute | solution.py:22
  77.3 5.6 %collective-permute-done.14 = f32[32,640]{1,0:T(8,128)S(1)} collective-permute-done((f32[32,640]{1,0:T(8,128)S(1)}, f32[32,640]{1,0:T(8,128)S(1)}, u32[]{:S(2)}, u32[]{:S(2)}) %collective-permute-start.14) | collective-permute-done | bytes 81952 | tf_op jit(solution)/shard_map/gather_image/ppermute | solution.py:22
  83.0 2.2 %copy-done.2 = bf16[2048,1024]{1,0:T(8,128)(2,1)S(1)} copy-done((bf16[2048,1024]{1,0:T(8,128)(2,1)S(1)}, bf16[2048,1024]{1,0:T(8,128)(2,1)}, u32[]{:S(2)}) %copy-start.2) | copy-done | bytes 4194328
  85.2 1.9 %copy-done.4 = bf16[1536,1024]{1,0:T(8,128)(2,1)S(1)} copy-done((bf16[1536,1024]{1,0:T(8,128)(2,1)S(1)}, bf16[1536,1024]{1,0:T(8,128)(2,1)}, u32[]{:S(2)}) %copy-start.4) | copy-done | bytes 3145752
  87.1 1.9 %copy-done.6 = bf16[1536,1024]{1,0:T(8,128)(2,1)S(1)} copy-done((bf16[1536,1024]{1,0:T(8,128)(2,1)S(1)}, bf16[1536,1024]{1,0:T(8,128)(2,1)}, u32[]{:S(2)}) %copy-start.6) | copy-done | bytes 3145752
  89.0 1.9 %copy-done.8 = bf16[512,3072]{1,0:T(8,128)(2,1)S(1)} copy-done((bf16[512,3072]{1,0:T(8,128)(2,1)S(1)}, bf16[512,3072]{1,0:T(8,128)(2,1)}, u32[]{:S(2)}) %copy-start.8) | copy-done | bytes 3145752
  90.9 1.9 %copy-done.10 = bf16[1536,1024]{1,0:T(8,128)(2,1)S(1)} copy-done((bf16[1536,1024]{1,0:T(8,128)(2,1)S(1)}, bf16[1536,1024]{1,0:T(8,128)(2,1)}, u32[]{:S(2)}) %copy-start.10) | copy-done | bytes 3145752
  92.8 2.5 %second_product.1 = (f32[16,2176]{1,0:T(8,128)S(1)}, f32[16,2176]{1,0:T(8,128)S(1)}, f32[3,16,512]{2,1,0:T(8,128)S(1)}) custom-call(bf16[1536,1024]{1,0:T(8,128)(2,1)S(1)} %copy-done.4, bf16[1536,1024]{1,0:T(8,128)(2,1)S(1)} %copy-done.6, bf16[1536,1024]{1,0:T(8,128)(2,1)S(1)} %copy-done.10, bf16[512,3072]{1,0:T(8,128)(2,1)S(1)} %copy-done.8, ...), custom_call_target="tpu_custom_call" | custom-call | flops 4294967296 | bytes 1048576 | tf_op jit(solution)/shard_map/second_product/pallas_call | solution.py:181
  96.8 3.2 %collective-permute-start.18 = (f32[16,640]{1,0:T(8,128)S(1)}, f32[16,640]{1,0:T(8,128)S(1)}, u32[]{:S(2)}, u32[]{:S(2)}) collective-permute-start(f32[16,640]{1,0:T(8,128)S(1)} %get-tuple-element.81), channel_id=1, source_target_pairs={{0,96},{32,0},{64,32},{96,64},{1,97},{33,1},{65,33},{97,65},{2,98}... | collective-permute-start | bytes 122888 | tf_op jit(solution)/shard_map/sum_over_yc/ppermute | solution.py:22
  100.0 2.0 %collective-permute-done.19 = f32[16,640]{1,0:T(8,128)S(1)} collective-permute-done((f32[16,640]{1,0:T(8,128)S(1)}, f32[16,640]{1,0:T(8,128)S(1)}, u32[]{:S(2)}, u32[]{:S(2)}) %collective-permute-start.19) | collective-permute-done | bytes 40992 | tf_op jit(solution)/shard_map/sum_over_yc/ppermute | solution.py:22
  102.0 3.5 %collective-permute-done.20 = f32[16,640]{1,0:T(8,128)S(1)} collective-permute-done((f32[16,640]{1,0:T(8,128)S(1)}, f32[16,640]{1,0:T(8,128)S(1)}, u32[]{:S(2)}, u32[]{:S(2)}) %collective-permute-start.20) | collective-permute-done | bytes 40992 | tf_op jit(solution)/shard_map/sum_over_yc/ppermute | solution.py:22
  108.7 2.0 %collective-permute-done.23 = f32[16,128]{1,0:T(8,128)S(1)} collective-permute-done((f32[16,128]{1,0:T(8,128)S(1)}, f32[16,128]{1,0:T(8,128)S(1)}, u32[]{:S(2)}, u32[]{:S(2)}) %collective-permute-start.23) | collective-permute-done | bytes 8224 | tf_op jit(solution)/shard_map/sum_sums_over_z/ppermute | solution.py:22
  110.7 2.1 %collective-permute-done.21 = f32[16,128]{1,0:T(8,128)S(1)} collective-permute-done((f32[16,128]{1,0:T(8,128)S(1)}, f32[16,128]{1,0:T(8,128)S(1)}, u32[]{:S(2)}, u32[]{:S(2)}) %collective-permute-start.21) | collective-permute-done | bytes 8224 | tf_op jit(solution)/shard_map/sum_sums_over_z/ppermute | solution.py:22
  (101 shorter events, 19.2 us)
Async XLA Ops:
  1.8 6.1 %copy-start.11 = (bf16[512,256]{1,0:T(8,128)(2,1)}, bf16[512,256]{1,0:T(8,128)(2,1)S(1)}, u32[]{:S(2)}) copy-start(bf16[512,256]{1,0:T(8,128)(2,1)S(1)} %constant_dynamic-slice_fusion.points_ref.refs_0_) | copy-start | bytes 786436
  1.8 45.9 %collective-permute-start.7 = (bf16[512,256]{1,0:T(8,128)(2,1)S(1)}, bf16[512,256]{1,0:T(8,128)(2,1)S(1)}, u32[]{:S(2)}, u32[]{:S(2)}) collective-permute-start(bf16[512,256]{1,0:T(8,128)(2,1)S(1)} %constant_dynamic-slice_fusion.points_ref.refs_0_), channel_id=1, source_target_pairs={{0,16},{8,24},{16,0},{24,8},{1,17},{9,25},{17,1},{25,9},{2,18},{10... | collective-permute-start | bytes 786440 | tf_op jit(solution)/shard_map/fetch_points/ppermute | solution.py:22
  5.8 31.3 %collective-permute-start.1 = (bf16[512,256]{1,0:T(8,128)(2,1)S(1)}, bf16[512,256]{1,0:T(8,128)(2,1)S(1)}, u32[]{:S(2)}, u32[]{:S(2)}) collective-permute-start(bf16[512,256]{1,0:T(8,128)(2,1)S(1)} %constant_dynamic-slice_fusion.points_ref.refs_0_), channel_id=1, source_target_pairs={{0,24},{8,0},{16,8},{24,16},{1,25},{9,1},{17,9},{25,17},{2,26},{10... | collective-permute-start | bytes 786440 | tf_op jit(solution)/shard_map/fetch_points/ppermute | solution.py:22
  6.5 31.1 %collective-permute-start = (bf16[512,256]{1,0:T(8,128)(2,1)S(1)}, bf16[512,256]{1,0:T(8,128)(2,1)S(1)}, u32[]{:S(2)}, u32[]{:S(2)}) collective-permute-start(bf16[512,256]{1,0:T(8,128)(2,1)S(1)} %constant_dynamic-slice_fusion.points_ref.refs_0_), channel_id=1, source_target_pairs={{0,8},{8,16},{16,24},{24,0},{1,9},{9,17},{17,25},{25,1},{2,10},{10... | collective-permute-start | bytes 786440 | tf_op jit(solution)/shard_map/fetch_points/ppermute | solution.py:22
  9.7 10.0 %collective-permute-start.8 = (bf16[608,256]{1,0:T(8,128)(2,1)}, bf16[608,256]{1,0:T(8,128)(2,1)S(1)}, u32[]{:S(2)}, u32[]{:S(2)}) collective-permute-start(bf16[608,256]{1,0:T(8,128)(2,1)} %pack.1.refs_3_.refs_1_), channel_id=1, source_target_pairs={{0,64},{32,96},{64,0},{96,32},{1,65},{33,97},{65,1},{97,33},{2,66}... | collective-permute-start | bytes 933896 | tf_op jit(solution)/shard_map/fetch_points/ppermute | solution.py:22
  12.9 13.8 %collective-permute-start.4 = (bf16[608,256]{1,0:T(8,128)(2,1)}, bf16[608,256]{1,0:T(8,128)(2,1)S(1)}, u32[]{:S(2)}, u32[]{:S(2)}) collective-permute-start(bf16[608,256]{1,0:T(8,128)(2,1)} %pack.1.refs_3_.refs_1_), channel_id=1, source_target_pairs={{0,96},{32,0},{64,32},{96,64},{1,97},{33,1},{65,33},{97,65},{2,98}... | collective-permute-start | bytes 933896 | tf_op jit(solution)/shard_map/fetch_points/ppermute | solution.py:22
  19.7 8.3 %collective-permute-start.2 = (bf16[608,256]{1,0:T(8,128)(2,1)}, bf16[608,256]{1,0:T(8,128)(2,1)S(1)}, u32[]{:S(2)}, u32[]{:S(2)}) collective-permute-start(bf16[608,256]{1,0:T(8,128)(2,1)} %pack.1.refs_3_.refs_1_), channel_id=1, source_target_pairs={{0,4},{4,0},{1,5},{5,1},{2,6},{6,2},{3,7},{7,3},{8,12},{12,8},{9,1... | collective-permute-start | bytes 933896 | tf_op jit(solution)/shard_map/fetch_points/ppermute | solution.py:22
  26.7 10.4 %collective-permute-start.3 = (bf16[608,256]{1,0:T(8,128)(2,1)}, bf16[608,256]{1,0:T(8,128)(2,1)S(1)}, u32[]{:S(2)}, u32[]{:S(2)}) collective-permute-start(bf16[608,256]{1,0:T(8,128)(2,1)} %pack.1.refs_3_.refs_1_), channel_id=1, source_target_pairs={{0,32},{32,64},{64,96},{96,0},{1,33},{33,65},{65,97},{97,1},{2,34}... | collective-permute-start | bytes 933896 | tf_op jit(solution)/shard_map/fetch_points/ppermute | solution.py:22
  27.9 27.1 %collective-permute-start.9 = (bf16[608,256]{1,0:T(8,128)(2,1)S(1)}, bf16[608,256]{1,0:T(8,128)(2,1)S(1)}, u32[]{:S(2)}, u32[]{:S(2)}) collective-permute-start(bf16[608,256]{1,0:T(8,128)(2,1)S(1)} %collective-permute-done.8.refs_4_), channel_id=1, source_target_pairs={{0,4},{4,0},{1,5},{5,1},{2,6},{6,2},{3,7},{7,3},{8,12},{12,8},{9,1... | collective-permute-start | bytes 933896 | tf_op jit(solution)/shard_map/fetch_points/ppermute | solution.py:22
  37.1 10.6 %collective-permute-start.6 = (bf16[608,256]{1,0:T(8,128)(2,1)S(1)}, bf16[608,256]{1,0:T(8,128)(2,1)S(1)}, u32[]{:S(2)}, u32[]{:S(2)}) collective-permute-start(bf16[608,256]{1,0:T(8,128)(2,1)S(1)} %collective-permute-done.4.refs_4_), channel_id=1, source_target_pairs={{0,4},{4,0},{1,5},{5,1},{2,6},{6,2},{3,7},{7,3},{8,12},{12,8},{9,1... | collective-permute-start | bytes 933896 | tf_op jit(solution)/shard_map/fetch_points/ppermute | solution.py:22
  37.1 10.6 %collective-permute-start.5 = (bf16[608,256]{1,0:T(8,128)(2,1)S(1)}, bf16[608,256]{1,0:T(8,128)(2,1)S(1)}, u32[]{:S(2)}, u32[]{:S(2)}) collective-permute-start(bf16[608,256]{1,0:T(8,128)(2,1)S(1)} %collective-permute-done.3.refs_3_), channel_id=1, source_target_pairs={{0,4},{4,0},{1,5},{5,1},{2,6},{6,2},{3,7},{7,3},{8,12},{12,8},{9,1... | collective-permute-start | bytes 933896 | tf_op jit(solution)/shard_map/fetch_points/ppermute | solution.py:22
  44.0 3.7 %copy-start.15 = (bf16[608,256]{1,0:T(8,128)(2,1)S(1)}, bf16[608,256]{1,0:T(8,128)(2,1)}, u32[]{:S(2)}) copy-start(bf16[608,256]{1,0:T(8,128)(2,1)} %pack.1.refs_3_.refs_1_) | copy-start | bytes 933892
  47.7 3.9 %copy-start.13 = (bf16[512,256]{1,0:T(8,128)(2,1)S(1)}, bf16[512,256]{1,0:T(8,128)(2,1)}, u32[]{:S(2)}) copy-start(bf16[512,256]{1,0:T(8,128)(2,1)} %copy-done.11) | copy-start | bytes 786436
  55.1 17.6 %copy-start.17 = (f32[512,16]{0,1:T(8,128)S(1)}, f32[512,16]{0,1:T(8,128)}, u32[]{:S(2)}) copy-start(f32[512,16]{0,1:T(8,128)} %param.5) | copy-start | bytes 98308
  57.5 2.0 %copy-start.1 = (bf16[2048,1024]{1,0:T(8,128)(2,1)}, bf16[2048,1024]{1,0:T(8,128)(2,1)S(1)}, u32[]{:S(2)}) copy-start(bf16[2048,1024]{1,0:T(8,128)(2,1)S(1)} %get-tuple-element.27.refs_4_) | copy-start | bytes 12582916
  59.5 9.4 %collective-permute-start.12 = (f32[16,2560]{1,0:T(8,128)S(1)}, f32[16,2560]{1,0:T(8,128)S(1)}, u32[]{:S(2)}, u32[]{:S(2)}) collective-permute-start(f32[16,2560]{1,0:T(8,128)S(1)} %pad_maximum_fusion), channel_id=1, source_target_pairs={{0,24},{8,0},{16,8},{24,16},{1,25},{9,1},{17,9},{25,17},{2,26},{10... | collective-permute-start | bytes 491528 | tf_op jit(solution)/shard_map/sum_over_z/ppermute | solution.py:22
  61.5 8.6 %collective-permute-start.11 = (f32[16,2560]{1,0:T(8,128)S(1)}, f32[16,2560]{1,0:T(8,128)S(1)}, u32[]{:S(2)}, u32[]{:S(2)}) collective-permute-start(f32[16,2560]{1,0:T(8,128)S(1)} %pad_maximum_fusion), channel_id=1, source_target_pairs={{0,16},{8,24},{16,0},{24,8},{1,17},{9,25},{17,1},{25,9},{2,18},{10... | collective-permute-start | bytes 491528 | tf_op jit(solution)/shard_map/sum_over_z/ppermute | solution.py:22
  62.7 9.9 %collective-permute-start.10 = (f32[16,2560]{1,0:T(8,128)S(1)}, f32[16,2560]{1,0:T(8,128)S(1)}, u32[]{:S(2)}, u32[]{:S(2)}) collective-permute-start(f32[16,2560]{1,0:T(8,128)S(1)} %pad_maximum_fusion), channel_id=1, source_target_pairs={{0,8},{8,16},{16,24},{24,0},{1,9},{9,17},{17,25},{25,1},{2,10},{10... | collective-permute-start | bytes 491528 | tf_op jit(solution)/shard_map/sum_over_z/ppermute | solution.py:22
  73.0 1.3 %collective-permute-start.13 = (f32[16,640]{1,0:T(8,128)S(1)}, f32[16,640]{1,0:T(8,128)S(1)}, u32[]{:S(2)}, u32[]{:S(2)}) collective-permute-start(f32[16,640]{1,0:T(8,128)S(1)} %pad_maximum_fusion.6), channel_id=1, source_target_pairs={{0,4},{4,0},{1,5},{5,1},{2,6},{6,2},{3,7},{7,3},{8,12},{12,8},{9,1... | collective-permute-start | bytes 122888 | tf_op jit(solution)/shard_map/gather_image/ppermute | solution.py:22
  74.3 8.6 %collective-permute-start.16 = (f32[32,640]{1,0:T(8,128)S(1)}, f32[32,640]{1,0:T(8,128)S(1)}, u32[]{:S(2)}, u32[]{:S(2)}) collective-permute-start(f32[32,640]{1,0:T(8,128)S(1)} %pad_maximum_fusion.3), channel_id=1, source_target_pairs={{0,64},{32,96},{64,0},{96,32},{1,65},{33,97},{65,1},{97,33},{2,66}... | collective-permute-start | bytes 245768 | tf_op jit(solution)/shard_map/gather_image/ppermute | solution.py:22
  75.1 7.8 %collective-permute-start.15 = (f32[32,640]{1,0:T(8,128)S(1)}, f32[32,640]{1,0:T(8,128)S(1)}, u32[]{:S(2)}, u32[]{:S(2)}) collective-permute-start(f32[32,640]{1,0:T(8,128)S(1)} %pad_maximum_fusion.3), channel_id=1, source_target_pairs={{0,96},{32,0},{64,32},{96,64},{1,97},{33,1},{65,33},{97,65},{2,98}... | collective-permute-start | bytes 245768 | tf_op jit(solution)/shard_map/gather_image/ppermute | solution.py:22
  77.3 5.7 %collective-permute-start.14 = (f32[32,640]{1,0:T(8,128)S(1)}, f32[32,640]{1,0:T(8,128)S(1)}, u32[]{:S(2)}, u32[]{:S(2)}) collective-permute-start(f32[32,640]{1,0:T(8,128)S(1)} %pad_maximum_fusion.3), channel_id=1, source_target_pairs={{0,32},{32,64},{64,96},{96,0},{1,33},{33,65},{65,97},{97,1},{2,34}... | collective-permute-start | bytes 245768 | tf_op jit(solution)/shard_map/gather_image/ppermute | solution.py:22
  83.0 2.2 %copy-start.2 = (bf16[2048,1024]{1,0:T(8,128)(2,1)S(1)}, bf16[2048,1024]{1,0:T(8,128)(2,1)}, u32[]{:S(2)}) copy-start(bf16[2048,1024]{1,0:T(8,128)(2,1)} %copy-done.1) | copy-start | bytes 12582916
  85.2 1.9 %copy-start.4 = (bf16[1536,1024]{1,0:T(8,128)(2,1)S(1)}, bf16[1536,1024]{1,0:T(8,128)(2,1)}, u32[]{:S(2)}) copy-start(bf16[1536,1024]{1,0:T(8,128)(2,1)} %copy-done.3) | copy-start | bytes 9437188
  87.1 1.9 %copy-start.6 = (bf16[1536,1024]{1,0:T(8,128)(2,1)S(1)}, bf16[1536,1024]{1,0:T(8,128)(2,1)}, u32[]{:S(2)}) copy-start(bf16[1536,1024]{1,0:T(8,128)(2,1)} %copy-done.5) | copy-start | bytes 9437188
  95.2 1.4 %collective-permute-start.17 = (f32[16,2176]{1,0:T(8,128)S(1)}, f32[16,2176]{1,0:T(8,128)S(1)}, u32[]{:S(2)}, u32[]{:S(2)}) collective-permute-start(f32[16,2176]{1,0:T(8,128)S(1)} %get-tuple-element.31), channel_id=1, source_target_pairs={{0,4},{4,0},{1,5},{5,1},{2,6},{6,2},{3,7},{7,3},{8,12},{12,8},{9,1... | collective-permute-start | bytes 417800 | tf_op jit(solution)/shard_map/sum_over_yc/ppermute | solution.py:22
  96.7 5.3 %collective-permute-start.19 = (f32[16,640]{1,0:T(8,128)S(1)}, f32[16,640]{1,0:T(8,128)S(1)}, u32[]{:S(2)}, u32[]{:S(2)}) collective-permute-start(f32[16,640]{1,0:T(8,128)S(1)} %concatenate.104), channel_id=1, source_target_pairs={{0,32},{32,64},{64,96},{96,0},{1,33},{33,65},{65,97},{97,1},{2,34}... | collective-permute-start | bytes 122888 | tf_op jit(solution)/shard_map/sum_over_yc/ppermute | solution.py:22
  96.8 5.2 %collective-permute-start.18 = (f32[16,640]{1,0:T(8,128)S(1)}, f32[16,640]{1,0:T(8,128)S(1)}, u32[]{:S(2)}, u32[]{:S(2)}) collective-permute-start(f32[16,640]{1,0:T(8,128)S(1)} %get-tuple-element.81), channel_id=1, source_target_pairs={{0,96},{32,0},{64,32},{96,64},{1,97},{33,1},{65,33},{97,65},{2,98}... | collective-permute-start | bytes 122888 | tf_op jit(solution)/shard_map/sum_over_yc/ppermute | solution.py:22
  100.0 5.5 %collective-permute-start.20 = (f32[16,640]{1,0:T(8,128)S(1)}, f32[16,640]{1,0:T(8,128)S(1)}, u32[]{:S(2)}, u32[]{:S(2)}) collective-permute-start(f32[16,640]{1,0:T(8,128)S(1)} %get-tuple-element.82), channel_id=1, source_target_pairs={{0,64},{32,96},{64,0},{96,32},{1,65},{33,97},{65,1},{97,33},{2,66}... | collective-permute-start | bytes 122888 | tf_op jit(solution)/shard_map/sum_over_yc/ppermute | solution.py:22
  105.5 5.2 %collective-permute-start.23 = (f32[16,128]{1,0:T(8,128)S(1)}, f32[16,128]{1,0:T(8,128)S(1)}, u32[]{:S(2)}, u32[]{:S(2)}) collective-permute-start(f32[16,128]{1,0:T(8,128)S(1)} %slice_add_fusion.15), channel_id=1, source_target_pairs={{0,16},{8,24},{16,0},{24,8},{1,17},{9,25},{17,1},{25,9},{2,18},{10... | collective-permute-start | bytes 24584 | tf_op jit(solution)/shard_map/sum_sums_over_z/ppermute | solution.py:22
  106.7 4.0 %collective-permute-start.22 = (f32[16,128]{1,0:T(8,128)S(1)}, f32[16,128]{1,0:T(8,128)S(1)}, u32[]{:S(2)}, u32[]{:S(2)}) collective-permute-start(f32[16,128]{1,0:T(8,128)S(1)} %slice_add_fusion.15), channel_id=1, source_target_pairs={{0,24},{8,0},{16,8},{24,16},{1,25},{9,1},{17,9},{25,17},{2,26},{10... | collective-permute-start | bytes 24584 | tf_op jit(solution)/shard_map/sum_sums_over_z/ppermute | solution.py:22
  107.9 4.9 %collective-permute-start.21 = (f32[16,128]{1,0:T(8,128)S(1)}, f32[16,128]{1,0:T(8,128)S(1)}, u32[]{:S(2)}, u32[]{:S(2)}) collective-permute-start(f32[16,128]{1,0:T(8,128)S(1)} %slice_add_fusion.15), channel_id=1, source_target_pairs={{0,8},{8,16},{16,24},{24,0},{1,9},{9,17},{17,25},{25,1},{2,10},{10... | collective-permute-start | bytes 24584 | tf_op jit(solution)/shard_map/sum_sums_over_z/ppermute | solution.py:22
  (10 other events, 14.3 us)

commit v3 on v2

--- a/solution.py
+++ b/solution.py
@@ -22,26 +22,30 @@
     return lax.ppermute(value, axis, [(i, (i + step) % size) for i in range(size)])
 
 
-def split_rows(value):
-    high = value.astype(jnp.bfloat16).astype(jnp.float32)
-    middle = (value - high).astype(jnp.bfloat16).astype(jnp.float32)
-    return high, middle, value - high - middle
+def split(value):
+    high = value.astype(jnp.bfloat16)
+    rest = value - high.astype(jnp.float32)
+    middle = rest.astype(jnp.bfloat16)
+    return high, middle, (rest - middle.astype(jnp.float32)).astype(jnp.bfloat16)
 
 
 def pack_kernel(points_ref, side_ref, out_ref):
     own, width = points_ref.shape
     probes = side_ref.shape[0]
     out_ref[:own, :] = points_ref[...]
-    norms = jnp.sum(points_ref[...].astype(jnp.float32) ** 2, axis=1, keepdims=True)
-    norms = jnp.broadcast_to(norms, (own, LANES)).T[:16, :]
-    high, middle, low = split_rows(norms)
+    high, middle, _ = split(points_ref[...].astype(jnp.float32) ** 2)
+    ones = jnp.ones((probes, width), jnp.bfloat16)
+    norms = 0.0
+    for term in (high, middle):
+        norms = norms + lax.dot_general(ones, term, (((1,), (1,)), ((), ())), preferred_element_type=jnp.float32)
+    high, middle, low = split(norms)
     row = lax.broadcasted_iota(jnp.int32, norms.shape, 0)
-    norms = jnp.where(row == 0, high, jnp.where(row == 1, middle, jnp.where(row == 2, low, 0.0)))
-    high, middle, _ = split_rows(side_ref[...])
+    norms = jnp.where(row == 0, high.astype(jnp.float32), jnp.where(row == 1, middle.astype(jnp.float32), low.astype(jnp.float32)))
+    high, middle, _ = split(side_ref[...])
     at = own
-    for part in (high, middle, norms):
+    for part in (high, middle, norms.astype(jnp.bfloat16)):
         for j in range(own // width):
-            out_ref[at : at + probes, :] = part[:, j * width : (j + 1) * width].astype(jnp.bfloat16)
+            out_ref[at : at + probes, :] = part[:, j * width : (j + 1) * width]
             at += probes
 
 
@@ -51,8 +55,14 @@
     return pl.pallas_call(
         pack_kernel,
         out_shape=jax.ShapeDtypeStruct((own + extra, width), jnp.bfloat16),
+        compiler_params=pltpu.CompilerParams(vmem_limit_bytes=8 << 20),
         name="pack",
     )(points, side)
+
+
+def unpack_side(messages, probes, own):
+    terms = [jnp.concatenate([unpack_rows(one, probes, own, t) for one in messages], axis=1) for t in (0, 1)]
+    return terms[0].astype(jnp.float32) + terms[1].astype(jnp.float32)
 
 
 def unpack_rows(message, probes, own, term):
@@ -71,7 +81,7 @@
     prior_refs = [refs.pop(0) for _ in range(prior_count)]
     side_ref = refs.pop(0) if has_side else None
     tile_ref, image_ref = refs.pop(0), refs.pop(0)
-    own = row_refs[0].shape[0]
+    own = tile_ref.shape[0] // rows_count
     if known_halves:
         pieces = []
         for half_ref in half_refs:
@@ -81,7 +91,7 @@
         new_ref = refs.pop(0)
         halves = []
         for i, row_ref in enumerate(row_refs):
-            squares = row_ref[...].astype(jnp.float32) ** 2
+            squares = row_ref[:own, :].astype(jnp.float32) ** 2
             halves.append(-kernel_rate * jnp.sum(squares, axis=1, keepdims=True))
             new_ref[i * own : (i + 1) * own, :] = halves[-1]
     if prior_count:
@@ -111,8 +121,8 @@
                 )
 
 
-def build(rows, cols, probes, halves=(), prior=(), side=None):
-    own, features = rows[0].shape
+def build(rows, cols, own, probes, halves=(), prior=(), side=None):
+    features = rows[0].shape[1]
     height, width = len(rows) * own, len(cols) * own
     counts = (len(rows), len(cols), len(halves), len(prior), side is not None)
     out_shape = [
@@ -127,13 +137,47 @@
         out_shape=out_shape,
         compiler_params=pltpu.CompilerParams(vmem_limit_bytes=16 << 20),
         cost_estimate=pl.CostEstimate(
-            flops=2 * height * width * (features + 256), bytes_accessed=1 << 20, transcendentals=height * width
+            flops=height * width * features // 8, bytes_accessed=1 << 10, transcendentals=0
         ),
         name="build_tile",
     )(*args)
 
 
-def second_kernel(own, tiles, image_r, side_r, image_c, side_c, sums_ref, mine_ref, other_ref, own_ref):
+def combine_kernel(own, side_ref, *refs):
+    parts, (image_ref, message_ref) = refs[:NZ], refs[NZ:]
+    side = side_ref[...]
+    sums = [0.0, 0.0, 0.0]
+    for i, p in enumerate(ROWS):
+        piece = 0.0
+        for s in range(NZ):
+            at = ROWS.index((p - s) % NZ) * own
+            piece = piece + parts[s][:, at : at + own]
+        here = slice(i * own, (i + 1) * own)
+        image_ref[:, here] = piece
+        if i == 0:
+            message_ref[:, :own] = piece
+        known = side[:, here]
+        sums[0] = sums[0] + jnp.sum(known * known, axis=1, keepdims=True)
+        sums[1] = sums[1] + jnp.sum(known * piece, axis=1, keepdims=True)
+        sums[2] = sums[2] + jnp.sum(piece * piece, axis=1, keepdims=True)
+    lane = lax.broadcasted_iota(jnp.int32, (side.shape[0], LANES), 1)
+    message_ref[:, own:] = jnp.where(lane == 0, sums[0], jnp.where(lane == 1, sums[1], sums[2]))
+
+
+def combine(side_r, parts, own):
+    probes, rows = side_r.shape
+    return pl.pallas_call(
+        functools.partial(combine_kernel, own),
+        out_shape=[
+            jax.ShapeDtypeStruct((probes, rows), jnp.float32),
+            jax.ShapeDtypeStruct((probes, own + LANES), jnp.float32),
+        ],
+        compiler_params=pltpu.CompilerParams(vmem_limit_bytes=8 << 20),
+        name="combine",
+    )(side_r, *parts)
+
+
+def second_kernel(own, tiles, side_own, image_r, side_r, image_c, side_c, sums_ref, mine_ref, other_ref, own_ref):
     sums = sums_ref[...]
     rr, curve, square = sums[:, 0:1], sums[:, 1:2], sums[:, 2:3]
     alpha = rr / curve
@@ -157,10 +201,11 @@
         dir_c = (side_c[:, cols] - alpha * image_c[:, cols]) + beta * side_c[:, cols]
         total = total + jnp.sum(part * dir_c, axis=1, keepdims=True)
         (other_ref if h else mine_ref)[:, m * own : (m + 1) * own] = part
-    own_res, own_dir = res_r[:, :own], dir_r[:, :own]
+    own_res = side_own[...] - alpha * image_r[:, :own]
+    own_dir = own_res + beta * side_own[...]
     own_ref[0] = own_res
     own_ref[1] = own_dir
-    own_ref[2] = alpha * side_r[:, :own]
+    own_ref[2] = alpha * side_own[...]
     total = total + noise_level * jnp.sum(own_dir * own_dir, axis=1, keepdims=True)
     rr_own = jnp.sum(own_res * own_res, axis=1, keepdims=True)
     lane = lax.broadcasted_iota(jnp.int32, (total.shape[0], LANES), 1)
@@ -169,7 +214,7 @@
     other_ref[:, NY * own :] = out_sums
 
 
-def second_product(tiles, image_r, side_r, image_c, side_c, sums, own):
+def second_product(tiles, side, image_r, side_r, image_c, side_c, sums, own):
     probes, rows = side_r.shape
     cols = side_c.shape[1]
     places = [(top, left) for _, top, left in tiles]
@@ -180,16 +225,16 @@
 
     return pl.pallas_call(
         kernel,
-        in_specs=[pl.BlockSpec(memory_space=pltpu.VMEM)] * (len(tiles) + 5),
+        in_specs=[pl.BlockSpec(memory_space=pltpu.VMEM)] * (len(tiles) + 6),
         out_shape=[
             jax.ShapeDtypeStruct((probes, cols // NC + LANES), jnp.float32),
             jax.ShapeDtypeStruct((probes, cols // NC + LANES), jnp.float32),
             jax.ShapeDtypeStruct((3, probes, own), jnp.float32),
         ],
         compiler_params=pltpu.CompilerParams(vmem_limit_bytes=16 << 20),
-        cost_estimate=pl.CostEstimate(flops=2 * rows * cols * 256, bytes_accessed=1 << 20, transcendentals=0),
+        cost_estimate=pl.CostEstimate(flops=rows * cols * 32, bytes_accessed=1 << 10, transcendentals=0),
         name="second_product",
-    )(*[tile for tile, _, _ in tiles], image_r, side_r, image_c, side_c, sums)
+    )(*[tile for tile, _, _ in tiles], side, image_r, side_r, image_c, side_c, sums)
 
 
 def on_device(states, offsets, right_side):
@@ -197,57 +242,49 @@
     side = right_side.T
     points = lax.dynamic_slice_in_dim(states, offsets[0], own, 0)
     with jax.named_scope("fetch_points"):
-        row = {0: points}
-        for k in (1, 3, 2):
-            row[k] = shift(points, "z", NZ, k)
         message = pack(points, side)
-        col = {(0, 0): message, (1, 0): shift(message, "c", NC, 1)}
-        for m in (1, 3, 2):
-            col[0, m] = shift(message, "y", NY, m)
-        for m in (1, 3, 2):
-            col[1, m] = shift(col[0, m], "c", NC, 1)
+        middle = message.shape[0] // 2
+        row, col = {0: message}, {(0, 0): message}
+        for k in (1, 3):
+            col[0, k] = shift(message, "y", NY, k)
+            row[k] = shift(message, "z", NZ, k)
+        col[1, 0] = shift(message, "c", NC, 1)
+        far = []
+        for axis, size, ahead, behind in (("z", NZ, row[1], row[3]), ("y", NY, col[0, 1], col[0, 3])):
+            far.append((shift(ahead[:middle], axis, size, 1), shift(behind[middle:], axis, size, -1)))
+        for k in (1, 3):
+            col[1, k] = shift(col[0, k], "c", NC, 1)
         near = [row[k] for k in ROWS[:3]]
-        col = [col[at] for at in COLS]
 
     with jax.named_scope("build_tiles"):
-        tile_a, image, half = build(near, col[:2], probes, side=side)
-        tile_b, image = build(near, col[2:4], probes, [half], [image])
-        tile_c, image = build(near, col[4:6], probes, [half], [image])
-        tile_d, image_far, half_far = build([row[2]], col[:6], probes)
-        tile_e, image = build(near + [row[2]], col[6:], probes, [half, half_far], [image, image_far])
-        far = 3 * own
+        at = [col[k] for k in COLS[:6]]
+        tile_a, image, half = build(near, at[:2], own, probes, side=side)
+        tile_b, image = build(near, at[2:4], own, probes, [half], [image])
+        tile_c, image = build(near, at[4:6], own, probes, [half], [image])
+        far, image = lax.optimization_barrier((far, image))
+        row[2] = jnp.concatenate(far[0], axis=0)
+        col[0, 2] = jnp.concatenate(far[1], axis=0)
+        col[1, 2] = shift(col[0, 2], "c", NC, 1)
+        tile_d, image_far, half_far = build([row[2]], at, own, probes)
+        at = [col[0, 2], col[1, 2]]
+        tile_e, image = build(near + [row[2]], at, own, probes, [half, half_far], [image, image_far])
         tiles = [
             (tile_a, 0, 0),
             (tile_b, 0, 2 * own),
             (tile_c, 0, 4 * own),
-            (tile_d, far, 0),
+            (tile_d, 3 * own, 0),
             (tile_e, 0, 6 * own),
         ]
-        side_c = [unpack_rows(one, probes, own, 0) + unpack_rows(one, probes, own, 1).astype(jnp.float32) for one in col]
-        side_c = jnp.concatenate(side_c, axis=1)
+        side_c = unpack_side([col[at] for at in COLS], probes, own)
+        side_r = unpack_side([row[k] for k in ROWS], probes, own)
 
     with jax.named_scope("sum_over_z"):
-        message = jnp.concatenate([image, side], axis=1)
-        every = {0: message}
+        parts = [image] + [None] * (NZ - 1)
         for s in (1, 3, 2):
-            every[s] = shift(message, "z", NZ, s)
-        pieces = []
-        for p in ROWS:
-            piece = 0.0
-            for s in range(NZ):
-                at = ROWS.index((p - s) % NZ) * own
-                piece = piece + every[s][:, at : at + own]
-            pieces.append(piece)
-        image_r = jnp.concatenate(pieces, axis=1)
-        side_r = jnp.concatenate([every[p][:, NZ * own :] for p in ROWS], axis=1)
-        sums = jnp.stack(
-            [jnp.sum(side_r * side_r, axis=1), jnp.sum(side_r * image_r, axis=1), jnp.sum(image_r * image_r, axis=1)],
-            axis=1,
-        )
-        sums = jnp.pad(sums, ((0, 0), (0, LANES - 3)))
+            parts[s] = shift(image, "z", NZ, s)
+        image_r, message = combine(side_r, parts, own)
 
     with jax.named_scope("gather_image"):
-        message = jnp.concatenate([image_r[:, :own], sums], axis=1)
         pair = jnp.concatenate([message, shift(message, "c", NC, 1)], axis=0)
         every = {0: pair}
         for m in (1, 3, 2):
@@ -255,7 +292,7 @@
         image_c = jnp.concatenate([every[m][h * probes : (h + 1) * probes, :own] for h, m in COLS], axis=1)
         sums = sum(every[m][h * probes : (h + 1) * probes, own:] for h, m in COLS)
 
-    mine, other, held = second_product(tiles, image_r, side_r, image_c, side_c, sums, own)
+    mine, other, held = second_product(tiles, side, image_r, side_r, image_c, side_c, sums, own)
 
     with jax.named_scope("sum_over_yc"):
         mine = mine + shift(other, "c", NC, 1)

time: 114 us -> 80.2 us (0.70)
  local copies, waits for them, and re-layouts: 22.6 us -> 2.16 us
  waiting for transfers between devices: 48.7 us -> 33.2 us
  starting transfers between devices: 24.8 us -> 28.6 us
  Pallas kernels: 14.7 us -> 13.2 us
    unnamed x42 -> x38, local copies, waits for them, and re-layouts: 21.6 us -> 1.99 us
    ppermute x24 -> x26, waiting for transfers between devices: 48.7 us -> 33.2 us  [shift(): lax.ppermute(value, axis, [(i, (i + step) % size) for i in range(size)])]
    ppermute x24 -> x26, starting transfers between devices: 24.8 us -> 28.6 us  [shift(): lax.ppermute(value, axis, [(i, (i + step) % size) for i in range(size)])]
    pallas_call x1, Pallas kernels: 1.88 us -> 0.28 us  [pack(): pl.pallas_call(pack_kernel, out_shape=jax.ShapeDtypeStruct((own + extra,...]
  transfers between devices with their start and end apart: 24 -> 26, of which waited for: 13 -> 13; matrix products, arithmetic and copies ran while one was open for 1% -> 0% of each run, Pallas kernels for 9% -> 10%
where the time goes in v3:
time: 80.2 us; the launch traced here: 79.9 us
  waiting for transfers between devices  33.2 us (41%)
  starting transfers between devices  28.6 us (36%)
  Pallas kernels  13.2 us (16%)
  local copies, waits for them, and re-layouts  2.16 us (3%)
  between operations  1.76 us (2%)
  other arithmetic  1 us (1%)
    ppermute x26, waiting for transfers between devices, shift(): lax.ppermute(value, axis, [(i, (i + step) % size) for i in range(size)])  33.2 us
    ppermute x26, starting transfers between devices, shift(): lax.ppermute(value, axis, [(i, (i + step) % size) for i in range(size)])  28.6 us
    pallas_call x5, Pallas kernels, build(): pl.pallas_call(functools.partial(tile_kernel, counts, probes), out_shape=...  10.3 us
    pallas_call x1, Pallas kernels, second_product(): pl.pallas_call(kernel, in_specs=[pl.BlockSpec(memory_space=pltpu.VMEM)] *...  2.49 us
    unnamed x38, local copies, waits for them, and re-layouts  1.99 us
  transfers between devices with their start and end apart: 26, of which 13 were waited for; matrix products, arithmetic and copies ran while one was open for 0% of the time, Pallas kernels for 10%

profile of v3, /device:TPU:0, one launch (start us, length us, event | category | flops | bytes accessed | tf_op | source)
XLA Modules:
  0.0 79.9 jit_solution(7309899675947962836)
XLA Ops:
  2.8 3.2 %collective-permute-start.4 = (bf16[608,256]{1,0:T(8,128)(2,1)S(1)}, bf16[608,256]{1,0:T(8,128)(2,1)S(1)}, u32[]{:S(2)}, u32[]{:S(2)}) collective-permute-start(bf16[608,256]{1,0:T(8,128)(2,1)S(1)} %pack.1.refs_0_.refs_3_.refs_1_), channel_id=1, source_target_pairs={{0,96},{32,0},{64,32},{96,64},{1,97},{33,1},{65,33},{97,65},{2,98}... | collective-permute-start | bytes 933896 | tf_op jit(solution)/shard_map/fetch_points/ppermute | solution.py:22
  6.0 4.0 %collective-permute-start.1 = (bf16[608,256]{1,0:T(8,128)(2,1)S(1)}, bf16[608,256]{1,0:T(8,128)(2,1)S(1)}, u32[]{:S(2)}, u32[]{:S(2)}) collective-permute-start(bf16[608,256]{1,0:T(8,128)(2,1)S(1)} %pack.1.refs_0_.refs_3_.refs_1_), channel_id=1, source_target_pairs={{0,24},{8,0},{16,8},{24,16},{1,25},{9,1},{17,9},{25,17},{2,26},{10... | collective-permute-start | bytes 933896 | tf_op jit(solution)/shard_map/fetch_points/ppermute | solution.py:22
  10.0 2.5 %collective-permute-done.4.refs_4_ = bf16[608,256]{1,0:T(8,128)(2,1)S(1)} collective-permute-done((bf16[608,256]{1,0:T(8,128)(2,1)S(1)}, bf16[608,256]{1,0:T(8,128)(2,1)S(1)}, u32[]{:S(2)}, u32[]{:S(2)}) %collective-permute-start.4) | collective-permute-done | bytes 311328 | tf_op jit(solution)/shard_map/fetch_points/ppermute | solution.py:22
  12.6 3.8 %collective-permute-start.10 = (bf16[304,256]{1,0:T(8,128)(2,1)S(1)}, bf16[304,256]{1,0:T(8,128)(2,1)S(1)}, u32[]{:S(2)}, u32[]{:S(2)}) collective-permute-start(bf16[304,256]{1,0:T(8,128)(2,1)S(1)} %slice.325), channel_id=1, source_target_pairs={{0,96},{32,0},{64,32},{96,64},{1,97},{33,1},{65,33},{97,65},{2,98}... | collective-permute-start | bytes 466952 | tf_op jit(solution)/shard_map/fetch_points/ppermute | solution.py:22
  16.5 0.8 %collective-permute-done.1.refs_2_ = bf16[608,256]{1,0:T(8,128)(2,1)S(1)} collective-permute-done((bf16[608,256]{1,0:T(8,128)(2,1)S(1)}, bf16[608,256]{1,0:T(8,128)(2,1)S(1)}, u32[]{:S(2)}, u32[]{:S(2)}) %collective-permute-start.1) | collective-permute-done | bytes 311328 | tf_op jit(solution)/shard_map/fetch_points/ppermute | solution.py:22
  17.3 3.8 %collective-permute-start.8 = (bf16[304,256]{1,0:T(8,128)(2,1)S(1)}, bf16[304,256]{1,0:T(8,128)(2,1)S(1)}, u32[]{:S(2)}, u32[]{:S(2)}) collective-permute-start(bf16[304,256]{1,0:T(8,128)(2,1)S(1)} %slice.323), channel_id=1, source_target_pairs={{0,24},{8,0},{16,8},{24,16},{1,25},{9,1},{17,9},{25,17},{2,26},{10... | collective-permute-start | bytes 466952 | tf_op jit(solution)/shard_map/fetch_points/ppermute | solution.py:22
  22.5 2.0 %build_tile.5 = (bf16[1536,1024]{1,0:T(8,128)(2,1)S(1)}, f32[16,1536]{1,0:T(8,128)S(1)}, f32[1536,1]{1,0:T(8,128)S(1)}) custom-call(bf16[608,256]{1,0:T(8,128)(2,1)S(1)} %pack.1.refs_0_.refs_3_.refs_1_, bf16[608,256]{1,0:T(8,128)(2,1)S(1)} %collective-permute-done.refs_1_, bf16[608,256]{1,0:T(8,128)(2,1)S(1)} %collective-permute-done.1.refs_2_, ...), custom_call_target="tpu_custom_call" | custom-call | flops 50331648 | bytes 1024 | tf_op jit(solution)/shard_map/build_tiles/build_tile/pallas_call | solution.py:135
  24.5 1.9 %build_tile.6 = (bf16[1536,1024]{1,0:T(8,128)(2,1)S(1)}, f32[16,1536]{1,0:T(8,128)S(1)}) custom-call(bf16[608,256]{1,0:T(8,128)(2,1)S(1)} %pack.1.refs_0_.refs_3_.refs_1_, bf16[608,256]{1,0:T(8,128)(2,1)S(1)} %collective-permute-done.refs_1_, bf16[608,256]{1,0:T(8,128)(2,1)S(1)} %collective-permute-done.1.refs_2_, ...), custom_call_target="tpu_custom_call" | custom-call | flops 50331648 | bytes 1024 | tf_op jit(solution)/shard_map/build_tiles/build_tile/pallas_call | solution.py:135
  26.5 1.9 %build_tile.7 = (bf16[1536,1024]{1,0:T(8,128)(2,1)S(1)}, f32[16,1536]{1,0:T(8,128)S(1)}) custom-call(bf16[608,256]{1,0:T(8,128)(2,1)S(1)} %pack.1.refs_0_.refs_3_.refs_1_, bf16[608,256]{1,0:T(8,128)(2,1)S(1)} %collective-permute-done.refs_1_, bf16[608,256]{1,0:T(8,128)(2,1)S(1)} %collective-permute-done.1.refs_2_, ...), custom_call_target="tpu_custom_call" | custom-call | flops 50331648 | bytes 1024 | tf_op jit(solution)/shard_map/build_tiles/build_tile/pallas_call | solution.py:135
  28.5 5.2 %collective-permute-done.7 = bf16[304,256]{1,0:T(8,128)(2,1)S(1)} collective-permute-done((bf16[304,256]{1,0:T(8,128)(2,1)S(1)}, bf16[304,256]{1,0:T(8,128)(2,1)S(1)}, u32[]{:S(2)}, u32[]{:S(2)}) %collective-permute-start.7) | collective-permute-done | bytes 155680 | tf_op jit(solution)/shard_map/fetch_points/ppermute | solution.py:22
  34.1 2.0 %build_tile.8 = (bf16[512,3072]{1,0:T(8,128)(2,1)S(1)}, f32[16,512]{1,0:T(8,128)S(1)}, f32[512,1]{1,0:T(8,128)S(1)}) custom-call(bf16[608,256]{1,0:T(8,128)(2,1)S(1)} %constant_dynamic-update-slice_fusion.refs_0_.refs_3_, bf16[608,256]{1,0:T(8,128)(2,1)S(1)} %pack.1.refs_0_.refs_3_.refs_1_, bf16[608,256]{1,0:T(8,128)(2,1)S(1)} %collective-permute-done.2.refs_4_.refs_2_, ...), custom_call_target="tpu_custom_call" | custom-call | flops 50331648 | bytes 1024 | tf_op jit(solution)/shard_map/build_tiles/build_tile/pallas_call | solution.py:135
  36.2 2.5 %build_tile.9 = (bf16[2048,1024]{1,0:T(8,128)(2,1)S(1)}, f32[16,2048]{1,0:T(8,128)S(1)}) custom-call(bf16[608,256]{1,0:T(8,128)(2,1)S(1)} %pack.1.refs_0_.refs_3_.refs_1_, bf16[608,256]{1,0:T(8,128)(2,1)S(1)} %collective-permute-done.refs_1_, bf16[608,256]{1,0:T(8,128)(2,1)S(1)} %collective-permute-done.1.refs_2_, ...), custom_call_target="tpu_custom_call" | custom-call | flops 67108864 | bytes 1024 | tf_op jit(solution)/shard_map/build_tiles/build_tile/pallas_call | solution.py:135
  38.7 1.1 %collective-permute-start.13 = (f32[16,2048]{1,0:T(8,128)S(1)}, f32[16,2048]{1,0:T(8,128)S(1)}, u32[]{:S(2)}, u32[]{:S(2)}) collective-permute-start(f32[16,2048]{1,0:T(8,128)S(1)} %get-tuple-element.40.refs_0_), channel_id=1, source_target_pairs={{0,16},{8,24},{16,0},{24,8},{1,17},{9,25},{17,1},{25,9},{2,18},{10... | collective-permute-start | bytes 393224 | tf_op jit(solution)/shard_map/sum_over_z/ppermute | solution.py:22
  39.8 0.9 %collective-permute-start.12 = (f32[16,2048]{1,0:T(8,128)S(1)}, f32[16,2048]{1,0:T(8,128)S(1)}, u32[]{:S(2)}, u32[]{:S(2)}) collective-permute-start(f32[16,2048]{1,0:T(8,128)S(1)} %get-tuple-element.40.refs_0_), channel_id=1, source_target_pairs={{0,8},{8,16},{16,24},{24,0},{1,9},{9,17},{17,25},{25,1},{2,10},{10... | collective-permute-start | bytes 393224 | tf_op jit(solution)/shard_map/sum_over_z/ppermute | solution.py:22
  40.7 4.2 %collective-permute-done.14.refs_3_ = f32[16,2048]{1,0:T(8,128)S(1)} collective-permute-done((f32[16,2048]{1,0:T(8,128)S(1)}, f32[16,2048]{1,0:T(8,128)S(1)}, u32[]{:S(2)}, u32[]{:S(2)}) %collective-permute-start.14) | collective-permute-done | bytes 131104 | tf_op jit(solution)/shard_map/sum_over_z/ppermute | solution.py:22
  45.0 1.6 %collective-permute-done.13.refs_2_ = f32[16,2048]{1,0:T(8,128)S(1)} collective-permute-done((f32[16,2048]{1,0:T(8,128)S(1)}, f32[16,2048]{1,0:T(8,128)S(1)}, u32[]{:S(2)}, u32[]{:S(2)}) %collective-permute-start.13) | collective-permute-done | bytes 131104 | tf_op jit(solution)/shard_map/sum_over_z/ppermute | solution.py:22
  46.6 2.4 %collective-permute-done.12.refs_1_ = f32[16,2048]{1,0:T(8,128)S(1)} collective-permute-done((f32[16,2048]{1,0:T(8,128)S(1)}, f32[16,2048]{1,0:T(8,128)S(1)}, u32[]{:S(2)}, u32[]{:S(2)}) %collective-permute-start.12) | collective-permute-done | bytes 131104 | tf_op jit(solution)/shard_map/sum_over_z/ppermute | solution.py:22
  49.2 1.2 %collective-permute-done.15 = f32[16,640]{1,0:T(8,128)S(1)} collective-permute-done((f32[16,640]{1,0:T(8,128)S(1)}, f32[16,640]{1,0:T(8,128)S(1)}, u32[]{:S(2)}, u32[]{:S(2)}) %collective-permute-start.15) | collective-permute-done | bytes 40992 | tf_op jit(solution)/shard_map/gather_image/ppermute | solution.py:22
  50.4 2.2 %collective-permute-start.18 = (f32[32,640]{1,0:T(8,128)S(1)}, f32[32,640]{1,0:T(8,128)S(1)}, u32[]{:S(2)}, u32[]{:S(2)}) collective-permute-start(f32[32,640]{1,0:T(8,128)S(1)} %constant_dynamic-update-slice_fusion.20), channel_id=1, source_target_pairs={{0,64},{32,96},{64,0},{96,32},{1,65},{33,97},{65,1},{97,33},{2,66}... | collective-permute-start | bytes 245768 | tf_op jit(solution)/shard_map/gather_image/ppermute | solution.py:22
  52.6 1.1 %collective-permute-start.17 = (f32[32,640]{1,0:T(8,128)S(1)}, f32[32,640]{1,0:T(8,128)S(1)}, u32[]{:S(2)}, u32[]{:S(2)}) collective-permute-start(f32[32,640]{1,0:T(8,128)S(1)} %constant_dynamic-update-slice_fusion.20), channel_id=1, source_target_pairs={{0,96},{32,0},{64,32},{96,64},{1,97},{33,1},{65,33},{97,65},{2,98}... | collective-permute-start | bytes 245768 | tf_op jit(solution)/shard_map/gather_image/ppermute | solution.py:22
  53.7 0.9 %collective-permute-start.16 = (f32[32,640]{1,0:T(8,128)S(1)}, f32[32,640]{1,0:T(8,128)S(1)}, u32[]{:S(2)}, u32[]{:S(2)}) collective-permute-start(f32[32,640]{1,0:T(8,128)S(1)} %constant_dynamic-update-slice_fusion.20), channel_id=1, source_target_pairs={{0,32},{32,64},{64,96},{96,0},{1,33},{33,65},{65,97},{97,1},{2,34}... | collective-permute-start | bytes 245768 | tf_op jit(solution)/shard_map/gather_image/ppermute | solution.py:22
  54.6 4.7 %collective-permute-done.16 = f32[32,640]{1,0:T(8,128)S(1)} collective-permute-done((f32[32,640]{1,0:T(8,128)S(1)}, f32[32,640]{1,0:T(8,128)S(1)}, u32[]{:S(2)}, u32[]{:S(2)}) %collective-permute-start.16) | collective-permute-done | bytes 81952 | tf_op jit(solution)/shard_map/gather_image/ppermute | solution.py:22
  59.5 2.5 %second_product.1 = (f32[16,2176]{1,0:T(8,128)S(1)}, f32[16,2176]{1,0:T(8,128)S(1)}, f32[3,16,512]{2,1,0:T(8,128)S(1)}) custom-call(bf16[1536,1024]{1,0:T(8,128)(2,1)S(1)} %get-tuple-element.24.refs_0_, bf16[1536,1024]{1,0:T(8,128)(2,1)S(1)} %get-tuple-element.27.refs_1_, bf16[1536,1024]{1,0:T(8,128)(2,1)S(1)} %get-tuple-element.29.refs_2_, ...), custom_call_target="tpu_custom_call" | custom-call | flops 268435456 | bytes 1024 | tf_op jit(solution)/shard_map/second_product/pallas_call | solution.py:226
  62.0 1.3 %collective-permute-done.19 = f32[16,2176]{1,0:T(8,128)S(1)} collective-permute-done((f32[16,2176]{1,0:T(8,128)S(1)}, f32[16,2176]{1,0:T(8,128)S(1)}, u32[]{:S(2)}, u32[]{:S(2)}) %collective-permute-start.19) | collective-permute-done | bytes 139296 | tf_op jit(solution)/shard_map/sum_over_yc/ppermute | solution.py:22
  63.5 3.2 %collective-permute-start.20 = (f32[16,640]{1,0:T(8,128)S(1)}, f32[16,640]{1,0:T(8,128)S(1)}, u32[]{:S(2)}, u32[]{:S(2)}) collective-permute-start(f32[16,640]{1,0:T(8,128)S(1)} %get-tuple-element.97), channel_id=1, source_target_pairs={{0,96},{32,0},{64,32},{96,64},{1,97},{33,1},{65,33},{97,65},{2,98}... | collective-permute-start | bytes 122888 | tf_op jit(solution)/shard_map/sum_over_yc/ppermute | solution.py:22
  67.1 1.5 %collective-permute-done.21 = f32[16,640]{1,0:T(8,128)S(1)} collective-permute-done((f32[16,640]{1,0:T(8,128)S(1)}, f32[16,640]{1,0:T(8,128)S(1)}, u32[]{:S(2)}, u32[]{:S(2)}) %collective-permute-start.21) | collective-permute-done | bytes 40992 | tf_op jit(solution)/shard_map/sum_over_yc/ppermute | solution.py:22
  68.7 3.5 %collective-permute-done.22 = f32[16,640]{1,0:T(8,128)S(1)} collective-permute-done((f32[16,640]{1,0:T(8,128)S(1)}, f32[16,640]{1,0:T(8,128)S(1)}, u32[]{:S(2)}, u32[]{:S(2)}) %collective-permute-start.22) | collective-permute-done | bytes 40992 | tf_op jit(solution)/shard_map/sum_over_yc/ppermute | solution.py:22
  72.2 0.8 collective-permute-start.25
  73.0 1.2 %collective-permute-start.24 = (f32[16,128]{1,0:T(8,128)S(1)}, f32[16,128]{1,0:T(8,128)S(1)}, u32[]{:S(2)}, u32[]{:S(2)}) collective-permute-start(f32[16,128]{1,0:T(8,128)S(1)} %slice_add_fusion.3), channel_id=1, source_target_pairs={{0,24},{8,0},{16,8},{24,16},{1,25},{9,1},{17,9},{25,17},{2,26},{10... | collective-permute-start | bytes 24584 | tf_op jit(solution)/shard_map/sum_sums_over_z/ppermute | solution.py:22
  74.2 0.9 %collective-permute-start.23 = (f32[16,128]{1,0:T(8,128)S(1)}, f32[16,128]{1,0:T(8,128)S(1)}, u32[]{:S(2)}, u32[]{:S(2)}) collective-permute-start(f32[16,128]{1,0:T(8,128)S(1)} %slice_add_fusion.3), channel_id=1, source_target_pairs={{0,8},{8,16},{16,24},{24,0},{1,9},{9,17},{17,25},{25,1},{2,10},{10... | collective-permute-start | bytes 24584 | tf_op jit(solution)/shard_map/sum_sums_over_z/ppermute | solution.py:22
  75.0 2.4 %collective-permute-done.25 = f32[16,128]{1,0:T(8,128)S(1)} collective-permute-done((f32[16,128]{1,0:T(8,128)S(1)}, f32[16,128]{1,0:T(8,128)S(1)}, u32[]{:S(2)}, u32[]{:S(2)}) %collective-permute-start.25) | collective-permute-done | bytes 8224 | tf_op jit(solution)/shard_map/sum_sums_over_z/ppermute | solution.py:22
  77.4 1.6 %collective-permute-done.23 = f32[16,128]{1,0:T(8,128)S(1)} collective-permute-done((f32[16,128]{1,0:T(8,128)S(1)}, f32[16,128]{1,0:T(8,128)S(1)}, u32[]{:S(2)}, u32[]{:S(2)}) %collective-permute-start.23) | collective-permute-done | bytes 8224 | tf_op jit(solution)/shard_map/sum_sums_over_z/ppermute | solution.py:22
  (89 shorter events, 5.2 us)
Async XLA Ops:
  0.6 1.1 %copy-start = (bf16[1024,256]{1,0:T(8,128)(2,1)S(1)}, bf16[1024,256]{1,0:T(8,128)(2,1)}, u32[]{:S(2)}) copy-start(bf16[1024,256]{1,0:T(8,128)(2,1)} %param.3) | copy-start | bytes 1572868
  1.8 0.8 copy-start.1
  2.8 9.8 %collective-permute-start.4 = (bf16[608,256]{1,0:T(8,128)(2,1)S(1)}, bf16[608,256]{1,0:T(8,128)(2,1)S(1)}, u32[]{:S(2)}, u32[]{:S(2)}) collective-permute-start(bf16[608,256]{1,0:T(8,128)(2,1)S(1)} %pack.1.refs_0_.refs_3_.refs_1_), channel_id=1, source_target_pairs={{0,96},{32,0},{64,32},{96,64},{1,97},{33,1},{65,33},{97,65},{2,98}... | collective-permute-start | bytes 933896 | tf_op jit(solution)/shard_map/fetch_points/ppermute | solution.py:22
  6.0 10.4 %collective-permute-start.3 = (bf16[608,256]{1,0:T(8,128)(2,1)S(1)}, bf16[608,256]{1,0:T(8,128)(2,1)S(1)}, u32[]{:S(2)}, u32[]{:S(2)}) collective-permute-start(bf16[608,256]{1,0:T(8,128)(2,1)S(1)} %pack.1.refs_0_.refs_3_.refs_1_), channel_id=1, source_target_pairs={{0,32},{32,64},{64,96},{96,0},{1,33},{33,65},{65,97},{97,1},{2,34}... | collective-permute-start | bytes 933896 | tf_op jit(solution)/shard_map/fetch_points/ppermute | solution.py:22
  6.0 15.1 %collective-permute-start.2 = (bf16[608,256]{1,0:T(8,128)(2,1)S(1)}, bf16[608,256]{1,0:T(8,128)(2,1)S(1)}, u32[]{:S(2)}, u32[]{:S(2)}) collective-permute-start(bf16[608,256]{1,0:T(8,128)(2,1)S(1)} %pack.1.refs_0_.refs_3_.refs_1_), channel_id=1, source_target_pairs={{0,4},{4,0},{1,5},{5,1},{2,6},{6,2},{3,7},{7,3},{8,12},{12,8},{9,1... | collective-permute-start | bytes 933896 | tf_op jit(solution)/shard_map/fetch_points/ppermute | solution.py:22
  6.0 11.3 %collective-permute-start.1 = (bf16[608,256]{1,0:T(8,128)(2,1)S(1)}, bf16[608,256]{1,0:T(8,128)(2,1)S(1)}, u32[]{:S(2)}, u32[]{:S(2)}) collective-permute-start(bf16[608,256]{1,0:T(8,128)(2,1)S(1)} %pack.1.refs_0_.refs_3_.refs_1_), channel_id=1, source_target_pairs={{0,24},{8,0},{16,8},{24,16},{1,25},{9,1},{17,9},{25,17},{2,26},{10... | collective-permute-start | bytes 933896 | tf_op jit(solution)/shard_map/fetch_points/ppermute | solution.py:22
  10.0 11.1 %collective-permute-start = (bf16[608,256]{1,0:T(8,128)(2,1)S(1)}, bf16[608,256]{1,0:T(8,128)(2,1)S(1)}, u32[]{:S(2)}, u32[]{:S(2)}) collective-permute-start(bf16[608,256]{1,0:T(8,128)(2,1)S(1)} %pack.1.refs_0_.refs_3_.refs_1_), channel_id=1, source_target_pairs={{0,8},{8,16},{16,24},{24,0},{1,9},{9,17},{17,25},{25,1},{2,10},{10... | collective-permute-start | bytes 933896 | tf_op jit(solution)/shard_map/fetch_points/ppermute | solution.py:22
  12.6 15.8 %collective-permute-start.10 = (bf16[304,256]{1,0:T(8,128)(2,1)S(1)}, bf16[304,256]{1,0:T(8,128)(2,1)S(1)}, u32[]{:S(2)}, u32[]{:S(2)}) collective-permute-start(bf16[304,256]{1,0:T(8,128)(2,1)S(1)} %slice.325), channel_id=1, source_target_pairs={{0,96},{32,0},{64,32},{96,64},{1,97},{33,1},{65,33},{97,65},{2,98}... | collective-permute-start | bytes 466952 | tf_op jit(solution)/shard_map/fetch_points/ppermute | solution.py:22
  16.4 12.1 %collective-permute-start.9 = (bf16[304,256]{1,0:T(8,128)(2,1)S(1)}, bf16[304,256]{1,0:T(8,128)(2,1)S(1)}, u32[]{:S(2)}, u32[]{:S(2)}) collective-permute-start(bf16[304,256]{1,0:T(8,128)(2,1)S(1)} %slice.324), channel_id=1, source_target_pairs={{0,32},{32,64},{64,96},{96,0},{1,33},{33,65},{65,97},{97,1},{2,34}... | collective-permute-start | bytes 466952 | tf_op jit(solution)/shard_map/fetch_points/ppermute | solution.py:22
  17.3 11.1 %collective-permute-start.8 = (bf16[304,256]{1,0:T(8,128)(2,1)S(1)}, bf16[304,256]{1,0:T(8,128)(2,1)S(1)}, u32[]{:S(2)}, u32[]{:S(2)}) collective-permute-start(bf16[304,256]{1,0:T(8,128)(2,1)S(1)} %slice.323), channel_id=1, source_target_pairs={{0,24},{8,0},{16,8},{24,16},{1,25},{9,1},{17,9},{25,17},{2,26},{10... | collective-permute-start | bytes 466952 | tf_op jit(solution)/shard_map/fetch_points/ppermute | solution.py:22
  21.1 5.4 %collective-permute-start.6 = (bf16[608,256]{1,0:T(8,128)(2,1)S(1)}, bf16[608,256]{1,0:T(8,128)(2,1)S(1)}, u32[]{:S(2)}, u32[]{:S(2)}) collective-permute-start(bf16[608,256]{1,0:T(8,128)(2,1)S(1)} %collective-permute-done.4.refs_4_), channel_id=1, source_target_pairs={{0,4},{4,0},{1,5},{5,1},{2,6},{6,2},{3,7},{7,3},{8,12},{12,8},{9,1... | collective-permute-start | bytes 933896 | tf_op jit(solution)/shard_map/fetch_points/ppermute | solution.py:22
  21.2 5.3 %collective-permute-start.5 = (bf16[608,256]{1,0:T(8,128)(2,1)S(1)}, bf16[608,256]{1,0:T(8,128)(2,1)S(1)}, u32[]{:S(2)}, u32[]{:S(2)}) collective-permute-start(bf16[608,256]{1,0:T(8,128)(2,1)S(1)} %collective-permute-done.3.refs_3_), channel_id=1, source_target_pairs={{0,4},{4,0},{1,5},{5,1},{2,6},{6,2},{3,7},{7,3},{8,12},{12,8},{9,1... | collective-permute-start | bytes 933896 | tf_op jit(solution)/shard_map/fetch_points/ppermute | solution.py:22
  21.8 0.8 copy-start.2
  26.5 7.2 %collective-permute-start.7 = (bf16[304,256]{1,0:T(8,128)(2,1)S(1)}, bf16[304,256]{1,0:T(8,128)(2,1)S(1)}, u32[]{:S(2)}, u32[]{:S(2)}) collective-permute-start(bf16[304,256]{1,0:T(8,128)(2,1)S(1)} %slice.322), channel_id=1, source_target_pairs={{0,8},{8,16},{16,24},{24,0},{1,9},{9,17},{17,25},{25,1},{2,10},{10... | collective-permute-start | bytes 466952 | tf_op jit(solution)/shard_map/fetch_points/ppermute | solution.py:22
  33.7 2.5 %collective-permute-start.11 = (bf16[608,256]{1,0:T(8,128)(2,1)S(1)}, bf16[608,256]{1,0:T(8,128)(2,1)S(1)}, u32[]{:S(2)}, u32[]{:S(2)}) collective-permute-start(bf16[608,256]{1,0:T(8,128)(2,1)S(1)} %constant_dynamic-update-slice_fusion.2.refs_4_), channel_id=1, source_target_pairs={{0,4},{4,0},{1,5},{5,1},{2,6},{6,2},{3,7},{7,3},{8,12},{12,8},{9,1... | collective-permute-start | bytes 933896 | tf_op jit(solution)/shard_map/build_tiles/ppermute | solution.py:22
  36.2 23.3 %copy-start.3 = (f32[512,16]{0,1:T(8,128)S(1)}, f32[512,16]{0,1:T(8,128)}, u32[]{:S(2)}) copy-start(f32[512,16]{0,1:T(8,128)} %param.5) | copy-start | bytes 98308
  38.7 6.3 %collective-permute-start.14 = (f32[16,2048]{1,0:T(8,128)S(1)}, f32[16,2048]{1,0:T(8,128)S(1)}, u32[]{:S(2)}, u32[]{:S(2)}) collective-permute-start(f32[16,2048]{1,0:T(8,128)S(1)} %get-tuple-element.40.refs_0_), channel_id=1, source_target_pairs={{0,24},{8,0},{16,8},{24,16},{1,25},{9,1},{17,9},{25,17},{2,26},{10... | collective-permute-start | bytes 393224 | tf_op jit(solution)/shard_map/sum_over_z/ppermute | solution.py:22
  38.7 7.9 %collective-permute-start.13 = (f32[16,2048]{1,0:T(8,128)S(1)}, f32[16,2048]{1,0:T(8,128)S(1)}, u32[]{:S(2)}, u32[]{:S(2)}) collective-permute-start(f32[16,2048]{1,0:T(8,128)S(1)} %get-tuple-element.40.refs_0_), channel_id=1, source_target_pairs={{0,16},{8,24},{16,0},{24,8},{1,17},{9,25},{17,1},{25,9},{2,18},{10... | collective-permute-start | bytes 393224 | tf_op jit(solution)/shard_map/sum_over_z/ppermute | solution.py:22
  39.8 9.2 %collective-permute-start.12 = (f32[16,2048]{1,0:T(8,128)S(1)}, f32[16,2048]{1,0:T(8,128)S(1)}, u32[]{:S(2)}, u32[]{:S(2)}) collective-permute-start(f32[16,2048]{1,0:T(8,128)S(1)} %get-tuple-element.40.refs_0_), channel_id=1, source_target_pairs={{0,8},{8,16},{16,24},{24,0},{1,9},{9,17},{17,25},{25,1},{2,10},{10... | collective-permute-start | bytes 393224 | tf_op jit(solution)/shard_map/sum_over_z/ppermute | solution.py:22
  49.1 1.3 %collective-permute-start.15 = (f32[16,640]{1,0:T(8,128)S(1)}, f32[16,640]{1,0:T(8,128)S(1)}, u32[]{:S(2)}, u32[]{:S(2)}) collective-permute-start(f32[16,640]{1,0:T(8,128)S(1)} %get-tuple-element.42), channel_id=1, source_target_pairs={{0,4},{4,0},{1,5},{5,1},{2,6},{6,2},{3,7},{7,3},{8,12},{12,8},{9,1... | collective-permute-start | bytes 122888 | tf_op jit(solution)/shard_map/gather_image/ppermute | solution.py:22
  50.4 9.0 %collective-permute-start.18 = (f32[32,640]{1,0:T(8,128)S(1)}, f32[32,640]{1,0:T(8,128)S(1)}, u32[]{:S(2)}, u32[]{:S(2)}) collective-permute-start(f32[32,640]{1,0:T(8,128)S(1)} %constant_dynamic-update-slice_fusion.20), channel_id=1, source_target_pairs={{0,64},{32,96},{64,0},{96,32},{1,65},{33,97},{65,1},{97,33},{2,66}... | collective-permute-start | bytes 245768 | tf_op jit(solution)/shard_map/gather_image/ppermute | solution.py:22
  52.6 6.8 %collective-permute-start.17 = (f32[32,640]{1,0:T(8,128)S(1)}, f32[32,640]{1,0:T(8,128)S(1)}, u32[]{:S(2)}, u32[]{:S(2)}) collective-permute-start(f32[32,640]{1,0:T(8,128)S(1)} %constant_dynamic-update-slice_fusion.20), channel_id=1, source_target_pairs={{0,96},{32,0},{64,32},{96,64},{1,97},{33,1},{65,33},{97,65},{2,98}... | collective-permute-start | bytes 245768 | tf_op jit(solution)/shard_map/gather_image/ppermute | solution.py:22
  53.7 5.7 %collective-permute-start.16 = (f32[32,640]{1,0:T(8,128)S(1)}, f32[32,640]{1,0:T(8,128)S(1)}, u32[]{:S(2)}, u32[]{:S(2)}) collective-permute-start(f32[32,640]{1,0:T(8,128)S(1)} %constant_dynamic-update-slice_fusion.20), channel_id=1, source_target_pairs={{0,32},{32,64},{64,96},{96,0},{1,33},{33,65},{65,97},{97,1},{2,34}... | collective-permute-start | bytes 245768 | tf_op jit(solution)/shard_map/gather_image/ppermute | solution.py:22
  62.0 1.4 %collective-permute-start.19 = (f32[16,2176]{1,0:T(8,128)S(1)}, f32[16,2176]{1,0:T(8,128)S(1)}, u32[]{:S(2)}, u32[]{:S(2)}) collective-permute-start(f32[16,2176]{1,0:T(8,128)S(1)} %get-tuple-element.45), channel_id=1, source_target_pairs={{0,4},{4,0},{1,5},{5,1},{2,6},{6,2},{3,7},{7,3},{8,12},{12,8},{9,1... | collective-permute-start | bytes 417800 | tf_op jit(solution)/shard_map/sum_over_yc/ppermute | solution.py:22
  63.4 5.3 %collective-permute-start.21 = (f32[16,640]{1,0:T(8,128)S(1)}, f32[16,640]{1,0:T(8,128)S(1)}, u32[]{:S(2)}, u32[]{:S(2)}) collective-permute-start(f32[16,640]{1,0:T(8,128)S(1)} %concatenate.44), channel_id=1, source_target_pairs={{0,32},{32,64},{64,96},{96,0},{1,33},{33,65},{65,97},{97,1},{2,34}... | collective-permute-start | bytes 122888 | tf_op jit(solution)/shard_map/sum_over_yc/ppermute | solution.py:22
  63.5 5.2 %collective-permute-start.20 = (f32[16,640]{1,0:T(8,128)S(1)}, f32[16,640]{1,0:T(8,128)S(1)}, u32[]{:S(2)}, u32[]{:S(2)}) collective-permute-start(f32[16,640]{1,0:T(8,128)S(1)} %get-tuple-element.97), channel_id=1, source_target_pairs={{0,96},{32,0},{64,32},{96,64},{1,97},{33,1},{65,33},{97,65},{2,98}... | collective-permute-start | bytes 122888 | tf_op jit(solution)/shard_map/sum_over_yc/ppermute | solution.py:22
  66.7 5.5 %collective-permute-start.22 = (f32[16,640]{1,0:T(8,128)S(1)}, f32[16,640]{1,0:T(8,128)S(1)}, u32[]{:S(2)}, u32[]{:S(2)}) collective-permute-start(f32[16,640]{1,0:T(8,128)S(1)} %get-tuple-element.98), channel_id=1, source_target_pairs={{0,64},{32,96},{64,0},{96,32},{1,65},{33,97},{65,1},{97,33},{2,66}... | collective-permute-start | bytes 122888 | tf_op jit(solution)/shard_map/sum_over_yc/ppermute | solution.py:22
  72.2 5.2 %collective-permute-start.25 = (f32[16,128]{1,0:T(8,128)S(1)}, f32[16,128]{1,0:T(8,128)S(1)}, u32[]{:S(2)}, u32[]{:S(2)}) collective-permute-start(f32[16,128]{1,0:T(8,128)S(1)} %slice_add_fusion.3), channel_id=1, source_target_pairs={{0,16},{8,24},{16,0},{24,8},{1,17},{9,25},{17,1},{25,9},{2,18},{10... | collective-permute-start | bytes 24584 | tf_op jit(solution)/shard_map/sum_sums_over_z/ppermute | solution.py:22
  73.0 4.4 %collective-permute-start.24 = (f32[16,128]{1,0:T(8,128)S(1)}, f32[16,128]{1,0:T(8,128)S(1)}, u32[]{:S(2)}, u32[]{:S(2)}) collective-permute-start(f32[16,128]{1,0:T(8,128)S(1)} %slice_add_fusion.3), channel_id=1, source_target_pairs={{0,24},{8,0},{16,8},{24,16},{1,25},{9,1},{17,9},{25,17},{2,26},{10... | collective-permute-start | bytes 24584 | tf_op jit(solution)/shard_map/sum_sums_over_z/ppermute | solution.py:22
  74.2 4.9 %collective-permute-start.23 = (f32[16,128]{1,0:T(8,128)S(1)}, f32[16,128]{1,0:T(8,128)S(1)}, u32[]{:S(2)}, u32[]{:S(2)}) collective-permute-start(f32[16,128]{1,0:T(8,128)S(1)} %slice_add_fusion.3), channel_id=1, source_target_pairs={{0,8},{8,16},{16,24},{24,0},{1,9},{9,17},{17,25},{25,1},{2,10},{10... | collective-permute-start | bytes 24584 | tf_op jit(solution)/shard_map/sum_sums_over_z/ppermute | solution.py:22

commit v4 on v3

--- a/solution.py
+++ b/solution.py
@@ -246,34 +246,45 @@
         middle = message.shape[0] // 2
         row, col = {0: message}, {(0, 0): message}
         for k in (1, 3):
-            col[0, k] = shift(message, "y", NY, k)
             row[k] = shift(message, "z", NZ, k)
         col[1, 0] = shift(message, "c", NC, 1)
-        far = []
-        for axis, size, ahead, behind in (("z", NZ, row[1], row[3]), ("y", NY, col[0, 1], col[0, 3])):
-            far.append((shift(ahead[:middle], axis, size, 1), shift(behind[middle:], axis, size, -1)))
         for k in (1, 3):
-            col[1, k] = shift(col[0, k], "c", NC, 1)
+            col[0, k] = shift(message, "y", NY, k)
         near = [row[k] for k in ROWS[:3]]
 
     with jax.named_scope("build_tiles"):
+        at = [col[0, 0], col[1, 0]]
+        tile_a, image, half = build(near, at, own, probes, side=side)
+        ring = {"z": (row[1], row[3]), "y": (col[0, 1], col[0, 3])}
+        ring, image = lax.optimization_barrier((ring, image))
+        far = {}
+        for axis, size in (("z", NZ), ("y", NY)):
+            ahead, behind = ring[axis]
+            far[axis] = shift(ahead[:middle], axis, size, 1), shift(behind[middle:], axis, size, -1)
+        tile_b, image = build(near, [ring["y"][0]], own, probes, [half], [image])
+        other, image = lax.optimization_barrier((ring["y"][0], image))
+        col[1, 1] = shift(other, "c", NC, 1)
+        tile_c, image = build(near, [ring["y"][1]], own, probes, [half], [image])
+        other, image = lax.optimization_barrier((ring["y"][1], image))
+        col[1, 3] = shift(other, "c", NC, 1)
+        tile_d, image = build(near, [col[1, 1]], own, probes, [half], [image])
+        tile_e, image = build(near, [col[1, 3]], own, probes, [half], [image])
+        far, image = lax.optimization_barrier((far, image))
+        row[2] = jnp.concatenate(far["z"], axis=0)
+        col[0, 2] = jnp.concatenate(far["y"], axis=0)
+        col[1, 2] = shift(col[0, 2], "c", NC, 1)
         at = [col[k] for k in COLS[:6]]
-        tile_a, image, half = build(near, at[:2], own, probes, side=side)
-        tile_b, image = build(near, at[2:4], own, probes, [half], [image])
-        tile_c, image = build(near, at[4:6], own, probes, [half], [image])
-        far, image = lax.optimization_barrier((far, image))
-        row[2] = jnp.concatenate(far[0], axis=0)
-        col[0, 2] = jnp.concatenate(far[1], axis=0)
-        col[1, 2] = shift(col[0, 2], "c", NC, 1)
-        tile_d, image_far, half_far = build([row[2]], at, own, probes)
+        tile_f, image_far, half_far = build([row[2]], at, own, probes)
         at = [col[0, 2], col[1, 2]]
-        tile_e, image = build(near + [row[2]], at, own, probes, [half, half_far], [image, image_far])
+        tile_g, image = build(near + [row[2]], at, own, probes, [half, half_far], [image, image_far])
         tiles = [
             (tile_a, 0, 0),
             (tile_b, 0, 2 * own),
-            (tile_c, 0, 4 * own),
-            (tile_d, 3 * own, 0),
-            (tile_e, 0, 6 * own),
+            (tile_c, 0, 3 * own),
+            (tile_d, 0, 4 * own),
+            (tile_e, 0, 5 * own),
+            (tile_f, 3 * own, 0),
+            (tile_g, 0, 6 * own),
         ]
         side_c = unpack_side([col[at] for at in COLS], probes, own)
         side_r = unpack_side([row[k] for k in ROWS], probes, own)
@@ -285,12 +296,14 @@
         image_r, message = combine(side_r, parts, own)
 
     with jax.named_scope("gather_image"):
-        pair = jnp.concatenate([message, shift(message, "c", NC, 1)], axis=0)
-        every = {0: pair}
+        every = {0: message}
         for m in (1, 3, 2):
-            every[m] = shift(pair, "y", NY, m)
-        image_c = jnp.concatenate([every[m][h * probes : (h + 1) * probes, :own] for h, m in COLS], axis=1)
-        sums = sum(every[m][h * probes : (h + 1) * probes, own:] for h, m in COLS)
+            every[m] = shift(message, "y", NY, m)
+        line = jnp.concatenate([every[m] for m in range(NY)], axis=1)
+        pair = line, shift(line, "c", NC, 1)
+        width = own + LANES
+        image_c = jnp.concatenate([pair[h][:, m * width : m * width + own] for h, m in COLS], axis=1)
+        sums = sum(pair[h][:, m * width + own : (m + 1) * width] for h, m in COLS)
 
     mine, other, held = second_product(tiles, side, image_r, side_r, image_c, side_c, sums, own)
 

time: 80.2 us -> 85.5 us (1.066)
  waiting for transfers between devices: 33.2 us -> 38.3 us
    ppermute x26, waiting for transfers between devices: 33.2 us -> 38.3 us  [shift(): lax.ppermute(value, axis, [(i, (i + step) % size) for i in range(size)])]
    pallas_call x5 -> x7, Pallas kernels: 10.3 us -> 10.8 us  [build(): pl.pallas_call(functools.partial(tile_kernel, counts, probes), out_shape=...]
    unnamed x38 -> x35, local copies, waits for them, and re-layouts: 1.99 us -> 1.99 us
  transfers between devices with their start and end apart: 26 -> 26, of which waited for: 13 -> 16; matrix products, arithmetic and copies ran while one was open for 0% -> 0% of each run, Pallas kernels for 10% -> 10%
where the time goes in v4:
time: 85.5 us; the launch traced here: 85.2 us
  waiting for transfers between devices  38.3 us (45%)
  starting transfers between devices  28.3 us (33%)
  Pallas kernels  13.7 us (16%)
  local copies, waits for them, and re-layouts  2.15 us (3%)
  between operations  1.78 us (2%)
  other arithmetic  1.01 us (1%)
    ppermute x26, waiting for transfers between devices, shift(): lax.ppermute(value, axis, [(i, (i + step) % size) for i in range(size)])  38.3 us
    ppermute x26, starting transfers between devices, shift(): lax.ppermute(value, axis, [(i, (i + step) % size) for i in range(size)])  28.3 us
    pallas_call x7, Pallas kernels, build(): pl.pallas_call(functools.partial(tile_kernel, counts, probes), out_shape=...  10.8 us
    pallas_call x1, Pallas kernels, second_product(): pl.pallas_call(kernel, in_specs=[pl.BlockSpec(memory_space=pltpu.VMEM)] *...  2.49 us
    unnamed x35, local copies, waits for them, and re-layouts  1.99 us
  transfers between devices with their start and end apart: 26, of which 16 were waited for; matrix products, arithmetic and copies ran while one was open for 0% of the time, Pallas kernels for 10%

profile of v4, /device:TPU:0, one launch (start us, length us, event | category | flops | bytes accessed | tf_op | source)
XLA Modules:
  0.0 85.2 jit_solution(11512924257867640250)
XLA Ops:
  2.8 3.2 %collective-permute-start.4 = (bf16[608,256]{1,0:T(8,128)(2,1)S(1)}, bf16[608,256]{1,0:T(8,128)(2,1)S(1)}, u32[]{:S(2)}, u32[]{:S(2)}) collective-permute-start(bf16[608,256]{1,0:T(8,128)(2,1)S(1)} %pack.1.refs_0_.refs_3_.refs_1_), channel_id=1, source_target_pairs={{0,96},{32,0},{64,32},{96,64},{1,97},{33,1},{65,33},{97,65},{2,98}... | collective-permute-start | bytes 933896 | tf_op jit(solution)/shard_map/fetch_points/ppermute | solution.py:22
  6.0 4.0 %collective-permute-start.1 = (bf16[608,256]{1,0:T(8,128)(2,1)S(1)}, bf16[608,256]{1,0:T(8,128)(2,1)S(1)}, u32[]{:S(2)}, u32[]{:S(2)}) collective-permute-start(bf16[608,256]{1,0:T(8,128)(2,1)S(1)} %pack.1.refs_0_.refs_3_.refs_1_), channel_id=1, source_target_pairs={{0,24},{8,0},{16,8},{24,16},{1,25},{9,1},{17,9},{25,17},{2,26},{10... | collective-permute-start | bytes 933896 | tf_op jit(solution)/shard_map/fetch_points/ppermute | solution.py:22
  10.1 7.3 %collective-permute-done.1.refs_2_ = bf16[608,256]{1,0:T(8,128)(2,1)S(1)} collective-permute-done((bf16[608,256]{1,0:T(8,128)(2,1)S(1)}, bf16[608,256]{1,0:T(8,128)(2,1)S(1)}, u32[]{:S(2)}, u32[]{:S(2)}) %collective-permute-start.1) | collective-permute-done | bytes 311328 | tf_op jit(solution)/shard_map/fetch_points/ppermute | solution.py:22
  17.3 3.4 %collective-permute-done.refs_1_ = bf16[608,256]{1,0:T(8,128)(2,1)S(1)} collective-permute-done((bf16[608,256]{1,0:T(8,128)(2,1)S(1)}, bf16[608,256]{1,0:T(8,128)(2,1)S(1)}, u32[]{:S(2)}, u32[]{:S(2)}) %collective-permute-start) | collective-permute-done | bytes 311328 | tf_op jit(solution)/shard_map/fetch_points/ppermute | solution.py:22
  20.7 0.8 copy-done.2
  21.5 2.0 %build_tile.7 = (bf16[1536,1024]{1,0:T(8,128)(2,1)S(1)}, f32[16,1536]{1,0:T(8,128)S(1)}, f32[1536,1]{1,0:T(8,128)S(1)}) custom-call(bf16[608,256]{1,0:T(8,128)(2,1)S(1)} %pack.1.refs_0_.refs_3_.refs_1_, bf16[608,256]{1,0:T(8,128)(2,1)S(1)} %collective-permute-done.refs_1_, bf16[608,256]{1,0:T(8,128)(2,1)S(1)} %collective-permute-done.1.refs_2_, ...), custom_call_target="tpu_custom_call" | custom-call | flops 50331648 | bytes 1024 | tf_op jit(solution)/shard_map/build_tiles/build_tile/pallas_call | solution.py:135
  23.6 3.3 %collective-permute-start.8 = (bf16[304,256]{1,0:T(8,128)(2,1)S(1)}, bf16[304,256]{1,0:T(8,128)(2,1)S(1)}, u32[]{:S(2)}, u32[]{:S(2)}) collective-permute-start(bf16[304,256]{1,0:T(8,128)(2,1)S(1)} %slice.244), channel_id=1, source_target_pairs={{0,96},{32,0},{64,32},{96,64},{1,97},{33,1},{65,33},{97,65},{2,98}... | collective-permute-start | bytes 466952 | tf_op jit(solution)/shard_map/build_tiles/ppermute | solution.py:22
  27.2 1.1 %build_tile.8 = (bf16[1536,512]{1,0:T(8,128)(2,1)S(1)}, f32[16,1536]{1,0:T(8,128)S(1)}) custom-call(bf16[608,256]{1,0:T(8,128)(2,1)S(1)} %pack.1.refs_0_.refs_3_.refs_1_, bf16[608,256]{1,0:T(8,128)(2,1)S(1)} %collective-permute-done.refs_1_, bf16[608,256]{1,0:T(8,128)(2,1)S(1)} %collective-permute-done.1.refs_2_, ...), custom_call_target="tpu_custom_call" | custom-call | flops 25165824 | bytes 1024 | tf_op jit(solution)/shard_map/build_tiles/build_tile/pallas_call | solution.py:135
  28.3 1.1 %build_tile.9 = (bf16[1536,512]{1,0:T(8,128)(2,1)S(1)}, f32[16,1536]{1,0:T(8,128)S(1)}) custom-call(bf16[608,256]{1,0:T(8,128)(2,1)S(1)} %pack.1.refs_0_.refs_3_.refs_1_, bf16[608,256]{1,0:T(8,128)(2,1)S(1)} %collective-permute-done.refs_1_, bf16[608,256]{1,0:T(8,128)(2,1)S(1)} %collective-permute-done.1.refs_2_, ...), custom_call_target="tpu_custom_call" | custom-call | flops 25165824 | bytes 1024 | tf_op jit(solution)/shard_map/build_tiles/build_tile/pallas_call | solution.py:135
  30.0 1.8 %collective-permute-start.9 = (bf16[304,256]{1,0:T(8,128)(2,1)S(1)}, bf16[304,256]{1,0:T(8,128)(2,1)S(1)}, u32[]{:S(2)}, u32[]{:S(2)}) collective-permute-start(bf16[304,256]{1,0:T(8,128)(2,1)S(1)} %slice.245), channel_id=1, source_target_pairs={{0,8},{8,16},{16,24},{24,0},{1,9},{9,17},{17,25},{25,1},{2,10},{10... | collective-permute-start | bytes 466952 | tf_op jit(solution)/shard_map/build_tiles/ppermute | solution.py:22
  31.8 1.1 %build_tile.10 = (bf16[1536,512]{1,0:T(8,128)(2,1)S(1)}, f32[16,1536]{1,0:T(8,128)S(1)}) custom-call(bf16[608,256]{1,0:T(8,128)(2,1)S(1)} %pack.1.refs_0_.refs_3_.refs_1_, bf16[608,256]{1,0:T(8,128)(2,1)S(1)} %collective-permute-done.refs_1_, bf16[608,256]{1,0:T(8,128)(2,1)S(1)} %collective-permute-done.1.refs_2_, ...), custom_call_target="tpu_custom_call" | custom-call | flops 25165824 | bytes 1024 | tf_op jit(solution)/shard_map/build_tiles/build_tile/pallas_call | solution.py:135
  32.9 1.1 %build_tile.11 = (bf16[1536,512]{1,0:T(8,128)(2,1)S(1)}, f32[16,1536]{1,0:T(8,128)S(1)}) custom-call(bf16[608,256]{1,0:T(8,128)(2,1)S(1)} %pack.1.refs_0_.refs_3_.refs_1_, bf16[608,256]{1,0:T(8,128)(2,1)S(1)} %collective-permute-done.refs_1_, bf16[608,256]{1,0:T(8,128)(2,1)S(1)} %collective-permute-done.1.refs_2_, ...), custom_call_target="tpu_custom_call" | custom-call | flops 25165824 | bytes 1024 | tf_op jit(solution)/shard_map/build_tiles/build_tile/pallas_call | solution.py:135
  34.1 3.2 %collective-permute-done.9 = bf16[304,256]{1,0:T(8,128)(2,1)S(1)} collective-permute-done((bf16[304,256]{1,0:T(8,128)(2,1)S(1)}, bf16[304,256]{1,0:T(8,128)(2,1)S(1)}, u32[]{:S(2)}, u32[]{:S(2)}) %collective-permute-start.9) | collective-permute-done | bytes 155680 | tf_op jit(solution)/shard_map/build_tiles/ppermute | solution.py:22
  37.7 2.0 %build_tile.12 = (bf16[512,3072]{1,0:T(8,128)(2,1)S(1)}, f32[16,512]{1,0:T(8,128)S(1)}, f32[512,1]{1,0:T(8,128)S(1)}) custom-call(bf16[608,256]{1,0:T(8,128)(2,1)S(1)} %constant_dynamic-update-slice_fusion.refs_0_.refs_3_, bf16[608,256]{1,0:T(8,128)(2,1)S(1)} %pack.1.refs_0_.refs_3_.refs_1_, bf16[608,256]{1,0:T(8,128)(2,1)S(1)} %collective-permute-done.2.refs_4_.refs_2_, ...), custom_call_target="tpu_custom_call" | custom-call | flops 50331648 | bytes 1024 | tf_op jit(solution)/shard_map/build_tiles/build_tile/pallas_call | solution.py:135
  39.8 2.5 %build_tile.13 = (bf16[2048,1024]{1,0:T(8,128)(2,1)S(1)}, f32[16,2048]{1,0:T(8,128)S(1)}) custom-call(bf16[608,256]{1,0:T(8,128)(2,1)S(1)} %pack.1.refs_0_.refs_3_.refs_1_, bf16[608,256]{1,0:T(8,128)(2,1)S(1)} %collective-permute-done.refs_1_, bf16[608,256]{1,0:T(8,128)(2,1)S(1)} %collective-permute-done.1.refs_2_, ...), custom_call_target="tpu_custom_call" | custom-call | flops 67108864 | bytes 1024 | tf_op jit(solution)/shard_map/build_tiles/build_tile/pallas_call | solution.py:135
  42.3 2.6 %collective-permute-start.13 = (f32[16,2048]{1,0:T(8,128)S(1)}, f32[16,2048]{1,0:T(8,128)S(1)}, u32[]{:S(2)}, u32[]{:S(2)}) collective-permute-start(f32[16,2048]{1,0:T(8,128)S(1)} %get-tuple-element.66.refs_0_), channel_id=1, source_target_pairs={{0,16},{8,24},{16,0},{24,8},{1,17},{9,25},{17,1},{25,9},{2,18},{10... | collective-permute-start | bytes 393224 | tf_op jit(solution)/shard_map/sum_over_z/ppermute | solution.py:22
  44.9 3.7 %collective-permute-done.14.refs_3_ = f32[16,2048]{1,0:T(8,128)S(1)} collective-permute-done((f32[16,2048]{1,0:T(8,128)S(1)}, f32[16,2048]{1,0:T(8,128)S(1)}, u32[]{:S(2)}, u32[]{:S(2)}) %collective-permute-start.14) | collective-permute-done | bytes 131104 | tf_op jit(solution)/shard_map/sum_over_z/ppermute | solution.py:22
  48.6 1.6 %collective-permute-done.13.refs_2_ = f32[16,2048]{1,0:T(8,128)S(1)} collective-permute-done((f32[16,2048]{1,0:T(8,128)S(1)}, f32[16,2048]{1,0:T(8,128)S(1)}, u32[]{:S(2)}, u32[]{:S(2)}) %collective-permute-start.13) | collective-permute-done | bytes 131104 | tf_op jit(solution)/shard_map/sum_over_z/ppermute | solution.py:22
  50.2 2.4 %collective-permute-done.12.refs_1_ = f32[16,2048]{1,0:T(8,128)S(1)} collective-permute-done((f32[16,2048]{1,0:T(8,128)S(1)}, f32[16,2048]{1,0:T(8,128)S(1)}, u32[]{:S(2)}, u32[]{:S(2)}) %collective-permute-start.12) | collective-permute-done | bytes 131104 | tf_op jit(solution)/shard_map/sum_over_z/ppermute | solution.py:22
  52.7 3.3 %collective-permute-start.17 = (f32[16,640]{1,0:T(8,128)S(1)}, f32[16,640]{1,0:T(8,128)S(1)}, u32[]{:S(2)}, u32[]{:S(2)}) collective-permute-start(f32[16,640]{1,0:T(8,128)S(1)} %get-tuple-element.68), channel_id=1, source_target_pairs={{0,96},{32,0},{64,32},{96,64},{1,97},{33,1},{65,33},{97,65},{2,98}... | collective-permute-start | bytes 122888 | tf_op jit(solution)/shard_map/gather_image/ppermute | solution.py:22
  56.0 0.9 %collective-permute-start.15 = (f32[16,640]{1,0:T(8,128)S(1)}, f32[16,640]{1,0:T(8,128)S(1)}, u32[]{:S(2)}, u32[]{:S(2)}) collective-permute-start(f32[16,640]{1,0:T(8,128)S(1)} %get-tuple-element.68), channel_id=1, source_target_pairs={{0,32},{32,64},{64,96},{96,0},{1,33},{33,65},{65,97},{97,1},{2,34}... | collective-permute-start | bytes 122888 | tf_op jit(solution)/shard_map/gather_image/ppermute | solution.py:22
  57.7 3.9 %collective-permute-done.16 = f32[16,640]{1,0:T(8,128)S(1)} collective-permute-done((f32[16,640]{1,0:T(8,128)S(1)}, f32[16,640]{1,0:T(8,128)S(1)}, u32[]{:S(2)}, u32[]{:S(2)}) %collective-permute-start.16) | collective-permute-done | bytes 40992 | tf_op jit(solution)/shard_map/gather_image/ppermute | solution.py:22
  61.8 1.4 %collective-permute-done.18 = f32[16,2560]{1,0:T(8,128)S(1)} collective-permute-done((f32[16,2560]{1,0:T(8,128)S(1)}, f32[16,2560]{1,0:T(8,128)S(1)}, u32[]{:S(2)}, u32[]{:S(2)}) %collective-permute-start.18) | collective-permute-done | bytes 163872 | tf_op jit(solution)/shard_map/gather_image/ppermute | solution.py:22
  63.3 2.5 %second_product.1 = (f32[16,2176]{1,0:T(8,128)S(1)}, f32[16,2176]{1,0:T(8,128)S(1)}, f32[3,16,512]{2,1,0:T(8,128)S(1)}) custom-call(bf16[1536,1024]{1,0:T(8,128)(2,1)S(1)} %get-tuple-element.37.refs_0_, bf16[1536,512]{1,0:T(8,128)(2,1)S(1)} %get-tuple-element.42.refs_1_, bf16[1536,512]{1,0:T(8,128)(2,1)S(1)} %get-tuple-element.46.refs_2_, ...), custom_call_target="tpu_custom_call" | custom-call | flops 268435456 | bytes 1024 | tf_op jit(solution)/shard_map/second_product/pallas_call | solution.py:226
  65.9 1.2 %collective-permute-done.19 = f32[16,2176]{1,0:T(8,128)S(1)} collective-permute-done((f32[16,2176]{1,0:T(8,128)S(1)}, f32[16,2176]{1,0:T(8,128)S(1)}, u32[]{:S(2)}, u32[]{:S(2)}) %collective-permute-start.19) | collective-permute-done | bytes 139296 | tf_op jit(solution)/shard_map/sum_over_yc/ppermute | solution.py:22
  67.3 3.2 %collective-permute-start.20 = (f32[16,640]{1,0:T(8,128)S(1)}, f32[16,640]{1,0:T(8,128)S(1)}, u32[]{:S(2)}, u32[]{:S(2)}) collective-permute-start(f32[16,640]{1,0:T(8,128)S(1)} %get-tuple-element.123), channel_id=1, source_target_pairs={{0,96},{32,0},{64,32},{96,64},{1,97},{33,1},{65,33},{97,65},{2,98}... | collective-permute-start | bytes 122888 | tf_op jit(solution)/shard_map/sum_over_yc/ppermute | solution.py:22
  71.2 1.3 %collective-permute-done.21 = f32[16,640]{1,0:T(8,128)S(1)} collective-permute-done((f32[16,640]{1,0:T(8,128)S(1)}, f32[16,640]{1,0:T(8,128)S(1)}, u32[]{:S(2)}, u32[]{:S(2)}) %collective-permute-start.21) | collective-permute-done | bytes 40992 | tf_op jit(solution)/shard_map/sum_over_yc/ppermute | solution.py:22
  72.5 3.5 %collective-permute-done.22 = f32[16,640]{1,0:T(8,128)S(1)} collective-permute-done((f32[16,640]{1,0:T(8,128)S(1)}, f32[16,640]{1,0:T(8,128)S(1)}, u32[]{:S(2)}, u32[]{:S(2)}) %collective-permute-start.22) | collective-permute-done | bytes 40992 | tf_op jit(solution)/shard_map/sum_over_yc/ppermute | solution.py:22
  76.0 1.7 %collective-permute-start.25 = (f32[16,128]{1,0:T(8,128)S(1)}, f32[16,128]{1,0:T(8,128)S(1)}, u32[]{:S(2)}, u32[]{:S(2)}) collective-permute-start(f32[16,128]{1,0:T(8,128)S(1)} %slice_add_fusion.3), channel_id=1, source_target_pairs={{0,16},{8,24},{16,0},{24,8},{1,17},{9,25},{17,1},{25,9},{2,18},{10... | collective-permute-start | bytes 24584 | tf_op jit(solution)/shard_map/sum_sums_over_z/ppermute | solution.py:22
  77.8 1.7 %collective-permute-start.24 = (f32[16,128]{1,0:T(8,128)S(1)}, f32[16,128]{1,0:T(8,128)S(1)}, u32[]{:S(2)}, u32[]{:S(2)}) collective-permute-start(f32[16,128]{1,0:T(8,128)S(1)} %slice_add_fusion.3), channel_id=1, source_target_pairs={{0,24},{8,0},{16,8},{24,16},{1,25},{9,1},{17,9},{25,17},{2,26},{10... | collective-permute-start | bytes 24584 | tf_op jit(solution)/shard_map/sum_sums_over_z/ppermute | solution.py:22
  79.8 1.4 %collective-permute-done.25 = f32[16,128]{1,0:T(8,128)S(1)} collective-permute-done((f32[16,128]{1,0:T(8,128)S(1)}, f32[16,128]{1,0:T(8,128)S(1)}, u32[]{:S(2)}, u32[]{:S(2)}) %collective-permute-start.25) | collective-permute-done | bytes 8224 | tf_op jit(solution)/shard_map/sum_sums_over_z/ppermute | solution.py:22
  81.4 2.9 %collective-permute-done.23 = f32[16,128]{1,0:T(8,128)S(1)} collective-permute-done((f32[16,128]{1,0:T(8,128)S(1)}, f32[16,128]{1,0:T(8,128)S(1)}, u32[]{:S(2)}, u32[]{:S(2)}) %collective-permute-start.23) | collective-permute-done | bytes 8224 | tf_op jit(solution)/shard_map/sum_sums_over_z/ppermute | solution.py:22
  (88 shorter events, 6.5 us)
Async XLA Ops:
  0.6 1.1 %copy-start = (bf16[1024,256]{1,0:T(8,128)(2,1)S(1)}, bf16[1024,256]{1,0:T(8,128)(2,1)}, u32[]{:S(2)}) copy-start(bf16[1024,256]{1,0:T(8,128)(2,1)} %param.3) | copy-start | bytes 1572868
  1.8 0.8 copy-start.1
  2.8 20.7 %collective-permute-start.4 = (bf16[608,256]{1,0:T(8,128)(2,1)S(1)}, bf16[608,256]{1,0:T(8,128)(2,1)S(1)}, u32[]{:S(2)}, u32[]{:S(2)}) collective-permute-start(bf16[608,256]{1,0:T(8,128)(2,1)S(1)} %pack.1.refs_0_.refs_3_.refs_1_), channel_id=1, source_target_pairs={{0,96},{32,0},{64,32},{96,64},{1,97},{33,1},{65,33},{97,65},{2,98}... | collective-permute-start | bytes 933896 | tf_op jit(solution)/shard_map/fetch_points/ppermute | solution.py:22
  6.0 17.5 %collective-permute-start.3 = (bf16[608,256]{1,0:T(8,128)(2,1)S(1)}, bf16[608,256]{1,0:T(8,128)(2,1)S(1)}, u32[]{:S(2)}, u32[]{:S(2)}) collective-permute-start(bf16[608,256]{1,0:T(8,128)(2,1)S(1)} %pack.1.refs_0_.refs_3_.refs_1_), channel_id=1, source_target_pairs={{0,32},{32,64},{64,96},{96,0},{1,33},{33,65},{65,97},{97,1},{2,34}... | collective-permute-start | bytes 933896 | tf_op jit(solution)/shard_map/fetch_points/ppermute | solution.py:22
  6.0 4.1 %collective-permute-start.2 = (bf16[608,256]{1,0:T(8,128)(2,1)S(1)}, bf16[608,256]{1,0:T(8,128)(2,1)S(1)}, u32[]{:S(2)}, u32[]{:S(2)}) collective-permute-start(bf16[608,256]{1,0:T(8,128)(2,1)S(1)} %pack.1.refs_0_.refs_3_.refs_1_), channel_id=1, source_target_pairs={{0,4},{4,0},{1,5},{5,1},{2,6},{6,2},{3,7},{7,3},{8,12},{12,8},{9,1... | collective-permute-start | bytes 933896 | tf_op jit(solution)/shard_map/fetch_points/ppermute | solution.py:22
  6.0 11.3 %collective-permute-start.1 = (bf16[608,256]{1,0:T(8,128)(2,1)S(1)}, bf16[608,256]{1,0:T(8,128)(2,1)S(1)}, u32[]{:S(2)}, u32[]{:S(2)}) collective-permute-start(bf16[608,256]{1,0:T(8,128)(2,1)S(1)} %pack.1.refs_0_.refs_3_.refs_1_), channel_id=1, source_target_pairs={{0,24},{8,0},{16,8},{24,16},{1,25},{9,1},{17,9},{25,17},{2,26},{10... | collective-permute-start | bytes 933896 | tf_op jit(solution)/shard_map/fetch_points/ppermute | solution.py:22
  10.0 10.7 %collective-permute-start = (bf16[608,256]{1,0:T(8,128)(2,1)S(1)}, bf16[608,256]{1,0:T(8,128)(2,1)S(1)}, u32[]{:S(2)}, u32[]{:S(2)}) collective-permute-start(bf16[608,256]{1,0:T(8,128)(2,1)S(1)} %pack.1.refs_0_.refs_3_.refs_1_), channel_id=1, source_target_pairs={{0,8},{8,16},{16,24},{24,0},{1,9},{9,17},{17,25},{25,1},{2,10},{10... | collective-permute-start | bytes 933896 | tf_op jit(solution)/shard_map/fetch_points/ppermute | solution.py:22
  20.7 0.8 copy-start.2
  23.6 10.4 %collective-permute-start.8 = (bf16[304,256]{1,0:T(8,128)(2,1)S(1)}, bf16[304,256]{1,0:T(8,128)(2,1)S(1)}, u32[]{:S(2)}, u32[]{:S(2)}) collective-permute-start(bf16[304,256]{1,0:T(8,128)(2,1)S(1)} %slice.244), channel_id=1, source_target_pairs={{0,96},{32,0},{64,32},{96,64},{1,97},{33,1},{65,33},{97,65},{2,98}... | collective-permute-start | bytes 466952 | tf_op jit(solution)/shard_map/build_tiles/ppermute | solution.py:22
  26.9 7.1 %collective-permute-start.7 = (bf16[304,256]{1,0:T(8,128)(2,1)S(1)}, bf16[304,256]{1,0:T(8,128)(2,1)S(1)}, u32[]{:S(2)}, u32[]{:S(2)}) collective-permute-start(bf16[304,256]{1,0:T(8,128)(2,1)S(1)} %slice.243), channel_id=1, source_target_pairs={{0,32},{32,64},{64,96},{96,0},{1,33},{33,65},{65,97},{97,1},{2,34}... | collective-permute-start | bytes 466952 | tf_op jit(solution)/shard_map/build_tiles/ppermute | solution.py:22
  26.9 7.1 %collective-permute-start.10 = (bf16[304,256]{1,0:T(8,128)(2,1)S(1)}, bf16[304,256]{1,0:T(8,128)(2,1)S(1)}, u32[]{:S(2)}, u32[]{:S(2)}) collective-permute-start(bf16[304,256]{1,0:T(8,128)(2,1)S(1)} %slice.246), channel_id=1, source_target_pairs={{0,24},{8,0},{16,8},{24,16},{1,25},{9,1},{17,9},{25,17},{2,26},{10... | collective-permute-start | bytes 466952 | tf_op jit(solution)/shard_map/build_tiles/ppermute | solution.py:22
  28.3 1.8 %collective-permute-start.5 = (bf16[608,256]{1,0:T(8,128)(2,1)S(1)}, bf16[608,256]{1,0:T(8,128)(2,1)S(1)}, u32[]{:S(2)}, u32[]{:S(2)}) collective-permute-start(bf16[608,256]{1,0:T(8,128)(2,1)S(1)} %collective-permute-done.3.refs_3_), channel_id=1, source_target_pairs={{0,4},{4,0},{1,5},{5,1},{2,6},{6,2},{3,7},{7,3},{8,12},{12,8},{9,1... | collective-permute-start | bytes 933896 | tf_op jit(solution)/shard_map/build_tiles/ppermute | solution.py:22
  29.4 3.5 %collective-permute-start.6 = (bf16[608,256]{1,0:T(8,128)(2,1)S(1)}, bf16[608,256]{1,0:T(8,128)(2,1)S(1)}, u32[]{:S(2)}, u32[]{:S(2)}) collective-permute-start(bf16[608,256]{1,0:T(8,128)(2,1)S(1)} %collective-permute-done.4.refs_3_.refs_4_), channel_id=1, source_target_pairs={{0,4},{4,0},{1,5},{5,1},{2,6},{6,2},{3,7},{7,3},{8,12},{12,8},{9,1... | collective-permute-start | bytes 933896 | tf_op jit(solution)/shard_map/build_tiles/ppermute | solution.py:22
  30.0 7.3 %collective-permute-start.9 = (bf16[304,256]{1,0:T(8,128)(2,1)S(1)}, bf16[304,256]{1,0:T(8,128)(2,1)S(1)}, u32[]{:S(2)}, u32[]{:S(2)}) collective-permute-start(bf16[304,256]{1,0:T(8,128)(2,1)S(1)} %slice.245), channel_id=1, source_target_pairs={{0,8},{8,16},{16,24},{24,0},{1,9},{9,17},{17,25},{25,1},{2,10},{10... | collective-permute-start | bytes 466952 | tf_op jit(solution)/shard_map/build_tiles/ppermute | solution.py:22
  37.3 2.5 %collective-permute-start.11 = (bf16[608,256]{1,0:T(8,128)(2,1)S(1)}, bf16[608,256]{1,0:T(8,128)(2,1)S(1)}, u32[]{:S(2)}, u32[]{:S(2)}) collective-permute-start(bf16[608,256]{1,0:T(8,128)(2,1)S(1)} %constant_dynamic-update-slice_fusion.2.refs_4_), channel_id=1, source_target_pairs={{0,4},{4,0},{1,5},{5,1},{2,6},{6,2},{3,7},{7,3},{8,12},{12,8},{9,1... | collective-permute-start | bytes 933896 | tf_op jit(solution)/shard_map/build_tiles/ppermute | solution.py:22
  42.3 6.3 %collective-permute-start.14 = (f32[16,2048]{1,0:T(8,128)S(1)}, f32[16,2048]{1,0:T(8,128)S(1)}, u32[]{:S(2)}, u32[]{:S(2)}) collective-permute-start(f32[16,2048]{1,0:T(8,128)S(1)} %get-tuple-element.66.refs_0_), channel_id=1, source_target_pairs={{0,24},{8,0},{16,8},{24,16},{1,25},{9,1},{17,9},{25,17},{2,26},{10... | collective-permute-start | bytes 393224 | tf_op jit(solution)/shard_map/sum_over_z/ppermute | solution.py:22
  42.3 7.9 %collective-permute-start.13 = (f32[16,2048]{1,0:T(8,128)S(1)}, f32[16,2048]{1,0:T(8,128)S(1)}, u32[]{:S(2)}, u32[]{:S(2)}) collective-permute-start(f32[16,2048]{1,0:T(8,128)S(1)} %get-tuple-element.66.refs_0_), channel_id=1, source_target_pairs={{0,16},{8,24},{16,0},{24,8},{1,17},{9,25},{17,1},{25,9},{2,18},{10... | collective-permute-start | bytes 393224 | tf_op jit(solution)/shard_map/sum_over_z/ppermute | solution.py:22
  44.9 7.7 %collective-permute-start.12 = (f32[16,2048]{1,0:T(8,128)S(1)}, f32[16,2048]{1,0:T(8,128)S(1)}, u32[]{:S(2)}, u32[]{:S(2)}) collective-permute-start(f32[16,2048]{1,0:T(8,128)S(1)} %get-tuple-element.66.refs_0_), channel_id=1, source_target_pairs={{0,8},{8,16},{16,24},{24,0},{1,9},{9,17},{17,25},{25,1},{2,10},{10... | collective-permute-start | bytes 393224 | tf_op jit(solution)/shard_map/sum_over_z/ppermute | solution.py:22
  52.7 5.0 %collective-permute-start.17 = (f32[16,640]{1,0:T(8,128)S(1)}, f32[16,640]{1,0:T(8,128)S(1)}, u32[]{:S(2)}, u32[]{:S(2)}) collective-permute-start(f32[16,640]{1,0:T(8,128)S(1)} %get-tuple-element.68), channel_id=1, source_target_pairs={{0,96},{32,0},{64,32},{96,64},{1,97},{33,1},{65,33},{97,65},{2,98}... | collective-permute-start | bytes 122888 | tf_op jit(solution)/shard_map/gather_image/ppermute | solution.py:22
  56.0 5.6 %collective-permute-start.16 = (f32[16,640]{1,0:T(8,128)S(1)}, f32[16,640]{1,0:T(8,128)S(1)}, u32[]{:S(2)}, u32[]{:S(2)}) collective-permute-start(f32[16,640]{1,0:T(8,128)S(1)} %get-tuple-element.68), channel_id=1, source_target_pairs={{0,64},{32,96},{64,0},{96,32},{1,65},{33,97},{65,1},{97,33},{2,66}... | collective-permute-start | bytes 122888 | tf_op jit(solution)/shard_map/gather_image/ppermute | solution.py:22
  56.0 5.7 %collective-permute-start.15 = (f32[16,640]{1,0:T(8,128)S(1)}, f32[16,640]{1,0:T(8,128)S(1)}, u32[]{:S(2)}, u32[]{:S(2)}) collective-permute-start(f32[16,640]{1,0:T(8,128)S(1)} %get-tuple-element.68), channel_id=1, source_target_pairs={{0,32},{32,64},{64,96},{96,0},{1,33},{33,65},{65,97},{97,1},{2,34}... | collective-permute-start | bytes 122888 | tf_op jit(solution)/shard_map/gather_image/ppermute | solution.py:22
  61.7 1.5 %collective-permute-start.18 = (f32[16,2560]{1,0:T(8,128)S(1)}, f32[16,2560]{1,0:T(8,128)S(1)}, u32[]{:S(2)}, u32[]{:S(2)}) collective-permute-start(f32[16,2560]{1,0:T(8,128)S(1)} %pad_maximum_fusion), channel_id=1, source_target_pairs={{0,4},{4,0},{1,5},{5,1},{2,6},{6,2},{3,7},{7,3},{8,12},{12,8},{9,1... | collective-permute-start | bytes 491528 | tf_op jit(solution)/shard_map/gather_image/ppermute | solution.py:22
  65.7 1.4 %collective-permute-start.19 = (f32[16,2176]{1,0:T(8,128)S(1)}, f32[16,2176]{1,0:T(8,128)S(1)}, u32[]{:S(2)}, u32[]{:S(2)}) collective-permute-start(f32[16,2176]{1,0:T(8,128)S(1)} %get-tuple-element.71), channel_id=1, source_target_pairs={{0,4},{4,0},{1,5},{5,1},{2,6},{6,2},{3,7},{7,3},{8,12},{12,8},{9,1... | collective-permute-start | bytes 417800 | tf_op jit(solution)/shard_map/sum_over_yc/ppermute | solution.py:22
  67.2 5.3 %collective-permute-start.21 = (f32[16,640]{1,0:T(8,128)S(1)}, f32[16,640]{1,0:T(8,128)S(1)}, u32[]{:S(2)}, u32[]{:S(2)}) collective-permute-start(f32[16,640]{1,0:T(8,128)S(1)} %concatenate.44), channel_id=1, source_target_pairs={{0,32},{32,64},{64,96},{96,0},{1,33},{33,65},{65,97},{97,1},{2,34}... | collective-permute-start | bytes 122888 | tf_op jit(solution)/shard_map/sum_over_yc/ppermute | solution.py:22
  67.3 5.2 %collective-permute-start.20 = (f32[16,640]{1,0:T(8,128)S(1)}, f32[16,640]{1,0:T(8,128)S(1)}, u32[]{:S(2)}, u32[]{:S(2)}) collective-permute-start(f32[16,640]{1,0:T(8,128)S(1)} %get-tuple-element.123), channel_id=1, source_target_pairs={{0,96},{32,0},{64,32},{96,64},{1,97},{33,1},{65,33},{97,65},{2,98}... | collective-permute-start | bytes 122888 | tf_op jit(solution)/shard_map/sum_over_yc/ppermute | solution.py:22
  70.5 5.5 %collective-permute-start.22 = (f32[16,640]{1,0:T(8,128)S(1)}, f32[16,640]{1,0:T(8,128)S(1)}, u32[]{:S(2)}, u32[]{:S(2)}) collective-permute-start(f32[16,640]{1,0:T(8,128)S(1)} %get-tuple-element.124), channel_id=1, source_target_pairs={{0,64},{32,96},{64,0},{96,32},{1,65},{33,97},{65,1},{97,33},{2,66}... | collective-permute-start | bytes 122888 | tf_op jit(solution)/shard_map/sum_over_yc/ppermute | solution.py:22
  76.0 5.2 %collective-permute-start.25 = (f32[16,128]{1,0:T(8,128)S(1)}, f32[16,128]{1,0:T(8,128)S(1)}, u32[]{:S(2)}, u32[]{:S(2)}) collective-permute-start(f32[16,128]{1,0:T(8,128)S(1)} %slice_add_fusion.3), channel_id=1, source_target_pairs={{0,16},{8,24},{16,0},{24,8},{1,17},{9,25},{17,1},{25,9},{2,18},{10... | collective-permute-start | bytes 24584 | tf_op jit(solution)/shard_map/sum_sums_over_z/ppermute | solution.py:22
  77.8 3.7 %collective-permute-start.24 = (f32[16,128]{1,0:T(8,128)S(1)}, f32[16,128]{1,0:T(8,128)S(1)}, u32[]{:S(2)}, u32[]{:S(2)}) collective-permute-start(f32[16,128]{1,0:T(8,128)S(1)} %slice_add_fusion.3), channel_id=1, source_target_pairs={{0,24},{8,0},{16,8},{24,16},{1,25},{9,1},{17,9},{25,17},{2,26},{10... | collective-permute-start | bytes 24584 | tf_op jit(solution)/shard_map/sum_sums_over_z/ppermute | solution.py:22
  79.4 4.9 %collective-permute-start.23 = (f32[16,128]{1,0:T(8,128)S(1)}, f32[16,128]{1,0:T(8,128)S(1)}, u32[]{:S(2)}, u32[]{:S(2)}) collective-permute-start(f32[16,128]{1,0:T(8,128)S(1)} %slice_add_fusion.3), channel_id=1, source_target_pairs={{0,8},{8,16},{16,24},{24,0},{1,9},{9,17},{17,25},{25,1},{2,10},{10... | collective-permute-start | bytes 24584 | tf_op jit(solution)/shard_map/sum_sums_over_z/ppermute | solution.py:22

commit v5 on v3

--- a/solution.py
+++ b/solution.py
@@ -252,8 +252,8 @@
         far = []
         for axis, size, ahead, behind in (("z", NZ, row[1], row[3]), ("y", NY, col[0, 1], col[0, 3])):
             far.append((shift(ahead[:middle], axis, size, 1), shift(behind[middle:], axis, size, -1)))
-        for k in (1, 3):
-            col[1, k] = shift(col[0, k], "c", NC, 1)
+        pair = shift(jnp.concatenate([col[0, 1], col[0, 3]], axis=0), "c", NC, 1)
+        col[1, 1], col[1, 3] = pair[: 2 * middle], pair[2 * middle :]
         near = [row[k] for k in ROWS[:3]]
 
     with jax.named_scope("build_tiles"):

time: 80.2 us -> 76.2 us (0.950)
  waiting for transfers between devices: 33.2 us -> 28.3 us
  starting transfers between devices: 28.6 us -> 30.2 us
    ppermute x26 -> x25, waiting for transfers between devices: 33.2 us -> 28.3 us  [shift(): lax.ppermute(value, axis, [(i, (i + step) % size) for i in range(size)])]
    ppermute x26 -> x25, starting transfers between devices: 28.6 us -> 30.2 us  [shift(): lax.ppermute(value, axis, [(i, (i + step) % size) for i in range(size)])]
    unnamed x38 -> x36, local copies, waits for them, and re-layouts: 1.99 us -> 1.25 us
  transfers between devices with their start and end apart: 26 -> 25, of which waited for: 13 -> 13; matrix products, arithmetic and copies ran while one was open for 0% -> 0% of each run, Pallas kernels for 10% -> 10%
where the time goes in v5:
time: 76.2 us; the launch traced here: 76 us
  starting transfers between devices  30.2 us (40%)
  waiting for transfers between devices  28.3 us (37%)
  Pallas kernels  13.2 us (17%)
  between operations  1.78 us (2%)
  local copies, waits for them, and re-layouts  1.46 us (2%)
  other arithmetic  1.04 us (1%)
    ppermute x25, starting transfers between devices, shift(): lax.ppermute(value, axis, [(i, (i + step) % size) for i in range(size)])  30.2 us
    ppermute x25, waiting for transfers between devices, shift(): lax.ppermute(value, axis, [(i, (i + step) % size) for i in range(size)])  28.3 us
    pallas_call x5, Pallas kernels, build(): pl.pallas_call(functools.partial(tile_kernel, counts, probes), out_shape=...  10.3 us
    pallas_call x1, Pallas kernels, second_product(): pl.pallas_call(kernel, in_specs=[pl.BlockSpec(memory_space=pltpu.VMEM)] *...  2.49 us
  transfers between devices with their start and end apart: 25, of which 13 were waited for; matrix products, arithmetic and copies ran while one was open for 0% of the time, Pallas kernels for 10%

profile of v5, /device:TPU:0, one launch (start us, length us, event | category | flops | bytes accessed | tf_op | source)
XLA Modules:
  0.0 76.0 jit_solution(4904097943301889342)
XLA Ops:
  1.8 0.7 copy-done.1
  2.8 3.2 %collective-permute-start.4 = (bf16[608,256]{1,0:T(8,128)(2,1)S(1)}, bf16[608,256]{1,0:T(8,128)(2,1)S(1)}, u32[]{:S(2)}, u32[]{:S(2)}) collective-permute-start(bf16[608,256]{1,0:T(8,128)(2,1)S(1)} %pack.1.refs_0_.refs_3_.refs_1_), channel_id=1, source_target_pairs={{0,96},{32,0},{64,32},{96,64},{1,97},{33,1},{65,33},{97,65},{2,98}... | collective-permute-start | bytes 933896 | tf_op jit(solution)/shard_map/fetch_points/ppermute | solution.py:22
  6.0 4.0 %collective-permute-start.1 = (bf16[608,256]{1,0:T(8,128)(2,1)S(1)}, bf16[608,256]{1,0:T(8,128)(2,1)S(1)}, u32[]{:S(2)}, u32[]{:S(2)}) collective-permute-start(bf16[608,256]{1,0:T(8,128)(2,1)S(1)} %pack.1.refs_0_.refs_3_.refs_1_), channel_id=1, source_target_pairs={{0,24},{8,0},{16,8},{24,16},{1,25},{9,1},{17,9},{25,17},{2,26},{10... | collective-permute-start | bytes 933896 | tf_op jit(solution)/shard_map/fetch_points/ppermute | solution.py:22
  10.0 2.5 %collective-permute-done.4.refs_4_ = bf16[608,256]{1,0:T(8,128)(2,1)S(1)} collective-permute-done((bf16[608,256]{1,0:T(8,128)(2,1)S(1)}, bf16[608,256]{1,0:T(8,128)(2,1)S(1)}, u32[]{:S(2)}, u32[]{:S(2)}) %collective-permute-start.4) | collective-permute-done | bytes 311328 | tf_op jit(solution)/shard_map/fetch_points/ppermute | solution.py:22
  12.6 3.8 %collective-permute-start.9 = (bf16[304,256]{1,0:T(8,128)(2,1)S(1)}, bf16[304,256]{1,0:T(8,128)(2,1)S(1)}, u32[]{:S(2)}, u32[]{:S(2)}) collective-permute-start(bf16[304,256]{1,0:T(8,128)(2,1)S(1)} %slice.343), channel_id=1, source_target_pairs={{0,96},{32,0},{64,32},{96,64},{1,97},{33,1},{65,33},{97,65},{2,98}... | collective-permute-start | bytes 466952 | tf_op jit(solution)/shard_map/fetch_points/ppermute | solution.py:22
  16.5 0.8 %collective-permute-done.1.refs_2_ = bf16[608,256]{1,0:T(8,128)(2,1)S(1)} collective-permute-done((bf16[608,256]{1,0:T(8,128)(2,1)S(1)}, bf16[608,256]{1,0:T(8,128)(2,1)S(1)}, u32[]{:S(2)}, u32[]{:S(2)}) %collective-permute-start.1) | collective-permute-done | bytes 311328 | tf_op jit(solution)/shard_map/fetch_points/ppermute | solution.py:22
  17.3 3.8 %collective-permute-start.7 = (bf16[304,256]{1,0:T(8,128)(2,1)S(1)}, bf16[304,256]{1,0:T(8,128)(2,1)S(1)}, u32[]{:S(2)}, u32[]{:S(2)}) collective-permute-start(bf16[304,256]{1,0:T(8,128)(2,1)S(1)} %slice.341), channel_id=1, source_target_pairs={{0,24},{8,0},{16,8},{24,16},{1,25},{9,1},{17,9},{25,17},{2,26},{10... | collective-permute-start | bytes 466952 | tf_op jit(solution)/shard_map/fetch_points/ppermute | solution.py:22
  21.4 2.0 %build_tile.5 = (bf16[1536,1024]{1,0:T(8,128)(2,1)S(1)}, f32[16,1536]{1,0:T(8,128)S(1)}, f32[1536,1]{1,0:T(8,128)S(1)}) custom-call(bf16[608,256]{1,0:T(8,128)(2,1)S(1)} %pack.1.refs_0_.refs_3_.refs_1_, bf16[608,256]{1,0:T(8,128)(2,1)S(1)} %collective-permute-done.refs_1_, bf16[608,256]{1,0:T(8,128)(2,1)S(1)} %collective-permute-done.1.refs_2_, ...), custom_call_target="tpu_custom_call" | custom-call | flops 50331648 | bytes 1024 | tf_op jit(solution)/shard_map/build_tiles/build_tile/pallas_call | solution.py:135
  23.5 1.9 %build_tile.6 = (bf16[1536,1024]{1,0:T(8,128)(2,1)S(1)}, f32[16,1536]{1,0:T(8,128)S(1)}) custom-call(bf16[608,256]{1,0:T(8,128)(2,1)S(1)} %pack.1.refs_0_.refs_3_.refs_1_, bf16[608,256]{1,0:T(8,128)(2,1)S(1)} %collective-permute-done.refs_1_, bf16[608,256]{1,0:T(8,128)(2,1)S(1)} %collective-permute-done.1.refs_2_, ...), custom_call_target="tpu_custom_call" | custom-call | flops 50331648 | bytes 1024 | tf_op jit(solution)/shard_map/build_tiles/build_tile/pallas_call | solution.py:135
  25.5 1.9 %build_tile.7 = (bf16[1536,1024]{1,0:T(8,128)(2,1)S(1)}, f32[16,1536]{1,0:T(8,128)S(1)}) custom-call(bf16[608,256]{1,0:T(8,128)(2,1)S(1)} %pack.1.refs_0_.refs_3_.refs_1_, bf16[608,256]{1,0:T(8,128)(2,1)S(1)} %collective-permute-done.refs_1_, bf16[608,256]{1,0:T(8,128)(2,1)S(1)} %collective-permute-done.1.refs_2_, ...), custom_call_target="tpu_custom_call" | custom-call | flops 50331648 | bytes 1024 | tf_op jit(solution)/shard_map/build_tiles/build_tile/pallas_call | solution.py:135
  28.3 2.0 %build_tile.8 = (bf16[512,3072]{1,0:T(8,128)(2,1)S(1)}, f32[16,512]{1,0:T(8,128)S(1)}, f32[512,1]{1,0:T(8,128)S(1)}) custom-call(bf16[608,256]{1,0:T(8,128)(2,1)S(1)} %constant_dynamic-update-slice_fusion.refs_0_.refs_3_, bf16[608,256]{1,0:T(8,128)(2,1)S(1)} %pack.1.refs_0_.refs_3_.refs_1_, bf16[608,256]{1,0:T(8,128)(2,1)S(1)} %collective-permute-done.2.refs_4_.refs_2_, ...), custom_call_target="tpu_custom_call" | custom-call | flops 50331648 | bytes 1024 | tf_op jit(solution)/shard_map/build_tiles/build_tile/pallas_call | solution.py:135
  30.4 2.5 %build_tile.9 = (bf16[2048,1024]{1,0:T(8,128)(2,1)S(1)}, f32[16,2048]{1,0:T(8,128)S(1)}) custom-call(bf16[608,256]{1,0:T(8,128)(2,1)S(1)} %pack.1.refs_0_.refs_3_.refs_1_, bf16[608,256]{1,0:T(8,128)(2,1)S(1)} %collective-permute-done.refs_1_, bf16[608,256]{1,0:T(8,128)(2,1)S(1)} %collective-permute-done.1.refs_2_, ...), custom_call_target="tpu_custom_call" | custom-call | flops 67108864 | bytes 1024 | tf_op jit(solution)/shard_map/build_tiles/build_tile/pallas_call | solution.py:135
  32.9 3.2 %collective-permute-start.13 = (f32[16,2048]{1,0:T(8,128)S(1)}, f32[16,2048]{1,0:T(8,128)S(1)}, u32[]{:S(2)}, u32[]{:S(2)}) collective-permute-start(f32[16,2048]{1,0:T(8,128)S(1)} %get-tuple-element.40.refs_0_), channel_id=1, source_target_pairs={{0,24},{8,0},{16,8},{24,16},{1,25},{9,1},{17,9},{25,17},{2,26},{10... | collective-permute-start | bytes 393224 | tf_op jit(solution)/shard_map/sum_over_z/ppermute | solution.py:22
  36.1 0.9 %collective-permute-start.11 = (f32[16,2048]{1,0:T(8,128)S(1)}, f32[16,2048]{1,0:T(8,128)S(1)}, u32[]{:S(2)}, u32[]{:S(2)}) collective-permute-start(f32[16,2048]{1,0:T(8,128)S(1)} %get-tuple-element.40.refs_0_), channel_id=1, source_target_pairs={{0,8},{8,16},{16,24},{24,0},{1,9},{9,17},{17,25},{25,1},{2,10},{10... | collective-permute-start | bytes 393224 | tf_op jit(solution)/shard_map/sum_over_z/ppermute | solution.py:22
  37.1 4.8 %collective-permute-done.13.refs_3_ = f32[16,2048]{1,0:T(8,128)S(1)} collective-permute-done((f32[16,2048]{1,0:T(8,128)S(1)}, f32[16,2048]{1,0:T(8,128)S(1)}, u32[]{:S(2)}, u32[]{:S(2)}) %collective-permute-start.13) | collective-permute-done | bytes 131104 | tf_op jit(solution)/shard_map/sum_over_z/ppermute | solution.py:22
  41.9 2.2 %collective-permute-done.12.refs_2_ = f32[16,2048]{1,0:T(8,128)S(1)} collective-permute-done((f32[16,2048]{1,0:T(8,128)S(1)}, f32[16,2048]{1,0:T(8,128)S(1)}, u32[]{:S(2)}, u32[]{:S(2)}) %collective-permute-start.12) | collective-permute-done | bytes 131104 | tf_op jit(solution)/shard_map/sum_over_z/ppermute | solution.py:22
  44.0 1.3 %collective-permute-done.11.refs_1_ = f32[16,2048]{1,0:T(8,128)S(1)} collective-permute-done((f32[16,2048]{1,0:T(8,128)S(1)}, f32[16,2048]{1,0:T(8,128)S(1)}, u32[]{:S(2)}, u32[]{:S(2)}) %collective-permute-start.11) | collective-permute-done | bytes 131104 | tf_op jit(solution)/shard_map/sum_over_z/ppermute | solution.py:22
  45.5 1.2 %collective-permute-done.14 = f32[16,640]{1,0:T(8,128)S(1)} collective-permute-done((f32[16,640]{1,0:T(8,128)S(1)}, f32[16,640]{1,0:T(8,128)S(1)}, u32[]{:S(2)}, u32[]{:S(2)}) %collective-permute-start.14) | collective-permute-done | bytes 40992 | tf_op jit(solution)/shard_map/gather_image/ppermute | solution.py:22
  46.7 2.2 %collective-permute-start.17 = (f32[32,640]{1,0:T(8,128)S(1)}, f32[32,640]{1,0:T(8,128)S(1)}, u32[]{:S(2)}, u32[]{:S(2)}) collective-permute-start(f32[32,640]{1,0:T(8,128)S(1)} %constant_dynamic-update-slice_fusion.20), channel_id=1, source_target_pairs={{0,64},{32,96},{64,0},{96,32},{1,65},{33,97},{65,1},{97,33},{2,66}... | collective-permute-start | bytes 245768 | tf_op jit(solution)/shard_map/gather_image/ppermute | solution.py:22
  48.9 1.1 %collective-permute-start.16 = (f32[32,640]{1,0:T(8,128)S(1)}, f32[32,640]{1,0:T(8,128)S(1)}, u32[]{:S(2)}, u32[]{:S(2)}) collective-permute-start(f32[32,640]{1,0:T(8,128)S(1)} %constant_dynamic-update-slice_fusion.20), channel_id=1, source_target_pairs={{0,96},{32,0},{64,32},{96,64},{1,97},{33,1},{65,33},{97,65},{2,98}... | collective-permute-start | bytes 245768 | tf_op jit(solution)/shard_map/gather_image/ppermute | solution.py:22
  50.0 0.9 %collective-permute-start.15 = (f32[32,640]{1,0:T(8,128)S(1)}, f32[32,640]{1,0:T(8,128)S(1)}, u32[]{:S(2)}, u32[]{:S(2)}) collective-permute-start(f32[32,640]{1,0:T(8,128)S(1)} %constant_dynamic-update-slice_fusion.20), channel_id=1, source_target_pairs={{0,32},{32,64},{64,96},{96,0},{1,33},{33,65},{65,97},{97,1},{2,34}... | collective-permute-start | bytes 245768 | tf_op jit(solution)/shard_map/gather_image/ppermute | solution.py:22
  50.9 4.7 %collective-permute-done.15 = f32[32,640]{1,0:T(8,128)S(1)} collective-permute-done((f32[32,640]{1,0:T(8,128)S(1)}, f32[32,640]{1,0:T(8,128)S(1)}, u32[]{:S(2)}, u32[]{:S(2)}) %collective-permute-start.15) | collective-permute-done | bytes 81952 | tf_op jit(solution)/shard_map/gather_image/ppermute | solution.py:22
  55.7 2.5 %second_product.1 = (f32[16,2176]{1,0:T(8,128)S(1)}, f32[16,2176]{1,0:T(8,128)S(1)}, f32[3,16,512]{2,1,0:T(8,128)S(1)}) custom-call(bf16[1536,1024]{1,0:T(8,128)(2,1)S(1)} %get-tuple-element.24.refs_0_, bf16[1536,1024]{1,0:T(8,128)(2,1)S(1)} %get-tuple-element.27.refs_1_, bf16[1536,1024]{1,0:T(8,128)(2,1)S(1)} %get-tuple-element.29.refs_2_, ...), custom_call_target="tpu_custom_call" | custom-call | flops 268435456 | bytes 1024 | tf_op jit(solution)/shard_map/second_product/pallas_call | solution.py:226
  58.3 1.3 %collective-permute-done.18 = f32[16,2176]{1,0:T(8,128)S(1)} collective-permute-done((f32[16,2176]{1,0:T(8,128)S(1)}, f32[16,2176]{1,0:T(8,128)S(1)}, u32[]{:S(2)}, u32[]{:S(2)}) %collective-permute-start.18) | collective-permute-done | bytes 139296 | tf_op jit(solution)/shard_map/sum_over_yc/ppermute | solution.py:22
  59.8 3.2 %collective-permute-start.19 = (f32[16,640]{1,0:T(8,128)S(1)}, f32[16,640]{1,0:T(8,128)S(1)}, u32[]{:S(2)}, u32[]{:S(2)}) collective-permute-start(f32[16,640]{1,0:T(8,128)S(1)} %get-tuple-element.99), channel_id=1, source_target_pairs={{0,96},{32,0},{64,32},{96,64},{1,97},{33,1},{65,33},{97,65},{2,98}... | collective-permute-start | bytes 122888 | tf_op jit(solution)/shard_map/sum_over_yc/ppermute | solution.py:22
  63.4 1.5 %collective-permute-done.20 = f32[16,640]{1,0:T(8,128)S(1)} collective-permute-done((f32[16,640]{1,0:T(8,128)S(1)}, f32[16,640]{1,0:T(8,128)S(1)}, u32[]{:S(2)}, u32[]{:S(2)}) %collective-permute-start.20) | collective-permute-done | bytes 40992 | tf_op jit(solution)/shard_map/sum_over_yc/ppermute | solution.py:22
  65.0 3.5 %collective-permute-done.21 = f32[16,640]{1,0:T(8,128)S(1)} collective-permute-done((f32[16,640]{1,0:T(8,128)S(1)}, f32[16,640]{1,0:T(8,128)S(1)}, u32[]{:S(2)}, u32[]{:S(2)}) %collective-permute-start.21) | collective-permute-done | bytes 40992 | tf_op jit(solution)/shard_map/sum_over_yc/ppermute | solution.py:22
  69.1 1.2 %collective-permute-start.23 = (f32[16,128]{1,0:T(8,128)S(1)}, f32[16,128]{1,0:T(8,128)S(1)}, u32[]{:S(2)}, u32[]{:S(2)}) collective-permute-start(f32[16,128]{1,0:T(8,128)S(1)} %slice_add_fusion.3), channel_id=1, source_target_pairs={{0,24},{8,0},{16,8},{24,16},{1,25},{9,1},{17,9},{25,17},{2,26},{10... | collective-permute-start | bytes 24584 | tf_op jit(solution)/shard_map/sum_sums_over_z/ppermute | solution.py:22
  70.2 0.9 %collective-permute-start.22 = (f32[16,128]{1,0:T(8,128)S(1)}, f32[16,128]{1,0:T(8,128)S(1)}, u32[]{:S(2)}, u32[]{:S(2)}) collective-permute-start(f32[16,128]{1,0:T(8,128)S(1)} %slice_add_fusion.3), channel_id=1, source_target_pairs={{0,8},{8,16},{16,24},{24,0},{1,9},{9,17},{17,25},{25,1},{2,10},{10... | collective-permute-start | bytes 24584 | tf_op jit(solution)/shard_map/sum_sums_over_z/ppermute | solution.py:22
  71.1 2.6 %collective-permute-done.24 = f32[16,128]{1,0:T(8,128)S(1)} collective-permute-done((f32[16,128]{1,0:T(8,128)S(1)}, f32[16,128]{1,0:T(8,128)S(1)}, u32[]{:S(2)}, u32[]{:S(2)}) %collective-permute-start.24) | collective-permute-done | bytes 8224 | tf_op jit(solution)/shard_map/sum_sums_over_z/ppermute | solution.py:22
  73.7 1.4 %collective-permute-done.22 = f32[16,128]{1,0:T(8,128)S(1)} collective-permute-done((f32[16,128]{1,0:T(8,128)S(1)}, f32[16,128]{1,0:T(8,128)S(1)}, u32[]{:S(2)}, u32[]{:S(2)}) %collective-permute-start.22) | collective-permute-done | bytes 8224 | tf_op jit(solution)/shard_map/sum_sums_over_z/ppermute | solution.py:22
  75.3 0.7 fusion.3
  (87 shorter events, 3.7 us)
Async XLA Ops:
  0.6 1.1 %copy-start = (bf16[1024,256]{1,0:T(8,128)(2,1)S(1)}, bf16[1024,256]{1,0:T(8,128)(2,1)}, u32[]{:S(2)}) copy-start(bf16[1024,256]{1,0:T(8,128)(2,1)} %param.3) | copy-start | bytes 1572868
  0.6 20.7 %copy-start.2 = (f32[512,16]{0,1:T(8,128)S(1)}, f32[512,16]{0,1:T(8,128)}, u32[]{:S(2)}) copy-start(f32[512,16]{0,1:T(8,128)} %param.5) | copy-start | bytes 98308
  1.8 0.8 %copy-start.1 = (f32[512,16]{0,1:T(8,128)S(1)}, f32[512,16]{0,1:T(8,128)}, u32[]{:S(2)}) copy-start(f32[512,16]{0,1:T(8,128)} %param.5) | copy-start | bytes 98308
  2.8 9.8 %collective-permute-start.4 = (bf16[608,256]{1,0:T(8,128)(2,1)S(1)}, bf16[608,256]{1,0:T(8,128)(2,1)S(1)}, u32[]{:S(2)}, u32[]{:S(2)}) collective-permute-start(bf16[608,256]{1,0:T(8,128)(2,1)S(1)} %pack.1.refs_0_.refs_3_.refs_1_), channel_id=1, source_target_pairs={{0,96},{32,0},{64,32},{96,64},{1,97},{33,1},{65,33},{97,65},{2,98}... | collective-permute-start | bytes 933896 | tf_op jit(solution)/shard_map/fetch_points/ppermute | solution.py:22
  6.0 10.4 %collective-permute-start.3 = (bf16[608,256]{1,0:T(8,128)(2,1)S(1)}, bf16[608,256]{1,0:T(8,128)(2,1)S(1)}, u32[]{:S(2)}, u32[]{:S(2)}) collective-permute-start(bf16[608,256]{1,0:T(8,128)(2,1)S(1)} %pack.1.refs_0_.refs_3_.refs_1_), channel_id=1, source_target_pairs={{0,32},{32,64},{64,96},{96,0},{1,33},{33,65},{65,97},{97,1},{2,34}... | collective-permute-start | bytes 933896 | tf_op jit(solution)/shard_map/fetch_points/ppermute | solution.py:22
  6.0 15.3 %collective-permute-start.2 = (bf16[608,256]{1,0:T(8,128)(2,1)S(1)}, bf16[608,256]{1,0:T(8,128)(2,1)S(1)}, u32[]{:S(2)}, u32[]{:S(2)}) collective-permute-start(bf16[608,256]{1,0:T(8,128)(2,1)S(1)} %pack.1.refs_0_.refs_3_.refs_1_), channel_id=1, source_target_pairs={{0,4},{4,0},{1,5},{5,1},{2,6},{6,2},{3,7},{7,3},{8,12},{12,8},{9,1... | collective-permute-start | bytes 933896 | tf_op jit(solution)/shard_map/fetch_points/ppermute | solution.py:22
  6.0 11.3 %collective-permute-start.1 = (bf16[608,256]{1,0:T(8,128)(2,1)S(1)}, bf16[608,256]{1,0:T(8,128)(2,1)S(1)}, u32[]{:S(2)}, u32[]{:S(2)}) collective-permute-start(bf16[608,256]{1,0:T(8,128)(2,1)S(1)} %pack.1.refs_0_.refs_3_.refs_1_), channel_id=1, source_target_pairs={{0,24},{8,0},{16,8},{24,16},{1,25},{9,1},{17,9},{25,17},{2,26},{10... | collective-permute-start | bytes 933896 | tf_op jit(solution)/shard_map/fetch_points/ppermute | solution.py:22
  10.0 11.1 %collective-permute-start = (bf16[608,256]{1,0:T(8,128)(2,1)S(1)}, bf16[608,256]{1,0:T(8,128)(2,1)S(1)}, u32[]{:S(2)}, u32[]{:S(2)}) collective-permute-start(bf16[608,256]{1,0:T(8,128)(2,1)S(1)} %pack.1.refs_0_.refs_3_.refs_1_), channel_id=1, source_target_pairs={{0,8},{8,16},{16,24},{24,0},{1,9},{9,17},{17,25},{25,1},{2,10},{10... | collective-permute-start | bytes 933896 | tf_op jit(solution)/shard_map/fetch_points/ppermute | solution.py:22
  12.6 14.8 %collective-permute-start.9 = (bf16[304,256]{1,0:T(8,128)(2,1)S(1)}, bf16[304,256]{1,0:T(8,128)(2,1)S(1)}, u32[]{:S(2)}, u32[]{:S(2)}) collective-permute-start(bf16[304,256]{1,0:T(8,128)(2,1)S(1)} %slice.343), channel_id=1, source_target_pairs={{0,96},{32,0},{64,32},{96,64},{1,97},{33,1},{65,33},{97,65},{2,98}... | collective-permute-start | bytes 466952 | tf_op jit(solution)/shard_map/fetch_points/ppermute | solution.py:22
  16.4 11.0 %collective-permute-start.8 = (bf16[304,256]{1,0:T(8,128)(2,1)S(1)}, bf16[304,256]{1,0:T(8,128)(2,1)S(1)}, u32[]{:S(2)}, u32[]{:S(2)}) collective-permute-start(bf16[304,256]{1,0:T(8,128)(2,1)S(1)} %slice.342), channel_id=1, source_target_pairs={{0,32},{32,64},{64,96},{96,0},{1,33},{33,65},{65,97},{97,1},{2,34}... | collective-permute-start | bytes 466952 | tf_op jit(solution)/shard_map/fetch_points/ppermute | solution.py:22
  17.3 10.1 %collective-permute-start.7 = (bf16[304,256]{1,0:T(8,128)(2,1)S(1)}, bf16[304,256]{1,0:T(8,128)(2,1)S(1)}, u32[]{:S(2)}, u32[]{:S(2)}) collective-permute-start(bf16[304,256]{1,0:T(8,128)(2,1)S(1)} %slice.341), channel_id=1, source_target_pairs={{0,24},{8,0},{16,8},{24,16},{1,25},{9,1},{17,9},{25,17},{2,26},{10... | collective-permute-start | bytes 466952 | tf_op jit(solution)/shard_map/fetch_points/ppermute | solution.py:22
  21.1 6.7 %collective-permute-start.6 = (bf16[304,256]{1,0:T(8,128)(2,1)S(1)}, bf16[304,256]{1,0:T(8,128)(2,1)S(1)}, u32[]{:S(2)}, u32[]{:S(2)}) collective-permute-start(bf16[304,256]{1,0:T(8,128)(2,1)S(1)} %slice.340), channel_id=1, source_target_pairs={{0,8},{8,16},{16,24},{24,0},{1,9},{9,17},{17,25},{25,1},{2,10},{10... | collective-permute-start | bytes 466952 | tf_op jit(solution)/shard_map/fetch_points/ppermute | solution.py:22
  21.2 4.1 %collective-permute-start.5 = (bf16[1216,256]{1,0:T(8,128)(2,1)S(1)}, bf16[1216,256]{1,0:T(8,128)(2,1)S(1)}, u32[]{:S(2)}, u32[]{:S(2)}) collective-permute-start(bf16[1216,256]{1,0:T(8,128)(2,1)S(1)} %pad_maximum_fusion), channel_id=1, source_target_pairs={{0,4},{4,0},{1,5},{5,1},{2,6},{6,2},{3,7},{7,3},{8,12},{12,8},{9,1... | collective-permute-start | bytes 1867784 | tf_op jit(solution)/shard_map/fetch_points/ppermute | solution.py:22
  27.8 2.6 %collective-permute-start.10 = (bf16[608,256]{1,0:T(8,128)(2,1)S(1)}, bf16[608,256]{1,0:T(8,128)(2,1)S(1)}, u32[]{:S(2)}, u32[]{:S(2)}) collective-permute-start(bf16[608,256]{1,0:T(8,128)(2,1)S(1)} %constant_dynamic-update-slice_fusion.2.refs_4_), channel_id=1, source_target_pairs={{0,4},{4,0},{1,5},{5,1},{2,6},{6,2},{3,7},{7,3},{8,12},{12,8},{9,1... | collective-permute-start | bytes 933896 | tf_op jit(solution)/shard_map/build_tiles/ppermute | solution.py:22
  32.9 9.0 %collective-permute-start.13 = (f32[16,2048]{1,0:T(8,128)S(1)}, f32[16,2048]{1,0:T(8,128)S(1)}, u32[]{:S(2)}, u32[]{:S(2)}) collective-permute-start(f32[16,2048]{1,0:T(8,128)S(1)} %get-tuple-element.40.refs_0_), channel_id=1, source_target_pairs={{0,24},{8,0},{16,8},{24,16},{1,25},{9,1},{17,9},{25,17},{2,26},{10... | collective-permute-start | bytes 393224 | tf_op jit(solution)/shard_map/sum_over_z/ppermute | solution.py:22
  36.1 7.9 %collective-permute-start.12 = (f32[16,2048]{1,0:T(8,128)S(1)}, f32[16,2048]{1,0:T(8,128)S(1)}, u32[]{:S(2)}, u32[]{:S(2)}) collective-permute-start(f32[16,2048]{1,0:T(8,128)S(1)} %get-tuple-element.40.refs_0_), channel_id=1, source_target_pairs={{0,16},{8,24},{16,0},{24,8},{1,17},{9,25},{17,1},{25,9},{2,18},{10... | collective-permute-start | bytes 393224 | tf_op jit(solution)/shard_map/sum_over_z/ppermute | solution.py:22
  36.1 9.2 %collective-permute-start.11 = (f32[16,2048]{1,0:T(8,128)S(1)}, f32[16,2048]{1,0:T(8,128)S(1)}, u32[]{:S(2)}, u32[]{:S(2)}) collective-permute-start(f32[16,2048]{1,0:T(8,128)S(1)} %get-tuple-element.40.refs_0_), channel_id=1, source_target_pairs={{0,8},{8,16},{16,24},{24,0},{1,9},{9,17},{17,25},{25,1},{2,10},{10... | collective-permute-start | bytes 393224 | tf_op jit(solution)/shard_map/sum_over_z/ppermute | solution.py:22
  45.4 1.3 %collective-permute-start.14 = (f32[16,640]{1,0:T(8,128)S(1)}, f32[16,640]{1,0:T(8,128)S(1)}, u32[]{:S(2)}, u32[]{:S(2)}) collective-permute-start(f32[16,640]{1,0:T(8,128)S(1)} %get-tuple-element.42), channel_id=1, source_target_pairs={{0,4},{4,0},{1,5},{5,1},{2,6},{6,2},{3,7},{7,3},{8,12},{12,8},{9,1... | collective-permute-start | bytes 122888 | tf_op jit(solution)/shard_map/gather_image/ppermute | solution.py:22
  46.7 9.0 %collective-permute-start.17 = (f32[32,640]{1,0:T(8,128)S(1)}, f32[32,640]{1,0:T(8,128)S(1)}, u32[]{:S(2)}, u32[]{:S(2)}) collective-permute-start(f32[32,640]{1,0:T(8,128)S(1)} %constant_dynamic-update-slice_fusion.20), channel_id=1, source_target_pairs={{0,64},{32,96},{64,0},{96,32},{1,65},{33,97},{65,1},{97,33},{2,66}... | collective-permute-start | bytes 245768 | tf_op jit(solution)/shard_map/gather_image/ppermute | solution.py:22
  48.9 6.8 %collective-permute-start.16 = (f32[32,640]{1,0:T(8,128)S(1)}, f32[32,640]{1,0:T(8,128)S(1)}, u32[]{:S(2)}, u32[]{:S(2)}) collective-permute-start(f32[32,640]{1,0:T(8,128)S(1)} %constant_dynamic-update-slice_fusion.20), channel_id=1, source_target_pairs={{0,96},{32,0},{64,32},{96,64},{1,97},{33,1},{65,33},{97,65},{2,98}... | collective-permute-start | bytes 245768 | tf_op jit(solution)/shard_map/gather_image/ppermute | solution.py:22
  50.0 5.7 %collective-permute-start.15 = (f32[32,640]{1,0:T(8,128)S(1)}, f32[32,640]{1,0:T(8,128)S(1)}, u32[]{:S(2)}, u32[]{:S(2)}) collective-permute-start(f32[32,640]{1,0:T(8,128)S(1)} %constant_dynamic-update-slice_fusion.20), channel_id=1, source_target_pairs={{0,32},{32,64},{64,96},{96,0},{1,33},{33,65},{65,97},{97,1},{2,34}... | collective-permute-start | bytes 245768 | tf_op jit(solution)/shard_map/gather_image/ppermute | solution.py:22
  58.2 1.4 %collective-permute-start.18 = (f32[16,2176]{1,0:T(8,128)S(1)}, f32[16,2176]{1,0:T(8,128)S(1)}, u32[]{:S(2)}, u32[]{:S(2)}) collective-permute-start(f32[16,2176]{1,0:T(8,128)S(1)} %get-tuple-element.45), channel_id=1, source_target_pairs={{0,4},{4,0},{1,5},{5,1},{2,6},{6,2},{3,7},{7,3},{8,12},{12,8},{9,1... | collective-permute-start | bytes 417800 | tf_op jit(solution)/shard_map/sum_over_yc/ppermute | solution.py:22
  59.7 5.3 %collective-permute-start.20 = (f32[16,640]{1,0:T(8,128)S(1)}, f32[16,640]{1,0:T(8,128)S(1)}, u32[]{:S(2)}, u32[]{:S(2)}) collective-permute-start(f32[16,640]{1,0:T(8,128)S(1)} %concatenate.48), channel_id=1, source_target_pairs={{0,32},{32,64},{64,96},{96,0},{1,33},{33,65},{65,97},{97,1},{2,34}... | collective-permute-start | bytes 122888 | tf_op jit(solution)/shard_map/sum_over_yc/ppermute | solution.py:22
  59.8 5.2 %collective-permute-start.19 = (f32[16,640]{1,0:T(8,128)S(1)}, f32[16,640]{1,0:T(8,128)S(1)}, u32[]{:S(2)}, u32[]{:S(2)}) collective-permute-start(f32[16,640]{1,0:T(8,128)S(1)} %get-tuple-element.99), channel_id=1, source_target_pairs={{0,96},{32,0},{64,32},{96,64},{1,97},{33,1},{65,33},{97,65},{2,98}... | collective-permute-start | bytes 122888 | tf_op jit(solution)/shard_map/sum_over_yc/ppermute | solution.py:22
  63.0 5.5 %collective-permute-start.21 = (f32[16,640]{1,0:T(8,128)S(1)}, f32[16,640]{1,0:T(8,128)S(1)}, u32[]{:S(2)}, u32[]{:S(2)}) collective-permute-start(f32[16,640]{1,0:T(8,128)S(1)} %get-tuple-element.100), channel_id=1, source_target_pairs={{0,64},{32,96},{64,0},{96,32},{1,65},{33,97},{65,1},{97,33},{2,66}... | collective-permute-start | bytes 122888 | tf_op jit(solution)/shard_map/sum_over_yc/ppermute | solution.py:22
  68.5 5.2 %collective-permute-start.24 = (f32[16,128]{1,0:T(8,128)S(1)}, f32[16,128]{1,0:T(8,128)S(1)}, u32[]{:S(2)}, u32[]{:S(2)}) collective-permute-start(f32[16,128]{1,0:T(8,128)S(1)} %slice_add_fusion.3), channel_id=1, source_target_pairs={{0,16},{8,24},{16,0},{24,8},{1,17},{9,25},{17,1},{25,9},{2,18},{10... | collective-permute-start | bytes 24584 | tf_op jit(solution)/shard_map/sum_sums_over_z/ppermute | solution.py:22
  69.1 4.6 %collective-permute-start.23 = (f32[16,128]{1,0:T(8,128)S(1)}, f32[16,128]{1,0:T(8,128)S(1)}, u32[]{:S(2)}, u32[]{:S(2)}) collective-permute-start(f32[16,128]{1,0:T(8,128)S(1)} %slice_add_fusion.3), channel_id=1, source_target_pairs={{0,24},{8,0},{16,8},{24,16},{1,25},{9,1},{17,9},{25,17},{2,26},{10... | collective-permute-start | bytes 24584 | tf_op jit(solution)/shard_map/sum_sums_over_z/ppermute | solution.py:22
  70.2 4.9 %collective-permute-start.22 = (f32[16,128]{1,0:T(8,128)S(1)}, f32[16,128]{1,0:T(8,128)S(1)}, u32[]{:S(2)}, u32[]{:S(2)}) collective-permute-start(f32[16,128]{1,0:T(8,128)S(1)} %slice_add_fusion.3), channel_id=1, source_target_pairs={{0,8},{8,16},{16,24},{24,0},{1,9},{9,17},{17,25},{25,1},{2,10},{10... | collective-permute-start | bytes 24584 | tf_op jit(solution)/shard_map/sum_sums_over_z/ppermute | solution.py:22

commit v6 on v5

v6 whole, which is shorter than its diff:
```python
import functools

import jax
import jax.numpy as jnp
from jax import lax
from jax.experimental import pallas as pl
from jax.experimental.pallas import tpu as pltpu
from jax.sharding import Mesh
from jax.sharding import PartitionSpec as P

NY, NZ, NC, NX = 4, 4, 2, 4
LANES = 128
CHUNK = 256
ROWS = (0, 1, 3, 2)
COLS = ((0, 0), (1, 0), (0, 1), (0, 3), (1, 1), (1, 3), (0, 2), (1, 2))

noise_level = 1.0
kernel_rate = 0.5
STEP = 1.0 / (1.0 + noise_level)


def shift(value, axis, size, step):
    return lax.ppermute(value, axis, [(i, (i + step) % size) for i in range(size)])


def split(value):
    high = value.astype(jnp.bfloat16)
    rest = value - high.astype(jnp.float32)
    middle = rest.astype(jnp.bfloat16)
    return high, middle, (rest - middle.astype(jnp.float32)).astype(jnp.bfloat16)


def pack_kernel(points_ref, side_ref, out_ref):
    own, width = points_ref.shape
    probes = side_ref.shape[0]
    out_ref[:own, :] = points_ref[...]
    high, middle, _ = split(points_ref[...].astype(jnp.float32) ** 2)
    ones = jnp.ones((probes, width), jnp.bfloat16)
    norms = 0.0
    for term in (high, middle):
        norms = norms + lax.dot_general(ones, term, (((1,), (1,)), ((), ())), preferred_element_type=jnp.float32)
    high, middle, low = split(norms)
    row = lax.broadcasted_iota(jnp.int32, norms.shape, 0)
    norms = jnp.where(row == 0, high.astype(jnp.float32), jnp.where(row == 1, middle.astype(jnp.float32), low.astype(jnp.float32)))
    at = own
    for part in (side_ref[...].astype(jnp.bfloat16), norms.astype(jnp.bfloat16)):
        for j in range(own // width):
            out_ref[at : at + probes, :] = part[:, j * width : (j + 1) * width]
            at += probes


def pack(points, side):
    own, width = points.shape
    extra = side.shape[0] * 2 * own // width
    return pl.pallas_call(
        pack_kernel,
        out_shape=jax.ShapeDtypeStruct((own + extra, width), jnp.bfloat16),
        compiler_params=pltpu.CompilerParams(vmem_limit_bytes=8 << 20),
        name="pack",
    )(points, side)


def unpack_rows(message, probes, own, term):
    width = message.shape[1]
    count = own // width
    at = own + term * count * probes
    return jnp.concatenate([message[at + j * probes : at + (j + 1) * probes] for j in range(count)], axis=1)


def tile_kernel(counts, probes, *refs):
    rows_count, cols_count, known_halves, prior_count, has_side = counts
    refs = list(refs)
    row_refs = [refs.pop(0) for _ in range(rows_count)]
    col_refs = [refs.pop(0) for _ in range(cols_count)]
    half_refs = [refs.pop(0) for _ in range(known_halves)]
    prior_refs = [refs.pop(0) for _ in range(prior_count)]
    side_ref = refs.pop(0) if has_side else None
    tile_ref, image_ref = refs.pop(0), refs.pop(0)
    own = tile_ref.shape[0] // rows_count
    if known_halves:
        pieces = []
        for half_ref in half_refs:
            pieces += [half_ref[j * own : (j + 1) * own, :] for j in range(half_ref.shape[0] // own)]
        halves = pieces
    else:
        new_ref = refs.pop(0)
        halves = []
        for i, row_ref in enumerate(row_refs):
            squares = row_ref[:own, :].astype(jnp.float32) ** 2
            halves.append(-kernel_rate * jnp.sum(squares, axis=1, keepdims=True))
            new_ref[i * own : (i + 1) * own, :] = halves[-1]
    if prior_count:
        at = 0
        for prior_ref in prior_refs:
            image_ref[:, at : at + prior_ref.shape[1]] = prior_ref[...]
            at += prior_ref.shape[1]
    else:
        image_ref[...] = jnp.zeros_like(image_ref)
        if has_side:
            image_ref[:, :own] = (noise_level - 1.0 / STEP) * side_ref[...]
    for j, col_ref in enumerate(col_refs):
        field = unpack_rows(col_ref, probes, own, 0)
        norms = unpack_rows(col_ref, probes, own, 1).astype(jnp.float32)
        col_half = -kernel_rate * (norms[0:1] + norms[1:2] + norms[2:3])
        for i, row_ref in enumerate(row_refs):
            for k in range(own // CHUNK):
                part = slice(k * CHUNK, (k + 1) * CHUNK)
                place = slice(i * own + k * CHUNK, i * own + (k + 1) * CHUNK)
                cross = lax.dot_general(
                    row_ref[part, :], col_ref[:own, :], (((1,), (1,)), ((), ())), preferred_element_type=jnp.float32
                )
                kern = jnp.exp(2.0 * kernel_rate * cross + halves[i][part, :] + col_half).astype(jnp.bfloat16)
                tile_ref[place, j * own : (j + 1) * own] = kern
                image_ref[:, place] += lax.dot_general(
                    field, kern, (((1,), (1,)), ((), ())), preferred_element_type=jnp.float32
                )


def build(rows, cols, own, probes, halves=(), prior=(), side=None):
    features = rows[0].shape[1]
    height, width = len(rows) * own, len(cols) * own
    counts = (len(rows), len(cols), len(halves), len(prior), side is not None)
    out_shape = [
        pltpu.VMEM((height, width), jnp.bfloat16),
        jax.ShapeDtypeStruct((probes, height), jnp.float32),
    ]
    if not halves:
        out_shape.append(jax.ShapeDtypeStruct((height, 1), jnp.float32))
    args = [*rows, *cols, *halves, *prior] + ([] if side is None else [side])
    return pl.pallas_call(
        functools.partial(tile_kernel, counts, probes),
        out_shape=out_shape,
        compiler_params=pltpu.CompilerParams(vmem_limit_bytes=16 << 20),
        cost_estimate=pl.CostEstimate(
            flops=height * width * features // 8, bytes_accessed=1 << 10, transcendentals=0
        ),
        name="build_tile",
    )(*args)


def second_kernel(own, places, *refs):
    parts, refs = refs[:NZ], refs[NZ:]
    tiles, (mine_ref, other_ref, rho_ref) = refs[: len(places)], refs[len(places) :]
    probes = rho_ref.shape[0]
    pieces = []
    for p in ROWS:
        piece = 0.0
        for s in range(NZ):
            at = ROWS.index((p - s) % NZ) * own
            piece = piece + parts[s][:, at : at + own]
        pieces.append(-STEP * piece)
    rho_ref[...] = pieces[0]
    rho = jnp.concatenate(pieces, axis=1)
    high, low, _ = split(rho)
    narrow = jnp.concatenate([high, low], axis=0)
    for j, (h, m) in enumerate(COLS):
        part = 0.0
        for tile_ref, (top, left) in zip(tiles, places):
            at = j * own - left
            if 0 <= at < tile_ref.shape[1]:
                part = part + jnp.dot(
                    narrow[:, top : top + tile_ref.shape[0]],
                    tile_ref[:, at : at + own],
                    preferred_element_type=jnp.float32,
                )
        (other_ref if h else mine_ref)[:, m * own : (m + 1) * own] = part[:probes] + part[probes:]


def second_product(tiles, parts, own):
    probes, rows = parts[0].shape
    cols = len(COLS) * own
    places = [(top, left) for _, top, left in tiles]
    return pl.pallas_call(
        functools.partial(second_kernel, own, places),
        in_specs=[pl.BlockSpec(memory_space=pltpu.VMEM)] * (NZ + len(tiles)),
        out_shape=[
            jax.ShapeDtypeStruct((probes, cols // NC), jnp.float32),
            jax.ShapeDtypeStruct((probes, cols // NC), jnp.float32),
            jax.ShapeDtypeStruct((probes, own), jnp.float32),
        ],
        compiler_params=pltpu.CompilerParams(vmem_limit_bytes=16 << 20),
        cost_estimate=pl.CostEstimate(flops=rows * cols * 32, bytes_accessed=1 << 10, transcendentals=0),
        name="second_product",
    )(*parts, *[tile for tile, _, _ in tiles])


def sums_kernel(side_ref, rho_ref, *refs):
    shares, (image_ref, sums_ref) = refs[:NY], refs[NY:]
    side, rho = side_ref[...], rho_ref[...]
    image = noise_level * rho
    for share in shares:
        image = image + share[...]
    image_ref[...] = image
    total = lambda a, b: jnp.sum(a * b, axis=1, keepdims=True)
    lane = lax.broadcasted_iota(jnp.int32, (side.shape[0], LANES), 1)
    sums = 0.0
    for k, one in enumerate((total(side, side), total(side, rho), total(rho, rho), total(rho, image))):
        sums = jnp.where(lane == k, one, sums)
    sums_ref[...] = jnp.pad(sums.T[:8], ((0, 0), (0, LANES - side.shape[0])))


def local_sums(side, rho, shares):
    return pl.pallas_call(
        sums_kernel,
        out_shape=[
            jax.ShapeDtypeStruct(side.shape, jnp.float32),
            jax.ShapeDtypeStruct((8, LANES), jnp.float32),
        ],
        compiler_params=pltpu.CompilerParams(vmem_limit_bytes=4 << 20),
        name="local_sums",
    )(side, rho, *shares)


def finish_kernel(side_ref, rho_ref, image_ref, sums_ref, field_ref, residual_ref):
    side, rho, image = side_ref[...], rho_ref[...], image_ref[...]
    sums = jnp.sum(sums_ref[...], axis=0).T[: side.shape[0]]
    rr, side_rho, rho_rho, rho_image = (sums[:, k : k + 1] for k in range(4))
    curve = (rr - side_rho) / STEP
    alpha = rr / curve
    turn = alpha / STEP
    rest = 1.0 - turn
    rr_next = rest * rest * rr + 2.0 * rest * turn * side_rho + turn * turn * rho_rho
    gain = rest + rr_next / rr
    cross = (side_rho - rho_rho) / STEP
    curve = gain * gain * curve + 2.0 * gain * turn * cross + turn * turn * rho_image
    alpha_next = rr_next / curve
    direction = gain * side + turn * rho
    field_ref[...] = alpha * side + alpha_next * direction
    residual_ref[...] = rest * side + turn * rho - alpha_next * (gain / STEP * (side - rho) + turn * image)


def finish(side, rho, image, sums):
    return pl.pallas_call(
        finish_kernel,
        out_shape=[jax.ShapeDtypeStruct(side.shape, jnp.float32)] * 2,
        compiler_params=pltpu.CompilerParams(vmem_limit_bytes=4 << 20),
        name="finish",
    )(side, rho, image, sums)


def on_device(states, offsets, right_side):
    own, probes = right_side.shape
    side = right_side.T
    points = lax.dynamic_slice_in_dim(states, offsets[0], own, 0)
    with jax.named_scope("fetch_points"):
        message = pack(points, side)
        row, col = {0: points}, {(0, 0): message}
        for k in (1, 3):
            col[0, k] = shift(message, "y", NY, k)
            row[k] = shift(points, "z", NZ, k)
        col[1, 0] = shift(message, "c", NC, 1)
        row[1], row[3], col[0, 1], col[0, 3] = lax.optimization_barrier((row[1], row[3], col[0, 1], col[0, 3]))
        far = []
        for axis, size, ahead, behind in (("z", NZ, row[1], row[3]), ("y", NY, col[0, 1], col[0, 3])):
            middle = ahead.shape[0] // 2
            far.append((shift(ahead[:middle], axis, size, 1), shift(behind[middle:], axis, size, -1)))
        pair = shift(jnp.concatenate([col[0, 1], col[0, 3]], axis=0), "c", NC, 1)
        col[1, 1], col[1, 3] = pair[: message.shape[0]], pair[message.shape[0] :]
        near = [row[k] for k in ROWS[:3]]

    with jax.named_scope("build_tiles"):
        at = [col[k] for k in COLS[:6]]
        tile_a, image, half = build(near, at[:2], own, probes, side=side)
        tile_b, image = build(near, at[2:4], own, probes, [half], [image])
        tile_c, image = build(near, at[4:6], own, probes, [half], [image])
        far, image = lax.optimization_barrier((far, image))
        row[2] = jnp.concatenate(far[0], axis=0)
        col[0, 2] = jnp.concatenate(far[1], axis=0)
        col[1, 2] = shift(col[0, 2], "c", NC, 1)
        tile_d, image_far, half_far = build([row[2]], at, own, probes)
        at = [col[0, 2], col[1, 2]]
        tile_e, image = build(near + [row[2]], at, own, probes, [half, half_far], [image, image_far])
        tiles = [
            (tile_a, 0, 0),
            (tile_b, 0, 2 * own),
            (tile_c, 0, 4 * own),
            (tile_d, 3 * own, 0),
            (tile_e, 0, 6 * own),
        ]

    with jax.named_scope("sum_over_z"):
        parts = [image] + [None] * (NZ - 1)
        for k in (1, 3, 2):
            parts[k] = shift(image, "z", NZ, k)

    mine, other, rho = second_product(tiles, parts, own)

    with jax.named_scope("sum_over_yc"):
        mine = mine + shift(other, "c", NC, 1)
        shares = [mine[:, :own]]
        for m in (1, 3, 2):
            shares.append(shift(mine[:, m * own : (m + 1) * own], "y", NY, -m))

    with jax.named_scope("final_sums"):
        image, sums = local_sums(side, rho, shares)
        sums = jnp.broadcast_to(sums, (NY * NZ * NC, 8, LANES))
        sums = lax.all_to_all(sums, ("y", "z", "c"), 0, 0, tiled=True)

    field, residual = finish(side, rho, image, sums)
    return field.T, residual.T


def solution(mesh):
    fine = Mesh(mesh.devices.reshape(NY, NZ, NC, NX), ("y", "z", "c", "x"))
    rows = ("y", "z", "c")
    in_specs = (P(rows, None), P(rows), P(rows, "x"))
    out_specs = (P(rows, "x"), P(rows, "x"))
    return jax.shard_map(on_device, mesh=fine, in_specs=in_specs, out_specs=out_specs, check_vma=False)
```

time: 76.2 us -> 72.6 us (0.953); the launches traced: 76 us -> 71.3 us
  blocking collectives: 0 us -> 11.2 us
  starting transfers between devices: 30.2 us -> 20 us
  waiting for transfers between devices: 28.3 us -> 22.7 us
  Pallas kernels: 13.2 us -> 14.5 us
  other arithmetic: 1.04 us -> 0.05 us
    all_to_all x0 -> x1, blocking collectives: none -> 11.2 us  [on_device(): sums = lax.all_to_all(sums, ('y', 'z', 'c'), 0, 0, tiled=True)]
    ppermute x25 -> x18, starting transfers between devices: 30.2 us -> 20 us  [shift(): lax.ppermute(value, axis, [(i, (i + step) % size) for i in range(size)])]
    ppermute x25 -> x18, waiting for transfers between devices: 28.3 us -> 22.7 us  [shift(): lax.ppermute(value, axis, [(i, (i + step) % size) for i in range(size)])]
    pallas_call x2 -> x3, Pallas kernels: 2.6 us -> 3.85 us  [the longest x1 2.74 us: second_product(): pl.pallas_call(functools.partial(second_kernel, own, places), in_specs=[p...]
  transfers between devices with their start and end apart: 25 -> 18, of which waited for: 13 -> 10; matrix products, arithmetic and copies ran while one was open for 0% -> 0% of each run, Pallas kernels for 10% -> 11%
where the time goes in v6:
time: 72.6 us; the launch traced here: 71.3 us
  waiting for transfers between devices  22.7 us (31%)
  starting transfers between devices  20 us (28%)
  Pallas kernels  14.5 us (20%)
  blocking collectives  11.2 us (15%)
  between operations  1.5 us (2%)
  local copies, waits for them, and re-layouts  1.33 us (2%)
    ppermute x18, waiting for transfers between devices, shift(): lax.ppermute(value, axis, [(i, (i + step) % size) for i in range(size)])  22.7 us
    ppermute x18, starting transfers between devices, shift(): lax.ppermute(value, axis, [(i, (i + step) % size) for i in range(size)])  20 us
    all_to_all x1, blocking collectives, on_device(): sums = lax.all_to_all(sums, ('y', 'z', 'c'), 0, 0, tiled=True)  11.2 us
    pallas_call x5, Pallas kernels, build(): pl.pallas_call(functools.partial(tile_kernel, counts, probes), out_shape=...  10.4 us
    pallas_call x1, Pallas kernels, second_product(): pl.pallas_call(functools.partial(second_kernel, own, places), in_specs=[p...  2.74 us
  transfers between devices with their start and end apart: 18, of which 10 were waited for; matrix products, arithmetic and copies ran while one was open for 0% of the time, Pallas kernels for 11%

profile of v6, /device:TPU:0, one launch (start us, length us, event | category | flops | bytes accessed | tf_op | source)
XLA Modules:
  0.0 71.3 jit_solution(12404753335698366129)
XLA Ops:
  1.4 0.3 copy-done
  1.8 0.7 %copy-done.1 = f32[512,16]{0,1:T(8,128)S(1)} copy-done((f32[512,16]{0,1:T(8,128)S(1)}, f32[512,16]{0,1:T(8,128)}, u32[]{:S(2)}) %copy-start.1) | copy-done | bytes 32792
  2.5 0.3 pack.1.refs_3_.refs_1_
  2.8 3.2 %collective-permute-start.3 = (bf16[576,256]{1,0:T(8,128)(2,1)S(1)}, bf16[576,256]{1,0:T(8,128)(2,1)S(1)}, u32[]{:S(2)}, u32[]{:S(2)}) collective-permute-start(bf16[576,256]{1,0:T(8,128)(2,1)S(1)} %pack.1.refs_3_.refs_1_), channel_id=1, source_target_pairs={{0,96},{32,0},{64,32},{96,64},{1,97},{33,1},{65,33},{97,65},{2,98}... | collective-permute-start | bytes 884744 | tf_op jit(solution)/shard_map/fetch_points/ppermute | solution.py:23
  6.0 4.0 %collective-permute-start.1 = (bf16[512,256]{1,0:T(8,128)(2,1)S(1)}, bf16[512,256]{1,0:T(8,128)(2,1)S(1)}, u32[]{:S(2)}, u32[]{:S(2)}) collective-permute-start(bf16[512,256]{1,0:T(8,128)(2,1)S(1)} %constant_dynamic-slice_fusion.points_ref.refs_0_), channel_id=1, source_target_pairs={{0,24},{8,0},{16,8},{24,16},{1,25},{9,1},{17,9},{25,17},{2,26},{10... | collective-permute-start | bytes 786440 | tf_op jit(solution)/shard_map/fetch_points/ppermute | solution.py:23
  10.0 5.3 %collective-permute-done.1.refs_2_ = bf16[512,256]{1,0:T(8,128)(2,1)S(1)} collective-permute-done((bf16[512,256]{1,0:T(8,128)(2,1)S(1)}, bf16[512,256]{1,0:T(8,128)(2,1)S(1)}, u32[]{:S(2)}, u32[]{:S(2)}) %collective-permute-start.1) | collective-permute-done | bytes 262176 | tf_op jit(solution)/shard_map/fetch_points/ppermute | solution.py:23
  15.3 3.4 %collective-permute-done.refs_1_ = bf16[512,256]{1,0:T(8,128)(2,1)S(1)} collective-permute-done((bf16[512,256]{1,0:T(8,128)(2,1)S(1)}, bf16[512,256]{1,0:T(8,128)(2,1)S(1)}, u32[]{:S(2)}, u32[]{:S(2)}) %collective-permute-start) | collective-permute-done | bytes 262176 | tf_op jit(solution)/shard_map/fetch_points/ppermute | solution.py:23
  18.9 0.5 collective-permute-start.9
  19.4 1.0 %collective-permute-start.5 = (bf16[256,256]{1,0:T(8,128)(2,1)S(1)}, bf16[256,256]{1,0:T(8,128)(2,1)S(1)}, u32[]{:S(2)}, u32[]{:S(2)}) collective-permute-start(bf16[256,256]{1,0:T(8,128)(2,1)S(1)} %slice.31), channel_id=1, source_target_pairs={{0,24},{8,0},{16,8},{24,16},{1,25},{9,1},{17,9},{25,17},{2,26},{10... | collective-permute-start | bytes 393224 | tf_op jit(solution)/shard_map/fetch_points/ppermute | solution.py:23
  20.5 1.1 %collective-permute-start.4 = (bf16[256,256]{1,0:T(8,128)(2,1)S(1)}, bf16[256,256]{1,0:T(8,128)(2,1)S(1)}, u32[]{:S(2)}, u32[]{:S(2)}) collective-permute-start(bf16[256,256]{1,0:T(8,128)(2,1)S(1)} %slice.30), channel_id=1, source_target_pairs={{0,8},{8,16},{16,24},{24,0},{1,9},{9,17},{17,25},{25,1},{2,10},{10... | collective-permute-start | bytes 393224 | tf_op jit(solution)/shard_map/fetch_points/ppermute | solution.py:23
  21.5 3.0 %collective-permute-start.7 = (bf16[288,256]{1,0:T(8,128)(2,1)S(1)}, bf16[288,256]{1,0:T(8,128)(2,1)S(1)}, u32[]{:S(2)}, u32[]{:S(2)}) collective-permute-start(bf16[288,256]{1,0:T(8,128)(2,1)S(1)} %slice.33), channel_id=1, source_target_pairs={{0,96},{32,0},{64,32},{96,64},{1,97},{33,1},{65,33},{97,65},{2,98}... | collective-permute-start | bytes 442376 | tf_op jit(solution)/shard_map/fetch_points/ppermute | solution.py:23
  24.5 2.0 %build_tile.5 = (bf16[1536,1024]{1,0:T(8,128)(2,1)S(1)}, f32[16,1536]{1,0:T(8,128)S(1)}, f32[1536,1]{1,0:T(8,128)S(1)}) custom-call(bf16[512,256]{1,0:T(8,128)(2,1)S(1)} %constant_dynamic-slice_fusion.points_ref.refs_0_, bf16[512,256]{1,0:T(8,128)(2,1)S(1)} %collective-permute-done.refs_1_, bf16[512,256]{1,0:T(8,128)(2,1)S(1)} %collective-permute-done.1.refs_2_, ...), custom_call_target="tpu_custom_call" | custom-call | flops 50331648 | bytes 1024 | tf_op jit(solution)/shard_map/build_tiles/build_tile/pallas_call | solution.py:130
  26.5 1.9 %build_tile.6 = (bf16[1536,1024]{1,0:T(8,128)(2,1)S(1)}, f32[16,1536]{1,0:T(8,128)S(1)}) custom-call(bf16[512,256]{1,0:T(8,128)(2,1)S(1)} %constant_dynamic-slice_fusion.points_ref.refs_0_, bf16[512,256]{1,0:T(8,128)(2,1)S(1)} %collective-permute-done.refs_1_, bf16[512,256]{1,0:T(8,128)(2,1)S(1)} %collective-permute-done.1.refs_2_, ...), custom_call_target="tpu_custom_call" | custom-call | flops 50331648 | bytes 1024 | tf_op jit(solution)/shard_map/build_tiles/build_tile/pallas_call | solution.py:130
  28.5 1.9 %build_tile.7 = (bf16[1536,1024]{1,0:T(8,128)(2,1)S(1)}, f32[16,1536]{1,0:T(8,128)S(1)}) custom-call(bf16[512,256]{1,0:T(8,128)(2,1)S(1)} %constant_dynamic-slice_fusion.points_ref.refs_0_, bf16[512,256]{1,0:T(8,128)(2,1)S(1)} %collective-permute-done.refs_1_, bf16[512,256]{1,0:T(8,128)(2,1)S(1)} %collective-permute-done.1.refs_2_, ...), custom_call_target="tpu_custom_call" | custom-call | flops 50331648 | bytes 1024 | tf_op jit(solution)/shard_map/build_tiles/build_tile/pallas_call | solution.py:130
  30.4 0.4 collective-permute-done.6
  31.2 2.0 %build_tile.8 = (bf16[512,3072]{1,0:T(8,128)(2,1)S(1)}, f32[16,512]{1,0:T(8,128)S(1)}, f32[512,1]{1,0:T(8,128)S(1)}) custom-call(bf16[512,256]{1,0:T(8,128)(2,1)S(1)} %constant_dynamic-update-slice_fusion.refs_0_.refs_3_, bf16[576,256]{1,0:T(8,128)(2,1)S(1)} %pack.1.refs_3_.refs_1_, bf16[576,256]{1,0:T(8,128)(2,1)S(1)} %collective-permute-done.9.refs_4_.refs_2_, ...), custom_call_target="tpu_custom_call" | custom-call | flops 50331648 | bytes 1024 | tf_op jit(solution)/shard_map/build_tiles/build_tile/pallas_call | solution.py:130
  33.2 2.5 %build_tile.9 = (bf16[2048,1024]{1,0:T(8,128)(2,1)S(1)}, f32[16,2048]{1,0:T(8,128)S(1)}) custom-call(bf16[512,256]{1,0:T(8,128)(2,1)S(1)} %constant_dynamic-slice_fusion.points_ref.refs_0_, bf16[512,256]{1,0:T(8,128)(2,1)S(1)} %collective-permute-done.refs_1_, bf16[512,256]{1,0:T(8,128)(2,1)S(1)} %collective-permute-done.1.refs_2_, ...), custom_call_target="tpu_custom_call" | custom-call | flops 67108864 | bytes 1024 | tf_op jit(solution)/shard_map/build_tiles/build_tile/pallas_call | solution.py:130
  35.7 1.5 %collective-permute-start.13 = (f32[16,2048]{1,0:T(8,128)S(1)}, f32[16,2048]{1,0:T(8,128)S(1)}, u32[]{:S(2)}, u32[]{:S(2)}) collective-permute-start(f32[16,2048]{1,0:T(8,128)S(1)} %get-tuple-element.45.refs_0_), channel_id=1, source_target_pairs={{0,24},{8,0},{16,8},{24,16},{1,25},{9,1},{17,9},{25,17},{2,26},{10... | collective-permute-start | bytes 393224 | tf_op jit(solution)/shard_map/sum_over_z/ppermute | solution.py:23
  37.2 0.7 collective-permute-start.12
  38.2 3.8 %collective-permute-done.13.refs_3_ = f32[16,2048]{1,0:T(8,128)S(1)} collective-permute-done((f32[16,2048]{1,0:T(8,128)S(1)}, f32[16,2048]{1,0:T(8,128)S(1)}, u32[]{:S(2)}, u32[]{:S(2)}) %collective-permute-start.13) | collective-permute-done | bytes 131104 | tf_op jit(solution)/shard_map/sum_over_z/ppermute | solution.py:23
  42.0 3.1 %collective-permute-done.12.refs_2_ = f32[16,2048]{1,0:T(8,128)S(1)} collective-permute-done((f32[16,2048]{1,0:T(8,128)S(1)}, f32[16,2048]{1,0:T(8,128)S(1)}, u32[]{:S(2)}, u32[]{:S(2)}) %collective-permute-start.12) | collective-permute-done | bytes 131104 | tf_op jit(solution)/shard_map/sum_over_z/ppermute | solution.py:23
  45.1 2.0 %collective-permute-done.11.refs_1_ = f32[16,2048]{1,0:T(8,128)S(1)} collective-permute-done((f32[16,2048]{1,0:T(8,128)S(1)}, f32[16,2048]{1,0:T(8,128)S(1)}, u32[]{:S(2)}, u32[]{:S(2)}) %collective-permute-start.11) | collective-permute-done | bytes 131104 | tf_op jit(solution)/shard_map/sum_over_z/ppermute | solution.py:23
  47.1 2.7 %second_product.1 = (f32[16,2048]{1,0:T(8,128)S(1)}, f32[16,2048]{1,0:T(8,128)S(1)}, f32[16,512]{1,0:T(8,128)S(1)}) custom-call(f32[16,2048]{1,0:T(8,128)S(1)} %get-tuple-element.45.refs_0_, f32[16,2048]{1,0:T(8,128)S(1)} %collective-permute-done.11.refs_1_, f32[16,2048]{1,0:T(8,128)S(1)} %collective-permute-done.12.refs_2_, ...), custom_call_target="tpu_custom_call" | custom-call | flops 268435456 | bytes 1024 | tf_op jit(solution)/shard_map/second_product/pallas_call | solution.py:173
  49.9 1.3 %collective-permute-done.14 = f32[16,2048]{1,0:T(8,128)S(1)} collective-permute-done((f32[16,2048]{1,0:T(8,128)S(1)}, f32[16,2048]{1,0:T(8,128)S(1)}, u32[]{:S(2)}, u32[]{:S(2)}) %collective-permute-start.14) | collective-permute-done | bytes 131104 | tf_op jit(solution)/shard_map/sum_over_yc/ppermute | solution.py:23
  51.3 1.2 %collective-permute-start.17 = (f32[16,512]{1,0:T(8,128)S(1)}, f32[16,512]{1,0:T(8,128)S(1)}, u32[]{:S(2)}, u32[]{:S(2)}) collective-permute-start(f32[16,512]{1,0:T(8,128)S(1)} %get-tuple-element.60), channel_id=1, source_target_pairs={{0,64},{32,96},{64,0},{96,32},{1,65},{33,97},{65,1},{97,33},{2,66}... | collective-permute-start | bytes 98312 | tf_op jit(solution)/shard_map/sum_over_yc/ppermute | solution.py:23
  52.4 2.6 %collective-permute-start.16 = (f32[16,512]{1,0:T(8,128)S(1)}, f32[16,512]{1,0:T(8,128)S(1)}, u32[]{:S(2)}, u32[]{:S(2)}) collective-permute-start(f32[16,512]{1,0:T(8,128)S(1)} %get-tuple-element.61), channel_id=1, source_target_pairs={{0,32},{32,64},{64,96},{96,0},{1,33},{33,65},{65,97},{97,1},{2,34}... | collective-permute-start | bytes 98312 | tf_op jit(solution)/shard_map/sum_over_yc/ppermute | solution.py:23
  55.1 0.6 collective-permute-start.15
  55.7 1.4 %collective-permute-done.17.refs_3_ = f32[16,512]{1,0:T(8,128)S(1)} collective-permute-done((f32[16,512]{1,0:T(8,128)S(1)}, f32[16,512]{1,0:T(8,128)S(1)}, u32[]{:S(2)}, u32[]{:S(2)}) %collective-permute-start.17) | collective-permute-done | bytes 32800 | tf_op jit(solution)/shard_map/sum_over_yc/ppermute | solution.py:23
  57.1 0.5 collective-permute-done.16.refs_2_
  57.6 1.4 %collective-permute-done.15.refs_1_ = f32[16,512]{1,0:T(8,128)S(1)} collective-permute-done((f32[16,512]{1,0:T(8,128)S(1)}, f32[16,512]{1,0:T(8,128)S(1)}, u32[]{:S(2)}, u32[]{:S(2)}) %collective-permute-start.15) | collective-permute-done | bytes 32800 | tf_op jit(solution)/shard_map/sum_over_yc/ppermute | solution.py:23
  59.2 11.2 %all_to_all.5.sums_ref = f32[32,8,128]{2,1,0:T(8,128)S(1)} all-to-all(f32[32,8,128]{2,1,0:T(8,128)S(1)} %broadcast_in_dim.3), channel_id=1, replica_groups=mesh['y'=4,'z'=4,'c'=2,'x'=4] {'y','z','c'}, dimensions={0} | all-to-all | bytes 262144 | tf_op jit(solution)/shard_map/final_sums/all_to_all | solution.py:297
  70.4 0.9 %finish.1 = (f32[16,512]{1,0:T(8,128)}, f32[16,512]{1,0:T(8,128)}) custom-call(f32[16,512]{1,0:T(8,128)S(1)} %bitcast.10, f32[16,512]{1,0:T(8,128)S(1)} %get-tuple-element.51.rho_ref, f32[16,512]{1,0:T(8,128)S(1)} %get-tuple-element.54.image_ref, f32[32,8,128]{2,1,0:T(8,128)S(1)} %all_to_all.5.sums_ref), custom_call_target="tpu_custom_call" | custom-call | tf_op jit(solution)/shard_map/finish/pallas_call | solution.py:233
  (32 shorter events, 1.1 us)
Async XLA Ops:
  0.6 1.1 %copy-start = (bf16[1024,256]{1,0:T(8,128)(2,1)S(1)}, bf16[1024,256]{1,0:T(8,128)(2,1)}, u32[]{:S(2)}) copy-start(bf16[1024,256]{1,0:T(8,128)(2,1)} %param.3) | copy-start | bytes 1572868
  1.8 0.8 %copy-start.1 = (f32[512,16]{0,1:T(8,128)S(1)}, f32[512,16]{0,1:T(8,128)}, u32[]{:S(2)}) copy-start(f32[512,16]{0,1:T(8,128)} %param.5) | copy-start | bytes 98308
  2.8 15.9 %collective-permute-start.3 = (bf16[576,256]{1,0:T(8,128)(2,1)S(1)}, bf16[576,256]{1,0:T(8,128)(2,1)S(1)}, u32[]{:S(2)}, u32[]{:S(2)}) collective-permute-start(bf16[576,256]{1,0:T(8,128)(2,1)S(1)} %pack.1.refs_3_.refs_1_), channel_id=1, source_target_pairs={{0,96},{32,0},{64,32},{96,64},{1,97},{33,1},{65,33},{97,65},{2,98}... | collective-permute-start | bytes 884744 | tf_op jit(solution)/shard_map/fetch_points/ppermute | solution.py:23
  6.0 12.7 %collective-permute-start.2 = (bf16[576,256]{1,0:T(8,128)(2,1)S(1)}, bf16[576,256]{1,0:T(8,128)(2,1)S(1)}, u32[]{:S(2)}, u32[]{:S(2)}) collective-permute-start(bf16[576,256]{1,0:T(8,128)(2,1)S(1)} %pack.1.refs_3_.refs_1_), channel_id=1, source_target_pairs={{0,32},{32,64},{64,96},{96,0},{1,33},{33,65},{65,97},{97,1},{2,34}... | collective-permute-start | bytes 884744 | tf_op jit(solution)/shard_map/fetch_points/ppermute | solution.py:23
  6.0 9.3 %collective-permute-start.1 = (bf16[512,256]{1,0:T(8,128)(2,1)S(1)}, bf16[512,256]{1,0:T(8,128)(2,1)S(1)}, u32[]{:S(2)}, u32[]{:S(2)}) collective-permute-start(bf16[512,256]{1,0:T(8,128)(2,1)S(1)} %constant_dynamic-slice_fusion.points_ref.refs_0_), channel_id=1, source_target_pairs={{0,24},{8,0},{16,8},{24,16},{1,25},{9,1},{17,9},{25,17},{2,26},{10... | collective-permute-start | bytes 786440 | tf_op jit(solution)/shard_map/fetch_points/ppermute | solution.py:23
  10.0 8.7 %collective-permute-start = (bf16[512,256]{1,0:T(8,128)(2,1)S(1)}, bf16[512,256]{1,0:T(8,128)(2,1)S(1)}, u32[]{:S(2)}, u32[]{:S(2)}) collective-permute-start(bf16[512,256]{1,0:T(8,128)(2,1)S(1)} %constant_dynamic-slice_fusion.points_ref.refs_0_), channel_id=1, source_target_pairs={{0,8},{8,16},{16,24},{24,0},{1,9},{9,17},{17,25},{25,1},{2,10},{10... | collective-permute-start | bytes 786440 | tf_op jit(solution)/shard_map/fetch_points/ppermute | solution.py:23
  18.8 9.7 %collective-permute-start.8 = (bf16[1152,256]{1,0:T(8,128)(2,1)S(1)}, bf16[1152,256]{1,0:T(8,128)(2,1)S(1)}, u32[]{:S(2)}, u32[]{:S(2)}) collective-permute-start(bf16[1152,256]{1,0:T(8,128)(2,1)S(1)} %pad_maximum_fusion), channel_id=1, source_target_pairs={{0,4},{4,0},{1,5},{5,1},{2,6},{6,2},{3,7},{7,3},{8,12},{12,8},{9,1... | collective-permute-start | bytes 1769480 | tf_op jit(solution)/shard_map/fetch_points/ppermute | solution.py:23
  18.9 5.6 %collective-permute-start.9 = (bf16[576,256]{1,0:T(8,128)(2,1)S(1)}, bf16[576,256]{1,0:T(8,128)(2,1)S(1)}, u32[]{:S(2)}, u32[]{:S(2)}) collective-permute-start(bf16[576,256]{1,0:T(8,128)(2,1)S(1)} %pack.1.refs_3_.refs_1_), channel_id=1, source_target_pairs={{0,4},{4,0},{1,5},{5,1},{2,6},{6,2},{3,7},{7,3},{8,12},{12,8},{9,1... | collective-permute-start | bytes 884744 | tf_op jit(solution)/shard_map/fetch_points/ppermute | solution.py:23
  19.4 11.0 %collective-permute-start.5 = (bf16[256,256]{1,0:T(8,128)(2,1)S(1)}, bf16[256,256]{1,0:T(8,128)(2,1)S(1)}, u32[]{:S(2)}, u32[]{:S(2)}) collective-permute-start(bf16[256,256]{1,0:T(8,128)(2,1)S(1)} %slice.31), channel_id=1, source_target_pairs={{0,24},{8,0},{16,8},{24,16},{1,25},{9,1},{17,9},{25,17},{2,26},{10... | collective-permute-start | bytes 393224 | tf_op jit(solution)/shard_map/fetch_points/ppermute | solution.py:23
  20.5 10.0 %collective-permute-start.4 = (bf16[256,256]{1,0:T(8,128)(2,1)S(1)}, bf16[256,256]{1,0:T(8,128)(2,1)S(1)}, u32[]{:S(2)}, u32[]{:S(2)}) collective-permute-start(bf16[256,256]{1,0:T(8,128)(2,1)S(1)} %slice.30), channel_id=1, source_target_pairs={{0,8},{8,16},{16,24},{24,0},{1,9},{9,17},{17,25},{25,1},{2,10},{10... | collective-permute-start | bytes 393224 | tf_op jit(solution)/shard_map/fetch_points/ppermute | solution.py:23
  21.5 8.9 %collective-permute-start.7 = (bf16[288,256]{1,0:T(8,128)(2,1)S(1)}, bf16[288,256]{1,0:T(8,128)(2,1)S(1)}, u32[]{:S(2)}, u32[]{:S(2)}) collective-permute-start(bf16[288,256]{1,0:T(8,128)(2,1)S(1)} %slice.33), channel_id=1, source_target_pairs={{0,96},{32,0},{64,32},{96,64},{1,97},{33,1},{65,33},{97,65},{2,98}... | collective-permute-start | bytes 442376 | tf_op jit(solution)/shard_map/fetch_points/ppermute | solution.py:23
  24.5 6.4 %collective-permute-start.6 = (bf16[288,256]{1,0:T(8,128)(2,1)S(1)}, bf16[288,256]{1,0:T(8,128)(2,1)S(1)}, u32[]{:S(2)}, u32[]{:S(2)}) collective-permute-start(bf16[288,256]{1,0:T(8,128)(2,1)S(1)} %slice.32), channel_id=1, source_target_pairs={{0,32},{32,64},{64,96},{96,0},{1,33},{33,65},{65,97},{97,1},{2,34}... | collective-permute-start | bytes 442376 | tf_op jit(solution)/shard_map/fetch_points/ppermute | solution.py:23
  30.9 2.4 %collective-permute-start.10 = (bf16[576,256]{1,0:T(8,128)(2,1)S(1)}, bf16[576,256]{1,0:T(8,128)(2,1)S(1)}, u32[]{:S(2)}, u32[]{:S(2)}) collective-permute-start(bf16[576,256]{1,0:T(8,128)(2,1)S(1)} %constant_dynamic-update-slice_fusion.2.refs_4_), channel_id=1, source_target_pairs={{0,4},{4,0},{1,5},{5,1},{2,6},{6,2},{3,7},{7,3},{8,12},{12,8},{9,1... | collective-permute-start | bytes 884744 | tf_op jit(solution)/shard_map/build_tiles/ppermute | solution.py:23
  35.7 6.3 %collective-permute-start.13 = (f32[16,2048]{1,0:T(8,128)S(1)}, f32[16,2048]{1,0:T(8,128)S(1)}, u32[]{:S(2)}, u32[]{:S(2)}) collective-permute-start(f32[16,2048]{1,0:T(8,128)S(1)} %get-tuple-element.45.refs_0_), channel_id=1, source_target_pairs={{0,24},{8,0},{16,8},{24,16},{1,25},{9,1},{17,9},{25,17},{2,26},{10... | collective-permute-start | bytes 393224 | tf_op jit(solution)/shard_map/sum_over_z/ppermute | solution.py:23
  37.2 7.9 %collective-permute-start.12 = (f32[16,2048]{1,0:T(8,128)S(1)}, f32[16,2048]{1,0:T(8,128)S(1)}, u32[]{:S(2)}, u32[]{:S(2)}) collective-permute-start(f32[16,2048]{1,0:T(8,128)S(1)} %get-tuple-element.45.refs_0_), channel_id=1, source_target_pairs={{0,16},{8,24},{16,0},{24,8},{1,17},{9,25},{17,1},{25,9},{2,18},{10... | collective-permute-start | bytes 393224 | tf_op jit(solution)/shard_map/sum_over_z/ppermute | solution.py:23
  37.9 9.2 %collective-permute-start.11 = (f32[16,2048]{1,0:T(8,128)S(1)}, f32[16,2048]{1,0:T(8,128)S(1)}, u32[]{:S(2)}, u32[]{:S(2)}) collective-permute-start(f32[16,2048]{1,0:T(8,128)S(1)} %get-tuple-element.45.refs_0_), channel_id=1, source_target_pairs={{0,8},{8,16},{16,24},{24,0},{1,9},{9,17},{17,25},{25,1},{2,10},{10... | collective-permute-start | bytes 393224 | tf_op jit(solution)/shard_map/sum_over_z/ppermute | solution.py:23
  49.9 1.4 %collective-permute-start.14 = (f32[16,2048]{1,0:T(8,128)S(1)}, f32[16,2048]{1,0:T(8,128)S(1)}, u32[]{:S(2)}, u32[]{:S(2)}) collective-permute-start(f32[16,2048]{1,0:T(8,128)S(1)} %get-tuple-element.53), channel_id=1, source_target_pairs={{0,4},{4,0},{1,5},{5,1},{2,6},{6,2},{3,7},{7,3},{8,12},{12,8},{9,1... | collective-permute-start | bytes 393224 | tf_op jit(solution)/shard_map/sum_over_yc/ppermute | solution.py:23
  51.3 5.8 %collective-permute-start.17 = (f32[16,512]{1,0:T(8,128)S(1)}, f32[16,512]{1,0:T(8,128)S(1)}, u32[]{:S(2)}, u32[]{:S(2)}) collective-permute-start(f32[16,512]{1,0:T(8,128)S(1)} %get-tuple-element.60), channel_id=1, source_target_pairs={{0,64},{32,96},{64,0},{96,32},{1,65},{33,97},{65,1},{97,33},{2,66}... | collective-permute-start | bytes 98312 | tf_op jit(solution)/shard_map/sum_over_yc/ppermute | solution.py:23
  52.4 5.1 %collective-permute-start.16 = (f32[16,512]{1,0:T(8,128)S(1)}, f32[16,512]{1,0:T(8,128)S(1)}, u32[]{:S(2)}, u32[]{:S(2)}) collective-permute-start(f32[16,512]{1,0:T(8,128)S(1)} %get-tuple-element.61), channel_id=1, source_target_pairs={{0,32},{32,64},{64,96},{96,0},{1,33},{33,65},{65,97},{97,1},{2,34}... | collective-permute-start | bytes 98312 | tf_op jit(solution)/shard_map/sum_over_yc/ppermute | solution.py:23
  55.1 3.9 %collective-permute-start.15 = (f32[16,512]{1,0:T(8,128)S(1)}, f32[16,512]{1,0:T(8,128)S(1)}, u32[]{:S(2)}, u32[]{:S(2)}) collective-permute-start(f32[16,512]{1,0:T(8,128)S(1)} %get-tuple-element.62), channel_id=1, source_target_pairs={{0,96},{32,0},{64,32},{96,64},{1,97},{33,1},{65,33},{97,65},{2,98}... | collective-permute-start | bytes 98312 | tf_op jit(solution)/shard_map/sum_over_yc/ppermute | solution.py:23

commit v7 on v6

--- a/solution.py
+++ b/solution.py
@@ -21,6 +21,14 @@
 
 def shift(value, axis, size, step):
     return lax.ppermute(value, axis, [(i, (i + step) % size) for i in range(size)])
+
+
+def hand_on(behind, ahead, axis, size):
+    value = jnp.where(lax.axis_index("c") == 0, behind, ahead)
+    pairs = []
+    for i in range(size):
+        pairs += [(i * NC, (i + 1) % size * NC), (i * NC + 1, (i - 1) % size * NC + 1)]
+    return lax.ppermute(value, (axis, "c"), pairs)
 
 
 def split(value):
@@ -249,33 +257,38 @@
             col[0, k] = shift(message, "y", NY, k)
             row[k] = shift(points, "z", NZ, k)
         col[1, 0] = shift(message, "c", NC, 1)
-        row[1], row[3], col[0, 1], col[0, 3] = lax.optimization_barrier((row[1], row[3], col[0, 1], col[0, 3]))
-        far = []
-        for axis, size, ahead, behind in (("z", NZ, row[1], row[3]), ("y", NY, col[0, 1], col[0, 3])):
-            middle = ahead.shape[0] // 2
-            far.append((shift(ahead[:middle], axis, size, 1), shift(behind[middle:], axis, size, -1)))
+        first = [col[0, 0], col[1, 0]]
+        tile_a, image_a, half_a = build([points], first, own, probes, side=side)
+        tile_b, image_b, half_b = build([row[1]], first, own, probes)
+        near = row[1], row[3], col[0, 1], col[0, 3]
+        near, image_a, image_b = lax.optimization_barrier((near, image_a, image_b))
+        row[1], row[3], col[0, 1], col[0, 3] = near
+        row[2] = hand_on(row[1], row[3], "z", NZ)
+        col[0, 2] = hand_on(col[0, 1], col[0, 3], "y", NY)
         pair = shift(jnp.concatenate([col[0, 1], col[0, 3]], axis=0), "c", NC, 1)
         col[1, 1], col[1, 3] = pair[: message.shape[0]], pair[message.shape[0] :]
-        near = [row[k] for k in ROWS[:3]]
 
     with jax.named_scope("build_tiles"):
+        near = [points, row[1], row[3]]
+        tile_c, image_c, half_c = build([row[3]], first, own, probes)
+        half = [half_a, half_b, half_c]
+        tile_d, image = build(near, [col[0, 1], col[0, 3]], own, probes, half, [image_a, image_b, image_c])
+        tile_e, image = build(near, [col[1, 1], col[1, 3]], own, probes, half, [image])
+        far, image = lax.optimization_barrier(((row[2], col[0, 2]), image))
+        row[2], col[0, 2] = far
+        col[1, 2] = shift(col[0, 2], "c", NC, 1)
         at = [col[k] for k in COLS[:6]]
-        tile_a, image, half = build(near, at[:2], own, probes, side=side)
-        tile_b, image = build(near, at[2:4], own, probes, [half], [image])
-        tile_c, image = build(near, at[4:6], own, probes, [half], [image])
-        far, image = lax.optimization_barrier((far, image))
-        row[2] = jnp.concatenate(far[0], axis=0)
-        col[0, 2] = jnp.concatenate(far[1], axis=0)
-        col[1, 2] = shift(col[0, 2], "c", NC, 1)
-        tile_d, image_far, half_far = build([row[2]], at, own, probes)
+        tile_f, image_far, half_far = build([row[2]], at, own, probes)
         at = [col[0, 2], col[1, 2]]
-        tile_e, image = build(near + [row[2]], at, own, probes, [half, half_far], [image, image_far])
+        tile_g, image = build(near + [row[2]], at, own, probes, half + [half_far], [image, image_far])
         tiles = [
             (tile_a, 0, 0),
-            (tile_b, 0, 2 * own),
-            (tile_c, 0, 4 * own),
-            (tile_d, 3 * own, 0),
-            (tile_e, 0, 6 * own),
+            (tile_b, own, 0),
+            (tile_c, 2 * own, 0),
+            (tile_d, 0, 2 * own),
+            (tile_e, 0, 4 * own),
+            (tile_f, 3 * own, 0),
+            (tile_g, 0, 6 * own),
         ]
 
     with jax.named_scope("sum_over_z"):

time: 72.6 us -> 72.3 us (level)
  waiting for transfers between devices: 22.7 us -> 16.8 us
  local copies, waits for them, and re-layouts: 1.33 us -> 5.05 us
  blocking collectives: 11.2 us -> 12.8 us
  starting transfers between devices: 20 us -> 19 us
  other arithmetic: 0.05 us -> 0.94 us
    ppermute x18 -> x14, waiting for transfers between devices: 22.7 us -> 15 us  [shift(): lax.ppermute(value, axis, [(i, (i + step) % size) for i in range(size)])]
    unnamed x6 -> x16, local copies, waits for them, and re-layouts: 1.12 us -> 3.85 us
    ppermute x0 -> x2, waiting for transfers between devices: none -> 1.76 us  [hand_on(): return lax.ppermute(value, (axis, 'c'), pairs)]
    all_to_all x1, blocking collectives: 11.2 us -> 12.8 us  [on_device(): sums = lax.all_to_all(sums, ('y', 'z', 'c'), 0, 0, tiled=True)]
    ppermute x18 -> x14, starting transfers between devices: 20 us -> 18.5 us  [shift(): lax.ppermute(value, axis, [(i, (i + step) % size) for i in range(size)])]
    slice x1, local copies, waits for them, and re-layouts: 0.05 us -> 1.11 us  [on_device(): col[1, 1], col[1, 3] = (pair[:message.shape[0]], pair[message.shape[0]:])]
    concatenate x1, other arithmetic: 0.04 us -> 0.87 us  [on_device(): pair = shift(jnp.concatenate([col[0, 1], col[0, 3]], axis=0), 'c', NC, 1)]
    pallas_call x5 -> x7, Pallas kernels: 10.4 us -> 10.9 us  [build(): pl.pallas_call(functools.partial(tile_kernel, counts, probes), out_shape=...]
  transfers between devices with their start and end apart: 18 -> 16, of which waited for: 10 -> 7; matrix products, arithmetic and copies ran while one was open for 0% -> 2% of each run, Pallas kernels for 11% -> 12%
where the time goes in v7:
time: 72.3 us; the launch traced here: 71 us
  starting transfers between devices  19 us (26%)
  waiting for transfers between devices  16.8 us (23%)
  Pallas kernels  15 us (21%)
  blocking collectives  12.8 us (18%)
  local copies, waits for them, and re-layouts  5.05 us (7%)
  between operations  1.45 us (2%)
  other arithmetic  0.94 us (1%)
    ppermute x14, starting transfers between devices, shift(): lax.ppermute(value, axis, [(i, (i + step) % size) for i in range(size)])  18.5 us
    ppermute x14, waiting for transfers between devices, shift(): lax.ppermute(value, axis, [(i, (i + step) % size) for i in range(size)])  15 us
    all_to_all x1, blocking collectives, on_device(): sums = lax.all_to_all(sums, ('y', 'z', 'c'), 0, 0, tiled=True)  12.8 us
    pallas_call x7, Pallas kernels, build(): pl.pallas_call(functools.partial(tile_kernel, counts, probes), out_shape=...  10.9 us
    unnamed x16, local copies, waits for them, and re-layouts  3.85 us
    pallas_call x1, Pallas kernels, second_product(): pl.pallas_call(functools.partial(second_kernel, own, places), in_specs=[p...  2.74 us
    ppermute x2, waiting for transfers between devices, hand_on(): return lax.ppermute(value, (axis, 'c'), pairs)  1.76 us
  transfers between devices with their start and end apart: 16, of which 7 were waited for; matrix products, arithmetic and copies ran while one was open for 2% of the time, Pallas kernels for 12%

profile of v7, /device:TPU:0, one launch (start us, length us, event | category | flops | bytes accessed | tf_op | source)
XLA Modules:
  0.0 71.0 jit_solution(12879449254450303264)
XLA Ops:
  1.8 0.7 %copy-done.5 = f32[512,16]{0,1:T(8,128)S(1)} copy-done((f32[512,16]{0,1:T(8,128)S(1)}, f32[512,16]{0,1:T(8,128)}, u32[]{:S(2)}) %copy-start.5) | copy-done | bytes 32792
  2.9 3.2 %collective-permute-start.3 = (bf16[576,256]{1,0:T(8,128)(2,1)S(1)}, bf16[576,256]{1,0:T(8,128)(2,1)S(1)}, u32[]{:S(2)}, u32[]{:S(2)}) collective-permute-start(bf16[576,256]{1,0:T(8,128)(2,1)S(1)} %pack.1.refs_1_), channel_id=1, source_target_pairs={{0,96},{32,0},{64,32},{96,64},{1,97},{33,1},{65,33},{97,65},{2,98}... | collective-permute-start | bytes 884744 | tf_op jit(solution)/shard_map/fetch_points/ppermute | solution.py:23
  6.1 1.9 %collective-permute-start = (bf16[512,256]{1,0:T(8,128)(2,1)S(1)}, bf16[512,256]{1,0:T(8,128)(2,1)S(1)}, u32[]{:S(2)}, u32[]{:S(2)}) collective-permute-start(bf16[512,256]{1,0:T(8,128)(2,1)S(1)} %constant_dynamic-slice_fusion.points_ref.refs_0_), channel_id=1, source_target_pairs={{0,8},{8,16},{16,24},{24,0},{1,9},{9,17},{17,25},{25,1},{2,10},{10... | collective-permute-start | bytes 786440 | tf_op jit(solution)/shard_map/fetch_points/ppermute | solution.py:23
  8.0 2.1 %collective-permute-start.1 = (bf16[512,256]{1,0:T(8,128)(2,1)S(1)}, bf16[512,256]{1,0:T(8,128)(2,1)S(1)}, u32[]{:S(2)}, u32[]{:S(2)}) collective-permute-start(bf16[512,256]{1,0:T(8,128)(2,1)S(1)} %constant_dynamic-slice_fusion.points_ref.refs_0_), channel_id=1, source_target_pairs={{0,24},{8,0},{16,8},{24,16},{1,25},{9,1},{17,9},{25,17},{2,26},{10... | collective-permute-start | bytes 786440 | tf_op jit(solution)/shard_map/fetch_points/ppermute | solution.py:23
  10.1 0.8 %copy-done.6 = f32[512,16]{0,1:T(8,128)S(1)} copy-done((f32[512,16]{0,1:T(8,128)S(1)}, f32[512,16]{0,1:T(8,128)}, u32[]{:S(2)}) %copy-start.6) | copy-done | bytes 32792
  10.9 0.8 %build_tile.7 = (bf16[512,1024]{1,0:T(8,128)(2,1)S(1)}, f32[16,512]{1,0:T(8,128)S(1)}, f32[512,1]{1,0:T(8,128)S(1)}) custom-call(bf16[512,256]{1,0:T(8,128)(2,1)S(1)} %constant_dynamic-slice_fusion.points_ref.refs_0_, bf16[576,256]{1,0:T(8,128)(2,1)S(1)} %pack.1.refs_1_, bf16[576,256]{1,0:T(8,128)(2,1)S(1)} %collective-permute-done.4.refs_2_, ...), custom_call_target="tpu_custom_call" | custom-call | flops 16777216 | bytes 1024 | tf_op jit(solution)/shard_map/fetch_points/build_tile/pallas_call | solution.py:138
  11.7 1.0 %copy-done.1 = bf16[512,1024]{1,0:T(8,128)(2,1)} copy-done((bf16[512,1024]{1,0:T(8,128)(2,1)}, bf16[512,1024]{1,0:T(8,128)(2,1)S(1)}, u32[]{:S(2)}) %copy-start.1) | copy-done | bytes 1048600
  12.7 4.0 %collective-permute-done.refs_0_.refs_1_ = bf16[512,256]{1,0:T(8,128)(2,1)S(1)} collective-permute-done((bf16[512,256]{1,0:T(8,128)(2,1)S(1)}, bf16[512,256]{1,0:T(8,128)(2,1)S(1)}, u32[]{:S(2)}, u32[]{:S(2)}) %collective-permute-start) | collective-permute-done | bytes 262176 | tf_op jit(solution)/shard_map/fetch_points/ppermute | solution.py:23
  16.7 0.8 %build_tile.8 = (bf16[512,1024]{1,0:T(8,128)(2,1)S(1)}, f32[16,512]{1,0:T(8,128)S(1)}, f32[512,1]{1,0:T(8,128)S(1)}) custom-call(bf16[512,256]{1,0:T(8,128)(2,1)S(1)} %collective-permute-done.refs_0_.refs_1_, bf16[576,256]{1,0:T(8,128)(2,1)S(1)} %pack.1.refs_1_, bf16[576,256]{1,0:T(8,128)(2,1)S(1)} %collective-permute-done.4.refs_2_), custom_call_target="tpu_custom_call" | custom-call | flops 16777216 | bytes 1024 | tf_op jit(solution)/shard_map/fetch_points/build_tile/pallas_call | solution.py:138
  17.6 1.0 %copy-done.3 = bf16[512,1024]{1,0:T(8,128)(2,1)} copy-done((bf16[512,1024]{1,0:T(8,128)(2,1)}, bf16[512,1024]{1,0:T(8,128)(2,1)S(1)}, u32[]{:S(2)}) %copy-start.3) | copy-done | bytes 1048600
  18.6 0.9 %pad_maximum_fusion = bf16[1152,256]{1,0:T(8,128)(2,1)} fusion(bf16[576,256]{1,0:T(8,128)(2,1)S(1)} %collective-permute-done.3.refs_4_, bf16[576,256]{1,0:T(8,128)(2,1)S(1)} %collective-permute-done.2.refs_3_), kind=kLoop, calls=%fused_computation | loop fusion | flops 1179648 | bytes 1179648 | tf_op jit(solution)/shard_map/fetch_points/concatenate | solution.py:268
  19.5 0.4 collective-permute-start.6
  20.0 0.8 %build_tile.9 = (bf16[512,1024]{1,0:T(8,128)(2,1)S(1)}, f32[16,512]{1,0:T(8,128)S(1)}, f32[512,1]{1,0:T(8,128)S(1)}) custom-call(bf16[512,256]{1,0:T(8,128)(2,1)S(1)} %collective-permute-done.1.refs_0_.refs_2_, bf16[576,256]{1,0:T(8,128)(2,1)S(1)} %pack.1.refs_1_, bf16[576,256]{1,0:T(8,128)(2,1)S(1)} %collective-permute-done.4.refs_2_), custom_call_target="tpu_custom_call" | custom-call | flops 16777216 | bytes 1024 | tf_op jit(solution)/shard_map/build_tiles/build_tile/pallas_call | solution.py:138
  20.8 1.9 %build_tile.10 = (bf16[1536,1024]{1,0:T(8,128)(2,1)S(1)}, f32[16,1536]{1,0:T(8,128)S(1)}) custom-call(bf16[512,256]{1,0:T(8,128)(2,1)S(1)} %constant_dynamic-slice_fusion.points_ref.refs_0_, bf16[512,256]{1,0:T(8,128)(2,1)S(1)} %collective-permute-done.refs_0_.refs_1_, bf16[512,256]{1,0:T(8,128)(2,1)S(1)} %collective-permute-done.1.refs_0_.refs_2_, ...), custom_call_target="tpu_custom_call" | custom-call | flops 50331648 | bytes 1024 | tf_op jit(solution)/shard_map/build_tiles/build_tile/pallas_call | solution.py:138
  22.7 1.1 %fusion = (bf16[576,256]{1,0:T(8,128)(2,1)S(1)}, bf16[576,256]{1,0:T(8,128)(2,1)S(1)}) fusion(bf16[1152,256]{1,0:T(8,128)(2,1)} %collective-permute-done.7), kind=kLoop, calls=%fused_computation.4 | loop fusion | bytes 1179648 | tf_op jit(solution)/shard_map/fetch_points/slice | solution.py:269
  23.9 1.9 %build_tile.11 = (bf16[1536,1024]{1,0:T(8,128)(2,1)S(1)}, f32[16,1536]{1,0:T(8,128)S(1)}) custom-call(bf16[512,256]{1,0:T(8,128)(2,1)S(1)} %constant_dynamic-slice_fusion.points_ref.refs_0_, bf16[512,256]{1,0:T(8,128)(2,1)S(1)} %collective-permute-done.refs_0_.refs_1_, bf16[512,256]{1,0:T(8,128)(2,1)S(1)} %collective-permute-done.1.refs_0_.refs_2_, ...), custom_call_target="tpu_custom_call" | custom-call | flops 50331648 | bytes 1024 | tf_op jit(solution)/shard_map/build_tiles/build_tile/pallas_call | solution.py:138
  25.8 1.8 %collective-permute-done.5.refs_0_.refs_3_ = bf16[512,256]{1,0:T(8,128)(2,1)S(1)} collective-permute-done((bf16[512,256]{1,0:T(8,128)(2,1)S(1)}, bf16[512,256]{1,0:T(8,128)(2,1)S(1)}, u32[]{:S(2)}, u32[]{:S(2)}) %collective-permute-start.5) | collective-permute-done | bytes 262176 | tf_op jit(solution)/shard_map/fetch_points/ppermute | solution.py:31
  27.6 2.9 %collective-permute-start.8 = (bf16[576,256]{1,0:T(8,128)(2,1)S(1)}, bf16[576,256]{1,0:T(8,128)(2,1)S(1)}, u32[]{:S(2)}, u32[]{:S(2)}) collective-permute-start(bf16[576,256]{1,0:T(8,128)(2,1)S(1)} %collective-permute-done.6.refs_4_), channel_id=1, source_target_pairs={{0,4},{4,0},{1,5},{5,1},{2,6},{6,2},{3,7},{7,3},{8,12},{12,8},{9,1... | collective-permute-start | bytes 884744 | tf_op jit(solution)/shard_map/build_tiles/ppermute | solution.py:23
  30.4 2.0 %build_tile.12 = (bf16[512,3072]{1,0:T(8,128)(2,1)S(1)}, f32[16,512]{1,0:T(8,128)S(1)}, f32[512,1]{1,0:T(8,128)S(1)}) custom-call(bf16[512,256]{1,0:T(8,128)(2,1)S(1)} %collective-permute-done.5.refs_0_.refs_3_, bf16[576,256]{1,0:T(8,128)(2,1)S(1)} %pack.1.refs_1_, bf16[576,256]{1,0:T(8,128)(2,1)S(1)} %collective-permute-done.4.refs_2_, ...), custom_call_target="tpu_custom_call" | custom-call | flops 50331648 | bytes 1024 | tf_op jit(solution)/shard_map/build_tiles/build_tile/pallas_call | solution.py:138
  32.4 2.5 %build_tile.13 = (bf16[2048,1024]{1,0:T(8,128)(2,1)S(1)}, f32[16,2048]{1,0:T(8,128)S(1)}) custom-call(bf16[512,256]{1,0:T(8,128)(2,1)S(1)} %constant_dynamic-slice_fusion.points_ref.refs_0_, bf16[512,256]{1,0:T(8,128)(2,1)S(1)} %collective-permute-done.refs_0_.refs_1_, bf16[512,256]{1,0:T(8,128)(2,1)S(1)} %collective-permute-done.1.refs_0_.refs_2_, ...), custom_call_target="tpu_custom_call" | custom-call | flops 67108864 | bytes 1024 | tf_op jit(solution)/shard_map/build_tiles/build_tile/pallas_call | solution.py:138
  34.9 0.6 collective-permute-start.11
  35.6 1.7 %collective-permute-start.10 = (f32[16,2048]{1,0:T(8,128)S(1)}, f32[16,2048]{1,0:T(8,128)S(1)}, u32[]{:S(2)}, u32[]{:S(2)}) collective-permute-start(f32[16,2048]{1,0:T(8,128)S(1)} %get-tuple-element.55.refs_0_), channel_id=1, source_target_pairs={{0,16},{8,24},{16,0},{24,8},{1,17},{9,25},{17,1},{25,9},{2,18},{10... | collective-permute-start | bytes 393224 | tf_op jit(solution)/shard_map/sum_over_z/ppermute | solution.py:23
  37.3 4.0 %collective-permute-done.11.refs_3_ = f32[16,2048]{1,0:T(8,128)S(1)} collective-permute-done((f32[16,2048]{1,0:T(8,128)S(1)}, f32[16,2048]{1,0:T(8,128)S(1)}, u32[]{:S(2)}, u32[]{:S(2)}) %collective-permute-start.11) | collective-permute-done | bytes 131104 | tf_op jit(solution)/shard_map/sum_over_z/ppermute | solution.py:23
  41.3 2.0 %collective-permute-done.10.refs_2_ = f32[16,2048]{1,0:T(8,128)S(1)} collective-permute-done((f32[16,2048]{1,0:T(8,128)S(1)}, f32[16,2048]{1,0:T(8,128)S(1)}, u32[]{:S(2)}, u32[]{:S(2)}) %collective-permute-start.10) | collective-permute-done | bytes 131104 | tf_op jit(solution)/shard_map/sum_over_z/ppermute | solution.py:23
  43.2 1.7 %collective-permute-done.9.refs_1_ = f32[16,2048]{1,0:T(8,128)S(1)} collective-permute-done((f32[16,2048]{1,0:T(8,128)S(1)}, f32[16,2048]{1,0:T(8,128)S(1)}, u32[]{:S(2)}, u32[]{:S(2)}) %collective-permute-start.9) | collective-permute-done | bytes 131104 | tf_op jit(solution)/shard_map/sum_over_z/ppermute | solution.py:23
  45.0 2.7 %second_product.1 = (f32[16,2048]{1,0:T(8,128)S(1)}, f32[16,2048]{1,0:T(8,128)S(1)}, f32[16,512]{1,0:T(8,128)S(1)}) custom-call(f32[16,2048]{1,0:T(8,128)S(1)} %get-tuple-element.55.refs_0_, f32[16,2048]{1,0:T(8,128)S(1)} %collective-permute-done.9.refs_1_, f32[16,2048]{1,0:T(8,128)S(1)} %collective-permute-done.10.refs_2_, ...), custom_call_target="tpu_custom_call" | custom-call | flops 268435456 | bytes 1024 | tf_op jit(solution)/shard_map/second_product/pallas_call | solution.py:181
  47.7 1.4 %collective-permute-done.12 = f32[16,2048]{1,0:T(8,128)S(1)} collective-permute-done((f32[16,2048]{1,0:T(8,128)S(1)}, f32[16,2048]{1,0:T(8,128)S(1)}, u32[]{:S(2)}, u32[]{:S(2)}) %collective-permute-start.12) | collective-permute-done | bytes 131104 | tf_op jit(solution)/shard_map/sum_over_yc/ppermute | solution.py:23
  49.1 2.8 %collective-permute-start.15 = (f32[16,512]{1,0:T(8,128)S(1)}, f32[16,512]{1,0:T(8,128)S(1)}, u32[]{:S(2)}, u32[]{:S(2)}) collective-permute-start(f32[16,512]{1,0:T(8,128)S(1)} %get-tuple-element.72), channel_id=1, source_target_pairs={{0,64},{32,96},{64,0},{96,32},{1,65},{33,97},{65,1},{97,33},{2,66}... | collective-permute-start | bytes 98312 | tf_op jit(solution)/shard_map/sum_over_yc/ppermute | solution.py:23
  51.9 3.2 %collective-permute-start.13 = (f32[16,512]{1,0:T(8,128)S(1)}, f32[16,512]{1,0:T(8,128)S(1)}, u32[]{:S(2)}, u32[]{:S(2)}) collective-permute-start(f32[16,512]{1,0:T(8,128)S(1)} %get-tuple-element.74), channel_id=1, source_target_pairs={{0,96},{32,0},{64,32},{96,64},{1,97},{33,1},{65,33},{97,65},{2,98}... | collective-permute-start | bytes 98312 | tf_op jit(solution)/shard_map/sum_over_yc/ppermute | solution.py:23
  55.2 1.9 %collective-permute-done.14.refs_2_ = f32[16,512]{1,0:T(8,128)S(1)} collective-permute-done((f32[16,512]{1,0:T(8,128)S(1)}, f32[16,512]{1,0:T(8,128)S(1)}, u32[]{:S(2)}, u32[]{:S(2)}) %collective-permute-start.14) | collective-permute-done | bytes 32800 | tf_op jit(solution)/shard_map/sum_over_yc/ppermute | solution.py:23
  57.2 12.8 %all_to_all.5.sums_ref = f32[32,8,128]{2,1,0:T(8,128)S(1)} all-to-all(f32[32,8,128]{2,1,0:T(8,128)S(1)} %broadcast_in_dim.3), channel_id=1, replica_groups=mesh['y'=4,'z'=4,'c'=2,'x'=4] {'y','z','c'}, dimensions={0} | all-to-all | bytes 262144 | tf_op jit(solution)/shard_map/final_sums/all_to_all | solution.py:310
  70.0 0.9 %finish.1 = (f32[16,512]{1,0:T(8,128)}, f32[16,512]{1,0:T(8,128)}) custom-call(f32[16,512]{1,0:T(8,128)S(1)} %bitcast.10, f32[16,512]{1,0:T(8,128)S(1)} %get-tuple-element.63.rho_ref, f32[16,512]{1,0:T(8,128)S(1)} %get-tuple-element.66.image_ref, f32[32,8,128]{2,1,0:T(8,128)S(1)} %all_to_all.5.sums_ref), custom_call_target="tpu_custom_call" | custom-call | tf_op jit(solution)/shard_map/finish/pallas_call | solution.py:241
  (36 shorter events, 1.2 us)
Async XLA Ops:
  0.6 1.1 %copy-start = (bf16[1024,256]{1,0:T(8,128)(2,1)S(1)}, bf16[1024,256]{1,0:T(8,128)(2,1)}, u32[]{:S(2)}) copy-start(bf16[1024,256]{1,0:T(8,128)(2,1)} %param.3) | copy-start | bytes 1572868
  1.8 0.8 %copy-start.5 = (f32[512,16]{0,1:T(8,128)S(1)}, f32[512,16]{0,1:T(8,128)}, u32[]{:S(2)}) copy-start(f32[512,16]{0,1:T(8,128)} %param.5) | copy-start | bytes 98308
  2.8 7.3 %collective-permute-start.4 = (bf16[576,256]{1,0:T(8,128)(2,1)S(1)}, bf16[576,256]{1,0:T(8,128)(2,1)S(1)}, u32[]{:S(2)}, u32[]{:S(2)}) collective-permute-start(bf16[576,256]{1,0:T(8,128)(2,1)S(1)} %pack.1.refs_1_), channel_id=1, source_target_pairs={{0,4},{4,0},{1,5},{5,1},{2,6},{6,2},{3,7},{7,3},{8,12},{12,8},{9,1... | collective-permute-start | bytes 884744 | tf_op jit(solution)/shard_map/fetch_points/ppermute | solution.py:23
  2.9 15.7 %collective-permute-start.3 = (bf16[576,256]{1,0:T(8,128)(2,1)S(1)}, bf16[576,256]{1,0:T(8,128)(2,1)S(1)}, u32[]{:S(2)}, u32[]{:S(2)}) collective-permute-start(bf16[576,256]{1,0:T(8,128)(2,1)S(1)} %pack.1.refs_1_), channel_id=1, source_target_pairs={{0,96},{32,0},{64,32},{96,64},{1,97},{33,1},{65,33},{97,65},{2,98}... | collective-permute-start | bytes 884744 | tf_op jit(solution)/shard_map/fetch_points/ppermute | solution.py:23
  6.1 12.5 %collective-permute-start.2 = (bf16[576,256]{1,0:T(8,128)(2,1)S(1)}, bf16[576,256]{1,0:T(8,128)(2,1)S(1)}, u32[]{:S(2)}, u32[]{:S(2)}) collective-permute-start(bf16[576,256]{1,0:T(8,128)(2,1)S(1)} %pack.1.refs_1_), channel_id=1, source_target_pairs={{0,32},{32,64},{64,96},{96,0},{1,33},{33,65},{65,97},{97,1},{2,34}... | collective-permute-start | bytes 884744 | tf_op jit(solution)/shard_map/fetch_points/ppermute | solution.py:23
  6.1 10.7 %collective-permute-start = (bf16[512,256]{1,0:T(8,128)(2,1)S(1)}, bf16[512,256]{1,0:T(8,128)(2,1)S(1)}, u32[]{:S(2)}, u32[]{:S(2)}) collective-permute-start(bf16[512,256]{1,0:T(8,128)(2,1)S(1)} %constant_dynamic-slice_fusion.points_ref.refs_0_), channel_id=1, source_target_pairs={{0,8},{8,16},{16,24},{24,0},{1,9},{9,17},{17,25},{25,1},{2,10},{10... | collective-permute-start | bytes 786440 | tf_op jit(solution)/shard_map/fetch_points/ppermute | solution.py:23
  8.0 10.6 %collective-permute-start.1 = (bf16[512,256]{1,0:T(8,128)(2,1)S(1)}, bf16[512,256]{1,0:T(8,128)(2,1)S(1)}, u32[]{:S(2)}, u32[]{:S(2)}) collective-permute-start(bf16[512,256]{1,0:T(8,128)(2,1)S(1)} %constant_dynamic-slice_fusion.points_ref.refs_0_), channel_id=1, source_target_pairs={{0,24},{8,0},{16,8},{24,16},{1,25},{9,1},{17,9},{25,17},{2,26},{10... | collective-permute-start | bytes 786440 | tf_op jit(solution)/shard_map/fetch_points/ppermute | solution.py:23
  10.1 0.8 %copy-start.6 = (f32[512,16]{0,1:T(8,128)S(1)}, f32[512,16]{0,1:T(8,128)}, u32[]{:S(2)}) copy-start(f32[512,16]{0,1:T(8,128)} %param.5) | copy-start | bytes 98308
  11.7 1.0 %copy-start.1 = (bf16[512,1024]{1,0:T(8,128)(2,1)}, bf16[512,1024]{1,0:T(8,128)(2,1)S(1)}, u32[]{:S(2)}) copy-start(bf16[512,1024]{1,0:T(8,128)(2,1)S(1)} %get-tuple-element.56.refs_4_) | copy-start | bytes 3145732
  17.6 1.0 %copy-start.3 = (bf16[512,1024]{1,0:T(8,128)(2,1)}, bf16[512,1024]{1,0:T(8,128)(2,1)S(1)}, u32[]{:S(2)}) copy-start(bf16[512,1024]{1,0:T(8,128)(2,1)S(1)} %get-tuple-element.57.refs_5_) | copy-start | bytes 3145732
  19.4 3.3 %collective-permute-start.7 = (bf16[1152,256]{1,0:T(8,128)(2,1)}, bf16[1152,256]{1,0:T(8,128)(2,1)}, u32[]{:S(2)}, u32[]{:S(2)}) collective-permute-start(bf16[1152,256]{1,0:T(8,128)(2,1)} %pad_maximum_fusion), channel_id=1, source_target_pairs={{0,4},{4,0},{1,5},{5,1},{2,6},{6,2},{3,7},{7,3},{8,12},{12,8},{9,1... | collective-permute-start | bytes 1769480 | tf_op jit(solution)/shard_map/fetch_points/ppermute | solution.py:23
  19.5 8.1 %collective-permute-start.6 = (bf16[576,256]{1,0:T(8,128)(2,1)S(1)}, bf16[576,256]{1,0:T(8,128)(2,1)S(1)}, u32[]{:S(2)}, u32[]{:S(2)}) collective-permute-start(bf16[576,256]{1,0:T(8,128)(2,1)S(1)} %broadcast_select_fusion), channel_id=1, source_target_pairs={{0,32},{4,100},{32,64},{36,4},{64,96},{68,36},{96,0},{100,68},{1,3... | collective-permute-start | bytes 884744 | tf_op jit(solution)/shard_map/fetch_points/ppermute | solution.py:31
  19.9 7.7 %collective-permute-start.5 = (bf16[512,256]{1,0:T(8,128)(2,1)S(1)}, bf16[512,256]{1,0:T(8,128)(2,1)S(1)}, u32[]{:S(2)}, u32[]{:S(2)}) collective-permute-start(bf16[512,256]{1,0:T(8,128)(2,1)S(1)} %broadcast_select_fusion.1), channel_id=1, source_target_pairs={{0,8},{4,28},{8,16},{12,4},{16,24},{20,12},{24,0},{28,20},{1,9},{5... | collective-permute-start | bytes 786440 | tf_op jit(solution)/shard_map/fetch_points/ppermute | solution.py:31
  23.9 21.1 %copy-start.2 = (bf16[512,1024]{1,0:T(8,128)(2,1)S(1)}, bf16[512,1024]{1,0:T(8,128)(2,1)}, u32[]{:S(2)}) copy-start(bf16[512,1024]{1,0:T(8,128)(2,1)} %copy-done.1) | copy-start | bytes 3145732
  23.9 21.1 %copy-start.4 = (bf16[512,1024]{1,0:T(8,128)(2,1)S(1)}, bf16[512,1024]{1,0:T(8,128)(2,1)}, u32[]{:S(2)}) copy-start(bf16[512,1024]{1,0:T(8,128)(2,1)} %copy-done.3) | copy-start | bytes 3145732
  27.6 4.9 %collective-permute-start.8 = (bf16[576,256]{1,0:T(8,128)(2,1)S(1)}, bf16[576,256]{1,0:T(8,128)(2,1)S(1)}, u32[]{:S(2)}, u32[]{:S(2)}) collective-permute-start(bf16[576,256]{1,0:T(8,128)(2,1)S(1)} %collective-permute-done.6.refs_4_), channel_id=1, source_target_pairs={{0,4},{4,0},{1,5},{5,1},{2,6},{6,2},{3,7},{7,3},{8,12},{12,8},{9,1... | collective-permute-start | bytes 884744 | tf_op jit(solution)/shard_map/build_tiles/ppermute | solution.py:23
  34.9 6.4 %collective-permute-start.11 = (f32[16,2048]{1,0:T(8,128)S(1)}, f32[16,2048]{1,0:T(8,128)S(1)}, u32[]{:S(2)}, u32[]{:S(2)}) collective-permute-start(f32[16,2048]{1,0:T(8,128)S(1)} %get-tuple-element.55.refs_0_), channel_id=1, source_target_pairs={{0,24},{8,0},{16,8},{24,16},{1,25},{9,1},{17,9},{25,17},{2,26},{10... | collective-permute-start | bytes 393224 | tf_op jit(solution)/shard_map/sum_over_z/ppermute | solution.py:23
  35.6 7.7 %collective-permute-start.10 = (f32[16,2048]{1,0:T(8,128)S(1)}, f32[16,2048]{1,0:T(8,128)S(1)}, u32[]{:S(2)}, u32[]{:S(2)}) collective-permute-start(f32[16,2048]{1,0:T(8,128)S(1)} %get-tuple-element.55.refs_0_), channel_id=1, source_target_pairs={{0,16},{8,24},{16,0},{24,8},{1,17},{9,25},{17,1},{25,9},{2,18},{10... | collective-permute-start | bytes 393224 | tf_op jit(solution)/shard_map/sum_over_z/ppermute | solution.py:23
  37.3 7.7 %collective-permute-start.9 = (f32[16,2048]{1,0:T(8,128)S(1)}, f32[16,2048]{1,0:T(8,128)S(1)}, u32[]{:S(2)}, u32[]{:S(2)}) collective-permute-start(f32[16,2048]{1,0:T(8,128)S(1)} %get-tuple-element.55.refs_0_), channel_id=1, source_target_pairs={{0,8},{8,16},{16,24},{24,0},{1,9},{9,17},{17,25},{25,1},{2,10},{10... | collective-permute-start | bytes 393224 | tf_op jit(solution)/shard_map/sum_over_z/ppermute | solution.py:23
  45.0 12.1 %copy-start.7 = (f32[512,16]{0,1:T(8,128)S(1)}, f32[512,16]{0,1:T(8,128)}, u32[]{:S(2)}) copy-start(f32[512,16]{0,1:T(8,128)} %param.5) | copy-start | bytes 98308
  47.7 1.4 %collective-permute-start.12 = (f32[16,2048]{1,0:T(8,128)S(1)}, f32[16,2048]{1,0:T(8,128)S(1)}, u32[]{:S(2)}, u32[]{:S(2)}) collective-permute-start(f32[16,2048]{1,0:T(8,128)S(1)} %get-tuple-element.65), channel_id=1, source_target_pairs={{0,4},{4,0},{1,5},{5,1},{2,6},{6,2},{3,7},{7,3},{8,12},{12,8},{9,1... | collective-permute-start | bytes 393224 | tf_op jit(solution)/shard_map/sum_over_yc/ppermute | solution.py:23
  49.1 6.0 %collective-permute-start.15 = (f32[16,512]{1,0:T(8,128)S(1)}, f32[16,512]{1,0:T(8,128)S(1)}, u32[]{:S(2)}, u32[]{:S(2)}) collective-permute-start(f32[16,512]{1,0:T(8,128)S(1)} %get-tuple-element.72), channel_id=1, source_target_pairs={{0,64},{32,96},{64,0},{96,32},{1,65},{33,97},{65,1},{97,33},{2,66}... | collective-permute-start | bytes 98312 | tf_op jit(solution)/shard_map/sum_over_yc/ppermute | solution.py:23
  51.9 5.1 %collective-permute-start.14 = (f32[16,512]{1,0:T(8,128)S(1)}, f32[16,512]{1,0:T(8,128)S(1)}, u32[]{:S(2)}, u32[]{:S(2)}) collective-permute-start(f32[16,512]{1,0:T(8,128)S(1)} %get-tuple-element.73), channel_id=1, source_target_pairs={{0,32},{32,64},{64,96},{96,0},{1,33},{33,65},{65,97},{97,1},{2,34}... | collective-permute-start | bytes 98312 | tf_op jit(solution)/shard_map/sum_over_yc/ppermute | solution.py:23
  51.9 5.1 %collective-permute-start.13 = (f32[16,512]{1,0:T(8,128)S(1)}, f32[16,512]{1,0:T(8,128)S(1)}, u32[]{:S(2)}, u32[]{:S(2)}) collective-permute-start(f32[16,512]{1,0:T(8,128)S(1)} %get-tuple-element.74), channel_id=1, source_target_pairs={{0,96},{32,0},{64,32},{96,64},{1,97},{33,1},{65,33},{97,65},{2,98}... | collective-permute-start | bytes 98312 | tf_op jit(solution)/shard_map/sum_over_yc/ppermute | solution.py:23

commit v8 on v7

--- a/solution.py
+++ b/solution.py
@@ -138,7 +138,7 @@
     return pl.pallas_call(
         functools.partial(tile_kernel, counts, probes),
         out_shape=out_shape,
-        compiler_params=pltpu.CompilerParams(vmem_limit_bytes=16 << 20),
+        compiler_params=pltpu.CompilerParams(vmem_limit_bytes=8 << 20),
         cost_estimate=pl.CostEstimate(
             flops=height * width * features // 8, bytes_accessed=1 << 10, transcendentals=0
         ),
@@ -186,7 +186,7 @@
             jax.ShapeDtypeStruct((probes, cols // NC), jnp.float32),
             jax.ShapeDtypeStruct((probes, own), jnp.float32),
         ],
-        compiler_params=pltpu.CompilerParams(vmem_limit_bytes=16 << 20),
+        compiler_params=pltpu.CompilerParams(vmem_limit_bytes=8 << 20),
         cost_estimate=pl.CostEstimate(flops=rows * cols * 32, bytes_accessed=1 << 10, transcendentals=0),
         name="second_product",
     )(*parts, *[tile for tile, _, _ in tiles])
@@ -265,8 +265,8 @@
         row[1], row[3], col[0, 1], col[0, 3] = near
         row[2] = hand_on(row[1], row[3], "z", NZ)
         col[0, 2] = hand_on(col[0, 1], col[0, 3], "y", NY)
-        pair = shift(jnp.concatenate([col[0, 1], col[0, 3]], axis=0), "c", NC, 1)
-        col[1, 1], col[1, 3] = pair[: message.shape[0]], pair[message.shape[0] :]
+        for k in (1, 3):
+            col[1, k] = shift(col[0, k], "c", NC, 1)
 
     with jax.named_scope("build_tiles"):
         near = [points, row[1], row[3]]
@@ -274,13 +274,15 @@
         half = [half_a, half_b, half_c]
         tile_d, image = build(near, [col[0, 1], col[0, 3]], own, probes, half, [image_a, image_b, image_c])
         tile_e, image = build(near, [col[1, 1], col[1, 3]], own, probes, half, [image])
-        far, image = lax.optimization_barrier(((row[2], col[0, 2]), image))
-        row[2], col[0, 2] = far
+        at = [col[k] for k in COLS[:6]]
+        row[2], image = lax.optimization_barrier((row[2], image))
+        tile_f, image_far, half_far = build([row[2]], at, own, probes)
+        col[0, 2], image_far = lax.optimization_barrier((col[0, 2], image_far))
         col[1, 2] = shift(col[0, 2], "c", NC, 1)
-        at = [col[k] for k in COLS[:6]]
-        tile_f, image_far, half_far = build([row[2]], at, own, probes)
-        at = [col[0, 2], col[1, 2]]
-        tile_g, image = build(near + [row[2]], at, own, probes, half + [half_far], [image, image_far])
+        near.append(row[2])
+        half.append(half_far)
+        tile_g, image = build(near, [col[0, 2]], own, probes, half, [image, image_far])
+        tile_h, image = build(near, [col[1, 2]], own, probes, half, [image])
         tiles = [
             (tile_a, 0, 0),
             (tile_b, own, 0),
@@ -289,6 +291,7 @@
             (tile_e, 0, 4 * own),
             (tile_f, 3 * own, 0),
             (tile_g, 0, 6 * own),
+            (tile_h, 0, 7 * own),
         ]
 
     with jax.named_scope("sum_over_z"):

time: 72.3 us -> 70.7 us (0.978)
  local copies, waits for them, and re-layouts: 5.05 us -> 1.95 us
  waiting for transfers between devices: 16.8 us -> 19.3 us
  other arithmetic: 0.94 us -> 0.08 us
    unnamed x16 -> x8, local copies, waits for them, and re-layouts: 3.85 us -> 1.86 us
    ppermute x14 -> x15, waiting for transfers between devices: 15 us -> 16.7 us  [shift(): lax.ppermute(value, axis, [(i, (i + step) % size) for i in range(size)])]
    slice x1 -> x0, local copies, waits for them, and re-layouts: 1.11 us -> none  [on_device(): col[1, 1], col[1, 3] = (pair[:message.shape[0]], pair[message.shape[0]:])]
    concatenate x1 -> x0, other arithmetic: 0.87 us -> none  [on_device(): pair = shift(jnp.concatenate([col[0, 1], col[0, 3]], axis=0), 'c', NC, 1)]
    ppermute x2, waiting for transfers between devices: 1.76 us -> 2.55 us  [hand_on(): return lax.ppermute(value, (axis, 'c'), pairs)]
    ppermute x14 -> x15, starting transfers between devices: 18.5 us -> 17.9 us  [shift(): lax.ppermute(value, axis, [(i, (i + step) % size) for i in range(size)])]
    pallas_call x7 -> x8, Pallas kernels: 10.9 us -> 11.2 us  [build(): pl.pallas_call(functools.partial(tile_kernel, counts, probes), out_shape=...]
  transfers between devices with their start and end apart: 16 -> 17, of which waited for: 7 -> 7; matrix products, arithmetic and copies ran while one was open for 2% -> 0% of each run, Pallas kernels for 12% -> 14%
where the time goes in v8:
time: 70.7 us; the launch traced here: 69.3 us
  waiting for transfers between devices  19.3 us (27%)
  starting transfers between devices  18.7 us (26%)
  Pallas kernels  15.3 us (22%)
  blocking collectives  12.7 us (18%)
  local copies, waits for them, and re-layouts  1.95 us (3%)
  between operations  1.45 us (2%)
    ppermute x15, starting transfers between devices, shift(): lax.ppermute(value, axis, [(i, (i + step) % size) for i in range(size)])  17.9 us
    ppermute x15, waiting for transfers between devices, shift(): lax.ppermute(value, axis, [(i, (i + step) % size) for i in range(size)])  16.7 us
    all_to_all x1, blocking collectives, on_device(): sums = lax.all_to_all(sums, ('y', 'z', 'c'), 0, 0, tiled=True)  12.7 us
    pallas_call x8, Pallas kernels, build(): pl.pallas_call(functools.partial(tile_kernel, counts, probes), out_shape=...  11.2 us
    pallas_call x1, Pallas kernels, second_product(): pl.pallas_call(functools.partial(second_kernel, own, places), in_specs=[p...  2.73 us
    ppermute x2, waiting for transfers between devices, hand_on(): return lax.ppermute(value, (axis, 'c'), pairs)  2.55 us
    unnamed x8, local copies, waits for them, and re-layouts  1.86 us
  transfers between devices with their start and end apart: 17, of which 7 were waited for; matrix products, arithmetic and copies ran while one was open for 0% of the time, Pallas kernels for 14%

profile of v8, /device:TPU:0, one launch (start us, length us, event | category | flops | bytes accessed | tf_op | source)
XLA Modules:
  0.0 69.3 jit_solution(5929924043429900257)
XLA Ops:
  1.4 0.3 copy-done
  1.8 0.7 %copy-done.1 = f32[512,16]{0,1:T(8,128)S(1)} copy-done((f32[512,16]{0,1:T(8,128)S(1)}, f32[512,16]{0,1:T(8,128)}, u32[]{:S(2)}) %copy-start.1) | copy-done | bytes 32792
  2.9 3.2 %collective-permute-start.3 = (bf16[576,256]{1,0:T(8,128)(2,1)S(1)}, bf16[576,256]{1,0:T(8,128)(2,1)S(1)}, u32[]{:S(2)}, u32[]{:S(2)}) collective-permute-start(bf16[576,256]{1,0:T(8,128)(2,1)S(1)} %pack.1.refs_1_), channel_id=1, source_target_pairs={{0,96},{32,0},{64,32},{96,64},{1,97},{33,1},{65,33},{97,65},{2,98}... | collective-permute-start | bytes 884744 | tf_op jit(solution)/shard_map/fetch_points/ppermute | solution.py:23
  6.1 1.9 %collective-permute-start = (bf16[512,256]{1,0:T(8,128)(2,1)S(1)}, bf16[512,256]{1,0:T(8,128)(2,1)S(1)}, u32[]{:S(2)}, u32[]{:S(2)}) collective-permute-start(bf16[512,256]{1,0:T(8,128)(2,1)S(1)} %constant_dynamic-slice_fusion.points_ref.refs_0_), channel_id=1, source_target_pairs={{0,8},{8,16},{16,24},{24,0},{1,9},{9,17},{17,25},{25,1},{2,10},{10... | collective-permute-start | bytes 786440 | tf_op jit(solution)/shard_map/fetch_points/ppermute | solution.py:23
  8.0 2.1 %collective-permute-start.1 = (bf16[512,256]{1,0:T(8,128)(2,1)S(1)}, bf16[512,256]{1,0:T(8,128)(2,1)S(1)}, u32[]{:S(2)}, u32[]{:S(2)}) collective-permute-start(bf16[512,256]{1,0:T(8,128)(2,1)S(1)} %constant_dynamic-slice_fusion.points_ref.refs_0_), channel_id=1, source_target_pairs={{0,24},{8,0},{16,8},{24,16},{1,25},{9,1},{17,9},{25,17},{2,26},{10... | collective-permute-start | bytes 786440 | tf_op jit(solution)/shard_map/fetch_points/ppermute | solution.py:23
  10.1 0.8 %copy-done.2 = f32[512,16]{0,1:T(8,128)S(1)} copy-done((f32[512,16]{0,1:T(8,128)S(1)}, f32[512,16]{0,1:T(8,128)}, u32[]{:S(2)}) %copy-start.2) | copy-done | bytes 32792
  10.9 0.8 %build_tile.8 = (bf16[512,1024]{1,0:T(8,128)(2,1)S(1)}, f32[16,512]{1,0:T(8,128)S(1)}, f32[512,1]{1,0:T(8,128)S(1)}) custom-call(bf16[512,256]{1,0:T(8,128)(2,1)S(1)} %constant_dynamic-slice_fusion.points_ref.refs_0_, bf16[576,256]{1,0:T(8,128)(2,1)S(1)} %pack.1.refs_1_, bf16[576,256]{1,0:T(8,128)(2,1)S(1)} %collective-permute-done.4.refs_2_, ...), custom_call_target="tpu_custom_call" | custom-call | flops 16777216 | bytes 1024 | tf_op jit(solution)/shard_map/fetch_points/build_tile/pallas_call | solution.py:138
  11.7 5.0 %collective-permute-done.refs_0_.refs_1_ = bf16[512,256]{1,0:T(8,128)(2,1)S(1)} collective-permute-done((bf16[512,256]{1,0:T(8,128)(2,1)S(1)}, bf16[512,256]{1,0:T(8,128)(2,1)S(1)}, u32[]{:S(2)}, u32[]{:S(2)}) %collective-permute-start) | collective-permute-done | bytes 262176 | tf_op jit(solution)/shard_map/fetch_points/ppermute | solution.py:23
  16.7 0.8 %build_tile.9 = (bf16[512,1024]{1,0:T(8,128)(2,1)S(1)}, f32[16,512]{1,0:T(8,128)S(1)}, f32[512,1]{1,0:T(8,128)S(1)}) custom-call(bf16[512,256]{1,0:T(8,128)(2,1)S(1)} %collective-permute-done.refs_0_.refs_1_, bf16[576,256]{1,0:T(8,128)(2,1)S(1)} %pack.1.refs_1_, bf16[576,256]{1,0:T(8,128)(2,1)S(1)} %collective-permute-done.4.refs_2_), custom_call_target="tpu_custom_call" | custom-call | flops 16777216 | bytes 1024 | tf_op jit(solution)/shard_map/fetch_points/build_tile/pallas_call | solution.py:138
  17.7 0.5 collective-permute-start.7
  18.2 0.4 collective-permute-start.8
  18.7 0.4 collective-permute-start.5
  19.0 0.8 %build_tile.10 = (bf16[512,1024]{1,0:T(8,128)(2,1)S(1)}, f32[16,512]{1,0:T(8,128)S(1)}, f32[512,1]{1,0:T(8,128)S(1)}) custom-call(bf16[512,256]{1,0:T(8,128)(2,1)S(1)} %collective-permute-done.1.refs_0_.refs_2_, bf16[576,256]{1,0:T(8,128)(2,1)S(1)} %pack.1.refs_1_, bf16[576,256]{1,0:T(8,128)(2,1)S(1)} %collective-permute-done.4.refs_2_), custom_call_target="tpu_custom_call" | custom-call | flops 16777216 | bytes 1024 | tf_op jit(solution)/shard_map/build_tiles/build_tile/pallas_call | solution.py:138
  19.9 1.9 %build_tile.11 = (bf16[1536,1024]{1,0:T(8,128)(2,1)S(1)}, f32[16,1536]{1,0:T(8,128)S(1)}) custom-call(bf16[512,256]{1,0:T(8,128)(2,1)S(1)} %constant_dynamic-slice_fusion.points_ref.refs_0_, bf16[512,256]{1,0:T(8,128)(2,1)S(1)} %collective-permute-done.refs_0_.refs_1_, bf16[512,256]{1,0:T(8,128)(2,1)S(1)} %collective-permute-done.1.refs_0_.refs_2_, ...), custom_call_target="tpu_custom_call" | custom-call | flops 50331648 | bytes 1024 | tf_op jit(solution)/shard_map/build_tiles/build_tile/pallas_call | solution.py:138
  21.8 1.9 %build_tile.12 = (bf16[1536,1024]{1,0:T(8,128)(2,1)S(1)}, f32[16,1536]{1,0:T(8,128)S(1)}) custom-call(bf16[512,256]{1,0:T(8,128)(2,1)S(1)} %constant_dynamic-slice_fusion.points_ref.refs_0_, bf16[512,256]{1,0:T(8,128)(2,1)S(1)} %collective-permute-done.refs_0_.refs_1_, bf16[512,256]{1,0:T(8,128)(2,1)S(1)} %collective-permute-done.1.refs_0_.refs_2_, ...), custom_call_target="tpu_custom_call" | custom-call | flops 50331648 | bytes 1024 | tf_op jit(solution)/shard_map/build_tiles/build_tile/pallas_call | solution.py:138
  23.8 2.5 %collective-permute-done.5.refs_0_.refs_3_ = bf16[512,256]{1,0:T(8,128)(2,1)S(1)} collective-permute-done((bf16[512,256]{1,0:T(8,128)(2,1)S(1)}, bf16[512,256]{1,0:T(8,128)(2,1)S(1)}, u32[]{:S(2)}, u32[]{:S(2)}) %collective-permute-start.5) | collective-permute-done | bytes 262176 | tf_op jit(solution)/shard_map/fetch_points/ppermute | solution.py:31
  26.3 2.1 %build_tile.13 = (bf16[512,3072]{1,0:T(8,128)(2,1)S(1)}, f32[16,512]{1,0:T(8,128)S(1)}, f32[512,1]{1,0:T(8,128)S(1)}) custom-call(bf16[512,256]{1,0:T(8,128)(2,1)S(1)} %collective-permute-done.5.refs_0_.refs_3_, bf16[576,256]{1,0:T(8,128)(2,1)S(1)} %pack.1.refs_1_, bf16[576,256]{1,0:T(8,128)(2,1)S(1)} %collective-permute-done.4.refs_2_, ...), custom_call_target="tpu_custom_call" | custom-call | flops 50331648 | bytes 1024 | tf_op jit(solution)/shard_map/build_tiles/build_tile/pallas_call | solution.py:138
  28.4 1.6 %collective-permute-start.9 = (bf16[576,256]{1,0:T(8,128)(2,1)S(1)}, bf16[576,256]{1,0:T(8,128)(2,1)S(1)}, u32[]{:S(2)}, u32[]{:S(2)}) collective-permute-start(bf16[576,256]{1,0:T(8,128)(2,1)S(1)} %collective-permute-done.8.refs_4_), channel_id=1, source_target_pairs={{0,4},{4,0},{1,5},{5,1},{2,6},{6,2},{3,7},{7,3},{8,12},{12,8},{9,1... | collective-permute-start | bytes 884744 | tf_op jit(solution)/shard_map/build_tiles/ppermute | solution.py:23
  29.9 1.3 %build_tile.14 = (bf16[2048,512]{1,0:T(8,128)(2,1)S(1)}, f32[16,2048]{1,0:T(8,128)S(1)}) custom-call(bf16[512,256]{1,0:T(8,128)(2,1)S(1)} %constant_dynamic-slice_fusion.points_ref.refs_0_, bf16[512,256]{1,0:T(8,128)(2,1)S(1)} %collective-permute-done.refs_0_.refs_1_, bf16[512,256]{1,0:T(8,128)(2,1)S(1)} %collective-permute-done.1.refs_0_.refs_2_, ...), custom_call_target="tpu_custom_call" | custom-call | flops 33554432 | bytes 1024 | tf_op jit(solution)/shard_map/build_tiles/build_tile/pallas_call | solution.py:138
  31.3 1.4 %build_tile.15 = (bf16[2048,512]{1,0:T(8,128)(2,1)S(1)}, f32[16,2048]{1,0:T(8,128)S(1)}) custom-call(bf16[512,256]{1,0:T(8,128)(2,1)S(1)} %constant_dynamic-slice_fusion.points_ref.refs_0_, bf16[512,256]{1,0:T(8,128)(2,1)S(1)} %collective-permute-done.refs_0_.refs_1_, bf16[512,256]{1,0:T(8,128)(2,1)S(1)} %collective-permute-done.1.refs_0_.refs_2_, ...), custom_call_target="tpu_custom_call" | custom-call | flops 33554432 | bytes 1024 | tf_op jit(solution)/shard_map/build_tiles/build_tile/pallas_call | solution.py:138
  32.7 2.0 %collective-permute-start.12 = (f32[16,2048]{1,0:T(8,128)S(1)}, f32[16,2048]{1,0:T(8,128)S(1)}, u32[]{:S(2)}, u32[]{:S(2)}) collective-permute-start(f32[16,2048]{1,0:T(8,128)S(1)} %get-tuple-element.60.refs_0_), channel_id=1, source_target_pairs={{0,24},{8,0},{16,8},{24,16},{1,25},{9,1},{17,9},{25,17},{2,26},{10... | collective-permute-start | bytes 393224 | tf_op jit(solution)/shard_map/sum_over_z/ppermute | solution.py:23
  34.8 0.8 %collective-permute-start.10 = (f32[16,2048]{1,0:T(8,128)S(1)}, f32[16,2048]{1,0:T(8,128)S(1)}, u32[]{:S(2)}, u32[]{:S(2)}) collective-permute-start(f32[16,2048]{1,0:T(8,128)S(1)} %get-tuple-element.60.refs_0_), channel_id=1, source_target_pairs={{0,8},{8,16},{16,24},{24,0},{1,9},{9,17},{17,25},{25,1},{2,10},{10... | collective-permute-start | bytes 393224 | tf_op jit(solution)/shard_map/sum_over_z/ppermute | solution.py:23
  35.6 5.0 %collective-permute-done.12.refs_3_ = f32[16,2048]{1,0:T(8,128)S(1)} collective-permute-done((f32[16,2048]{1,0:T(8,128)S(1)}, f32[16,2048]{1,0:T(8,128)S(1)}, u32[]{:S(2)}, u32[]{:S(2)}) %collective-permute-start.12) | collective-permute-done | bytes 131104 | tf_op jit(solution)/shard_map/sum_over_z/ppermute | solution.py:23
  40.6 1.9 %collective-permute-done.11.refs_2_ = f32[16,2048]{1,0:T(8,128)S(1)} collective-permute-done((f32[16,2048]{1,0:T(8,128)S(1)}, f32[16,2048]{1,0:T(8,128)S(1)}, u32[]{:S(2)}, u32[]{:S(2)}) %collective-permute-start.11) | collective-permute-done | bytes 131104 | tf_op jit(solution)/shard_map/sum_over_z/ppermute | solution.py:23
  42.5 1.5 %collective-permute-done.10.refs_1_ = f32[16,2048]{1,0:T(8,128)S(1)} collective-permute-done((f32[16,2048]{1,0:T(8,128)S(1)}, f32[16,2048]{1,0:T(8,128)S(1)}, u32[]{:S(2)}, u32[]{:S(2)}) %collective-permute-start.10) | collective-permute-done | bytes 131104 | tf_op jit(solution)/shard_map/sum_over_z/ppermute | solution.py:23
  44.0 2.7 %second_product.1 = (f32[16,2048]{1,0:T(8,128)S(1)}, f32[16,2048]{1,0:T(8,128)S(1)}, f32[16,512]{1,0:T(8,128)S(1)}) custom-call(f32[16,2048]{1,0:T(8,128)S(1)} %get-tuple-element.60.refs_0_, f32[16,2048]{1,0:T(8,128)S(1)} %collective-permute-done.10.refs_1_, f32[16,2048]{1,0:T(8,128)S(1)} %collective-permute-done.11.refs_2_, ...), custom_call_target="tpu_custom_call" | custom-call | flops 268435456 | bytes 1024 | tf_op jit(solution)/shard_map/second_product/pallas_call | solution.py:181
  46.7 1.4 %collective-permute-done.13 = f32[16,2048]{1,0:T(8,128)S(1)} collective-permute-done((f32[16,2048]{1,0:T(8,128)S(1)}, f32[16,2048]{1,0:T(8,128)S(1)}, u32[]{:S(2)}, u32[]{:S(2)}) %collective-permute-start.13) | collective-permute-done | bytes 131104 | tf_op jit(solution)/shard_map/sum_over_yc/ppermute | solution.py:23
  48.1 2.3 %collective-permute-start.16 = (f32[16,512]{1,0:T(8,128)S(1)}, f32[16,512]{1,0:T(8,128)S(1)}, u32[]{:S(2)}, u32[]{:S(2)}) collective-permute-start(f32[16,512]{1,0:T(8,128)S(1)} %get-tuple-element.76), channel_id=1, source_target_pairs={{0,64},{32,96},{64,0},{96,32},{1,65},{33,97},{65,1},{97,33},{2,66}... | collective-permute-start | bytes 98312 | tf_op jit(solution)/shard_map/sum_over_yc/ppermute | solution.py:23
  50.5 3.2 %collective-permute-start.14 = (f32[16,512]{1,0:T(8,128)S(1)}, f32[16,512]{1,0:T(8,128)S(1)}, u32[]{:S(2)}, u32[]{:S(2)}) collective-permute-start(f32[16,512]{1,0:T(8,128)S(1)} %get-tuple-element.78), channel_id=1, source_target_pairs={{0,96},{32,0},{64,32},{96,64},{1,97},{33,1},{65,33},{97,65},{2,98}... | collective-permute-start | bytes 98312 | tf_op jit(solution)/shard_map/sum_over_yc/ppermute | solution.py:23
  53.7 1.9 %collective-permute-done.15.refs_2_ = f32[16,512]{1,0:T(8,128)S(1)} collective-permute-done((f32[16,512]{1,0:T(8,128)S(1)}, f32[16,512]{1,0:T(8,128)S(1)}, u32[]{:S(2)}, u32[]{:S(2)}) %collective-permute-start.15) | collective-permute-done | bytes 32800 | tf_op jit(solution)/shard_map/sum_over_yc/ppermute | solution.py:23
  55.7 12.7 %all_to_all.5.sums_ref = f32[32,8,128]{2,1,0:T(8,128)S(1)} all-to-all(f32[32,8,128]{2,1,0:T(8,128)S(1)} %broadcast_in_dim.3), channel_id=1, replica_groups=mesh['y'=4,'z'=4,'c'=2,'x'=4] {'y','z','c'}, dimensions={0} | all-to-all | bytes 262144 | tf_op jit(solution)/shard_map/final_sums/all_to_all | solution.py:313
  68.4 0.9 %finish.1 = (f32[16,512]{1,0:T(8,128)}, f32[16,512]{1,0:T(8,128)}) custom-call(f32[16,512]{1,0:T(8,128)S(1)} %bitcast.10, f32[16,512]{1,0:T(8,128)S(1)} %get-tuple-element.69.rho_ref, f32[16,512]{1,0:T(8,128)S(1)} %get-tuple-element.72.image_ref, f32[32,8,128]{2,1,0:T(8,128)S(1)} %all_to_all.5.sums_ref), custom_call_target="tpu_custom_call" | custom-call | tf_op jit(solution)/shard_map/finish/pallas_call | solution.py:241
  (29 shorter events, 1.1 us)
Async XLA Ops:
  0.6 1.1 %copy-start = (bf16[1024,256]{1,0:T(8,128)(2,1)S(1)}, bf16[1024,256]{1,0:T(8,128)(2,1)}, u32[]{:S(2)}) copy-start(bf16[1024,256]{1,0:T(8,128)(2,1)} %param.3) | copy-start | bytes 1572868
  1.8 0.8 %copy-start.1 = (f32[512,16]{0,1:T(8,128)S(1)}, f32[512,16]{0,1:T(8,128)}, u32[]{:S(2)}) copy-start(f32[512,16]{0,1:T(8,128)} %param.5) | copy-start | bytes 98308
  2.8 7.3 %collective-permute-start.4 = (bf16[576,256]{1,0:T(8,128)(2,1)S(1)}, bf16[576,256]{1,0:T(8,128)(2,1)S(1)}, u32[]{:S(2)}, u32[]{:S(2)}) collective-permute-start(bf16[576,256]{1,0:T(8,128)(2,1)S(1)} %pack.1.refs_1_), channel_id=1, source_target_pairs={{0,4},{4,0},{1,5},{5,1},{2,6},{6,2},{3,7},{7,3},{8,12},{12,8},{9,1... | collective-permute-start | bytes 884744 | tf_op jit(solution)/shard_map/fetch_points/ppermute | solution.py:23
  2.9 14.7 %collective-permute-start.3 = (bf16[576,256]{1,0:T(8,128)(2,1)S(1)}, bf16[576,256]{1,0:T(8,128)(2,1)S(1)}, u32[]{:S(2)}, u32[]{:S(2)}) collective-permute-start(bf16[576,256]{1,0:T(8,128)(2,1)S(1)} %pack.1.refs_1_), channel_id=1, source_target_pairs={{0,96},{32,0},{64,32},{96,64},{1,97},{33,1},{65,33},{97,65},{2,98}... | collective-permute-start | bytes 884744 | tf_op jit(solution)/shard_map/fetch_points/ppermute | solution.py:23
  6.1 11.5 %collective-permute-start.2 = (bf16[576,256]{1,0:T(8,128)(2,1)S(1)}, bf16[576,256]{1,0:T(8,128)(2,1)S(1)}, u32[]{:S(2)}, u32[]{:S(2)}) collective-permute-start(bf16[576,256]{1,0:T(8,128)(2,1)S(1)} %pack.1.refs_1_), channel_id=1, source_target_pairs={{0,32},{32,64},{64,96},{96,0},{1,33},{33,65},{65,97},{97,1},{2,34}... | collective-permute-start | bytes 884744 | tf_op jit(solution)/shard_map/fetch_points/ppermute | solution.py:23
  6.1 10.7 %collective-permute-start = (bf16[512,256]{1,0:T(8,128)(2,1)S(1)}, bf16[512,256]{1,0:T(8,128)(2,1)S(1)}, u32[]{:S(2)}, u32[]{:S(2)}) collective-permute-start(bf16[512,256]{1,0:T(8,128)(2,1)S(1)} %constant_dynamic-slice_fusion.points_ref.refs_0_), channel_id=1, source_target_pairs={{0,8},{8,16},{16,24},{24,0},{1,9},{9,17},{17,25},{25,1},{2,10},{10... | collective-permute-start | bytes 786440 | tf_op jit(solution)/shard_map/fetch_points/ppermute | solution.py:23
  8.0 9.6 %collective-permute-start.1 = (bf16[512,256]{1,0:T(8,128)(2,1)S(1)}, bf16[512,256]{1,0:T(8,128)(2,1)S(1)}, u32[]{:S(2)}, u32[]{:S(2)}) collective-permute-start(bf16[512,256]{1,0:T(8,128)(2,1)S(1)} %constant_dynamic-slice_fusion.points_ref.refs_0_), channel_id=1, source_target_pairs={{0,24},{8,0},{16,8},{24,16},{1,25},{9,1},{17,9},{25,17},{2,26},{10... | collective-permute-start | bytes 786440 | tf_op jit(solution)/shard_map/fetch_points/ppermute | solution.py:23
  10.1 0.8 %copy-start.2 = (f32[512,16]{0,1:T(8,128)S(1)}, f32[512,16]{0,1:T(8,128)}, u32[]{:S(2)}) copy-start(f32[512,16]{0,1:T(8,128)} %param.5) | copy-start | bytes 98308
  17.6 4.2 %collective-permute-start.6 = (bf16[576,256]{1,0:T(8,128)(2,1)S(1)}, bf16[576,256]{1,0:T(8,128)(2,1)S(1)}, u32[]{:S(2)}, u32[]{:S(2)}) collective-permute-start(bf16[576,256]{1,0:T(8,128)(2,1)S(1)} %collective-permute-done.2.refs_3_), channel_id=1, source_target_pairs={{0,4},{4,0},{1,5},{5,1},{2,6},{6,2},{3,7},{7,3},{8,12},{12,8},{9,1... | collective-permute-start | bytes 884744 | tf_op jit(solution)/shard_map/fetch_points/ppermute | solution.py:23
  17.7 4.1 %collective-permute-start.7 = (bf16[576,256]{1,0:T(8,128)(2,1)S(1)}, bf16[576,256]{1,0:T(8,128)(2,1)S(1)}, u32[]{:S(2)}, u32[]{:S(2)}) collective-permute-start(bf16[576,256]{1,0:T(8,128)(2,1)S(1)} %collective-permute-done.3.refs_4_), channel_id=1, source_target_pairs={{0,4},{4,0},{1,5},{5,1},{2,6},{6,2},{3,7},{7,3},{8,12},{12,8},{9,1... | collective-permute-start | bytes 884744 | tf_op jit(solution)/shard_map/fetch_points/ppermute | solution.py:23
  18.2 10.1 %collective-permute-start.8 = (bf16[576,256]{1,0:T(8,128)(2,1)S(1)}, bf16[576,256]{1,0:T(8,128)(2,1)S(1)}, u32[]{:S(2)}, u32[]{:S(2)}) collective-permute-start(bf16[576,256]{1,0:T(8,128)(2,1)S(1)} %broadcast_select_fusion), channel_id=1, source_target_pairs={{0,32},{4,100},{32,64},{36,4},{64,96},{68,36},{96,0},{100,68},{1,3... | collective-permute-start | bytes 884744 | tf_op jit(solution)/shard_map/fetch_points/ppermute | solution.py:31
  18.7 7.7 %collective-permute-start.5 = (bf16[512,256]{1,0:T(8,128)(2,1)S(1)}, bf16[512,256]{1,0:T(8,128)(2,1)S(1)}, u32[]{:S(2)}, u32[]{:S(2)}) collective-permute-start(bf16[512,256]{1,0:T(8,128)(2,1)S(1)} %broadcast_select_fusion.1), channel_id=1, source_target_pairs={{0,8},{4,28},{8,16},{12,4},{16,24},{20,12},{24,0},{28,20},{1,9},{5... | collective-permute-start | bytes 786440 | tf_op jit(solution)/shard_map/fetch_points/ppermute | solution.py:31
  28.4 2.9 %collective-permute-start.9 = (bf16[576,256]{1,0:T(8,128)(2,1)S(1)}, bf16[576,256]{1,0:T(8,128)(2,1)S(1)}, u32[]{:S(2)}, u32[]{:S(2)}) collective-permute-start(bf16[576,256]{1,0:T(8,128)(2,1)S(1)} %collective-permute-done.8.refs_4_), channel_id=1, source_target_pairs={{0,4},{4,0},{1,5},{5,1},{2,6},{6,2},{3,7},{7,3},{8,12},{12,8},{9,1... | collective-permute-start | bytes 884744 | tf_op jit(solution)/shard_map/build_tiles/ppermute | solution.py:23
  32.7 8.0 %collective-permute-start.12 = (f32[16,2048]{1,0:T(8,128)S(1)}, f32[16,2048]{1,0:T(8,128)S(1)}, u32[]{:S(2)}, u32[]{:S(2)}) collective-permute-start(f32[16,2048]{1,0:T(8,128)S(1)} %get-tuple-element.60.refs_0_), channel_id=1, source_target_pairs={{0,24},{8,0},{16,8},{24,16},{1,25},{9,1},{17,9},{25,17},{2,26},{10... | collective-permute-start | bytes 393224 | tf_op jit(solution)/shard_map/sum_over_z/ppermute | solution.py:23
  34.7 7.9 %collective-permute-start.11 = (f32[16,2048]{1,0:T(8,128)S(1)}, f32[16,2048]{1,0:T(8,128)S(1)}, u32[]{:S(2)}, u32[]{:S(2)}) collective-permute-start(f32[16,2048]{1,0:T(8,128)S(1)} %get-tuple-element.60.refs_0_), channel_id=1, source_target_pairs={{0,16},{8,24},{16,0},{24,8},{1,17},{9,25},{17,1},{25,9},{2,18},{10... | collective-permute-start | bytes 393224 | tf_op jit(solution)/shard_map/sum_over_z/ppermute | solution.py:23
  34.8 9.2 %collective-permute-start.10 = (f32[16,2048]{1,0:T(8,128)S(1)}, f32[16,2048]{1,0:T(8,128)S(1)}, u32[]{:S(2)}, u32[]{:S(2)}) collective-permute-start(f32[16,2048]{1,0:T(8,128)S(1)} %get-tuple-element.60.refs_0_), channel_id=1, source_target_pairs={{0,8},{8,16},{16,24},{24,0},{1,9},{9,17},{17,25},{25,1},{2,10},{10... | collective-permute-start | bytes 393224 | tf_op jit(solution)/shard_map/sum_over_z/ppermute | solution.py:23
  44.0 11.6 %copy-start.3 = (f32[512,16]{0,1:T(8,128)S(1)}, f32[512,16]{0,1:T(8,128)}, u32[]{:S(2)}) copy-start(f32[512,16]{0,1:T(8,128)} %param.5) | copy-start | bytes 98308
  46.7 1.4 %collective-permute-start.13 = (f32[16,2048]{1,0:T(8,128)S(1)}, f32[16,2048]{1,0:T(8,128)S(1)}, u32[]{:S(2)}, u32[]{:S(2)}) collective-permute-start(f32[16,2048]{1,0:T(8,128)S(1)} %get-tuple-element.71), channel_id=1, source_target_pairs={{0,4},{4,0},{1,5},{5,1},{2,6},{6,2},{3,7},{7,3},{8,12},{12,8},{9,1... | collective-permute-start | bytes 393224 | tf_op jit(solution)/shard_map/sum_over_yc/ppermute | solution.py:23
  48.1 5.5 %collective-permute-start.16 = (f32[16,512]{1,0:T(8,128)S(1)}, f32[16,512]{1,0:T(8,128)S(1)}, u32[]{:S(2)}, u32[]{:S(2)}) collective-permute-start(f32[16,512]{1,0:T(8,128)S(1)} %get-tuple-element.76), channel_id=1, source_target_pairs={{0,64},{32,96},{64,0},{96,32},{1,65},{33,97},{65,1},{97,33},{2,66}... | collective-permute-start | bytes 98312 | tf_op jit(solution)/shard_map/sum_over_yc/ppermute | solution.py:23
  50.4 5.1 %collective-permute-start.15 = (f32[16,512]{1,0:T(8,128)S(1)}, f32[16,512]{1,0:T(8,128)S(1)}, u32[]{:S(2)}, u32[]{:S(2)}) collective-permute-start(f32[16,512]{1,0:T(8,128)S(1)} %get-tuple-element.77), channel_id=1, source_target_pairs={{0,32},{32,64},{64,96},{96,0},{1,33},{33,65},{65,97},{97,1},{2,34}... | collective-permute-start | bytes 98312 | tf_op jit(solution)/shard_map/sum_over_yc/ppermute | solution.py:23
  50.5 5.1 %collective-permute-start.14 = (f32[16,512]{1,0:T(8,128)S(1)}, f32[16,512]{1,0:T(8,128)S(1)}, u32[]{:S(2)}, u32[]{:S(2)}) collective-permute-start(f32[16,512]{1,0:T(8,128)S(1)} %get-tuple-element.78), channel_id=1, source_target_pairs={{0,96},{32,0},{64,32},{96,64},{1,97},{33,1},{65,33},{97,65},{2,98}... | collective-permute-start | bytes 98312 | tf_op jit(solution)/shard_map/sum_over_yc/ppermute | solution.py:23

commit v9 on v8

--- a/solution.py
+++ b/solution.py
@@ -11,24 +11,26 @@
 NY, NZ, NC, NX = 4, 4, 2, 4
 LANES = 128
 CHUNK = 256
-ROWS = (0, 1, 3, 2)
-COLS = ((0, 0), (1, 0), (0, 1), (0, 3), (1, 1), (1, 3), (0, 2), (1, 2))
+HERE = (0, 0)
+ROWS = (HERE, (3, 0), (0, 3), (3, 3))
+SQUARE = (HERE, (1, 0), (0, 1), (1, 1))
+COLS = ((0, 0), (1, 0), (0, 1), (0, 2), (1, 1), (1, 2), (0, 3), (1, 3))
 
 noise_level = 1.0
 kernel_rate = 0.5
 STEP = 1.0 / (1.0 + noise_level)
 
 
-def shift(value, axis, size, step):
-    return lax.ppermute(value, axis, [(i, (i + step) % size) for i in range(size)])
-
-
-def hand_on(behind, ahead, axis, size):
-    value = jnp.where(lax.axis_index("c") == 0, behind, ahead)
+def swap(value, offset):
     pairs = []
-    for i in range(size):
-        pairs += [(i * NC, (i + 1) % size * NC), (i * NC + 1, (i - 1) % size * NC + 1)]
-    return lax.ppermute(value, (axis, "c"), pairs)
+    for y in range(NY):
+        for z in range(NZ):
+            pairs.append((y * NZ + z, (y ^ offset[0]) * NZ + (z ^ offset[1])))
+    return lax.ppermute(value, ("y", "z"), pairs)
+
+
+def swap_core(value):
+    return lax.ppermute(value, "c", [(0, 1), (1, 0)])
 
 
 def split(value):
@@ -147,15 +149,15 @@
 
 
 def second_kernel(own, places, *refs):
-    parts, refs = refs[:NZ], refs[NZ:]
+    parts, refs = refs[: len(ROWS)], refs[len(ROWS) :]
     tiles, (mine_ref, other_ref, rho_ref) = refs[: len(places)], refs[len(places) :]
     probes = rho_ref.shape[0]
     pieces = []
     for p in ROWS:
         piece = 0.0
-        for s in range(NZ):
-            at = ROWS.index((p - s) % NZ) * own
-            piece = piece + parts[s][:, at : at + own]
+        for s, part in zip(ROWS, parts):
+            at = ROWS.index((p[0] ^ s[0], p[1] ^ s[1])) * own
+            piece = piece + part[:, at : at + own]
         pieces.append(-STEP * piece)
     rho_ref[...] = pieces[0]
     rho = jnp.concatenate(pieces, axis=1)
@@ -180,7 +182,7 @@
     places = [(top, left) for _, top, left in tiles]
     return pl.pallas_call(
         functools.partial(second_kernel, own, places),
-        in_specs=[pl.BlockSpec(memory_space=pltpu.VMEM)] * (NZ + len(tiles)),
+        in_specs=[pl.BlockSpec(memory_space=pltpu.VMEM)] * (len(ROWS) + len(tiles)),
         out_shape=[
             jax.ShapeDtypeStruct((probes, cols // NC), jnp.float32),
             jax.ShapeDtypeStruct((probes, cols // NC), jnp.float32),
@@ -193,7 +195,7 @@
 
 
 def sums_kernel(side_ref, rho_ref, *refs):
-    shares, (image_ref, sums_ref) = refs[:NY], refs[NY:]
+    shares, (image_ref, sums_ref) = refs[: len(SQUARE)], refs[len(SQUARE) :]
     side, rho = side_ref[...], rho_ref[...]
     image = noise_level * rho
     for share in shares:
@@ -252,41 +254,30 @@
     points = lax.dynamic_slice_in_dim(states, offsets[0], own, 0)
     with jax.named_scope("fetch_points"):
         message = pack(points, side)
-        row, col = {0: points}, {(0, 0): message}
-        for k in (1, 3):
-            col[0, k] = shift(message, "y", NY, k)
-            row[k] = shift(points, "z", NZ, k)
-        col[1, 0] = shift(message, "c", NC, 1)
-        first = [col[0, 0], col[1, 0]]
+        rows = [points] + [swap(points, offset) for offset in ROWS[1:]]
+        cols = [message] + [swap(message, offset) for offset in SQUARE[1:]]
+        first = [message, swap_core(message)]
         tile_a, image_a, half_a = build([points], first, own, probes, side=side)
-        tile_b, image_b, half_b = build([row[1]], first, own, probes)
-        near = row[1], row[3], col[0, 1], col[0, 3]
-        near, image_a, image_b = lax.optimization_barrier((near, image_a, image_b))
-        row[1], row[3], col[0, 1], col[0, 3] = near
-        row[2] = hand_on(row[1], row[3], "z", NZ)
-        col[0, 2] = hand_on(col[0, 1], col[0, 3], "y", NY)
-        for k in (1, 3):
-            col[1, k] = shift(col[0, k], "c", NC, 1)
+        (rows[1], rows[2], cols[1], cols[2]), image_a = lax.optimization_barrier(
+            ((rows[1], rows[2], cols[1], cols[2]), image_a)
+        )
+        others = [swap_core(cols[1]), swap_core(cols[2])]
 
     with jax.named_scope("build_tiles"):
-        near = [points, row[1], row[3]]
-        tile_c, image_c, half_c = build([row[3]], first, own, probes)
-        half = [half_a, half_b, half_c]
-        tile_d, image = build(near, [col[0, 1], col[0, 3]], own, probes, half, [image_a, image_b, image_c])
-        tile_e, image = build(near, [col[1, 1], col[1, 3]], own, probes, half, [image])
-        at = [col[k] for k in COLS[:6]]
-        row[2], image = lax.optimization_barrier((row[2], image))
-        tile_f, image_far, half_far = build([row[2]], at, own, probes)
-        col[0, 2], image_far = lax.optimization_barrier((col[0, 2], image_far))
-        col[1, 2] = shift(col[0, 2], "c", NC, 1)
-        near.append(row[2])
+        tile_b, image_b, half_b = build(rows[1:3], first, own, probes)
+        half = [half_a, half_b]
+        tile_d, image = build(rows[:3], cols[1:3], own, probes, half, [image_a, image_b])
+        tile_e, image = build(rows[:3], others, own, probes, half, [image])
+        rows[3], image = lax.optimization_barrier((rows[3], image))
+        tile_f, image_far, half_far = build([rows[3]], first + cols[1:3] + others, own, probes)
+        cols[3], image_far = lax.optimization_barrier((cols[3], image_far))
+        last = swap_core(cols[3])
         half.append(half_far)
-        tile_g, image = build(near, [col[0, 2]], own, probes, half, [image, image_far])
-        tile_h, image = build(near, [col[1, 2]], own, probes, half, [image])
+        tile_g, image = build(rows, [cols[3]], own, probes, half, [image, image_far])
+        tile_h, image = build(rows, [last], own, probes, half, [image])
         tiles = [
             (tile_a, 0, 0),
             (tile_b, own, 0),
-            (tile_c, 2 * own, 0),
             (tile_d, 0, 2 * own),
             (tile_e, 0, 4 * own),
             (tile_f, 3 * own, 0),
@@ -294,18 +285,16 @@
             (tile_h, 0, 7 * own),
         ]
 
-    with jax.named_scope("sum_over_z"):
-        parts = [image] + [None] * (NZ - 1)
-        for k in (1, 3, 2):
-            parts[k] = shift(image, "z", NZ, k)
+    with jax.named_scope("sum_over_rows"):
+        parts = [image] + [swap(image, offset) for offset in ROWS[1:]]
 
     mine, other, rho = second_product(tiles, parts, own)
 
-    with jax.named_scope("sum_over_yc"):
-        mine = mine + shift(other, "c", NC, 1)
+    with jax.named_scope("sum_over_columns"):
+        mine = mine + swap_core(other)
         shares = [mine[:, :own]]
-        for m in (1, 3, 2):
-            shares.append(shift(mine[:, m * own : (m + 1) * own], "y", NY, -m))
+        for m, offset in enumerate(SQUARE[1:], 1):
+            shares.append(swap(mine[:, m * own : (m + 1) * own], offset))
 
     with jax.named_scope("final_sums"):
         image, sums = local_sums(side, rho, shares)

time: 70.7 us -> 72.9 us (1.031)
  starting transfers between devices: 18.7 us -> 21.8 us
  blocking collectives: 12.7 us -> 13.5 us
  local copies, waits for them, and re-layouts: 1.95 us -> 1.2 us
    ppermute x17, starting transfers between devices: 18.7 us -> 21.8 us  [the longest x12 21 us: swap(): return lax.ppermute(value, ('y', 'z'), pairs)]
    all_to_all x1, blocking collectives: 12.7 us -> 13.5 us  [on_device(): sums = lax.all_to_all(sums, ('y', 'z', 'c'), 0, 0, tiled=True)]
    unnamed x8 -> x6, local copies, waits for them, and re-layouts: 1.86 us -> 1.11 us
    pallas_call x8 -> x7, Pallas kernels: 11.2 us -> 10.8 us  [build(): pl.pallas_call(functools.partial(tile_kernel, counts, probes), out_shape=...]
  transfers between devices with their start and end apart: 17 -> 17, of which waited for: 7 -> 9; matrix products, arithmetic and copies ran while one was open for 0% -> 0% of each run, Pallas kernels for 14% -> 13%
where the time goes in v9:
time: 72.9 us; the launch traced here: 71.7 us
  starting transfers between devices  21.8 us (30%)
  waiting for transfers between devices  18.7 us (26%)
  Pallas kernels  14.9 us (20%)
  blocking collectives  13.5 us (19%)
  between operations  1.44 us (2%)
  local copies, waits for them, and re-layouts  1.2 us (2%)
    ppermute x12, starting transfers between devices, swap(): return lax.ppermute(value, ('y', 'z'), pairs)  21 us
    ppermute x12, waiting for transfers between devices, swap(): return lax.ppermute(value, ('y', 'z'), pairs)  17.1 us
    all_to_all x1, blocking collectives, on_device(): sums = lax.all_to_all(sums, ('y', 'z', 'c'), 0, 0, tiled=True)  13.5 us
    pallas_call x7, Pallas kernels, build(): pl.pallas_call(functools.partial(tile_kernel, counts, probes), out_shape=...  10.8 us
    pallas_call x1, Pallas kernels, second_product(): pl.pallas_call(functools.partial(second_kernel, own, places), in_specs=[p...  2.74 us
    ppermute x5, waiting for transfers between devices, swap_core(): return lax.ppermute(value, 'c', [(0, 1), (1, 0)])  1.58 us
  transfers between devices with their start and end apart: 17, of which 9 were waited for; matrix products, arithmetic and copies ran while one was open for 0% of the time, Pallas kernels for 13%

profile of v9, /device:TPU:0, one launch (start us, length us, event | category | flops | bytes accessed | tf_op | source)
XLA Modules:
  0.0 71.7 jit_solution(4641333776237642192)
XLA Ops:
  1.4 0.3 copy-done
  1.8 0.7 %copy-done.1 = f32[512,16]{0,1:T(8,128)S(1)} copy-done((f32[512,16]{0,1:T(8,128)S(1)}, f32[512,16]{0,1:T(8,128)}, u32[]{:S(2)}) %copy-start.1) | copy-done | bytes 32792
  2.9 2.1 %collective-permute-start.3 = (bf16[576,256]{1,0:T(8,128)(2,1)S(1)}, bf16[576,256]{1,0:T(8,128)(2,1)S(1)}, u32[]{:S(2)}, u32[]{:S(2)}) collective-permute-start(bf16[576,256]{1,0:T(8,128)(2,1)S(1)} %pack.1.refs_1_.refs_2_), channel_id=1, source_target_pairs={{0,8},{8,0},{16,24},{24,16},{32,40},{40,32},{48,56},{56,48},{64,72... | collective-permute-start | bytes 884744 | tf_op jit(solution)/shard_map/fetch_points/ppermute | solution.py:29
  5.0 1.6 %collective-permute-start.2 = (bf16[576,256]{1,0:T(8,128)(2,1)S(1)}, bf16[576,256]{1,0:T(8,128)(2,1)S(1)}, u32[]{:S(2)}, u32[]{:S(2)}) collective-permute-start(bf16[576,256]{1,0:T(8,128)(2,1)S(1)} %pack.1.refs_1_.refs_2_), channel_id=1, source_target_pairs={{0,32},{8,40},{16,48},{24,56},{32,0},{40,8},{48,16},{56,24},{64,96... | collective-permute-start | bytes 884744 | tf_op jit(solution)/shard_map/fetch_points/ppermute | solution.py:29
  6.6 2.5 %collective-permute-start.1 = (bf16[512,256]{1,0:T(8,128)(2,1)S(1)}, bf16[512,256]{1,0:T(8,128)(2,1)S(1)}, u32[]{:S(2)}, u32[]{:S(2)}) collective-permute-start(bf16[512,256]{1,0:T(8,128)(2,1)S(1)} %constant_dynamic-slice_fusion.points_ref.refs_0_), channel_id=1, source_target_pairs={{0,24},{8,16},{16,8},{24,0},{32,56},{40,48},{48,40},{56,32},{64,88... | collective-permute-start | bytes 786440 | tf_op jit(solution)/shard_map/fetch_points/ppermute | solution.py:29
  9.1 2.2 %collective-permute-start = (bf16[512,256]{1,0:T(8,128)(2,1)S(1)}, bf16[512,256]{1,0:T(8,128)(2,1)S(1)}, u32[]{:S(2)}, u32[]{:S(2)}) collective-permute-start(bf16[512,256]{1,0:T(8,128)(2,1)S(1)} %constant_dynamic-slice_fusion.points_ref.refs_0_), channel_id=1, source_target_pairs={{0,96},{8,104},{16,112},{24,120},{32,64},{40,72},{48,80},{56,88},{... | collective-permute-start | bytes 786440 | tf_op jit(solution)/shard_map/fetch_points/ppermute | solution.py:29
  11.3 0.8 %build_tile.7 = (bf16[512,1024]{1,0:T(8,128)(2,1)S(1)}, f32[16,512]{1,0:T(8,128)S(1)}, f32[512,1]{1,0:T(8,128)S(1)}) custom-call(bf16[512,256]{1,0:T(8,128)(2,1)S(1)} %constant_dynamic-slice_fusion.points_ref.refs_0_, bf16[576,256]{1,0:T(8,128)(2,1)S(1)} %pack.1.refs_1_.refs_2_, bf16[576,256]{1,0:T(8,128)(2,1)S(1)} %collective-permute-done.4.refs_2_.refs_3_, ...), custom_call_target="tpu_custom_call" | custom-call | flops 16777216 | bytes 1024 | tf_op jit(solution)/shard_map/fetch_points/build_tile/pallas_call | solution.py:140
  12.1 3.7 %collective-permute-done.1.refs_1_.refs_2_ = bf16[512,256]{1,0:T(8,128)(2,1)S(1)} collective-permute-done((bf16[512,256]{1,0:T(8,128)(2,1)S(1)}, bf16[512,256]{1,0:T(8,128)(2,1)S(1)}, u32[]{:S(2)}, u32[]{:S(2)}) %collective-permute-start.1) | collective-permute-done | bytes 262176 | tf_op jit(solution)/shard_map/fetch_points/ppermute | solution.py:29
  15.9 2.2 %collective-permute-done.refs_0_.refs_1_ = bf16[512,256]{1,0:T(8,128)(2,1)S(1)} collective-permute-done((bf16[512,256]{1,0:T(8,128)(2,1)S(1)}, bf16[512,256]{1,0:T(8,128)(2,1)S(1)}, u32[]{:S(2)}, u32[]{:S(2)}) %collective-permute-start) | collective-permute-done | bytes 262176 | tf_op jit(solution)/shard_map/fetch_points/ppermute | solution.py:29
  18.1 0.5 collective-permute-start.7
  18.6 0.4 collective-permute-start.8
  19.0 2.8 %collective-permute-start.5 = (bf16[512,256]{1,0:T(8,128)(2,1)S(1)}, bf16[512,256]{1,0:T(8,128)(2,1)S(1)}, u32[]{:S(2)}, u32[]{:S(2)}) collective-permute-start(bf16[512,256]{1,0:T(8,128)(2,1)S(1)} %constant_dynamic-slice_fusion.points_ref.refs_0_), channel_id=1, source_target_pairs={{0,120},{8,112},{16,104},{24,96},{32,88},{40,80},{48,72},{56,64},{... | collective-permute-start | bytes 786440 | tf_op jit(solution)/shard_map/fetch_points/ppermute | solution.py:29
  21.7 1.4 %build_tile.8 = (bf16[1024,1024]{1,0:T(8,128)(2,1)S(1)}, f32[16,1024]{1,0:T(8,128)S(1)}, f32[1024,1]{1,0:T(8,128)S(1)}) custom-call(bf16[512,256]{1,0:T(8,128)(2,1)S(1)} %collective-permute-done.refs_0_.refs_1_, bf16[512,256]{1,0:T(8,128)(2,1)S(1)} %collective-permute-done.1.refs_1_.refs_2_, bf16[576,256]{1,0:T(8,128)(2,1)S(1)} %pack.1.refs_1_.refs_2_, ...), custom_call_target="tpu_custom_call" | custom-call | flops 33554432 | bytes 1024 | tf_op jit(solution)/shard_map/build_tiles/build_tile/pallas_call | solution.py:140
  23.2 1.9 %build_tile.9 = (bf16[1536,1024]{1,0:T(8,128)(2,1)S(1)}, f32[16,1536]{1,0:T(8,128)S(1)}) custom-call(bf16[512,256]{1,0:T(8,128)(2,1)S(1)} %constant_dynamic-slice_fusion.points_ref.refs_0_, bf16[512,256]{1,0:T(8,128)(2,1)S(1)} %collective-permute-done.refs_0_.refs_1_, bf16[512,256]{1,0:T(8,128)(2,1)S(1)} %collective-permute-done.1.refs_1_.refs_2_, ...), custom_call_target="tpu_custom_call" | custom-call | flops 50331648 | bytes 1024 | tf_op jit(solution)/shard_map/build_tiles/build_tile/pallas_call | solution.py:140
  25.1 1.9 %build_tile.10 = (bf16[1536,1024]{1,0:T(8,128)(2,1)S(1)}, f32[16,1536]{1,0:T(8,128)S(1)}) custom-call(bf16[512,256]{1,0:T(8,128)(2,1)S(1)} %constant_dynamic-slice_fusion.points_ref.refs_0_, bf16[512,256]{1,0:T(8,128)(2,1)S(1)} %collective-permute-done.refs_0_.refs_1_, bf16[512,256]{1,0:T(8,128)(2,1)S(1)} %collective-permute-done.1.refs_1_.refs_2_, ...), custom_call_target="tpu_custom_call" | custom-call | flops 50331648 | bytes 1024 | tf_op jit(solution)/shard_map/build_tiles/build_tile/pallas_call | solution.py:140
  27.0 3.3 %collective-permute-done.5.refs_0_.refs_3_ = bf16[512,256]{1,0:T(8,128)(2,1)S(1)} collective-permute-done((bf16[512,256]{1,0:T(8,128)(2,1)S(1)}, bf16[512,256]{1,0:T(8,128)(2,1)S(1)}, u32[]{:S(2)}, u32[]{:S(2)}) %collective-permute-start.5) | collective-permute-done | bytes 262176 | tf_op jit(solution)/shard_map/fetch_points/ppermute | solution.py:29
  30.3 2.0 %build_tile.11 = (bf16[512,3072]{1,0:T(8,128)(2,1)S(1)}, f32[16,512]{1,0:T(8,128)S(1)}, f32[512,1]{1,0:T(8,128)S(1)}) custom-call(bf16[512,256]{1,0:T(8,128)(2,1)S(1)} %collective-permute-done.5.refs_0_.refs_3_, bf16[576,256]{1,0:T(8,128)(2,1)S(1)} %pack.1.refs_1_.refs_2_, bf16[576,256]{1,0:T(8,128)(2,1)S(1)} %collective-permute-done.4.refs_2_.refs_3_, ...), custom_call_target="tpu_custom_call" | custom-call | flops 50331648 | bytes 1024 | tf_op jit(solution)/shard_map/build_tiles/build_tile/pallas_call | solution.py:140
  32.6 1.3 %build_tile.12 = (bf16[2048,512]{1,0:T(8,128)(2,1)S(1)}, f32[16,2048]{1,0:T(8,128)S(1)}) custom-call(bf16[512,256]{1,0:T(8,128)(2,1)S(1)} %constant_dynamic-slice_fusion.points_ref.refs_0_, bf16[512,256]{1,0:T(8,128)(2,1)S(1)} %collective-permute-done.refs_0_.refs_1_, bf16[512,256]{1,0:T(8,128)(2,1)S(1)} %collective-permute-done.1.refs_1_.refs_2_, ...), custom_call_target="tpu_custom_call" | custom-call | flops 33554432 | bytes 1024 | tf_op jit(solution)/shard_map/build_tiles/build_tile/pallas_call | solution.py:140
  34.1 1.3 %build_tile.13 = (bf16[2048,512]{1,0:T(8,128)(2,1)S(1)}, f32[16,2048]{1,0:T(8,128)S(1)}) custom-call(bf16[512,256]{1,0:T(8,128)(2,1)S(1)} %constant_dynamic-slice_fusion.points_ref.refs_0_, bf16[512,256]{1,0:T(8,128)(2,1)S(1)} %collective-permute-done.refs_0_.refs_1_, bf16[512,256]{1,0:T(8,128)(2,1)S(1)} %collective-permute-done.1.refs_1_.refs_2_, ...), custom_call_target="tpu_custom_call" | custom-call | flops 33554432 | bytes 1024 | tf_op jit(solution)/shard_map/build_tiles/build_tile/pallas_call | solution.py:140
  35.5 2.8 %collective-permute-start.12 = (f32[16,2048]{1,0:T(8,128)S(1)}, f32[16,2048]{1,0:T(8,128)S(1)}, u32[]{:S(2)}, u32[]{:S(2)}) collective-permute-start(f32[16,2048]{1,0:T(8,128)S(1)} %get-tuple-element.53.refs_0_), channel_id=1, source_target_pairs={{0,120},{8,112},{16,104},{24,96},{32,88},{40,80},{48,72},{56,64},{... | collective-permute-start | bytes 393224 | tf_op jit(solution)/shard_map/sum_over_rows/ppermute | solution.py:29
  38.3 2.3 %collective-permute-start.11 = (f32[16,2048]{1,0:T(8,128)S(1)}, f32[16,2048]{1,0:T(8,128)S(1)}, u32[]{:S(2)}, u32[]{:S(2)}) collective-permute-start(f32[16,2048]{1,0:T(8,128)S(1)} %get-tuple-element.53.refs_0_), channel_id=1, source_target_pairs={{0,24},{8,16},{16,8},{24,0},{32,56},{40,48},{48,40},{56,32},{64,88... | collective-permute-start | bytes 393224 | tf_op jit(solution)/shard_map/sum_over_rows/ppermute | solution.py:29
  40.6 0.9 %collective-permute-start.10 = (f32[16,2048]{1,0:T(8,128)S(1)}, f32[16,2048]{1,0:T(8,128)S(1)}, u32[]{:S(2)}, u32[]{:S(2)}) collective-permute-start(f32[16,2048]{1,0:T(8,128)S(1)} %get-tuple-element.53.refs_0_), channel_id=1, source_target_pairs={{0,96},{8,104},{16,112},{24,120},{32,64},{40,72},{48,80},{56,88},{... | collective-permute-start | bytes 393224 | tf_op jit(solution)/shard_map/sum_over_rows/ppermute | solution.py:29
  41.4 3.2 %collective-permute-done.12.refs_3_ = f32[16,2048]{1,0:T(8,128)S(1)} collective-permute-done((f32[16,2048]{1,0:T(8,128)S(1)}, f32[16,2048]{1,0:T(8,128)S(1)}, u32[]{:S(2)}, u32[]{:S(2)}) %collective-permute-start.12) | collective-permute-done | bytes 131104 | tf_op jit(solution)/shard_map/sum_over_rows/ppermute | solution.py:29
  44.7 2.7 %collective-permute-done.11.refs_2_ = f32[16,2048]{1,0:T(8,128)S(1)} collective-permute-done((f32[16,2048]{1,0:T(8,128)S(1)}, f32[16,2048]{1,0:T(8,128)S(1)}, u32[]{:S(2)}, u32[]{:S(2)}) %collective-permute-start.11) | collective-permute-done | bytes 131104 | tf_op jit(solution)/shard_map/sum_over_rows/ppermute | solution.py:29
  47.4 2.7 %second_product.1 = (f32[16,2048]{1,0:T(8,128)S(1)}, f32[16,2048]{1,0:T(8,128)S(1)}, f32[16,512]{1,0:T(8,128)S(1)}) custom-call(f32[16,2048]{1,0:T(8,128)S(1)} %get-tuple-element.53.refs_0_, f32[16,2048]{1,0:T(8,128)S(1)} %collective-permute-done.10.refs_1_, f32[16,2048]{1,0:T(8,128)S(1)} %collective-permute-done.11.refs_2_, ...), custom_call_target="tpu_custom_call" | custom-call | flops 268435456 | bytes 1024 | tf_op jit(solution)/shard_map/second_product/pallas_call | solution.py:183
  50.2 1.3 %collective-permute-done.13 = f32[16,2048]{1,0:T(8,128)S(1)} collective-permute-done((f32[16,2048]{1,0:T(8,128)S(1)}, f32[16,2048]{1,0:T(8,128)S(1)}, u32[]{:S(2)}, u32[]{:S(2)}) %collective-permute-start.13) | collective-permute-done | bytes 131104 | tf_op jit(solution)/shard_map/sum_over_columns/ppermute | solution.py:33
  51.6 1.1 %collective-permute-start.15 = (f32[16,512]{1,0:T(8,128)S(1)}, f32[16,512]{1,0:T(8,128)S(1)}, u32[]{:S(2)}, u32[]{:S(2)}) collective-permute-start(f32[16,512]{1,0:T(8,128)S(1)} %get-tuple-element.69), channel_id=1, source_target_pairs={{0,8},{8,0},{16,24},{24,16},{32,40},{40,32},{48,56},{56,48},{64,72... | collective-permute-start | bytes 98312 | tf_op jit(solution)/shard_map/sum_over_columns/ppermute | solution.py:29
  52.8 2.3 %collective-permute-start.14 = (f32[16,512]{1,0:T(8,128)S(1)}, f32[16,512]{1,0:T(8,128)S(1)}, u32[]{:S(2)}, u32[]{:S(2)}) collective-permute-start(f32[16,512]{1,0:T(8,128)S(1)} %get-tuple-element.70), channel_id=1, source_target_pairs={{0,32},{8,40},{16,48},{24,56},{32,0},{40,8},{48,16},{56,24},{64,96... | collective-permute-start | bytes 98312 | tf_op jit(solution)/shard_map/sum_over_columns/ppermute | solution.py:29
  55.1 1.3 %collective-permute-done.16.refs_3_ = f32[16,512]{1,0:T(8,128)S(1)} collective-permute-done((f32[16,512]{1,0:T(8,128)S(1)}, f32[16,512]{1,0:T(8,128)S(1)}, u32[]{:S(2)}, u32[]{:S(2)}) %collective-permute-start.16) | collective-permute-done | bytes 32800 | tf_op jit(solution)/shard_map/sum_over_columns/ppermute | solution.py:29
  56.4 0.6 collective-permute-done.14.refs_1_
  57.2 13.5 %all_to_all.5.sums_ref = f32[32,8,128]{2,1,0:T(8,128)S(1)} all-to-all(f32[32,8,128]{2,1,0:T(8,128)S(1)} %broadcast_in_dim.3), channel_id=1, replica_groups=mesh['y'=4,'z'=4,'c'=2,'x'=4] {'y','z','c'}, dimensions={0} | all-to-all | bytes 262144 | tf_op jit(solution)/shard_map/final_sums/all_to_all | solution.py:302
  70.7 0.9 %finish.1 = (f32[16,512]{1,0:T(8,128)}, f32[16,512]{1,0:T(8,128)}) custom-call(f32[16,512]{1,0:T(8,128)S(1)} %bitcast.10, f32[16,512]{1,0:T(8,128)S(1)} %get-tuple-element.61.rho_ref, f32[16,512]{1,0:T(8,128)S(1)} %get-tuple-element.64.image_ref, f32[32,8,128]{2,1,0:T(8,128)S(1)} %all_to_all.5.sums_ref), custom_call_target="tpu_custom_call" | custom-call | tf_op jit(solution)/shard_map/finish/pallas_call | solution.py:243
  (24 shorter events, 1.3 us)
Async XLA Ops:
  0.6 1.1 %copy-start = (bf16[1024,256]{1,0:T(8,128)(2,1)S(1)}, bf16[1024,256]{1,0:T(8,128)(2,1)}, u32[]{:S(2)}) copy-start(bf16[1024,256]{1,0:T(8,128)(2,1)} %param.3) | copy-start | bytes 1572868
  1.8 0.8 %copy-start.1 = (f32[512,16]{0,1:T(8,128)S(1)}, f32[512,16]{0,1:T(8,128)}, u32[]{:S(2)}) copy-start(f32[512,16]{0,1:T(8,128)} %param.5) | copy-start | bytes 98308
  2.8 8.5 %collective-permute-start.4 = (bf16[576,256]{1,0:T(8,128)(2,1)S(1)}, bf16[576,256]{1,0:T(8,128)(2,1)S(1)}, u32[]{:S(2)}, u32[]{:S(2)}) collective-permute-start(bf16[576,256]{1,0:T(8,128)(2,1)S(1)} %pack.1.refs_1_.refs_2_), channel_id=1, source_target_pairs={{0,4},{4,0},{1,5},{5,1},{2,6},{6,2},{3,7},{7,3},{8,12},{12,8},{9,1... | collective-permute-start | bytes 884744 | tf_op jit(solution)/shard_map/fetch_points/ppermute | solution.py:33
  2.9 15.2 %collective-permute-start.3 = (bf16[576,256]{1,0:T(8,128)(2,1)S(1)}, bf16[576,256]{1,0:T(8,128)(2,1)S(1)}, u32[]{:S(2)}, u32[]{:S(2)}) collective-permute-start(bf16[576,256]{1,0:T(8,128)(2,1)S(1)} %pack.1.refs_1_.refs_2_), channel_id=1, source_target_pairs={{0,8},{8,0},{16,24},{24,16},{32,40},{40,32},{48,56},{56,48},{64,72... | collective-permute-start | bytes 884744 | tf_op jit(solution)/shard_map/fetch_points/ppermute | solution.py:29
  5.0 13.1 %collective-permute-start.2 = (bf16[576,256]{1,0:T(8,128)(2,1)S(1)}, bf16[576,256]{1,0:T(8,128)(2,1)S(1)}, u32[]{:S(2)}, u32[]{:S(2)}) collective-permute-start(bf16[576,256]{1,0:T(8,128)(2,1)S(1)} %pack.1.refs_1_.refs_2_), channel_id=1, source_target_pairs={{0,32},{8,40},{16,48},{24,56},{32,0},{40,8},{48,16},{56,24},{64,96... | collective-permute-start | bytes 884744 | tf_op jit(solution)/shard_map/fetch_points/ppermute | solution.py:29
  6.6 9.3 %collective-permute-start.1 = (bf16[512,256]{1,0:T(8,128)(2,1)S(1)}, bf16[512,256]{1,0:T(8,128)(2,1)S(1)}, u32[]{:S(2)}, u32[]{:S(2)}) collective-permute-start(bf16[512,256]{1,0:T(8,128)(2,1)S(1)} %constant_dynamic-slice_fusion.points_ref.refs_0_), channel_id=1, source_target_pairs={{0,24},{8,16},{16,8},{24,0},{32,56},{40,48},{48,40},{56,32},{64,88... | collective-permute-start | bytes 786440 | tf_op jit(solution)/shard_map/fetch_points/ppermute | solution.py:29
  9.1 9.0 %collective-permute-start = (bf16[512,256]{1,0:T(8,128)(2,1)S(1)}, bf16[512,256]{1,0:T(8,128)(2,1)S(1)}, u32[]{:S(2)}, u32[]{:S(2)}) collective-permute-start(bf16[512,256]{1,0:T(8,128)(2,1)S(1)} %constant_dynamic-slice_fusion.points_ref.refs_0_), channel_id=1, source_target_pairs={{0,96},{8,104},{16,112},{24,120},{32,64},{40,72},{48,80},{56,88},{... | collective-permute-start | bytes 786440 | tf_op jit(solution)/shard_map/fetch_points/ppermute | solution.py:29
  18.1 7.0 %collective-permute-start.6 = (bf16[576,256]{1,0:T(8,128)(2,1)S(1)}, bf16[576,256]{1,0:T(8,128)(2,1)S(1)}, u32[]{:S(2)}, u32[]{:S(2)}) collective-permute-start(bf16[576,256]{1,0:T(8,128)(2,1)S(1)} %collective-permute-done.2.refs_3_), channel_id=1, source_target_pairs={{0,4},{4,0},{1,5},{5,1},{2,6},{6,2},{3,7},{7,3},{8,12},{12,8},{9,1... | collective-permute-start | bytes 884744 | tf_op jit(solution)/shard_map/fetch_points/ppermute | solution.py:33
  18.1 7.0 %collective-permute-start.7 = (bf16[576,256]{1,0:T(8,128)(2,1)S(1)}, bf16[576,256]{1,0:T(8,128)(2,1)S(1)}, u32[]{:S(2)}, u32[]{:S(2)}) collective-permute-start(bf16[576,256]{1,0:T(8,128)(2,1)S(1)} %collective-permute-done.3.refs_4_), channel_id=1, source_target_pairs={{0,4},{4,0},{1,5},{5,1},{2,6},{6,2},{3,7},{7,3},{8,12},{12,8},{9,1... | collective-permute-start | bytes 884744 | tf_op jit(solution)/shard_map/fetch_points/ppermute | solution.py:33
  18.6 13.7 %collective-permute-start.8 = (bf16[576,256]{1,0:T(8,128)(2,1)S(1)}, bf16[576,256]{1,0:T(8,128)(2,1)S(1)}, u32[]{:S(2)}, u32[]{:S(2)}) collective-permute-start(bf16[576,256]{1,0:T(8,128)(2,1)S(1)} %pack.1.refs_1_.refs_2_), channel_id=1, source_target_pairs={{0,40},{8,32},{16,56},{24,48},{32,8},{40,0},{48,24},{56,16},{64,10... | collective-permute-start | bytes 884744 | tf_op jit(solution)/shard_map/fetch_points/ppermute | solution.py:29
  19.0 11.3 %collective-permute-start.5 = (bf16[512,256]{1,0:T(8,128)(2,1)S(1)}, bf16[512,256]{1,0:T(8,128)(2,1)S(1)}, u32[]{:S(2)}, u32[]{:S(2)}) collective-permute-start(bf16[512,256]{1,0:T(8,128)(2,1)S(1)} %constant_dynamic-slice_fusion.points_ref.refs_0_), channel_id=1, source_target_pairs={{0,120},{8,112},{16,104},{24,96},{32,88},{40,80},{48,72},{56,64},{... | collective-permute-start | bytes 786440 | tf_op jit(solution)/shard_map/fetch_points/ppermute | solution.py:29
  32.4 1.8 %collective-permute-start.9 = (bf16[576,256]{1,0:T(8,128)(2,1)S(1)}, bf16[576,256]{1,0:T(8,128)(2,1)S(1)}, u32[]{:S(2)}, u32[]{:S(2)}) collective-permute-start(bf16[576,256]{1,0:T(8,128)(2,1)S(1)} %collective-permute-done.8.refs_4_), channel_id=1, source_target_pairs={{0,4},{4,0},{1,5},{5,1},{2,6},{6,2},{3,7},{7,3},{8,12},{12,8},{9,1... | collective-permute-start | bytes 884744 | tf_op jit(solution)/shard_map/build_tiles/ppermute | solution.py:33
  35.5 9.2 %collective-permute-start.12 = (f32[16,2048]{1,0:T(8,128)S(1)}, f32[16,2048]{1,0:T(8,128)S(1)}, u32[]{:S(2)}, u32[]{:S(2)}) collective-permute-start(f32[16,2048]{1,0:T(8,128)S(1)} %get-tuple-element.53.refs_0_), channel_id=1, source_target_pairs={{0,120},{8,112},{16,104},{24,96},{32,88},{40,80},{48,72},{56,64},{... | collective-permute-start | bytes 393224 | tf_op jit(solution)/shard_map/sum_over_rows/ppermute | solution.py:29
  38.3 9.1 %collective-permute-start.11 = (f32[16,2048]{1,0:T(8,128)S(1)}, f32[16,2048]{1,0:T(8,128)S(1)}, u32[]{:S(2)}, u32[]{:S(2)}) collective-permute-start(f32[16,2048]{1,0:T(8,128)S(1)} %get-tuple-element.53.refs_0_), channel_id=1, source_target_pairs={{0,24},{8,16},{16,8},{24,0},{32,56},{40,48},{48,40},{56,32},{64,88... | collective-permute-start | bytes 393224 | tf_op jit(solution)/shard_map/sum_over_rows/ppermute | solution.py:29
  40.6 6.8 %collective-permute-start.10 = (f32[16,2048]{1,0:T(8,128)S(1)}, f32[16,2048]{1,0:T(8,128)S(1)}, u32[]{:S(2)}, u32[]{:S(2)}) collective-permute-start(f32[16,2048]{1,0:T(8,128)S(1)} %get-tuple-element.53.refs_0_), channel_id=1, source_target_pairs={{0,96},{8,104},{16,112},{24,120},{32,64},{40,72},{48,80},{56,88},{... | collective-permute-start | bytes 393224 | tf_op jit(solution)/shard_map/sum_over_rows/ppermute | solution.py:29
  47.4 9.6 %copy-start.2 = (f32[512,16]{0,1:T(8,128)S(1)}, f32[512,16]{0,1:T(8,128)}, u32[]{:S(2)}) copy-start(f32[512,16]{0,1:T(8,128)} %param.5) | copy-start | bytes 98308
  50.1 1.4 %collective-permute-start.13 = (f32[16,2048]{1,0:T(8,128)S(1)}, f32[16,2048]{1,0:T(8,128)S(1)}, u32[]{:S(2)}, u32[]{:S(2)}) collective-permute-start(f32[16,2048]{1,0:T(8,128)S(1)} %get-tuple-element.63), channel_id=1, source_target_pairs={{0,4},{4,0},{1,5},{5,1},{2,6},{6,2},{3,7},{7,3},{8,12},{12,8},{9,1... | collective-permute-start | bytes 393224 | tf_op jit(solution)/shard_map/sum_over_columns/ppermute | solution.py:33
  51.5 4.9 %collective-permute-start.16 = (f32[16,512]{1,0:T(8,128)S(1)}, f32[16,512]{1,0:T(8,128)S(1)}, u32[]{:S(2)}, u32[]{:S(2)}) collective-permute-start(f32[16,512]{1,0:T(8,128)S(1)} %get-tuple-element.68), channel_id=1, source_target_pairs={{0,40},{8,32},{16,56},{24,48},{32,8},{40,0},{48,24},{56,16},{64,10... | collective-permute-start | bytes 98312 | tf_op jit(solution)/shard_map/sum_over_columns/ppermute | solution.py:29
  51.6 4.8 %collective-permute-start.15 = (f32[16,512]{1,0:T(8,128)S(1)}, f32[16,512]{1,0:T(8,128)S(1)}, u32[]{:S(2)}, u32[]{:S(2)}) collective-permute-start(f32[16,512]{1,0:T(8,128)S(1)} %get-tuple-element.69), channel_id=1, source_target_pairs={{0,8},{8,0},{16,24},{24,16},{32,40},{40,32},{48,56},{56,48},{64,72... | collective-permute-start | bytes 98312 | tf_op jit(solution)/shard_map/sum_over_columns/ppermute | solution.py:29
  52.8 4.2 %collective-permute-start.14 = (f32[16,512]{1,0:T(8,128)S(1)}, f32[16,512]{1,0:T(8,128)S(1)}, u32[]{:S(2)}, u32[]{:S(2)}) collective-permute-start(f32[16,512]{1,0:T(8,128)S(1)} %get-tuple-element.70), channel_id=1, source_target_pairs={{0,32},{8,40},{16,48},{24,56},{32,0},{40,8},{48,16},{56,24},{64,96... | collective-permute-start | bytes 98312 | tf_op jit(solution)/shard_map/sum_over_columns/ppermute | solution.py:29

commit v10 on v9

--- a/solution.py
+++ b/solution.py
@@ -27,6 +27,21 @@
         for z in range(NZ):
             pairs.append((y * NZ + z, (y ^ offset[0]) * NZ + (z ^ offset[1])))
     return lax.ppermute(value, ("y", "z"), pairs)
+
+
+def swap_each(values, offsets):
+    received = [swap(value, offset) for value, offset in reversed(list(zip(values, offsets)))]
+    return received[::-1]
+
+
+def hand_on(along_y, along_z, step):
+    value = jnp.where(lax.axis_index("c") == 0, along_z, along_y)
+    pairs = []
+    for y in range(NY):
+        for z in range(NZ):
+            here = (y * NZ + z) * NC
+            pairs += [(here, ((y ^ step) * NZ + z) * NC), (here + 1, (y * NZ + (z ^ step)) * NC + 1)]
+    return lax.ppermute(value, ("y", "z", "c"), pairs)
 
 
 def swap_core(value):
@@ -148,16 +163,40 @@
     )(*args)
 
 
+def share_kernel(own, image_ref, *out_refs):
+    probes = image_ref.shape[0]
+    for k, out_ref in enumerate(out_refs, 1):
+        for i in range(len(ROWS)):
+            high, middle, _ = split(image_ref[:, i * own : (i + 1) * own])
+            out_ref[i * probes : (i + 1) * probes, :] = high
+            if i == k:
+                out_ref[len(ROWS) * probes :, :] = middle
+
+
+def share(image, own):
+    probes = image.shape[0]
+    height = (len(ROWS) + 1) * probes
+    return pl.pallas_call(
+        functools.partial(share_kernel, own),
+        out_shape=[jax.ShapeDtypeStruct((height, own), jnp.bfloat16)] * (len(ROWS) - 1),
+        compiler_params=pltpu.CompilerParams(vmem_limit_bytes=4 << 20),
+        name="share",
+    )(image)
+
+
 def second_kernel(own, places, *refs):
     parts, refs = refs[: len(ROWS)], refs[len(ROWS) :]
     tiles, (mine_ref, other_ref, rho_ref) = refs[: len(places)], refs[len(places) :]
     probes = rho_ref.shape[0]
     pieces = []
     for p in ROWS:
-        piece = 0.0
-        for s, part in zip(ROWS, parts):
-            at = ROWS.index((p[0] ^ s[0], p[1] ^ s[1])) * own
-            piece = piece + part[:, at : at + own]
+        at = ROWS.index(p) * own
+        piece = parts[0][:, at : at + own]
+        for s, part in zip(ROWS[1:], parts[1:]):
+            at = ROWS.index((p[0] ^ s[0], p[1] ^ s[1])) * probes
+            piece = piece + part[at : at + probes, :].astype(jnp.float32)
+            if p == HERE:
+                piece = piece + part[len(ROWS) * probes :, :].astype(jnp.float32)
         pieces.append(-STEP * piece)
     rho_ref[...] = pieces[0]
     rho = jnp.concatenate(pieces, axis=1)
@@ -254,13 +293,15 @@
     points = lax.dynamic_slice_in_dim(states, offsets[0], own, 0)
     with jax.named_scope("fetch_points"):
         message = pack(points, side)
-        rows = [points] + [swap(points, offset) for offset in ROWS[1:]]
-        cols = [message] + [swap(message, offset) for offset in SQUARE[1:]]
+        rows = [points] + [swap(points, offset) for offset in ROWS[1:3]]
+        cols = [message] + [swap(message, offset) for offset in SQUARE[1:3]]
         first = [message, swap_core(message)]
         tile_a, image_a, half_a = build([points], first, own, probes, side=side)
         (rows[1], rows[2], cols[1], cols[2]), image_a = lax.optimization_barrier(
             ((rows[1], rows[2], cols[1], cols[2]), image_a)
         )
+        rows.append(hand_on(rows[1], rows[2], 3))
+        cols.append(hand_on(cols[1], cols[2], 1))
         others = [swap_core(cols[1]), swap_core(cols[2])]
 
     with jax.named_scope("build_tiles"):
@@ -286,15 +327,14 @@
         ]
 
     with jax.named_scope("sum_over_rows"):
-        parts = [image] + [swap(image, offset) for offset in ROWS[1:]]
+        parts = [image] + swap_each(share(image, own), ROWS[1:])
 
     mine, other, rho = second_product(tiles, parts, own)
 
     with jax.named_scope("sum_over_columns"):
         mine = mine + swap_core(other)
-        shares = [mine[:, :own]]
-        for m, offset in enumerate(SQUARE[1:], 1):
-            shares.append(swap(mine[:, m * own : (m + 1) * own], offset))
+        blocks = [mine[:, m * own : (m + 1) * own] for m in range(len(SQUARE))]
+        shares = blocks[:1] + swap_each(blocks[1:], SQUARE[1:])
 
     with jax.named_scope("final_sums"):
         image, sums = local_sums(side, rho, shares)

time: 72.9 us -> 68.3 us (0.937)
  waiting for transfers between devices: 18.7 us -> 14.4 us
  local copies, waits for them, and re-layouts: 1.2 us -> 1.95 us
    ppermute x12 -> x10, waiting for transfers between devices: 17.1 us -> 12.8 us  [swap(): return lax.ppermute(value, ('y', 'z'), pairs)]
    ppermute x12 -> x10, starting transfers between devices: 21 us -> 17.9 us  [swap(): return lax.ppermute(value, ('y', 'z'), pairs)]
    ppermute x0 -> x2, starting transfers between devices: none -> 2.4 us  [hand_on(): return lax.ppermute(value, ('y', 'z', 'c'), pairs)]
    unnamed x6 -> x8, local copies, waits for them, and re-layouts: 1.11 us -> 1.86 us
  transfers between devices with their start and end apart: 17 -> 17, of which waited for: 9 -> 8; matrix products, arithmetic and copies ran while one was open for 0% -> 0% of each run, Pallas kernels for 13% -> 14%
where the time goes in v10:
time: 68.3 us; the launch traced here: 67 us
  starting transfers between devices  21.1 us (31%)
  Pallas kernels  15.1 us (22%)
  waiting for transfers between devices  14.4 us (21%)
  blocking collectives  12.9 us (19%)
  local copies, waits for them, and re-layouts  1.95 us (3%)
  between operations  1.47 us (2%)
    ppermute x10, starting transfers between devices, swap(): return lax.ppermute(value, ('y', 'z'), pairs)  17.9 us
    all_to_all x1, blocking collectives, on_device(): sums = lax.all_to_all(sums, ('y', 'z', 'c'), 0, 0, tiled=True)  12.9 us
    ppermute x10, waiting for transfers between devices, swap(): return lax.ppermute(value, ('y', 'z'), pairs)  12.8 us
    pallas_call x7, Pallas kernels, build(): pl.pallas_call(functools.partial(tile_kernel, counts, probes), out_shape=...  10.9 us
    pallas_call x1, Pallas kernels, second_product(): pl.pallas_call(functools.partial(second_kernel, own, places), in_specs=[p...  2.78 us
    ppermute x2, starting transfers between devices, hand_on(): return lax.ppermute(value, ('y', 'z', 'c'), pairs)  2.4 us
    unnamed x8, local copies, waits for them, and re-layouts  1.86 us
    ppermute x5, waiting for transfers between devices, swap_core(): return lax.ppermute(value, 'c', [(0, 1), (1, 0)])  1.61 us
  transfers between devices with their start and end apart: 17, of which 8 were waited for; matrix products, arithmetic and copies ran while one was open for 0% of the time, Pallas kernels for 14%

profile of v10, /device:TPU:0, one launch (start us, length us, event | category | flops | bytes accessed | tf_op | source)
XLA Modules:
  0.0 67.0 jit_solution(5691055921286709800)
XLA Ops:
  1.4 0.3 copy-done
  1.8 0.7 %copy-done.1 = f32[512,16]{0,1:T(8,128)S(1)} copy-done((f32[512,16]{0,1:T(8,128)S(1)}, f32[512,16]{0,1:T(8,128)}, u32[]{:S(2)}) %copy-start.1) | copy-done | bytes 32792
  2.5 0.3 pack.1.refs_1_.refs_2_
  2.9 2.1 %collective-permute-start.3 = (bf16[576,256]{1,0:T(8,128)(2,1)S(1)}, bf16[576,256]{1,0:T(8,128)(2,1)S(1)}, u32[]{:S(2)}, u32[]{:S(2)}) collective-permute-start(bf16[576,256]{1,0:T(8,128)(2,1)S(1)} %pack.1.refs_1_.refs_2_), channel_id=1, source_target_pairs={{0,8},{8,0},{16,24},{24,16},{32,40},{40,32},{48,56},{56,48},{64,72... | collective-permute-start | bytes 884744 | tf_op jit(solution)/shard_map/fetch_points/ppermute | solution.py:29
  5.0 1.6 %collective-permute-start.2 = (bf16[576,256]{1,0:T(8,128)(2,1)S(1)}, bf16[576,256]{1,0:T(8,128)(2,1)S(1)}, u32[]{:S(2)}, u32[]{:S(2)}) collective-permute-start(bf16[576,256]{1,0:T(8,128)(2,1)S(1)} %pack.1.refs_1_.refs_2_), channel_id=1, source_target_pairs={{0,32},{8,40},{16,48},{24,56},{32,0},{40,8},{48,16},{56,24},{64,96... | collective-permute-start | bytes 884744 | tf_op jit(solution)/shard_map/fetch_points/ppermute | solution.py:29
  6.6 2.5 %collective-permute-start.1 = (bf16[512,256]{1,0:T(8,128)(2,1)S(1)}, bf16[512,256]{1,0:T(8,128)(2,1)S(1)}, u32[]{:S(2)}, u32[]{:S(2)}) collective-permute-start(bf16[512,256]{1,0:T(8,128)(2,1)S(1)} %constant_dynamic-slice_fusion.points_ref.refs_0_), channel_id=1, source_target_pairs={{0,24},{8,16},{16,8},{24,0},{32,56},{40,48},{48,40},{56,32},{64,88... | collective-permute-start | bytes 786440 | tf_op jit(solution)/shard_map/fetch_points/ppermute | solution.py:29
  9.1 2.2 %collective-permute-start = (bf16[512,256]{1,0:T(8,128)(2,1)S(1)}, bf16[512,256]{1,0:T(8,128)(2,1)S(1)}, u32[]{:S(2)}, u32[]{:S(2)}) collective-permute-start(bf16[512,256]{1,0:T(8,128)(2,1)S(1)} %constant_dynamic-slice_fusion.points_ref.refs_0_), channel_id=1, source_target_pairs={{0,96},{8,104},{16,112},{24,120},{32,64},{40,72},{48,80},{56,88},{... | collective-permute-start | bytes 786440 | tf_op jit(solution)/shard_map/fetch_points/ppermute | solution.py:29
  11.3 0.8 %copy-done.2 = f32[512,16]{0,1:T(8,128)S(1)} copy-done((f32[512,16]{0,1:T(8,128)S(1)}, f32[512,16]{0,1:T(8,128)}, u32[]{:S(2)}) %copy-start.2) | copy-done | bytes 32792
  12.0 0.8 %build_tile.7 = (bf16[512,1024]{1,0:T(8,128)(2,1)S(1)}, f32[16,512]{1,0:T(8,128)S(1)}, f32[512,1]{1,0:T(8,128)S(1)}) custom-call(bf16[512,256]{1,0:T(8,128)(2,1)S(1)} %constant_dynamic-slice_fusion.points_ref.refs_0_, bf16[576,256]{1,0:T(8,128)(2,1)S(1)} %pack.1.refs_1_.refs_2_, bf16[576,256]{1,0:T(8,128)(2,1)S(1)} %collective-permute-done.4.refs_2_.refs_3_, ...), custom_call_target="tpu_custom_call" | custom-call | flops 16777216 | bytes 1024 | tf_op jit(solution)/shard_map/fetch_points/build_tile/pallas_call | solution.py:155
  12.9 3.0 %collective-permute-done.1.refs_1_.refs_2_ = bf16[512,256]{1,0:T(8,128)(2,1)S(1)} collective-permute-done((bf16[512,256]{1,0:T(8,128)(2,1)S(1)}, bf16[512,256]{1,0:T(8,128)(2,1)S(1)}, u32[]{:S(2)}, u32[]{:S(2)}) %collective-permute-start.1) | collective-permute-done | bytes 262176 | tf_op jit(solution)/shard_map/fetch_points/ppermute | solution.py:29
  15.9 2.2 %collective-permute-done.refs_0_.refs_1_ = bf16[512,256]{1,0:T(8,128)(2,1)S(1)} collective-permute-done((bf16[512,256]{1,0:T(8,128)(2,1)S(1)}, bf16[512,256]{1,0:T(8,128)(2,1)S(1)}, u32[]{:S(2)}, u32[]{:S(2)}) %collective-permute-start) | collective-permute-done | bytes 262176 | tf_op jit(solution)/shard_map/fetch_points/ppermute | solution.py:29
  18.1 0.5 collective-permute-start.7
  18.8 2.3 %collective-permute-start.5 = (bf16[512,256]{1,0:T(8,128)(2,1)S(1)}, bf16[512,256]{1,0:T(8,128)(2,1)S(1)}, u32[]{:S(2)}, u32[]{:S(2)}) collective-permute-start(bf16[512,256]{1,0:T(8,128)(2,1)S(1)} %broadcast_select_fusion.1), channel_id=1, source_target_pairs={{0,96},{4,28},{8,104},{12,20},{16,112},{20,12},{24,120},{28,4},{32... | collective-permute-start | bytes 786440 | tf_op jit(solution)/shard_map/fetch_points/ppermute | solution.py:44
  21.1 1.4 %build_tile.8 = (bf16[1024,1024]{1,0:T(8,128)(2,1)S(1)}, f32[16,1024]{1,0:T(8,128)S(1)}, f32[1024,1]{1,0:T(8,128)S(1)}) custom-call(bf16[512,256]{1,0:T(8,128)(2,1)S(1)} %collective-permute-done.refs_0_.refs_1_, bf16[512,256]{1,0:T(8,128)(2,1)S(1)} %collective-permute-done.1.refs_1_.refs_2_, bf16[576,256]{1,0:T(8,128)(2,1)S(1)} %pack.1.refs_1_.refs_2_, ...), custom_call_target="tpu_custom_call" | custom-call | flops 33554432 | bytes 1024 | tf_op jit(solution)/shard_map/build_tiles/build_tile/pallas_call | solution.py:155
  22.5 1.9 %build_tile.9 = (bf16[1536,1024]{1,0:T(8,128)(2,1)S(1)}, f32[16,1536]{1,0:T(8,128)S(1)}) custom-call(bf16[512,256]{1,0:T(8,128)(2,1)S(1)} %constant_dynamic-slice_fusion.points_ref.refs_0_, bf16[512,256]{1,0:T(8,128)(2,1)S(1)} %collective-permute-done.refs_0_.refs_1_, bf16[512,256]{1,0:T(8,128)(2,1)S(1)} %collective-permute-done.1.refs_1_.refs_2_, ...), custom_call_target="tpu_custom_call" | custom-call | flops 50331648 | bytes 1024 | tf_op jit(solution)/shard_map/build_tiles/build_tile/pallas_call | solution.py:155
  24.5 1.9 %build_tile.10 = (bf16[1536,1024]{1,0:T(8,128)(2,1)S(1)}, f32[16,1536]{1,0:T(8,128)S(1)}) custom-call(bf16[512,256]{1,0:T(8,128)(2,1)S(1)} %constant_dynamic-slice_fusion.points_ref.refs_0_, bf16[512,256]{1,0:T(8,128)(2,1)S(1)} %collective-permute-done.refs_0_.refs_1_, bf16[512,256]{1,0:T(8,128)(2,1)S(1)} %collective-permute-done.1.refs_1_.refs_2_, ...), custom_call_target="tpu_custom_call" | custom-call | flops 50331648 | bytes 1024 | tf_op jit(solution)/shard_map/build_tiles/build_tile/pallas_call | solution.py:155
  26.4 2.1 %build_tile.11 = (bf16[512,3072]{1,0:T(8,128)(2,1)S(1)}, f32[16,512]{1,0:T(8,128)S(1)}, f32[512,1]{1,0:T(8,128)S(1)}) custom-call(bf16[512,256]{1,0:T(8,128)(2,1)S(1)} %collective-permute-done.5.refs_0_.refs_3_, bf16[576,256]{1,0:T(8,128)(2,1)S(1)} %pack.1.refs_1_.refs_2_, bf16[576,256]{1,0:T(8,128)(2,1)S(1)} %collective-permute-done.4.refs_2_.refs_3_, ...), custom_call_target="tpu_custom_call" | custom-call | flops 50331648 | bytes 1024 | tf_op jit(solution)/shard_map/build_tiles/build_tile/pallas_call | solution.py:155
  28.7 1.3 %build_tile.12 = (bf16[2048,512]{1,0:T(8,128)(2,1)S(1)}, f32[16,2048]{1,0:T(8,128)S(1)}) custom-call(bf16[512,256]{1,0:T(8,128)(2,1)S(1)} %constant_dynamic-slice_fusion.points_ref.refs_0_, bf16[512,256]{1,0:T(8,128)(2,1)S(1)} %collective-permute-done.refs_0_.refs_1_, bf16[512,256]{1,0:T(8,128)(2,1)S(1)} %collective-permute-done.1.refs_1_.refs_2_, ...), custom_call_target="tpu_custom_call" | custom-call | flops 33554432 | bytes 1024 | tf_op jit(solution)/shard_map/build_tiles/build_tile/pallas_call | solution.py:155
  30.1 0.2 collective-permute-done.9.refs_4_
  30.3 1.3 %build_tile.13 = (bf16[2048,512]{1,0:T(8,128)(2,1)S(1)}, f32[16,2048]{1,0:T(8,128)S(1)}) custom-call(bf16[512,256]{1,0:T(8,128)(2,1)S(1)} %constant_dynamic-slice_fusion.points_ref.refs_0_, bf16[512,256]{1,0:T(8,128)(2,1)S(1)} %collective-permute-done.refs_0_.refs_1_, bf16[512,256]{1,0:T(8,128)(2,1)S(1)} %collective-permute-done.1.refs_1_.refs_2_, ...), custom_call_target="tpu_custom_call" | custom-call | flops 33554432 | bytes 1024 | tf_op jit(solution)/shard_map/build_tiles/build_tile/pallas_call | solution.py:155
  31.7 2.3 %collective-permute-start.10 = (bf16[80,512]{1,0:T(8,128)(2,1)S(1)}, bf16[80,512]{1,0:T(8,128)(2,1)S(1)}, u32[]{:S(2)}, u32[]{:S(2)}) collective-permute-start(bf16[80,512]{1,0:T(8,128)(2,1)S(1)} %get-tuple-element.57), channel_id=1, source_target_pairs={{0,96},{8,104},{16,112},{24,120},{32,64},{40,72},{48,80},{56,88},{... | collective-permute-start | bytes 245768 | tf_op jit(solution)/shard_map/sum_over_rows/ppermute | solution.py:29
  34.0 1.6 %collective-permute-start.11 = (bf16[80,512]{1,0:T(8,128)(2,1)S(1)}, bf16[80,512]{1,0:T(8,128)(2,1)S(1)}, u32[]{:S(2)}, u32[]{:S(2)}) collective-permute-start(bf16[80,512]{1,0:T(8,128)(2,1)S(1)} %get-tuple-element.58), channel_id=1, source_target_pairs={{0,24},{8,16},{16,8},{24,0},{32,56},{40,48},{48,40},{56,32},{64,88... | collective-permute-start | bytes 245768 | tf_op jit(solution)/shard_map/sum_over_rows/ppermute | solution.py:29
  35.6 2.1 %collective-permute-start.12 = (bf16[80,512]{1,0:T(8,128)(2,1)S(1)}, bf16[80,512]{1,0:T(8,128)(2,1)S(1)}, u32[]{:S(2)}, u32[]{:S(2)}) collective-permute-start(bf16[80,512]{1,0:T(8,128)(2,1)S(1)} %get-tuple-element.59), channel_id=1, source_target_pairs={{0,120},{8,112},{16,104},{24,96},{32,88},{40,80},{48,72},{56,64},{... | collective-permute-start | bytes 245768 | tf_op jit(solution)/shard_map/sum_over_rows/ppermute | solution.py:29
  37.7 2.0 %collective-permute-done.11.refs_2_ = bf16[80,512]{1,0:T(8,128)(2,1)S(1)} collective-permute-done((bf16[80,512]{1,0:T(8,128)(2,1)S(1)}, bf16[80,512]{1,0:T(8,128)(2,1)S(1)}, u32[]{:S(2)}, u32[]{:S(2)}) %collective-permute-start.11) | collective-permute-done | bytes 81952 | tf_op jit(solution)/shard_map/sum_over_rows/ppermute | solution.py:29
  39.7 3.7 %collective-permute-done.12.refs_3_ = bf16[80,512]{1,0:T(8,128)(2,1)S(1)} collective-permute-done((bf16[80,512]{1,0:T(8,128)(2,1)S(1)}, bf16[80,512]{1,0:T(8,128)(2,1)S(1)}, u32[]{:S(2)}, u32[]{:S(2)}) %collective-permute-start.12) | collective-permute-done | bytes 81952 | tf_op jit(solution)/shard_map/sum_over_rows/ppermute | solution.py:29
  43.4 2.8 %second_product.1 = (f32[16,2048]{1,0:T(8,128)S(1)}, f32[16,2048]{1,0:T(8,128)S(1)}, f32[16,512]{1,0:T(8,128)S(1)}) custom-call(f32[16,2048]{1,0:T(8,128)S(1)} %get-tuple-element.56.image_ref.refs_0_, bf16[80,512]{1,0:T(8,128)(2,1)S(1)} %collective-permute-done.10.refs_1_, bf16[80,512]{1,0:T(8,128)(2,1)S(1)} %collective-permute-done.11.refs_2_, ...), custom_call_target="tpu_custom_call" | custom-call | flops 268435456 | bytes 1024 | tf_op jit(solution)/shard_map/second_product/pallas_call | solution.py:222
  46.1 1.4 %collective-permute-done.13 = f32[16,2048]{1,0:T(8,128)S(1)} collective-permute-done((f32[16,2048]{1,0:T(8,128)S(1)}, f32[16,2048]{1,0:T(8,128)S(1)}, u32[]{:S(2)}, u32[]{:S(2)}) %collective-permute-start.13) | collective-permute-done | bytes 131104 | tf_op jit(solution)/shard_map/sum_over_columns/ppermute | solution.py:48
  47.7 3.4 %collective-permute-start.14 = (f32[16,512]{1,0:T(8,128)S(1)}, f32[16,512]{1,0:T(8,128)S(1)}, u32[]{:S(2)}, u32[]{:S(2)}) collective-permute-start(f32[16,512]{1,0:T(8,128)S(1)} %get-tuple-element.76), channel_id=1, source_target_pairs={{0,32},{8,40},{16,48},{24,56},{32,0},{40,8},{48,16},{56,24},{64,96... | collective-permute-start | bytes 98312 | tf_op jit(solution)/shard_map/sum_over_columns/ppermute | solution.py:29
  51.1 1.3 %collective-permute-done.16.refs_3_ = f32[16,512]{1,0:T(8,128)S(1)} collective-permute-done((f32[16,512]{1,0:T(8,128)S(1)}, f32[16,512]{1,0:T(8,128)S(1)}, u32[]{:S(2)}, u32[]{:S(2)}) %collective-permute-start.16) | collective-permute-done | bytes 32800 | tf_op jit(solution)/shard_map/sum_over_columns/ppermute | solution.py:29
  52.4 0.6 collective-permute-done.14.refs_1_
  53.2 12.9 %all_to_all.5.sums_ref = f32[32,8,128]{2,1,0:T(8,128)S(1)} all-to-all(f32[32,8,128]{2,1,0:T(8,128)S(1)} %broadcast_in_dim.3), channel_id=1, replica_groups=mesh['y'=4,'z'=4,'c'=2,'x'=4] {'y','z','c'}, dimensions={0} | all-to-all | bytes 262144 | tf_op jit(solution)/shard_map/final_sums/all_to_all | solution.py:342
  66.1 0.9 %finish.1 = (f32[16,512]{1,0:T(8,128)}, f32[16,512]{1,0:T(8,128)}) custom-call(f32[16,512]{1,0:T(8,128)S(1)} %bitcast.10, f32[16,512]{1,0:T(8,128)S(1)} %get-tuple-element.67.rho_ref, f32[16,512]{1,0:T(8,128)S(1)} %get-tuple-element.70.image_ref, f32[32,8,128]{2,1,0:T(8,128)S(1)} %all_to_all.5.sums_ref), custom_call_target="tpu_custom_call" | custom-call | tf_op jit(solution)/shard_map/finish/pallas_call | solution.py:282
  (29 shorter events, 1.0 us)
Async XLA Ops:
  0.6 1.1 %copy-start = (bf16[1024,256]{1,0:T(8,128)(2,1)S(1)}, bf16[1024,256]{1,0:T(8,128)(2,1)}, u32[]{:S(2)}) copy-start(bf16[1024,256]{1,0:T(8,128)(2,1)} %param.3) | copy-start | bytes 1572868
  1.8 0.8 %copy-start.1 = (f32[512,16]{0,1:T(8,128)S(1)}, f32[512,16]{0,1:T(8,128)}, u32[]{:S(2)}) copy-start(f32[512,16]{0,1:T(8,128)} %param.5) | copy-start | bytes 98308
  2.8 8.5 %collective-permute-start.4 = (bf16[576,256]{1,0:T(8,128)(2,1)S(1)}, bf16[576,256]{1,0:T(8,128)(2,1)S(1)}, u32[]{:S(2)}, u32[]{:S(2)}) collective-permute-start(bf16[576,256]{1,0:T(8,128)(2,1)S(1)} %pack.1.refs_1_.refs_2_), channel_id=1, source_target_pairs={{0,4},{4,0},{1,5},{5,1},{2,6},{6,2},{3,7},{7,3},{8,12},{12,8},{9,1... | collective-permute-start | bytes 884744 | tf_op jit(solution)/shard_map/fetch_points/ppermute | solution.py:48
  2.9 15.2 %collective-permute-start.3 = (bf16[576,256]{1,0:T(8,128)(2,1)S(1)}, bf16[576,256]{1,0:T(8,128)(2,1)S(1)}, u32[]{:S(2)}, u32[]{:S(2)}) collective-permute-start(bf16[576,256]{1,0:T(8,128)(2,1)S(1)} %pack.1.refs_1_.refs_2_), channel_id=1, source_target_pairs={{0,8},{8,0},{16,24},{24,16},{32,40},{40,32},{48,56},{56,48},{64,72... | collective-permute-start | bytes 884744 | tf_op jit(solution)/shard_map/fetch_points/ppermute | solution.py:29
  5.0 13.1 %collective-permute-start.2 = (bf16[576,256]{1,0:T(8,128)(2,1)S(1)}, bf16[576,256]{1,0:T(8,128)(2,1)S(1)}, u32[]{:S(2)}, u32[]{:S(2)}) collective-permute-start(bf16[576,256]{1,0:T(8,128)(2,1)S(1)} %pack.1.refs_1_.refs_2_), channel_id=1, source_target_pairs={{0,32},{8,40},{16,48},{24,56},{32,0},{40,8},{48,16},{56,24},{64,96... | collective-permute-start | bytes 884744 | tf_op jit(solution)/shard_map/fetch_points/ppermute | solution.py:29
  6.6 9.3 %collective-permute-start.1 = (bf16[512,256]{1,0:T(8,128)(2,1)S(1)}, bf16[512,256]{1,0:T(8,128)(2,1)S(1)}, u32[]{:S(2)}, u32[]{:S(2)}) collective-permute-start(bf16[512,256]{1,0:T(8,128)(2,1)S(1)} %constant_dynamic-slice_fusion.points_ref.refs_0_), channel_id=1, source_target_pairs={{0,24},{8,16},{16,8},{24,0},{32,56},{40,48},{48,40},{56,32},{64,88... | collective-permute-start | bytes 786440 | tf_op jit(solution)/shard_map/fetch_points/ppermute | solution.py:29
  9.1 9.0 %collective-permute-start = (bf16[512,256]{1,0:T(8,128)(2,1)S(1)}, bf16[512,256]{1,0:T(8,128)(2,1)S(1)}, u32[]{:S(2)}, u32[]{:S(2)}) collective-permute-start(bf16[512,256]{1,0:T(8,128)(2,1)S(1)} %constant_dynamic-slice_fusion.points_ref.refs_0_), channel_id=1, source_target_pairs={{0,96},{8,104},{16,112},{24,120},{32,64},{40,72},{48,80},{56,88},{... | collective-permute-start | bytes 786440 | tf_op jit(solution)/shard_map/fetch_points/ppermute | solution.py:29
  11.3 0.8 %copy-start.2 = (f32[512,16]{0,1:T(8,128)S(1)}, f32[512,16]{0,1:T(8,128)}, u32[]{:S(2)}) copy-start(f32[512,16]{0,1:T(8,128)} %param.5) | copy-start | bytes 98308
  18.1 6.3 %collective-permute-start.6 = (bf16[576,256]{1,0:T(8,128)(2,1)S(1)}, bf16[576,256]{1,0:T(8,128)(2,1)S(1)}, u32[]{:S(2)}, u32[]{:S(2)}) collective-permute-start(bf16[576,256]{1,0:T(8,128)(2,1)S(1)} %collective-permute-done.2.refs_3_), channel_id=1, source_target_pairs={{0,4},{4,0},{1,5},{5,1},{2,6},{6,2},{3,7},{7,3},{8,12},{12,8},{9,1... | collective-permute-start | bytes 884744 | tf_op jit(solution)/shard_map/fetch_points/ppermute | solution.py:48
  18.1 6.4 %collective-permute-start.7 = (bf16[576,256]{1,0:T(8,128)(2,1)S(1)}, bf16[576,256]{1,0:T(8,128)(2,1)S(1)}, u32[]{:S(2)}, u32[]{:S(2)}) collective-permute-start(bf16[576,256]{1,0:T(8,128)(2,1)S(1)} %collective-permute-done.3.refs_4_), channel_id=1, source_target_pairs={{0,4},{4,0},{1,5},{5,1},{2,6},{6,2},{3,7},{7,3},{8,12},{12,8},{9,1... | collective-permute-start | bytes 884744 | tf_op jit(solution)/shard_map/fetch_points/ppermute | solution.py:48
  18.7 9.9 %collective-permute-start.8 = (bf16[576,256]{1,0:T(8,128)(2,1)S(1)}, bf16[576,256]{1,0:T(8,128)(2,1)S(1)}, u32[]{:S(2)}, u32[]{:S(2)}) collective-permute-start(bf16[576,256]{1,0:T(8,128)(2,1)S(1)} %broadcast_select_fusion), channel_id=1, source_target_pairs={{0,32},{4,12},{8,40},{12,4},{16,48},{20,28},{24,56},{28,20},{32,0}... | collective-permute-start | bytes 884744 | tf_op jit(solution)/shard_map/fetch_points/ppermute | solution.py:44
  18.8 7.7 %collective-permute-start.5 = (bf16[512,256]{1,0:T(8,128)(2,1)S(1)}, bf16[512,256]{1,0:T(8,128)(2,1)S(1)}, u32[]{:S(2)}, u32[]{:S(2)}) collective-permute-start(bf16[512,256]{1,0:T(8,128)(2,1)S(1)} %broadcast_select_fusion.1), channel_id=1, source_target_pairs={{0,96},{4,28},{8,104},{12,20},{16,112},{20,12},{24,120},{28,4},{32... | collective-permute-start | bytes 786440 | tf_op jit(solution)/shard_map/fetch_points/ppermute | solution.py:44
  28.5 1.8 %collective-permute-start.9 = (bf16[576,256]{1,0:T(8,128)(2,1)S(1)}, bf16[576,256]{1,0:T(8,128)(2,1)S(1)}, u32[]{:S(2)}, u32[]{:S(2)}) collective-permute-start(bf16[576,256]{1,0:T(8,128)(2,1)S(1)} %collective-permute-done.8.refs_4_), channel_id=1, source_target_pairs={{0,4},{4,0},{1,5},{5,1},{2,6},{6,2},{3,7},{7,3},{8,12},{12,8},{9,1... | collective-permute-start | bytes 884744 | tf_op jit(solution)/shard_map/build_tiles/ppermute | solution.py:48
  31.7 6.0 %collective-permute-start.10 = (bf16[80,512]{1,0:T(8,128)(2,1)S(1)}, bf16[80,512]{1,0:T(8,128)(2,1)S(1)}, u32[]{:S(2)}, u32[]{:S(2)}) collective-permute-start(bf16[80,512]{1,0:T(8,128)(2,1)S(1)} %get-tuple-element.57), channel_id=1, source_target_pairs={{0,96},{8,104},{16,112},{24,120},{32,64},{40,72},{48,80},{56,88},{... | collective-permute-start | bytes 245768 | tf_op jit(solution)/shard_map/sum_over_rows/ppermute | solution.py:29
  34.0 5.7 %collective-permute-start.11 = (bf16[80,512]{1,0:T(8,128)(2,1)S(1)}, bf16[80,512]{1,0:T(8,128)(2,1)S(1)}, u32[]{:S(2)}, u32[]{:S(2)}) collective-permute-start(bf16[80,512]{1,0:T(8,128)(2,1)S(1)} %get-tuple-element.58), channel_id=1, source_target_pairs={{0,24},{8,16},{16,8},{24,0},{32,56},{40,48},{48,40},{56,32},{64,88... | collective-permute-start | bytes 245768 | tf_op jit(solution)/shard_map/sum_over_rows/ppermute | solution.py:29
  35.6 7.8 %collective-permute-start.12 = (bf16[80,512]{1,0:T(8,128)(2,1)S(1)}, bf16[80,512]{1,0:T(8,128)(2,1)S(1)}, u32[]{:S(2)}, u32[]{:S(2)}) collective-permute-start(bf16[80,512]{1,0:T(8,128)(2,1)S(1)} %get-tuple-element.59), channel_id=1, source_target_pairs={{0,120},{8,112},{16,104},{24,96},{32,88},{40,80},{48,72},{56,64},{... | collective-permute-start | bytes 245768 | tf_op jit(solution)/shard_map/sum_over_rows/ppermute | solution.py:29
  43.4 9.6 %copy-start.3 = (f32[512,16]{0,1:T(8,128)S(1)}, f32[512,16]{0,1:T(8,128)}, u32[]{:S(2)}) copy-start(f32[512,16]{0,1:T(8,128)} %param.5) | copy-start | bytes 98308
  46.1 1.4 %collective-permute-start.13 = (f32[16,2048]{1,0:T(8,128)S(1)}, f32[16,2048]{1,0:T(8,128)S(1)}, u32[]{:S(2)}, u32[]{:S(2)}) collective-permute-start(f32[16,2048]{1,0:T(8,128)S(1)} %get-tuple-element.69), channel_id=1, source_target_pairs={{0,4},{4,0},{1,5},{5,1},{2,6},{6,2},{3,7},{7,3},{8,12},{12,8},{9,1... | collective-permute-start | bytes 393224 | tf_op jit(solution)/shard_map/sum_over_columns/ppermute | solution.py:48
  47.5 4.9 %collective-permute-start.16 = (f32[16,512]{1,0:T(8,128)S(1)}, f32[16,512]{1,0:T(8,128)S(1)}, u32[]{:S(2)}, u32[]{:S(2)}) collective-permute-start(f32[16,512]{1,0:T(8,128)S(1)} %get-tuple-element.74), channel_id=1, source_target_pairs={{0,40},{8,32},{16,56},{24,48},{32,8},{40,0},{48,24},{56,16},{64,10... | collective-permute-start | bytes 98312 | tf_op jit(solution)/shard_map/sum_over_columns/ppermute | solution.py:29
  47.6 4.8 %collective-permute-start.15 = (f32[16,512]{1,0:T(8,128)S(1)}, f32[16,512]{1,0:T(8,128)S(1)}, u32[]{:S(2)}, u32[]{:S(2)}) collective-permute-start(f32[16,512]{1,0:T(8,128)S(1)} %get-tuple-element.75), channel_id=1, source_target_pairs={{0,8},{8,0},{16,24},{24,16},{32,40},{40,32},{48,56},{56,48},{64,72... | collective-permute-start | bytes 98312 | tf_op jit(solution)/shard_map/sum_over_columns/ppermute | solution.py:29
  47.7 5.3 %collective-permute-start.14 = (f32[16,512]{1,0:T(8,128)S(1)}, f32[16,512]{1,0:T(8,128)S(1)}, u32[]{:S(2)}, u32[]{:S(2)}) collective-permute-start(f32[16,512]{1,0:T(8,128)S(1)} %get-tuple-element.76), channel_id=1, source_target_pairs={{0,32},{8,40},{16,48},{24,56},{32,0},{40,8},{48,16},{56,24},{64,96... | collective-permute-start | bytes 98312 | tf_op jit(solution)/shard_map/sum_over_columns/ppermute | solution.py:29

commit v11 on v10

--- a/solution.py
+++ b/solution.py
@@ -12,8 +12,8 @@
 LANES = 128
 CHUNK = 256
 HERE = (0, 0)
-ROWS = (HERE, (3, 0), (0, 3), (3, 3))
-SQUARE = (HERE, (1, 0), (0, 1), (1, 1))
+ROWS = (HERE, (1, 0), (0, 1), (1, 1))
+SQUARE = (HERE, (3, 0), (0, 3), (3, 3))
 COLS = ((0, 0), (1, 0), (0, 1), (0, 2), (1, 1), (1, 2), (0, 3), (1, 3))
 
 noise_level = 1.0
@@ -300,8 +300,8 @@
         (rows[1], rows[2], cols[1], cols[2]), image_a = lax.optimization_barrier(
             ((rows[1], rows[2], cols[1], cols[2]), image_a)
         )
-        rows.append(hand_on(rows[1], rows[2], 3))
-        cols.append(hand_on(cols[1], cols[2], 1))
+        rows.append(hand_on(rows[1], rows[2], 1))
+        cols.append(hand_on(cols[1], cols[2], 3))
         others = [swap_core(cols[1]), swap_core(cols[2])]
 
     with jax.named_scope("build_tiles"):

time: 68.3 us -> 67.3 us (0.985)
  blocking collectives: 12.9 us -> 10.8 us
  waiting for transfers between devices: 14.4 us -> 16.5 us
  starting transfers between devices: 21.1 us -> 20.1 us
    all_to_all x1, blocking collectives: 12.9 us -> 10.8 us  [on_device(): sums = lax.all_to_all(sums, ('y', 'z', 'c'), 0, 0, tiled=True)]
    ppermute x10, waiting for transfers between devices: 12.8 us -> 13.9 us  [swap(): return lax.ppermute(value, ('y', 'z'), pairs)]
    ppermute x2, waiting for transfers between devices: 0.04 us -> 1.05 us  [hand_on(): return lax.ppermute(value, ('y', 'z', 'c'), pairs)]
    ppermute x10, starting transfers between devices: 17.9 us -> 16.9 us  [swap(): return lax.ppermute(value, ('y', 'z'), pairs)]
where the time goes in v11:
time: 67.3 us; the launch traced here: 66 us
  starting transfers between devices  20.1 us (30%)
  waiting for transfers between devices  16.5 us (25%)
  Pallas kernels  15.1 us (22%)
  blocking collectives  10.8 us (16%)
  local copies, waits for them, and re-layouts  1.95 us (3%)
  between operations  1.46 us (2%)
    ppermute x10, starting transfers between devices, swap(): return lax.ppermute(value, ('y', 'z'), pairs)  16.9 us
    ppermute x10, waiting for transfers between devices, swap(): return lax.ppermute(value, ('y', 'z'), pairs)  13.9 us
    pallas_call x7, Pallas kernels, build(): pl.pallas_call(functools.partial(tile_kernel, counts, probes), out_shape=...  10.9 us
    all_to_all x1, blocking collectives, on_device(): sums = lax.all_to_all(sums, ('y', 'z', 'c'), 0, 0, tiled=True)  10.8 us
    pallas_call x1, Pallas kernels, second_product(): pl.pallas_call(functools.partial(second_kernel, own, places), in_specs=[p...  2.78 us
    ppermute x2, starting transfers between devices, hand_on(): return lax.ppermute(value, ('y', 'z', 'c'), pairs)  2.26 us
    unnamed x8, local copies, waits for them, and re-layouts  1.86 us
    ppermute x5, waiting for transfers between devices, swap_core(): return lax.ppermute(value, 'c', [(0, 1), (1, 0)])  1.61 us
  transfers between devices with their start and end apart: 17, of which 8 were waited for; matrix products, arithmetic and copies ran while one was open for 0% of the time, Pallas kernels for 14%

profile of v11, /device:TPU:0, one launch (start us, length us, event | category | flops | bytes accessed | tf_op | source)
XLA Modules:
  0.0 66.0 jit_solution(2449300020759796245)
XLA Ops:
  1.4 0.3 copy-done
  1.8 0.7 %copy-done.1 = f32[512,16]{0,1:T(8,128)S(1)} copy-done((f32[512,16]{0,1:T(8,128)S(1)}, f32[512,16]{0,1:T(8,128)}, u32[]{:S(2)}) %copy-start.1) | copy-done | bytes 32792
  2.5 0.3 pack.1.refs_1_.refs_2_
  2.9 4.2 %collective-permute-start.3 = (bf16[576,256]{1,0:T(8,128)(2,1)S(1)}, bf16[576,256]{1,0:T(8,128)(2,1)S(1)}, u32[]{:S(2)}, u32[]{:S(2)}) collective-permute-start(bf16[576,256]{1,0:T(8,128)(2,1)S(1)} %pack.1.refs_1_.refs_2_), channel_id=1, source_target_pairs={{0,24},{8,16},{16,8},{24,0},{32,56},{40,48},{48,40},{56,32},{64,88... | collective-permute-start | bytes 884744 | tf_op jit(solution)/shard_map/fetch_points/ppermute | solution.py:29
  7.1 3.0 %collective-permute-start.2 = (bf16[576,256]{1,0:T(8,128)(2,1)S(1)}, bf16[576,256]{1,0:T(8,128)(2,1)S(1)}, u32[]{:S(2)}, u32[]{:S(2)}) collective-permute-start(bf16[576,256]{1,0:T(8,128)(2,1)S(1)} %pack.1.refs_1_.refs_2_), channel_id=1, source_target_pairs={{0,96},{8,104},{16,112},{24,120},{32,64},{40,72},{48,80},{56,88},{... | collective-permute-start | bytes 884744 | tf_op jit(solution)/shard_map/fetch_points/ppermute | solution.py:29
  10.3 0.8 %copy-done.2 = f32[512,16]{0,1:T(8,128)S(1)} copy-done((f32[512,16]{0,1:T(8,128)S(1)}, f32[512,16]{0,1:T(8,128)}, u32[]{:S(2)}) %copy-start.2) | copy-done | bytes 32792
  11.0 0.8 %build_tile.7 = (bf16[512,1024]{1,0:T(8,128)(2,1)S(1)}, f32[16,512]{1,0:T(8,128)S(1)}, f32[512,1]{1,0:T(8,128)S(1)}) custom-call(bf16[512,256]{1,0:T(8,128)(2,1)S(1)} %constant_dynamic-slice_fusion.points_ref.refs_0_, bf16[576,256]{1,0:T(8,128)(2,1)S(1)} %pack.1.refs_1_.refs_2_, bf16[576,256]{1,0:T(8,128)(2,1)S(1)} %collective-permute-done.4.refs_2_.refs_3_, ...), custom_call_target="tpu_custom_call" | custom-call | flops 16777216 | bytes 1024 | tf_op jit(solution)/shard_map/fetch_points/build_tile/pallas_call | solution.py:155
  11.9 6.3 %collective-permute-done.1.refs_1_.refs_2_ = bf16[512,256]{1,0:T(8,128)(2,1)S(1)} collective-permute-done((bf16[512,256]{1,0:T(8,128)(2,1)S(1)}, bf16[512,256]{1,0:T(8,128)(2,1)S(1)}, u32[]{:S(2)}, u32[]{:S(2)}) %collective-permute-start.1) | collective-permute-done | bytes 262176 | tf_op jit(solution)/shard_map/fetch_points/ppermute | solution.py:29
  18.3 0.5 collective-permute-start.7
  18.8 2.2 %collective-permute-start.8 = (bf16[576,256]{1,0:T(8,128)(2,1)S(1)}, bf16[576,256]{1,0:T(8,128)(2,1)S(1)}, u32[]{:S(2)}, u32[]{:S(2)}) collective-permute-start(bf16[576,256]{1,0:T(8,128)(2,1)S(1)} %broadcast_select_fusion), channel_id=1, source_target_pairs={{0,96},{4,28},{8,104},{12,20},{16,112},{20,12},{24,120},{28,4},{32... | collective-permute-start | bytes 884744 | tf_op jit(solution)/shard_map/fetch_points/ppermute | solution.py:44
  21.1 1.4 %build_tile.8 = (bf16[1024,1024]{1,0:T(8,128)(2,1)S(1)}, f32[16,1024]{1,0:T(8,128)S(1)}, f32[1024,1]{1,0:T(8,128)S(1)}) custom-call(bf16[512,256]{1,0:T(8,128)(2,1)S(1)} %collective-permute-done.refs_0_.refs_1_, bf16[512,256]{1,0:T(8,128)(2,1)S(1)} %collective-permute-done.1.refs_1_.refs_2_, bf16[576,256]{1,0:T(8,128)(2,1)S(1)} %pack.1.refs_1_.refs_2_, ...), custom_call_target="tpu_custom_call" | custom-call | flops 33554432 | bytes 1024 | tf_op jit(solution)/shard_map/build_tiles/build_tile/pallas_call | solution.py:155
  22.6 1.9 %build_tile.9 = (bf16[1536,1024]{1,0:T(8,128)(2,1)S(1)}, f32[16,1536]{1,0:T(8,128)S(1)}) custom-call(bf16[512,256]{1,0:T(8,128)(2,1)S(1)} %constant_dynamic-slice_fusion.points_ref.refs_0_, bf16[512,256]{1,0:T(8,128)(2,1)S(1)} %collective-permute-done.refs_0_.refs_1_, bf16[512,256]{1,0:T(8,128)(2,1)S(1)} %collective-permute-done.1.refs_1_.refs_2_, ...), custom_call_target="tpu_custom_call" | custom-call | flops 50331648 | bytes 1024 | tf_op jit(solution)/shard_map/build_tiles/build_tile/pallas_call | solution.py:155
  24.5 1.9 %build_tile.10 = (bf16[1536,1024]{1,0:T(8,128)(2,1)S(1)}, f32[16,1536]{1,0:T(8,128)S(1)}) custom-call(bf16[512,256]{1,0:T(8,128)(2,1)S(1)} %constant_dynamic-slice_fusion.points_ref.refs_0_, bf16[512,256]{1,0:T(8,128)(2,1)S(1)} %collective-permute-done.refs_0_.refs_1_, bf16[512,256]{1,0:T(8,128)(2,1)S(1)} %collective-permute-done.1.refs_1_.refs_2_, ...), custom_call_target="tpu_custom_call" | custom-call | flops 50331648 | bytes 1024 | tf_op jit(solution)/shard_map/build_tiles/build_tile/pallas_call | solution.py:155
  26.5 1.0 %collective-permute-done.5.refs_0_.refs_3_ = bf16[512,256]{1,0:T(8,128)(2,1)S(1)} collective-permute-done((bf16[512,256]{1,0:T(8,128)(2,1)S(1)}, bf16[512,256]{1,0:T(8,128)(2,1)S(1)}, u32[]{:S(2)}, u32[]{:S(2)}) %collective-permute-start.5) | collective-permute-done | bytes 262176 | tf_op jit(solution)/shard_map/fetch_points/ppermute | solution.py:44
  27.5 2.1 %build_tile.11 = (bf16[512,3072]{1,0:T(8,128)(2,1)S(1)}, f32[16,512]{1,0:T(8,128)S(1)}, f32[512,1]{1,0:T(8,128)S(1)}) custom-call(bf16[512,256]{1,0:T(8,128)(2,1)S(1)} %collective-permute-done.5.refs_0_.refs_3_, bf16[576,256]{1,0:T(8,128)(2,1)S(1)} %pack.1.refs_1_.refs_2_, bf16[576,256]{1,0:T(8,128)(2,1)S(1)} %collective-permute-done.4.refs_2_.refs_3_, ...), custom_call_target="tpu_custom_call" | custom-call | flops 50331648 | bytes 1024 | tf_op jit(solution)/shard_map/build_tiles/build_tile/pallas_call | solution.py:155
  29.6 0.2 collective-permute-start.9
  29.8 1.3 %build_tile.12 = (bf16[2048,512]{1,0:T(8,128)(2,1)S(1)}, f32[16,2048]{1,0:T(8,128)S(1)}) custom-call(bf16[512,256]{1,0:T(8,128)(2,1)S(1)} %constant_dynamic-slice_fusion.points_ref.refs_0_, bf16[512,256]{1,0:T(8,128)(2,1)S(1)} %collective-permute-done.refs_0_.refs_1_, bf16[512,256]{1,0:T(8,128)(2,1)S(1)} %collective-permute-done.1.refs_1_.refs_2_, ...), custom_call_target="tpu_custom_call" | custom-call | flops 33554432 | bytes 1024 | tf_op jit(solution)/shard_map/build_tiles/build_tile/pallas_call | solution.py:155
  31.1 0.2 collective-permute-done.9.refs_4_
  31.4 1.3 %build_tile.13 = (bf16[2048,512]{1,0:T(8,128)(2,1)S(1)}, f32[16,2048]{1,0:T(8,128)S(1)}) custom-call(bf16[512,256]{1,0:T(8,128)(2,1)S(1)} %constant_dynamic-slice_fusion.points_ref.refs_0_, bf16[512,256]{1,0:T(8,128)(2,1)S(1)} %collective-permute-done.refs_0_.refs_1_, bf16[512,256]{1,0:T(8,128)(2,1)S(1)} %collective-permute-done.1.refs_1_.refs_2_, ...), custom_call_target="tpu_custom_call" | custom-call | flops 33554432 | bytes 1024 | tf_op jit(solution)/shard_map/build_tiles/build_tile/pallas_call | solution.py:155
  32.8 1.1 %collective-permute-start.10 = (bf16[80,512]{1,0:T(8,128)(2,1)S(1)}, bf16[80,512]{1,0:T(8,128)(2,1)S(1)}, u32[]{:S(2)}, u32[]{:S(2)}) collective-permute-start(bf16[80,512]{1,0:T(8,128)(2,1)S(1)} %get-tuple-element.57), channel_id=1, source_target_pairs={{0,32},{8,40},{16,48},{24,56},{32,0},{40,8},{48,16},{56,24},{64,96... | collective-permute-start | bytes 245768 | tf_op jit(solution)/shard_map/sum_over_rows/ppermute | solution.py:29
  33.8 2.5 %collective-permute-start.12 = (bf16[80,512]{1,0:T(8,128)(2,1)S(1)}, bf16[80,512]{1,0:T(8,128)(2,1)S(1)}, u32[]{:S(2)}, u32[]{:S(2)}) collective-permute-start(bf16[80,512]{1,0:T(8,128)(2,1)S(1)} %get-tuple-element.59), channel_id=1, source_target_pairs={{0,40},{8,32},{16,56},{24,48},{32,8},{40,0},{48,24},{56,16},{64,10... | collective-permute-start | bytes 245768 | tf_op jit(solution)/shard_map/sum_over_rows/ppermute | solution.py:29
  36.3 1.2 %collective-permute-done.10.refs_1_ = bf16[80,512]{1,0:T(8,128)(2,1)S(1)} collective-permute-done((bf16[80,512]{1,0:T(8,128)(2,1)S(1)}, bf16[80,512]{1,0:T(8,128)(2,1)S(1)}, u32[]{:S(2)}, u32[]{:S(2)}) %collective-permute-start.10) | collective-permute-done | bytes 81952 | tf_op jit(solution)/shard_map/sum_over_rows/ppermute | solution.py:29
  37.5 2.5 %collective-permute-done.11.refs_2_ = bf16[80,512]{1,0:T(8,128)(2,1)S(1)} collective-permute-done((bf16[80,512]{1,0:T(8,128)(2,1)S(1)}, bf16[80,512]{1,0:T(8,128)(2,1)S(1)}, u32[]{:S(2)}, u32[]{:S(2)}) %collective-permute-start.11) | collective-permute-done | bytes 81952 | tf_op jit(solution)/shard_map/sum_over_rows/ppermute | solution.py:29
  40.0 2.8 %second_product.1 = (f32[16,2048]{1,0:T(8,128)S(1)}, f32[16,2048]{1,0:T(8,128)S(1)}, f32[16,512]{1,0:T(8,128)S(1)}) custom-call(f32[16,2048]{1,0:T(8,128)S(1)} %get-tuple-element.56.image_ref.refs_0_, bf16[80,512]{1,0:T(8,128)(2,1)S(1)} %collective-permute-done.10.refs_1_, bf16[80,512]{1,0:T(8,128)(2,1)S(1)} %collective-permute-done.11.refs_2_, ...), custom_call_target="tpu_custom_call" | custom-call | flops 268435456 | bytes 1024 | tf_op jit(solution)/shard_map/second_product/pallas_call | solution.py:222
  42.8 1.4 %collective-permute-done.13 = f32[16,2048]{1,0:T(8,128)S(1)} collective-permute-done((f32[16,2048]{1,0:T(8,128)S(1)}, f32[16,2048]{1,0:T(8,128)S(1)}, u32[]{:S(2)}, u32[]{:S(2)}) %collective-permute-start.13) | collective-permute-done | bytes 131104 | tf_op jit(solution)/shard_map/sum_over_columns/ppermute | solution.py:48
  44.2 1.8 %collective-permute-start.16 = (f32[16,512]{1,0:T(8,128)S(1)}, f32[16,512]{1,0:T(8,128)S(1)}, u32[]{:S(2)}, u32[]{:S(2)}) collective-permute-start(f32[16,512]{1,0:T(8,128)S(1)} %get-tuple-element.74), channel_id=1, source_target_pairs={{0,120},{8,112},{16,104},{24,96},{32,88},{40,80},{48,72},{56,64},{... | collective-permute-start | bytes 98312 | tf_op jit(solution)/shard_map/sum_over_columns/ppermute | solution.py:29
  45.9 3.0 %collective-permute-start.15 = (f32[16,512]{1,0:T(8,128)S(1)}, f32[16,512]{1,0:T(8,128)S(1)}, u32[]{:S(2)}, u32[]{:S(2)}) collective-permute-start(f32[16,512]{1,0:T(8,128)S(1)} %get-tuple-element.75), channel_id=1, source_target_pairs={{0,24},{8,16},{16,8},{24,0},{32,56},{40,48},{48,40},{56,32},{64,88... | collective-permute-start | bytes 98312 | tf_op jit(solution)/shard_map/sum_over_columns/ppermute | solution.py:29
  48.9 1.3 %collective-permute-start.14 = (f32[16,512]{1,0:T(8,128)S(1)}, f32[16,512]{1,0:T(8,128)S(1)}, u32[]{:S(2)}, u32[]{:S(2)}) collective-permute-start(f32[16,512]{1,0:T(8,128)S(1)} %get-tuple-element.76), channel_id=1, source_target_pairs={{0,96},{8,104},{16,112},{24,120},{32,64},{40,72},{48,80},{56,88},{... | collective-permute-start | bytes 98312 | tf_op jit(solution)/shard_map/sum_over_columns/ppermute | solution.py:29
  50.2 1.3 %collective-permute-done.16.refs_3_ = f32[16,512]{1,0:T(8,128)S(1)} collective-permute-done((f32[16,512]{1,0:T(8,128)S(1)}, f32[16,512]{1,0:T(8,128)S(1)}, u32[]{:S(2)}, u32[]{:S(2)}) %collective-permute-start.16) | collective-permute-done | bytes 32800 | tf_op jit(solution)/shard_map/sum_over_columns/ppermute | solution.py:29
  51.5 2.5 %collective-permute-done.14.refs_1_ = f32[16,512]{1,0:T(8,128)S(1)} collective-permute-done((f32[16,512]{1,0:T(8,128)S(1)}, f32[16,512]{1,0:T(8,128)S(1)}, u32[]{:S(2)}, u32[]{:S(2)}) %collective-permute-start.14) | collective-permute-done | bytes 32800 | tf_op jit(solution)/shard_map/sum_over_columns/ppermute | solution.py:29
  54.2 10.8 %all_to_all.5.sums_ref = f32[32,8,128]{2,1,0:T(8,128)S(1)} all-to-all(f32[32,8,128]{2,1,0:T(8,128)S(1)} %broadcast_in_dim.3), channel_id=1, replica_groups=mesh['y'=4,'z'=4,'c'=2,'x'=4] {'y','z','c'}, dimensions={0} | all-to-all | bytes 262144 | tf_op jit(solution)/shard_map/final_sums/all_to_all | solution.py:342
  65.0 0.9 %finish.1 = (f32[16,512]{1,0:T(8,128)}, f32[16,512]{1,0:T(8,128)}) custom-call(f32[16,512]{1,0:T(8,128)S(1)} %bitcast.10, f32[16,512]{1,0:T(8,128)S(1)} %get-tuple-element.67.rho_ref, f32[16,512]{1,0:T(8,128)S(1)} %get-tuple-element.70.image_ref, f32[32,8,128]{2,1,0:T(8,128)S(1)} %all_to_all.5.sums_ref), custom_call_target="tpu_custom_call" | custom-call | tf_op jit(solution)/shard_map/finish/pallas_call | solution.py:282
  (29 shorter events, 0.8 us)
Async XLA Ops:
  0.6 1.1 %copy-start = (bf16[1024,256]{1,0:T(8,128)(2,1)S(1)}, bf16[1024,256]{1,0:T(8,128)(2,1)}, u32[]{:S(2)}) copy-start(bf16[1024,256]{1,0:T(8,128)(2,1)} %param.3) | copy-start | bytes 1572868
  1.8 0.8 %copy-start.1 = (f32[512,16]{0,1:T(8,128)S(1)}, f32[512,16]{0,1:T(8,128)}, u32[]{:S(2)}) copy-start(f32[512,16]{0,1:T(8,128)} %param.5) | copy-start | bytes 98308
  2.8 7.5 %collective-permute-start.4 = (bf16[576,256]{1,0:T(8,128)(2,1)S(1)}, bf16[576,256]{1,0:T(8,128)(2,1)S(1)}, u32[]{:S(2)}, u32[]{:S(2)}) collective-permute-start(bf16[576,256]{1,0:T(8,128)(2,1)S(1)} %pack.1.refs_1_.refs_2_), channel_id=1, source_target_pairs={{0,4},{4,0},{1,5},{5,1},{2,6},{6,2},{3,7},{7,3},{8,12},{12,8},{9,1... | collective-permute-start | bytes 884744 | tf_op jit(solution)/shard_map/fetch_points/ppermute | solution.py:48
  2.9 15.3 %collective-permute-start.3 = (bf16[576,256]{1,0:T(8,128)(2,1)S(1)}, bf16[576,256]{1,0:T(8,128)(2,1)S(1)}, u32[]{:S(2)}, u32[]{:S(2)}) collective-permute-start(bf16[576,256]{1,0:T(8,128)(2,1)S(1)} %pack.1.refs_1_.refs_2_), channel_id=1, source_target_pairs={{0,24},{8,16},{16,8},{24,0},{32,56},{40,48},{48,40},{56,32},{64,88... | collective-permute-start | bytes 884744 | tf_op jit(solution)/shard_map/fetch_points/ppermute | solution.py:29
  7.1 11.1 %collective-permute-start.2 = (bf16[576,256]{1,0:T(8,128)(2,1)S(1)}, bf16[576,256]{1,0:T(8,128)(2,1)S(1)}, u32[]{:S(2)}, u32[]{:S(2)}) collective-permute-start(bf16[576,256]{1,0:T(8,128)(2,1)S(1)} %pack.1.refs_1_.refs_2_), channel_id=1, source_target_pairs={{0,96},{8,104},{16,112},{24,120},{32,64},{40,72},{48,80},{56,88},{... | collective-permute-start | bytes 884744 | tf_op jit(solution)/shard_map/fetch_points/ppermute | solution.py:29
  10.1 8.1 %collective-permute-start.1 = (bf16[512,256]{1,0:T(8,128)(2,1)S(1)}, bf16[512,256]{1,0:T(8,128)(2,1)S(1)}, u32[]{:S(2)}, u32[]{:S(2)}) collective-permute-start(bf16[512,256]{1,0:T(8,128)(2,1)S(1)} %constant_dynamic-slice_fusion.points_ref.refs_0_), channel_id=1, source_target_pairs={{0,8},{8,0},{16,24},{24,16},{32,40},{40,32},{48,56},{56,48},{64,72... | collective-permute-start | bytes 786440 | tf_op jit(solution)/shard_map/fetch_points/ppermute | solution.py:29
  10.1 8.1 %collective-permute-start = (bf16[512,256]{1,0:T(8,128)(2,1)S(1)}, bf16[512,256]{1,0:T(8,128)(2,1)S(1)}, u32[]{:S(2)}, u32[]{:S(2)}) collective-permute-start(bf16[512,256]{1,0:T(8,128)(2,1)S(1)} %constant_dynamic-slice_fusion.points_ref.refs_0_), channel_id=1, source_target_pairs={{0,32},{8,40},{16,48},{24,56},{32,0},{40,8},{48,16},{56,24},{64,96... | collective-permute-start | bytes 786440 | tf_op jit(solution)/shard_map/fetch_points/ppermute | solution.py:29
  10.3 0.8 %copy-start.2 = (f32[512,16]{0,1:T(8,128)S(1)}, f32[512,16]{0,1:T(8,128)}, u32[]{:S(2)}) copy-start(f32[512,16]{0,1:T(8,128)} %param.5) | copy-start | bytes 98308
  18.2 6.3 %collective-permute-start.6 = (bf16[576,256]{1,0:T(8,128)(2,1)S(1)}, bf16[576,256]{1,0:T(8,128)(2,1)S(1)}, u32[]{:S(2)}, u32[]{:S(2)}) collective-permute-start(bf16[576,256]{1,0:T(8,128)(2,1)S(1)} %collective-permute-done.2.refs_3_), channel_id=1, source_target_pairs={{0,4},{4,0},{1,5},{5,1},{2,6},{6,2},{3,7},{7,3},{8,12},{12,8},{9,1... | collective-permute-start | bytes 884744 | tf_op jit(solution)/shard_map/fetch_points/ppermute | solution.py:48
  18.3 6.2 %collective-permute-start.7 = (bf16[576,256]{1,0:T(8,128)(2,1)S(1)}, bf16[576,256]{1,0:T(8,128)(2,1)S(1)}, u32[]{:S(2)}, u32[]{:S(2)}) collective-permute-start(bf16[576,256]{1,0:T(8,128)(2,1)S(1)} %collective-permute-done.3.refs_4_), channel_id=1, source_target_pairs={{0,4},{4,0},{1,5},{5,1},{2,6},{6,2},{3,7},{7,3},{8,12},{12,8},{9,1... | collective-permute-start | bytes 884744 | tf_op jit(solution)/shard_map/fetch_points/ppermute | solution.py:48
  18.8 10.7 %collective-permute-start.8 = (bf16[576,256]{1,0:T(8,128)(2,1)S(1)}, bf16[576,256]{1,0:T(8,128)(2,1)S(1)}, u32[]{:S(2)}, u32[]{:S(2)}) collective-permute-start(bf16[576,256]{1,0:T(8,128)(2,1)S(1)} %broadcast_select_fusion), channel_id=1, source_target_pairs={{0,96},{4,28},{8,104},{12,20},{16,112},{20,12},{24,120},{28,4},{32... | collective-permute-start | bytes 884744 | tf_op jit(solution)/shard_map/fetch_points/ppermute | solution.py:44
  21.1 6.5 %collective-permute-start.5 = (bf16[512,256]{1,0:T(8,128)(2,1)S(1)}, bf16[512,256]{1,0:T(8,128)(2,1)S(1)}, u32[]{:S(2)}, u32[]{:S(2)}) collective-permute-start(bf16[512,256]{1,0:T(8,128)(2,1)S(1)} %broadcast_select_fusion.1), channel_id=1, source_target_pairs={{0,32},{4,12},{8,40},{12,4},{16,48},{20,28},{24,56},{28,20},{32,0}... | collective-permute-start | bytes 786440 | tf_op jit(solution)/shard_map/fetch_points/ppermute | solution.py:44
  29.6 1.8 %collective-permute-start.9 = (bf16[576,256]{1,0:T(8,128)(2,1)S(1)}, bf16[576,256]{1,0:T(8,128)(2,1)S(1)}, u32[]{:S(2)}, u32[]{:S(2)}) collective-permute-start(bf16[576,256]{1,0:T(8,128)(2,1)S(1)} %collective-permute-done.8.refs_4_), channel_id=1, source_target_pairs={{0,4},{4,0},{1,5},{5,1},{2,6},{6,2},{3,7},{7,3},{8,12},{12,8},{9,1... | collective-permute-start | bytes 884744 | tf_op jit(solution)/shard_map/build_tiles/ppermute | solution.py:48
  32.8 4.7 %collective-permute-start.10 = (bf16[80,512]{1,0:T(8,128)(2,1)S(1)}, bf16[80,512]{1,0:T(8,128)(2,1)S(1)}, u32[]{:S(2)}, u32[]{:S(2)}) collective-permute-start(bf16[80,512]{1,0:T(8,128)(2,1)S(1)} %get-tuple-element.57), channel_id=1, source_target_pairs={{0,32},{8,40},{16,48},{24,56},{32,0},{40,8},{48,16},{56,24},{64,96... | collective-permute-start | bytes 245768 | tf_op jit(solution)/shard_map/sum_over_rows/ppermute | solution.py:29
  33.8 6.2 %collective-permute-start.11 = (bf16[80,512]{1,0:T(8,128)(2,1)S(1)}, bf16[80,512]{1,0:T(8,128)(2,1)S(1)}, u32[]{:S(2)}, u32[]{:S(2)}) collective-permute-start(bf16[80,512]{1,0:T(8,128)(2,1)S(1)} %get-tuple-element.58), channel_id=1, source_target_pairs={{0,8},{8,0},{16,24},{24,16},{32,40},{40,32},{48,56},{56,48},{64,72... | collective-permute-start | bytes 245768 | tf_op jit(solution)/shard_map/sum_over_rows/ppermute | solution.py:29
  33.8 6.2 %collective-permute-start.12 = (bf16[80,512]{1,0:T(8,128)(2,1)S(1)}, bf16[80,512]{1,0:T(8,128)(2,1)S(1)}, u32[]{:S(2)}, u32[]{:S(2)}) collective-permute-start(bf16[80,512]{1,0:T(8,128)(2,1)S(1)} %get-tuple-element.59), channel_id=1, source_target_pairs={{0,40},{8,32},{16,56},{24,48},{32,8},{40,0},{48,24},{56,16},{64,10... | collective-permute-start | bytes 245768 | tf_op jit(solution)/shard_map/sum_over_rows/ppermute | solution.py:29
  40.0 14.0 %copy-start.3 = (f32[512,16]{0,1:T(8,128)S(1)}, f32[512,16]{0,1:T(8,128)}, u32[]{:S(2)}) copy-start(f32[512,16]{0,1:T(8,128)} %param.5) | copy-start | bytes 98308
  42.8 1.4 %collective-permute-start.13 = (f32[16,2048]{1,0:T(8,128)S(1)}, f32[16,2048]{1,0:T(8,128)S(1)}, u32[]{:S(2)}, u32[]{:S(2)}) collective-permute-start(f32[16,2048]{1,0:T(8,128)S(1)} %get-tuple-element.69), channel_id=1, source_target_pairs={{0,4},{4,0},{1,5},{5,1},{2,6},{6,2},{3,7},{7,3},{8,12},{12,8},{9,1... | collective-permute-start | bytes 393224 | tf_op jit(solution)/shard_map/sum_over_columns/ppermute | solution.py:48
  44.2 7.3 %collective-permute-start.16 = (f32[16,512]{1,0:T(8,128)S(1)}, f32[16,512]{1,0:T(8,128)S(1)}, u32[]{:S(2)}, u32[]{:S(2)}) collective-permute-start(f32[16,512]{1,0:T(8,128)S(1)} %get-tuple-element.74), channel_id=1, source_target_pairs={{0,120},{8,112},{16,104},{24,96},{32,88},{40,80},{48,72},{56,64},{... | collective-permute-start | bytes 98312 | tf_op jit(solution)/shard_map/sum_over_columns/ppermute | solution.py:29
  45.9 5.6 %collective-permute-start.15 = (f32[16,512]{1,0:T(8,128)S(1)}, f32[16,512]{1,0:T(8,128)S(1)}, u32[]{:S(2)}, u32[]{:S(2)}) collective-permute-start(f32[16,512]{1,0:T(8,128)S(1)} %get-tuple-element.75), channel_id=1, source_target_pairs={{0,24},{8,16},{16,8},{24,0},{32,56},{40,48},{48,40},{56,32},{64,88... | collective-permute-start | bytes 98312 | tf_op jit(solution)/shard_map/sum_over_columns/ppermute | solution.py:29
  48.9 5.1 %collective-permute-start.14 = (f32[16,512]{1,0:T(8,128)S(1)}, f32[16,512]{1,0:T(8,128)S(1)}, u32[]{:S(2)}, u32[]{:S(2)}) collective-permute-start(f32[16,512]{1,0:T(8,128)S(1)} %get-tuple-element.76), channel_id=1, source_target_pairs={{0,96},{8,104},{16,112},{24,120},{32,64},{40,72},{48,80},{56,88},{... | collective-permute-start | bytes 98312 | tf_op jit(solution)/shard_map/sum_over_columns/ppermute | solution.py:29

commit v12 on v11

--- a/solution.py
+++ b/solution.py
@@ -68,7 +68,7 @@
     row = lax.broadcasted_iota(jnp.int32, norms.shape, 0)
     norms = jnp.where(row == 0, high.astype(jnp.float32), jnp.where(row == 1, middle.astype(jnp.float32), low.astype(jnp.float32)))
     at = own
-    for part in (side_ref[...].astype(jnp.bfloat16), norms.astype(jnp.bfloat16)):
+    for part in (side_ref[...], norms.astype(jnp.bfloat16)):
         for j in range(own // width):
             out_ref[at : at + probes, :] = part[:, j * width : (j + 1) * width]
             at += probes
@@ -184,53 +184,83 @@
     )(image)
 
 
-def second_kernel(own, places, *refs):
-    parts, refs = refs[: len(ROWS)], refs[len(ROWS) :]
-    tiles, (mine_ref, other_ref, rho_ref) = refs[: len(places)], refs[len(places) :]
+def rho_kernel(own, *refs):
+    parts, (rho_ref, narrow_ref) = refs[: len(ROWS)], refs[len(ROWS) :]
     probes = rho_ref.shape[0]
-    pieces = []
-    for p in ROWS:
-        at = ROWS.index(p) * own
+    for j, p in enumerate(ROWS):
+        at = j * own
         piece = parts[0][:, at : at + own]
         for s, part in zip(ROWS[1:], parts[1:]):
             at = ROWS.index((p[0] ^ s[0], p[1] ^ s[1])) * probes
             piece = piece + part[at : at + probes, :].astype(jnp.float32)
             if p == HERE:
                 piece = piece + part[len(ROWS) * probes :, :].astype(jnp.float32)
-        pieces.append(-STEP * piece)
-    rho_ref[...] = pieces[0]
-    rho = jnp.concatenate(pieces, axis=1)
-    high, low, _ = split(rho)
-    narrow = jnp.concatenate([high, low], axis=0)
+        rho = -STEP * piece
+        if p == HERE:
+            rho_ref[...] = rho
+        high, low, _ = split(rho)
+        narrow_ref[:probes, j * own : (j + 1) * own] = high
+        narrow_ref[probes:, j * own : (j + 1) * own] = low
+
+
+def sum_rows(parts, own):
+    probes, rows = parts[0].shape
+    return pl.pallas_call(
+        functools.partial(rho_kernel, own),
+        out_shape=[
+            jax.ShapeDtypeStruct((probes, own), jnp.float32),
+            jax.ShapeDtypeStruct((2 * probes, rows), jnp.bfloat16),
+        ],
+        compiler_params=pltpu.CompilerParams(vmem_limit_bytes=4 << 20),
+        name="sum_rows",
+    )(*parts)
+
+
+def second_kernel(own, half, places, narrow_ref, *refs):
+    tiles, out_ref = refs[: len(places)], refs[len(places)]
+    probes = out_ref.shape[0]
     for j, (h, m) in enumerate(COLS):
+        if h != half:
+            continue
         part = 0.0
         for tile_ref, (top, left) in zip(tiles, places):
             at = j * own - left
             if 0 <= at < tile_ref.shape[1]:
                 part = part + jnp.dot(
-                    narrow[:, top : top + tile_ref.shape[0]],
+                    narrow_ref[:, top : top + tile_ref.shape[0]],
                     tile_ref[:, at : at + own],
                     preferred_element_type=jnp.float32,
                 )
-        (other_ref if h else mine_ref)[:, m * own : (m + 1) * own] = part[:probes] + part[probes:]
-
-
-def second_product(tiles, parts, own):
-    probes, rows = parts[0].shape
-    cols = len(COLS) * own
+        out_ref[:, m * own : (m + 1) * own] = part[:probes] + part[probes:]
+
+
+def second_product(tiles, narrow, own, half):
+    height, rows = narrow.shape
+    cols = len(SQUARE) * own
     places = [(top, left) for _, top, left in tiles]
     return pl.pallas_call(
-        functools.partial(second_kernel, own, places),
-        in_specs=[pl.BlockSpec(memory_space=pltpu.VMEM)] * (len(ROWS) + len(tiles)),
-        out_shape=[
-            jax.ShapeDtypeStruct((probes, cols // NC), jnp.float32),
-            jax.ShapeDtypeStruct((probes, cols // NC), jnp.float32),
-            jax.ShapeDtypeStruct((probes, own), jnp.float32),
-        ],
+        functools.partial(second_kernel, own, half, places),
+        in_specs=[pl.BlockSpec(memory_space=pltpu.VMEM)] * (1 + len(tiles)),
+        out_shape=jax.ShapeDtypeStruct((height // 2, cols), jnp.float32),
         compiler_params=pltpu.CompilerParams(vmem_limit_bytes=8 << 20),
         cost_estimate=pl.CostEstimate(flops=rows * cols * 32, bytes_accessed=1 << 10, transcendentals=0),
         name="second_product",
-    )(*parts, *[tile for tile, _, _ in tiles])
+    )(narrow, *[tile for tile, _, _ in tiles])
+
+
+def merge_kernel(own, mine_ref, other_ref, *out_refs):
+    for m, out_ref in enumerate(out_refs):
+        here = slice(m * own, (m + 1) * own)
+        out_ref[...] = mine_ref[:, here] + other_ref[:, here]
+
+
+def merge(mine, other, own):
+    return pl.pallas_call(
+        functools.partial(merge_kernel, own),
+        out_shape=[jax.ShapeDtypeStruct((mine.shape[0], own), jnp.float32)] * len(SQUARE),
+        compiler_params=pltpu.CompilerParams(vmem_limit_bytes=4 << 20),
+        name="merge",
+    )(mine, other)
 
 
 def sums_kernel(side_ref, rho_ref, *refs):
@@ -292,7 +322,7 @@
     side = right_side.T
     points = lax.dynamic_slice_in_dim(states, offsets[0], own, 0)
     with jax.named_scope("fetch_points"):
-        message = pack(points, side)
+        message = pack(points, side.astype(jnp.bfloat16))
         rows = [points] + [swap(points, offset) for offset in ROWS[1:3]]
         cols = [message] + [swap(message, offset) for offset in SQUARE[1:3]]
         first = [message, swap_core(message)]
@@ -302,11 +332,11 @@
         )
         rows.append(hand_on(rows[1], rows[2], 1))
         cols.append(hand_on(cols[1], cols[2], 3))
-        others = [swap_core(cols[1]), swap_core(cols[2])]
 
     with jax.named_scope("build_tiles"):
         tile_b, image_b, half_b = build(rows[1:3], first, own, probes)
         half = [half_a, half_b]
+        others = [swap_core(cols[1]), swap_core(cols[2])]
         tile_d, image = build(rows[:3], cols[1:3], own, probes, half, [image_a, image_b])
         tile_e, image = build(rows[:3], others, own, probes, half, [image])
         rows[3], image = lax.optimization_barrier((rows[3], image))
@@ -329,12 +359,14 @@
     with jax.named_scope("sum_over_rows"):
         parts = [image] + swap_each(share(image, own), ROWS[1:])
 
-    mine, other, rho = second_product(tiles, parts, own)
+    rho, narrow = sum_rows(parts, own)
+    other = second_product(tiles, narrow, own, 1)
+    narrow, other = lax.optimization_barrier((narrow, other))
+    mine = second_product(tiles, narrow, own, 0)
 
     with jax.named_scope("sum_over_columns"):
-        mine = mine + swap_core(other)
-        blocks = [mine[:, m * own : (m + 1) * own] for m in range(len(SQUARE))]
-        shares = blocks[:1] + swap_each(blocks[1:], SQUARE[1:])
+        blocks = merge(mine, swap_core(other), own)
+        shares = [blocks[0]] + swap_each(blocks[1:], SQUARE[1:])
 
     with jax.named_scope("final_sums"):
         image, sums = local_sums(side, rho, shares)

time: 67.3 us -> 67.6 us (level)
  blocking collectives: 10.8 us -> 13 us
  waiting for transfers between devices: 16.5 us -> 14.9 us
  local copies, waits for them, and re-layouts: 1.95 us -> 0.85 us
  other arithmetic: 0.08 us -> 0.83 us
    all_to_all x1, blocking collectives: 10.8 us -> 13 us  [on_device(): sums = lax.all_to_all(sums, ('y', 'z', 'c'), 0, 0, tiled=True)]
    ppermute x5, waiting for transfers between devices: 1.61 us -> 0.25 us  [swap_core(): return lax.ppermute(value, 'c', [(0, 1), (1, 0)])]
    unnamed x8 -> x6, local copies, waits for them, and re-layouts: 1.86 us -> 0.77 us
    convert_element_type x0 -> x1, other arithmetic: none -> 0.76 us  [on_device(): message = pack(points, side.astype(jnp.bfloat16))]
    pallas_call x1 -> x4, Pallas kernels: 2.78 us -> 2.98 us  [the longest x2 2.9 us: second_product(): pl.pallas_call(functools.partial(second_kernel, own, half, places), in_sp...]
  transfers between devices with their start and end apart: 17 -> 17, of which waited for: 8 -> 7; matrix products, arithmetic and copies ran while one was open for 0% -> 0% of each run, Pallas kernels for 14% -> 17%
where the time goes in v12:
time: 67.6 us; the launch traced here: 66.4 us
  starting transfers between devices  20.1 us (30%)
  Pallas kernels  15.3 us (23%)
  waiting for transfers between devices  14.9 us (22%)
  blocking collectives  13 us (19%)
  between operations  1.45 us (2%)
  local copies, waits for them, and re-layouts  0.85 us (1%)
  other arithmetic  0.83 us (1%)
    ppermute x10, starting transfers between devices, swap(): return lax.ppermute(value, ('y', 'z'), pairs)  16.9 us
    ppermute x10, waiting for transfers between devices, swap(): return lax.ppermute(value, ('y', 'z'), pairs)  13.6 us
    all_to_all x1, blocking collectives, on_device(): sums = lax.all_to_all(sums, ('y', 'z', 'c'), 0, 0, tiled=True)  13 us
    pallas_call x7, Pallas kernels, build(): pl.pallas_call(functools.partial(tile_kernel, counts, probes), out_shape=...  10.9 us
    pallas_call x2, Pallas kernels, second_product(): pl.pallas_call(functools.partial(second_kernel, own, half, places), in_sp...  2.9 us
    ppermute x2, starting transfers between devices, hand_on(): return lax.ppermute(value, ('y', 'z', 'c'), pairs)  2.26 us
  transfers between devices with their start and end apart: 17, of which 7 were waited for; matrix products, arithmetic and copies ran while one was open for 0% of the time, Pallas kernels for 17%

profile of v12, /device:TPU:0, one launch (start us, length us, event | category | flops | bytes accessed | tf_op | source)
XLA Modules:
  0.0 66.4 jit_solution(15494372883107322952)
XLA Ops:
  1.3 0.8 %bitcast_convert_fusion.side_ref = bf16[16,512]{1,0:T(8,128)(2,1)S(1)} fusion(f32[512,16]{0,1:T(8,128)} %param.5), kind=kLoop, calls=%fused_computation.3 | loop fusion | flops 8192 | bytes 49152 | tf_op jit(solution)/shard_map/fetch_points/convert_element_type | solution.py:325
  2.2 0.3 pack.1.refs_1_.refs_2_
  2.6 4.2 %collective-permute-start.3 = (bf16[576,256]{1,0:T(8,128)(2,1)S(1)}, bf16[576,256]{1,0:T(8,128)(2,1)S(1)}, u32[]{:S(2)}, u32[]{:S(2)}) collective-permute-start(bf16[576,256]{1,0:T(8,128)(2,1)S(1)} %pack.1.refs_1_.refs_2_), channel_id=1, source_target_pairs={{0,24},{8,16},{16,8},{24,0},{32,56},{40,48},{48,40},{56,32},{64,88... | collective-permute-start | bytes 884744 | tf_op jit(solution)/shard_map/fetch_points/ppermute | solution.py:29
  6.8 3.0 %collective-permute-start.2 = (bf16[576,256]{1,0:T(8,128)(2,1)S(1)}, bf16[576,256]{1,0:T(8,128)(2,1)S(1)}, u32[]{:S(2)}, u32[]{:S(2)}) collective-permute-start(bf16[576,256]{1,0:T(8,128)(2,1)S(1)} %pack.1.refs_1_.refs_2_), channel_id=1, source_target_pairs={{0,96},{8,104},{16,112},{24,120},{32,64},{40,72},{48,80},{56,88},{... | collective-permute-start | bytes 884744 | tf_op jit(solution)/shard_map/fetch_points/ppermute | solution.py:29
  9.9 0.8 %copy-done.1 = f32[512,16]{0,1:T(8,128)S(1)} copy-done((f32[512,16]{0,1:T(8,128)S(1)}, f32[512,16]{0,1:T(8,128)}, u32[]{:S(2)}) %copy-start.1) | copy-done | bytes 32792
  10.7 0.8 %build_tile.7 = (bf16[512,1024]{1,0:T(8,128)(2,1)S(1)}, f32[16,512]{1,0:T(8,128)S(1)}, f32[512,1]{1,0:T(8,128)S(1)}) custom-call(bf16[512,256]{1,0:T(8,128)(2,1)S(1)} %constant_dynamic-slice_fusion.points_ref.refs_0_, bf16[576,256]{1,0:T(8,128)(2,1)S(1)} %pack.1.refs_1_.refs_2_, bf16[576,256]{1,0:T(8,128)(2,1)S(1)} %collective-permute-done.4.refs_2_.refs_3_, ...), custom_call_target="tpu_custom_call" | custom-call | flops 16777216 | bytes 1024 | tf_op jit(solution)/shard_map/fetch_points/build_tile/pallas_call | solution.py:155
  11.5 6.3 %collective-permute-done.1.refs_1_.refs_2_ = bf16[512,256]{1,0:T(8,128)(2,1)S(1)} collective-permute-done((bf16[512,256]{1,0:T(8,128)(2,1)S(1)}, bf16[512,256]{1,0:T(8,128)(2,1)S(1)}, u32[]{:S(2)}, u32[]{:S(2)}) %collective-permute-start.1) | collective-permute-done | bytes 262176 | tf_op jit(solution)/shard_map/fetch_points/ppermute | solution.py:29
  18.0 0.5 collective-permute-start.7
  18.5 2.2 %collective-permute-start.8 = (bf16[576,256]{1,0:T(8,128)(2,1)S(1)}, bf16[576,256]{1,0:T(8,128)(2,1)S(1)}, u32[]{:S(2)}, u32[]{:S(2)}) collective-permute-start(bf16[576,256]{1,0:T(8,128)(2,1)S(1)} %broadcast_select_fusion), channel_id=1, source_target_pairs={{0,96},{4,28},{8,104},{12,20},{16,112},{20,12},{24,120},{28,4},{32... | collective-permute-start | bytes 884744 | tf_op jit(solution)/shard_map/fetch_points/ppermute | solution.py:44
  20.8 1.4 %build_tile.8 = (bf16[1024,1024]{1,0:T(8,128)(2,1)S(1)}, f32[16,1024]{1,0:T(8,128)S(1)}, f32[1024,1]{1,0:T(8,128)S(1)}) custom-call(bf16[512,256]{1,0:T(8,128)(2,1)S(1)} %collective-permute-done.refs_0_.refs_1_, bf16[512,256]{1,0:T(8,128)(2,1)S(1)} %collective-permute-done.1.refs_1_.refs_2_, bf16[576,256]{1,0:T(8,128)(2,1)S(1)} %pack.1.refs_1_.refs_2_, ...), custom_call_target="tpu_custom_call" | custom-call | flops 33554432 | bytes 1024 | tf_op jit(solution)/shard_map/build_tiles/build_tile/pallas_call | solution.py:155
  22.2 1.9 %build_tile.9 = (bf16[1536,1024]{1,0:T(8,128)(2,1)S(1)}, f32[16,1536]{1,0:T(8,128)S(1)}) custom-call(bf16[512,256]{1,0:T(8,128)(2,1)S(1)} %constant_dynamic-slice_fusion.points_ref.refs_0_, bf16[512,256]{1,0:T(8,128)(2,1)S(1)} %collective-permute-done.refs_0_.refs_1_, bf16[512,256]{1,0:T(8,128)(2,1)S(1)} %collective-permute-done.1.refs_1_.refs_2_, ...), custom_call_target="tpu_custom_call" | custom-call | flops 50331648 | bytes 1024 | tf_op jit(solution)/shard_map/build_tiles/build_tile/pallas_call | solution.py:155
  24.2 1.9 %build_tile.10 = (bf16[1536,1024]{1,0:T(8,128)(2,1)S(1)}, f32[16,1536]{1,0:T(8,128)S(1)}) custom-call(bf16[512,256]{1,0:T(8,128)(2,1)S(1)} %constant_dynamic-slice_fusion.points_ref.refs_0_, bf16[512,256]{1,0:T(8,128)(2,1)S(1)} %collective-permute-done.refs_0_.refs_1_, bf16[512,256]{1,0:T(8,128)(2,1)S(1)} %collective-permute-done.1.refs_1_.refs_2_, ...), custom_call_target="tpu_custom_call" | custom-call | flops 50331648 | bytes 1024 | tf_op jit(solution)/shard_map/build_tiles/build_tile/pallas_call | solution.py:155
  26.1 1.0 %collective-permute-done.5.refs_0_.refs_3_ = bf16[512,256]{1,0:T(8,128)(2,1)S(1)} collective-permute-done((bf16[512,256]{1,0:T(8,128)(2,1)S(1)}, bf16[512,256]{1,0:T(8,128)(2,1)S(1)}, u32[]{:S(2)}, u32[]{:S(2)}) %collective-permute-start.5) | collective-permute-done | bytes 262176 | tf_op jit(solution)/shard_map/fetch_points/ppermute | solution.py:44
  27.2 2.1 %build_tile.11 = (bf16[512,3072]{1,0:T(8,128)(2,1)S(1)}, f32[16,512]{1,0:T(8,128)S(1)}, f32[512,1]{1,0:T(8,128)S(1)}) custom-call(bf16[512,256]{1,0:T(8,128)(2,1)S(1)} %collective-permute-done.5.refs_0_.refs_3_, bf16[576,256]{1,0:T(8,128)(2,1)S(1)} %pack.1.refs_1_.refs_2_, bf16[576,256]{1,0:T(8,128)(2,1)S(1)} %collective-permute-done.4.refs_2_.refs_3_, ...), custom_call_target="tpu_custom_call" | custom-call | flops 50331648 | bytes 1024 | tf_op jit(solution)/shard_map/build_tiles/build_tile/pallas_call | solution.py:155
  29.2 0.2 collective-permute-start.9
  29.4 1.3 %build_tile.12 = (bf16[2048,512]{1,0:T(8,128)(2,1)S(1)}, f32[16,2048]{1,0:T(8,128)S(1)}) custom-call(bf16[512,256]{1,0:T(8,128)(2,1)S(1)} %constant_dynamic-slice_fusion.points_ref.refs_0_, bf16[512,256]{1,0:T(8,128)(2,1)S(1)} %collective-permute-done.refs_0_.refs_1_, bf16[512,256]{1,0:T(8,128)(2,1)S(1)} %collective-permute-done.1.refs_1_.refs_2_, ...), custom_call_target="tpu_custom_call" | custom-call | flops 33554432 | bytes 1024 | tf_op jit(solution)/shard_map/build_tiles/build_tile/pallas_call | solution.py:155
  30.8 0.2 collective-permute-done.9.refs_4_
  31.0 1.3 %build_tile.13 = (bf16[2048,512]{1,0:T(8,128)(2,1)S(1)}, f32[16,2048]{1,0:T(8,128)S(1)}) custom-call(bf16[512,256]{1,0:T(8,128)(2,1)S(1)} %constant_dynamic-slice_fusion.points_ref.refs_0_, bf16[512,256]{1,0:T(8,128)(2,1)S(1)} %collective-permute-done.refs_0_.refs_1_, bf16[512,256]{1,0:T(8,128)(2,1)S(1)} %collective-permute-done.1.refs_1_.refs_2_, ...), custom_call_target="tpu_custom_call" | custom-call | flops 33554432 | bytes 1024 | tf_op jit(solution)/shard_map/build_tiles/build_tile/pallas_call | solution.py:155
  32.4 1.1 %collective-permute-start.10 = (bf16[80,512]{1,0:T(8,128)(2,1)S(1)}, bf16[80,512]{1,0:T(8,128)(2,1)S(1)}, u32[]{:S(2)}, u32[]{:S(2)}) collective-permute-start(bf16[80,512]{1,0:T(8,128)(2,1)S(1)} %get-tuple-element.62), channel_id=1, source_target_pairs={{0,32},{8,40},{16,48},{24,56},{32,0},{40,8},{48,16},{56,24},{64,96... | collective-permute-start | bytes 245768 | tf_op jit(solution)/shard_map/sum_over_rows/ppermute | solution.py:29
  33.5 2.5 %collective-permute-start.12 = (bf16[80,512]{1,0:T(8,128)(2,1)S(1)}, bf16[80,512]{1,0:T(8,128)(2,1)S(1)}, u32[]{:S(2)}, u32[]{:S(2)}) collective-permute-start(bf16[80,512]{1,0:T(8,128)(2,1)S(1)} %get-tuple-element.64), channel_id=1, source_target_pairs={{0,40},{8,32},{16,56},{24,48},{32,8},{40,0},{48,24},{56,16},{64,10... | collective-permute-start | bytes 245768 | tf_op jit(solution)/shard_map/sum_over_rows/ppermute | solution.py:29
  36.0 1.2 %collective-permute-done.10.refs_1_ = bf16[80,512]{1,0:T(8,128)(2,1)S(1)} collective-permute-done((bf16[80,512]{1,0:T(8,128)(2,1)S(1)}, bf16[80,512]{1,0:T(8,128)(2,1)S(1)}, u32[]{:S(2)}, u32[]{:S(2)}) %collective-permute-start.10) | collective-permute-done | bytes 81952 | tf_op jit(solution)/shard_map/sum_over_rows/ppermute | solution.py:29
  37.2 2.5 %collective-permute-done.11.refs_2_ = bf16[80,512]{1,0:T(8,128)(2,1)S(1)} collective-permute-done((bf16[80,512]{1,0:T(8,128)(2,1)S(1)}, bf16[80,512]{1,0:T(8,128)(2,1)S(1)}, u32[]{:S(2)}, u32[]{:S(2)}) %collective-permute-start.11) | collective-permute-done | bytes 81952 | tf_op jit(solution)/shard_map/sum_over_rows/ppermute | solution.py:29
  39.7 1.4 %second_product.2 = f32[16,2048]{1,0:T(8,128)S(1)} custom-call(bf16[32,2048]{1,0:T(8,128)(2,1)S(1)} %get-tuple-element.74.narrow_ref, bf16[512,1024]{1,0:T(8,128)(2,1)S(1)} %get-tuple-element.67.refs_0_, bf16[1024,1024]{1,0:T(8,128)(2,1)S(1)} %get-tuple-element.68.refs_1_, bf16[1536,1024]{1,0:T(8,128)(2,1)S(1)} %get-tuple-element.69.refs_2_, ...), custom_call_target="tpu_custom_call" | custom-call | flops 134217728 | bytes 1024 | tf_op jit(solution)/shard_map/second_product/pallas_call | solution.py:241
  41.2 1.5 %second_product.3.mine_ref = f32[16,2048]{1,0:T(8,128)S(1)} custom-call(bf16[32,2048]{1,0:T(8,128)(2,1)S(1)} %get-tuple-element.74.narrow_ref, bf16[512,1024]{1,0:T(8,128)(2,1)S(1)} %get-tuple-element.67.refs_0_, bf16[1024,1024]{1,0:T(8,128)(2,1)S(1)} %get-tuple-element.68.refs_1_, bf16[1536,1024]{1,0:T(8,128)(2,1)S(1)} %get-tuple-element.69.refs_2_, ...), custom_call_target="tpu_custom_call" | custom-call | flops 134217728 | bytes 1024 | tf_op jit(solution)/shard_map/second_product/pallas_call | solution.py:241
  42.7 2.1 %collective-permute-start.14 = (f32[16,512]{1,0:T(8,128)S(1)}, f32[16,512]{1,0:T(8,128)S(1)}, u32[]{:S(2)}, u32[]{:S(2)}) collective-permute-start(f32[16,512]{1,0:T(8,128)S(1)} %get-tuple-element.77), channel_id=1, source_target_pairs={{0,96},{8,104},{16,112},{24,120},{32,64},{40,72},{48,80},{56,88},{... | collective-permute-start | bytes 98312 | tf_op jit(solution)/shard_map/sum_over_columns/ppermute | solution.py:29
  44.7 0.3 collective-permute-start.15
  45.0 3.7 %collective-permute-start.16 = (f32[16,512]{1,0:T(8,128)S(1)}, f32[16,512]{1,0:T(8,128)S(1)}, u32[]{:S(2)}, u32[]{:S(2)}) collective-permute-start(f32[16,512]{1,0:T(8,128)S(1)} %get-tuple-element.79), channel_id=1, source_target_pairs={{0,120},{8,112},{16,104},{24,96},{32,88},{40,80},{48,72},{56,64},{... | collective-permute-start | bytes 98312 | tf_op jit(solution)/shard_map/sum_over_columns/ppermute | solution.py:29
  48.7 1.2 %collective-permute-done.15.refs_2_ = f32[16,512]{1,0:T(8,128)S(1)} collective-permute-done((f32[16,512]{1,0:T(8,128)S(1)}, f32[16,512]{1,0:T(8,128)S(1)}, u32[]{:S(2)}, u32[]{:S(2)}) %collective-permute-start.15) | collective-permute-done | bytes 32800 | tf_op jit(solution)/shard_map/sum_over_columns/ppermute | solution.py:29
  49.9 2.4 %collective-permute-done.16.refs_3_ = f32[16,512]{1,0:T(8,128)S(1)} collective-permute-done((f32[16,512]{1,0:T(8,128)S(1)}, f32[16,512]{1,0:T(8,128)S(1)}, u32[]{:S(2)}, u32[]{:S(2)}) %collective-permute-start.16) | collective-permute-done | bytes 32800 | tf_op jit(solution)/shard_map/sum_over_columns/ppermute | solution.py:29
  52.2 0.2 local_sums.1
  52.4 13.0 %all_to_all.5.sums_ref = f32[32,8,128]{2,1,0:T(8,128)S(1)} all-to-all(f32[32,8,128]{2,1,0:T(8,128)S(1)} %broadcast_in_dim.3), channel_id=1, replica_groups=mesh['y'=4,'z'=4,'c'=2,'x'=4] {'y','z','c'}, dimensions={0} | all-to-all | bytes 262144 | tf_op jit(solution)/shard_map/final_sums/all_to_all | solution.py:374
  65.4 0.9 %finish.1 = (f32[16,512]{1,0:T(8,128)}, f32[16,512]{1,0:T(8,128)}) custom-call(f32[16,512]{1,0:T(8,128)S(1)} %bitcast.10, f32[16,512]{1,0:T(8,128)S(1)} %get-tuple-element.65.rho_ref, f32[16,512]{1,0:T(8,128)S(1)} %get-tuple-element.80.image_ref, f32[32,8,128]{2,1,0:T(8,128)S(1)} %all_to_all.5.sums_ref), custom_call_target="tpu_custom_call" | custom-call | tf_op jit(solution)/shard_map/finish/pallas_call | solution.py:312
  (29 shorter events, 0.7 us)
Async XLA Ops:
  0.6 1.5 %copy-start = (bf16[1024,256]{1,0:T(8,128)(2,1)S(1)}, bf16[1024,256]{1,0:T(8,128)(2,1)}, u32[]{:S(2)}) copy-start(bf16[1024,256]{1,0:T(8,128)(2,1)} %param.3) | copy-start | bytes 1572868
  2.5 7.5 %collective-permute-start.4 = (bf16[576,256]{1,0:T(8,128)(2,1)S(1)}, bf16[576,256]{1,0:T(8,128)(2,1)S(1)}, u32[]{:S(2)}, u32[]{:S(2)}) collective-permute-start(bf16[576,256]{1,0:T(8,128)(2,1)S(1)} %pack.1.refs_1_.refs_2_), channel_id=1, source_target_pairs={{0,4},{4,0},{1,5},{5,1},{2,6},{6,2},{3,7},{7,3},{8,12},{12,8},{9,1... | collective-permute-start | bytes 884744 | tf_op jit(solution)/shard_map/fetch_points/ppermute | solution.py:48
  2.6 15.3 %collective-permute-start.3 = (bf16[576,256]{1,0:T(8,128)(2,1)S(1)}, bf16[576,256]{1,0:T(8,128)(2,1)S(1)}, u32[]{:S(2)}, u32[]{:S(2)}) collective-permute-start(bf16[576,256]{1,0:T(8,128)(2,1)S(1)} %pack.1.refs_1_.refs_2_), channel_id=1, source_target_pairs={{0,24},{8,16},{16,8},{24,0},{32,56},{40,48},{48,40},{56,32},{64,88... | collective-permute-start | bytes 884744 | tf_op jit(solution)/shard_map/fetch_points/ppermute | solution.py:29
  6.8 11.1 %collective-permute-start.2 = (bf16[576,256]{1,0:T(8,128)(2,1)S(1)}, bf16[576,256]{1,0:T(8,128)(2,1)S(1)}, u32[]{:S(2)}, u32[]{:S(2)}) collective-permute-start(bf16[576,256]{1,0:T(8,128)(2,1)S(1)} %pack.1.refs_1_.refs_2_), channel_id=1, source_target_pairs={{0,96},{8,104},{16,112},{24,120},{32,64},{40,72},{48,80},{56,88},{... | collective-permute-start | bytes 884744 | tf_op jit(solution)/shard_map/fetch_points/ppermute | solution.py:29
  9.8 8.1 %collective-permute-start.1 = (bf16[512,256]{1,0:T(8,128)(2,1)S(1)}, bf16[512,256]{1,0:T(8,128)(2,1)S(1)}, u32[]{:S(2)}, u32[]{:S(2)}) collective-permute-start(bf16[512,256]{1,0:T(8,128)(2,1)S(1)} %constant_dynamic-slice_fusion.points_ref.refs_0_), channel_id=1, source_target_pairs={{0,8},{8,0},{16,24},{24,16},{32,40},{40,32},{48,56},{56,48},{64,72... | collective-permute-start | bytes 786440 | tf_op jit(solution)/shard_map/fetch_points/ppermute | solution.py:29
  9.8 8.1 %collective-permute-start = (bf16[512,256]{1,0:T(8,128)(2,1)S(1)}, bf16[512,256]{1,0:T(8,128)(2,1)S(1)}, u32[]{:S(2)}, u32[]{:S(2)}) collective-permute-start(bf16[512,256]{1,0:T(8,128)(2,1)S(1)} %constant_dynamic-slice_fusion.points_ref.refs_0_), channel_id=1, source_target_pairs={{0,32},{8,40},{16,48},{24,56},{32,0},{40,8},{48,16},{56,24},{64,96... | collective-permute-start | bytes 786440 | tf_op jit(solution)/shard_map/fetch_points/ppermute | solution.py:29
  9.9 0.8 %copy-start.1 = (f32[512,16]{0,1:T(8,128)S(1)}, f32[512,16]{0,1:T(8,128)}, u32[]{:S(2)}) copy-start(f32[512,16]{0,1:T(8,128)} %param.5) | copy-start | bytes 98308
  17.9 6.3 %collective-permute-start.6 = (bf16[576,256]{1,0:T(8,128)(2,1)S(1)}, bf16[576,256]{1,0:T(8,128)(2,1)S(1)}, u32[]{:S(2)}, u32[]{:S(2)}) collective-permute-start(bf16[576,256]{1,0:T(8,128)(2,1)S(1)} %collective-permute-done.2.refs_3_), channel_id=1, source_target_pairs={{0,4},{4,0},{1,5},{5,1},{2,6},{6,2},{3,7},{7,3},{8,12},{12,8},{9,1... | collective-permute-start | bytes 884744 | tf_op jit(solution)/shard_map/build_tiles/ppermute | solution.py:48
  18.0 6.2 %collective-permute-start.7 = (bf16[576,256]{1,0:T(8,128)(2,1)S(1)}, bf16[576,256]{1,0:T(8,128)(2,1)S(1)}, u32[]{:S(2)}, u32[]{:S(2)}) collective-permute-start(bf16[576,256]{1,0:T(8,128)(2,1)S(1)} %collective-permute-done.3.refs_4_), channel_id=1, source_target_pairs={{0,4},{4,0},{1,5},{5,1},{2,6},{6,2},{3,7},{7,3},{8,12},{12,8},{9,1... | collective-permute-start | bytes 884744 | tf_op jit(solution)/shard_map/build_tiles/ppermute | solution.py:48
  18.5 10.7 %collective-permute-start.8 = (bf16[576,256]{1,0:T(8,128)(2,1)S(1)}, bf16[576,256]{1,0:T(8,128)(2,1)S(1)}, u32[]{:S(2)}, u32[]{:S(2)}) collective-permute-start(bf16[576,256]{1,0:T(8,128)(2,1)S(1)} %broadcast_select_fusion), channel_id=1, source_target_pairs={{0,96},{4,28},{8,104},{12,20},{16,112},{20,12},{24,120},{28,4},{32... | collective-permute-start | bytes 884744 | tf_op jit(solution)/shard_map/fetch_points/ppermute | solution.py:44
  20.7 6.5 %collective-permute-start.5 = (bf16[512,256]{1,0:T(8,128)(2,1)S(1)}, bf16[512,256]{1,0:T(8,128)(2,1)S(1)}, u32[]{:S(2)}, u32[]{:S(2)}) collective-permute-start(bf16[512,256]{1,0:T(8,128)(2,1)S(1)} %broadcast_select_fusion.1), channel_id=1, source_target_pairs={{0,32},{4,12},{8,40},{12,4},{16,48},{20,28},{24,56},{28,20},{32,0}... | collective-permute-start | bytes 786440 | tf_op jit(solution)/shard_map/fetch_points/ppermute | solution.py:44
  29.2 1.8 %collective-permute-start.9 = (bf16[576,256]{1,0:T(8,128)(2,1)S(1)}, bf16[576,256]{1,0:T(8,128)(2,1)S(1)}, u32[]{:S(2)}, u32[]{:S(2)}) collective-permute-start(bf16[576,256]{1,0:T(8,128)(2,1)S(1)} %collective-permute-done.8.refs_4_), channel_id=1, source_target_pairs={{0,4},{4,0},{1,5},{5,1},{2,6},{6,2},{3,7},{7,3},{8,12},{12,8},{9,1... | collective-permute-start | bytes 884744 | tf_op jit(solution)/shard_map/build_tiles/ppermute | solution.py:48
  32.4 4.7 %collective-permute-start.10 = (bf16[80,512]{1,0:T(8,128)(2,1)S(1)}, bf16[80,512]{1,0:T(8,128)(2,1)S(1)}, u32[]{:S(2)}, u32[]{:S(2)}) collective-permute-start(bf16[80,512]{1,0:T(8,128)(2,1)S(1)} %get-tuple-element.62), channel_id=1, source_target_pairs={{0,32},{8,40},{16,48},{24,56},{32,0},{40,8},{48,16},{56,24},{64,96... | collective-permute-start | bytes 245768 | tf_op jit(solution)/shard_map/sum_over_rows/ppermute | solution.py:29
  33.5 6.2 %collective-permute-start.11 = (bf16[80,512]{1,0:T(8,128)(2,1)S(1)}, bf16[80,512]{1,0:T(8,128)(2,1)S(1)}, u32[]{:S(2)}, u32[]{:S(2)}) collective-permute-start(bf16[80,512]{1,0:T(8,128)(2,1)S(1)} %get-tuple-element.63), channel_id=1, source_target_pairs={{0,8},{8,0},{16,24},{24,16},{32,40},{40,32},{48,56},{56,48},{64,72... | collective-permute-start | bytes 245768 | tf_op jit(solution)/shard_map/sum_over_rows/ppermute | solution.py:29
  33.5 6.2 %collective-permute-start.12 = (bf16[80,512]{1,0:T(8,128)(2,1)S(1)}, bf16[80,512]{1,0:T(8,128)(2,1)S(1)}, u32[]{:S(2)}, u32[]{:S(2)}) collective-permute-start(bf16[80,512]{1,0:T(8,128)(2,1)S(1)} %get-tuple-element.64), channel_id=1, source_target_pairs={{0,40},{8,32},{16,56},{24,48},{32,8},{40,0},{48,24},{56,16},{64,10... | collective-permute-start | bytes 245768 | tf_op jit(solution)/shard_map/sum_over_rows/ppermute | solution.py:29
  41.2 11.1 %copy-start.2 = (f32[512,16]{0,1:T(8,128)S(1)}, f32[512,16]{0,1:T(8,128)}, u32[]{:S(2)}) copy-start(f32[512,16]{0,1:T(8,128)} %param.5) | copy-start | bytes 98308
  41.2 1.5 %collective-permute-start.13 = (f32[16,2048]{1,0:T(8,128)S(1)}, f32[16,2048]{1,0:T(8,128)S(1)}, u32[]{:S(2)}, u32[]{:S(2)}) collective-permute-start(f32[16,2048]{1,0:T(8,128)S(1)} %second_product.2), channel_id=1, source_target_pairs={{0,4},{4,0},{1,5},{5,1},{2,6},{6,2},{3,7},{7,3},{8,12},{12,8},{9,1... | collective-permute-start | bytes 393224 | tf_op jit(solution)/shard_map/sum_over_columns/ppermute | solution.py:48
  42.7 6.0 %collective-permute-start.14 = (f32[16,512]{1,0:T(8,128)S(1)}, f32[16,512]{1,0:T(8,128)S(1)}, u32[]{:S(2)}, u32[]{:S(2)}) collective-permute-start(f32[16,512]{1,0:T(8,128)S(1)} %get-tuple-element.77), channel_id=1, source_target_pairs={{0,96},{8,104},{16,112},{24,120},{32,64},{40,72},{48,80},{56,88},{... | collective-permute-start | bytes 98312 | tf_op jit(solution)/shard_map/sum_over_columns/ppermute | solution.py:29
  44.7 5.1 %collective-permute-start.15 = (f32[16,512]{1,0:T(8,128)S(1)}, f32[16,512]{1,0:T(8,128)S(1)}, u32[]{:S(2)}, u32[]{:S(2)}) collective-permute-start(f32[16,512]{1,0:T(8,128)S(1)} %get-tuple-element.78), channel_id=1, source_target_pairs={{0,24},{8,16},{16,8},{24,0},{32,56},{40,48},{48,40},{56,32},{64,88... | collective-permute-start | bytes 98312 | tf_op jit(solution)/shard_map/sum_over_columns/ppermute | solution.py:29
  45.0 7.2 %collective-permute-start.16 = (f32[16,512]{1,0:T(8,128)S(1)}, f32[16,512]{1,0:T(8,128)S(1)}, u32[]{:S(2)}, u32[]{:S(2)}) collective-permute-start(f32[16,512]{1,0:T(8,128)S(1)} %get-tuple-element.79), channel_id=1, source_target_pairs={{0,120},{8,112},{16,104},{24,96},{32,88},{40,80},{48,72},{56,64},{... | collective-permute-start | bytes 98312 | tf_op jit(solution)/shard_map/sum_over_columns/ppermute | solution.py:29

commit v13 on v12

--- a/solution.py
+++ b/solution.py
@@ -34,13 +34,13 @@
     return received[::-1]
 
 
-def hand_on(along_y, along_z, step):
+def hand_on(along_y, along_z, offset):
     value = jnp.where(lax.axis_index("c") == 0, along_z, along_y)
     pairs = []
     for y in range(NY):
         for z in range(NZ):
             here = (y * NZ + z) * NC
-            pairs += [(here, ((y ^ step) * NZ + z) * NC), (here + 1, (y * NZ + (z ^ step)) * NC + 1)]
+            pairs += [(here, ((y ^ offset[0]) * NZ + z) * NC), (here + 1, (y * NZ + (z ^ offset[1])) * NC + 1)]
     return lax.ppermute(value, ("y", "z", "c"), pairs)
 
 
@@ -275,7 +275,8 @@
     sums = 0.0
     for k, one in enumerate((total(side, side), total(side, rho), total(rho, rho), total(rho, image))):
         sums = jnp.where(lane == k, one, sums)
-    sums_ref[...] = jnp.pad(sums.T[:8], ((0, 0), (0, LANES - side.shape[0])))
+    sums = sums.T
+    sums_ref[...] = jnp.concatenate([sums[k : k + 1] for k in range(LANES // sums.shape[1])], axis=1)
 
 
 def local_sums(side, rho, shares):
@@ -283,7 +284,7 @@
         sums_kernel,
         out_shape=[
             jax.ShapeDtypeStruct(side.shape, jnp.float32),
-            jax.ShapeDtypeStruct((8, LANES), jnp.float32),
+            jax.ShapeDtypeStruct((1, LANES), jnp.float32),
         ],
         compiler_params=pltpu.CompilerParams(vmem_limit_bytes=4 << 20),
         name="local_sums",
@@ -292,7 +293,9 @@
 
 def finish_kernel(side_ref, rho_ref, image_ref, sums_ref, field_ref, residual_ref):
     side, rho, image = side_ref[...], rho_ref[...], image_ref[...]
-    sums = jnp.sum(sums_ref[...], axis=0).T[: side.shape[0]]
+    probes = side.shape[0]
+    sums = jnp.sum(sums_ref[...], axis=0, keepdims=True)
+    sums = jnp.concatenate([sums[:, k * probes : (k + 1) * probes] for k in range(4)] * 2, axis=0).T
     rr, side_rho, rho_rho, rho_image = (sums[:, k : k + 1] for k in range(4))
     curve = (rr - side_rho) / STEP
     alpha = rr / curve
@@ -327,14 +330,14 @@
         cols = [message] + [swap(message, offset) for offset in SQUARE[1:3]]
         first = [message, swap_core(message)]
         tile_a, image_a, half_a = build([points], first, own, probes, side=side)
-        (rows[1], rows[2], cols[1], cols[2]), image_a = lax.optimization_barrier(
-            ((rows[1], rows[2], cols[1], cols[2]), image_a)
+        tile_b, image_b, half_b = build(rows[1:3], first, own, probes)
+        (rows[1], rows[2], cols[1], cols[2]), image_a, image_b = lax.optimization_barrier(
+            ((rows[1], rows[2], cols[1], cols[2]), image_a, image_b)
         )
-        rows.append(hand_on(rows[1], rows[2], 1))
-        cols.append(hand_on(cols[1], cols[2], 3))
+        cols.append(hand_on(cols[1], cols[2], SQUARE[3]))
+        rows.append(hand_on(rows[1], rows[2], ROWS[3]))
 
     with jax.named_scope("build_tiles"):
-        tile_b, image_b, half_b = build(rows[1:3], first, own, probes)
         half = [half_a, half_b]
         others = [swap_core(cols[1]), swap_core(cols[2])]
         tile_d, image = build(rows[:3], cols[1:3], own, probes, half, [image_a, image_b])
@@ -370,7 +373,7 @@
 
     with jax.named_scope("final_sums"):
         image, sums = local_sums(side, rho, shares)
-        sums = jnp.broadcast_to(sums, (NY * NZ * NC, 8, LANES))
+        sums = jnp.broadcast_to(sums, (NY * NZ * NC, LANES))
         sums = lax.all_to_all(sums, ("y", "z", "c"), 0, 0, tiled=True)
 
     field, residual = finish(side, rho, image, sums)

time: 67.6 us -> 67.4 us (level)
  waiting for transfers between devices: 14.9 us -> 17.4 us
  starting transfers between devices: 20.1 us -> 18.6 us
  blocking collectives: 13 us -> 11.8 us
    ppermute x2, starting transfers between devices: 2.26 us -> 0.82 us  [hand_on(): return lax.ppermute(value, ('y', 'z', 'c'), pairs)]
    ppermute x2, waiting for transfers between devices: 1.05 us -> 2.49 us  [hand_on(): return lax.ppermute(value, ('y', 'z', 'c'), pairs)]
    all_to_all x1, blocking collectives: 13 us -> 11.8 us  [on_device(): sums = lax.all_to_all(sums, ('y', 'z', 'c'), 0, 0, tiled=True)]
    ppermute x10, waiting for transfers between devices: 13.6 us -> 14.6 us  [swap(): return lax.ppermute(value, ('y', 'z'), pairs)]
where the time goes in v13:
time: 67.4 us; the launch traced here: 66.3 us
  starting transfers between devices  18.6 us (28%)
  waiting for transfers between devices  17.4 us (26%)
  Pallas kernels  15.4 us (23%)
  blocking collectives  11.8 us (18%)
  between operations  1.47 us (2%)
  local copies, waits for them, and re-layouts  0.85 us (1%)
  other arithmetic  0.83 us (1%)
    ppermute x10, starting transfers between devices, swap(): return lax.ppermute(value, ('y', 'z'), pairs)  16.9 us
    ppermute x10, waiting for transfers between devices, swap(): return lax.ppermute(value, ('y', 'z'), pairs)  14.6 us
    all_to_all x1, blocking collectives, on_device(): sums = lax.all_to_all(sums, ('y', 'z', 'c'), 0, 0, tiled=True)  11.8 us
    pallas_call x7, Pallas kernels, build(): pl.pallas_call(functools.partial(tile_kernel, counts, probes), out_shape=...  10.9 us
    pallas_call x2, Pallas kernels, second_product(): pl.pallas_call(functools.partial(second_kernel, own, half, places), in_sp...  2.9 us
    ppermute x2, waiting for transfers between devices, hand_on(): return lax.ppermute(value, ('y', 'z', 'c'), pairs)  2.49 us
  transfers between devices with their start and end apart: 17, of which 7 were waited for; matrix products, arithmetic and copies ran while one was open for 0% of the time, Pallas kernels for 17%

profile of v13, /device:TPU:0, one launch (start us, length us, event | category | flops | bytes accessed | tf_op | source)
XLA Modules:
  0.0 66.3 jit_solution(10966897950414530665)
XLA Ops:
  1.3 0.8 %bitcast_convert_fusion.side_ref = bf16[16,512]{1,0:T(8,128)(2,1)S(1)} fusion(f32[512,16]{0,1:T(8,128)} %param.5), kind=kLoop, calls=%fused_computation.3 | loop fusion | flops 8192 | bytes 49152 | tf_op jit(solution)/shard_map/fetch_points/convert_element_type | solution.py:328
  2.2 0.3 pack.1.refs_1_.refs_2_
  2.6 4.2 %collective-permute-start.3 = (bf16[576,256]{1,0:T(8,128)(2,1)S(1)}, bf16[576,256]{1,0:T(8,128)(2,1)S(1)}, u32[]{:S(2)}, u32[]{:S(2)}) collective-permute-start(bf16[576,256]{1,0:T(8,128)(2,1)S(1)} %pack.1.refs_1_.refs_2_), channel_id=1, source_target_pairs={{0,24},{8,16},{16,8},{24,0},{32,56},{40,48},{48,40},{56,32},{64,88... | collective-permute-start | bytes 884744 | tf_op jit(solution)/shard_map/fetch_points/ppermute | solution.py:29
  6.8 3.0 %collective-permute-start.2 = (bf16[576,256]{1,0:T(8,128)(2,1)S(1)}, bf16[576,256]{1,0:T(8,128)(2,1)S(1)}, u32[]{:S(2)}, u32[]{:S(2)}) collective-permute-start(bf16[576,256]{1,0:T(8,128)(2,1)S(1)} %pack.1.refs_1_.refs_2_), channel_id=1, source_target_pairs={{0,96},{8,104},{16,112},{24,120},{32,64},{40,72},{48,80},{56,88},{... | collective-permute-start | bytes 884744 | tf_op jit(solution)/shard_map/fetch_points/ppermute | solution.py:29
  9.9 0.8 %copy-done.1 = f32[512,16]{0,1:T(8,128)S(1)} copy-done((f32[512,16]{0,1:T(8,128)S(1)}, f32[512,16]{0,1:T(8,128)}, u32[]{:S(2)}) %copy-start.1) | copy-done | bytes 32792
  10.7 0.8 %build_tile.7 = (bf16[512,1024]{1,0:T(8,128)(2,1)S(1)}, f32[16,512]{1,0:T(8,128)S(1)}, f32[512,1]{1,0:T(8,128)S(1)}) custom-call(bf16[512,256]{1,0:T(8,128)(2,1)S(1)} %constant_dynamic-slice_fusion.points_ref.refs_0_, bf16[576,256]{1,0:T(8,128)(2,1)S(1)} %pack.1.refs_1_.refs_2_, bf16[576,256]{1,0:T(8,128)(2,1)S(1)} %collective-permute-done.4.refs_2_.refs_3_, ...), custom_call_target="tpu_custom_call" | custom-call | flops 16777216 | bytes 1024 | tf_op jit(solution)/shard_map/fetch_points/build_tile/pallas_call | solution.py:155
  11.5 6.3 %collective-permute-done.1.refs_1_.refs_2_ = bf16[512,256]{1,0:T(8,128)(2,1)S(1)} collective-permute-done((bf16[512,256]{1,0:T(8,128)(2,1)S(1)}, bf16[512,256]{1,0:T(8,128)(2,1)S(1)}, u32[]{:S(2)}, u32[]{:S(2)}) %collective-permute-start.1) | collective-permute-done | bytes 262176 | tf_op jit(solution)/shard_map/fetch_points/ppermute | solution.py:29
  17.9 1.4 %build_tile.8 = (bf16[1024,1024]{1,0:T(8,128)(2,1)S(1)}, f32[16,1024]{1,0:T(8,128)S(1)}, f32[1024,1]{1,0:T(8,128)S(1)}) custom-call(bf16[512,256]{1,0:T(8,128)(2,1)S(1)} %collective-permute-done.refs_0_.refs_1_, bf16[512,256]{1,0:T(8,128)(2,1)S(1)} %collective-permute-done.1.refs_1_.refs_2_, bf16[576,256]{1,0:T(8,128)(2,1)S(1)} %pack.1.refs_1_.refs_2_, ...), custom_call_target="tpu_custom_call" | custom-call | flops 33554432 | bytes 1024 | tf_op jit(solution)/shard_map/fetch_points/build_tile/pallas_call | solution.py:155
  19.4 0.5 collective-permute-start.7
  19.9 0.7 %collective-permute-start.8 = (bf16[576,256]{1,0:T(8,128)(2,1)S(1)}, bf16[576,256]{1,0:T(8,128)(2,1)S(1)}, u32[]{:S(2)}, u32[]{:S(2)}) collective-permute-start(bf16[576,256]{1,0:T(8,128)(2,1)S(1)} %broadcast_select_fusion), channel_id=1, source_target_pairs={{0,96},{4,28},{8,104},{12,20},{16,112},{20,12},{24,120},{28,4},{32... | collective-permute-start | bytes 884744 | tf_op jit(solution)/shard_map/fetch_points/ppermute | solution.py:44
  20.8 1.9 %build_tile.9 = (bf16[1536,1024]{1,0:T(8,128)(2,1)S(1)}, f32[16,1536]{1,0:T(8,128)S(1)}) custom-call(bf16[512,256]{1,0:T(8,128)(2,1)S(1)} %constant_dynamic-slice_fusion.points_ref.refs_0_, bf16[512,256]{1,0:T(8,128)(2,1)S(1)} %collective-permute-done.refs_0_.refs_1_, bf16[512,256]{1,0:T(8,128)(2,1)S(1)} %collective-permute-done.1.refs_1_.refs_2_, ...), custom_call_target="tpu_custom_call" | custom-call | flops 50331648 | bytes 1024 | tf_op jit(solution)/shard_map/build_tiles/build_tile/pallas_call | solution.py:155
  22.7 1.9 %build_tile.10 = (bf16[1536,1024]{1,0:T(8,128)(2,1)S(1)}, f32[16,1536]{1,0:T(8,128)S(1)}) custom-call(bf16[512,256]{1,0:T(8,128)(2,1)S(1)} %constant_dynamic-slice_fusion.points_ref.refs_0_, bf16[512,256]{1,0:T(8,128)(2,1)S(1)} %collective-permute-done.refs_0_.refs_1_, bf16[512,256]{1,0:T(8,128)(2,1)S(1)} %collective-permute-done.1.refs_1_.refs_2_, ...), custom_call_target="tpu_custom_call" | custom-call | flops 50331648 | bytes 1024 | tf_op jit(solution)/shard_map/build_tiles/build_tile/pallas_call | solution.py:155
  24.7 2.5 %collective-permute-done.5.refs_0_.refs_3_ = bf16[512,256]{1,0:T(8,128)(2,1)S(1)} collective-permute-done((bf16[512,256]{1,0:T(8,128)(2,1)S(1)}, bf16[512,256]{1,0:T(8,128)(2,1)S(1)}, u32[]{:S(2)}, u32[]{:S(2)}) %collective-permute-start.5) | collective-permute-done | bytes 262176 | tf_op jit(solution)/shard_map/fetch_points/ppermute | solution.py:44
  27.2 2.1 %build_tile.11 = (bf16[512,3072]{1,0:T(8,128)(2,1)S(1)}, f32[16,512]{1,0:T(8,128)S(1)}, f32[512,1]{1,0:T(8,128)S(1)}) custom-call(bf16[512,256]{1,0:T(8,128)(2,1)S(1)} %collective-permute-done.5.refs_0_.refs_3_, bf16[576,256]{1,0:T(8,128)(2,1)S(1)} %pack.1.refs_1_.refs_2_, bf16[576,256]{1,0:T(8,128)(2,1)S(1)} %collective-permute-done.4.refs_2_.refs_3_, ...), custom_call_target="tpu_custom_call" | custom-call | flops 50331648 | bytes 1024 | tf_op jit(solution)/shard_map/build_tiles/build_tile/pallas_call | solution.py:155
  29.2 0.2 collective-permute-start.9
  29.4 1.3 %build_tile.12 = (bf16[2048,512]{1,0:T(8,128)(2,1)S(1)}, f32[16,2048]{1,0:T(8,128)S(1)}) custom-call(bf16[512,256]{1,0:T(8,128)(2,1)S(1)} %constant_dynamic-slice_fusion.points_ref.refs_0_, bf16[512,256]{1,0:T(8,128)(2,1)S(1)} %collective-permute-done.refs_0_.refs_1_, bf16[512,256]{1,0:T(8,128)(2,1)S(1)} %collective-permute-done.1.refs_1_.refs_2_, ...), custom_call_target="tpu_custom_call" | custom-call | flops 33554432 | bytes 1024 | tf_op jit(solution)/shard_map/build_tiles/build_tile/pallas_call | solution.py:155
  30.8 0.2 collective-permute-done.9.refs_4_
  31.0 1.3 %build_tile.13 = (bf16[2048,512]{1,0:T(8,128)(2,1)S(1)}, f32[16,2048]{1,0:T(8,128)S(1)}) custom-call(bf16[512,256]{1,0:T(8,128)(2,1)S(1)} %constant_dynamic-slice_fusion.points_ref.refs_0_, bf16[512,256]{1,0:T(8,128)(2,1)S(1)} %collective-permute-done.refs_0_.refs_1_, bf16[512,256]{1,0:T(8,128)(2,1)S(1)} %collective-permute-done.1.refs_1_.refs_2_, ...), custom_call_target="tpu_custom_call" | custom-call | flops 33554432 | bytes 1024 | tf_op jit(solution)/shard_map/build_tiles/build_tile/pallas_call | solution.py:155
  32.5 1.7 %collective-permute-start.11 = (bf16[80,512]{1,0:T(8,128)(2,1)S(1)}, bf16[80,512]{1,0:T(8,128)(2,1)S(1)}, u32[]{:S(2)}, u32[]{:S(2)}) collective-permute-start(bf16[80,512]{1,0:T(8,128)(2,1)S(1)} %get-tuple-element.65), channel_id=1, source_target_pairs={{0,8},{8,0},{16,24},{24,16},{32,40},{40,32},{48,56},{56,48},{64,72... | collective-permute-start | bytes 245768 | tf_op jit(solution)/shard_map/sum_over_rows/ppermute | solution.py:29
  34.2 1.8 %collective-permute-start.12 = (bf16[80,512]{1,0:T(8,128)(2,1)S(1)}, bf16[80,512]{1,0:T(8,128)(2,1)S(1)}, u32[]{:S(2)}, u32[]{:S(2)}) collective-permute-start(bf16[80,512]{1,0:T(8,128)(2,1)S(1)} %get-tuple-element.66), channel_id=1, source_target_pairs={{0,40},{8,32},{16,56},{24,48},{32,8},{40,0},{48,24},{56,16},{64,10... | collective-permute-start | bytes 245768 | tf_op jit(solution)/shard_map/sum_over_rows/ppermute | solution.py:29
  36.0 1.7 %collective-permute-done.10.refs_1_ = bf16[80,512]{1,0:T(8,128)(2,1)S(1)} collective-permute-done((bf16[80,512]{1,0:T(8,128)(2,1)S(1)}, bf16[80,512]{1,0:T(8,128)(2,1)S(1)}, u32[]{:S(2)}, u32[]{:S(2)}) %collective-permute-start.10) | collective-permute-done | bytes 81952 | tf_op jit(solution)/shard_map/sum_over_rows/ppermute | solution.py:29
  37.7 2.0 %collective-permute-done.12.refs_3_ = bf16[80,512]{1,0:T(8,128)(2,1)S(1)} collective-permute-done((bf16[80,512]{1,0:T(8,128)(2,1)S(1)}, bf16[80,512]{1,0:T(8,128)(2,1)S(1)}, u32[]{:S(2)}, u32[]{:S(2)}) %collective-permute-start.12) | collective-permute-done | bytes 81952 | tf_op jit(solution)/shard_map/sum_over_rows/ppermute | solution.py:29
  39.8 1.4 %second_product.2 = f32[16,2048]{1,0:T(8,128)S(1)} custom-call(bf16[32,2048]{1,0:T(8,128)(2,1)S(1)} %get-tuple-element.76.narrow_ref, bf16[512,1024]{1,0:T(8,128)(2,1)S(1)} %get-tuple-element.69.refs_0_, bf16[1024,1024]{1,0:T(8,128)(2,1)S(1)} %get-tuple-element.70.refs_1_, bf16[1536,1024]{1,0:T(8,128)(2,1)S(1)} %get-tuple-element.71.refs_2_, ...), custom_call_target="tpu_custom_call" | custom-call | flops 134217728 | bytes 1024 | tf_op jit(solution)/shard_map/second_product/pallas_call | solution.py:241
  41.2 1.5 %second_product.3.mine_ref = f32[16,2048]{1,0:T(8,128)S(1)} custom-call(bf16[32,2048]{1,0:T(8,128)(2,1)S(1)} %get-tuple-element.76.narrow_ref, bf16[512,1024]{1,0:T(8,128)(2,1)S(1)} %get-tuple-element.69.refs_0_, bf16[1024,1024]{1,0:T(8,128)(2,1)S(1)} %get-tuple-element.70.refs_1_, bf16[1536,1024]{1,0:T(8,128)(2,1)S(1)} %get-tuple-element.71.refs_2_, ...), custom_call_target="tpu_custom_call" | custom-call | flops 134217728 | bytes 1024 | tf_op jit(solution)/shard_map/second_product/pallas_call | solution.py:241
  42.7 3.0 %collective-permute-start.14 = (f32[16,512]{1,0:T(8,128)S(1)}, f32[16,512]{1,0:T(8,128)S(1)}, u32[]{:S(2)}, u32[]{:S(2)}) collective-permute-start(f32[16,512]{1,0:T(8,128)S(1)} %get-tuple-element.79), channel_id=1, source_target_pairs={{0,96},{8,104},{16,112},{24,120},{32,64},{40,72},{48,80},{56,88},{... | collective-permute-start | bytes 98312 | tf_op jit(solution)/shard_map/sum_over_columns/ppermute | solution.py:29
  45.8 0.3 collective-permute-start.15
  46.1 2.7 %collective-permute-start.16 = (f32[16,512]{1,0:T(8,128)S(1)}, f32[16,512]{1,0:T(8,128)S(1)}, u32[]{:S(2)}, u32[]{:S(2)}) collective-permute-start(f32[16,512]{1,0:T(8,128)S(1)} %get-tuple-element.81), channel_id=1, source_target_pairs={{0,120},{8,112},{16,104},{24,96},{32,88},{40,80},{48,72},{56,64},{... | collective-permute-start | bytes 98312 | tf_op jit(solution)/shard_map/sum_over_columns/ppermute | solution.py:29
  48.7 2.2 %collective-permute-done.15.refs_2_ = f32[16,512]{1,0:T(8,128)S(1)} collective-permute-done((f32[16,512]{1,0:T(8,128)S(1)}, f32[16,512]{1,0:T(8,128)S(1)}, u32[]{:S(2)}, u32[]{:S(2)}) %collective-permute-start.15) | collective-permute-done | bytes 32800 | tf_op jit(solution)/shard_map/sum_over_columns/ppermute | solution.py:29
  50.9 2.4 %collective-permute-done.16.refs_3_ = f32[16,512]{1,0:T(8,128)S(1)} collective-permute-done((f32[16,512]{1,0:T(8,128)S(1)}, f32[16,512]{1,0:T(8,128)S(1)}, u32[]{:S(2)}, u32[]{:S(2)}) %collective-permute-start.16) | collective-permute-done | bytes 32800 | tf_op jit(solution)/shard_map/sum_over_columns/ppermute | solution.py:29
  53.3 0.2 local_sums.1
  53.5 11.8 %all_to_all.8 = f32[32,1,128]{2,1,0:T(1,128)S(1)} all-to-all(f32[32,1,128]{2,1,0:T(1,128)S(1)} %broadcast_in_dim.2), channel_id=1, replica_groups=mesh['y'=4,'z'=4,'c'=2,'x'=4] {'y','z','c'}, dimensions={0} | all-to-all | bytes 32768 | tf_op jit(solution)/shard_map/final_sums/all_to_all | solution.py:377
  65.3 1.0 %finish.1 = (f32[16,512]{1,0:T(8,128)}, f32[16,512]{1,0:T(8,128)}) custom-call(f32[16,512]{1,0:T(8,128)S(1)} %bitcast.12, f32[16,512]{1,0:T(8,128)S(1)} %get-tuple-element.67.rho_ref, f32[16,512]{1,0:T(8,128)S(1)} %get-tuple-element.82.image_ref, f32[32,128]{1,0:T(8,128)S(1)} %bitcast.13), custom_call_target="tpu_custom_call" | custom-call | tf_op jit(solution)/shard_map/finish/pallas_call | solution.py:315
  (29 shorter events, 0.8 us)
Async XLA Ops:
  0.6 1.5 %copy-start = (bf16[1024,256]{1,0:T(8,128)(2,1)S(1)}, bf16[1024,256]{1,0:T(8,128)(2,1)}, u32[]{:S(2)}) copy-start(bf16[1024,256]{1,0:T(8,128)(2,1)} %param.3) | copy-start | bytes 1572868
  2.5 7.5 %collective-permute-start.4 = (bf16[576,256]{1,0:T(8,128)(2,1)S(1)}, bf16[576,256]{1,0:T(8,128)(2,1)S(1)}, u32[]{:S(2)}, u32[]{:S(2)}) collective-permute-start(bf16[576,256]{1,0:T(8,128)(2,1)S(1)} %pack.1.refs_1_.refs_2_), channel_id=1, source_target_pairs={{0,4},{4,0},{1,5},{5,1},{2,6},{6,2},{3,7},{7,3},{8,12},{12,8},{9,1... | collective-permute-start | bytes 884744 | tf_op jit(solution)/shard_map/fetch_points/ppermute | solution.py:48
  2.6 16.7 %collective-permute-start.3 = (bf16[576,256]{1,0:T(8,128)(2,1)S(1)}, bf16[576,256]{1,0:T(8,128)(2,1)S(1)}, u32[]{:S(2)}, u32[]{:S(2)}) collective-permute-start(bf16[576,256]{1,0:T(8,128)(2,1)S(1)} %pack.1.refs_1_.refs_2_), channel_id=1, source_target_pairs={{0,24},{8,16},{16,8},{24,0},{32,56},{40,48},{48,40},{56,32},{64,88... | collective-permute-start | bytes 884744 | tf_op jit(solution)/shard_map/fetch_points/ppermute | solution.py:29
  6.8 12.5 %collective-permute-start.2 = (bf16[576,256]{1,0:T(8,128)(2,1)S(1)}, bf16[576,256]{1,0:T(8,128)(2,1)S(1)}, u32[]{:S(2)}, u32[]{:S(2)}) collective-permute-start(bf16[576,256]{1,0:T(8,128)(2,1)S(1)} %pack.1.refs_1_.refs_2_), channel_id=1, source_target_pairs={{0,96},{8,104},{16,112},{24,120},{32,64},{40,72},{48,80},{56,88},{... | collective-permute-start | bytes 884744 | tf_op jit(solution)/shard_map/fetch_points/ppermute | solution.py:29
  9.8 8.1 %collective-permute-start.1 = (bf16[512,256]{1,0:T(8,128)(2,1)S(1)}, bf16[512,256]{1,0:T(8,128)(2,1)S(1)}, u32[]{:S(2)}, u32[]{:S(2)}) collective-permute-start(bf16[512,256]{1,0:T(8,128)(2,1)S(1)} %constant_dynamic-slice_fusion.points_ref.refs_0_), channel_id=1, source_target_pairs={{0,8},{8,0},{16,24},{24,16},{32,40},{40,32},{48,56},{56,48},{64,72... | collective-permute-start | bytes 786440 | tf_op jit(solution)/shard_map/fetch_points/ppermute | solution.py:29
  9.8 8.1 %collective-permute-start = (bf16[512,256]{1,0:T(8,128)(2,1)S(1)}, bf16[512,256]{1,0:T(8,128)(2,1)S(1)}, u32[]{:S(2)}, u32[]{:S(2)}) collective-permute-start(bf16[512,256]{1,0:T(8,128)(2,1)S(1)} %constant_dynamic-slice_fusion.points_ref.refs_0_), channel_id=1, source_target_pairs={{0,32},{8,40},{16,48},{24,56},{32,0},{40,8},{48,16},{56,24},{64,96... | collective-permute-start | bytes 786440 | tf_op jit(solution)/shard_map/fetch_points/ppermute | solution.py:29
  9.9 0.8 %copy-start.1 = (f32[512,16]{0,1:T(8,128)S(1)}, f32[512,16]{0,1:T(8,128)}, u32[]{:S(2)}) copy-start(f32[512,16]{0,1:T(8,128)} %param.5) | copy-start | bytes 98308
  19.3 3.4 %collective-permute-start.6 = (bf16[576,256]{1,0:T(8,128)(2,1)S(1)}, bf16[576,256]{1,0:T(8,128)(2,1)S(1)}, u32[]{:S(2)}, u32[]{:S(2)}) collective-permute-start(bf16[576,256]{1,0:T(8,128)(2,1)S(1)} %collective-permute-done.2.refs_3_), channel_id=1, source_target_pairs={{0,4},{4,0},{1,5},{5,1},{2,6},{6,2},{3,7},{7,3},{8,12},{12,8},{9,1... | collective-permute-start | bytes 884744 | tf_op jit(solution)/shard_map/build_tiles/ppermute | solution.py:48
  19.4 3.3 %collective-permute-start.7 = (bf16[576,256]{1,0:T(8,128)(2,1)S(1)}, bf16[576,256]{1,0:T(8,128)(2,1)S(1)}, u32[]{:S(2)}, u32[]{:S(2)}) collective-permute-start(bf16[576,256]{1,0:T(8,128)(2,1)S(1)} %collective-permute-done.3.refs_4_), channel_id=1, source_target_pairs={{0,4},{4,0},{1,5},{5,1},{2,6},{6,2},{3,7},{7,3},{8,12},{12,8},{9,1... | collective-permute-start | bytes 884744 | tf_op jit(solution)/shard_map/build_tiles/ppermute | solution.py:48
  19.9 9.3 %collective-permute-start.8 = (bf16[576,256]{1,0:T(8,128)(2,1)S(1)}, bf16[576,256]{1,0:T(8,128)(2,1)S(1)}, u32[]{:S(2)}, u32[]{:S(2)}) collective-permute-start(bf16[576,256]{1,0:T(8,128)(2,1)S(1)} %broadcast_select_fusion), channel_id=1, source_target_pairs={{0,96},{4,28},{8,104},{12,20},{16,112},{20,12},{24,120},{28,4},{32... | collective-permute-start | bytes 884744 | tf_op jit(solution)/shard_map/fetch_points/ppermute | solution.py:44
  20.7 6.5 %collective-permute-start.5 = (bf16[512,256]{1,0:T(8,128)(2,1)S(1)}, bf16[512,256]{1,0:T(8,128)(2,1)S(1)}, u32[]{:S(2)}, u32[]{:S(2)}) collective-permute-start(bf16[512,256]{1,0:T(8,128)(2,1)S(1)} %broadcast_select_fusion.1), channel_id=1, source_target_pairs={{0,32},{4,12},{8,40},{12,4},{16,48},{20,28},{24,56},{28,20},{32,0}... | collective-permute-start | bytes 786440 | tf_op jit(solution)/shard_map/fetch_points/ppermute | solution.py:44
  29.2 1.8 %collective-permute-start.9 = (bf16[576,256]{1,0:T(8,128)(2,1)S(1)}, bf16[576,256]{1,0:T(8,128)(2,1)S(1)}, u32[]{:S(2)}, u32[]{:S(2)}) collective-permute-start(bf16[576,256]{1,0:T(8,128)(2,1)S(1)} %collective-permute-done.8.refs_4_), channel_id=1, source_target_pairs={{0,4},{4,0},{1,5},{5,1},{2,6},{6,2},{3,7},{7,3},{8,12},{12,8},{9,1... | collective-permute-start | bytes 884744 | tf_op jit(solution)/shard_map/build_tiles/ppermute | solution.py:48
  32.4 5.3 %collective-permute-start.10 = (bf16[80,512]{1,0:T(8,128)(2,1)S(1)}, bf16[80,512]{1,0:T(8,128)(2,1)S(1)}, u32[]{:S(2)}, u32[]{:S(2)}) collective-permute-start(bf16[80,512]{1,0:T(8,128)(2,1)S(1)} %get-tuple-element.64), channel_id=1, source_target_pairs={{0,32},{8,40},{16,48},{24,56},{32,0},{40,8},{48,16},{56,24},{64,96... | collective-permute-start | bytes 245768 | tf_op jit(solution)/shard_map/sum_over_rows/ppermute | solution.py:29
  32.5 5.2 %collective-permute-start.11 = (bf16[80,512]{1,0:T(8,128)(2,1)S(1)}, bf16[80,512]{1,0:T(8,128)(2,1)S(1)}, u32[]{:S(2)}, u32[]{:S(2)}) collective-permute-start(bf16[80,512]{1,0:T(8,128)(2,1)S(1)} %get-tuple-element.65), channel_id=1, source_target_pairs={{0,8},{8,0},{16,24},{24,16},{32,40},{40,32},{48,56},{56,48},{64,72... | collective-permute-start | bytes 245768 | tf_op jit(solution)/shard_map/sum_over_rows/ppermute | solution.py:29
  34.2 5.5 %collective-permute-start.12 = (bf16[80,512]{1,0:T(8,128)(2,1)S(1)}, bf16[80,512]{1,0:T(8,128)(2,1)S(1)}, u32[]{:S(2)}, u32[]{:S(2)}) collective-permute-start(bf16[80,512]{1,0:T(8,128)(2,1)S(1)} %get-tuple-element.66), channel_id=1, source_target_pairs={{0,40},{8,32},{16,56},{24,48},{32,8},{40,0},{48,24},{56,16},{64,10... | collective-permute-start | bytes 245768 | tf_op jit(solution)/shard_map/sum_over_rows/ppermute | solution.py:29
  41.2 12.0 %copy-start.2 = (f32[512,16]{0,1:T(8,128)S(1)}, f32[512,16]{0,1:T(8,128)}, u32[]{:S(2)}) copy-start(f32[512,16]{0,1:T(8,128)} %param.5) | copy-start | bytes 98308
  41.2 1.5 %collective-permute-start.13 = (f32[16,2048]{1,0:T(8,128)S(1)}, f32[16,2048]{1,0:T(8,128)S(1)}, u32[]{:S(2)}, u32[]{:S(2)}) collective-permute-start(f32[16,2048]{1,0:T(8,128)S(1)} %second_product.2), channel_id=1, source_target_pairs={{0,4},{4,0},{1,5},{5,1},{2,6},{6,2},{3,7},{7,3},{8,12},{12,8},{9,1... | collective-permute-start | bytes 393224 | tf_op jit(solution)/shard_map/sum_over_columns/ppermute | solution.py:48
  42.7 6.0 %collective-permute-start.14 = (f32[16,512]{1,0:T(8,128)S(1)}, f32[16,512]{1,0:T(8,128)S(1)}, u32[]{:S(2)}, u32[]{:S(2)}) collective-permute-start(f32[16,512]{1,0:T(8,128)S(1)} %get-tuple-element.79), channel_id=1, source_target_pairs={{0,96},{8,104},{16,112},{24,120},{32,64},{40,72},{48,80},{56,88},{... | collective-permute-start | bytes 98312 | tf_op jit(solution)/shard_map/sum_over_columns/ppermute | solution.py:29
  45.8 5.1 %collective-permute-start.15 = (f32[16,512]{1,0:T(8,128)S(1)}, f32[16,512]{1,0:T(8,128)S(1)}, u32[]{:S(2)}, u32[]{:S(2)}) collective-permute-start(f32[16,512]{1,0:T(8,128)S(1)} %get-tuple-element.80), channel_id=1, source_target_pairs={{0,24},{8,16},{16,8},{24,0},{32,56},{40,48},{48,40},{56,32},{64,88... | collective-permute-start | bytes 98312 | tf_op jit(solution)/shard_map/sum_over_columns/ppermute | solution.py:29
  46.1 7.2 %collective-permute-start.16 = (f32[16,512]{1,0:T(8,128)S(1)}, f32[16,512]{1,0:T(8,128)S(1)}, u32[]{:S(2)}, u32[]{:S(2)}) collective-permute-start(f32[16,512]{1,0:T(8,128)S(1)} %get-tuple-element.81), channel_id=1, source_target_pairs={{0,120},{8,112},{16,104},{24,96},{32,88},{40,80},{48,72},{56,64},{... | collective-permute-start | bytes 98312 | tf_op jit(solution)/shard_map/sum_over_columns/ppermute | solution.py:29

commit v14 on v13

--- a/solution.py
+++ b/solution.py
@@ -339,8 +339,9 @@
 
     with jax.named_scope("build_tiles"):
         half = [half_a, half_b]
-        others = [swap_core(cols[1]), swap_core(cols[2])]
         tile_d, image = build(rows[:3], cols[1:3], own, probes, half, [image_a, image_b])
+        (near_y, near_z), image = lax.optimization_barrier(((cols[1], cols[2]), image))
+        others = [swap_core(near_y), swap_core(near_z)]
         tile_e, image = build(rows[:3], others, own, probes, half, [image])
         rows[3], image = lax.optimization_barrier((rows[3], image))
         tile_f, image_far, half_far = build([rows[3]], first + cols[1:3] + others, own, probes)

time: 67.4 us -> 69.2 us (1.027)
  waiting for transfers between devices: 17.4 us -> 19.2 us
    ppermute x5, waiting for transfers between devices: 0.25 us -> 1.61 us  [swap_core(): return lax.ppermute(value, 'c', [(0, 1), (1, 0)])]
  transfers between devices with their start and end apart: 17 -> 17, of which waited for: 7 -> 9; matrix products, arithmetic and copies ran while one was open for 0% -> 0% of each run, Pallas kernels for 17% -> 16%
where the time goes in v14:
time: 69.2 us; the launch traced here: 68.2 us
  waiting for transfers between devices  19.2 us (28%)
  starting transfers between devices  18.6 us (27%)
  Pallas kernels  15.4 us (22%)
  blocking collectives  11.8 us (17%)
  between operations  1.46 us (2%)
  local copies, waits for them, and re-layouts  0.85 us (1%)
  other arithmetic  0.83 us (1%)
    ppermute x10, starting transfers between devices, swap(): return lax.ppermute(value, ('y', 'z'), pairs)  16.9 us
    ppermute x10, waiting for transfers between devices, swap(): return lax.ppermute(value, ('y', 'z'), pairs)  14.6 us
    all_to_all x1, blocking collectives, on_device(): sums = lax.all_to_all(sums, ('y', 'z', 'c'), 0, 0, tiled=True)  11.8 us
    pallas_call x7, Pallas kernels, build(): pl.pallas_call(functools.partial(tile_kernel, counts, probes), out_shape=...  10.8 us
    ppermute x2, waiting for transfers between devices, hand_on(): return lax.ppermute(value, ('y', 'z', 'c'), pairs)  3.07 us
    pallas_call x2, Pallas kernels, second_product(): pl.pallas_call(functools.partial(second_kernel, own, half, places), in_sp...  2.9 us
    ppermute x5, waiting for transfers between devices, swap_core(): return lax.ppermute(value, 'c', [(0, 1), (1, 0)])  1.61 us
  transfers between devices with their start and end apart: 17, of which 9 were waited for; matrix products, arithmetic and copies ran while one was open for 0% of the time, Pallas kernels for 16%

profile of v14, /device:TPU:0, one launch (start us, length us, event | category | flops | bytes accessed | tf_op | source)
XLA Modules:
  0.0 68.2 jit_solution(7885714689025037303)
XLA Ops:
  1.3 0.8 %bitcast_convert_fusion.side_ref = bf16[16,512]{1,0:T(8,128)(2,1)S(1)} fusion(f32[512,16]{0,1:T(8,128)} %param.5), kind=kLoop, calls=%fused_computation.3 | loop fusion | flops 8192 | bytes 49152 | tf_op jit(solution)/shard_map/fetch_points/convert_element_type | solution.py:328
  2.2 0.3 pack.1.refs_1_.refs_2_
  2.6 4.2 %collective-permute-start.3 = (bf16[576,256]{1,0:T(8,128)(2,1)S(1)}, bf16[576,256]{1,0:T(8,128)(2,1)S(1)}, u32[]{:S(2)}, u32[]{:S(2)}) collective-permute-start(bf16[576,256]{1,0:T(8,128)(2,1)S(1)} %pack.1.refs_1_.refs_2_), channel_id=1, source_target_pairs={{0,24},{8,16},{16,8},{24,0},{32,56},{40,48},{48,40},{56,32},{64,88... | collective-permute-start | bytes 884744 | tf_op jit(solution)/shard_map/fetch_points/ppermute | solution.py:29
  6.8 3.0 %collective-permute-start.2 = (bf16[576,256]{1,0:T(8,128)(2,1)S(1)}, bf16[576,256]{1,0:T(8,128)(2,1)S(1)}, u32[]{:S(2)}, u32[]{:S(2)}) collective-permute-start(bf16[576,256]{1,0:T(8,128)(2,1)S(1)} %pack.1.refs_1_.refs_2_), channel_id=1, source_target_pairs={{0,96},{8,104},{16,112},{24,120},{32,64},{40,72},{48,80},{56,88},{... | collective-permute-start | bytes 884744 | tf_op jit(solution)/shard_map/fetch_points/ppermute | solution.py:29
  9.9 0.8 %copy-done.1 = f32[512,16]{0,1:T(8,128)S(1)} copy-done((f32[512,16]{0,1:T(8,128)S(1)}, f32[512,16]{0,1:T(8,128)}, u32[]{:S(2)}) %copy-start.1) | copy-done | bytes 32792
  10.7 0.8 %build_tile.7 = (bf16[512,1024]{1,0:T(8,128)(2,1)S(1)}, f32[16,512]{1,0:T(8,128)S(1)}, f32[512,1]{1,0:T(8,128)S(1)}) custom-call(bf16[512,256]{1,0:T(8,128)(2,1)S(1)} %constant_dynamic-slice_fusion.points_ref.refs_0_, bf16[576,256]{1,0:T(8,128)(2,1)S(1)} %pack.1.refs_1_.refs_2_, bf16[576,256]{1,0:T(8,128)(2,1)S(1)} %collective-permute-done.4.refs_2_.refs_3_, ...), custom_call_target="tpu_custom_call" | custom-call | flops 16777216 | bytes 1024 | tf_op jit(solution)/shard_map/fetch_points/build_tile/pallas_call | solution.py:155
  11.5 6.3 %collective-permute-done.1.refs_1_.refs_2_ = bf16[512,256]{1,0:T(8,128)(2,1)S(1)} collective-permute-done((bf16[512,256]{1,0:T(8,128)(2,1)S(1)}, bf16[512,256]{1,0:T(8,128)(2,1)S(1)}, u32[]{:S(2)}, u32[]{:S(2)}) %collective-permute-start.1) | collective-permute-done | bytes 262176 | tf_op jit(solution)/shard_map/fetch_points/ppermute | solution.py:29
  17.9 1.4 %build_tile.8 = (bf16[1024,1024]{1,0:T(8,128)(2,1)S(1)}, f32[16,1024]{1,0:T(8,128)S(1)}, f32[1024,1]{1,0:T(8,128)S(1)}) custom-call(bf16[512,256]{1,0:T(8,128)(2,1)S(1)} %collective-permute-done.refs_0_.refs_1_, bf16[512,256]{1,0:T(8,128)(2,1)S(1)} %collective-permute-done.1.refs_1_.refs_2_, bf16[576,256]{1,0:T(8,128)(2,1)S(1)} %pack.1.refs_1_.refs_2_, ...), custom_call_target="tpu_custom_call" | custom-call | flops 33554432 | bytes 1024 | tf_op jit(solution)/shard_map/fetch_points/build_tile/pallas_call | solution.py:155
  19.4 0.8 %collective-permute-start.8 = (bf16[576,256]{1,0:T(8,128)(2,1)S(1)}, bf16[576,256]{1,0:T(8,128)(2,1)S(1)}, u32[]{:S(2)}, u32[]{:S(2)}) collective-permute-start(bf16[576,256]{1,0:T(8,128)(2,1)S(1)} %broadcast_select_fusion), channel_id=1, source_target_pairs={{0,96},{4,28},{8,104},{12,20},{16,112},{20,12},{24,120},{28,4},{32... | collective-permute-start | bytes 884744 | tf_op jit(solution)/shard_map/fetch_points/ppermute | solution.py:44
  20.2 1.9 %build_tile.9 = (bf16[1536,1024]{1,0:T(8,128)(2,1)S(1)}, f32[16,1536]{1,0:T(8,128)S(1)}) custom-call(bf16[512,256]{1,0:T(8,128)(2,1)S(1)} %constant_dynamic-slice_fusion.points_ref.refs_0_, bf16[512,256]{1,0:T(8,128)(2,1)S(1)} %collective-permute-done.refs_0_.refs_1_, bf16[512,256]{1,0:T(8,128)(2,1)S(1)} %collective-permute-done.1.refs_1_.refs_2_, ...), custom_call_target="tpu_custom_call" | custom-call | flops 50331648 | bytes 1024 | tf_op jit(solution)/shard_map/build_tiles/build_tile/pallas_call | solution.py:155
  22.1 0.5 collective-permute-start.7
  22.7 0.9 %collective-permute-done.6.refs_3_.refs_5_ = bf16[576,256]{1,0:T(8,128)(2,1)S(1)} collective-permute-done((bf16[576,256]{1,0:T(8,128)(2,1)S(1)}, bf16[576,256]{1,0:T(8,128)(2,1)S(1)}, u32[]{:S(2)}, u32[]{:S(2)}) %collective-permute-start.6) | collective-permute-done | bytes 294944 | tf_op jit(solution)/shard_map/build_tiles/ppermute | solution.py:48
  23.7 0.4 collective-permute-done.7.refs_4_.refs_6_
  24.1 1.9 %build_tile.10 = (bf16[1536,1024]{1,0:T(8,128)(2,1)S(1)}, f32[16,1536]{1,0:T(8,128)S(1)}) custom-call(bf16[512,256]{1,0:T(8,128)(2,1)S(1)} %constant_dynamic-slice_fusion.points_ref.refs_0_, bf16[512,256]{1,0:T(8,128)(2,1)S(1)} %collective-permute-done.refs_0_.refs_1_, bf16[512,256]{1,0:T(8,128)(2,1)S(1)} %collective-permute-done.1.refs_1_.refs_2_, ...), custom_call_target="tpu_custom_call" | custom-call | flops 50331648 | bytes 1024 | tf_op jit(solution)/shard_map/build_tiles/build_tile/pallas_call | solution.py:155
  26.0 3.1 %collective-permute-done.5.refs_0_.refs_3_ = bf16[512,256]{1,0:T(8,128)(2,1)S(1)} collective-permute-done((bf16[512,256]{1,0:T(8,128)(2,1)S(1)}, bf16[512,256]{1,0:T(8,128)(2,1)S(1)}, u32[]{:S(2)}, u32[]{:S(2)}) %collective-permute-start.5) | collective-permute-done | bytes 262176 | tf_op jit(solution)/shard_map/fetch_points/ppermute | solution.py:44
  29.1 2.0 %build_tile.11 = (bf16[512,3072]{1,0:T(8,128)(2,1)S(1)}, f32[16,512]{1,0:T(8,128)S(1)}, f32[512,1]{1,0:T(8,128)S(1)}) custom-call(bf16[512,256]{1,0:T(8,128)(2,1)S(1)} %collective-permute-done.5.refs_0_.refs_3_, bf16[576,256]{1,0:T(8,128)(2,1)S(1)} %pack.1.refs_1_.refs_2_, bf16[576,256]{1,0:T(8,128)(2,1)S(1)} %collective-permute-done.4.refs_2_.refs_3_, ...), custom_call_target="tpu_custom_call" | custom-call | flops 50331648 | bytes 1024 | tf_op jit(solution)/shard_map/build_tiles/build_tile/pallas_call | solution.py:155
  31.4 1.3 %build_tile.12 = (bf16[2048,512]{1,0:T(8,128)(2,1)S(1)}, f32[16,2048]{1,0:T(8,128)S(1)}) custom-call(bf16[512,256]{1,0:T(8,128)(2,1)S(1)} %constant_dynamic-slice_fusion.points_ref.refs_0_, bf16[512,256]{1,0:T(8,128)(2,1)S(1)} %collective-permute-done.refs_0_.refs_1_, bf16[512,256]{1,0:T(8,128)(2,1)S(1)} %collective-permute-done.1.refs_1_.refs_2_, ...), custom_call_target="tpu_custom_call" | custom-call | flops 33554432 | bytes 1024 | tf_op jit(solution)/shard_map/build_tiles/build_tile/pallas_call | solution.py:155
  32.7 0.2 collective-permute-done.9.refs_4_
  32.9 1.3 %build_tile.13 = (bf16[2048,512]{1,0:T(8,128)(2,1)S(1)}, f32[16,2048]{1,0:T(8,128)S(1)}) custom-call(bf16[512,256]{1,0:T(8,128)(2,1)S(1)} %constant_dynamic-slice_fusion.points_ref.refs_0_, bf16[512,256]{1,0:T(8,128)(2,1)S(1)} %collective-permute-done.refs_0_.refs_1_, bf16[512,256]{1,0:T(8,128)(2,1)S(1)} %collective-permute-done.1.refs_1_.refs_2_, ...), custom_call_target="tpu_custom_call" | custom-call | flops 33554432 | bytes 1024 | tf_op jit(solution)/shard_map/build_tiles/build_tile/pallas_call | solution.py:155
  34.4 1.6 %collective-permute-start.11 = (bf16[80,512]{1,0:T(8,128)(2,1)S(1)}, bf16[80,512]{1,0:T(8,128)(2,1)S(1)}, u32[]{:S(2)}, u32[]{:S(2)}) collective-permute-start(bf16[80,512]{1,0:T(8,128)(2,1)S(1)} %get-tuple-element.71), channel_id=1, source_target_pairs={{0,8},{8,0},{16,24},{24,16},{32,40},{40,32},{48,56},{56,48},{64,72... | collective-permute-start | bytes 245768 | tf_op jit(solution)/shard_map/sum_over_rows/ppermute | solution.py:29
  36.0 1.9 %collective-permute-start.12 = (bf16[80,512]{1,0:T(8,128)(2,1)S(1)}, bf16[80,512]{1,0:T(8,128)(2,1)S(1)}, u32[]{:S(2)}, u32[]{:S(2)}) collective-permute-start(bf16[80,512]{1,0:T(8,128)(2,1)S(1)} %get-tuple-element.72), channel_id=1, source_target_pairs={{0,40},{8,32},{16,56},{24,48},{32,8},{40,0},{48,24},{56,16},{64,10... | collective-permute-start | bytes 245768 | tf_op jit(solution)/shard_map/sum_over_rows/ppermute | solution.py:29
  37.9 1.7 %collective-permute-done.10.refs_1_ = bf16[80,512]{1,0:T(8,128)(2,1)S(1)} collective-permute-done((bf16[80,512]{1,0:T(8,128)(2,1)S(1)}, bf16[80,512]{1,0:T(8,128)(2,1)S(1)}, u32[]{:S(2)}, u32[]{:S(2)}) %collective-permute-start.10) | collective-permute-done | bytes 81952 | tf_op jit(solution)/shard_map/sum_over_rows/ppermute | solution.py:29
  39.6 2.0 %collective-permute-done.12.refs_3_ = bf16[80,512]{1,0:T(8,128)(2,1)S(1)} collective-permute-done((bf16[80,512]{1,0:T(8,128)(2,1)S(1)}, bf16[80,512]{1,0:T(8,128)(2,1)S(1)}, u32[]{:S(2)}, u32[]{:S(2)}) %collective-permute-start.12) | collective-permute-done | bytes 81952 | tf_op jit(solution)/shard_map/sum_over_rows/ppermute | solution.py:29
  41.6 1.4 %second_product.2 = f32[16,2048]{1,0:T(8,128)S(1)} custom-call(bf16[32,2048]{1,0:T(8,128)(2,1)S(1)} %get-tuple-element.82.narrow_ref, bf16[512,1024]{1,0:T(8,128)(2,1)S(1)} %get-tuple-element.75.refs_0_, bf16[1024,1024]{1,0:T(8,128)(2,1)S(1)} %get-tuple-element.76.refs_1_, bf16[1536,1024]{1,0:T(8,128)(2,1)S(1)} %get-tuple-element.77.refs_2_, ...), custom_call_target="tpu_custom_call" | custom-call | flops 134217728 | bytes 1024 | tf_op jit(solution)/shard_map/second_product/pallas_call | solution.py:241
  43.1 1.5 %second_product.3.mine_ref = f32[16,2048]{1,0:T(8,128)S(1)} custom-call(bf16[32,2048]{1,0:T(8,128)(2,1)S(1)} %get-tuple-element.82.narrow_ref, bf16[512,1024]{1,0:T(8,128)(2,1)S(1)} %get-tuple-element.75.refs_0_, bf16[1024,1024]{1,0:T(8,128)(2,1)S(1)} %get-tuple-element.76.refs_1_, bf16[1536,1024]{1,0:T(8,128)(2,1)S(1)} %get-tuple-element.77.refs_2_, ...), custom_call_target="tpu_custom_call" | custom-call | flops 134217728 | bytes 1024 | tf_op jit(solution)/shard_map/second_product/pallas_call | solution.py:241
  44.6 3.0 %collective-permute-start.14 = (f32[16,512]{1,0:T(8,128)S(1)}, f32[16,512]{1,0:T(8,128)S(1)}, u32[]{:S(2)}, u32[]{:S(2)}) collective-permute-start(f32[16,512]{1,0:T(8,128)S(1)} %get-tuple-element.85), channel_id=1, source_target_pairs={{0,96},{8,104},{16,112},{24,120},{32,64},{40,72},{48,80},{56,88},{... | collective-permute-start | bytes 98312 | tf_op jit(solution)/shard_map/sum_over_columns/ppermute | solution.py:29
  47.6 0.3 collective-permute-start.15
  47.9 2.7 %collective-permute-start.16 = (f32[16,512]{1,0:T(8,128)S(1)}, f32[16,512]{1,0:T(8,128)S(1)}, u32[]{:S(2)}, u32[]{:S(2)}) collective-permute-start(f32[16,512]{1,0:T(8,128)S(1)} %get-tuple-element.87), channel_id=1, source_target_pairs={{0,120},{8,112},{16,104},{24,96},{32,88},{40,80},{48,72},{56,64},{... | collective-permute-start | bytes 98312 | tf_op jit(solution)/shard_map/sum_over_columns/ppermute | solution.py:29
  50.6 2.2 %collective-permute-done.15.refs_2_ = f32[16,512]{1,0:T(8,128)S(1)} collective-permute-done((f32[16,512]{1,0:T(8,128)S(1)}, f32[16,512]{1,0:T(8,128)S(1)}, u32[]{:S(2)}, u32[]{:S(2)}) %collective-permute-start.15) | collective-permute-done | bytes 32800 | tf_op jit(solution)/shard_map/sum_over_columns/ppermute | solution.py:29
  52.7 2.4 %collective-permute-done.16.refs_3_ = f32[16,512]{1,0:T(8,128)S(1)} collective-permute-done((f32[16,512]{1,0:T(8,128)S(1)}, f32[16,512]{1,0:T(8,128)S(1)}, u32[]{:S(2)}, u32[]{:S(2)}) %collective-permute-start.16) | collective-permute-done | bytes 32800 | tf_op jit(solution)/shard_map/sum_over_columns/ppermute | solution.py:29
  55.4 11.8 %all_to_all.8 = f32[32,1,128]{2,1,0:T(1,128)S(1)} all-to-all(f32[32,1,128]{2,1,0:T(1,128)S(1)} %broadcast_in_dim.2), channel_id=1, replica_groups=mesh['y'=4,'z'=4,'c'=2,'x'=4] {'y','z','c'}, dimensions={0} | all-to-all | bytes 32768 | tf_op jit(solution)/shard_map/final_sums/all_to_all | solution.py:378
  67.2 1.0 %finish.1 = (f32[16,512]{1,0:T(8,128)}, f32[16,512]{1,0:T(8,128)}) custom-call(f32[16,512]{1,0:T(8,128)S(1)} %bitcast.12, f32[16,512]{1,0:T(8,128)S(1)} %get-tuple-element.73.rho_ref, f32[16,512]{1,0:T(8,128)S(1)} %get-tuple-element.88.image_ref, f32[32,128]{1,0:T(8,128)S(1)} %bitcast.13), custom_call_target="tpu_custom_call" | custom-call | tf_op jit(solution)/shard_map/finish/pallas_call | solution.py:315
  (29 shorter events, 1.2 us)
Async XLA Ops:
  0.6 1.5 %copy-start = (bf16[1024,256]{1,0:T(8,128)(2,1)S(1)}, bf16[1024,256]{1,0:T(8,128)(2,1)}, u32[]{:S(2)}) copy-start(bf16[1024,256]{1,0:T(8,128)(2,1)} %param.3) | copy-start | bytes 1572868
  2.5 7.5 %collective-permute-start.4 = (bf16[576,256]{1,0:T(8,128)(2,1)S(1)}, bf16[576,256]{1,0:T(8,128)(2,1)S(1)}, u32[]{:S(2)}, u32[]{:S(2)}) collective-permute-start(bf16[576,256]{1,0:T(8,128)(2,1)S(1)} %pack.1.refs_1_.refs_2_), channel_id=1, source_target_pairs={{0,4},{4,0},{1,5},{5,1},{2,6},{6,2},{3,7},{7,3},{8,12},{12,8},{9,1... | collective-permute-start | bytes 884744 | tf_op jit(solution)/shard_map/fetch_points/ppermute | solution.py:48
  2.6 16.7 %collective-permute-start.3 = (bf16[576,256]{1,0:T(8,128)(2,1)S(1)}, bf16[576,256]{1,0:T(8,128)(2,1)S(1)}, u32[]{:S(2)}, u32[]{:S(2)}) collective-permute-start(bf16[576,256]{1,0:T(8,128)(2,1)S(1)} %pack.1.refs_1_.refs_2_), channel_id=1, source_target_pairs={{0,24},{8,16},{16,8},{24,0},{32,56},{40,48},{48,40},{56,32},{64,88... | collective-permute-start | bytes 884744 | tf_op jit(solution)/shard_map/fetch_points/ppermute | solution.py:29
  6.8 12.5 %collective-permute-start.2 = (bf16[576,256]{1,0:T(8,128)(2,1)S(1)}, bf16[576,256]{1,0:T(8,128)(2,1)S(1)}, u32[]{:S(2)}, u32[]{:S(2)}) collective-permute-start(bf16[576,256]{1,0:T(8,128)(2,1)S(1)} %pack.1.refs_1_.refs_2_), channel_id=1, source_target_pairs={{0,96},{8,104},{16,112},{24,120},{32,64},{40,72},{48,80},{56,88},{... | collective-permute-start | bytes 884744 | tf_op jit(solution)/shard_map/fetch_points/ppermute | solution.py:29
  9.8 8.1 %collective-permute-start.1 = (bf16[512,256]{1,0:T(8,128)(2,1)S(1)}, bf16[512,256]{1,0:T(8,128)(2,1)S(1)}, u32[]{:S(2)}, u32[]{:S(2)}) collective-permute-start(bf16[512,256]{1,0:T(8,128)(2,1)S(1)} %constant_dynamic-slice_fusion.points_ref.refs_0_), channel_id=1, source_target_pairs={{0,8},{8,0},{16,24},{24,16},{32,40},{40,32},{48,56},{56,48},{64,72... | collective-permute-start | bytes 786440 | tf_op jit(solution)/shard_map/fetch_points/ppermute | solution.py:29
  9.8 8.1 %collective-permute-start = (bf16[512,256]{1,0:T(8,128)(2,1)S(1)}, bf16[512,256]{1,0:T(8,128)(2,1)S(1)}, u32[]{:S(2)}, u32[]{:S(2)}) collective-permute-start(bf16[512,256]{1,0:T(8,128)(2,1)S(1)} %constant_dynamic-slice_fusion.points_ref.refs_0_), channel_id=1, source_target_pairs={{0,32},{8,40},{16,48},{24,56},{32,0},{40,8},{48,16},{56,24},{64,96... | collective-permute-start | bytes 786440 | tf_op jit(solution)/shard_map/fetch_points/ppermute | solution.py:29
  9.9 0.8 %copy-start.1 = (f32[512,16]{0,1:T(8,128)S(1)}, f32[512,16]{0,1:T(8,128)}, u32[]{:S(2)}) copy-start(f32[512,16]{0,1:T(8,128)} %param.5) | copy-start | bytes 98308
  19.4 11.8 %collective-permute-start.8 = (bf16[576,256]{1,0:T(8,128)(2,1)S(1)}, bf16[576,256]{1,0:T(8,128)(2,1)S(1)}, u32[]{:S(2)}, u32[]{:S(2)}) collective-permute-start(bf16[576,256]{1,0:T(8,128)(2,1)S(1)} %broadcast_select_fusion), channel_id=1, source_target_pairs={{0,96},{4,28},{8,104},{12,20},{16,112},{20,12},{24,120},{28,4},{32... | collective-permute-start | bytes 884744 | tf_op jit(solution)/shard_map/fetch_points/ppermute | solution.py:44
  22.1 1.6 %collective-permute-start.6 = (bf16[576,256]{1,0:T(8,128)(2,1)S(1)}, bf16[576,256]{1,0:T(8,128)(2,1)S(1)}, u32[]{:S(2)}, u32[]{:S(2)}) collective-permute-start(bf16[576,256]{1,0:T(8,128)(2,1)S(1)} %collective-permute-done.2.refs_3_), channel_id=1, source_target_pairs={{0,4},{4,0},{1,5},{5,1},{2,6},{6,2},{3,7},{7,3},{8,12},{12,8},{9,1... | collective-permute-start | bytes 884744 | tf_op jit(solution)/shard_map/build_tiles/ppermute | solution.py:48
  22.1 2.0 %collective-permute-start.7 = (bf16[576,256]{1,0:T(8,128)(2,1)S(1)}, bf16[576,256]{1,0:T(8,128)(2,1)S(1)}, u32[]{:S(2)}, u32[]{:S(2)}) collective-permute-start(bf16[576,256]{1,0:T(8,128)(2,1)S(1)} %collective-permute-done.3.refs_4_), channel_id=1, source_target_pairs={{0,4},{4,0},{1,5},{5,1},{2,6},{6,2},{3,7},{7,3},{8,12},{12,8},{9,1... | collective-permute-start | bytes 884744 | tf_op jit(solution)/shard_map/build_tiles/ppermute | solution.py:48
  22.6 6.5 %collective-permute-start.5 = (bf16[512,256]{1,0:T(8,128)(2,1)S(1)}, bf16[512,256]{1,0:T(8,128)(2,1)S(1)}, u32[]{:S(2)}, u32[]{:S(2)}) collective-permute-start(bf16[512,256]{1,0:T(8,128)(2,1)S(1)} %broadcast_select_fusion.1), channel_id=1, source_target_pairs={{0,32},{4,12},{8,40},{12,4},{16,48},{20,28},{24,56},{28,20},{32,0}... | collective-permute-start | bytes 786440 | tf_op jit(solution)/shard_map/fetch_points/ppermute | solution.py:44
  31.1 1.8 %collective-permute-start.9 = (bf16[576,256]{1,0:T(8,128)(2,1)S(1)}, bf16[576,256]{1,0:T(8,128)(2,1)S(1)}, u32[]{:S(2)}, u32[]{:S(2)}) collective-permute-start(bf16[576,256]{1,0:T(8,128)(2,1)S(1)} %collective-permute-done.8.refs_4_), channel_id=1, source_target_pairs={{0,4},{4,0},{1,5},{5,1},{2,6},{6,2},{3,7},{7,3},{8,12},{12,8},{9,1... | collective-permute-start | bytes 884744 | tf_op jit(solution)/shard_map/build_tiles/ppermute | solution.py:48
  34.3 5.3 %collective-permute-start.10 = (bf16[80,512]{1,0:T(8,128)(2,1)S(1)}, bf16[80,512]{1,0:T(8,128)(2,1)S(1)}, u32[]{:S(2)}, u32[]{:S(2)}) collective-permute-start(bf16[80,512]{1,0:T(8,128)(2,1)S(1)} %get-tuple-element.70), channel_id=1, source_target_pairs={{0,32},{8,40},{16,48},{24,56},{32,0},{40,8},{48,16},{56,24},{64,96... | collective-permute-start | bytes 245768 | tf_op jit(solution)/shard_map/sum_over_rows/ppermute | solution.py:29
  34.4 5.2 %collective-permute-start.11 = (bf16[80,512]{1,0:T(8,128)(2,1)S(1)}, bf16[80,512]{1,0:T(8,128)(2,1)S(1)}, u32[]{:S(2)}, u32[]{:S(2)}) collective-permute-start(bf16[80,512]{1,0:T(8,128)(2,1)S(1)} %get-tuple-element.71), channel_id=1, source_target_pairs={{0,8},{8,0},{16,24},{24,16},{32,40},{40,32},{48,56},{56,48},{64,72... | collective-permute-start | bytes 245768 | tf_op jit(solution)/shard_map/sum_over_rows/ppermute | solution.py:29
  36.0 5.5 %collective-permute-start.12 = (bf16[80,512]{1,0:T(8,128)(2,1)S(1)}, bf16[80,512]{1,0:T(8,128)(2,1)S(1)}, u32[]{:S(2)}, u32[]{:S(2)}) collective-permute-start(bf16[80,512]{1,0:T(8,128)(2,1)S(1)} %get-tuple-element.72), channel_id=1, source_target_pairs={{0,40},{8,32},{16,56},{24,48},{32,8},{40,0},{48,24},{56,16},{64,10... | collective-permute-start | bytes 245768 | tf_op jit(solution)/shard_map/sum_over_rows/ppermute | solution.py:29
  43.1 12.0 %copy-start.2 = (f32[512,16]{0,1:T(8,128)S(1)}, f32[512,16]{0,1:T(8,128)}, u32[]{:S(2)}) copy-start(f32[512,16]{0,1:T(8,128)} %param.5) | copy-start | bytes 98308
  43.1 1.5 %collective-permute-start.13 = (f32[16,2048]{1,0:T(8,128)S(1)}, f32[16,2048]{1,0:T(8,128)S(1)}, u32[]{:S(2)}, u32[]{:S(2)}) collective-permute-start(f32[16,2048]{1,0:T(8,128)S(1)} %second_product.2), channel_id=1, source_target_pairs={{0,4},{4,0},{1,5},{5,1},{2,6},{6,2},{3,7},{7,3},{8,12},{12,8},{9,1... | collective-permute-start | bytes 393224 | tf_op jit(solution)/shard_map/sum_over_columns/ppermute | solution.py:48
  44.6 6.0 %collective-permute-start.14 = (f32[16,512]{1,0:T(8,128)S(1)}, f32[16,512]{1,0:T(8,128)S(1)}, u32[]{:S(2)}, u32[]{:S(2)}) collective-permute-start(f32[16,512]{1,0:T(8,128)S(1)} %get-tuple-element.85), channel_id=1, source_target_pairs={{0,96},{8,104},{16,112},{24,120},{32,64},{40,72},{48,80},{56,88},{... | collective-permute-start | bytes 98312 | tf_op jit(solution)/shard_map/sum_over_columns/ppermute | solution.py:29
  47.6 5.1 %collective-permute-start.15 = (f32[16,512]{1,0:T(8,128)S(1)}, f32[16,512]{1,0:T(8,128)S(1)}, u32[]{:S(2)}, u32[]{:S(2)}) collective-permute-start(f32[16,512]{1,0:T(8,128)S(1)} %get-tuple-element.86), channel_id=1, source_target_pairs={{0,24},{8,16},{16,8},{24,0},{32,56},{40,48},{48,40},{56,32},{64,88... | collective-permute-start | bytes 98312 | tf_op jit(solution)/shard_map/sum_over_columns/ppermute | solution.py:29
  47.9 7.2 %collective-permute-start.16 = (f32[16,512]{1,0:T(8,128)S(1)}, f32[16,512]{1,0:T(8,128)S(1)}, u32[]{:S(2)}, u32[]{:S(2)}) collective-permute-start(f32[16,512]{1,0:T(8,128)S(1)} %get-tuple-element.87), channel_id=1, source_target_pairs={{0,120},{8,112},{16,104},{24,96},{32,88},{40,80},{48,72},{56,64},{... | collective-permute-start | bytes 98312 | tf_op jit(solution)/shard_map/sum_over_columns/ppermute | solution.py:29

commit v15 on v13

--- a/solution.py
+++ b/solution.py
@@ -12,8 +12,8 @@
 LANES = 128
 CHUNK = 256
 HERE = (0, 0)
-ROWS = (HERE, (1, 0), (0, 1), (1, 1))
-SQUARE = (HERE, (3, 0), (0, 3), (3, 3))
+ROWS = (HERE, (1, 0), (0, 3), (1, 3))
+SQUARE = (HERE, (3, 0), (0, 1), (3, 1))
 COLS = ((0, 0), (1, 0), (0, 1), (0, 2), (1, 1), (1, 2), (0, 3), (1, 3))
 
 noise_level = 1.0

time: 67.4 us -> 67.2 us (level)
  waiting for transfers between devices: 17.4 us -> 15.3 us
  starting transfers between devices: 18.6 us -> 19.8 us
  blocking collectives: 11.8 us -> 12.5 us
    ppermute x10, waiting for transfers between devices: 14.6 us -> 13.1 us  [swap(): return lax.ppermute(value, ('y', 'z'), pairs)]
    ppermute x5, starting transfers between devices: 0.88 us -> 1.78 us  [swap_core(): return lax.ppermute(value, 'c', [(0, 1), (1, 0)])]
  transfers between devices with their start and end apart: 17 -> 17, of which waited for: 7 -> 8; matrix products, arithmetic and copies ran while one was open for 0% -> 0% of each run, Pallas kernels for 17% -> 17%
where the time goes in v15:
time: 67.2 us; the launch traced here: 66.2 us
  starting transfers between devices  19.8 us (29%)
  Pallas kernels  15.5 us (23%)
  waiting for transfers between devices  15.3 us (23%)
  blocking collectives  12.5 us (19%)
  between operations  1.45 us (2%)
  local copies, waits for them, and re-layouts  0.85 us (1%)
  other arithmetic  0.83 us (1%)
    ppermute x10, starting transfers between devices, swap(): return lax.ppermute(value, ('y', 'z'), pairs)  17.3 us
    ppermute x10, waiting for transfers between devices, swap(): return lax.ppermute(value, ('y', 'z'), pairs)  13.1 us
    all_to_all x1, blocking collectives, on_device(): sums = lax.all_to_all(sums, ('y', 'z', 'c'), 0, 0, tiled=True)  12.5 us
    pallas_call x7, Pallas kernels, build(): pl.pallas_call(functools.partial(tile_kernel, counts, probes), out_shape=...  10.9 us
    pallas_call x2, Pallas kernels, second_product(): pl.pallas_call(functools.partial(second_kernel, own, half, places), in_sp...  2.9 us
    ppermute x2, waiting for transfers between devices, hand_on(): return lax.ppermute(value, ('y', 'z', 'c'), pairs)  2.2 us
    ppermute x5, starting transfers between devices, swap_core(): return lax.ppermute(value, 'c', [(0, 1), (1, 0)])  1.78 us
  transfers between devices with their start and end apart: 17, of which 8 were waited for; matrix products, arithmetic and copies ran while one was open for 0% of the time, Pallas kernels for 17%

profile of v15, /device:TPU:0, one launch (start us, length us, event | category | flops | bytes accessed | tf_op | source)
XLA Modules:
  0.0 66.2 jit_solution(1613741493116142821)
XLA Ops:
  1.3 0.8 %bitcast_convert_fusion.side_ref = bf16[16,512]{1,0:T(8,128)(2,1)S(1)} fusion(f32[512,16]{0,1:T(8,128)} %param.5), kind=kLoop, calls=%fused_computation.3 | loop fusion | flops 8192 | bytes 49152 | tf_op jit(solution)/shard_map/fetch_points/convert_element_type | solution.py:328
  2.6 2.1 %collective-permute-start.3 = (bf16[576,256]{1,0:T(8,128)(2,1)S(1)}, bf16[576,256]{1,0:T(8,128)(2,1)S(1)}, u32[]{:S(2)}, u32[]{:S(2)}) collective-permute-start(bf16[576,256]{1,0:T(8,128)(2,1)S(1)} %pack.1.refs_1_.refs_2_), channel_id=1, source_target_pairs={{0,8},{8,0},{16,24},{24,16},{32,40},{40,32},{48,56},{56,48},{64,72... | collective-permute-start | bytes 884744 | tf_op jit(solution)/shard_map/fetch_points/ppermute | solution.py:29
  4.6 3.0 %collective-permute-start.2 = (bf16[576,256]{1,0:T(8,128)(2,1)S(1)}, bf16[576,256]{1,0:T(8,128)(2,1)S(1)}, u32[]{:S(2)}, u32[]{:S(2)}) collective-permute-start(bf16[576,256]{1,0:T(8,128)(2,1)S(1)} %pack.1.refs_1_.refs_2_), channel_id=1, source_target_pairs={{0,96},{8,104},{16,112},{24,120},{32,64},{40,72},{48,80},{56,88},{... | collective-permute-start | bytes 884744 | tf_op jit(solution)/shard_map/fetch_points/ppermute | solution.py:29
  7.7 2.5 %collective-permute-start.1 = (bf16[512,256]{1,0:T(8,128)(2,1)S(1)}, bf16[512,256]{1,0:T(8,128)(2,1)S(1)}, u32[]{:S(2)}, u32[]{:S(2)}) collective-permute-start(bf16[512,256]{1,0:T(8,128)(2,1)S(1)} %constant_dynamic-slice_fusion.points_ref.refs_0_), channel_id=1, source_target_pairs={{0,24},{8,16},{16,8},{24,0},{32,56},{40,48},{48,40},{56,32},{64,88... | collective-permute-start | bytes 786440 | tf_op jit(solution)/shard_map/fetch_points/ppermute | solution.py:29
  10.3 0.8 %copy-done.1 = f32[512,16]{0,1:T(8,128)S(1)} copy-done((f32[512,16]{0,1:T(8,128)S(1)}, f32[512,16]{0,1:T(8,128)}, u32[]{:S(2)}) %copy-start.1) | copy-done | bytes 32792
  11.1 0.8 %build_tile.7 = (bf16[512,1024]{1,0:T(8,128)(2,1)S(1)}, f32[16,512]{1,0:T(8,128)S(1)}, f32[512,1]{1,0:T(8,128)S(1)}) custom-call(bf16[512,256]{1,0:T(8,128)(2,1)S(1)} %constant_dynamic-slice_fusion.points_ref.refs_0_, bf16[576,256]{1,0:T(8,128)(2,1)S(1)} %pack.1.refs_1_.refs_2_, bf16[576,256]{1,0:T(8,128)(2,1)S(1)} %collective-permute-done.4.refs_2_.refs_3_, ...), custom_call_target="tpu_custom_call" | custom-call | flops 16777216 | bytes 1024 | tf_op jit(solution)/shard_map/fetch_points/build_tile/pallas_call | solution.py:155
  11.9 5.0 %collective-permute-done.1.refs_1_.refs_2_ = bf16[512,256]{1,0:T(8,128)(2,1)S(1)} collective-permute-done((bf16[512,256]{1,0:T(8,128)(2,1)S(1)}, bf16[512,256]{1,0:T(8,128)(2,1)S(1)}, u32[]{:S(2)}, u32[]{:S(2)}) %collective-permute-start.1) | collective-permute-done | bytes 262176 | tf_op jit(solution)/shard_map/fetch_points/ppermute | solution.py:29
  17.0 1.0 %collective-permute-done.refs_0_.refs_1_ = bf16[512,256]{1,0:T(8,128)(2,1)S(1)} collective-permute-done((bf16[512,256]{1,0:T(8,128)(2,1)S(1)}, bf16[512,256]{1,0:T(8,128)(2,1)S(1)}, u32[]{:S(2)}, u32[]{:S(2)}) %collective-permute-start) | collective-permute-done | bytes 262176 | tf_op jit(solution)/shard_map/fetch_points/ppermute | solution.py:29
  18.0 1.4 %build_tile.8 = (bf16[1024,1024]{1,0:T(8,128)(2,1)S(1)}, f32[16,1024]{1,0:T(8,128)S(1)}, f32[1024,1]{1,0:T(8,128)S(1)}) custom-call(bf16[512,256]{1,0:T(8,128)(2,1)S(1)} %collective-permute-done.refs_0_.refs_1_, bf16[512,256]{1,0:T(8,128)(2,1)S(1)} %collective-permute-done.1.refs_1_.refs_2_, bf16[576,256]{1,0:T(8,128)(2,1)S(1)} %pack.1.refs_1_.refs_2_, ...), custom_call_target="tpu_custom_call" | custom-call | flops 33554432 | bytes 1024 | tf_op jit(solution)/shard_map/fetch_points/build_tile/pallas_call | solution.py:155
  19.5 0.5 collective-permute-start.7
  20.1 0.4 collective-permute-start.8
  20.5 0.4 collective-permute-start.5
  20.8 1.9 %build_tile.9 = (bf16[1536,1024]{1,0:T(8,128)(2,1)S(1)}, f32[16,1536]{1,0:T(8,128)S(1)}) custom-call(bf16[512,256]{1,0:T(8,128)(2,1)S(1)} %constant_dynamic-slice_fusion.points_ref.refs_0_, bf16[512,256]{1,0:T(8,128)(2,1)S(1)} %collective-permute-done.refs_0_.refs_1_, bf16[512,256]{1,0:T(8,128)(2,1)S(1)} %collective-permute-done.1.refs_1_.refs_2_, ...), custom_call_target="tpu_custom_call" | custom-call | flops 50331648 | bytes 1024 | tf_op jit(solution)/shard_map/build_tiles/build_tile/pallas_call | solution.py:155
  22.8 1.9 %build_tile.10 = (bf16[1536,1024]{1,0:T(8,128)(2,1)S(1)}, f32[16,1536]{1,0:T(8,128)S(1)}) custom-call(bf16[512,256]{1,0:T(8,128)(2,1)S(1)} %constant_dynamic-slice_fusion.points_ref.refs_0_, bf16[512,256]{1,0:T(8,128)(2,1)S(1)} %collective-permute-done.refs_0_.refs_1_, bf16[512,256]{1,0:T(8,128)(2,1)S(1)} %collective-permute-done.1.refs_1_.refs_2_, ...), custom_call_target="tpu_custom_call" | custom-call | flops 50331648 | bytes 1024 | tf_op jit(solution)/shard_map/build_tiles/build_tile/pallas_call | solution.py:155
  24.7 2.2 %collective-permute-done.5.refs_0_.refs_3_ = bf16[512,256]{1,0:T(8,128)(2,1)S(1)} collective-permute-done((bf16[512,256]{1,0:T(8,128)(2,1)S(1)}, bf16[512,256]{1,0:T(8,128)(2,1)S(1)}, u32[]{:S(2)}, u32[]{:S(2)}) %collective-permute-start.5) | collective-permute-done | bytes 262176 | tf_op jit(solution)/shard_map/fetch_points/ppermute | solution.py:44
  26.9 2.1 %build_tile.11 = (bf16[512,3072]{1,0:T(8,128)(2,1)S(1)}, f32[16,512]{1,0:T(8,128)S(1)}, f32[512,1]{1,0:T(8,128)S(1)}) custom-call(bf16[512,256]{1,0:T(8,128)(2,1)S(1)} %collective-permute-done.5.refs_0_.refs_3_, bf16[576,256]{1,0:T(8,128)(2,1)S(1)} %pack.1.refs_1_.refs_2_, bf16[576,256]{1,0:T(8,128)(2,1)S(1)} %collective-permute-done.4.refs_2_.refs_3_, ...), custom_call_target="tpu_custom_call" | custom-call | flops 50331648 | bytes 1024 | tf_op jit(solution)/shard_map/build_tiles/build_tile/pallas_call | solution.py:155
  29.0 1.1 %collective-permute-start.9 = (bf16[576,256]{1,0:T(8,128)(2,1)S(1)}, bf16[576,256]{1,0:T(8,128)(2,1)S(1)}, u32[]{:S(2)}, u32[]{:S(2)}) collective-permute-start(bf16[576,256]{1,0:T(8,128)(2,1)S(1)} %collective-permute-done.8.refs_4_), channel_id=1, source_target_pairs={{0,4},{4,0},{1,5},{5,1},{2,6},{6,2},{3,7},{7,3},{8,12},{12,8},{9,1... | collective-permute-start | bytes 884744 | tf_op jit(solution)/shard_map/build_tiles/ppermute | solution.py:48
  30.1 1.3 %build_tile.12 = (bf16[2048,512]{1,0:T(8,128)(2,1)S(1)}, f32[16,2048]{1,0:T(8,128)S(1)}) custom-call(bf16[512,256]{1,0:T(8,128)(2,1)S(1)} %constant_dynamic-slice_fusion.points_ref.refs_0_, bf16[512,256]{1,0:T(8,128)(2,1)S(1)} %collective-permute-done.refs_0_.refs_1_, bf16[512,256]{1,0:T(8,128)(2,1)S(1)} %collective-permute-done.1.refs_1_.refs_2_, ...), custom_call_target="tpu_custom_call" | custom-call | flops 33554432 | bytes 1024 | tf_op jit(solution)/shard_map/build_tiles/build_tile/pallas_call | solution.py:155
  31.4 1.4 %build_tile.13 = (bf16[2048,512]{1,0:T(8,128)(2,1)S(1)}, f32[16,2048]{1,0:T(8,128)S(1)}) custom-call(bf16[512,256]{1,0:T(8,128)(2,1)S(1)} %constant_dynamic-slice_fusion.points_ref.refs_0_, bf16[512,256]{1,0:T(8,128)(2,1)S(1)} %collective-permute-done.refs_0_.refs_1_, bf16[512,256]{1,0:T(8,128)(2,1)S(1)} %collective-permute-done.1.refs_1_.refs_2_, ...), custom_call_target="tpu_custom_call" | custom-call | flops 33554432 | bytes 1024 | tf_op jit(solution)/shard_map/build_tiles/build_tile/pallas_call | solution.py:155
  33.0 1.1 %collective-permute-start.11 = (bf16[80,512]{1,0:T(8,128)(2,1)S(1)}, bf16[80,512]{1,0:T(8,128)(2,1)S(1)}, u32[]{:S(2)}, u32[]{:S(2)}) collective-permute-start(bf16[80,512]{1,0:T(8,128)(2,1)S(1)} %get-tuple-element.65), channel_id=1, source_target_pairs={{0,24},{8,16},{16,8},{24,0},{32,56},{40,48},{48,40},{56,32},{64,88... | collective-permute-start | bytes 245768 | tf_op jit(solution)/shard_map/sum_over_rows/ppermute | solution.py:29
  34.1 3.6 %collective-permute-start.12 = (bf16[80,512]{1,0:T(8,128)(2,1)S(1)}, bf16[80,512]{1,0:T(8,128)(2,1)S(1)}, u32[]{:S(2)}, u32[]{:S(2)}) collective-permute-start(bf16[80,512]{1,0:T(8,128)(2,1)S(1)} %get-tuple-element.66), channel_id=1, source_target_pairs={{0,56},{8,48},{16,40},{24,32},{32,24},{40,16},{48,8},{56,0},{64,12... | collective-permute-start | bytes 245768 | tf_op jit(solution)/shard_map/sum_over_rows/ppermute | solution.py:29
  37.7 2.0 %collective-permute-done.11.refs_2_ = bf16[80,512]{1,0:T(8,128)(2,1)S(1)} collective-permute-done((bf16[80,512]{1,0:T(8,128)(2,1)S(1)}, bf16[80,512]{1,0:T(8,128)(2,1)S(1)}, u32[]{:S(2)}, u32[]{:S(2)}) %collective-permute-start.11) | collective-permute-done | bytes 81952 | tf_op jit(solution)/shard_map/sum_over_rows/ppermute | solution.py:29
  39.7 0.9 %collective-permute-done.12.refs_3_ = bf16[80,512]{1,0:T(8,128)(2,1)S(1)} collective-permute-done((bf16[80,512]{1,0:T(8,128)(2,1)S(1)}, bf16[80,512]{1,0:T(8,128)(2,1)S(1)}, u32[]{:S(2)}, u32[]{:S(2)}) %collective-permute-start.12) | collective-permute-done | bytes 81952 | tf_op jit(solution)/shard_map/sum_over_rows/ppermute | solution.py:29
  40.7 1.4 %second_product.2 = f32[16,2048]{1,0:T(8,128)S(1)} custom-call(bf16[32,2048]{1,0:T(8,128)(2,1)S(1)} %get-tuple-element.76.narrow_ref, bf16[512,1024]{1,0:T(8,128)(2,1)S(1)} %get-tuple-element.69.refs_0_, bf16[1024,1024]{1,0:T(8,128)(2,1)S(1)} %get-tuple-element.70.refs_1_, bf16[1536,1024]{1,0:T(8,128)(2,1)S(1)} %get-tuple-element.71.refs_2_, ...), custom_call_target="tpu_custom_call" | custom-call | flops 134217728 | bytes 1024 | tf_op jit(solution)/shard_map/second_product/pallas_call | solution.py:241
  42.1 1.5 %second_product.3.mine_ref = f32[16,2048]{1,0:T(8,128)S(1)} custom-call(bf16[32,2048]{1,0:T(8,128)(2,1)S(1)} %get-tuple-element.76.narrow_ref, bf16[512,1024]{1,0:T(8,128)(2,1)S(1)} %get-tuple-element.69.refs_0_, bf16[1024,1024]{1,0:T(8,128)(2,1)S(1)} %get-tuple-element.70.refs_1_, bf16[1536,1024]{1,0:T(8,128)(2,1)S(1)} %get-tuple-element.71.refs_2_, ...), custom_call_target="tpu_custom_call" | custom-call | flops 134217728 | bytes 1024 | tf_op jit(solution)/shard_map/second_product/pallas_call | solution.py:241
  43.6 2.8 %collective-permute-start.14 = (f32[16,512]{1,0:T(8,128)S(1)}, f32[16,512]{1,0:T(8,128)S(1)}, u32[]{:S(2)}, u32[]{:S(2)}) collective-permute-start(f32[16,512]{1,0:T(8,128)S(1)} %get-tuple-element.79), channel_id=1, source_target_pairs={{0,96},{8,104},{16,112},{24,120},{32,64},{40,72},{48,80},{56,88},{... | collective-permute-start | bytes 98312 | tf_op jit(solution)/shard_map/sum_over_columns/ppermute | solution.py:29
  46.4 2.0 %collective-permute-start.16 = (f32[16,512]{1,0:T(8,128)S(1)}, f32[16,512]{1,0:T(8,128)S(1)}, u32[]{:S(2)}, u32[]{:S(2)}) collective-permute-start(f32[16,512]{1,0:T(8,128)S(1)} %get-tuple-element.81), channel_id=1, source_target_pairs={{0,104},{8,96},{16,120},{24,112},{32,72},{40,64},{48,88},{56,80},{... | collective-permute-start | bytes 98312 | tf_op jit(solution)/shard_map/sum_over_columns/ppermute | solution.py:29
  48.4 0.4 collective-permute-done.14.refs_1_
  48.8 1.5 %collective-permute-done.15.refs_2_ = f32[16,512]{1,0:T(8,128)S(1)} collective-permute-done((f32[16,512]{1,0:T(8,128)S(1)}, f32[16,512]{1,0:T(8,128)S(1)}, u32[]{:S(2)}, u32[]{:S(2)}) %collective-permute-start.15) | collective-permute-done | bytes 32800 | tf_op jit(solution)/shard_map/sum_over_columns/ppermute | solution.py:29
  50.4 2.1 %collective-permute-done.16.refs_3_ = f32[16,512]{1,0:T(8,128)S(1)} collective-permute-done((f32[16,512]{1,0:T(8,128)S(1)}, f32[16,512]{1,0:T(8,128)S(1)}, u32[]{:S(2)}, u32[]{:S(2)}) %collective-permute-start.16) | collective-permute-done | bytes 32800 | tf_op jit(solution)/shard_map/sum_over_columns/ppermute | solution.py:29
  52.7 12.5 %all_to_all.8 = f32[32,1,128]{2,1,0:T(1,128)S(1)} all-to-all(f32[32,1,128]{2,1,0:T(1,128)S(1)} %broadcast_in_dim.2), channel_id=1, replica_groups=mesh['y'=4,'z'=4,'c'=2,'x'=4] {'y','z','c'}, dimensions={0} | all-to-all | bytes 32768 | tf_op jit(solution)/shard_map/final_sums/all_to_all | solution.py:377
  65.2 1.0 %finish.1 = (f32[16,512]{1,0:T(8,128)}, f32[16,512]{1,0:T(8,128)}) custom-call(f32[16,512]{1,0:T(8,128)S(1)} %bitcast.12, f32[16,512]{1,0:T(8,128)S(1)} %get-tuple-element.67.rho_ref, f32[16,512]{1,0:T(8,128)S(1)} %get-tuple-element.82.image_ref, f32[32,128]{1,0:T(8,128)S(1)} %bitcast.13), custom_call_target="tpu_custom_call" | custom-call | tf_op jit(solution)/shard_map/finish/pallas_call | solution.py:315
  (29 shorter events, 1.3 us)
Async XLA Ops:
  0.6 1.5 %copy-start = (bf16[1024,256]{1,0:T(8,128)(2,1)S(1)}, bf16[1024,256]{1,0:T(8,128)(2,1)}, u32[]{:S(2)}) copy-start(bf16[1024,256]{1,0:T(8,128)(2,1)} %param.3) | copy-start | bytes 1572868
  2.5 7.9 %collective-permute-start.4 = (bf16[576,256]{1,0:T(8,128)(2,1)S(1)}, bf16[576,256]{1,0:T(8,128)(2,1)S(1)}, u32[]{:S(2)}, u32[]{:S(2)}) collective-permute-start(bf16[576,256]{1,0:T(8,128)(2,1)S(1)} %pack.1.refs_1_.refs_2_), channel_id=1, source_target_pairs={{0,4},{4,0},{1,5},{5,1},{2,6},{6,2},{3,7},{7,3},{8,12},{12,8},{9,1... | collective-permute-start | bytes 884744 | tf_op jit(solution)/shard_map/fetch_points/ppermute | solution.py:48
  2.6 16.9 %collective-permute-start.3 = (bf16[576,256]{1,0:T(8,128)(2,1)S(1)}, bf16[576,256]{1,0:T(8,128)(2,1)S(1)}, u32[]{:S(2)}, u32[]{:S(2)}) collective-permute-start(bf16[576,256]{1,0:T(8,128)(2,1)S(1)} %pack.1.refs_1_.refs_2_), channel_id=1, source_target_pairs={{0,8},{8,0},{16,24},{24,16},{32,40},{40,32},{48,56},{56,48},{64,72... | collective-permute-start | bytes 884744 | tf_op jit(solution)/shard_map/fetch_points/ppermute | solution.py:29
  4.6 14.8 %collective-permute-start.2 = (bf16[576,256]{1,0:T(8,128)(2,1)S(1)}, bf16[576,256]{1,0:T(8,128)(2,1)S(1)}, u32[]{:S(2)}, u32[]{:S(2)}) collective-permute-start(bf16[576,256]{1,0:T(8,128)(2,1)S(1)} %pack.1.refs_1_.refs_2_), channel_id=1, source_target_pairs={{0,96},{8,104},{16,112},{24,120},{32,64},{40,72},{48,80},{56,88},{... | collective-permute-start | bytes 884744 | tf_op jit(solution)/shard_map/fetch_points/ppermute | solution.py:29
  7.7 9.3 %collective-permute-start.1 = (bf16[512,256]{1,0:T(8,128)(2,1)S(1)}, bf16[512,256]{1,0:T(8,128)(2,1)S(1)}, u32[]{:S(2)}, u32[]{:S(2)}) collective-permute-start(bf16[512,256]{1,0:T(8,128)(2,1)S(1)} %constant_dynamic-slice_fusion.points_ref.refs_0_), channel_id=1, source_target_pairs={{0,24},{8,16},{16,8},{24,0},{32,56},{40,48},{48,40},{56,32},{64,88... | collective-permute-start | bytes 786440 | tf_op jit(solution)/shard_map/fetch_points/ppermute | solution.py:29
  10.2 7.8 %collective-permute-start = (bf16[512,256]{1,0:T(8,128)(2,1)S(1)}, bf16[512,256]{1,0:T(8,128)(2,1)S(1)}, u32[]{:S(2)}, u32[]{:S(2)}) collective-permute-start(bf16[512,256]{1,0:T(8,128)(2,1)S(1)} %constant_dynamic-slice_fusion.points_ref.refs_0_), channel_id=1, source_target_pairs={{0,32},{8,40},{16,48},{24,56},{32,0},{40,8},{48,16},{56,24},{64,96... | collective-permute-start | bytes 786440 | tf_op jit(solution)/shard_map/fetch_points/ppermute | solution.py:29
  10.3 0.8 %copy-start.1 = (f32[512,16]{0,1:T(8,128)S(1)}, f32[512,16]{0,1:T(8,128)}, u32[]{:S(2)}) copy-start(f32[512,16]{0,1:T(8,128)} %param.5) | copy-start | bytes 98308
  19.4 3.3 %collective-permute-start.6 = (bf16[576,256]{1,0:T(8,128)(2,1)S(1)}, bf16[576,256]{1,0:T(8,128)(2,1)S(1)}, u32[]{:S(2)}, u32[]{:S(2)}) collective-permute-start(bf16[576,256]{1,0:T(8,128)(2,1)S(1)} %collective-permute-done.2.refs_3_), channel_id=1, source_target_pairs={{0,4},{4,0},{1,5},{5,1},{2,6},{6,2},{3,7},{7,3},{8,12},{12,8},{9,1... | collective-permute-start | bytes 884744 | tf_op jit(solution)/shard_map/build_tiles/ppermute | solution.py:48
  19.5 3.2 %collective-permute-start.7 = (bf16[576,256]{1,0:T(8,128)(2,1)S(1)}, bf16[576,256]{1,0:T(8,128)(2,1)S(1)}, u32[]{:S(2)}, u32[]{:S(2)}) collective-permute-start(bf16[576,256]{1,0:T(8,128)(2,1)S(1)} %collective-permute-done.3.refs_4_), channel_id=1, source_target_pairs={{0,4},{4,0},{1,5},{5,1},{2,6},{6,2},{3,7},{7,3},{8,12},{12,8},{9,1... | collective-permute-start | bytes 884744 | tf_op jit(solution)/shard_map/build_tiles/ppermute | solution.py:48
  20.1 8.9 %collective-permute-start.8 = (bf16[576,256]{1,0:T(8,128)(2,1)S(1)}, bf16[576,256]{1,0:T(8,128)(2,1)S(1)}, u32[]{:S(2)}, u32[]{:S(2)}) collective-permute-start(bf16[576,256]{1,0:T(8,128)(2,1)S(1)} %broadcast_select_fusion), channel_id=1, source_target_pairs={{0,96},{4,12},{8,104},{12,4},{16,112},{20,28},{24,120},{28,20},{32... | collective-permute-start | bytes 884744 | tf_op jit(solution)/shard_map/fetch_points/ppermute | solution.py:44
  20.5 6.5 %collective-permute-start.5 = (bf16[512,256]{1,0:T(8,128)(2,1)S(1)}, bf16[512,256]{1,0:T(8,128)(2,1)S(1)}, u32[]{:S(2)}, u32[]{:S(2)}) collective-permute-start(bf16[512,256]{1,0:T(8,128)(2,1)S(1)} %broadcast_select_fusion.1), channel_id=1, source_target_pairs={{0,32},{4,28},{8,40},{12,20},{16,48},{20,12},{24,56},{28,4},{32,0}... | collective-permute-start | bytes 786440 | tf_op jit(solution)/shard_map/fetch_points/ppermute | solution.py:44
  29.0 2.4 %collective-permute-start.9 = (bf16[576,256]{1,0:T(8,128)(2,1)S(1)}, bf16[576,256]{1,0:T(8,128)(2,1)S(1)}, u32[]{:S(2)}, u32[]{:S(2)}) collective-permute-start(bf16[576,256]{1,0:T(8,128)(2,1)S(1)} %collective-permute-done.8.refs_4_), channel_id=1, source_target_pairs={{0,4},{4,0},{1,5},{5,1},{2,6},{6,2},{3,7},{7,3},{8,12},{12,8},{9,1... | collective-permute-start | bytes 884744 | tf_op jit(solution)/shard_map/build_tiles/ppermute | solution.py:48
  32.9 4.8 %collective-permute-start.10 = (bf16[80,512]{1,0:T(8,128)(2,1)S(1)}, bf16[80,512]{1,0:T(8,128)(2,1)S(1)}, u32[]{:S(2)}, u32[]{:S(2)}) collective-permute-start(bf16[80,512]{1,0:T(8,128)(2,1)S(1)} %get-tuple-element.64), channel_id=1, source_target_pairs={{0,32},{8,40},{16,48},{24,56},{32,0},{40,8},{48,16},{56,24},{64,96... | collective-permute-start | bytes 245768 | tf_op jit(solution)/shard_map/sum_over_rows/ppermute | solution.py:29
  33.0 6.7 %collective-permute-start.11 = (bf16[80,512]{1,0:T(8,128)(2,1)S(1)}, bf16[80,512]{1,0:T(8,128)(2,1)S(1)}, u32[]{:S(2)}, u32[]{:S(2)}) collective-permute-start(bf16[80,512]{1,0:T(8,128)(2,1)S(1)} %get-tuple-element.65), channel_id=1, source_target_pairs={{0,24},{8,16},{16,8},{24,0},{32,56},{40,48},{48,40},{56,32},{64,88... | collective-permute-start | bytes 245768 | tf_op jit(solution)/shard_map/sum_over_rows/ppermute | solution.py:29
  34.1 6.6 %collective-permute-start.12 = (bf16[80,512]{1,0:T(8,128)(2,1)S(1)}, bf16[80,512]{1,0:T(8,128)(2,1)S(1)}, u32[]{:S(2)}, u32[]{:S(2)}) collective-permute-start(bf16[80,512]{1,0:T(8,128)(2,1)S(1)} %get-tuple-element.66), channel_id=1, source_target_pairs={{0,56},{8,48},{16,40},{24,32},{32,24},{40,16},{48,8},{56,0},{64,12... | collective-permute-start | bytes 245768 | tf_op jit(solution)/shard_map/sum_over_rows/ppermute | solution.py:29
  42.1 10.4 %copy-start.2 = (f32[512,16]{0,1:T(8,128)S(1)}, f32[512,16]{0,1:T(8,128)}, u32[]{:S(2)}) copy-start(f32[512,16]{0,1:T(8,128)} %param.5) | copy-start | bytes 98308
  42.1 1.5 %collective-permute-start.13 = (f32[16,2048]{1,0:T(8,128)S(1)}, f32[16,2048]{1,0:T(8,128)S(1)}, u32[]{:S(2)}, u32[]{:S(2)}) collective-permute-start(f32[16,2048]{1,0:T(8,128)S(1)} %second_product.2), channel_id=1, source_target_pairs={{0,4},{4,0},{1,5},{5,1},{2,6},{6,2},{3,7},{7,3},{8,12},{12,8},{9,1... | collective-permute-start | bytes 393224 | tf_op jit(solution)/shard_map/sum_over_columns/ppermute | solution.py:48
  43.6 5.2 %collective-permute-start.14 = (f32[16,512]{1,0:T(8,128)S(1)}, f32[16,512]{1,0:T(8,128)S(1)}, u32[]{:S(2)}, u32[]{:S(2)}) collective-permute-start(f32[16,512]{1,0:T(8,128)S(1)} %get-tuple-element.79), channel_id=1, source_target_pairs={{0,96},{8,104},{16,112},{24,120},{32,64},{40,72},{48,80},{56,88},{... | collective-permute-start | bytes 98312 | tf_op jit(solution)/shard_map/sum_over_columns/ppermute | solution.py:29
  46.4 3.9 %collective-permute-start.15 = (f32[16,512]{1,0:T(8,128)S(1)}, f32[16,512]{1,0:T(8,128)S(1)}, u32[]{:S(2)}, u32[]{:S(2)}) collective-permute-start(f32[16,512]{1,0:T(8,128)S(1)} %get-tuple-element.80), channel_id=1, source_target_pairs={{0,8},{8,0},{16,24},{24,16},{32,40},{40,32},{48,56},{56,48},{64,72... | collective-permute-start | bytes 98312 | tf_op jit(solution)/shard_map/sum_over_columns/ppermute | solution.py:29
  46.4 6.0 %collective-permute-start.16 = (f32[16,512]{1,0:T(8,128)S(1)}, f32[16,512]{1,0:T(8,128)S(1)}, u32[]{:S(2)}, u32[]{:S(2)}) collective-permute-start(f32[16,512]{1,0:T(8,128)S(1)} %get-tuple-element.81), channel_id=1, source_target_pairs={{0,104},{8,96},{16,120},{24,112},{32,72},{40,64},{48,88},{56,80},{... | collective-permute-start | bytes 98312 | tf_op jit(solution)/shard_map/sum_over_columns/ppermute | solution.py:29

commit v16 on v13

--- a/solution.py
+++ b/solution.py
@@ -157,7 +157,7 @@
         out_shape=out_shape,
         compiler_params=pltpu.CompilerParams(vmem_limit_bytes=8 << 20),
         cost_estimate=pl.CostEstimate(
-            flops=height * width * features // 8, bytes_accessed=1 << 10, transcendentals=0
+            flops=height * width * features * 8, bytes_accessed=1 << 10, transcendentals=0
         ),
         name="build_tile",
     )(*args)
@@ -326,7 +326,7 @@
     points = lax.dynamic_slice_in_dim(states, offsets[0], own, 0)
     with jax.named_scope("fetch_points"):
         message = pack(points, side.astype(jnp.bfloat16))
-        rows = [points] + [swap(points, offset) for offset in ROWS[1:3]]
+        rows = [points] + [swap(points, offset) for offset in ROWS[1:]]
         cols = [message] + [swap(message, offset) for offset in SQUARE[1:3]]
         first = [message, swap_core(message)]
         tile_a, image_a, half_a = build([points], first, own, probes, side=side)
@@ -335,7 +335,6 @@
             ((rows[1], rows[2], cols[1], cols[2]), image_a, image_b)
         )
         cols.append(hand_on(cols[1], cols[2], SQUARE[3]))
-        rows.append(hand_on(rows[1], rows[2], ROWS[3]))
 
     with jax.named_scope("build_tiles"):
         half = [half_a, half_b]

time: 67.4 us -> 66.4 us (0.985)
  waiting for transfers between devices: 17.4 us -> 10.7 us
  starting transfers between devices: 18.6 us -> 24.1 us
    ppermute x10 -> x11, waiting for transfers between devices: 14.6 us -> 10.4 us  [swap(): return lax.ppermute(value, ('y', 'z'), pairs)]
    ppermute x10 -> x11, starting transfers between devices: 16.9 us -> 20.2 us  [swap(): return lax.ppermute(value, ('y', 'z'), pairs)]
    ppermute x2 -> x1, waiting for transfers between devices: 2.49 us -> 0.01 us  [hand_on(): return lax.ppermute(value, ('y', 'z', 'c'), pairs)]
    ppermute x2 -> x1, starting transfers between devices: 0.82 us -> 3.03 us  [hand_on(): return lax.ppermute(value, ('y', 'z', 'c'), pairs)]
where the time goes in v16:
time: 66.4 us; the launch traced here: 65.4 us
  starting transfers between devices  24.1 us (36%)
  Pallas kernels  15.4 us (23%)
  blocking collectives  12.1 us (18%)
  waiting for transfers between devices  10.7 us (16%)
  between operations  1.46 us (2%)
  local copies, waits for them, and re-layouts  0.85 us (1%)
  other arithmetic  0.8 us (1%)
    ppermute x11, starting transfers between devices, swap(): return lax.ppermute(value, ('y', 'z'), pairs)  20.2 us
    all_to_all x1, blocking collectives, on_device(): sums = lax.all_to_all(sums, ('y', 'z', 'c'), 0, 0, tiled=True)  12.1 us
    pallas_call x7, Pallas kernels, build(): pl.pallas_call(functools.partial(tile_kernel, counts, probes), out_shape=...  10.8 us
    ppermute x11, waiting for transfers between devices, swap(): return lax.ppermute(value, ('y', 'z'), pairs)  10.4 us
    ppermute x1, starting transfers between devices, hand_on(): return lax.ppermute(value, ('y', 'z', 'c'), pairs)  3.03 us
    pallas_call x2, Pallas kernels, second_product(): pl.pallas_call(functools.partial(second_kernel, own, half, places), in_sp...  2.9 us
  transfers between devices with their start and end apart: 17, of which 7 were waited for; matrix products, arithmetic and copies ran while one was open for 0% of the time, Pallas kernels for 17%

profile of v16, /device:TPU:0, one launch (start us, length us, event | category | flops | bytes accessed | tf_op | source)
XLA Modules:
  0.0 65.4 jit_solution(4720680713264821834)
XLA Ops:
  1.3 0.8 %bitcast_convert_fusion.side_ref = bf16[16,512]{1,0:T(8,128)(2,1)S(1)} fusion(f32[512,16]{0,1:T(8,128)} %param.5), kind=kLoop, calls=%fused_computation.2 | loop fusion | flops 8192 | bytes 49152 | tf_op jit(solution)/shard_map/fetch_points/convert_element_type | solution.py:328
  2.2 0.3 pack.1.refs_1_.refs_2_
  2.6 2.1 %collective-permute-start.1 = (bf16[512,256]{1,0:T(8,128)(2,1)S(1)}, bf16[512,256]{1,0:T(8,128)(2,1)S(1)}, u32[]{:S(2)}, u32[]{:S(2)}) collective-permute-start(bf16[512,256]{1,0:T(8,128)(2,1)S(1)} %constant_dynamic-slice_fusion.points_ref.refs_0_), channel_id=1, source_target_pairs={{0,8},{8,0},{16,24},{24,16},{32,40},{40,32},{48,56},{56,48},{64,72... | collective-permute-start | bytes 786440 | tf_op jit(solution)/shard_map/fetch_points/ppermute | solution.py:29
  4.6 1.6 %collective-permute-start = (bf16[512,256]{1,0:T(8,128)(2,1)S(1)}, bf16[512,256]{1,0:T(8,128)(2,1)S(1)}, u32[]{:S(2)}, u32[]{:S(2)}) collective-permute-start(bf16[512,256]{1,0:T(8,128)(2,1)S(1)} %constant_dynamic-slice_fusion.points_ref.refs_0_), channel_id=1, source_target_pairs={{0,32},{8,40},{16,48},{24,56},{32,0},{40,8},{48,16},{56,24},{64,96... | collective-permute-start | bytes 786440 | tf_op jit(solution)/shard_map/fetch_points/ppermute | solution.py:29
  6.2 4.0 %collective-permute-start.3 = (bf16[576,256]{1,0:T(8,128)(2,1)S(1)}, bf16[576,256]{1,0:T(8,128)(2,1)S(1)}, u32[]{:S(2)}, u32[]{:S(2)}) collective-permute-start(bf16[576,256]{1,0:T(8,128)(2,1)S(1)} %pack.1.refs_1_.refs_2_), channel_id=1, source_target_pairs={{0,24},{8,16},{16,8},{24,0},{32,56},{40,48},{48,40},{56,32},{64,88... | collective-permute-start | bytes 884744 | tf_op jit(solution)/shard_map/fetch_points/ppermute | solution.py:29
  10.3 3.0 %collective-permute-start.2 = (bf16[576,256]{1,0:T(8,128)(2,1)S(1)}, bf16[576,256]{1,0:T(8,128)(2,1)S(1)}, u32[]{:S(2)}, u32[]{:S(2)}) collective-permute-start(bf16[576,256]{1,0:T(8,128)(2,1)S(1)} %pack.1.refs_1_.refs_2_), channel_id=1, source_target_pairs={{0,96},{8,104},{16,112},{24,120},{32,64},{40,72},{48,80},{56,88},{... | collective-permute-start | bytes 884744 | tf_op jit(solution)/shard_map/fetch_points/ppermute | solution.py:29
  13.3 0.8 %copy-done.1 = f32[512,16]{0,1:T(8,128)S(1)} copy-done((f32[512,16]{0,1:T(8,128)S(1)}, f32[512,16]{0,1:T(8,128)}, u32[]{:S(2)}) %copy-start.1) | copy-done | bytes 32792
  14.0 0.8 %build_tile.7 = (bf16[512,1024]{1,0:T(8,128)(2,1)S(1)}, f32[16,512]{1,0:T(8,128)S(1)}, f32[512,1]{1,0:T(8,128)S(1)}) custom-call(bf16[512,256]{1,0:T(8,128)(2,1)S(1)} %constant_dynamic-slice_fusion.points_ref.refs_0_, bf16[576,256]{1,0:T(8,128)(2,1)S(1)} %pack.1.refs_1_.refs_2_, bf16[576,256]{1,0:T(8,128)(2,1)S(1)} %collective-permute-done.4.refs_2_.refs_3_, ...), custom_call_target="tpu_custom_call" | custom-call | flops 1073741824 | bytes 1024 | tf_op jit(solution)/shard_map/fetch_points/build_tile/pallas_call | solution.py:155
  14.9 1.4 %build_tile.8 = (bf16[1024,1024]{1,0:T(8,128)(2,1)S(1)}, f32[16,1024]{1,0:T(8,128)S(1)}, f32[1024,1]{1,0:T(8,128)S(1)}) custom-call(bf16[512,256]{1,0:T(8,128)(2,1)S(1)} %collective-permute-done.refs_0_.refs_1_, bf16[512,256]{1,0:T(8,128)(2,1)S(1)} %collective-permute-done.1.refs_1_.refs_2_, bf16[576,256]{1,0:T(8,128)(2,1)S(1)} %pack.1.refs_1_.refs_2_, ...), custom_call_target="tpu_custom_call" | custom-call | flops 2147483648 | bytes 1024 | tf_op jit(solution)/shard_map/fetch_points/build_tile/pallas_call | solution.py:155
  16.3 0.7 %collective-permute-done.3.refs_4_ = bf16[576,256]{1,0:T(8,128)(2,1)S(1)} collective-permute-done((bf16[576,256]{1,0:T(8,128)(2,1)S(1)}, bf16[576,256]{1,0:T(8,128)(2,1)S(1)}, u32[]{:S(2)}, u32[]{:S(2)}) %collective-permute-start.3) | collective-permute-done | bytes 294944 | tf_op jit(solution)/shard_map/fetch_points/ppermute | solution.py:29
  17.0 2.7 %collective-permute-done.2.refs_3_ = bf16[576,256]{1,0:T(8,128)(2,1)S(1)} collective-permute-done((bf16[576,256]{1,0:T(8,128)(2,1)S(1)}, bf16[576,256]{1,0:T(8,128)(2,1)S(1)}, u32[]{:S(2)}, u32[]{:S(2)}) %collective-permute-start.2) | collective-permute-done | bytes 294944 | tf_op jit(solution)/shard_map/fetch_points/ppermute | solution.py:29
  19.8 0.5 collective-permute-start.7
  20.3 3.0 %collective-permute-start.8 = (bf16[576,256]{1,0:T(8,128)(2,1)S(1)}, bf16[576,256]{1,0:T(8,128)(2,1)S(1)}, u32[]{:S(2)}, u32[]{:S(2)}) collective-permute-start(bf16[576,256]{1,0:T(8,128)(2,1)S(1)} %broadcast_select_fusion), channel_id=1, source_target_pairs={{0,96},{4,28},{8,104},{12,20},{16,112},{20,12},{24,120},{28,4},{32... | collective-permute-start | bytes 884744 | tf_op jit(solution)/shard_map/fetch_points/ppermute | solution.py:44
  23.3 1.9 %build_tile.9 = (bf16[1536,1024]{1,0:T(8,128)(2,1)S(1)}, f32[16,1536]{1,0:T(8,128)S(1)}) custom-call(bf16[512,256]{1,0:T(8,128)(2,1)S(1)} %constant_dynamic-slice_fusion.points_ref.refs_0_, bf16[512,256]{1,0:T(8,128)(2,1)S(1)} %collective-permute-done.refs_0_.refs_1_, bf16[512,256]{1,0:T(8,128)(2,1)S(1)} %collective-permute-done.1.refs_1_.refs_2_, ...), custom_call_target="tpu_custom_call" | custom-call | flops 3221225472 | bytes 1024 | tf_op jit(solution)/shard_map/build_tiles/build_tile/pallas_call | solution.py:155
  25.3 1.9 %build_tile.10 = (bf16[1536,1024]{1,0:T(8,128)(2,1)S(1)}, f32[16,1536]{1,0:T(8,128)S(1)}) custom-call(bf16[512,256]{1,0:T(8,128)(2,1)S(1)} %constant_dynamic-slice_fusion.points_ref.refs_0_, bf16[512,256]{1,0:T(8,128)(2,1)S(1)} %collective-permute-done.refs_0_.refs_1_, bf16[512,256]{1,0:T(8,128)(2,1)S(1)} %collective-permute-done.1.refs_1_.refs_2_, ...), custom_call_target="tpu_custom_call" | custom-call | flops 3221225472 | bytes 1024 | tf_op jit(solution)/shard_map/build_tiles/build_tile/pallas_call | solution.py:155
  27.2 2.1 %build_tile.11 = (bf16[512,3072]{1,0:T(8,128)(2,1)S(1)}, f32[16,512]{1,0:T(8,128)S(1)}, f32[512,1]{1,0:T(8,128)S(1)}) custom-call(bf16[512,256]{1,0:T(8,128)(2,1)S(1)} %collective-permute-done.5.refs_0_.refs_3_, bf16[576,256]{1,0:T(8,128)(2,1)S(1)} %pack.1.refs_1_.refs_2_, bf16[576,256]{1,0:T(8,128)(2,1)S(1)} %collective-permute-done.4.refs_2_.refs_3_, ...), custom_call_target="tpu_custom_call" | custom-call | flops 3221225472 | bytes 1024 | tf_op jit(solution)/shard_map/build_tiles/build_tile/pallas_call | solution.py:155
  29.5 1.3 %build_tile.12 = (bf16[2048,512]{1,0:T(8,128)(2,1)S(1)}, f32[16,2048]{1,0:T(8,128)S(1)}) custom-call(bf16[512,256]{1,0:T(8,128)(2,1)S(1)} %constant_dynamic-slice_fusion.points_ref.refs_0_, bf16[512,256]{1,0:T(8,128)(2,1)S(1)} %collective-permute-done.refs_0_.refs_1_, bf16[512,256]{1,0:T(8,128)(2,1)S(1)} %collective-permute-done.1.refs_1_.refs_2_, ...), custom_call_target="tpu_custom_call" | custom-call | flops 2147483648 | bytes 1024 | tf_op jit(solution)/shard_map/build_tiles/build_tile/pallas_call | solution.py:155
  30.8 0.2 collective-permute-done.9.refs_4_
  31.1 1.3 %build_tile.13 = (bf16[2048,512]{1,0:T(8,128)(2,1)S(1)}, f32[16,2048]{1,0:T(8,128)S(1)}) custom-call(bf16[512,256]{1,0:T(8,128)(2,1)S(1)} %constant_dynamic-slice_fusion.points_ref.refs_0_, bf16[512,256]{1,0:T(8,128)(2,1)S(1)} %collective-permute-done.refs_0_.refs_1_, bf16[512,256]{1,0:T(8,128)(2,1)S(1)} %collective-permute-done.1.refs_1_.refs_2_, ...), custom_call_target="tpu_custom_call" | custom-call | flops 2147483648 | bytes 1024 | tf_op jit(solution)/shard_map/build_tiles/build_tile/pallas_call | solution.py:155
  32.6 3.4 %collective-permute-start.12 = (bf16[80,512]{1,0:T(8,128)(2,1)S(1)}, bf16[80,512]{1,0:T(8,128)(2,1)S(1)}, u32[]{:S(2)}, u32[]{:S(2)}) collective-permute-start(bf16[80,512]{1,0:T(8,128)(2,1)S(1)} %get-tuple-element.66), channel_id=1, source_target_pairs={{0,40},{8,32},{16,56},{24,48},{32,8},{40,0},{48,24},{56,16},{64,10... | collective-permute-start | bytes 245768 | tf_op jit(solution)/shard_map/sum_over_rows/ppermute | solution.py:29
  36.0 1.7 %collective-permute-done.10.refs_1_ = bf16[80,512]{1,0:T(8,128)(2,1)S(1)} collective-permute-done((bf16[80,512]{1,0:T(8,128)(2,1)S(1)}, bf16[80,512]{1,0:T(8,128)(2,1)S(1)}, u32[]{:S(2)}, u32[]{:S(2)}) %collective-permute-start.10) | collective-permute-done | bytes 81952 | tf_op jit(solution)/shard_map/sum_over_rows/ppermute | solution.py:29
  37.7 1.3 %collective-permute-done.11.refs_2_ = bf16[80,512]{1,0:T(8,128)(2,1)S(1)} collective-permute-done((bf16[80,512]{1,0:T(8,128)(2,1)S(1)}, bf16[80,512]{1,0:T(8,128)(2,1)S(1)}, u32[]{:S(2)}, u32[]{:S(2)}) %collective-permute-start.11) | collective-permute-done | bytes 81952 | tf_op jit(solution)/shard_map/sum_over_rows/ppermute | solution.py:29
  39.1 1.4 %second_product.2 = f32[16,2048]{1,0:T(8,128)S(1)} custom-call(bf16[32,2048]{1,0:T(8,128)(2,1)S(1)} %get-tuple-element.76.narrow_ref, bf16[512,1024]{1,0:T(8,128)(2,1)S(1)} %get-tuple-element.69.refs_0_, bf16[1024,1024]{1,0:T(8,128)(2,1)S(1)} %get-tuple-element.70.refs_1_, bf16[1536,1024]{1,0:T(8,128)(2,1)S(1)} %get-tuple-element.71.refs_2_, ...), custom_call_target="tpu_custom_call" | custom-call | flops 134217728 | bytes 1024 | tf_op jit(solution)/shard_map/second_product/pallas_call | solution.py:241
  40.6 1.5 %second_product.3.mine_ref = f32[16,2048]{1,0:T(8,128)S(1)} custom-call(bf16[32,2048]{1,0:T(8,128)(2,1)S(1)} %get-tuple-element.76.narrow_ref, bf16[512,1024]{1,0:T(8,128)(2,1)S(1)} %get-tuple-element.69.refs_0_, bf16[1024,1024]{1,0:T(8,128)(2,1)S(1)} %get-tuple-element.70.refs_1_, bf16[1536,1024]{1,0:T(8,128)(2,1)S(1)} %get-tuple-element.71.refs_2_, ...), custom_call_target="tpu_custom_call" | custom-call | flops 134217728 | bytes 1024 | tf_op jit(solution)/shard_map/second_product/pallas_call | solution.py:241
  42.1 1.9 %collective-permute-start.14 = (f32[16,512]{1,0:T(8,128)S(1)}, f32[16,512]{1,0:T(8,128)S(1)}, u32[]{:S(2)}, u32[]{:S(2)}) collective-permute-start(f32[16,512]{1,0:T(8,128)S(1)} %get-tuple-element.79), channel_id=1, source_target_pairs={{0,96},{8,104},{16,112},{24,120},{32,64},{40,72},{48,80},{56,88},{... | collective-permute-start | bytes 98312 | tf_op jit(solution)/shard_map/sum_over_columns/ppermute | solution.py:29
  43.9 0.8 %collective-permute-start.15 = (f32[16,512]{1,0:T(8,128)S(1)}, f32[16,512]{1,0:T(8,128)S(1)}, u32[]{:S(2)}, u32[]{:S(2)}) collective-permute-start(f32[16,512]{1,0:T(8,128)S(1)} %get-tuple-element.80), channel_id=1, source_target_pairs={{0,24},{8,16},{16,8},{24,0},{32,56},{40,48},{48,40},{56,32},{64,88... | collective-permute-start | bytes 98312 | tf_op jit(solution)/shard_map/sum_over_columns/ppermute | solution.py:29
  44.8 3.3 %collective-permute-start.16 = (f32[16,512]{1,0:T(8,128)S(1)}, f32[16,512]{1,0:T(8,128)S(1)}, u32[]{:S(2)}, u32[]{:S(2)}) collective-permute-start(f32[16,512]{1,0:T(8,128)S(1)} %get-tuple-element.81), channel_id=1, source_target_pairs={{0,120},{8,112},{16,104},{24,96},{32,88},{40,80},{48,72},{56,64},{... | collective-permute-start | bytes 98312 | tf_op jit(solution)/shard_map/sum_over_columns/ppermute | solution.py:29
  48.0 1.0 %collective-permute-done.15.refs_2_ = f32[16,512]{1,0:T(8,128)S(1)} collective-permute-done((f32[16,512]{1,0:T(8,128)S(1)}, f32[16,512]{1,0:T(8,128)S(1)}, u32[]{:S(2)}, u32[]{:S(2)}) %collective-permute-start.15) | collective-permute-done | bytes 32800 | tf_op jit(solution)/shard_map/sum_over_columns/ppermute | solution.py:29
  49.1 3.0 %collective-permute-done.16.refs_3_ = f32[16,512]{1,0:T(8,128)S(1)} collective-permute-done((f32[16,512]{1,0:T(8,128)S(1)}, f32[16,512]{1,0:T(8,128)S(1)}, u32[]{:S(2)}, u32[]{:S(2)}) %collective-permute-start.16) | collective-permute-done | bytes 32800 | tf_op jit(solution)/shard_map/sum_over_columns/ppermute | solution.py:29
  52.0 0.2 local_sums.1
  52.3 12.1 %all_to_all.8 = f32[32,1,128]{2,1,0:T(1,128)S(1)} all-to-all(f32[32,1,128]{2,1,0:T(1,128)S(1)} %broadcast_in_dim.2), channel_id=1, replica_groups=mesh['y'=4,'z'=4,'c'=2,'x'=4] {'y','z','c'}, dimensions={0} | all-to-all | bytes 32768 | tf_op jit(solution)/shard_map/final_sums/all_to_all | solution.py:376
  64.4 1.0 %finish.1 = (f32[16,512]{1,0:T(8,128)}, f32[16,512]{1,0:T(8,128)}) custom-call(f32[16,512]{1,0:T(8,128)S(1)} %bitcast.12, f32[16,512]{1,0:T(8,128)S(1)} %get-tuple-element.67.rho_ref, f32[16,512]{1,0:T(8,128)S(1)} %get-tuple-element.82.image_ref, f32[32,128]{1,0:T(8,128)S(1)} %bitcast.13), custom_call_target="tpu_custom_call" | custom-call | tf_op jit(solution)/shard_map/finish/pallas_call | solution.py:315
  (28 shorter events, 0.8 us)
Async XLA Ops:
  0.6 1.5 %copy-start = (bf16[1024,256]{1,0:T(8,128)(2,1)S(1)}, bf16[1024,256]{1,0:T(8,128)(2,1)}, u32[]{:S(2)}) copy-start(bf16[1024,256]{1,0:T(8,128)(2,1)} %param.3) | copy-start | bytes 1572868
  2.5 7.8 %collective-permute-start.4 = (bf16[576,256]{1,0:T(8,128)(2,1)S(1)}, bf16[576,256]{1,0:T(8,128)(2,1)S(1)}, u32[]{:S(2)}, u32[]{:S(2)}) collective-permute-start(bf16[576,256]{1,0:T(8,128)(2,1)S(1)} %pack.1.refs_1_.refs_2_), channel_id=1, source_target_pairs={{0,4},{4,0},{1,5},{5,1},{2,6},{6,2},{3,7},{7,3},{8,12},{12,8},{9,1... | collective-permute-start | bytes 884744 | tf_op jit(solution)/shard_map/fetch_points/ppermute | solution.py:48
  2.6 12.3 %collective-permute-start.1 = (bf16[512,256]{1,0:T(8,128)(2,1)S(1)}, bf16[512,256]{1,0:T(8,128)(2,1)S(1)}, u32[]{:S(2)}, u32[]{:S(2)}) collective-permute-start(bf16[512,256]{1,0:T(8,128)(2,1)S(1)} %constant_dynamic-slice_fusion.points_ref.refs_0_), channel_id=1, source_target_pairs={{0,8},{8,0},{16,24},{24,16},{32,40},{40,32},{48,56},{56,48},{64,72... | collective-permute-start | bytes 786440 | tf_op jit(solution)/shard_map/fetch_points/ppermute | solution.py:29
  4.6 10.3 %collective-permute-start = (bf16[512,256]{1,0:T(8,128)(2,1)S(1)}, bf16[512,256]{1,0:T(8,128)(2,1)S(1)}, u32[]{:S(2)}, u32[]{:S(2)}) collective-permute-start(bf16[512,256]{1,0:T(8,128)(2,1)S(1)} %constant_dynamic-slice_fusion.points_ref.refs_0_), channel_id=1, source_target_pairs={{0,32},{8,40},{16,48},{24,56},{32,0},{40,8},{48,16},{56,24},{64,96... | collective-permute-start | bytes 786440 | tf_op jit(solution)/shard_map/fetch_points/ppermute | solution.py:29
  6.2 21.0 %collective-permute-start.5 = (bf16[512,256]{1,0:T(8,128)(2,1)S(1)}, bf16[512,256]{1,0:T(8,128)(2,1)S(1)}, u32[]{:S(2)}, u32[]{:S(2)}) collective-permute-start(bf16[512,256]{1,0:T(8,128)(2,1)S(1)} %constant_dynamic-slice_fusion.points_ref.refs_0_), channel_id=1, source_target_pairs={{0,40},{8,32},{16,56},{24,48},{32,8},{40,0},{48,24},{56,16},{64,10... | collective-permute-start | bytes 786440 | tf_op jit(solution)/shard_map/fetch_points/ppermute | solution.py:29
  6.2 10.8 %collective-permute-start.3 = (bf16[576,256]{1,0:T(8,128)(2,1)S(1)}, bf16[576,256]{1,0:T(8,128)(2,1)S(1)}, u32[]{:S(2)}, u32[]{:S(2)}) collective-permute-start(bf16[576,256]{1,0:T(8,128)(2,1)S(1)} %pack.1.refs_1_.refs_2_), channel_id=1, source_target_pairs={{0,24},{8,16},{16,8},{24,0},{32,56},{40,48},{48,40},{56,32},{64,88... | collective-permute-start | bytes 884744 | tf_op jit(solution)/shard_map/fetch_points/ppermute | solution.py:29
  10.3 9.5 %collective-permute-start.2 = (bf16[576,256]{1,0:T(8,128)(2,1)S(1)}, bf16[576,256]{1,0:T(8,128)(2,1)S(1)}, u32[]{:S(2)}, u32[]{:S(2)}) collective-permute-start(bf16[576,256]{1,0:T(8,128)(2,1)S(1)} %pack.1.refs_1_.refs_2_), channel_id=1, source_target_pairs={{0,96},{8,104},{16,112},{24,120},{32,64},{40,72},{48,80},{56,88},{... | collective-permute-start | bytes 884744 | tf_op jit(solution)/shard_map/fetch_points/ppermute | solution.py:29
  13.3 0.8 %copy-start.1 = (f32[512,16]{0,1:T(8,128)S(1)}, f32[512,16]{0,1:T(8,128)}, u32[]{:S(2)}) copy-start(f32[512,16]{0,1:T(8,128)} %param.5) | copy-start | bytes 98308
  19.8 5.5 %collective-permute-start.6 = (bf16[576,256]{1,0:T(8,128)(2,1)S(1)}, bf16[576,256]{1,0:T(8,128)(2,1)S(1)}, u32[]{:S(2)}, u32[]{:S(2)}) collective-permute-start(bf16[576,256]{1,0:T(8,128)(2,1)S(1)} %collective-permute-done.2.refs_3_), channel_id=1, source_target_pairs={{0,4},{4,0},{1,5},{5,1},{2,6},{6,2},{3,7},{7,3},{8,12},{12,8},{9,1... | collective-permute-start | bytes 884744 | tf_op jit(solution)/shard_map/build_tiles/ppermute | solution.py:48
  19.8 5.5 %collective-permute-start.7 = (bf16[576,256]{1,0:T(8,128)(2,1)S(1)}, bf16[576,256]{1,0:T(8,128)(2,1)S(1)}, u32[]{:S(2)}, u32[]{:S(2)}) collective-permute-start(bf16[576,256]{1,0:T(8,128)(2,1)S(1)} %collective-permute-done.3.refs_4_), channel_id=1, source_target_pairs={{0,4},{4,0},{1,5},{5,1},{2,6},{6,2},{3,7},{7,3},{8,12},{12,8},{9,1... | collective-permute-start | bytes 884744 | tf_op jit(solution)/shard_map/build_tiles/ppermute | solution.py:48
  20.3 9.0 %collective-permute-start.8 = (bf16[576,256]{1,0:T(8,128)(2,1)S(1)}, bf16[576,256]{1,0:T(8,128)(2,1)S(1)}, u32[]{:S(2)}, u32[]{:S(2)}) collective-permute-start(bf16[576,256]{1,0:T(8,128)(2,1)S(1)} %broadcast_select_fusion), channel_id=1, source_target_pairs={{0,96},{4,28},{8,104},{12,20},{16,112},{20,12},{24,120},{28,4},{32... | collective-permute-start | bytes 884744 | tf_op jit(solution)/shard_map/fetch_points/ppermute | solution.py:44
  29.3 1.8 %collective-permute-start.9 = (bf16[576,256]{1,0:T(8,128)(2,1)S(1)}, bf16[576,256]{1,0:T(8,128)(2,1)S(1)}, u32[]{:S(2)}, u32[]{:S(2)}) collective-permute-start(bf16[576,256]{1,0:T(8,128)(2,1)S(1)} %collective-permute-done.8.refs_4_), channel_id=1, source_target_pairs={{0,4},{4,0},{1,5},{5,1},{2,6},{6,2},{3,7},{7,3},{8,12},{12,8},{9,1... | collective-permute-start | bytes 884744 | tf_op jit(solution)/shard_map/build_tiles/ppermute | solution.py:48
  32.5 5.3 %collective-permute-start.10 = (bf16[80,512]{1,0:T(8,128)(2,1)S(1)}, bf16[80,512]{1,0:T(8,128)(2,1)S(1)}, u32[]{:S(2)}, u32[]{:S(2)}) collective-permute-start(bf16[80,512]{1,0:T(8,128)(2,1)S(1)} %get-tuple-element.64), channel_id=1, source_target_pairs={{0,32},{8,40},{16,48},{24,56},{32,0},{40,8},{48,16},{56,24},{64,96... | collective-permute-start | bytes 245768 | tf_op jit(solution)/shard_map/sum_over_rows/ppermute | solution.py:29
  32.6 6.5 %collective-permute-start.11 = (bf16[80,512]{1,0:T(8,128)(2,1)S(1)}, bf16[80,512]{1,0:T(8,128)(2,1)S(1)}, u32[]{:S(2)}, u32[]{:S(2)}) collective-permute-start(bf16[80,512]{1,0:T(8,128)(2,1)S(1)} %get-tuple-element.65), channel_id=1, source_target_pairs={{0,8},{8,0},{16,24},{24,16},{32,40},{40,32},{48,56},{56,48},{64,72... | collective-permute-start | bytes 245768 | tf_op jit(solution)/shard_map/sum_over_rows/ppermute | solution.py:29
  32.6 6.4 %collective-permute-start.12 = (bf16[80,512]{1,0:T(8,128)(2,1)S(1)}, bf16[80,512]{1,0:T(8,128)(2,1)S(1)}, u32[]{:S(2)}, u32[]{:S(2)}) collective-permute-start(bf16[80,512]{1,0:T(8,128)(2,1)S(1)} %get-tuple-element.66), channel_id=1, source_target_pairs={{0,40},{8,32},{16,56},{24,48},{32,8},{40,0},{48,24},{56,16},{64,10... | collective-permute-start | bytes 245768 | tf_op jit(solution)/shard_map/sum_over_rows/ppermute | solution.py:29
  40.6 11.5 %copy-start.2 = (f32[512,16]{0,1:T(8,128)S(1)}, f32[512,16]{0,1:T(8,128)}, u32[]{:S(2)}) copy-start(f32[512,16]{0,1:T(8,128)} %param.5) | copy-start | bytes 98308
  40.6 1.5 %collective-permute-start.13 = (f32[16,2048]{1,0:T(8,128)S(1)}, f32[16,2048]{1,0:T(8,128)S(1)}, u32[]{:S(2)}, u32[]{:S(2)}) collective-permute-start(f32[16,2048]{1,0:T(8,128)S(1)} %second_product.2), channel_id=1, source_target_pairs={{0,4},{4,0},{1,5},{5,1},{2,6},{6,2},{3,7},{7,3},{8,12},{12,8},{9,1... | collective-permute-start | bytes 393224 | tf_op jit(solution)/shard_map/sum_over_columns/ppermute | solution.py:48
  42.1 6.0 %collective-permute-start.14 = (f32[16,512]{1,0:T(8,128)S(1)}, f32[16,512]{1,0:T(8,128)S(1)}, u32[]{:S(2)}, u32[]{:S(2)}) collective-permute-start(f32[16,512]{1,0:T(8,128)S(1)} %get-tuple-element.79), channel_id=1, source_target_pairs={{0,96},{8,104},{16,112},{24,120},{32,64},{40,72},{48,80},{56,88},{... | collective-permute-start | bytes 98312 | tf_op jit(solution)/shard_map/sum_over_columns/ppermute | solution.py:29
  43.9 5.1 %collective-permute-start.15 = (f32[16,512]{1,0:T(8,128)S(1)}, f32[16,512]{1,0:T(8,128)S(1)}, u32[]{:S(2)}, u32[]{:S(2)}) collective-permute-start(f32[16,512]{1,0:T(8,128)S(1)} %get-tuple-element.80), channel_id=1, source_target_pairs={{0,24},{8,16},{16,8},{24,0},{32,56},{40,48},{48,40},{56,32},{64,88... | collective-permute-start | bytes 98312 | tf_op jit(solution)/shard_map/sum_over_columns/ppermute | solution.py:29
  44.8 7.2 %collective-permute-start.16 = (f32[16,512]{1,0:T(8,128)S(1)}, f32[16,512]{1,0:T(8,128)S(1)}, u32[]{:S(2)}, u32[]{:S(2)}) collective-permute-start(f32[16,512]{1,0:T(8,128)S(1)} %get-tuple-element.81), channel_id=1, source_target_pairs={{0,120},{8,112},{16,104},{24,96},{32,88},{40,80},{48,72},{56,64},{... | collective-permute-start | bytes 98312 | tf_op jit(solution)/shard_map/sum_over_columns/ppermute | solution.py:29

commit v17 on v16

--- a/solution.py
+++ b/solution.py
@@ -32,16 +32,6 @@
 def swap_each(values, offsets):
     received = [swap(value, offset) for value, offset in reversed(list(zip(values, offsets)))]
     return received[::-1]
-
-
-def hand_on(along_y, along_z, offset):
-    value = jnp.where(lax.axis_index("c") == 0, along_z, along_y)
-    pairs = []
-    for y in range(NY):
-        for z in range(NZ):
-            here = (y * NZ + z) * NC
-            pairs += [(here, ((y ^ offset[0]) * NZ + z) * NC), (here + 1, (y * NZ + (z ^ offset[1])) * NC + 1)]
-    return lax.ppermute(value, ("y", "z", "c"), pairs)
 
 
 def swap_core(value):
@@ -327,14 +317,13 @@
     with jax.named_scope("fetch_points"):
         message = pack(points, side.astype(jnp.bfloat16))
         rows = [points] + [swap(points, offset) for offset in ROWS[1:]]
-        cols = [message] + [swap(message, offset) for offset in SQUARE[1:3]]
+        cols = [message] + [swap(message, offset) for offset in SQUARE[1:]]
         first = [message, swap_core(message)]
         tile_a, image_a, half_a = build([points], first, own, probes, side=side)
         tile_b, image_b, half_b = build(rows[1:3], first, own, probes)
         (rows[1], rows[2], cols[1], cols[2]), image_a, image_b = lax.optimization_barrier(
             ((rows[1], rows[2], cols[1], cols[2]), image_a, image_b)
         )
-        cols.append(hand_on(cols[1], cols[2], SQUARE[3]))
 
     with jax.named_scope("build_tiles"):
         half = [half_a, half_b]

time: 66.4 us -> 64.9 us (0.977)
  blocking collectives: 12.1 us -> 11 us
    ppermute x1 -> x0, starting transfers between devices: 3.03 us -> none  [hand_on(): return lax.ppermute(value, ('y', 'z', 'c'), pairs)]
    ppermute x11 -> x12, starting transfers between devices: 20.2 us -> 23.2 us  [swap(): return lax.ppermute(value, ('y', 'z'), pairs)]
    all_to_all x1, blocking collectives: 12.1 us -> 11 us  [on_device(): sums = lax.all_to_all(sums, ('y', 'z', 'c'), 0, 0, tiled=True)]
    ppermute x11 -> x12, waiting for transfers between devices: 10.4 us -> 10.1 us  [swap(): return lax.ppermute(value, ('y', 'z'), pairs)]
  transfers between devices with their start and end apart: 17 -> 17, of which waited for: 7 -> 6; matrix products, arithmetic and copies ran while one was open for 0% -> 0% of each run, Pallas kernels for 17% -> 17%
where the time goes in v17:
time: 64.9 us; the launch traced here: 63.9 us
  starting transfers between devices  24 us (37%)
  Pallas kernels  15.4 us (24%)
  blocking collectives  11 us (17%)
  waiting for transfers between devices  10.4 us (16%)
  between operations  1.43 us (2%)
  local copies, waits for them, and re-layouts  0.85 us (1%)
  other arithmetic  0.76 us (1%)
    ppermute x12, starting transfers between devices, swap(): return lax.ppermute(value, ('y', 'z'), pairs)  23.2 us
    all_to_all x1, blocking collectives, on_device(): sums = lax.all_to_all(sums, ('y', 'z', 'c'), 0, 0, tiled=True)  11 us
    pallas_call x7, Pallas kernels, build(): pl.pallas_call(functools.partial(tile_kernel, counts, probes), out_shape=...  10.8 us
    ppermute x12, waiting for transfers between devices, swap(): return lax.ppermute(value, ('y', 'z'), pairs)  10.1 us
    pallas_call x2, Pallas kernels, second_product(): pl.pallas_call(functools.partial(second_kernel, own, half, places), in_sp...  2.9 us
  transfers between devices with their start and end apart: 17, of which 6 were waited for; matrix products, arithmetic and copies ran while one was open for 0% of the time, Pallas kernels for 17%

profile of v17, /device:TPU:0, one launch (start us, length us, event | category | flops | bytes accessed | tf_op | source)
XLA Modules:
  0.0 63.9 jit_solution(9185538423813556433)
XLA Ops:
  1.3 0.8 %bitcast_convert_fusion.side_ref = bf16[16,512]{1,0:T(8,128)(2,1)S(1)} fusion(f32[512,16]{0,1:T(8,128)} %param.5), kind=kLoop, calls=%fused_computation.1 | loop fusion | flops 8192 | bytes 49152 | tf_op jit(solution)/shard_map/fetch_points/convert_element_type | solution.py:318
  2.2 0.3 pack.1.refs_1_.refs_2_
  2.6 2.1 %collective-permute-start.1 = (bf16[512,256]{1,0:T(8,128)(2,1)S(1)}, bf16[512,256]{1,0:T(8,128)(2,1)S(1)}, u32[]{:S(2)}, u32[]{:S(2)}) collective-permute-start(bf16[512,256]{1,0:T(8,128)(2,1)S(1)} %constant_dynamic-slice_fusion.points_ref.refs_0_), channel_id=1, source_target_pairs={{0,8},{8,0},{16,24},{24,16},{32,40},{40,32},{48,56},{56,48},{64,72... | collective-permute-start | bytes 786440 | tf_op jit(solution)/shard_map/fetch_points/ppermute | solution.py:29
  4.6 1.6 %collective-permute-start = (bf16[512,256]{1,0:T(8,128)(2,1)S(1)}, bf16[512,256]{1,0:T(8,128)(2,1)S(1)}, u32[]{:S(2)}, u32[]{:S(2)}) collective-permute-start(bf16[512,256]{1,0:T(8,128)(2,1)S(1)} %constant_dynamic-slice_fusion.points_ref.refs_0_), channel_id=1, source_target_pairs={{0,32},{8,40},{16,48},{24,56},{32,0},{40,8},{48,16},{56,24},{64,96... | collective-permute-start | bytes 786440 | tf_op jit(solution)/shard_map/fetch_points/ppermute | solution.py:29
  6.2 4.0 %collective-permute-start.3 = (bf16[576,256]{1,0:T(8,128)(2,1)S(1)}, bf16[576,256]{1,0:T(8,128)(2,1)S(1)}, u32[]{:S(2)}, u32[]{:S(2)}) collective-permute-start(bf16[576,256]{1,0:T(8,128)(2,1)S(1)} %pack.1.refs_1_.refs_2_), channel_id=1, source_target_pairs={{0,24},{8,16},{16,8},{24,0},{32,56},{40,48},{48,40},{56,32},{64,88... | collective-permute-start | bytes 884744 | tf_op jit(solution)/shard_map/fetch_points/ppermute | solution.py:29
  10.3 3.0 %collective-permute-start.2 = (bf16[576,256]{1,0:T(8,128)(2,1)S(1)}, bf16[576,256]{1,0:T(8,128)(2,1)S(1)}, u32[]{:S(2)}, u32[]{:S(2)}) collective-permute-start(bf16[576,256]{1,0:T(8,128)(2,1)S(1)} %pack.1.refs_1_.refs_2_), channel_id=1, source_target_pairs={{0,96},{8,104},{16,112},{24,120},{32,64},{40,72},{48,80},{56,88},{... | collective-permute-start | bytes 884744 | tf_op jit(solution)/shard_map/fetch_points/ppermute | solution.py:29
  13.3 0.8 %copy-done.1 = f32[512,16]{0,1:T(8,128)S(1)} copy-done((f32[512,16]{0,1:T(8,128)S(1)}, f32[512,16]{0,1:T(8,128)}, u32[]{:S(2)}) %copy-start.1) | copy-done | bytes 32792
  14.0 0.8 %build_tile.7 = (bf16[512,1024]{1,0:T(8,128)(2,1)S(1)}, f32[16,512]{1,0:T(8,128)S(1)}, f32[512,1]{1,0:T(8,128)S(1)}) custom-call(bf16[512,256]{1,0:T(8,128)(2,1)S(1)} %constant_dynamic-slice_fusion.points_ref.refs_0_, bf16[576,256]{1,0:T(8,128)(2,1)S(1)} %pack.1.refs_1_.refs_2_, bf16[576,256]{1,0:T(8,128)(2,1)S(1)} %collective-permute-done.4.refs_2_.refs_3_, ...), custom_call_target="tpu_custom_call" | custom-call | flops 1073741824 | bytes 1024 | tf_op jit(solution)/shard_map/fetch_points/build_tile/pallas_call | solution.py:145
  14.9 3.0 %collective-permute-start.8 = (bf16[576,256]{1,0:T(8,128)(2,1)S(1)}, bf16[576,256]{1,0:T(8,128)(2,1)S(1)}, u32[]{:S(2)}, u32[]{:S(2)}) collective-permute-start(bf16[576,256]{1,0:T(8,128)(2,1)S(1)} %pack.1.refs_1_.refs_2_), channel_id=1, source_target_pairs={{0,120},{8,112},{16,104},{24,96},{32,88},{40,80},{48,72},{56,64},{... | collective-permute-start | bytes 884744 | tf_op jit(solution)/shard_map/fetch_points/ppermute | solution.py:29
  17.9 1.4 %build_tile.8 = (bf16[1024,1024]{1,0:T(8,128)(2,1)S(1)}, f32[16,1024]{1,0:T(8,128)S(1)}, f32[1024,1]{1,0:T(8,128)S(1)}) custom-call(bf16[512,256]{1,0:T(8,128)(2,1)S(1)} %collective-permute-done.refs_0_.refs_1_, bf16[512,256]{1,0:T(8,128)(2,1)S(1)} %collective-permute-done.1.refs_1_.refs_2_, bf16[576,256]{1,0:T(8,128)(2,1)S(1)} %pack.1.refs_1_.refs_2_, ...), custom_call_target="tpu_custom_call" | custom-call | flops 2147483648 | bytes 1024 | tf_op jit(solution)/shard_map/fetch_points/build_tile/pallas_call | solution.py:145
  19.3 1.9 %collective-permute-done.2.refs_3_ = bf16[576,256]{1,0:T(8,128)(2,1)S(1)} collective-permute-done((bf16[576,256]{1,0:T(8,128)(2,1)S(1)}, bf16[576,256]{1,0:T(8,128)(2,1)S(1)}, u32[]{:S(2)}, u32[]{:S(2)}) %collective-permute-start.2) | collective-permute-done | bytes 294944 | tf_op jit(solution)/shard_map/fetch_points/ppermute | solution.py:29
  21.2 0.5 collective-permute-start.7
  21.7 1.9 %build_tile.9 = (bf16[1536,1024]{1,0:T(8,128)(2,1)S(1)}, f32[16,1536]{1,0:T(8,128)S(1)}) custom-call(bf16[512,256]{1,0:T(8,128)(2,1)S(1)} %constant_dynamic-slice_fusion.points_ref.refs_0_, bf16[512,256]{1,0:T(8,128)(2,1)S(1)} %collective-permute-done.refs_0_.refs_1_, bf16[512,256]{1,0:T(8,128)(2,1)S(1)} %collective-permute-done.1.refs_1_.refs_2_, ...), custom_call_target="tpu_custom_call" | custom-call | flops 3221225472 | bytes 1024 | tf_op jit(solution)/shard_map/build_tiles/build_tile/pallas_call | solution.py:145
  23.6 1.9 %build_tile.10 = (bf16[1536,1024]{1,0:T(8,128)(2,1)S(1)}, f32[16,1536]{1,0:T(8,128)S(1)}) custom-call(bf16[512,256]{1,0:T(8,128)(2,1)S(1)} %constant_dynamic-slice_fusion.points_ref.refs_0_, bf16[512,256]{1,0:T(8,128)(2,1)S(1)} %collective-permute-done.refs_0_.refs_1_, bf16[512,256]{1,0:T(8,128)(2,1)S(1)} %collective-permute-done.1.refs_1_.refs_2_, ...), custom_call_target="tpu_custom_call" | custom-call | flops 3221225472 | bytes 1024 | tf_op jit(solution)/shard_map/build_tiles/build_tile/pallas_call | solution.py:145
  25.5 2.1 %build_tile.11 = (bf16[512,3072]{1,0:T(8,128)(2,1)S(1)}, f32[16,512]{1,0:T(8,128)S(1)}, f32[512,1]{1,0:T(8,128)S(1)}) custom-call(bf16[512,256]{1,0:T(8,128)(2,1)S(1)} %collective-permute-done.5.refs_0_.refs_3_, bf16[576,256]{1,0:T(8,128)(2,1)S(1)} %pack.1.refs_1_.refs_2_, bf16[576,256]{1,0:T(8,128)(2,1)S(1)} %collective-permute-done.4.refs_2_.refs_3_, ...), custom_call_target="tpu_custom_call" | custom-call | flops 3221225472 | bytes 1024 | tf_op jit(solution)/shard_map/build_tiles/build_tile/pallas_call | solution.py:145
  27.8 1.3 %build_tile.12 = (bf16[2048,512]{1,0:T(8,128)(2,1)S(1)}, f32[16,2048]{1,0:T(8,128)S(1)}) custom-call(bf16[512,256]{1,0:T(8,128)(2,1)S(1)} %constant_dynamic-slice_fusion.points_ref.refs_0_, bf16[512,256]{1,0:T(8,128)(2,1)S(1)} %collective-permute-done.refs_0_.refs_1_, bf16[512,256]{1,0:T(8,128)(2,1)S(1)} %collective-permute-done.1.refs_1_.refs_2_, ...), custom_call_target="tpu_custom_call" | custom-call | flops 2147483648 | bytes 1024 | tf_op jit(solution)/shard_map/build_tiles/build_tile/pallas_call | solution.py:145
  29.1 0.2 collective-permute-done.9.refs_4_
  29.4 1.3 %build_tile.13 = (bf16[2048,512]{1,0:T(8,128)(2,1)S(1)}, f32[16,2048]{1,0:T(8,128)S(1)}) custom-call(bf16[512,256]{1,0:T(8,128)(2,1)S(1)} %constant_dynamic-slice_fusion.points_ref.refs_0_, bf16[512,256]{1,0:T(8,128)(2,1)S(1)} %collective-permute-done.refs_0_.refs_1_, bf16[512,256]{1,0:T(8,128)(2,1)S(1)} %collective-permute-done.1.refs_1_.refs_2_, ...), custom_call_target="tpu_custom_call" | custom-call | flops 2147483648 | bytes 1024 | tf_op jit(solution)/shard_map/build_tiles/build_tile/pallas_call | solution.py:145
  30.8 0.3 collective-permute-start.10
  31.1 3.2 %collective-permute-start.12 = (bf16[80,512]{1,0:T(8,128)(2,1)S(1)}, bf16[80,512]{1,0:T(8,128)(2,1)S(1)}, u32[]{:S(2)}, u32[]{:S(2)}) collective-permute-start(bf16[80,512]{1,0:T(8,128)(2,1)S(1)} %get-tuple-element.66), channel_id=1, source_target_pairs={{0,40},{8,32},{16,56},{24,48},{32,8},{40,0},{48,24},{56,16},{64,10... | collective-permute-start | bytes 245768 | tf_op jit(solution)/shard_map/sum_over_rows/ppermute | solution.py:29
  34.3 1.7 %collective-permute-done.10.refs_1_ = bf16[80,512]{1,0:T(8,128)(2,1)S(1)} collective-permute-done((bf16[80,512]{1,0:T(8,128)(2,1)S(1)}, bf16[80,512]{1,0:T(8,128)(2,1)S(1)}, u32[]{:S(2)}, u32[]{:S(2)}) %collective-permute-start.10) | collective-permute-done | bytes 81952 | tf_op jit(solution)/shard_map/sum_over_rows/ppermute | solution.py:29
  36.0 1.3 %collective-permute-done.11.refs_2_ = bf16[80,512]{1,0:T(8,128)(2,1)S(1)} collective-permute-done((bf16[80,512]{1,0:T(8,128)(2,1)S(1)}, bf16[80,512]{1,0:T(8,128)(2,1)S(1)}, u32[]{:S(2)}, u32[]{:S(2)}) %collective-permute-start.11) | collective-permute-done | bytes 81952 | tf_op jit(solution)/shard_map/sum_over_rows/ppermute | solution.py:29
  37.4 1.4 %second_product.2 = f32[16,2048]{1,0:T(8,128)S(1)} custom-call(bf16[32,2048]{1,0:T(8,128)(2,1)S(1)} %get-tuple-element.76.narrow_ref, bf16[512,1024]{1,0:T(8,128)(2,1)S(1)} %get-tuple-element.69.refs_0_, bf16[1024,1024]{1,0:T(8,128)(2,1)S(1)} %get-tuple-element.70.refs_1_, bf16[1536,1024]{1,0:T(8,128)(2,1)S(1)} %get-tuple-element.71.refs_2_, ...), custom_call_target="tpu_custom_call" | custom-call | flops 134217728 | bytes 1024 | tf_op jit(solution)/shard_map/second_product/pallas_call | solution.py:231
  38.9 1.5 %second_product.3.mine_ref = f32[16,2048]{1,0:T(8,128)S(1)} custom-call(bf16[32,2048]{1,0:T(8,128)(2,1)S(1)} %get-tuple-element.76.narrow_ref, bf16[512,1024]{1,0:T(8,128)(2,1)S(1)} %get-tuple-element.69.refs_0_, bf16[1024,1024]{1,0:T(8,128)(2,1)S(1)} %get-tuple-element.70.refs_1_, bf16[1536,1024]{1,0:T(8,128)(2,1)S(1)} %get-tuple-element.71.refs_2_, ...), custom_call_target="tpu_custom_call" | custom-call | flops 134217728 | bytes 1024 | tf_op jit(solution)/shard_map/second_product/pallas_call | solution.py:231
  40.4 3.0 %collective-permute-start.14 = (f32[16,512]{1,0:T(8,128)S(1)}, f32[16,512]{1,0:T(8,128)S(1)}, u32[]{:S(2)}, u32[]{:S(2)}) collective-permute-start(f32[16,512]{1,0:T(8,128)S(1)} %get-tuple-element.79), channel_id=1, source_target_pairs={{0,96},{8,104},{16,112},{24,120},{32,64},{40,72},{48,80},{56,88},{... | collective-permute-start | bytes 98312 | tf_op jit(solution)/shard_map/sum_over_columns/ppermute | solution.py:29
  43.3 1.0 %collective-permute-start.15 = (f32[16,512]{1,0:T(8,128)S(1)}, f32[16,512]{1,0:T(8,128)S(1)}, u32[]{:S(2)}, u32[]{:S(2)}) collective-permute-start(f32[16,512]{1,0:T(8,128)S(1)} %get-tuple-element.80), channel_id=1, source_target_pairs={{0,24},{8,16},{16,8},{24,0},{32,56},{40,48},{48,40},{56,32},{64,88... | collective-permute-start | bytes 98312 | tf_op jit(solution)/shard_map/sum_over_columns/ppermute | solution.py:29
  44.4 2.0 %collective-permute-start.16 = (f32[16,512]{1,0:T(8,128)S(1)}, f32[16,512]{1,0:T(8,128)S(1)}, u32[]{:S(2)}, u32[]{:S(2)}) collective-permute-start(f32[16,512]{1,0:T(8,128)S(1)} %get-tuple-element.81), channel_id=1, source_target_pairs={{0,120},{8,112},{16,104},{24,96},{32,88},{40,80},{48,72},{56,64},{... | collective-permute-start | bytes 98312 | tf_op jit(solution)/shard_map/sum_over_columns/ppermute | solution.py:29
  46.4 2.1 %collective-permute-done.15.refs_2_ = f32[16,512]{1,0:T(8,128)S(1)} collective-permute-done((f32[16,512]{1,0:T(8,128)S(1)}, f32[16,512]{1,0:T(8,128)S(1)}, u32[]{:S(2)}, u32[]{:S(2)}) %collective-permute-start.15) | collective-permute-done | bytes 32800 | tf_op jit(solution)/shard_map/sum_over_columns/ppermute | solution.py:29
  48.5 3.1 %collective-permute-done.16.refs_3_ = f32[16,512]{1,0:T(8,128)S(1)} collective-permute-done((f32[16,512]{1,0:T(8,128)S(1)}, f32[16,512]{1,0:T(8,128)S(1)}, u32[]{:S(2)}, u32[]{:S(2)}) %collective-permute-start.16) | collective-permute-done | bytes 32800 | tf_op jit(solution)/shard_map/sum_over_columns/ppermute | solution.py:29
  51.6 0.2 local_sums.1
  51.9 11.0 %all_to_all.8 = f32[32,1,128]{2,1,0:T(1,128)S(1)} all-to-all(f32[32,1,128]{2,1,0:T(1,128)S(1)} %broadcast_in_dim.2), channel_id=1, replica_groups=mesh['y'=4,'z'=4,'c'=2,'x'=4] {'y','z','c'}, dimensions={0} | all-to-all | bytes 32768 | tf_op jit(solution)/shard_map/final_sums/all_to_all | solution.py:365
  62.9 1.0 %finish.1 = (f32[16,512]{1,0:T(8,128)}, f32[16,512]{1,0:T(8,128)}) custom-call(f32[16,512]{1,0:T(8,128)S(1)} %bitcast.12, f32[16,512]{1,0:T(8,128)S(1)} %get-tuple-element.67.rho_ref, f32[16,512]{1,0:T(8,128)S(1)} %get-tuple-element.82.image_ref, f32[32,128]{1,0:T(8,128)S(1)} %bitcast.13), custom_call_target="tpu_custom_call" | custom-call | tf_op jit(solution)/shard_map/finish/pallas_call | solution.py:305
  (25 shorter events, 0.6 us)
Async XLA Ops:
  0.6 1.5 %copy-start = (bf16[1024,256]{1,0:T(8,128)(2,1)S(1)}, bf16[1024,256]{1,0:T(8,128)(2,1)}, u32[]{:S(2)}) copy-start(bf16[1024,256]{1,0:T(8,128)(2,1)} %param.3) | copy-start | bytes 1572868
  2.5 7.8 %collective-permute-start.4 = (bf16[576,256]{1,0:T(8,128)(2,1)S(1)}, bf16[576,256]{1,0:T(8,128)(2,1)S(1)}, u32[]{:S(2)}, u32[]{:S(2)}) collective-permute-start(bf16[576,256]{1,0:T(8,128)(2,1)S(1)} %pack.1.refs_1_.refs_2_), channel_id=1, source_target_pairs={{0,4},{4,0},{1,5},{5,1},{2,6},{6,2},{3,7},{7,3},{8,12},{12,8},{9,1... | collective-permute-start | bytes 884744 | tf_op jit(solution)/shard_map/fetch_points/ppermute | solution.py:38
  2.6 12.3 %collective-permute-start.1 = (bf16[512,256]{1,0:T(8,128)(2,1)S(1)}, bf16[512,256]{1,0:T(8,128)(2,1)S(1)}, u32[]{:S(2)}, u32[]{:S(2)}) collective-permute-start(bf16[512,256]{1,0:T(8,128)(2,1)S(1)} %constant_dynamic-slice_fusion.points_ref.refs_0_), channel_id=1, source_target_pairs={{0,8},{8,0},{16,24},{24,16},{32,40},{40,32},{48,56},{56,48},{64,72... | collective-permute-start | bytes 786440 | tf_op jit(solution)/shard_map/fetch_points/ppermute | solution.py:29
  4.6 13.2 %collective-permute-start = (bf16[512,256]{1,0:T(8,128)(2,1)S(1)}, bf16[512,256]{1,0:T(8,128)(2,1)S(1)}, u32[]{:S(2)}, u32[]{:S(2)}) collective-permute-start(bf16[512,256]{1,0:T(8,128)(2,1)S(1)} %constant_dynamic-slice_fusion.points_ref.refs_0_), channel_id=1, source_target_pairs={{0,32},{8,40},{16,48},{24,56},{32,0},{40,8},{48,16},{56,24},{64,96... | collective-permute-start | bytes 786440 | tf_op jit(solution)/shard_map/fetch_points/ppermute | solution.py:29
  6.2 19.3 %collective-permute-start.5 = (bf16[512,256]{1,0:T(8,128)(2,1)S(1)}, bf16[512,256]{1,0:T(8,128)(2,1)S(1)}, u32[]{:S(2)}, u32[]{:S(2)}) collective-permute-start(bf16[512,256]{1,0:T(8,128)(2,1)S(1)} %constant_dynamic-slice_fusion.points_ref.refs_0_), channel_id=1, source_target_pairs={{0,40},{8,32},{16,56},{24,48},{32,8},{40,0},{48,24},{56,16},{64,10... | collective-permute-start | bytes 786440 | tf_op jit(solution)/shard_map/fetch_points/ppermute | solution.py:29
  6.2 13.1 %collective-permute-start.3 = (bf16[576,256]{1,0:T(8,128)(2,1)S(1)}, bf16[576,256]{1,0:T(8,128)(2,1)S(1)}, u32[]{:S(2)}, u32[]{:S(2)}) collective-permute-start(bf16[576,256]{1,0:T(8,128)(2,1)S(1)} %pack.1.refs_1_.refs_2_), channel_id=1, source_target_pairs={{0,24},{8,16},{16,8},{24,0},{32,56},{40,48},{48,40},{56,32},{64,88... | collective-permute-start | bytes 884744 | tf_op jit(solution)/shard_map/fetch_points/ppermute | solution.py:29
  10.3 10.9 %collective-permute-start.2 = (bf16[576,256]{1,0:T(8,128)(2,1)S(1)}, bf16[576,256]{1,0:T(8,128)(2,1)S(1)}, u32[]{:S(2)}, u32[]{:S(2)}) collective-permute-start(bf16[576,256]{1,0:T(8,128)(2,1)S(1)} %pack.1.refs_1_.refs_2_), channel_id=1, source_target_pairs={{0,96},{8,104},{16,112},{24,120},{32,64},{40,72},{48,80},{56,88},{... | collective-permute-start | bytes 884744 | tf_op jit(solution)/shard_map/fetch_points/ppermute | solution.py:29
  13.3 0.8 %copy-start.1 = (f32[512,16]{0,1:T(8,128)S(1)}, f32[512,16]{0,1:T(8,128)}, u32[]{:S(2)}) copy-start(f32[512,16]{0,1:T(8,128)} %param.5) | copy-start | bytes 98308
  14.9 12.7 %collective-permute-start.8 = (bf16[576,256]{1,0:T(8,128)(2,1)S(1)}, bf16[576,256]{1,0:T(8,128)(2,1)S(1)}, u32[]{:S(2)}, u32[]{:S(2)}) collective-permute-start(bf16[576,256]{1,0:T(8,128)(2,1)S(1)} %pack.1.refs_1_.refs_2_), channel_id=1, source_target_pairs={{0,120},{8,112},{16,104},{24,96},{32,88},{40,80},{48,72},{56,64},{... | collective-permute-start | bytes 884744 | tf_op jit(solution)/shard_map/fetch_points/ppermute | solution.py:29
  21.2 2.4 %collective-permute-start.6 = (bf16[576,256]{1,0:T(8,128)(2,1)S(1)}, bf16[576,256]{1,0:T(8,128)(2,1)S(1)}, u32[]{:S(2)}, u32[]{:S(2)}) collective-permute-start(bf16[576,256]{1,0:T(8,128)(2,1)S(1)} %collective-permute-done.2.refs_3_), channel_id=1, source_target_pairs={{0,4},{4,0},{1,5},{5,1},{2,6},{6,2},{3,7},{7,3},{8,12},{12,8},{9,1... | collective-permute-start | bytes 884744 | tf_op jit(solution)/shard_map/build_tiles/ppermute | solution.py:38
  21.2 2.4 %collective-permute-start.7 = (bf16[576,256]{1,0:T(8,128)(2,1)S(1)}, bf16[576,256]{1,0:T(8,128)(2,1)S(1)}, u32[]{:S(2)}, u32[]{:S(2)}) collective-permute-start(bf16[576,256]{1,0:T(8,128)(2,1)S(1)} %collective-permute-done.3.refs_4_), channel_id=1, source_target_pairs={{0,4},{4,0},{1,5},{5,1},{2,6},{6,2},{3,7},{7,3},{8,12},{12,8},{9,1... | collective-permute-start | bytes 884744 | tf_op jit(solution)/shard_map/build_tiles/ppermute | solution.py:38
  27.6 1.8 %collective-permute-start.9 = (bf16[576,256]{1,0:T(8,128)(2,1)S(1)}, bf16[576,256]{1,0:T(8,128)(2,1)S(1)}, u32[]{:S(2)}, u32[]{:S(2)}) collective-permute-start(bf16[576,256]{1,0:T(8,128)(2,1)S(1)} %collective-permute-done.8.refs_4_), channel_id=1, source_target_pairs={{0,4},{4,0},{1,5},{5,1},{2,6},{6,2},{3,7},{7,3},{8,12},{12,8},{9,1... | collective-permute-start | bytes 884744 | tf_op jit(solution)/shard_map/build_tiles/ppermute | solution.py:38
  30.8 5.3 %collective-permute-start.10 = (bf16[80,512]{1,0:T(8,128)(2,1)S(1)}, bf16[80,512]{1,0:T(8,128)(2,1)S(1)}, u32[]{:S(2)}, u32[]{:S(2)}) collective-permute-start(bf16[80,512]{1,0:T(8,128)(2,1)S(1)} %get-tuple-element.64), channel_id=1, source_target_pairs={{0,32},{8,40},{16,48},{24,56},{32,0},{40,8},{48,16},{56,24},{64,96... | collective-permute-start | bytes 245768 | tf_op jit(solution)/shard_map/sum_over_rows/ppermute | solution.py:29
  31.1 6.3 %collective-permute-start.11 = (bf16[80,512]{1,0:T(8,128)(2,1)S(1)}, bf16[80,512]{1,0:T(8,128)(2,1)S(1)}, u32[]{:S(2)}, u32[]{:S(2)}) collective-permute-start(bf16[80,512]{1,0:T(8,128)(2,1)S(1)} %get-tuple-element.65), channel_id=1, source_target_pairs={{0,8},{8,0},{16,24},{24,16},{32,40},{40,32},{48,56},{56,48},{64,72... | collective-permute-start | bytes 245768 | tf_op jit(solution)/shard_map/sum_over_rows/ppermute | solution.py:29
  31.1 6.3 %collective-permute-start.12 = (bf16[80,512]{1,0:T(8,128)(2,1)S(1)}, bf16[80,512]{1,0:T(8,128)(2,1)S(1)}, u32[]{:S(2)}, u32[]{:S(2)}) collective-permute-start(bf16[80,512]{1,0:T(8,128)(2,1)S(1)} %get-tuple-element.66), channel_id=1, source_target_pairs={{0,40},{8,32},{16,56},{24,48},{32,8},{40,0},{48,24},{56,16},{64,10... | collective-permute-start | bytes 245768 | tf_op jit(solution)/shard_map/sum_over_rows/ppermute | solution.py:29
  38.9 1.5 %collective-permute-start.13 = (f32[16,2048]{1,0:T(8,128)S(1)}, f32[16,2048]{1,0:T(8,128)S(1)}, u32[]{:S(2)}, u32[]{:S(2)}) collective-permute-start(f32[16,2048]{1,0:T(8,128)S(1)} %second_product.2), channel_id=1, source_target_pairs={{0,4},{4,0},{1,5},{5,1},{2,6},{6,2},{3,7},{7,3},{8,12},{12,8},{9,1... | collective-permute-start | bytes 393224 | tf_op jit(solution)/shard_map/sum_over_columns/ppermute | solution.py:38
  40.4 6.0 %collective-permute-start.14 = (f32[16,512]{1,0:T(8,128)S(1)}, f32[16,512]{1,0:T(8,128)S(1)}, u32[]{:S(2)}, u32[]{:S(2)}) collective-permute-start(f32[16,512]{1,0:T(8,128)S(1)} %get-tuple-element.79), channel_id=1, source_target_pairs={{0,96},{8,104},{16,112},{24,120},{32,64},{40,72},{48,80},{56,88},{... | collective-permute-start | bytes 98312 | tf_op jit(solution)/shard_map/sum_over_columns/ppermute | solution.py:29
  43.3 5.1 %collective-permute-start.15 = (f32[16,512]{1,0:T(8,128)S(1)}, f32[16,512]{1,0:T(8,128)S(1)}, u32[]{:S(2)}, u32[]{:S(2)}) collective-permute-start(f32[16,512]{1,0:T(8,128)S(1)} %get-tuple-element.80), channel_id=1, source_target_pairs={{0,24},{8,16},{16,8},{24,0},{32,56},{40,48},{48,40},{56,32},{64,88... | collective-permute-start | bytes 98312 | tf_op jit(solution)/shard_map/sum_over_columns/ppermute | solution.py:29
  44.4 7.2 %collective-permute-start.16 = (f32[16,512]{1,0:T(8,128)S(1)}, f32[16,512]{1,0:T(8,128)S(1)}, u32[]{:S(2)}, u32[]{:S(2)}) collective-permute-start(f32[16,512]{1,0:T(8,128)S(1)} %get-tuple-element.81), channel_id=1, source_target_pairs={{0,120},{8,112},{16,104},{24,96},{32,88},{40,80},{48,72},{56,64},{... | collective-permute-start | bytes 98312 | tf_op jit(solution)/shard_map/sum_over_columns/ppermute | solution.py:29

commit v18 on v17

--- a/solution.py
+++ b/solution.py
@@ -131,7 +131,7 @@
                 )
 
 
-def build(rows, cols, own, probes, halves=(), prior=(), side=None):
+def build(rows, cols, own, probes, halves=(), prior=(), side=None, weight=64):
     features = rows[0].shape[1]
     height, width = len(rows) * own, len(cols) * own
     counts = (len(rows), len(cols), len(halves), len(prior), side is not None)
@@ -147,7 +147,7 @@
         out_shape=out_shape,
         compiler_params=pltpu.CompilerParams(vmem_limit_bytes=8 << 20),
         cost_estimate=pl.CostEstimate(
-            flops=height * width * features * 8, bytes_accessed=1 << 10, transcendentals=0
+            flops=height * width * features * weight // 8, bytes_accessed=1 << 10, transcendentals=0
         ),
         name="build_tile",
     )(*args)
@@ -319,8 +319,8 @@
         rows = [points] + [swap(points, offset) for offset in ROWS[1:]]
         cols = [message] + [swap(message, offset) for offset in SQUARE[1:]]
         first = [message, swap_core(message)]
-        tile_a, image_a, half_a = build([points], first, own, probes, side=side)
-        tile_b, image_b, half_b = build(rows[1:3], first, own, probes)
+        tile_a, image_a, half_a = build([points], first, own, probes, side=side, weight=1)
+        tile_b, image_b, half_b = build(rows[1:3], first, own, probes, weight=1)
         (rows[1], rows[2], cols[1], cols[2]), image_a, image_b = lax.optimization_barrier(
             ((rows[1], rows[2], cols[1], cols[2]), image_a, image_b)
         )

time: 64.9 us -> 66 us (1.017)
  waiting for transfers between devices: 10.4 us -> 14 us
  starting transfers between devices: 24 us -> 20.9 us
  blocking collectives: 11 us -> 11.7 us
    ppermute x12, waiting for transfers between devices: 10.1 us -> 13.7 us  [swap(): return lax.ppermute(value, ('y', 'z'), pairs)]
    ppermute x12, starting transfers between devices: 23.2 us -> 20.3 us  [swap(): return lax.ppermute(value, ('y', 'z'), pairs)]
  transfers between devices with their start and end apart: 17 -> 17, of which waited for: 6 -> 7; matrix products, arithmetic and copies ran while one was open for 0% -> 0% of each run, Pallas kernels for 17% -> 17%
where the time goes in v18:
time: 66 us; the launch traced here: 65 us
  starting transfers between devices  20.9 us (32%)
  Pallas kernels  15.4 us (23%)
  waiting for transfers between devices  14 us (21%)
  blocking collectives  11.7 us (18%)
  between operations  1.44 us (2%)
  local copies, waits for them, and re-layouts  0.85 us (1%)
  other arithmetic  0.76 us (1%)
    ppermute x12, starting transfers between devices, swap(): return lax.ppermute(value, ('y', 'z'), pairs)  20.3 us
    ppermute x12, waiting for transfers between devices, swap(): return lax.ppermute(value, ('y', 'z'), pairs)  13.7 us
    all_to_all x1, blocking collectives, on_device(): sums = lax.all_to_all(sums, ('y', 'z', 'c'), 0, 0, tiled=True)  11.7 us
    pallas_call x7, Pallas kernels, build(): pl.pallas_call(functools.partial(tile_kernel, counts, probes), out_shape=...  10.8 us
    pallas_call x2, Pallas kernels, second_product(): pl.pallas_call(functools.partial(second_kernel, own, half, places), in_sp...  2.9 us
  transfers between devices with their start and end apart: 17, of which 7 were waited for; matrix products, arithmetic and copies ran while one was open for 0% of the time, Pallas kernels for 17%

profile of v18, /device:TPU:0, one launch (start us, length us, event | category | flops | bytes accessed | tf_op | source)
XLA Modules:
  0.0 65.0 jit_solution(15894969541624195821)
XLA Ops:
  1.3 0.8 %bitcast_convert_fusion.side_ref = bf16[16,512]{1,0:T(8,128)(2,1)S(1)} fusion(f32[512,16]{0,1:T(8,128)} %param.5), kind=kLoop, calls=%fused_computation.1 | loop fusion | flops 8192 | bytes 49152 | tf_op jit(solution)/shard_map/fetch_points/convert_element_type | solution.py:318
  2.2 0.3 pack.1.refs_1_.refs_2_
  2.6 4.2 %collective-permute-start.3 = (bf16[576,256]{1,0:T(8,128)(2,1)S(1)}, bf16[576,256]{1,0:T(8,128)(2,1)S(1)}, u32[]{:S(2)}, u32[]{:S(2)}) collective-permute-start(bf16[576,256]{1,0:T(8,128)(2,1)S(1)} %pack.1.refs_1_.refs_2_), channel_id=1, source_target_pairs={{0,24},{8,16},{16,8},{24,0},{32,56},{40,48},{48,40},{56,32},{64,88... | collective-permute-start | bytes 884744 | tf_op jit(solution)/shard_map/fetch_points/ppermute | solution.py:29
  6.8 3.0 %collective-permute-start.2 = (bf16[576,256]{1,0:T(8,128)(2,1)S(1)}, bf16[576,256]{1,0:T(8,128)(2,1)S(1)}, u32[]{:S(2)}, u32[]{:S(2)}) collective-permute-start(bf16[576,256]{1,0:T(8,128)(2,1)S(1)} %pack.1.refs_1_.refs_2_), channel_id=1, source_target_pairs={{0,96},{8,104},{16,112},{24,120},{32,64},{40,72},{48,80},{56,88},{... | collective-permute-start | bytes 884744 | tf_op jit(solution)/shard_map/fetch_points/ppermute | solution.py:29
  9.8 0.1 collective-permute-start
  9.9 3.3 %collective-permute-start.5 = (bf16[512,256]{1,0:T(8,128)(2,1)S(1)}, bf16[512,256]{1,0:T(8,128)(2,1)S(1)}, u32[]{:S(2)}, u32[]{:S(2)}) collective-permute-start(bf16[512,256]{1,0:T(8,128)(2,1)S(1)} %constant_dynamic-slice_fusion.points_ref.refs_0_), channel_id=1, source_target_pairs={{0,40},{8,32},{16,56},{24,48},{32,8},{40,0},{48,24},{56,16},{64,10... | collective-permute-start | bytes 786440 | tf_op jit(solution)/shard_map/fetch_points/ppermute | solution.py:29
  13.3 0.8 %copy-done.1 = f32[512,16]{0,1:T(8,128)S(1)} copy-done((f32[512,16]{0,1:T(8,128)S(1)}, f32[512,16]{0,1:T(8,128)}, u32[]{:S(2)}) %copy-start.1) | copy-done | bytes 32792
  14.0 0.8 %build_tile.7 = (bf16[512,1024]{1,0:T(8,128)(2,1)S(1)}, f32[16,512]{1,0:T(8,128)S(1)}, f32[512,1]{1,0:T(8,128)S(1)}) custom-call(bf16[512,256]{1,0:T(8,128)(2,1)S(1)} %constant_dynamic-slice_fusion.points_ref.refs_0_, bf16[576,256]{1,0:T(8,128)(2,1)S(1)} %pack.1.refs_1_.refs_2_, bf16[576,256]{1,0:T(8,128)(2,1)S(1)} %collective-permute-done.4.refs_2_.refs_3_, ...), custom_call_target="tpu_custom_call" | custom-call | flops 16777216 | bytes 1024 | tf_op jit(solution)/shard_map/fetch_points/build_tile/pallas_call | solution.py:145
  14.9 3.2 %collective-permute-done.1.refs_1_.refs_2_ = bf16[512,256]{1,0:T(8,128)(2,1)S(1)} collective-permute-done((bf16[512,256]{1,0:T(8,128)(2,1)S(1)}, bf16[512,256]{1,0:T(8,128)(2,1)S(1)}, u32[]{:S(2)}, u32[]{:S(2)}) %collective-permute-start.1) | collective-permute-done | bytes 262176 | tf_op jit(solution)/shard_map/fetch_points/ppermute | solution.py:29
  18.1 0.9 %collective-permute-done.refs_0_.refs_1_ = bf16[512,256]{1,0:T(8,128)(2,1)S(1)} collective-permute-done((bf16[512,256]{1,0:T(8,128)(2,1)S(1)}, bf16[512,256]{1,0:T(8,128)(2,1)S(1)}, u32[]{:S(2)}, u32[]{:S(2)}) %collective-permute-start) | collective-permute-done | bytes 262176 | tf_op jit(solution)/shard_map/fetch_points/ppermute | solution.py:29
  19.0 1.4 %build_tile.8 = (bf16[1024,1024]{1,0:T(8,128)(2,1)S(1)}, f32[16,1024]{1,0:T(8,128)S(1)}, f32[1024,1]{1,0:T(8,128)S(1)}) custom-call(bf16[512,256]{1,0:T(8,128)(2,1)S(1)} %collective-permute-done.refs_0_.refs_1_, bf16[512,256]{1,0:T(8,128)(2,1)S(1)} %collective-permute-done.1.refs_1_.refs_2_, bf16[576,256]{1,0:T(8,128)(2,1)S(1)} %pack.1.refs_1_.refs_2_, ...), custom_call_target="tpu_custom_call" | custom-call | flops 33554432 | bytes 1024 | tf_op jit(solution)/shard_map/fetch_points/build_tile/pallas_call | solution.py:145
  20.5 0.5 collective-permute-start.7
  21.0 1.9 %build_tile.9 = (bf16[1536,1024]{1,0:T(8,128)(2,1)S(1)}, f32[16,1536]{1,0:T(8,128)S(1)}) custom-call(bf16[512,256]{1,0:T(8,128)(2,1)S(1)} %constant_dynamic-slice_fusion.points_ref.refs_0_, bf16[512,256]{1,0:T(8,128)(2,1)S(1)} %collective-permute-done.refs_0_.refs_1_, bf16[512,256]{1,0:T(8,128)(2,1)S(1)} %collective-permute-done.1.refs_1_.refs_2_, ...), custom_call_target="tpu_custom_call" | custom-call | flops 3221225472 | bytes 1024 | tf_op jit(solution)/shard_map/build_tiles/build_tile/pallas_call | solution.py:145
  22.9 1.9 %build_tile.10 = (bf16[1536,1024]{1,0:T(8,128)(2,1)S(1)}, f32[16,1536]{1,0:T(8,128)S(1)}) custom-call(bf16[512,256]{1,0:T(8,128)(2,1)S(1)} %constant_dynamic-slice_fusion.points_ref.refs_0_, bf16[512,256]{1,0:T(8,128)(2,1)S(1)} %collective-permute-done.refs_0_.refs_1_, bf16[512,256]{1,0:T(8,128)(2,1)S(1)} %collective-permute-done.1.refs_1_.refs_2_, ...), custom_call_target="tpu_custom_call" | custom-call | flops 3221225472 | bytes 1024 | tf_op jit(solution)/shard_map/build_tiles/build_tile/pallas_call | solution.py:145
  24.9 2.1 %build_tile.11 = (bf16[512,3072]{1,0:T(8,128)(2,1)S(1)}, f32[16,512]{1,0:T(8,128)S(1)}, f32[512,1]{1,0:T(8,128)S(1)}) custom-call(bf16[512,256]{1,0:T(8,128)(2,1)S(1)} %collective-permute-done.5.refs_0_.refs_3_, bf16[576,256]{1,0:T(8,128)(2,1)S(1)} %pack.1.refs_1_.refs_2_, bf16[576,256]{1,0:T(8,128)(2,1)S(1)} %collective-permute-done.4.refs_2_.refs_3_, ...), custom_call_target="tpu_custom_call" | custom-call | flops 3221225472 | bytes 1024 | tf_op jit(solution)/shard_map/build_tiles/build_tile/pallas_call | solution.py:145
  26.9 2.2 %collective-permute-done.8.refs_4_ = bf16[576,256]{1,0:T(8,128)(2,1)S(1)} collective-permute-done((bf16[576,256]{1,0:T(8,128)(2,1)S(1)}, bf16[576,256]{1,0:T(8,128)(2,1)S(1)}, u32[]{:S(2)}, u32[]{:S(2)}) %collective-permute-start.8) | collective-permute-done | bytes 294944 | tf_op jit(solution)/shard_map/fetch_points/ppermute | solution.py:29
  29.1 1.3 %build_tile.12 = (bf16[2048,512]{1,0:T(8,128)(2,1)S(1)}, f32[16,2048]{1,0:T(8,128)S(1)}) custom-call(bf16[512,256]{1,0:T(8,128)(2,1)S(1)} %constant_dynamic-slice_fusion.points_ref.refs_0_, bf16[512,256]{1,0:T(8,128)(2,1)S(1)} %collective-permute-done.refs_0_.refs_1_, bf16[512,256]{1,0:T(8,128)(2,1)S(1)} %collective-permute-done.1.refs_1_.refs_2_, ...), custom_call_target="tpu_custom_call" | custom-call | flops 2147483648 | bytes 1024 | tf_op jit(solution)/shard_map/build_tiles/build_tile/pallas_call | solution.py:145
  30.4 0.2 collective-permute-done.9.refs_4_
  30.7 1.3 %build_tile.13 = (bf16[2048,512]{1,0:T(8,128)(2,1)S(1)}, f32[16,2048]{1,0:T(8,128)S(1)}) custom-call(bf16[512,256]{1,0:T(8,128)(2,1)S(1)} %constant_dynamic-slice_fusion.points_ref.refs_0_, bf16[512,256]{1,0:T(8,128)(2,1)S(1)} %collective-permute-done.refs_0_.refs_1_, bf16[512,256]{1,0:T(8,128)(2,1)S(1)} %collective-permute-done.1.refs_1_.refs_2_, ...), custom_call_target="tpu_custom_call" | custom-call | flops 2147483648 | bytes 1024 | tf_op jit(solution)/shard_map/build_tiles/build_tile/pallas_call | solution.py:145
  32.2 0.2 collective-permute-start.11
  32.4 3.3 %collective-permute-start.12 = (bf16[80,512]{1,0:T(8,128)(2,1)S(1)}, bf16[80,512]{1,0:T(8,128)(2,1)S(1)}, u32[]{:S(2)}, u32[]{:S(2)}) collective-permute-start(bf16[80,512]{1,0:T(8,128)(2,1)S(1)} %get-tuple-element.66), channel_id=1, source_target_pairs={{0,40},{8,32},{16,56},{24,48},{32,8},{40,0},{48,24},{56,16},{64,10... | collective-permute-start | bytes 245768 | tf_op jit(solution)/shard_map/sum_over_rows/ppermute | solution.py:29
  35.7 1.7 %collective-permute-done.10.refs_1_ = bf16[80,512]{1,0:T(8,128)(2,1)S(1)} collective-permute-done((bf16[80,512]{1,0:T(8,128)(2,1)S(1)}, bf16[80,512]{1,0:T(8,128)(2,1)S(1)}, u32[]{:S(2)}, u32[]{:S(2)}) %collective-permute-start.10) | collective-permute-done | bytes 81952 | tf_op jit(solution)/shard_map/sum_over_rows/ppermute | solution.py:29
  37.4 1.3 %collective-permute-done.11.refs_2_ = bf16[80,512]{1,0:T(8,128)(2,1)S(1)} collective-permute-done((bf16[80,512]{1,0:T(8,128)(2,1)S(1)}, bf16[80,512]{1,0:T(8,128)(2,1)S(1)}, u32[]{:S(2)}, u32[]{:S(2)}) %collective-permute-start.11) | collective-permute-done | bytes 81952 | tf_op jit(solution)/shard_map/sum_over_rows/ppermute | solution.py:29
  38.7 1.4 %second_product.2 = f32[16,2048]{1,0:T(8,128)S(1)} custom-call(bf16[32,2048]{1,0:T(8,128)(2,1)S(1)} %get-tuple-element.76.narrow_ref, bf16[512,1024]{1,0:T(8,128)(2,1)S(1)} %get-tuple-element.69.refs_0_, bf16[1024,1024]{1,0:T(8,128)(2,1)S(1)} %get-tuple-element.70.refs_1_, bf16[1536,1024]{1,0:T(8,128)(2,1)S(1)} %get-tuple-element.71.refs_2_, ...), custom_call_target="tpu_custom_call" | custom-call | flops 134217728 | bytes 1024 | tf_op jit(solution)/shard_map/second_product/pallas_call | solution.py:231
  40.2 1.5 %second_product.3.mine_ref = f32[16,2048]{1,0:T(8,128)S(1)} custom-call(bf16[32,2048]{1,0:T(8,128)(2,1)S(1)} %get-tuple-element.76.narrow_ref, bf16[512,1024]{1,0:T(8,128)(2,1)S(1)} %get-tuple-element.69.refs_0_, bf16[1024,1024]{1,0:T(8,128)(2,1)S(1)} %get-tuple-element.70.refs_1_, bf16[1536,1024]{1,0:T(8,128)(2,1)S(1)} %get-tuple-element.71.refs_2_, ...), custom_call_target="tpu_custom_call" | custom-call | flops 134217728 | bytes 1024 | tf_op jit(solution)/shard_map/second_product/pallas_call | solution.py:231
  41.7 0.4 collective-permute-start.14
  42.1 2.7 %collective-permute-start.15 = (f32[16,512]{1,0:T(8,128)S(1)}, f32[16,512]{1,0:T(8,128)S(1)}, u32[]{:S(2)}, u32[]{:S(2)}) collective-permute-start(f32[16,512]{1,0:T(8,128)S(1)} %get-tuple-element.80), channel_id=1, source_target_pairs={{0,24},{8,16},{16,8},{24,0},{32,56},{40,48},{48,40},{56,32},{64,88... | collective-permute-start | bytes 98312 | tf_op jit(solution)/shard_map/sum_over_columns/ppermute | solution.py:29
  44.8 2.8 %collective-permute-start.16 = (f32[16,512]{1,0:T(8,128)S(1)}, f32[16,512]{1,0:T(8,128)S(1)}, u32[]{:S(2)}, u32[]{:S(2)}) collective-permute-start(f32[16,512]{1,0:T(8,128)S(1)} %get-tuple-element.81), channel_id=1, source_target_pairs={{0,120},{8,112},{16,104},{24,96},{32,88},{40,80},{48,72},{56,64},{... | collective-permute-start | bytes 98312 | tf_op jit(solution)/shard_map/sum_over_columns/ppermute | solution.py:29
  47.7 4.4 %collective-permute-done.16.refs_3_ = f32[16,512]{1,0:T(8,128)S(1)} collective-permute-done((f32[16,512]{1,0:T(8,128)S(1)}, f32[16,512]{1,0:T(8,128)S(1)}, u32[]{:S(2)}, u32[]{:S(2)}) %collective-permute-start.16) | collective-permute-done | bytes 32800 | tf_op jit(solution)/shard_map/sum_over_columns/ppermute | solution.py:29
  52.1 0.2 local_sums.1
  52.3 11.7 %all_to_all.8 = f32[32,1,128]{2,1,0:T(1,128)S(1)} all-to-all(f32[32,1,128]{2,1,0:T(1,128)S(1)} %broadcast_in_dim.2), channel_id=1, replica_groups=mesh['y'=4,'z'=4,'c'=2,'x'=4] {'y','z','c'}, dimensions={0} | all-to-all | bytes 32768 | tf_op jit(solution)/shard_map/final_sums/all_to_all | solution.py:365
  64.0 1.0 %finish.1 = (f32[16,512]{1,0:T(8,128)}, f32[16,512]{1,0:T(8,128)}) custom-call(f32[16,512]{1,0:T(8,128)S(1)} %bitcast.12, f32[16,512]{1,0:T(8,128)S(1)} %get-tuple-element.67.rho_ref, f32[16,512]{1,0:T(8,128)S(1)} %get-tuple-element.82.image_ref, f32[32,128]{1,0:T(8,128)S(1)} %bitcast.13), custom_call_target="tpu_custom_call" | custom-call | tf_op jit(solution)/shard_map/finish/pallas_call | solution.py:305
  (25 shorter events, 0.6 us)
Async XLA Ops:
  0.6 1.5 %copy-start = (bf16[1024,256]{1,0:T(8,128)(2,1)S(1)}, bf16[1024,256]{1,0:T(8,128)(2,1)}, u32[]{:S(2)}) copy-start(bf16[1024,256]{1,0:T(8,128)(2,1)} %param.3) | copy-start | bytes 1572868
  2.5 7.5 %collective-permute-start.4 = (bf16[576,256]{1,0:T(8,128)(2,1)S(1)}, bf16[576,256]{1,0:T(8,128)(2,1)S(1)}, u32[]{:S(2)}, u32[]{:S(2)}) collective-permute-start(bf16[576,256]{1,0:T(8,128)(2,1)S(1)} %pack.1.refs_1_.refs_2_), channel_id=1, source_target_pairs={{0,4},{4,0},{1,5},{5,1},{2,6},{6,2},{3,7},{7,3},{8,12},{12,8},{9,1... | collective-permute-start | bytes 884744 | tf_op jit(solution)/shard_map/fetch_points/ppermute | solution.py:38
  2.6 17.8 %collective-permute-start.3 = (bf16[576,256]{1,0:T(8,128)(2,1)S(1)}, bf16[576,256]{1,0:T(8,128)(2,1)S(1)}, u32[]{:S(2)}, u32[]{:S(2)}) collective-permute-start(bf16[576,256]{1,0:T(8,128)(2,1)S(1)} %pack.1.refs_1_.refs_2_), channel_id=1, source_target_pairs={{0,24},{8,16},{16,8},{24,0},{32,56},{40,48},{48,40},{56,32},{64,88... | collective-permute-start | bytes 884744 | tf_op jit(solution)/shard_map/fetch_points/ppermute | solution.py:29
  6.8 13.7 %collective-permute-start.2 = (bf16[576,256]{1,0:T(8,128)(2,1)S(1)}, bf16[576,256]{1,0:T(8,128)(2,1)S(1)}, u32[]{:S(2)}, u32[]{:S(2)}) collective-permute-start(bf16[576,256]{1,0:T(8,128)(2,1)S(1)} %pack.1.refs_1_.refs_2_), channel_id=1, source_target_pairs={{0,96},{8,104},{16,112},{24,120},{32,64},{40,72},{48,80},{56,88},{... | collective-permute-start | bytes 884744 | tf_op jit(solution)/shard_map/fetch_points/ppermute | solution.py:29
  9.8 8.3 %collective-permute-start.1 = (bf16[512,256]{1,0:T(8,128)(2,1)S(1)}, bf16[512,256]{1,0:T(8,128)(2,1)S(1)}, u32[]{:S(2)}, u32[]{:S(2)}) collective-permute-start(bf16[512,256]{1,0:T(8,128)(2,1)S(1)} %constant_dynamic-slice_fusion.points_ref.refs_0_), channel_id=1, source_target_pairs={{0,8},{8,0},{16,24},{24,16},{32,40},{40,32},{48,56},{56,48},{64,72... | collective-permute-start | bytes 786440 | tf_op jit(solution)/shard_map/fetch_points/ppermute | solution.py:29
  9.8 9.2 %collective-permute-start = (bf16[512,256]{1,0:T(8,128)(2,1)S(1)}, bf16[512,256]{1,0:T(8,128)(2,1)S(1)}, u32[]{:S(2)}, u32[]{:S(2)}) collective-permute-start(bf16[512,256]{1,0:T(8,128)(2,1)S(1)} %constant_dynamic-slice_fusion.points_ref.refs_0_), channel_id=1, source_target_pairs={{0,32},{8,40},{16,48},{24,56},{32,0},{40,8},{48,16},{56,24},{64,96... | collective-permute-start | bytes 786440 | tf_op jit(solution)/shard_map/fetch_points/ppermute | solution.py:29
  9.9 14.9 %collective-permute-start.5 = (bf16[512,256]{1,0:T(8,128)(2,1)S(1)}, bf16[512,256]{1,0:T(8,128)(2,1)S(1)}, u32[]{:S(2)}, u32[]{:S(2)}) collective-permute-start(bf16[512,256]{1,0:T(8,128)(2,1)S(1)} %constant_dynamic-slice_fusion.points_ref.refs_0_), channel_id=1, source_target_pairs={{0,40},{8,32},{16,56},{24,48},{32,8},{40,0},{48,24},{56,16},{64,10... | collective-permute-start | bytes 786440 | tf_op jit(solution)/shard_map/fetch_points/ppermute | solution.py:29
  13.3 0.8 %copy-start.1 = (f32[512,16]{0,1:T(8,128)S(1)}, f32[512,16]{0,1:T(8,128)}, u32[]{:S(2)}) copy-start(f32[512,16]{0,1:T(8,128)} %param.5) | copy-start | bytes 98308
  18.1 11.0 %collective-permute-start.8 = (bf16[576,256]{1,0:T(8,128)(2,1)S(1)}, bf16[576,256]{1,0:T(8,128)(2,1)S(1)}, u32[]{:S(2)}, u32[]{:S(2)}) collective-permute-start(bf16[576,256]{1,0:T(8,128)(2,1)S(1)} %pack.1.refs_1_.refs_2_), channel_id=1, source_target_pairs={{0,120},{8,112},{16,104},{24,96},{32,88},{40,80},{48,72},{56,64},{... | collective-permute-start | bytes 884744 | tf_op jit(solution)/shard_map/fetch_points/ppermute | solution.py:29
  20.4 2.5 %collective-permute-start.6 = (bf16[576,256]{1,0:T(8,128)(2,1)S(1)}, bf16[576,256]{1,0:T(8,128)(2,1)S(1)}, u32[]{:S(2)}, u32[]{:S(2)}) collective-permute-start(bf16[576,256]{1,0:T(8,128)(2,1)S(1)} %collective-permute-done.2.refs_3_), channel_id=1, source_target_pairs={{0,4},{4,0},{1,5},{5,1},{2,6},{6,2},{3,7},{7,3},{8,12},{12,8},{9,1... | collective-permute-start | bytes 884744 | tf_op jit(solution)/shard_map/build_tiles/ppermute | solution.py:38
  20.5 2.4 %collective-permute-start.7 = (bf16[576,256]{1,0:T(8,128)(2,1)S(1)}, bf16[576,256]{1,0:T(8,128)(2,1)S(1)}, u32[]{:S(2)}, u32[]{:S(2)}) collective-permute-start(bf16[576,256]{1,0:T(8,128)(2,1)S(1)} %collective-permute-done.3.refs_4_), channel_id=1, source_target_pairs={{0,4},{4,0},{1,5},{5,1},{2,6},{6,2},{3,7},{7,3},{8,12},{12,8},{9,1... | collective-permute-start | bytes 884744 | tf_op jit(solution)/shard_map/build_tiles/ppermute | solution.py:38
  29.1 1.6 %collective-permute-start.9 = (bf16[576,256]{1,0:T(8,128)(2,1)S(1)}, bf16[576,256]{1,0:T(8,128)(2,1)S(1)}, u32[]{:S(2)}, u32[]{:S(2)}) collective-permute-start(bf16[576,256]{1,0:T(8,128)(2,1)S(1)} %collective-permute-done.8.refs_4_), channel_id=1, source_target_pairs={{0,4},{4,0},{1,5},{5,1},{2,6},{6,2},{3,7},{7,3},{8,12},{12,8},{9,1... | collective-permute-start | bytes 884744 | tf_op jit(solution)/shard_map/build_tiles/ppermute | solution.py:38
  32.1 5.3 %collective-permute-start.10 = (bf16[80,512]{1,0:T(8,128)(2,1)S(1)}, bf16[80,512]{1,0:T(8,128)(2,1)S(1)}, u32[]{:S(2)}, u32[]{:S(2)}) collective-permute-start(bf16[80,512]{1,0:T(8,128)(2,1)S(1)} %get-tuple-element.64), channel_id=1, source_target_pairs={{0,32},{8,40},{16,48},{24,56},{32,0},{40,8},{48,16},{56,24},{64,96... | collective-permute-start | bytes 245768 | tf_op jit(solution)/shard_map/sum_over_rows/ppermute | solution.py:29
  32.2 6.5 %collective-permute-start.11 = (bf16[80,512]{1,0:T(8,128)(2,1)S(1)}, bf16[80,512]{1,0:T(8,128)(2,1)S(1)}, u32[]{:S(2)}, u32[]{:S(2)}) collective-permute-start(bf16[80,512]{1,0:T(8,128)(2,1)S(1)} %get-tuple-element.65), channel_id=1, source_target_pairs={{0,8},{8,0},{16,24},{24,16},{32,40},{40,32},{48,56},{56,48},{64,72... | collective-permute-start | bytes 245768 | tf_op jit(solution)/shard_map/sum_over_rows/ppermute | solution.py:29
  32.4 6.3 %collective-permute-start.12 = (bf16[80,512]{1,0:T(8,128)(2,1)S(1)}, bf16[80,512]{1,0:T(8,128)(2,1)S(1)}, u32[]{:S(2)}, u32[]{:S(2)}) collective-permute-start(bf16[80,512]{1,0:T(8,128)(2,1)S(1)} %get-tuple-element.66), channel_id=1, source_target_pairs={{0,40},{8,32},{16,56},{24,48},{32,8},{40,0},{48,24},{56,16},{64,10... | collective-permute-start | bytes 245768 | tf_op jit(solution)/shard_map/sum_over_rows/ppermute | solution.py:29
  40.2 1.5 %collective-permute-start.13 = (f32[16,2048]{1,0:T(8,128)S(1)}, f32[16,2048]{1,0:T(8,128)S(1)}, u32[]{:S(2)}, u32[]{:S(2)}) collective-permute-start(f32[16,2048]{1,0:T(8,128)S(1)} %second_product.2), channel_id=1, source_target_pairs={{0,4},{4,0},{1,5},{5,1},{2,6},{6,2},{3,7},{7,3},{8,12},{12,8},{9,1... | collective-permute-start | bytes 393224 | tf_op jit(solution)/shard_map/sum_over_columns/ppermute | solution.py:38
  41.7 6.0 %collective-permute-start.14 = (f32[16,512]{1,0:T(8,128)S(1)}, f32[16,512]{1,0:T(8,128)S(1)}, u32[]{:S(2)}, u32[]{:S(2)}) collective-permute-start(f32[16,512]{1,0:T(8,128)S(1)} %get-tuple-element.79), channel_id=1, source_target_pairs={{0,96},{8,104},{16,112},{24,120},{32,64},{40,72},{48,80},{56,88},{... | collective-permute-start | bytes 98312 | tf_op jit(solution)/shard_map/sum_over_columns/ppermute | solution.py:29
  42.1 5.6 %collective-permute-start.15 = (f32[16,512]{1,0:T(8,128)S(1)}, f32[16,512]{1,0:T(8,128)S(1)}, u32[]{:S(2)}, u32[]{:S(2)}) collective-permute-start(f32[16,512]{1,0:T(8,128)S(1)} %get-tuple-element.80), channel_id=1, source_target_pairs={{0,24},{8,16},{16,8},{24,0},{32,56},{40,48},{48,40},{56,32},{64,88... | collective-permute-start | bytes 98312 | tf_op jit(solution)/shard_map/sum_over_columns/ppermute | solution.py:29
  44.8 7.2 %collective-permute-start.16 = (f32[16,512]{1,0:T(8,128)S(1)}, f32[16,512]{1,0:T(8,128)S(1)}, u32[]{:S(2)}, u32[]{:S(2)}) collective-permute-start(f32[16,512]{1,0:T(8,128)S(1)} %get-tuple-element.81), channel_id=1, source_target_pairs={{0,120},{8,112},{16,104},{24,96},{32,88},{40,80},{48,72},{56,64},{... | collective-permute-start | bytes 98312 | tf_op jit(solution)/shard_map/sum_over_columns/ppermute | solution.py:29

commit v19 on v18

--- a/solution.py
+++ b/solution.py
@@ -317,19 +317,26 @@
     with jax.named_scope("fetch_points"):
         message = pack(points, side.astype(jnp.bfloat16))
         rows = [points] + [swap(points, offset) for offset in ROWS[1:]]
-        cols = [message] + [swap(message, offset) for offset in SQUARE[1:]]
+        cols = [message] + [swap(message, offset) for offset in SQUARE[1:3]]
         first = [message, swap_core(message)]
         tile_a, image_a, half_a = build([points], first, own, probes, side=side, weight=1)
+        (rows[1], rows[2]), image_a = lax.optimization_barrier(((rows[1], rows[2]), image_a))
         tile_b, image_b, half_b = build(rows[1:3], first, own, probes, weight=1)
-        (rows[1], rows[2], cols[1], cols[2]), image_a, image_b = lax.optimization_barrier(
-            ((rows[1], rows[2], cols[1], cols[2]), image_a, image_b)
-        )
+        half = [half_a, half_b]
+        again, image_b = lax.optimization_barrier((message, image_b))
+        cols.append(swap(again, SQUARE[3]))
 
     with jax.named_scope("build_tiles"):
-        half = [half_a, half_b]
-        others = [swap_core(cols[1]), swap_core(cols[2])]
-        tile_d, image = build(rows[:3], cols[1:3], own, probes, half, [image_a, image_b])
-        tile_e, image = build(rows[:3], others, own, probes, half, [image])
+        cols[2], image_b = lax.optimization_barrier((cols[2], image_b))
+        tile_c, image = build(rows[:3], cols[2:3], own, probes, half, [image_a, image_b])
+        other_z = swap_core(cols[2])
+        cols[1], image = lax.optimization_barrier((cols[1], image))
+        tile_d, image = build(rows[:3], cols[1:2], own, probes, half, [image])
+        other_y = swap_core(cols[1])
+        others = [other_y, other_z]
+        tile_e, image = build(rows[:3], [other_z], own, probes, half, [image])
+        other_y, image = lax.optimization_barrier((other_y, image))
+        tile_i, image = build(rows[:3], [other_y], own, probes, half, [image])
         rows[3], image = lax.optimization_barrier((rows[3], image))
         tile_f, image_far, half_far = build([rows[3]], first + cols[1:3] + others, own, probes)
         cols[3], image_far = lax.optimization_barrier((cols[3], image_far))
@@ -341,7 +348,9 @@
             (tile_a, 0, 0),
             (tile_b, own, 0),
             (tile_d, 0, 2 * own),
-            (tile_e, 0, 4 * own),
+            (tile_c, 0, 3 * own),
+            (tile_i, 0, 4 * own),
+            (tile_e, 0, 5 * own),
             (tile_f, 3 * own, 0),
             (tile_g, 0, 6 * own),
             (tile_h, 0, 7 * own),

time: 66 us -> 67.6 us (1.024)
  starting transfers between devices: 20.9 us -> 23.1 us
  waiting for transfers between devices: 14 us -> 12.8 us
    ppermute x12, starting transfers between devices: 20.3 us -> 22.7 us  [swap(): return lax.ppermute(value, ('y', 'z'), pairs)]
    ppermute x12, waiting for transfers between devices: 13.7 us -> 12.6 us  [swap(): return lax.ppermute(value, ('y', 'z'), pairs)]
    pallas_call x7 -> x9, Pallas kernels: 10.8 us -> 11.3 us  [build(): pl.pallas_call(functools.partial(tile_kernel, counts, probes), out_shape=...]
  transfers between devices with their start and end apart: 17 -> 17, of which waited for: 7 -> 8; matrix products, arithmetic and copies ran while one was open for 0% -> 0% of each run, Pallas kernels for 17% -> 17%
where the time goes in v19:
time: 67.6 us; the launch traced here: 66.5 us
  starting transfers between devices  23.1 us (34%)
  Pallas kernels  15.9 us (24%)
  waiting for transfers between devices  12.8 us (19%)
  blocking collectives  11.7 us (17%)
  between operations  1.42 us (2%)
  local copies, waits for them, and re-layouts  0.85 us (1%)
  other arithmetic  0.76 us (1%)
    ppermute x12, starting transfers between devices, swap(): return lax.ppermute(value, ('y', 'z'), pairs)  22.7 us
    ppermute x12, waiting for transfers between devices, swap(): return lax.ppermute(value, ('y', 'z'), pairs)  12.6 us
    all_to_all x1, blocking collectives, on_device(): sums = lax.all_to_all(sums, ('y', 'z', 'c'), 0, 0, tiled=True)  11.7 us
    pallas_call x9, Pallas kernels, build(): pl.pallas_call(functools.partial(tile_kernel, counts, probes), out_shape=...  11.3 us
    pallas_call x2, Pallas kernels, second_product(): pl.pallas_call(functools.partial(second_kernel, own, half, places), in_sp...  2.87 us
  transfers between devices with their start and end apart: 17, of which 8 were waited for; matrix products, arithmetic and copies ran while one was open for 0% of the time, Pallas kernels for 17%

profile of v19, /device:TPU:0, one launch (start us, length us, event | category | flops | bytes accessed | tf_op | source)
XLA Modules:
  0.0 66.5 jit_solution(10951840693879759123)
XLA Ops:
  1.3 0.8 %bitcast_convert_fusion.side_ref = bf16[16,512]{1,0:T(8,128)(2,1)S(1)} fusion(f32[512,16]{0,1:T(8,128)} %param.5), kind=kLoop, calls=%fused_computation.1 | loop fusion | flops 8192 | bytes 49152 | tf_op jit(solution)/shard_map/fetch_points/convert_element_type | solution.py:318
  2.6 4.2 %collective-permute-start.5 = (bf16[576,256]{1,0:T(8,128)(2,1)S(1)}, bf16[576,256]{1,0:T(8,128)(2,1)S(1)}, u32[]{:S(2)}, u32[]{:S(2)}) collective-permute-start(bf16[576,256]{1,0:T(8,128)(2,1)S(1)} %pack.1.refs_1_.refs_2_), channel_id=1, source_target_pairs={{0,24},{8,16},{16,8},{24,0},{32,56},{40,48},{48,40},{56,32},{64,88... | collective-permute-start | bytes 884744 | tf_op jit(solution)/shard_map/fetch_points/ppermute | solution.py:29
  6.8 1.6 %collective-permute-start = (bf16[512,256]{1,0:T(8,128)(2,1)S(1)}, bf16[512,256]{1,0:T(8,128)(2,1)S(1)}, u32[]{:S(2)}, u32[]{:S(2)}) collective-permute-start(bf16[512,256]{1,0:T(8,128)(2,1)S(1)} %constant_dynamic-slice_fusion.points_ref.refs_0_), channel_id=1, source_target_pairs={{0,32},{8,40},{16,48},{24,56},{32,0},{40,8},{48,16},{56,24},{64,96... | collective-permute-start | bytes 786440 | tf_op jit(solution)/shard_map/fetch_points/ppermute | solution.py:29
  8.3 2.2 %collective-permute-start.4 = (bf16[576,256]{1,0:T(8,128)(2,1)S(1)}, bf16[576,256]{1,0:T(8,128)(2,1)S(1)}, u32[]{:S(2)}, u32[]{:S(2)}) collective-permute-start(bf16[576,256]{1,0:T(8,128)(2,1)S(1)} %pack.1.refs_1_.refs_2_), channel_id=1, source_target_pairs={{0,96},{8,104},{16,112},{24,120},{32,64},{40,72},{48,80},{56,88},{... | collective-permute-start | bytes 884744 | tf_op jit(solution)/shard_map/fetch_points/ppermute | solution.py:29
  10.5 2.1 %collective-permute-start.3 = (bf16[512,256]{1,0:T(8,128)(2,1)S(1)}, bf16[512,256]{1,0:T(8,128)(2,1)S(1)}, u32[]{:S(2)}, u32[]{:S(2)}) collective-permute-start(bf16[512,256]{1,0:T(8,128)(2,1)S(1)} %constant_dynamic-slice_fusion.points_ref.refs_0_), channel_id=1, source_target_pairs={{0,40},{8,32},{16,56},{24,48},{32,8},{40,0},{48,24},{56,16},{64,10... | collective-permute-start | bytes 786440 | tf_op jit(solution)/shard_map/fetch_points/ppermute | solution.py:29
  12.7 0.8 %copy-done.1 = f32[512,16]{0,1:T(8,128)S(1)} copy-done((f32[512,16]{0,1:T(8,128)S(1)}, f32[512,16]{0,1:T(8,128)}, u32[]{:S(2)}) %copy-start.1) | copy-done | bytes 32792
  13.4 0.8 %build_tile.9 = (bf16[512,1024]{1,0:T(8,128)(2,1)S(1)}, f32[16,512]{1,0:T(8,128)S(1)}, f32[512,1]{1,0:T(8,128)S(1)}) custom-call(bf16[512,256]{1,0:T(8,128)(2,1)S(1)} %constant_dynamic-slice_fusion.points_ref.refs_0_, bf16[576,256]{1,0:T(8,128)(2,1)S(1)} %pack.1.refs_1_.refs_2_, bf16[576,256]{1,0:T(8,128)(2,1)S(1)} %collective-permute-done.2.refs_2_.refs_3_, ...), custom_call_target="tpu_custom_call" | custom-call | flops 16777216 | bytes 1024 | tf_op jit(solution)/shard_map/fetch_points/build_tile/pallas_call | solution.py:145
  14.3 0.9 %collective-permute-done.1.refs_1_.refs_2_ = bf16[512,256]{1,0:T(8,128)(2,1)S(1)} collective-permute-done((bf16[512,256]{1,0:T(8,128)(2,1)S(1)}, bf16[512,256]{1,0:T(8,128)(2,1)S(1)}, u32[]{:S(2)}, u32[]{:S(2)}) %collective-permute-start.1) | collective-permute-done | bytes 262176 | tf_op jit(solution)/shard_map/fetch_points/ppermute | solution.py:29
  15.1 0.8 %collective-permute-done.refs_0_.refs_1_ = bf16[512,256]{1,0:T(8,128)(2,1)S(1)} collective-permute-done((bf16[512,256]{1,0:T(8,128)(2,1)S(1)}, bf16[512,256]{1,0:T(8,128)(2,1)S(1)}, u32[]{:S(2)}, u32[]{:S(2)}) %collective-permute-start) | collective-permute-done | bytes 262176 | tf_op jit(solution)/shard_map/fetch_points/ppermute | solution.py:29
  15.9 1.4 %build_tile.10 = (bf16[1024,1024]{1,0:T(8,128)(2,1)S(1)}, f32[16,1024]{1,0:T(8,128)S(1)}, f32[1024,1]{1,0:T(8,128)S(1)}) custom-call(bf16[512,256]{1,0:T(8,128)(2,1)S(1)} %collective-permute-done.refs_0_.refs_1_, bf16[512,256]{1,0:T(8,128)(2,1)S(1)} %collective-permute-done.1.refs_1_.refs_2_, bf16[576,256]{1,0:T(8,128)(2,1)S(1)} %pack.1.refs_1_.refs_2_, ...), custom_call_target="tpu_custom_call" | custom-call | flops 33554432 | bytes 1024 | tf_op jit(solution)/shard_map/fetch_points/build_tile/pallas_call | solution.py:145
  17.4 3.0 %collective-permute-start.8 = (bf16[576,256]{1,0:T(8,128)(2,1)S(1)}, bf16[576,256]{1,0:T(8,128)(2,1)S(1)}, u32[]{:S(2)}, u32[]{:S(2)}) collective-permute-start(bf16[576,256]{1,0:T(8,128)(2,1)S(1)} %pack.1.refs_1_.refs_2_), channel_id=1, source_target_pairs={{0,120},{8,112},{16,104},{24,96},{32,88},{40,80},{48,72},{56,64},{... | collective-permute-start | bytes 884744 | tf_op jit(solution)/shard_map/fetch_points/ppermute | solution.py:29
  20.4 1.1 %build_tile.11 = (bf16[1536,512]{1,0:T(8,128)(2,1)S(1)}, f32[16,1536]{1,0:T(8,128)S(1)}) custom-call(bf16[512,256]{1,0:T(8,128)(2,1)S(1)} %constant_dynamic-slice_fusion.points_ref.refs_0_, bf16[512,256]{1,0:T(8,128)(2,1)S(1)} %collective-permute-done.refs_0_.refs_1_, bf16[512,256]{1,0:T(8,128)(2,1)S(1)} %collective-permute-done.1.refs_1_.refs_2_, ...), custom_call_target="tpu_custom_call" | custom-call | flops 1610612736 | bytes 1024 | tf_op jit(solution)/shard_map/build_tiles/build_tile/pallas_call | solution.py:145
  21.7 1.1 %build_tile.12 = (bf16[1536,512]{1,0:T(8,128)(2,1)S(1)}, f32[16,1536]{1,0:T(8,128)S(1)}) custom-call(bf16[512,256]{1,0:T(8,128)(2,1)S(1)} %constant_dynamic-slice_fusion.points_ref.refs_0_, bf16[512,256]{1,0:T(8,128)(2,1)S(1)} %collective-permute-done.refs_0_.refs_1_, bf16[512,256]{1,0:T(8,128)(2,1)S(1)} %collective-permute-done.1.refs_1_.refs_2_, ...), custom_call_target="tpu_custom_call" | custom-call | flops 1610612736 | bytes 1024 | tf_op jit(solution)/shard_map/build_tiles/build_tile/pallas_call | solution.py:145
  22.8 1.1 %build_tile.13 = (bf16[1536,512]{1,0:T(8,128)(2,1)S(1)}, f32[16,1536]{1,0:T(8,128)S(1)}) custom-call(bf16[512,256]{1,0:T(8,128)(2,1)S(1)} %constant_dynamic-slice_fusion.points_ref.refs_0_, bf16[512,256]{1,0:T(8,128)(2,1)S(1)} %collective-permute-done.refs_0_.refs_1_, bf16[512,256]{1,0:T(8,128)(2,1)S(1)} %collective-permute-done.1.refs_1_.refs_2_, ...), custom_call_target="tpu_custom_call" | custom-call | flops 1610612736 | bytes 1024 | tf_op jit(solution)/shard_map/build_tiles/build_tile/pallas_call | solution.py:145
  23.9 1.1 %build_tile.14 = (bf16[1536,512]{1,0:T(8,128)(2,1)S(1)}, f32[16,1536]{1,0:T(8,128)S(1)}) custom-call(bf16[512,256]{1,0:T(8,128)(2,1)S(1)} %constant_dynamic-slice_fusion.points_ref.refs_0_, bf16[512,256]{1,0:T(8,128)(2,1)S(1)} %collective-permute-done.refs_0_.refs_1_, bf16[512,256]{1,0:T(8,128)(2,1)S(1)} %collective-permute-done.1.refs_1_.refs_2_, ...), custom_call_target="tpu_custom_call" | custom-call | flops 1610612736 | bytes 1024 | tf_op jit(solution)/shard_map/build_tiles/build_tile/pallas_call | solution.py:145
  25.0 2.1 %build_tile.15 = (bf16[512,3072]{1,0:T(8,128)(2,1)S(1)}, f32[16,512]{1,0:T(8,128)S(1)}, f32[512,1]{1,0:T(8,128)S(1)}) custom-call(bf16[512,256]{1,0:T(8,128)(2,1)S(1)} %collective-permute-done.3.refs_0_.refs_3_, bf16[576,256]{1,0:T(8,128)(2,1)S(1)} %pack.1.refs_1_.refs_2_, bf16[576,256]{1,0:T(8,128)(2,1)S(1)} %collective-permute-done.2.refs_2_.refs_3_, ...), custom_call_target="tpu_custom_call" | custom-call | flops 3221225472 | bytes 1024 | tf_op jit(solution)/shard_map/build_tiles/build_tile/pallas_call | solution.py:145
  27.1 3.0 %collective-permute-done.8.refs_4_ = bf16[576,256]{1,0:T(8,128)(2,1)S(1)} collective-permute-done((bf16[576,256]{1,0:T(8,128)(2,1)S(1)}, bf16[576,256]{1,0:T(8,128)(2,1)S(1)}, u32[]{:S(2)}, u32[]{:S(2)}) %collective-permute-start.8) | collective-permute-done | bytes 294944 | tf_op jit(solution)/shard_map/fetch_points/ppermute | solution.py:29
  30.1 1.3 %build_tile.16 = (bf16[2048,512]{1,0:T(8,128)(2,1)S(1)}, f32[16,2048]{1,0:T(8,128)S(1)}) custom-call(bf16[512,256]{1,0:T(8,128)(2,1)S(1)} %constant_dynamic-slice_fusion.points_ref.refs_0_, bf16[512,256]{1,0:T(8,128)(2,1)S(1)} %collective-permute-done.refs_0_.refs_1_, bf16[512,256]{1,0:T(8,128)(2,1)S(1)} %collective-permute-done.1.refs_1_.refs_2_, ...), custom_call_target="tpu_custom_call" | custom-call | flops 2147483648 | bytes 1024 | tf_op jit(solution)/shard_map/build_tiles/build_tile/pallas_call | solution.py:145
  31.7 1.3 %build_tile.17 = (bf16[2048,512]{1,0:T(8,128)(2,1)S(1)}, f32[16,2048]{1,0:T(8,128)S(1)}) custom-call(bf16[512,256]{1,0:T(8,128)(2,1)S(1)} %constant_dynamic-slice_fusion.points_ref.refs_0_, bf16[512,256]{1,0:T(8,128)(2,1)S(1)} %collective-permute-done.refs_0_.refs_1_, bf16[512,256]{1,0:T(8,128)(2,1)S(1)} %collective-permute-done.1.refs_1_.refs_2_, ...), custom_call_target="tpu_custom_call" | custom-call | flops 2147483648 | bytes 1024 | tf_op jit(solution)/shard_map/build_tiles/build_tile/pallas_call | solution.py:145
  33.1 0.4 collective-permute-start.10
  33.6 0.9 %collective-permute-start.11 = (bf16[80,512]{1,0:T(8,128)(2,1)S(1)}, bf16[80,512]{1,0:T(8,128)(2,1)S(1)}, u32[]{:S(2)}, u32[]{:S(2)}) collective-permute-start(bf16[80,512]{1,0:T(8,128)(2,1)S(1)} %get-tuple-element.81), channel_id=1, source_target_pairs={{0,8},{8,0},{16,24},{24,16},{32,40},{40,32},{48,56},{56,48},{64,72... | collective-permute-start | bytes 245768 | tf_op jit(solution)/shard_map/sum_over_rows/ppermute | solution.py:29
  34.4 2.3 %collective-permute-start.12 = (bf16[80,512]{1,0:T(8,128)(2,1)S(1)}, bf16[80,512]{1,0:T(8,128)(2,1)S(1)}, u32[]{:S(2)}, u32[]{:S(2)}) collective-permute-start(bf16[80,512]{1,0:T(8,128)(2,1)S(1)} %get-tuple-element.82), channel_id=1, source_target_pairs={{0,40},{8,32},{16,56},{24,48},{32,8},{40,0},{48,24},{56,16},{64,10... | collective-permute-start | bytes 245768 | tf_op jit(solution)/shard_map/sum_over_rows/ppermute | solution.py:29
  36.7 1.7 %collective-permute-done.10.refs_1_ = bf16[80,512]{1,0:T(8,128)(2,1)S(1)} collective-permute-done((bf16[80,512]{1,0:T(8,128)(2,1)S(1)}, bf16[80,512]{1,0:T(8,128)(2,1)S(1)}, u32[]{:S(2)}, u32[]{:S(2)}) %collective-permute-start.10) | collective-permute-done | bytes 81952 | tf_op jit(solution)/shard_map/sum_over_rows/ppermute | solution.py:29
  38.4 1.5 %collective-permute-done.12.refs_3_ = bf16[80,512]{1,0:T(8,128)(2,1)S(1)} collective-permute-done((bf16[80,512]{1,0:T(8,128)(2,1)S(1)}, bf16[80,512]{1,0:T(8,128)(2,1)S(1)}, u32[]{:S(2)}, u32[]{:S(2)}) %collective-permute-start.12) | collective-permute-done | bytes 81952 | tf_op jit(solution)/shard_map/sum_over_rows/ppermute | solution.py:29
  40.0 1.4 %second_product.2 = f32[16,2048]{1,0:T(8,128)S(1)} custom-call(bf16[32,2048]{1,0:T(8,128)(2,1)S(1)} %get-tuple-element.94.narrow_ref, bf16[512,1024]{1,0:T(8,128)(2,1)S(1)} %get-tuple-element.85.refs_0_, bf16[1024,1024]{1,0:T(8,128)(2,1)S(1)} %get-tuple-element.86.refs_1_, bf16[1536,512]{1,0:T(8,128)(2,1)S(1)} %get-tuple-element.87.refs_2_, ...), custom_call_target="tpu_custom_call" | custom-call | flops 134217728 | bytes 1024 | tf_op jit(solution)/shard_map/second_product/pallas_call | solution.py:231
  41.4 1.4 %second_product.3.mine_ref = f32[16,2048]{1,0:T(8,128)S(1)} custom-call(bf16[32,2048]{1,0:T(8,128)(2,1)S(1)} %get-tuple-element.94.narrow_ref, bf16[512,1024]{1,0:T(8,128)(2,1)S(1)} %get-tuple-element.85.refs_0_, bf16[1024,1024]{1,0:T(8,128)(2,1)S(1)} %get-tuple-element.86.refs_1_, bf16[1536,512]{1,0:T(8,128)(2,1)S(1)} %get-tuple-element.87.refs_2_, ...), custom_call_target="tpu_custom_call" | custom-call | flops 134217728 | bytes 1024 | tf_op jit(solution)/shard_map/second_product/pallas_call | solution.py:231
  42.9 3.1 %collective-permute-start.14 = (f32[16,512]{1,0:T(8,128)S(1)}, f32[16,512]{1,0:T(8,128)S(1)}, u32[]{:S(2)}, u32[]{:S(2)}) collective-permute-start(f32[16,512]{1,0:T(8,128)S(1)} %get-tuple-element.97), channel_id=1, source_target_pairs={{0,96},{8,104},{16,112},{24,120},{32,64},{40,72},{48,80},{56,88},{... | collective-permute-start | bytes 98312 | tf_op jit(solution)/shard_map/sum_over_columns/ppermute | solution.py:29
  46.3 2.6 %collective-permute-start.16 = (f32[16,512]{1,0:T(8,128)S(1)}, f32[16,512]{1,0:T(8,128)S(1)}, u32[]{:S(2)}, u32[]{:S(2)}) collective-permute-start(f32[16,512]{1,0:T(8,128)S(1)} %get-tuple-element.99), channel_id=1, source_target_pairs={{0,120},{8,112},{16,104},{24,96},{32,88},{40,80},{48,72},{56,64},{... | collective-permute-start | bytes 98312 | tf_op jit(solution)/shard_map/sum_over_columns/ppermute | solution.py:29
  48.9 2.2 %collective-permute-done.15.refs_2_ = f32[16,512]{1,0:T(8,128)S(1)} collective-permute-done((f32[16,512]{1,0:T(8,128)S(1)}, f32[16,512]{1,0:T(8,128)S(1)}, u32[]{:S(2)}, u32[]{:S(2)}) %collective-permute-start.15) | collective-permute-done | bytes 32800 | tf_op jit(solution)/shard_map/sum_over_columns/ppermute | solution.py:29
  51.1 2.4 %collective-permute-done.16.refs_3_ = f32[16,512]{1,0:T(8,128)S(1)} collective-permute-done((f32[16,512]{1,0:T(8,128)S(1)}, f32[16,512]{1,0:T(8,128)S(1)}, u32[]{:S(2)}, u32[]{:S(2)}) %collective-permute-start.16) | collective-permute-done | bytes 32800 | tf_op jit(solution)/shard_map/sum_over_columns/ppermute | solution.py:29
  53.8 11.7 %all_to_all.8 = f32[32,1,128]{2,1,0:T(1,128)S(1)} all-to-all(f32[32,1,128]{2,1,0:T(1,128)S(1)} %broadcast_in_dim.2), channel_id=1, replica_groups=mesh['y'=4,'z'=4,'c'=2,'x'=4] {'y','z','c'}, dimensions={0} | all-to-all | bytes 32768 | tf_op jit(solution)/shard_map/final_sums/all_to_all | solution.py:374
  65.5 1.0 %finish.1 = (f32[16,512]{1,0:T(8,128)}, f32[16,512]{1,0:T(8,128)}) custom-call(f32[16,512]{1,0:T(8,128)S(1)} %bitcast.12, f32[16,512]{1,0:T(8,128)S(1)} %get-tuple-element.83.rho_ref, f32[16,512]{1,0:T(8,128)S(1)} %get-tuple-element.100.image_ref, f32[32,128]{1,0:T(8,128)S(1)} %bitcast.13), custom_call_target="tpu_custom_call" | custom-call | tf_op jit(solution)/shard_map/finish/pallas_call | solution.py:305
  (29 shorter events, 1.7 us)
Async XLA Ops:
  0.6 1.5 %copy-start = (bf16[1024,256]{1,0:T(8,128)(2,1)S(1)}, bf16[1024,256]{1,0:T(8,128)(2,1)}, u32[]{:S(2)}) copy-start(bf16[1024,256]{1,0:T(8,128)(2,1)} %param.3) | copy-start | bytes 1572868
  2.5 8.1 %collective-permute-start.2 = (bf16[576,256]{1,0:T(8,128)(2,1)S(1)}, bf16[576,256]{1,0:T(8,128)(2,1)S(1)}, u32[]{:S(2)}, u32[]{:S(2)}) collective-permute-start(bf16[576,256]{1,0:T(8,128)(2,1)S(1)} %pack.1.refs_1_.refs_2_), channel_id=1, source_target_pairs={{0,4},{4,0},{1,5},{5,1},{2,6},{6,2},{3,7},{7,3},{8,12},{12,8},{9,1... | collective-permute-start | bytes 884744 | tf_op jit(solution)/shard_map/fetch_points/ppermute | solution.py:38
  2.6 14.8 %collective-permute-start.5 = (bf16[576,256]{1,0:T(8,128)(2,1)S(1)}, bf16[576,256]{1,0:T(8,128)(2,1)S(1)}, u32[]{:S(2)}, u32[]{:S(2)}) collective-permute-start(bf16[576,256]{1,0:T(8,128)(2,1)S(1)} %pack.1.refs_1_.refs_2_), channel_id=1, source_target_pairs={{0,24},{8,16},{16,8},{24,0},{32,56},{40,48},{48,40},{56,32},{64,88... | collective-permute-start | bytes 884744 | tf_op jit(solution)/shard_map/fetch_points/ppermute | solution.py:29
  6.8 8.4 %collective-permute-start.1 = (bf16[512,256]{1,0:T(8,128)(2,1)S(1)}, bf16[512,256]{1,0:T(8,128)(2,1)S(1)}, u32[]{:S(2)}, u32[]{:S(2)}) collective-permute-start(bf16[512,256]{1,0:T(8,128)(2,1)S(1)} %constant_dynamic-slice_fusion.points_ref.refs_0_), channel_id=1, source_target_pairs={{0,8},{8,0},{16,24},{24,16},{32,40},{40,32},{48,56},{56,48},{64,72... | collective-permute-start | bytes 786440 | tf_op jit(solution)/shard_map/fetch_points/ppermute | solution.py:29
  6.8 9.2 %collective-permute-start = (bf16[512,256]{1,0:T(8,128)(2,1)S(1)}, bf16[512,256]{1,0:T(8,128)(2,1)S(1)}, u32[]{:S(2)}, u32[]{:S(2)}) collective-permute-start(bf16[512,256]{1,0:T(8,128)(2,1)S(1)} %constant_dynamic-slice_fusion.points_ref.refs_0_), channel_id=1, source_target_pairs={{0,32},{8,40},{16,48},{24,56},{32,0},{40,8},{48,16},{56,24},{64,96... | collective-permute-start | bytes 786440 | tf_op jit(solution)/shard_map/fetch_points/ppermute | solution.py:29
  8.3 13.2 %collective-permute-start.4 = (bf16[576,256]{1,0:T(8,128)(2,1)S(1)}, bf16[576,256]{1,0:T(8,128)(2,1)S(1)}, u32[]{:S(2)}, u32[]{:S(2)}) collective-permute-start(bf16[576,256]{1,0:T(8,128)(2,1)S(1)} %pack.1.refs_1_.refs_2_), channel_id=1, source_target_pairs={{0,96},{8,104},{16,112},{24,120},{32,64},{40,72},{48,80},{56,88},{... | collective-permute-start | bytes 884744 | tf_op jit(solution)/shard_map/fetch_points/ppermute | solution.py:29
  10.5 14.5 %collective-permute-start.3 = (bf16[512,256]{1,0:T(8,128)(2,1)S(1)}, bf16[512,256]{1,0:T(8,128)(2,1)S(1)}, u32[]{:S(2)}, u32[]{:S(2)}) collective-permute-start(bf16[512,256]{1,0:T(8,128)(2,1)S(1)} %constant_dynamic-slice_fusion.points_ref.refs_0_), channel_id=1, source_target_pairs={{0,40},{8,32},{16,56},{24,48},{32,8},{40,0},{48,24},{56,16},{64,10... | collective-permute-start | bytes 786440 | tf_op jit(solution)/shard_map/fetch_points/ppermute | solution.py:29
  12.7 0.8 %copy-start.1 = (f32[512,16]{0,1:T(8,128)S(1)}, f32[512,16]{0,1:T(8,128)}, u32[]{:S(2)}) copy-start(f32[512,16]{0,1:T(8,128)} %param.5) | copy-start | bytes 98308
  17.4 5.4 %collective-permute-start.7 = (bf16[576,256]{1,0:T(8,128)(2,1)S(1)}, bf16[576,256]{1,0:T(8,128)(2,1)S(1)}, u32[]{:S(2)}, u32[]{:S(2)}) collective-permute-start(bf16[576,256]{1,0:T(8,128)(2,1)S(1)} %collective-permute-done.5.refs_3_.refs_4_), channel_id=1, source_target_pairs={{0,4},{4,0},{1,5},{5,1},{2,6},{6,2},{3,7},{7,3},{8,12},{12,8},{9,1... | collective-permute-start | bytes 884744 | tf_op jit(solution)/shard_map/build_tiles/ppermute | solution.py:38
  17.4 12.7 %collective-permute-start.8 = (bf16[576,256]{1,0:T(8,128)(2,1)S(1)}, bf16[576,256]{1,0:T(8,128)(2,1)S(1)}, u32[]{:S(2)}, u32[]{:S(2)}) collective-permute-start(bf16[576,256]{1,0:T(8,128)(2,1)S(1)} %pack.1.refs_1_.refs_2_), channel_id=1, source_target_pairs={{0,120},{8,112},{16,104},{24,96},{32,88},{40,80},{48,72},{56,64},{... | collective-permute-start | bytes 884744 | tf_op jit(solution)/shard_map/fetch_points/ppermute | solution.py:29
  21.5 2.4 %collective-permute-start.6 = (bf16[576,256]{1,0:T(8,128)(2,1)S(1)}, bf16[576,256]{1,0:T(8,128)(2,1)S(1)}, u32[]{:S(2)}, u32[]{:S(2)}) collective-permute-start(bf16[576,256]{1,0:T(8,128)(2,1)S(1)} %collective-permute-done.4.refs_3_), channel_id=1, source_target_pairs={{0,4},{4,0},{1,5},{5,1},{2,6},{6,2},{3,7},{7,3},{8,12},{12,8},{9,1... | collective-permute-start | bytes 884744 | tf_op jit(solution)/shard_map/build_tiles/ppermute | solution.py:38
  30.1 1.6 %collective-permute-start.9 = (bf16[576,256]{1,0:T(8,128)(2,1)S(1)}, bf16[576,256]{1,0:T(8,128)(2,1)S(1)}, u32[]{:S(2)}, u32[]{:S(2)}) collective-permute-start(bf16[576,256]{1,0:T(8,128)(2,1)S(1)} %collective-permute-done.8.refs_4_), channel_id=1, source_target_pairs={{0,4},{4,0},{1,5},{5,1},{2,6},{6,2},{3,7},{7,3},{8,12},{12,8},{9,1... | collective-permute-start | bytes 884744 | tf_op jit(solution)/shard_map/build_tiles/ppermute | solution.py:38
  33.1 5.3 %collective-permute-start.10 = (bf16[80,512]{1,0:T(8,128)(2,1)S(1)}, bf16[80,512]{1,0:T(8,128)(2,1)S(1)}, u32[]{:S(2)}, u32[]{:S(2)}) collective-permute-start(bf16[80,512]{1,0:T(8,128)(2,1)S(1)} %get-tuple-element.80), channel_id=1, source_target_pairs={{0,32},{8,40},{16,48},{24,56},{32,0},{40,8},{48,16},{56,24},{64,96... | collective-permute-start | bytes 245768 | tf_op jit(solution)/shard_map/sum_over_rows/ppermute | solution.py:29
  33.6 4.8 %collective-permute-start.11 = (bf16[80,512]{1,0:T(8,128)(2,1)S(1)}, bf16[80,512]{1,0:T(8,128)(2,1)S(1)}, u32[]{:S(2)}, u32[]{:S(2)}) collective-permute-start(bf16[80,512]{1,0:T(8,128)(2,1)S(1)} %get-tuple-element.81), channel_id=1, source_target_pairs={{0,8},{8,0},{16,24},{24,16},{32,40},{40,32},{48,56},{56,48},{64,72... | collective-permute-start | bytes 245768 | tf_op jit(solution)/shard_map/sum_over_rows/ppermute | solution.py:29
  34.4 5.5 %collective-permute-start.12 = (bf16[80,512]{1,0:T(8,128)(2,1)S(1)}, bf16[80,512]{1,0:T(8,128)(2,1)S(1)}, u32[]{:S(2)}, u32[]{:S(2)}) collective-permute-start(bf16[80,512]{1,0:T(8,128)(2,1)S(1)} %get-tuple-element.82), channel_id=1, source_target_pairs={{0,40},{8,32},{16,56},{24,48},{32,8},{40,0},{48,24},{56,16},{64,10... | collective-permute-start | bytes 245768 | tf_op jit(solution)/shard_map/sum_over_rows/ppermute | solution.py:29
  41.4 24.1 %copy-start.2 = (f32[512,16]{0,1:T(8,128)S(1)}, f32[512,16]{0,1:T(8,128)}, u32[]{:S(2)}) copy-start(f32[512,16]{0,1:T(8,128)} %param.5) | copy-start | bytes 98308
  41.4 1.5 %collective-permute-start.13 = (f32[16,2048]{1,0:T(8,128)S(1)}, f32[16,2048]{1,0:T(8,128)S(1)}, u32[]{:S(2)}, u32[]{:S(2)}) collective-permute-start(f32[16,2048]{1,0:T(8,128)S(1)} %second_product.2), channel_id=1, source_target_pairs={{0,4},{4,0},{1,5},{5,1},{2,6},{6,2},{3,7},{7,3},{8,12},{12,8},{9,1... | collective-permute-start | bytes 393224 | tf_op jit(solution)/shard_map/sum_over_columns/ppermute | solution.py:38
  42.9 6.0 %collective-permute-start.14 = (f32[16,512]{1,0:T(8,128)S(1)}, f32[16,512]{1,0:T(8,128)S(1)}, u32[]{:S(2)}, u32[]{:S(2)}) collective-permute-start(f32[16,512]{1,0:T(8,128)S(1)} %get-tuple-element.97), channel_id=1, source_target_pairs={{0,96},{8,104},{16,112},{24,120},{32,64},{40,72},{48,80},{56,88},{... | collective-permute-start | bytes 98312 | tf_op jit(solution)/shard_map/sum_over_columns/ppermute | solution.py:29
  46.0 5.1 %collective-permute-start.15 = (f32[16,512]{1,0:T(8,128)S(1)}, f32[16,512]{1,0:T(8,128)S(1)}, u32[]{:S(2)}, u32[]{:S(2)}) collective-permute-start(f32[16,512]{1,0:T(8,128)S(1)} %get-tuple-element.98), channel_id=1, source_target_pairs={{0,24},{8,16},{16,8},{24,0},{32,56},{40,48},{48,40},{56,32},{64,88... | collective-permute-start | bytes 98312 | tf_op jit(solution)/shard_map/sum_over_columns/ppermute | solution.py:29
  46.3 7.2 %collective-permute-start.16 = (f32[16,512]{1,0:T(8,128)S(1)}, f32[16,512]{1,0:T(8,128)S(1)}, u32[]{:S(2)}, u32[]{:S(2)}) collective-permute-start(f32[16,512]{1,0:T(8,128)S(1)} %get-tuple-element.99), channel_id=1, source_target_pairs={{0,120},{8,112},{16,104},{24,96},{32,88},{40,80},{48,72},{56,64},{... | collective-permute-start | bytes 98312 | tf_op jit(solution)/shard_map/sum_over_columns/ppermute | solution.py:29

commit v20 on v19

--- a/solution.py
+++ b/solution.py
@@ -316,15 +316,14 @@
     points = lax.dynamic_slice_in_dim(states, offsets[0], own, 0)
     with jax.named_scope("fetch_points"):
         message = pack(points, side.astype(jnp.bfloat16))
-        rows = [points] + [swap(points, offset) for offset in ROWS[1:]]
-        cols = [message] + [swap(message, offset) for offset in SQUARE[1:3]]
+        rows = [points] + [swap(points, offset) for offset in ROWS[1:3]]
+        cols = [message] + [swap(message, offset) for offset in SQUARE[1:]]
         first = [message, swap_core(message)]
         tile_a, image_a, half_a = build([points], first, own, probes, side=side, weight=1)
-        (rows[1], rows[2]), image_a = lax.optimization_barrier(((rows[1], rows[2]), image_a))
+        (rows[1], rows[2], again), image_a = lax.optimization_barrier(((rows[1], rows[2], points), image_a))
+        rows.append(swap(again, ROWS[3]))
         tile_b, image_b, half_b = build(rows[1:3], first, own, probes, weight=1)
         half = [half_a, half_b]
-        again, image_b = lax.optimization_barrier((message, image_b))
-        cols.append(swap(again, SQUARE[3]))
 
     with jax.named_scope("build_tiles"):
         cols[2], image_b = lax.optimization_barrier((cols[2], image_b))

time: 67.6 us -> 64.5 us (0.954)
  waiting for transfers between devices: 12.8 us -> 10.3 us
  starting transfers between devices: 23.1 us -> 22.2 us
    ppermute x12, waiting for transfers between devices: 12.6 us -> 10.1 us  [swap(): return lax.ppermute(value, ('y', 'z'), pairs)]
    ppermute x12, starting transfers between devices: 22.7 us -> 21.3 us  [swap(): return lax.ppermute(value, ('y', 'z'), pairs)]
  transfers between devices with their start and end apart: 17 -> 17, of which waited for: 8 -> 7; matrix products, arithmetic and copies ran while one was open for 0% -> 0% of each run, Pallas kernels for 17% -> 18%
where the time goes in v20:
time: 64.5 us; the launch traced here: 63.5 us
  starting transfers between devices  22.2 us (34%)
  Pallas kernels  15.9 us (25%)
  blocking collectives  12.1 us (19%)
  waiting for transfers between devices  10.3 us (16%)
  between operations  1.42 us (2%)
  local copies, waits for them, and re-layouts  0.85 us (1%)
  other arithmetic  0.76 us (1%)
    ppermute x12, starting transfers between devices, swap(): return lax.ppermute(value, ('y', 'z'), pairs)  21.3 us
    all_to_all x1, blocking collectives, on_device(): sums = lax.all_to_all(sums, ('y', 'z', 'c'), 0, 0, tiled=True)  12.1 us
    pallas_call x9, Pallas kernels, build(): pl.pallas_call(functools.partial(tile_kernel, counts, probes), out_shape=...  11.3 us
    ppermute x12, waiting for transfers between devices, swap(): return lax.ppermute(value, ('y', 'z'), pairs)  10.1 us
    pallas_call x2, Pallas kernels, second_product(): pl.pallas_call(functools.partial(second_kernel, own, half, places), in_sp...  2.87 us
  transfers between devices with their start and end apart: 17, of which 7 were waited for; matrix products, arithmetic and copies ran while one was open for 0% of the time, Pallas kernels for 18%

profile of v20, /device:TPU:0, one launch (start us, length us, event | category | flops | bytes accessed | tf_op | source)
XLA Modules:
  0.0 63.5 jit_solution(17007608658631452405)
XLA Ops:
  1.3 0.8 %bitcast_convert_fusion.side_ref = bf16[16,512]{1,0:T(8,128)(2,1)S(1)} fusion(f32[512,16]{0,1:T(8,128)} %param.5), kind=kLoop, calls=%fused_computation.1 | loop fusion | flops 8192 | bytes 49152 | tf_op jit(solution)/shard_map/fetch_points/convert_element_type | solution.py:318
  2.6 4.2 %collective-permute-start.5 = (bf16[576,256]{1,0:T(8,128)(2,1)S(1)}, bf16[576,256]{1,0:T(8,128)(2,1)S(1)}, u32[]{:S(2)}, u32[]{:S(2)}) collective-permute-start(bf16[576,256]{1,0:T(8,128)(2,1)S(1)} %pack.1.refs_1_.refs_2_), channel_id=1, source_target_pairs={{0,24},{8,16},{16,8},{24,0},{32,56},{40,48},{48,40},{56,32},{64,88... | collective-permute-start | bytes 884744 | tf_op jit(solution)/shard_map/fetch_points/ppermute | solution.py:29
  6.8 1.6 %collective-permute-start = (bf16[512,256]{1,0:T(8,128)(2,1)S(1)}, bf16[512,256]{1,0:T(8,128)(2,1)S(1)}, u32[]{:S(2)}, u32[]{:S(2)}) collective-permute-start(bf16[512,256]{1,0:T(8,128)(2,1)S(1)} %constant_dynamic-slice_fusion.points_ref.refs_0_), channel_id=1, source_target_pairs={{0,32},{8,40},{16,48},{24,56},{32,0},{40,8},{48,16},{56,24},{64,96... | collective-permute-start | bytes 786440 | tf_op jit(solution)/shard_map/fetch_points/ppermute | solution.py:29
  8.3 2.2 %collective-permute-start.4 = (bf16[576,256]{1,0:T(8,128)(2,1)S(1)}, bf16[576,256]{1,0:T(8,128)(2,1)S(1)}, u32[]{:S(2)}, u32[]{:S(2)}) collective-permute-start(bf16[576,256]{1,0:T(8,128)(2,1)S(1)} %pack.1.refs_1_.refs_2_), channel_id=1, source_target_pairs={{0,96},{8,104},{16,112},{24,120},{32,64},{40,72},{48,80},{56,88},{... | collective-permute-start | bytes 884744 | tf_op jit(solution)/shard_map/fetch_points/ppermute | solution.py:29
  10.5 1.0 %collective-permute-start.8 = (bf16[576,256]{1,0:T(8,128)(2,1)S(1)}, bf16[576,256]{1,0:T(8,128)(2,1)S(1)}, u32[]{:S(2)}, u32[]{:S(2)}) collective-permute-start(bf16[576,256]{1,0:T(8,128)(2,1)S(1)} %pack.1.refs_1_.refs_2_), channel_id=1, source_target_pairs={{0,120},{8,112},{16,104},{24,96},{32,88},{40,80},{48,72},{56,64},{... | collective-permute-start | bytes 884744 | tf_op jit(solution)/shard_map/fetch_points/ppermute | solution.py:29
  11.5 0.8 %copy-done.1 = f32[512,16]{0,1:T(8,128)S(1)} copy-done((f32[512,16]{0,1:T(8,128)S(1)}, f32[512,16]{0,1:T(8,128)}, u32[]{:S(2)}) %copy-start.1) | copy-done | bytes 32792
  12.3 0.8 %build_tile.9 = (bf16[512,1024]{1,0:T(8,128)(2,1)S(1)}, f32[16,512]{1,0:T(8,128)S(1)}, f32[512,1]{1,0:T(8,128)S(1)}) custom-call(bf16[512,256]{1,0:T(8,128)(2,1)S(1)} %constant_dynamic-slice_fusion.points_ref.refs_0_, bf16[576,256]{1,0:T(8,128)(2,1)S(1)} %pack.1.refs_1_.refs_2_, bf16[576,256]{1,0:T(8,128)(2,1)S(1)} %collective-permute-done.2.refs_2_.refs_3_, ...), custom_call_target="tpu_custom_call" | custom-call | flops 16777216 | bytes 1024 | tf_op jit(solution)/shard_map/fetch_points/build_tile/pallas_call | solution.py:145
  13.1 2.0 %collective-permute-done.1.refs_1_.refs_2_ = bf16[512,256]{1,0:T(8,128)(2,1)S(1)} collective-permute-done((bf16[512,256]{1,0:T(8,128)(2,1)S(1)}, bf16[512,256]{1,0:T(8,128)(2,1)S(1)}, u32[]{:S(2)}, u32[]{:S(2)}) %collective-permute-start.1) | collective-permute-done | bytes 262176 | tf_op jit(solution)/shard_map/fetch_points/ppermute | solution.py:29
  15.1 2.8 %collective-permute-start.3 = (bf16[512,256]{1,0:T(8,128)(2,1)S(1)}, bf16[512,256]{1,0:T(8,128)(2,1)S(1)}, u32[]{:S(2)}, u32[]{:S(2)}) collective-permute-start(bf16[512,256]{1,0:T(8,128)(2,1)S(1)} %constant_dynamic-slice_fusion.points_ref.refs_0_), channel_id=1, source_target_pairs={{0,40},{8,32},{16,56},{24,48},{32,8},{40,0},{48,24},{56,16},{64,10... | collective-permute-start | bytes 786440 | tf_op jit(solution)/shard_map/fetch_points/ppermute | solution.py:29
  17.9 1.4 %build_tile.10 = (bf16[1024,1024]{1,0:T(8,128)(2,1)S(1)}, f32[16,1024]{1,0:T(8,128)S(1)}, f32[1024,1]{1,0:T(8,128)S(1)}) custom-call(bf16[512,256]{1,0:T(8,128)(2,1)S(1)} %collective-permute-done.refs_0_.refs_1_, bf16[512,256]{1,0:T(8,128)(2,1)S(1)} %collective-permute-done.1.refs_1_.refs_2_, bf16[576,256]{1,0:T(8,128)(2,1)S(1)} %pack.1.refs_1_.refs_2_, ...), custom_call_target="tpu_custom_call" | custom-call | flops 33554432 | bytes 1024 | tf_op jit(solution)/shard_map/fetch_points/build_tile/pallas_call | solution.py:145
  19.4 1.1 %build_tile.11 = (bf16[1536,512]{1,0:T(8,128)(2,1)S(1)}, f32[16,1536]{1,0:T(8,128)S(1)}) custom-call(bf16[512,256]{1,0:T(8,128)(2,1)S(1)} %constant_dynamic-slice_fusion.points_ref.refs_0_, bf16[512,256]{1,0:T(8,128)(2,1)S(1)} %collective-permute-done.refs_0_.refs_1_, bf16[512,256]{1,0:T(8,128)(2,1)S(1)} %collective-permute-done.1.refs_1_.refs_2_, ...), custom_call_target="tpu_custom_call" | custom-call | flops 1610612736 | bytes 1024 | tf_op jit(solution)/shard_map/build_tiles/build_tile/pallas_call | solution.py:145
  20.4 0.6 collective-permute-start.6
  21.0 1.1 %build_tile.12 = (bf16[1536,512]{1,0:T(8,128)(2,1)S(1)}, f32[16,1536]{1,0:T(8,128)S(1)}) custom-call(bf16[512,256]{1,0:T(8,128)(2,1)S(1)} %constant_dynamic-slice_fusion.points_ref.refs_0_, bf16[512,256]{1,0:T(8,128)(2,1)S(1)} %collective-permute-done.refs_0_.refs_1_, bf16[512,256]{1,0:T(8,128)(2,1)S(1)} %collective-permute-done.1.refs_1_.refs_2_, ...), custom_call_target="tpu_custom_call" | custom-call | flops 1610612736 | bytes 1024 | tf_op jit(solution)/shard_map/build_tiles/build_tile/pallas_call | solution.py:145
  22.1 1.1 %build_tile.13 = (bf16[1536,512]{1,0:T(8,128)(2,1)S(1)}, f32[16,1536]{1,0:T(8,128)S(1)}) custom-call(bf16[512,256]{1,0:T(8,128)(2,1)S(1)} %constant_dynamic-slice_fusion.points_ref.refs_0_, bf16[512,256]{1,0:T(8,128)(2,1)S(1)} %collective-permute-done.refs_0_.refs_1_, bf16[512,256]{1,0:T(8,128)(2,1)S(1)} %collective-permute-done.1.refs_1_.refs_2_, ...), custom_call_target="tpu_custom_call" | custom-call | flops 1610612736 | bytes 1024 | tf_op jit(solution)/shard_map/build_tiles/build_tile/pallas_call | solution.py:145
  23.2 1.1 %build_tile.14 = (bf16[1536,512]{1,0:T(8,128)(2,1)S(1)}, f32[16,1536]{1,0:T(8,128)S(1)}) custom-call(bf16[512,256]{1,0:T(8,128)(2,1)S(1)} %constant_dynamic-slice_fusion.points_ref.refs_0_, bf16[512,256]{1,0:T(8,128)(2,1)S(1)} %collective-permute-done.refs_0_.refs_1_, bf16[512,256]{1,0:T(8,128)(2,1)S(1)} %collective-permute-done.1.refs_1_.refs_2_, ...), custom_call_target="tpu_custom_call" | custom-call | flops 1610612736 | bytes 1024 | tf_op jit(solution)/shard_map/build_tiles/build_tile/pallas_call | solution.py:145
  24.3 2.1 %build_tile.15 = (bf16[512,3072]{1,0:T(8,128)(2,1)S(1)}, f32[16,512]{1,0:T(8,128)S(1)}, f32[512,1]{1,0:T(8,128)S(1)}) custom-call(bf16[512,256]{1,0:T(8,128)(2,1)S(1)} %collective-permute-done.3.refs_0_.refs_3_, bf16[576,256]{1,0:T(8,128)(2,1)S(1)} %pack.1.refs_1_.refs_2_, bf16[576,256]{1,0:T(8,128)(2,1)S(1)} %collective-permute-done.2.refs_2_.refs_3_, ...), custom_call_target="tpu_custom_call" | custom-call | flops 3221225472 | bytes 1024 | tf_op jit(solution)/shard_map/build_tiles/build_tile/pallas_call | solution.py:145
  26.6 1.3 %build_tile.16 = (bf16[2048,512]{1,0:T(8,128)(2,1)S(1)}, f32[16,2048]{1,0:T(8,128)S(1)}) custom-call(bf16[512,256]{1,0:T(8,128)(2,1)S(1)} %constant_dynamic-slice_fusion.points_ref.refs_0_, bf16[512,256]{1,0:T(8,128)(2,1)S(1)} %collective-permute-done.refs_0_.refs_1_, bf16[512,256]{1,0:T(8,128)(2,1)S(1)} %collective-permute-done.1.refs_1_.refs_2_, ...), custom_call_target="tpu_custom_call" | custom-call | flops 2147483648 | bytes 1024 | tf_op jit(solution)/shard_map/build_tiles/build_tile/pallas_call | solution.py:145
  28.2 1.3 %build_tile.17 = (bf16[2048,512]{1,0:T(8,128)(2,1)S(1)}, f32[16,2048]{1,0:T(8,128)S(1)}) custom-call(bf16[512,256]{1,0:T(8,128)(2,1)S(1)} %constant_dynamic-slice_fusion.points_ref.refs_0_, bf16[512,256]{1,0:T(8,128)(2,1)S(1)} %collective-permute-done.refs_0_.refs_1_, bf16[512,256]{1,0:T(8,128)(2,1)S(1)} %collective-permute-done.1.refs_1_.refs_2_, ...), custom_call_target="tpu_custom_call" | custom-call | flops 2147483648 | bytes 1024 | tf_op jit(solution)/shard_map/build_tiles/build_tile/pallas_call | solution.py:145
  29.6 0.9 %collective-permute-start.10 = (bf16[80,512]{1,0:T(8,128)(2,1)S(1)}, bf16[80,512]{1,0:T(8,128)(2,1)S(1)}, u32[]{:S(2)}, u32[]{:S(2)}) collective-permute-start(bf16[80,512]{1,0:T(8,128)(2,1)S(1)} %get-tuple-element.78), channel_id=1, source_target_pairs={{0,32},{8,40},{16,48},{24,56},{32,0},{40,8},{48,16},{56,24},{64,96... | collective-permute-start | bytes 245768 | tf_op jit(solution)/shard_map/sum_over_rows/ppermute | solution.py:29
  30.5 1.4 %collective-permute-start.11 = (bf16[80,512]{1,0:T(8,128)(2,1)S(1)}, bf16[80,512]{1,0:T(8,128)(2,1)S(1)}, u32[]{:S(2)}, u32[]{:S(2)}) collective-permute-start(bf16[80,512]{1,0:T(8,128)(2,1)S(1)} %get-tuple-element.79), channel_id=1, source_target_pairs={{0,8},{8,0},{16,24},{24,16},{32,40},{40,32},{48,56},{56,48},{64,72... | collective-permute-start | bytes 245768 | tf_op jit(solution)/shard_map/sum_over_rows/ppermute | solution.py:29
  31.9 1.2 %collective-permute-start.12 = (bf16[80,512]{1,0:T(8,128)(2,1)S(1)}, bf16[80,512]{1,0:T(8,128)(2,1)S(1)}, u32[]{:S(2)}, u32[]{:S(2)}) collective-permute-start(bf16[80,512]{1,0:T(8,128)(2,1)S(1)} %get-tuple-element.80), channel_id=1, source_target_pairs={{0,40},{8,32},{16,56},{24,48},{32,8},{40,0},{48,24},{56,16},{64,10... | collective-permute-start | bytes 245768 | tf_op jit(solution)/shard_map/sum_over_rows/ppermute | solution.py:29
  33.1 1.2 %collective-permute-done.10.refs_1_ = bf16[80,512]{1,0:T(8,128)(2,1)S(1)} collective-permute-done((bf16[80,512]{1,0:T(8,128)(2,1)S(1)}, bf16[80,512]{1,0:T(8,128)(2,1)S(1)}, u32[]{:S(2)}, u32[]{:S(2)}) %collective-permute-start.10) | collective-permute-done | bytes 81952 | tf_op jit(solution)/shard_map/sum_over_rows/ppermute | solution.py:29
  34.3 1.3 %collective-permute-done.11.refs_2_ = bf16[80,512]{1,0:T(8,128)(2,1)S(1)} collective-permute-done((bf16[80,512]{1,0:T(8,128)(2,1)S(1)}, bf16[80,512]{1,0:T(8,128)(2,1)S(1)}, u32[]{:S(2)}, u32[]{:S(2)}) %collective-permute-start.11) | collective-permute-done | bytes 81952 | tf_op jit(solution)/shard_map/sum_over_rows/ppermute | solution.py:29
  35.6 1.6 %collective-permute-done.12.refs_3_ = bf16[80,512]{1,0:T(8,128)(2,1)S(1)} collective-permute-done((bf16[80,512]{1,0:T(8,128)(2,1)S(1)}, bf16[80,512]{1,0:T(8,128)(2,1)S(1)}, u32[]{:S(2)}, u32[]{:S(2)}) %collective-permute-start.12) | collective-permute-done | bytes 81952 | tf_op jit(solution)/shard_map/sum_over_rows/ppermute | solution.py:29
  37.3 1.4 %second_product.2 = f32[16,2048]{1,0:T(8,128)S(1)} custom-call(bf16[32,2048]{1,0:T(8,128)(2,1)S(1)} %get-tuple-element.92.narrow_ref, bf16[512,1024]{1,0:T(8,128)(2,1)S(1)} %get-tuple-element.83.refs_0_, bf16[1024,1024]{1,0:T(8,128)(2,1)S(1)} %get-tuple-element.84.refs_1_, bf16[1536,512]{1,0:T(8,128)(2,1)S(1)} %get-tuple-element.85.refs_2_, ...), custom_call_target="tpu_custom_call" | custom-call | flops 134217728 | bytes 1024 | tf_op jit(solution)/shard_map/second_product/pallas_call | solution.py:231
  38.7 1.4 %second_product.3.mine_ref = f32[16,2048]{1,0:T(8,128)S(1)} custom-call(bf16[32,2048]{1,0:T(8,128)(2,1)S(1)} %get-tuple-element.92.narrow_ref, bf16[512,1024]{1,0:T(8,128)(2,1)S(1)} %get-tuple-element.83.refs_0_, bf16[1024,1024]{1,0:T(8,128)(2,1)S(1)} %get-tuple-element.84.refs_1_, bf16[1536,512]{1,0:T(8,128)(2,1)S(1)} %get-tuple-element.85.refs_2_, ...), custom_call_target="tpu_custom_call" | custom-call | flops 134217728 | bytes 1024 | tf_op jit(solution)/shard_map/second_product/pallas_call | solution.py:231
  40.2 2.3 %collective-permute-start.14 = (f32[16,512]{1,0:T(8,128)S(1)}, f32[16,512]{1,0:T(8,128)S(1)}, u32[]{:S(2)}, u32[]{:S(2)}) collective-permute-start(f32[16,512]{1,0:T(8,128)S(1)} %get-tuple-element.95), channel_id=1, source_target_pairs={{0,96},{8,104},{16,112},{24,120},{32,64},{40,72},{48,80},{56,88},{... | collective-permute-start | bytes 98312 | tf_op jit(solution)/shard_map/sum_over_columns/ppermute | solution.py:29
  42.9 3.3 %collective-permute-start.16 = (f32[16,512]{1,0:T(8,128)S(1)}, f32[16,512]{1,0:T(8,128)S(1)}, u32[]{:S(2)}, u32[]{:S(2)}) collective-permute-start(f32[16,512]{1,0:T(8,128)S(1)} %get-tuple-element.97), channel_id=1, source_target_pairs={{0,120},{8,112},{16,104},{24,96},{32,88},{40,80},{48,72},{56,64},{... | collective-permute-start | bytes 98312 | tf_op jit(solution)/shard_map/sum_over_columns/ppermute | solution.py:29
  46.2 1.4 %collective-permute-done.15.refs_2_ = f32[16,512]{1,0:T(8,128)S(1)} collective-permute-done((f32[16,512]{1,0:T(8,128)S(1)}, f32[16,512]{1,0:T(8,128)S(1)}, u32[]{:S(2)}, u32[]{:S(2)}) %collective-permute-start.15) | collective-permute-done | bytes 32800 | tf_op jit(solution)/shard_map/sum_over_columns/ppermute | solution.py:29
  47.6 2.6 %collective-permute-done.16.refs_3_ = f32[16,512]{1,0:T(8,128)S(1)} collective-permute-done((f32[16,512]{1,0:T(8,128)S(1)}, f32[16,512]{1,0:T(8,128)S(1)}, u32[]{:S(2)}, u32[]{:S(2)}) %collective-permute-start.16) | collective-permute-done | bytes 32800 | tf_op jit(solution)/shard_map/sum_over_columns/ppermute | solution.py:29
  50.4 12.1 %all_to_all.8 = f32[32,1,128]{2,1,0:T(1,128)S(1)} all-to-all(f32[32,1,128]{2,1,0:T(1,128)S(1)} %broadcast_in_dim.2), channel_id=1, replica_groups=mesh['y'=4,'z'=4,'c'=2,'x'=4] {'y','z','c'}, dimensions={0} | all-to-all | bytes 32768 | tf_op jit(solution)/shard_map/final_sums/all_to_all | solution.py:373
  62.5 1.0 %finish.1 = (f32[16,512]{1,0:T(8,128)}, f32[16,512]{1,0:T(8,128)}) custom-call(f32[16,512]{1,0:T(8,128)S(1)} %bitcast.12, f32[16,512]{1,0:T(8,128)S(1)} %get-tuple-element.81.rho_ref, f32[16,512]{1,0:T(8,128)S(1)} %get-tuple-element.98.image_ref, f32[32,128]{1,0:T(8,128)S(1)} %bitcast.13), custom_call_target="tpu_custom_call" | custom-call | tf_op jit(solution)/shard_map/finish/pallas_call | solution.py:305
  (29 shorter events, 1.8 us)
Async XLA Ops:
  0.6 1.5 %copy-start = (bf16[1024,256]{1,0:T(8,128)(2,1)S(1)}, bf16[1024,256]{1,0:T(8,128)(2,1)}, u32[]{:S(2)}) copy-start(bf16[1024,256]{1,0:T(8,128)(2,1)} %param.3) | copy-start | bytes 1572868
  2.5 8.1 %collective-permute-start.2 = (bf16[576,256]{1,0:T(8,128)(2,1)S(1)}, bf16[576,256]{1,0:T(8,128)(2,1)S(1)}, u32[]{:S(2)}, u32[]{:S(2)}) collective-permute-start(bf16[576,256]{1,0:T(8,128)(2,1)S(1)} %pack.1.refs_1_.refs_2_), channel_id=1, source_target_pairs={{0,4},{4,0},{1,5},{5,1},{2,6},{6,2},{3,7},{7,3},{8,12},{12,8},{9,1... | collective-permute-start | bytes 884744 | tf_op jit(solution)/shard_map/fetch_points/ppermute | solution.py:38
  2.6 16.8 %collective-permute-start.5 = (bf16[576,256]{1,0:T(8,128)(2,1)S(1)}, bf16[576,256]{1,0:T(8,128)(2,1)S(1)}, u32[]{:S(2)}, u32[]{:S(2)}) collective-permute-start(bf16[576,256]{1,0:T(8,128)(2,1)S(1)} %pack.1.refs_1_.refs_2_), channel_id=1, source_target_pairs={{0,24},{8,16},{16,8},{24,0},{32,56},{40,48},{48,40},{56,32},{64,88... | collective-permute-start | bytes 884744 | tf_op jit(solution)/shard_map/fetch_points/ppermute | solution.py:29
  6.8 8.4 %collective-permute-start.1 = (bf16[512,256]{1,0:T(8,128)(2,1)S(1)}, bf16[512,256]{1,0:T(8,128)(2,1)S(1)}, u32[]{:S(2)}, u32[]{:S(2)}) collective-permute-start(bf16[512,256]{1,0:T(8,128)(2,1)S(1)} %constant_dynamic-slice_fusion.points_ref.refs_0_), channel_id=1, source_target_pairs={{0,8},{8,0},{16,24},{24,16},{32,40},{40,32},{48,56},{56,48},{64,72... | collective-permute-start | bytes 786440 | tf_op jit(solution)/shard_map/fetch_points/ppermute | solution.py:29
  6.8 8.4 %collective-permute-start = (bf16[512,256]{1,0:T(8,128)(2,1)S(1)}, bf16[512,256]{1,0:T(8,128)(2,1)S(1)}, u32[]{:S(2)}, u32[]{:S(2)}) collective-permute-start(bf16[512,256]{1,0:T(8,128)(2,1)S(1)} %constant_dynamic-slice_fusion.points_ref.refs_0_), channel_id=1, source_target_pairs={{0,32},{8,40},{16,48},{24,56},{32,0},{40,8},{48,16},{56,24},{64,96... | collective-permute-start | bytes 786440 | tf_op jit(solution)/shard_map/fetch_points/ppermute | solution.py:29
  8.3 12.1 %collective-permute-start.4 = (bf16[576,256]{1,0:T(8,128)(2,1)S(1)}, bf16[576,256]{1,0:T(8,128)(2,1)S(1)}, u32[]{:S(2)}, u32[]{:S(2)}) collective-permute-start(bf16[576,256]{1,0:T(8,128)(2,1)S(1)} %pack.1.refs_1_.refs_2_), channel_id=1, source_target_pairs={{0,96},{8,104},{16,112},{24,120},{32,64},{40,72},{48,80},{56,88},{... | collective-permute-start | bytes 884744 | tf_op jit(solution)/shard_map/fetch_points/ppermute | solution.py:29
  10.5 15.8 %collective-permute-start.8 = (bf16[576,256]{1,0:T(8,128)(2,1)S(1)}, bf16[576,256]{1,0:T(8,128)(2,1)S(1)}, u32[]{:S(2)}, u32[]{:S(2)}) collective-permute-start(bf16[576,256]{1,0:T(8,128)(2,1)S(1)} %pack.1.refs_1_.refs_2_), channel_id=1, source_target_pairs={{0,120},{8,112},{16,104},{24,96},{32,88},{40,80},{48,72},{56,64},{... | collective-permute-start | bytes 884744 | tf_op jit(solution)/shard_map/fetch_points/ppermute | solution.py:29
  11.5 0.8 %copy-start.1 = (f32[512,16]{0,1:T(8,128)S(1)}, f32[512,16]{0,1:T(8,128)}, u32[]{:S(2)}) copy-start(f32[512,16]{0,1:T(8,128)} %param.5) | copy-start | bytes 98308
  15.1 9.1 %collective-permute-start.3 = (bf16[512,256]{1,0:T(8,128)(2,1)S(1)}, bf16[512,256]{1,0:T(8,128)(2,1)S(1)}, u32[]{:S(2)}, u32[]{:S(2)}) collective-permute-start(bf16[512,256]{1,0:T(8,128)(2,1)S(1)} %constant_dynamic-slice_fusion.points_ref.refs_0_), channel_id=1, source_target_pairs={{0,40},{8,32},{16,56},{24,48},{32,8},{40,0},{48,24},{56,16},{64,10... | collective-permute-start | bytes 786440 | tf_op jit(solution)/shard_map/fetch_points/ppermute | solution.py:29
  19.3 2.7 %collective-permute-start.7 = (bf16[576,256]{1,0:T(8,128)(2,1)S(1)}, bf16[576,256]{1,0:T(8,128)(2,1)S(1)}, u32[]{:S(2)}, u32[]{:S(2)}) collective-permute-start(bf16[576,256]{1,0:T(8,128)(2,1)S(1)} %collective-permute-done.5.refs_3_.refs_4_), channel_id=1, source_target_pairs={{0,4},{4,0},{1,5},{5,1},{2,6},{6,2},{3,7},{7,3},{8,12},{12,8},{9,1... | collective-permute-start | bytes 884744 | tf_op jit(solution)/shard_map/build_tiles/ppermute | solution.py:38
  20.4 2.7 %collective-permute-start.6 = (bf16[576,256]{1,0:T(8,128)(2,1)S(1)}, bf16[576,256]{1,0:T(8,128)(2,1)S(1)}, u32[]{:S(2)}, u32[]{:S(2)}) collective-permute-start(bf16[576,256]{1,0:T(8,128)(2,1)S(1)} %collective-permute-done.4.refs_3_), channel_id=1, source_target_pairs={{0,4},{4,0},{1,5},{5,1},{2,6},{6,2},{3,7},{7,3},{8,12},{12,8},{9,1... | collective-permute-start | bytes 884744 | tf_op jit(solution)/shard_map/build_tiles/ppermute | solution.py:38
  26.4 1.8 %collective-permute-start.9 = (bf16[576,256]{1,0:T(8,128)(2,1)S(1)}, bf16[576,256]{1,0:T(8,128)(2,1)S(1)}, u32[]{:S(2)}, u32[]{:S(2)}) collective-permute-start(bf16[576,256]{1,0:T(8,128)(2,1)S(1)} %collective-permute-done.8.refs_4_), channel_id=1, source_target_pairs={{0,4},{4,0},{1,5},{5,1},{2,6},{6,2},{3,7},{7,3},{8,12},{12,8},{9,1... | collective-permute-start | bytes 884744 | tf_op jit(solution)/shard_map/build_tiles/ppermute | solution.py:38
  29.6 4.8 %collective-permute-start.10 = (bf16[80,512]{1,0:T(8,128)(2,1)S(1)}, bf16[80,512]{1,0:T(8,128)(2,1)S(1)}, u32[]{:S(2)}, u32[]{:S(2)}) collective-permute-start(bf16[80,512]{1,0:T(8,128)(2,1)S(1)} %get-tuple-element.78), channel_id=1, source_target_pairs={{0,32},{8,40},{16,48},{24,56},{32,0},{40,8},{48,16},{56,24},{64,96... | collective-permute-start | bytes 245768 | tf_op jit(solution)/shard_map/sum_over_rows/ppermute | solution.py:29
  30.5 5.2 %collective-permute-start.11 = (bf16[80,512]{1,0:T(8,128)(2,1)S(1)}, bf16[80,512]{1,0:T(8,128)(2,1)S(1)}, u32[]{:S(2)}, u32[]{:S(2)}) collective-permute-start(bf16[80,512]{1,0:T(8,128)(2,1)S(1)} %get-tuple-element.79), channel_id=1, source_target_pairs={{0,8},{8,0},{16,24},{24,16},{32,40},{40,32},{48,56},{56,48},{64,72... | collective-permute-start | bytes 245768 | tf_op jit(solution)/shard_map/sum_over_rows/ppermute | solution.py:29
  31.9 5.3 %collective-permute-start.12 = (bf16[80,512]{1,0:T(8,128)(2,1)S(1)}, bf16[80,512]{1,0:T(8,128)(2,1)S(1)}, u32[]{:S(2)}, u32[]{:S(2)}) collective-permute-start(bf16[80,512]{1,0:T(8,128)(2,1)S(1)} %get-tuple-element.80), channel_id=1, source_target_pairs={{0,40},{8,32},{16,56},{24,48},{32,8},{40,0},{48,24},{56,16},{64,10... | collective-permute-start | bytes 245768 | tf_op jit(solution)/shard_map/sum_over_rows/ppermute | solution.py:29
  38.7 23.8 %copy-start.2 = (f32[512,16]{0,1:T(8,128)S(1)}, f32[512,16]{0,1:T(8,128)}, u32[]{:S(2)}) copy-start(f32[512,16]{0,1:T(8,128)} %param.5) | copy-start | bytes 98308
  38.7 1.5 %collective-permute-start.13 = (f32[16,2048]{1,0:T(8,128)S(1)}, f32[16,2048]{1,0:T(8,128)S(1)}, u32[]{:S(2)}, u32[]{:S(2)}) collective-permute-start(f32[16,2048]{1,0:T(8,128)S(1)} %second_product.2), channel_id=1, source_target_pairs={{0,4},{4,0},{1,5},{5,1},{2,6},{6,2},{3,7},{7,3},{8,12},{12,8},{9,1... | collective-permute-start | bytes 393224 | tf_op jit(solution)/shard_map/sum_over_columns/ppermute | solution.py:38
  40.2 6.0 %collective-permute-start.14 = (f32[16,512]{1,0:T(8,128)S(1)}, f32[16,512]{1,0:T(8,128)S(1)}, u32[]{:S(2)}, u32[]{:S(2)}) collective-permute-start(f32[16,512]{1,0:T(8,128)S(1)} %get-tuple-element.95), channel_id=1, source_target_pairs={{0,96},{8,104},{16,112},{24,120},{32,64},{40,72},{48,80},{56,88},{... | collective-permute-start | bytes 98312 | tf_op jit(solution)/shard_map/sum_over_columns/ppermute | solution.py:29
  42.5 5.1 %collective-permute-start.15 = (f32[16,512]{1,0:T(8,128)S(1)}, f32[16,512]{1,0:T(8,128)S(1)}, u32[]{:S(2)}, u32[]{:S(2)}) collective-permute-start(f32[16,512]{1,0:T(8,128)S(1)} %get-tuple-element.96), channel_id=1, source_target_pairs={{0,24},{8,16},{16,8},{24,0},{32,56},{40,48},{48,40},{56,32},{64,88... | collective-permute-start | bytes 98312 | tf_op jit(solution)/shard_map/sum_over_columns/ppermute | solution.py:29
  42.9 7.2 %collective-permute-start.16 = (f32[16,512]{1,0:T(8,128)S(1)}, f32[16,512]{1,0:T(8,128)S(1)}, u32[]{:S(2)}, u32[]{:S(2)}) collective-permute-start(f32[16,512]{1,0:T(8,128)S(1)} %get-tuple-element.97), channel_id=1, source_target_pairs={{0,120},{8,112},{16,104},{24,96},{32,88},{40,80},{48,72},{56,64},{... | collective-permute-start | bytes 98312 | tf_op jit(solution)/shard_map/sum_over_columns/ppermute | solution.py:29

commit v21 on v20

--- a/solution.py
+++ b/solution.py
@@ -320,10 +320,11 @@
         cols = [message] + [swap(message, offset) for offset in SQUARE[1:]]
         first = [message, swap_core(message)]
         tile_a, image_a, half_a = build([points], first, own, probes, side=side, weight=1)
-        (rows[1], rows[2], again), image_a = lax.optimization_barrier(((rows[1], rows[2], points), image_a))
-        rows.append(swap(again, ROWS[3]))
+        (rows[1], rows[2]), image_a = lax.optimization_barrier(((rows[1], rows[2]), image_a))
         tile_b, image_b, half_b = build(rows[1:3], first, own, probes, weight=1)
         half = [half_a, half_b]
+        again, image_b = lax.optimization_barrier((points, image_b))
+        rows.append(swap(again, ROWS[3]))
 
     with jax.named_scope("build_tiles"):
         cols[2], image_b = lax.optimization_barrier((cols[2], image_b))

time: 64.5 us -> 66 us (1.023)
  waiting for transfers between devices: 10.3 us -> 11.8 us
    ppermute x12, waiting for transfers between devices: 10.1 us -> 11.6 us  [swap(): return lax.ppermute(value, ('y', 'z'), pairs)]
  transfers between devices with their start and end apart: 17 -> 17, of which waited for: 7 -> 8; matrix products, arithmetic and copies ran while one was open for 0% -> 0% of each run, Pallas kernels for 18% -> 18%
where the time goes in v21:
time: 66 us; the launch traced here: 65 us
  starting transfers between devices  22.2 us (34%)
  Pallas kernels  15.8 us (24%)
  blocking collectives  12.1 us (18%)
  waiting for transfers between devices  11.8 us (18%)
  between operations  1.42 us (2%)
  local copies, waits for them, and re-layouts  0.85 us (1%)
  other arithmetic  0.76 us (1%)
    ppermute x12, starting transfers between devices, swap(): return lax.ppermute(value, ('y', 'z'), pairs)  21.3 us
    all_to_all x1, blocking collectives, on_device(): sums = lax.all_to_all(sums, ('y', 'z', 'c'), 0, 0, tiled=True)  12.1 us
    ppermute x12, waiting for transfers between devices, swap(): return lax.ppermute(value, ('y', 'z'), pairs)  11.6 us
    pallas_call x9, Pallas kernels, build(): pl.pallas_call(functools.partial(tile_kernel, counts, probes), out_shape=...  11.3 us
    pallas_call x2, Pallas kernels, second_product(): pl.pallas_call(functools.partial(second_kernel, own, half, places), in_sp...  2.87 us
  transfers between devices with their start and end apart: 17, of which 8 were waited for; matrix products, arithmetic and copies ran while one was open for 0% of the time, Pallas kernels for 18%

profile of v21, /device:TPU:0, one launch (start us, length us, event | category | flops | bytes accessed | tf_op | source)
XLA Modules:
  0.0 65.0 jit_solution(1994428806368223148)
XLA Ops:
  1.3 0.8 %bitcast_convert_fusion.side_ref = bf16[16,512]{1,0:T(8,128)(2,1)S(1)} fusion(f32[512,16]{0,1:T(8,128)} %param.5), kind=kLoop, calls=%fused_computation.1 | loop fusion | flops 8192 | bytes 49152 | tf_op jit(solution)/shard_map/fetch_points/convert_element_type | solution.py:318
  2.6 4.2 %collective-permute-start.5 = (bf16[576,256]{1,0:T(8,128)(2,1)S(1)}, bf16[576,256]{1,0:T(8,128)(2,1)S(1)}, u32[]{:S(2)}, u32[]{:S(2)}) collective-permute-start(bf16[576,256]{1,0:T(8,128)(2,1)S(1)} %pack.1.refs_1_.refs_2_), channel_id=1, source_target_pairs={{0,24},{8,16},{16,8},{24,0},{32,56},{40,48},{48,40},{56,32},{64,88... | collective-permute-start | bytes 884744 | tf_op jit(solution)/shard_map/fetch_points/ppermute | solution.py:29
  6.8 1.6 %collective-permute-start = (bf16[512,256]{1,0:T(8,128)(2,1)S(1)}, bf16[512,256]{1,0:T(8,128)(2,1)S(1)}, u32[]{:S(2)}, u32[]{:S(2)}) collective-permute-start(bf16[512,256]{1,0:T(8,128)(2,1)S(1)} %constant_dynamic-slice_fusion.points_ref.refs_0_), channel_id=1, source_target_pairs={{0,32},{8,40},{16,48},{24,56},{32,0},{40,8},{48,16},{56,24},{64,96... | collective-permute-start | bytes 786440 | tf_op jit(solution)/shard_map/fetch_points/ppermute | solution.py:29
  8.3 2.2 %collective-permute-start.4 = (bf16[576,256]{1,0:T(8,128)(2,1)S(1)}, bf16[576,256]{1,0:T(8,128)(2,1)S(1)}, u32[]{:S(2)}, u32[]{:S(2)}) collective-permute-start(bf16[576,256]{1,0:T(8,128)(2,1)S(1)} %pack.1.refs_1_.refs_2_), channel_id=1, source_target_pairs={{0,96},{8,104},{16,112},{24,120},{32,64},{40,72},{48,80},{56,88},{... | collective-permute-start | bytes 884744 | tf_op jit(solution)/shard_map/fetch_points/ppermute | solution.py:29
  10.5 1.0 %collective-permute-start.8 = (bf16[576,256]{1,0:T(8,128)(2,1)S(1)}, bf16[576,256]{1,0:T(8,128)(2,1)S(1)}, u32[]{:S(2)}, u32[]{:S(2)}) collective-permute-start(bf16[576,256]{1,0:T(8,128)(2,1)S(1)} %pack.1.refs_1_.refs_2_), channel_id=1, source_target_pairs={{0,120},{8,112},{16,104},{24,96},{32,88},{40,80},{48,72},{56,64},{... | collective-permute-start | bytes 884744 | tf_op jit(solution)/shard_map/fetch_points/ppermute | solution.py:29
  11.5 0.8 %copy-done.1 = f32[512,16]{0,1:T(8,128)S(1)} copy-done((f32[512,16]{0,1:T(8,128)S(1)}, f32[512,16]{0,1:T(8,128)}, u32[]{:S(2)}) %copy-start.1) | copy-done | bytes 32792
  12.3 0.8 %build_tile.9 = (bf16[512,1024]{1,0:T(8,128)(2,1)S(1)}, f32[16,512]{1,0:T(8,128)S(1)}, f32[512,1]{1,0:T(8,128)S(1)}) custom-call(bf16[512,256]{1,0:T(8,128)(2,1)S(1)} %constant_dynamic-slice_fusion.points_ref.refs_0_, bf16[576,256]{1,0:T(8,128)(2,1)S(1)} %pack.1.refs_1_.refs_2_, bf16[576,256]{1,0:T(8,128)(2,1)S(1)} %collective-permute-done.2.refs_2_.refs_3_, ...), custom_call_target="tpu_custom_call" | custom-call | flops 16777216 | bytes 1024 | tf_op jit(solution)/shard_map/fetch_points/build_tile/pallas_call | solution.py:145
  13.1 2.0 %collective-permute-done.1.refs_1_.refs_2_ = bf16[512,256]{1,0:T(8,128)(2,1)S(1)} collective-permute-done((bf16[512,256]{1,0:T(8,128)(2,1)S(1)}, bf16[512,256]{1,0:T(8,128)(2,1)S(1)}, u32[]{:S(2)}, u32[]{:S(2)}) %collective-permute-start.1) | collective-permute-done | bytes 262176 | tf_op jit(solution)/shard_map/fetch_points/ppermute | solution.py:29
  15.1 1.4 %build_tile.10 = (bf16[1024,1024]{1,0:T(8,128)(2,1)S(1)}, f32[16,1024]{1,0:T(8,128)S(1)}, f32[1024,1]{1,0:T(8,128)S(1)}) custom-call(bf16[512,256]{1,0:T(8,128)(2,1)S(1)} %collective-permute-done.refs_0_.refs_1_, bf16[512,256]{1,0:T(8,128)(2,1)S(1)} %collective-permute-done.1.refs_1_.refs_2_, bf16[576,256]{1,0:T(8,128)(2,1)S(1)} %pack.1.refs_1_.refs_2_, ...), custom_call_target="tpu_custom_call" | custom-call | flops 33554432 | bytes 1024 | tf_op jit(solution)/shard_map/fetch_points/build_tile/pallas_call | solution.py:145
  16.6 2.8 %collective-permute-start.3 = (bf16[512,256]{1,0:T(8,128)(2,1)S(1)}, bf16[512,256]{1,0:T(8,128)(2,1)S(1)}, u32[]{:S(2)}, u32[]{:S(2)}) collective-permute-start(bf16[512,256]{1,0:T(8,128)(2,1)S(1)} %constant_dynamic-slice_fusion.points_ref.refs_0_), channel_id=1, source_target_pairs={{0,40},{8,32},{16,56},{24,48},{32,8},{40,0},{48,24},{56,16},{64,10... | collective-permute-start | bytes 786440 | tf_op jit(solution)/shard_map/fetch_points/ppermute | solution.py:29
  19.4 1.1 %build_tile.11 = (bf16[1536,512]{1,0:T(8,128)(2,1)S(1)}, f32[16,1536]{1,0:T(8,128)S(1)}) custom-call(bf16[512,256]{1,0:T(8,128)(2,1)S(1)} %constant_dynamic-slice_fusion.points_ref.refs_0_, bf16[512,256]{1,0:T(8,128)(2,1)S(1)} %collective-permute-done.refs_0_.refs_1_, bf16[512,256]{1,0:T(8,128)(2,1)S(1)} %collective-permute-done.1.refs_1_.refs_2_, ...), custom_call_target="tpu_custom_call" | custom-call | flops 1610612736 | bytes 1024 | tf_op jit(solution)/shard_map/build_tiles/build_tile/pallas_call | solution.py:145
  20.4 0.6 collective-permute-start.6
  21.0 1.1 %build_tile.12 = (bf16[1536,512]{1,0:T(8,128)(2,1)S(1)}, f32[16,1536]{1,0:T(8,128)S(1)}) custom-call(bf16[512,256]{1,0:T(8,128)(2,1)S(1)} %constant_dynamic-slice_fusion.points_ref.refs_0_, bf16[512,256]{1,0:T(8,128)(2,1)S(1)} %collective-permute-done.refs_0_.refs_1_, bf16[512,256]{1,0:T(8,128)(2,1)S(1)} %collective-permute-done.1.refs_1_.refs_2_, ...), custom_call_target="tpu_custom_call" | custom-call | flops 1610612736 | bytes 1024 | tf_op jit(solution)/shard_map/build_tiles/build_tile/pallas_call | solution.py:145
  22.1 1.1 %build_tile.13 = (bf16[1536,512]{1,0:T(8,128)(2,1)S(1)}, f32[16,1536]{1,0:T(8,128)S(1)}) custom-call(bf16[512,256]{1,0:T(8,128)(2,1)S(1)} %constant_dynamic-slice_fusion.points_ref.refs_0_, bf16[512,256]{1,0:T(8,128)(2,1)S(1)} %collective-permute-done.refs_0_.refs_1_, bf16[512,256]{1,0:T(8,128)(2,1)S(1)} %collective-permute-done.1.refs_1_.refs_2_, ...), custom_call_target="tpu_custom_call" | custom-call | flops 1610612736 | bytes 1024 | tf_op jit(solution)/shard_map/build_tiles/build_tile/pallas_call | solution.py:145
  23.2 1.1 %build_tile.14 = (bf16[1536,512]{1,0:T(8,128)(2,1)S(1)}, f32[16,1536]{1,0:T(8,128)S(1)}) custom-call(bf16[512,256]{1,0:T(8,128)(2,1)S(1)} %constant_dynamic-slice_fusion.points_ref.refs_0_, bf16[512,256]{1,0:T(8,128)(2,1)S(1)} %collective-permute-done.refs_0_.refs_1_, bf16[512,256]{1,0:T(8,128)(2,1)S(1)} %collective-permute-done.1.refs_1_.refs_2_, ...), custom_call_target="tpu_custom_call" | custom-call | flops 1610612736 | bytes 1024 | tf_op jit(solution)/shard_map/build_tiles/build_tile/pallas_call | solution.py:145
  24.3 0.8 %collective-permute-done.3.refs_0_.refs_3_ = bf16[512,256]{1,0:T(8,128)(2,1)S(1)} collective-permute-done((bf16[512,256]{1,0:T(8,128)(2,1)S(1)}, bf16[512,256]{1,0:T(8,128)(2,1)S(1)}, u32[]{:S(2)}, u32[]{:S(2)}) %collective-permute-start.3) | collective-permute-done | bytes 262176 | tf_op jit(solution)/shard_map/fetch_points/ppermute | solution.py:29
  25.0 2.0 %build_tile.15 = (bf16[512,3072]{1,0:T(8,128)(2,1)S(1)}, f32[16,512]{1,0:T(8,128)S(1)}, f32[512,1]{1,0:T(8,128)S(1)}) custom-call(bf16[512,256]{1,0:T(8,128)(2,1)S(1)} %collective-permute-done.3.refs_0_.refs_3_, bf16[576,256]{1,0:T(8,128)(2,1)S(1)} %pack.1.refs_1_.refs_2_, bf16[576,256]{1,0:T(8,128)(2,1)S(1)} %collective-permute-done.2.refs_2_.refs_3_, ...), custom_call_target="tpu_custom_call" | custom-call | flops 3221225472 | bytes 1024 | tf_op jit(solution)/shard_map/build_tiles/build_tile/pallas_call | solution.py:145
  27.3 1.3 %build_tile.16 = (bf16[2048,512]{1,0:T(8,128)(2,1)S(1)}, f32[16,2048]{1,0:T(8,128)S(1)}) custom-call(bf16[512,256]{1,0:T(8,128)(2,1)S(1)} %constant_dynamic-slice_fusion.points_ref.refs_0_, bf16[512,256]{1,0:T(8,128)(2,1)S(1)} %collective-permute-done.refs_0_.refs_1_, bf16[512,256]{1,0:T(8,128)(2,1)S(1)} %collective-permute-done.1.refs_1_.refs_2_, ...), custom_call_target="tpu_custom_call" | custom-call | flops 2147483648 | bytes 1024 | tf_op jit(solution)/shard_map/build_tiles/build_tile/pallas_call | solution.py:145
  28.9 1.3 %build_tile.17 = (bf16[2048,512]{1,0:T(8,128)(2,1)S(1)}, f32[16,2048]{1,0:T(8,128)S(1)}) custom-call(bf16[512,256]{1,0:T(8,128)(2,1)S(1)} %constant_dynamic-slice_fusion.points_ref.refs_0_, bf16[512,256]{1,0:T(8,128)(2,1)S(1)} %collective-permute-done.refs_0_.refs_1_, bf16[512,256]{1,0:T(8,128)(2,1)S(1)} %collective-permute-done.1.refs_1_.refs_2_, ...), custom_call_target="tpu_custom_call" | custom-call | flops 2147483648 | bytes 1024 | tf_op jit(solution)/shard_map/build_tiles/build_tile/pallas_call | solution.py:145
  30.3 1.7 %collective-permute-start.10 = (bf16[80,512]{1,0:T(8,128)(2,1)S(1)}, bf16[80,512]{1,0:T(8,128)(2,1)S(1)}, u32[]{:S(2)}, u32[]{:S(2)}) collective-permute-start(bf16[80,512]{1,0:T(8,128)(2,1)S(1)} %get-tuple-element.80), channel_id=1, source_target_pairs={{0,32},{8,40},{16,48},{24,56},{32,0},{40,8},{48,16},{56,24},{64,96... | collective-permute-start | bytes 245768 | tf_op jit(solution)/shard_map/sum_over_rows/ppermute | solution.py:29
  31.9 1.4 %collective-permute-start.11 = (bf16[80,512]{1,0:T(8,128)(2,1)S(1)}, bf16[80,512]{1,0:T(8,128)(2,1)S(1)}, u32[]{:S(2)}, u32[]{:S(2)}) collective-permute-start(bf16[80,512]{1,0:T(8,128)(2,1)S(1)} %get-tuple-element.81), channel_id=1, source_target_pairs={{0,8},{8,0},{16,24},{24,16},{32,40},{40,32},{48,56},{56,48},{64,72... | collective-permute-start | bytes 245768 | tf_op jit(solution)/shard_map/sum_over_rows/ppermute | solution.py:29
  33.8 1.2 %collective-permute-done.10.refs_1_ = bf16[80,512]{1,0:T(8,128)(2,1)S(1)} collective-permute-done((bf16[80,512]{1,0:T(8,128)(2,1)S(1)}, bf16[80,512]{1,0:T(8,128)(2,1)S(1)}, u32[]{:S(2)}, u32[]{:S(2)}) %collective-permute-start.10) | collective-permute-done | bytes 81952 | tf_op jit(solution)/shard_map/sum_over_rows/ppermute | solution.py:29
  35.0 2.1 %collective-permute-done.11.refs_2_ = bf16[80,512]{1,0:T(8,128)(2,1)S(1)} collective-permute-done((bf16[80,512]{1,0:T(8,128)(2,1)S(1)}, bf16[80,512]{1,0:T(8,128)(2,1)S(1)}, u32[]{:S(2)}, u32[]{:S(2)}) %collective-permute-start.11) | collective-permute-done | bytes 81952 | tf_op jit(solution)/shard_map/sum_over_rows/ppermute | solution.py:29
  37.1 1.6 %collective-permute-done.12.refs_3_ = bf16[80,512]{1,0:T(8,128)(2,1)S(1)} collective-permute-done((bf16[80,512]{1,0:T(8,128)(2,1)S(1)}, bf16[80,512]{1,0:T(8,128)(2,1)S(1)}, u32[]{:S(2)}, u32[]{:S(2)}) %collective-permute-start.12) | collective-permute-done | bytes 81952 | tf_op jit(solution)/shard_map/sum_over_rows/ppermute | solution.py:29
  38.7 1.4 %second_product.2 = f32[16,2048]{1,0:T(8,128)S(1)} custom-call(bf16[32,2048]{1,0:T(8,128)(2,1)S(1)} %get-tuple-element.94.narrow_ref, bf16[512,1024]{1,0:T(8,128)(2,1)S(1)} %get-tuple-element.85.refs_0_, bf16[1024,1024]{1,0:T(8,128)(2,1)S(1)} %get-tuple-element.86.refs_1_, bf16[1536,512]{1,0:T(8,128)(2,1)S(1)} %get-tuple-element.87.refs_2_, ...), custom_call_target="tpu_custom_call" | custom-call | flops 134217728 | bytes 1024 | tf_op jit(solution)/shard_map/second_product/pallas_call | solution.py:231
  40.2 1.4 %second_product.3.mine_ref = f32[16,2048]{1,0:T(8,128)S(1)} custom-call(bf16[32,2048]{1,0:T(8,128)(2,1)S(1)} %get-tuple-element.94.narrow_ref, bf16[512,1024]{1,0:T(8,128)(2,1)S(1)} %get-tuple-element.85.refs_0_, bf16[1024,1024]{1,0:T(8,128)(2,1)S(1)} %get-tuple-element.86.refs_1_, bf16[1536,512]{1,0:T(8,128)(2,1)S(1)} %get-tuple-element.87.refs_2_, ...), custom_call_target="tpu_custom_call" | custom-call | flops 134217728 | bytes 1024 | tf_op jit(solution)/shard_map/second_product/pallas_call | solution.py:231
  41.7 2.3 %collective-permute-start.14 = (f32[16,512]{1,0:T(8,128)S(1)}, f32[16,512]{1,0:T(8,128)S(1)}, u32[]{:S(2)}, u32[]{:S(2)}) collective-permute-start(f32[16,512]{1,0:T(8,128)S(1)} %get-tuple-element.97), channel_id=1, source_target_pairs={{0,96},{8,104},{16,112},{24,120},{32,64},{40,72},{48,80},{56,88},{... | collective-permute-start | bytes 98312 | tf_op jit(solution)/shard_map/sum_over_columns/ppermute | solution.py:29
  44.4 3.2 %collective-permute-start.16 = (f32[16,512]{1,0:T(8,128)S(1)}, f32[16,512]{1,0:T(8,128)S(1)}, u32[]{:S(2)}, u32[]{:S(2)}) collective-permute-start(f32[16,512]{1,0:T(8,128)S(1)} %get-tuple-element.99), channel_id=1, source_target_pairs={{0,120},{8,112},{16,104},{24,96},{32,88},{40,80},{48,72},{56,64},{... | collective-permute-start | bytes 98312 | tf_op jit(solution)/shard_map/sum_over_columns/ppermute | solution.py:29
  47.6 1.4 %collective-permute-done.15.refs_2_ = f32[16,512]{1,0:T(8,128)S(1)} collective-permute-done((f32[16,512]{1,0:T(8,128)S(1)}, f32[16,512]{1,0:T(8,128)S(1)}, u32[]{:S(2)}, u32[]{:S(2)}) %collective-permute-start.15) | collective-permute-done | bytes 32800 | tf_op jit(solution)/shard_map/sum_over_columns/ppermute | solution.py:29
  49.0 2.6 %collective-permute-done.16.refs_3_ = f32[16,512]{1,0:T(8,128)S(1)} collective-permute-done((f32[16,512]{1,0:T(8,128)S(1)}, f32[16,512]{1,0:T(8,128)S(1)}, u32[]{:S(2)}, u32[]{:S(2)}) %collective-permute-start.16) | collective-permute-done | bytes 32800 | tf_op jit(solution)/shard_map/sum_over_columns/ppermute | solution.py:29
  51.9 12.1 %all_to_all.8 = f32[32,1,128]{2,1,0:T(1,128)S(1)} all-to-all(f32[32,1,128]{2,1,0:T(1,128)S(1)} %broadcast_in_dim.2), channel_id=1, replica_groups=mesh['y'=4,'z'=4,'c'=2,'x'=4] {'y','z','c'}, dimensions={0} | all-to-all | bytes 32768 | tf_op jit(solution)/shard_map/final_sums/all_to_all | solution.py:374
  64.0 1.0 %finish.1 = (f32[16,512]{1,0:T(8,128)}, f32[16,512]{1,0:T(8,128)}) custom-call(f32[16,512]{1,0:T(8,128)S(1)} %bitcast.12, f32[16,512]{1,0:T(8,128)S(1)} %get-tuple-element.83.rho_ref, f32[16,512]{1,0:T(8,128)S(1)} %get-tuple-element.100.image_ref, f32[32,128]{1,0:T(8,128)S(1)} %bitcast.13), custom_call_target="tpu_custom_call" | custom-call | tf_op jit(solution)/shard_map/finish/pallas_call | solution.py:305
  (29 shorter events, 2.3 us)
Async XLA Ops:
  0.6 1.5 %copy-start = (bf16[1024,256]{1,0:T(8,128)(2,1)S(1)}, bf16[1024,256]{1,0:T(8,128)(2,1)}, u32[]{:S(2)}) copy-start(bf16[1024,256]{1,0:T(8,128)(2,1)} %param.3) | copy-start | bytes 1572868
  2.5 8.1 %collective-permute-start.2 = (bf16[576,256]{1,0:T(8,128)(2,1)S(1)}, bf16[576,256]{1,0:T(8,128)(2,1)S(1)}, u32[]{:S(2)}, u32[]{:S(2)}) collective-permute-start(bf16[576,256]{1,0:T(8,128)(2,1)S(1)} %pack.1.refs_1_.refs_2_), channel_id=1, source_target_pairs={{0,4},{4,0},{1,5},{5,1},{2,6},{6,2},{3,7},{7,3},{8,12},{12,8},{9,1... | collective-permute-start | bytes 884744 | tf_op jit(solution)/shard_map/fetch_points/ppermute | solution.py:38
  2.6 14.0 %collective-permute-start.5 = (bf16[576,256]{1,0:T(8,128)(2,1)S(1)}, bf16[576,256]{1,0:T(8,128)(2,1)S(1)}, u32[]{:S(2)}, u32[]{:S(2)}) collective-permute-start(bf16[576,256]{1,0:T(8,128)(2,1)S(1)} %pack.1.refs_1_.refs_2_), channel_id=1, source_target_pairs={{0,24},{8,16},{16,8},{24,0},{32,56},{40,48},{48,40},{56,32},{64,88... | collective-permute-start | bytes 884744 | tf_op jit(solution)/shard_map/fetch_points/ppermute | solution.py:29
  6.8 8.4 %collective-permute-start.1 = (bf16[512,256]{1,0:T(8,128)(2,1)S(1)}, bf16[512,256]{1,0:T(8,128)(2,1)S(1)}, u32[]{:S(2)}, u32[]{:S(2)}) collective-permute-start(bf16[512,256]{1,0:T(8,128)(2,1)S(1)} %constant_dynamic-slice_fusion.points_ref.refs_0_), channel_id=1, source_target_pairs={{0,8},{8,0},{16,24},{24,16},{32,40},{40,32},{48,56},{56,48},{64,72... | collective-permute-start | bytes 786440 | tf_op jit(solution)/shard_map/fetch_points/ppermute | solution.py:29
  6.8 8.4 %collective-permute-start = (bf16[512,256]{1,0:T(8,128)(2,1)S(1)}, bf16[512,256]{1,0:T(8,128)(2,1)S(1)}, u32[]{:S(2)}, u32[]{:S(2)}) collective-permute-start(bf16[512,256]{1,0:T(8,128)(2,1)S(1)} %constant_dynamic-slice_fusion.points_ref.refs_0_), channel_id=1, source_target_pairs={{0,32},{8,40},{16,48},{24,56},{32,0},{40,8},{48,16},{56,24},{64,96... | collective-permute-start | bytes 786440 | tf_op jit(solution)/shard_map/fetch_points/ppermute | solution.py:29
  8.3 12.1 %collective-permute-start.4 = (bf16[576,256]{1,0:T(8,128)(2,1)S(1)}, bf16[576,256]{1,0:T(8,128)(2,1)S(1)}, u32[]{:S(2)}, u32[]{:S(2)}) collective-permute-start(bf16[576,256]{1,0:T(8,128)(2,1)S(1)} %pack.1.refs_1_.refs_2_), channel_id=1, source_target_pairs={{0,96},{8,104},{16,112},{24,120},{32,64},{40,72},{48,80},{56,88},{... | collective-permute-start | bytes 884744 | tf_op jit(solution)/shard_map/fetch_points/ppermute | solution.py:29
  10.5 16.5 %collective-permute-start.8 = (bf16[576,256]{1,0:T(8,128)(2,1)S(1)}, bf16[576,256]{1,0:T(8,128)(2,1)S(1)}, u32[]{:S(2)}, u32[]{:S(2)}) collective-permute-start(bf16[576,256]{1,0:T(8,128)(2,1)S(1)} %pack.1.refs_1_.refs_2_), channel_id=1, source_target_pairs={{0,120},{8,112},{16,104},{24,96},{32,88},{40,80},{48,72},{56,64},{... | collective-permute-start | bytes 884744 | tf_op jit(solution)/shard_map/fetch_points/ppermute | solution.py:29
  11.5 0.8 %copy-start.1 = (f32[512,16]{0,1:T(8,128)S(1)}, f32[512,16]{0,1:T(8,128)}, u32[]{:S(2)}) copy-start(f32[512,16]{0,1:T(8,128)} %param.5) | copy-start | bytes 98308
  16.6 8.5 %collective-permute-start.3 = (bf16[512,256]{1,0:T(8,128)(2,1)S(1)}, bf16[512,256]{1,0:T(8,128)(2,1)S(1)}, u32[]{:S(2)}, u32[]{:S(2)}) collective-permute-start(bf16[512,256]{1,0:T(8,128)(2,1)S(1)} %constant_dynamic-slice_fusion.points_ref.refs_0_), channel_id=1, source_target_pairs={{0,40},{8,32},{16,56},{24,48},{32,8},{40,0},{48,24},{56,16},{64,10... | collective-permute-start | bytes 786440 | tf_op jit(solution)/shard_map/fetch_points/ppermute | solution.py:29
  19.3 2.7 %collective-permute-start.7 = (bf16[576,256]{1,0:T(8,128)(2,1)S(1)}, bf16[576,256]{1,0:T(8,128)(2,1)S(1)}, u32[]{:S(2)}, u32[]{:S(2)}) collective-permute-start(bf16[576,256]{1,0:T(8,128)(2,1)S(1)} %collective-permute-done.5.refs_3_.refs_4_), channel_id=1, source_target_pairs={{0,4},{4,0},{1,5},{5,1},{2,6},{6,2},{3,7},{7,3},{8,12},{12,8},{9,1... | collective-permute-start | bytes 884744 | tf_op jit(solution)/shard_map/build_tiles/ppermute | solution.py:38
  20.4 2.8 %collective-permute-start.6 = (bf16[576,256]{1,0:T(8,128)(2,1)S(1)}, bf16[576,256]{1,0:T(8,128)(2,1)S(1)}, u32[]{:S(2)}, u32[]{:S(2)}) collective-permute-start(bf16[576,256]{1,0:T(8,128)(2,1)S(1)} %collective-permute-done.4.refs_3_), channel_id=1, source_target_pairs={{0,4},{4,0},{1,5},{5,1},{2,6},{6,2},{3,7},{7,3},{8,12},{12,8},{9,1... | collective-permute-start | bytes 884744 | tf_op jit(solution)/shard_map/build_tiles/ppermute | solution.py:38
  27.1 1.8 %collective-permute-start.9 = (bf16[576,256]{1,0:T(8,128)(2,1)S(1)}, bf16[576,256]{1,0:T(8,128)(2,1)S(1)}, u32[]{:S(2)}, u32[]{:S(2)}) collective-permute-start(bf16[576,256]{1,0:T(8,128)(2,1)S(1)} %collective-permute-done.8.refs_4_), channel_id=1, source_target_pairs={{0,4},{4,0},{1,5},{5,1},{2,6},{6,2},{3,7},{7,3},{8,12},{12,8},{9,1... | collective-permute-start | bytes 884744 | tf_op jit(solution)/shard_map/build_tiles/ppermute | solution.py:38
  30.3 4.7 %collective-permute-start.10 = (bf16[80,512]{1,0:T(8,128)(2,1)S(1)}, bf16[80,512]{1,0:T(8,128)(2,1)S(1)}, u32[]{:S(2)}, u32[]{:S(2)}) collective-permute-start(bf16[80,512]{1,0:T(8,128)(2,1)S(1)} %get-tuple-element.80), channel_id=1, source_target_pairs={{0,32},{8,40},{16,48},{24,56},{32,0},{40,8},{48,16},{56,24},{64,96... | collective-permute-start | bytes 245768 | tf_op jit(solution)/shard_map/sum_over_rows/ppermute | solution.py:29
  31.9 5.2 %collective-permute-start.11 = (bf16[80,512]{1,0:T(8,128)(2,1)S(1)}, bf16[80,512]{1,0:T(8,128)(2,1)S(1)}, u32[]{:S(2)}, u32[]{:S(2)}) collective-permute-start(bf16[80,512]{1,0:T(8,128)(2,1)S(1)} %get-tuple-element.81), channel_id=1, source_target_pairs={{0,8},{8,0},{16,24},{24,16},{32,40},{40,32},{48,56},{56,48},{64,72... | collective-permute-start | bytes 245768 | tf_op jit(solution)/shard_map/sum_over_rows/ppermute | solution.py:29
  33.3 5.3 %collective-permute-start.12 = (bf16[80,512]{1,0:T(8,128)(2,1)S(1)}, bf16[80,512]{1,0:T(8,128)(2,1)S(1)}, u32[]{:S(2)}, u32[]{:S(2)}) collective-permute-start(bf16[80,512]{1,0:T(8,128)(2,1)S(1)} %get-tuple-element.82), channel_id=1, source_target_pairs={{0,40},{8,32},{16,56},{24,48},{32,8},{40,0},{48,24},{56,16},{64,10... | collective-permute-start | bytes 245768 | tf_op jit(solution)/shard_map/sum_over_rows/ppermute | solution.py:29
  40.2 23.8 %copy-start.2 = (f32[512,16]{0,1:T(8,128)S(1)}, f32[512,16]{0,1:T(8,128)}, u32[]{:S(2)}) copy-start(f32[512,16]{0,1:T(8,128)} %param.5) | copy-start | bytes 98308
  40.2 1.5 %collective-permute-start.13 = (f32[16,2048]{1,0:T(8,128)S(1)}, f32[16,2048]{1,0:T(8,128)S(1)}, u32[]{:S(2)}, u32[]{:S(2)}) collective-permute-start(f32[16,2048]{1,0:T(8,128)S(1)} %second_product.2), channel_id=1, source_target_pairs={{0,4},{4,0},{1,5},{5,1},{2,6},{6,2},{3,7},{7,3},{8,12},{12,8},{9,1... | collective-permute-start | bytes 393224 | tf_op jit(solution)/shard_map/sum_over_columns/ppermute | solution.py:38
  41.7 6.0 %collective-permute-start.14 = (f32[16,512]{1,0:T(8,128)S(1)}, f32[16,512]{1,0:T(8,128)S(1)}, u32[]{:S(2)}, u32[]{:S(2)}) collective-permute-start(f32[16,512]{1,0:T(8,128)S(1)} %get-tuple-element.97), channel_id=1, source_target_pairs={{0,96},{8,104},{16,112},{24,120},{32,64},{40,72},{48,80},{56,88},{... | collective-permute-start | bytes 98312 | tf_op jit(solution)/shard_map/sum_over_columns/ppermute | solution.py:29
  43.9 5.1 %collective-permute-start.15 = (f32[16,512]{1,0:T(8,128)S(1)}, f32[16,512]{1,0:T(8,128)S(1)}, u32[]{:S(2)}, u32[]{:S(2)}) collective-permute-start(f32[16,512]{1,0:T(8,128)S(1)} %get-tuple-element.98), channel_id=1, source_target_pairs={{0,24},{8,16},{16,8},{24,0},{32,56},{40,48},{48,40},{56,32},{64,88... | collective-permute-start | bytes 98312 | tf_op jit(solution)/shard_map/sum_over_columns/ppermute | solution.py:29
  44.4 7.2 %collective-permute-start.16 = (f32[16,512]{1,0:T(8,128)S(1)}, f32[16,512]{1,0:T(8,128)S(1)}, u32[]{:S(2)}, u32[]{:S(2)}) collective-permute-start(f32[16,512]{1,0:T(8,128)S(1)} %get-tuple-element.99), channel_id=1, source_target_pairs={{0,120},{8,112},{16,104},{24,96},{32,88},{40,80},{48,72},{56,64},{... | collective-permute-start | bytes 98312 | tf_op jit(solution)/shard_map/sum_over_columns/ppermute | solution.py:29

commit v22 on v20

--- a/solution.py
+++ b/solution.py
@@ -12,8 +12,8 @@
 LANES = 128
 CHUNK = 256
 HERE = (0, 0)
-ROWS = (HERE, (1, 0), (0, 1), (1, 1))
-SQUARE = (HERE, (3, 0), (0, 3), (3, 3))
+ROWS = (HERE, (1, 0), (0, 3), (1, 3))
+SQUARE = (HERE, (3, 0), (0, 1), (3, 1))
 COLS = ((0, 0), (1, 0), (0, 1), (0, 2), (1, 1), (1, 2), (0, 3), (1, 3))
 
 noise_level = 1.0

time: 64.5 us -> 65.6 us (1.017)
    ppermute x12, starting transfers between devices: 21.3 us -> 21.9 us  [swap(): return lax.ppermute(value, ('y', 'z'), pairs)]
  transfers between devices with their start and end apart: 17 -> 17, of which waited for: 7 -> 9; matrix products, arithmetic and copies ran while one was open for 0% -> 0% of each run, Pallas kernels for 18% -> 18%
where the time goes in v22:
time: 65.6 us; the launch traced here: 64.6 us
  starting transfers between devices  22.8 us (35%)
  Pallas kernels  15.8 us (24%)
  blocking collectives  12.2 us (19%)
  waiting for transfers between devices  10.6 us (16%)
  between operations  1.43 us (2%)
  local copies, waits for them, and re-layouts  0.85 us (1%)
  other arithmetic  0.76 us (1%)
    ppermute x12, starting transfers between devices, swap(): return lax.ppermute(value, ('y', 'z'), pairs)  21.9 us
    all_to_all x1, blocking collectives, on_device(): sums = lax.all_to_all(sums, ('y', 'z', 'c'), 0, 0, tiled=True)  12.2 us
    pallas_call x9, Pallas kernels, build(): pl.pallas_call(functools.partial(tile_kernel, counts, probes), out_shape=...  11.3 us
    ppermute x12, waiting for transfers between devices, swap(): return lax.ppermute(value, ('y', 'z'), pairs)  10.4 us
    pallas_call x2, Pallas kernels, second_product(): pl.pallas_call(functools.partial(second_kernel, own, half, places), in_sp...  2.87 us
  transfers between devices with their start and end apart: 17, of which 9 were waited for; matrix products, arithmetic and copies ran while one was open for 0% of the time, Pallas kernels for 18%

profile of v22, /device:TPU:0, one launch (start us, length us, event | category | flops | bytes accessed | tf_op | source)
XLA Modules:
  0.0 64.6 jit_solution(16601295571273862490)
XLA Ops:
  1.3 0.8 %bitcast_convert_fusion.side_ref = bf16[16,512]{1,0:T(8,128)(2,1)S(1)} fusion(f32[512,16]{0,1:T(8,128)} %param.5), kind=kLoop, calls=%fused_computation.1 | loop fusion | flops 8192 | bytes 49152 | tf_op jit(solution)/shard_map/fetch_points/convert_element_type | solution.py:318
  2.6 2.1 %collective-permute-start.5 = (bf16[576,256]{1,0:T(8,128)(2,1)S(1)}, bf16[576,256]{1,0:T(8,128)(2,1)S(1)}, u32[]{:S(2)}, u32[]{:S(2)}) collective-permute-start(bf16[576,256]{1,0:T(8,128)(2,1)S(1)} %pack.1.refs_1_.refs_2_), channel_id=1, source_target_pairs={{0,8},{8,0},{16,24},{24,16},{32,40},{40,32},{48,56},{56,48},{64,72... | collective-permute-start | bytes 884744 | tf_op jit(solution)/shard_map/fetch_points/ppermute | solution.py:29
  4.6 2.5 %collective-permute-start.1 = (bf16[512,256]{1,0:T(8,128)(2,1)S(1)}, bf16[512,256]{1,0:T(8,128)(2,1)S(1)}, u32[]{:S(2)}, u32[]{:S(2)}) collective-permute-start(bf16[512,256]{1,0:T(8,128)(2,1)S(1)} %constant_dynamic-slice_fusion.points_ref.refs_0_), channel_id=1, source_target_pairs={{0,24},{8,16},{16,8},{24,0},{32,56},{40,48},{48,40},{56,32},{64,88... | collective-permute-start | bytes 786440 | tf_op jit(solution)/shard_map/fetch_points/ppermute | solution.py:29
  7.2 1.6 %collective-permute-start = (bf16[512,256]{1,0:T(8,128)(2,1)S(1)}, bf16[512,256]{1,0:T(8,128)(2,1)S(1)}, u32[]{:S(2)}, u32[]{:S(2)}) collective-permute-start(bf16[512,256]{1,0:T(8,128)(2,1)S(1)} %constant_dynamic-slice_fusion.points_ref.refs_0_), channel_id=1, source_target_pairs={{0,32},{8,40},{16,48},{24,56},{32,0},{40,8},{48,16},{56,24},{64,96... | collective-permute-start | bytes 786440 | tf_op jit(solution)/shard_map/fetch_points/ppermute | solution.py:29
  8.7 2.2 %collective-permute-start.4 = (bf16[576,256]{1,0:T(8,128)(2,1)S(1)}, bf16[576,256]{1,0:T(8,128)(2,1)S(1)}, u32[]{:S(2)}, u32[]{:S(2)}) collective-permute-start(bf16[576,256]{1,0:T(8,128)(2,1)S(1)} %pack.1.refs_1_.refs_2_), channel_id=1, source_target_pairs={{0,96},{8,104},{16,112},{24,120},{32,64},{40,72},{48,80},{56,88},{... | collective-permute-start | bytes 884744 | tf_op jit(solution)/shard_map/fetch_points/ppermute | solution.py:29
  10.9 1.5 %collective-permute-start.8 = (bf16[576,256]{1,0:T(8,128)(2,1)S(1)}, bf16[576,256]{1,0:T(8,128)(2,1)S(1)}, u32[]{:S(2)}, u32[]{:S(2)}) collective-permute-start(bf16[576,256]{1,0:T(8,128)(2,1)S(1)} %pack.1.refs_1_.refs_2_), channel_id=1, source_target_pairs={{0,104},{8,96},{16,120},{24,112},{32,72},{40,64},{48,88},{56,80},{... | collective-permute-start | bytes 884744 | tf_op jit(solution)/shard_map/fetch_points/ppermute | solution.py:29
  12.4 0.8 %copy-done.1 = f32[512,16]{0,1:T(8,128)S(1)} copy-done((f32[512,16]{0,1:T(8,128)S(1)}, f32[512,16]{0,1:T(8,128)}, u32[]{:S(2)}) %copy-start.1) | copy-done | bytes 32792
  13.2 0.8 %build_tile.9 = (bf16[512,1024]{1,0:T(8,128)(2,1)S(1)}, f32[16,512]{1,0:T(8,128)S(1)}, f32[512,1]{1,0:T(8,128)S(1)}) custom-call(bf16[512,256]{1,0:T(8,128)(2,1)S(1)} %constant_dynamic-slice_fusion.points_ref.refs_0_, bf16[576,256]{1,0:T(8,128)(2,1)S(1)} %pack.1.refs_1_.refs_2_, bf16[576,256]{1,0:T(8,128)(2,1)S(1)} %collective-permute-done.2.refs_2_.refs_3_, ...), custom_call_target="tpu_custom_call" | custom-call | flops 16777216 | bytes 1024 | tf_op jit(solution)/shard_map/fetch_points/build_tile/pallas_call | solution.py:145
  14.2 1.0 %collective-permute-done.refs_0_.refs_1_ = bf16[512,256]{1,0:T(8,128)(2,1)S(1)} collective-permute-done((bf16[512,256]{1,0:T(8,128)(2,1)S(1)}, bf16[512,256]{1,0:T(8,128)(2,1)S(1)}, u32[]{:S(2)}, u32[]{:S(2)}) %collective-permute-start) | collective-permute-done | bytes 262176 | tf_op jit(solution)/shard_map/fetch_points/ppermute | solution.py:29
  15.3 2.5 %collective-permute-start.3 = (bf16[512,256]{1,0:T(8,128)(2,1)S(1)}, bf16[512,256]{1,0:T(8,128)(2,1)S(1)}, u32[]{:S(2)}, u32[]{:S(2)}) collective-permute-start(bf16[512,256]{1,0:T(8,128)(2,1)S(1)} %constant_dynamic-slice_fusion.points_ref.refs_0_), channel_id=1, source_target_pairs={{0,56},{8,48},{16,40},{24,32},{32,24},{40,16},{48,8},{56,0},{64,12... | collective-permute-start | bytes 786440 | tf_op jit(solution)/shard_map/fetch_points/ppermute | solution.py:29
  17.8 1.4 %build_tile.10 = (bf16[1024,1024]{1,0:T(8,128)(2,1)S(1)}, f32[16,1024]{1,0:T(8,128)S(1)}, f32[1024,1]{1,0:T(8,128)S(1)}) custom-call(bf16[512,256]{1,0:T(8,128)(2,1)S(1)} %collective-permute-done.refs_0_.refs_1_, bf16[512,256]{1,0:T(8,128)(2,1)S(1)} %collective-permute-done.1.refs_1_.refs_2_, bf16[576,256]{1,0:T(8,128)(2,1)S(1)} %pack.1.refs_1_.refs_2_, ...), custom_call_target="tpu_custom_call" | custom-call | flops 33554432 | bytes 1024 | tf_op jit(solution)/shard_map/fetch_points/build_tile/pallas_call | solution.py:145
  19.2 1.1 %build_tile.11 = (bf16[1536,512]{1,0:T(8,128)(2,1)S(1)}, f32[16,1536]{1,0:T(8,128)S(1)}) custom-call(bf16[512,256]{1,0:T(8,128)(2,1)S(1)} %constant_dynamic-slice_fusion.points_ref.refs_0_, bf16[512,256]{1,0:T(8,128)(2,1)S(1)} %collective-permute-done.refs_0_.refs_1_, bf16[512,256]{1,0:T(8,128)(2,1)S(1)} %collective-permute-done.1.refs_1_.refs_2_, ...), custom_call_target="tpu_custom_call" | custom-call | flops 1610612736 | bytes 1024 | tf_op jit(solution)/shard_map/build_tiles/build_tile/pallas_call | solution.py:145
  20.3 0.6 collective-permute-start.6
  20.9 1.1 %build_tile.12 = (bf16[1536,512]{1,0:T(8,128)(2,1)S(1)}, f32[16,1536]{1,0:T(8,128)S(1)}) custom-call(bf16[512,256]{1,0:T(8,128)(2,1)S(1)} %constant_dynamic-slice_fusion.points_ref.refs_0_, bf16[512,256]{1,0:T(8,128)(2,1)S(1)} %collective-permute-done.refs_0_.refs_1_, bf16[512,256]{1,0:T(8,128)(2,1)S(1)} %collective-permute-done.1.refs_1_.refs_2_, ...), custom_call_target="tpu_custom_call" | custom-call | flops 1610612736 | bytes 1024 | tf_op jit(solution)/shard_map/build_tiles/build_tile/pallas_call | solution.py:145
  21.9 1.1 %build_tile.13 = (bf16[1536,512]{1,0:T(8,128)(2,1)S(1)}, f32[16,1536]{1,0:T(8,128)S(1)}) custom-call(bf16[512,256]{1,0:T(8,128)(2,1)S(1)} %constant_dynamic-slice_fusion.points_ref.refs_0_, bf16[512,256]{1,0:T(8,128)(2,1)S(1)} %collective-permute-done.refs_0_.refs_1_, bf16[512,256]{1,0:T(8,128)(2,1)S(1)} %collective-permute-done.1.refs_1_.refs_2_, ...), custom_call_target="tpu_custom_call" | custom-call | flops 1610612736 | bytes 1024 | tf_op jit(solution)/shard_map/build_tiles/build_tile/pallas_call | solution.py:145
  23.0 1.1 %build_tile.14 = (bf16[1536,512]{1,0:T(8,128)(2,1)S(1)}, f32[16,1536]{1,0:T(8,128)S(1)}) custom-call(bf16[512,256]{1,0:T(8,128)(2,1)S(1)} %constant_dynamic-slice_fusion.points_ref.refs_0_, bf16[512,256]{1,0:T(8,128)(2,1)S(1)} %collective-permute-done.refs_0_.refs_1_, bf16[512,256]{1,0:T(8,128)(2,1)S(1)} %collective-permute-done.1.refs_1_.refs_2_, ...), custom_call_target="tpu_custom_call" | custom-call | flops 1610612736 | bytes 1024 | tf_op jit(solution)/shard_map/build_tiles/build_tile/pallas_call | solution.py:145
  24.6 2.0 %build_tile.15 = (bf16[512,3072]{1,0:T(8,128)(2,1)S(1)}, f32[16,512]{1,0:T(8,128)S(1)}, f32[512,1]{1,0:T(8,128)S(1)}) custom-call(bf16[512,256]{1,0:T(8,128)(2,1)S(1)} %collective-permute-done.3.refs_0_.refs_3_, bf16[576,256]{1,0:T(8,128)(2,1)S(1)} %pack.1.refs_1_.refs_2_, bf16[576,256]{1,0:T(8,128)(2,1)S(1)} %collective-permute-done.2.refs_2_.refs_3_, ...), custom_call_target="tpu_custom_call" | custom-call | flops 3221225472 | bytes 1024 | tf_op jit(solution)/shard_map/build_tiles/build_tile/pallas_call | solution.py:145
  26.8 1.3 %build_tile.16 = (bf16[2048,512]{1,0:T(8,128)(2,1)S(1)}, f32[16,2048]{1,0:T(8,128)S(1)}) custom-call(bf16[512,256]{1,0:T(8,128)(2,1)S(1)} %constant_dynamic-slice_fusion.points_ref.refs_0_, bf16[512,256]{1,0:T(8,128)(2,1)S(1)} %collective-permute-done.refs_0_.refs_1_, bf16[512,256]{1,0:T(8,128)(2,1)S(1)} %collective-permute-done.1.refs_1_.refs_2_, ...), custom_call_target="tpu_custom_call" | custom-call | flops 2147483648 | bytes 1024 | tf_op jit(solution)/shard_map/build_tiles/build_tile/pallas_call | solution.py:145
  28.4 1.3 %build_tile.17 = (bf16[2048,512]{1,0:T(8,128)(2,1)S(1)}, f32[16,2048]{1,0:T(8,128)S(1)}) custom-call(bf16[512,256]{1,0:T(8,128)(2,1)S(1)} %constant_dynamic-slice_fusion.points_ref.refs_0_, bf16[512,256]{1,0:T(8,128)(2,1)S(1)} %collective-permute-done.refs_0_.refs_1_, bf16[512,256]{1,0:T(8,128)(2,1)S(1)} %collective-permute-done.1.refs_1_.refs_2_, ...), custom_call_target="tpu_custom_call" | custom-call | flops 2147483648 | bytes 1024 | tf_op jit(solution)/shard_map/build_tiles/build_tile/pallas_call | solution.py:145
  29.8 1.7 %collective-permute-start.10 = (bf16[80,512]{1,0:T(8,128)(2,1)S(1)}, bf16[80,512]{1,0:T(8,128)(2,1)S(1)}, u32[]{:S(2)}, u32[]{:S(2)}) collective-permute-start(bf16[80,512]{1,0:T(8,128)(2,1)S(1)} %get-tuple-element.78), channel_id=1, source_target_pairs={{0,32},{8,40},{16,48},{24,56},{32,0},{40,8},{48,16},{56,24},{64,96... | collective-permute-start | bytes 245768 | tf_op jit(solution)/shard_map/sum_over_rows/ppermute | solution.py:29
  31.5 1.8 %collective-permute-start.11 = (bf16[80,512]{1,0:T(8,128)(2,1)S(1)}, bf16[80,512]{1,0:T(8,128)(2,1)S(1)}, u32[]{:S(2)}, u32[]{:S(2)}) collective-permute-start(bf16[80,512]{1,0:T(8,128)(2,1)S(1)} %get-tuple-element.79), channel_id=1, source_target_pairs={{0,24},{8,16},{16,8},{24,0},{32,56},{40,48},{48,40},{56,32},{64,88... | collective-permute-start | bytes 245768 | tf_op jit(solution)/shard_map/sum_over_rows/ppermute | solution.py:29
  33.3 1.3 %collective-permute-start.12 = (bf16[80,512]{1,0:T(8,128)(2,1)S(1)}, bf16[80,512]{1,0:T(8,128)(2,1)S(1)}, u32[]{:S(2)}, u32[]{:S(2)}) collective-permute-start(bf16[80,512]{1,0:T(8,128)(2,1)S(1)} %get-tuple-element.80), channel_id=1, source_target_pairs={{0,56},{8,48},{16,40},{24,32},{32,24},{40,16},{48,8},{56,0},{64,12... | collective-permute-start | bytes 245768 | tf_op jit(solution)/shard_map/sum_over_rows/ppermute | solution.py:29
  34.6 2.5 %collective-permute-done.11.refs_2_ = bf16[80,512]{1,0:T(8,128)(2,1)S(1)} collective-permute-done((bf16[80,512]{1,0:T(8,128)(2,1)S(1)}, bf16[80,512]{1,0:T(8,128)(2,1)S(1)}, u32[]{:S(2)}, u32[]{:S(2)}) %collective-permute-start.11) | collective-permute-done | bytes 81952 | tf_op jit(solution)/shard_map/sum_over_rows/ppermute | solution.py:29
  37.1 2.7 %collective-permute-done.12.refs_3_ = bf16[80,512]{1,0:T(8,128)(2,1)S(1)} collective-permute-done((bf16[80,512]{1,0:T(8,128)(2,1)S(1)}, bf16[80,512]{1,0:T(8,128)(2,1)S(1)}, u32[]{:S(2)}, u32[]{:S(2)}) %collective-permute-start.12) | collective-permute-done | bytes 81952 | tf_op jit(solution)/shard_map/sum_over_rows/ppermute | solution.py:29
  39.9 1.4 %second_product.2 = f32[16,2048]{1,0:T(8,128)S(1)} custom-call(bf16[32,2048]{1,0:T(8,128)(2,1)S(1)} %get-tuple-element.92.narrow_ref, bf16[512,1024]{1,0:T(8,128)(2,1)S(1)} %get-tuple-element.83.refs_0_, bf16[1024,1024]{1,0:T(8,128)(2,1)S(1)} %get-tuple-element.84.refs_1_, bf16[1536,512]{1,0:T(8,128)(2,1)S(1)} %get-tuple-element.85.refs_2_, ...), custom_call_target="tpu_custom_call" | custom-call | flops 134217728 | bytes 1024 | tf_op jit(solution)/shard_map/second_product/pallas_call | solution.py:231
  41.3 1.4 %second_product.3.mine_ref = f32[16,2048]{1,0:T(8,128)S(1)} custom-call(bf16[32,2048]{1,0:T(8,128)(2,1)S(1)} %get-tuple-element.92.narrow_ref, bf16[512,1024]{1,0:T(8,128)(2,1)S(1)} %get-tuple-element.83.refs_0_, bf16[1024,1024]{1,0:T(8,128)(2,1)S(1)} %get-tuple-element.84.refs_1_, bf16[1536,512]{1,0:T(8,128)(2,1)S(1)} %get-tuple-element.85.refs_2_, ...), custom_call_target="tpu_custom_call" | custom-call | flops 134217728 | bytes 1024 | tf_op jit(solution)/shard_map/second_product/pallas_call | solution.py:231
  42.8 2.3 %collective-permute-start.14 = (f32[16,512]{1,0:T(8,128)S(1)}, f32[16,512]{1,0:T(8,128)S(1)}, u32[]{:S(2)}, u32[]{:S(2)}) collective-permute-start(f32[16,512]{1,0:T(8,128)S(1)} %get-tuple-element.95), channel_id=1, source_target_pairs={{0,96},{8,104},{16,112},{24,120},{32,64},{40,72},{48,80},{56,88},{... | collective-permute-start | bytes 98312 | tf_op jit(solution)/shard_map/sum_over_columns/ppermute | solution.py:29
  45.1 2.5 %collective-permute-start.16 = (f32[16,512]{1,0:T(8,128)S(1)}, f32[16,512]{1,0:T(8,128)S(1)}, u32[]{:S(2)}, u32[]{:S(2)}) collective-permute-start(f32[16,512]{1,0:T(8,128)S(1)} %get-tuple-element.97), channel_id=1, source_target_pairs={{0,104},{8,96},{16,120},{24,112},{32,72},{40,64},{48,88},{56,80},{... | collective-permute-start | bytes 98312 | tf_op jit(solution)/shard_map/sum_over_columns/ppermute | solution.py:29
  48.0 1.0 %collective-permute-done.15.refs_2_ = f32[16,512]{1,0:T(8,128)S(1)} collective-permute-done((f32[16,512]{1,0:T(8,128)S(1)}, f32[16,512]{1,0:T(8,128)S(1)}, u32[]{:S(2)}, u32[]{:S(2)}) %collective-permute-start.15) | collective-permute-done | bytes 32800 | tf_op jit(solution)/shard_map/sum_over_columns/ppermute | solution.py:29
  49.0 2.1 %collective-permute-done.16.refs_3_ = f32[16,512]{1,0:T(8,128)S(1)} collective-permute-done((f32[16,512]{1,0:T(8,128)S(1)}, f32[16,512]{1,0:T(8,128)S(1)}, u32[]{:S(2)}, u32[]{:S(2)}) %collective-permute-start.16) | collective-permute-done | bytes 32800 | tf_op jit(solution)/shard_map/sum_over_columns/ppermute | solution.py:29
  51.4 12.2 %all_to_all.8 = f32[32,1,128]{2,1,0:T(1,128)S(1)} all-to-all(f32[32,1,128]{2,1,0:T(1,128)S(1)} %broadcast_in_dim.2), channel_id=1, replica_groups=mesh['y'=4,'z'=4,'c'=2,'x'=4] {'y','z','c'}, dimensions={0} | all-to-all | bytes 32768 | tf_op jit(solution)/shard_map/final_sums/all_to_all | solution.py:373
  63.6 1.0 %finish.1 = (f32[16,512]{1,0:T(8,128)}, f32[16,512]{1,0:T(8,128)}) custom-call(f32[16,512]{1,0:T(8,128)S(1)} %bitcast.12, f32[16,512]{1,0:T(8,128)S(1)} %get-tuple-element.81.rho_ref, f32[16,512]{1,0:T(8,128)S(1)} %get-tuple-element.98.image_ref, f32[32,128]{1,0:T(8,128)S(1)} %bitcast.13), custom_call_target="tpu_custom_call" | custom-call | tf_op jit(solution)/shard_map/finish/pallas_call | solution.py:305
  (29 shorter events, 2.4 us)
Async XLA Ops:
  0.6 1.5 %copy-start = (bf16[1024,256]{1,0:T(8,128)(2,1)S(1)}, bf16[1024,256]{1,0:T(8,128)(2,1)}, u32[]{:S(2)}) copy-start(bf16[1024,256]{1,0:T(8,128)(2,1)} %param.3) | copy-start | bytes 1572868
  2.5 8.5 %collective-permute-start.2 = (bf16[576,256]{1,0:T(8,128)(2,1)S(1)}, bf16[576,256]{1,0:T(8,128)(2,1)S(1)}, u32[]{:S(2)}, u32[]{:S(2)}) collective-permute-start(bf16[576,256]{1,0:T(8,128)(2,1)S(1)} %pack.1.refs_1_.refs_2_), channel_id=1, source_target_pairs={{0,4},{4,0},{1,5},{5,1},{2,6},{6,2},{3,7},{7,3},{8,12},{12,8},{9,1... | collective-permute-start | bytes 884744 | tf_op jit(solution)/shard_map/fetch_points/ppermute | solution.py:38
  2.6 16.6 %collective-permute-start.5 = (bf16[576,256]{1,0:T(8,128)(2,1)S(1)}, bf16[576,256]{1,0:T(8,128)(2,1)S(1)}, u32[]{:S(2)}, u32[]{:S(2)}) collective-permute-start(bf16[576,256]{1,0:T(8,128)(2,1)S(1)} %pack.1.refs_1_.refs_2_), channel_id=1, source_target_pairs={{0,8},{8,0},{16,24},{24,16},{32,40},{40,32},{48,56},{56,48},{64,72... | collective-permute-start | bytes 884744 | tf_op jit(solution)/shard_map/fetch_points/ppermute | solution.py:29
  4.6 9.6 %collective-permute-start.1 = (bf16[512,256]{1,0:T(8,128)(2,1)S(1)}, bf16[512,256]{1,0:T(8,128)(2,1)S(1)}, u32[]{:S(2)}, u32[]{:S(2)}) collective-permute-start(bf16[512,256]{1,0:T(8,128)(2,1)S(1)} %constant_dynamic-slice_fusion.points_ref.refs_0_), channel_id=1, source_target_pairs={{0,24},{8,16},{16,8},{24,0},{32,56},{40,48},{48,40},{56,32},{64,88... | collective-permute-start | bytes 786440 | tf_op jit(solution)/shard_map/fetch_points/ppermute | solution.py:29
  7.2 8.1 %collective-permute-start = (bf16[512,256]{1,0:T(8,128)(2,1)S(1)}, bf16[512,256]{1,0:T(8,128)(2,1)S(1)}, u32[]{:S(2)}, u32[]{:S(2)}) collective-permute-start(bf16[512,256]{1,0:T(8,128)(2,1)S(1)} %constant_dynamic-slice_fusion.points_ref.refs_0_), channel_id=1, source_target_pairs={{0,32},{8,40},{16,48},{24,56},{32,0},{40,8},{48,16},{56,24},{64,96... | collective-permute-start | bytes 786440 | tf_op jit(solution)/shard_map/fetch_points/ppermute | solution.py:29
  8.7 11.5 %collective-permute-start.4 = (bf16[576,256]{1,0:T(8,128)(2,1)S(1)}, bf16[576,256]{1,0:T(8,128)(2,1)S(1)}, u32[]{:S(2)}, u32[]{:S(2)}) collective-permute-start(bf16[576,256]{1,0:T(8,128)(2,1)S(1)} %pack.1.refs_1_.refs_2_), channel_id=1, source_target_pairs={{0,96},{8,104},{16,112},{24,120},{32,64},{40,72},{48,80},{56,88},{... | collective-permute-start | bytes 884744 | tf_op jit(solution)/shard_map/fetch_points/ppermute | solution.py:29
  10.9 15.7 %collective-permute-start.8 = (bf16[576,256]{1,0:T(8,128)(2,1)S(1)}, bf16[576,256]{1,0:T(8,128)(2,1)S(1)}, u32[]{:S(2)}, u32[]{:S(2)}) collective-permute-start(bf16[576,256]{1,0:T(8,128)(2,1)S(1)} %pack.1.refs_1_.refs_2_), channel_id=1, source_target_pairs={{0,104},{8,96},{16,120},{24,112},{32,72},{40,64},{48,88},{56,80},{... | collective-permute-start | bytes 884744 | tf_op jit(solution)/shard_map/fetch_points/ppermute | solution.py:29
  12.4 0.8 %copy-start.1 = (f32[512,16]{0,1:T(8,128)S(1)}, f32[512,16]{0,1:T(8,128)}, u32[]{:S(2)}) copy-start(f32[512,16]{0,1:T(8,128)} %param.5) | copy-start | bytes 98308
  15.3 9.3 %collective-permute-start.3 = (bf16[512,256]{1,0:T(8,128)(2,1)S(1)}, bf16[512,256]{1,0:T(8,128)(2,1)S(1)}, u32[]{:S(2)}, u32[]{:S(2)}) collective-permute-start(bf16[512,256]{1,0:T(8,128)(2,1)S(1)} %constant_dynamic-slice_fusion.points_ref.refs_0_), channel_id=1, source_target_pairs={{0,56},{8,48},{16,40},{24,32},{32,24},{40,16},{48,8},{56,0},{64,12... | collective-permute-start | bytes 786440 | tf_op jit(solution)/shard_map/fetch_points/ppermute | solution.py:29
  19.2 2.7 %collective-permute-start.7 = (bf16[576,256]{1,0:T(8,128)(2,1)S(1)}, bf16[576,256]{1,0:T(8,128)(2,1)S(1)}, u32[]{:S(2)}, u32[]{:S(2)}) collective-permute-start(bf16[576,256]{1,0:T(8,128)(2,1)S(1)} %collective-permute-done.5.refs_3_.refs_4_), channel_id=1, source_target_pairs={{0,4},{4,0},{1,5},{5,1},{2,6},{6,2},{3,7},{7,3},{8,12},{12,8},{9,1... | collective-permute-start | bytes 884744 | tf_op jit(solution)/shard_map/build_tiles/ppermute | solution.py:38
  20.3 2.7 %collective-permute-start.6 = (bf16[576,256]{1,0:T(8,128)(2,1)S(1)}, bf16[576,256]{1,0:T(8,128)(2,1)S(1)}, u32[]{:S(2)}, u32[]{:S(2)}) collective-permute-start(bf16[576,256]{1,0:T(8,128)(2,1)S(1)} %collective-permute-done.4.refs_3_), channel_id=1, source_target_pairs={{0,4},{4,0},{1,5},{5,1},{2,6},{6,2},{3,7},{7,3},{8,12},{12,8},{9,1... | collective-permute-start | bytes 884744 | tf_op jit(solution)/shard_map/build_tiles/ppermute | solution.py:38
  26.6 1.8 %collective-permute-start.9 = (bf16[576,256]{1,0:T(8,128)(2,1)S(1)}, bf16[576,256]{1,0:T(8,128)(2,1)S(1)}, u32[]{:S(2)}, u32[]{:S(2)}) collective-permute-start(bf16[576,256]{1,0:T(8,128)(2,1)S(1)} %collective-permute-done.8.refs_4_), channel_id=1, source_target_pairs={{0,4},{4,0},{1,5},{5,1},{2,6},{6,2},{3,7},{7,3},{8,12},{12,8},{9,1... | collective-permute-start | bytes 884744 | tf_op jit(solution)/shard_map/build_tiles/ppermute | solution.py:38
  29.8 4.8 %collective-permute-start.10 = (bf16[80,512]{1,0:T(8,128)(2,1)S(1)}, bf16[80,512]{1,0:T(8,128)(2,1)S(1)}, u32[]{:S(2)}, u32[]{:S(2)}) collective-permute-start(bf16[80,512]{1,0:T(8,128)(2,1)S(1)} %get-tuple-element.78), channel_id=1, source_target_pairs={{0,32},{8,40},{16,48},{24,56},{32,0},{40,8},{48,16},{56,24},{64,96... | collective-permute-start | bytes 245768 | tf_op jit(solution)/shard_map/sum_over_rows/ppermute | solution.py:29
  31.5 5.7 %collective-permute-start.11 = (bf16[80,512]{1,0:T(8,128)(2,1)S(1)}, bf16[80,512]{1,0:T(8,128)(2,1)S(1)}, u32[]{:S(2)}, u32[]{:S(2)}) collective-permute-start(bf16[80,512]{1,0:T(8,128)(2,1)S(1)} %get-tuple-element.79), channel_id=1, source_target_pairs={{0,24},{8,16},{16,8},{24,0},{32,56},{40,48},{48,40},{56,32},{64,88... | collective-permute-start | bytes 245768 | tf_op jit(solution)/shard_map/sum_over_rows/ppermute | solution.py:29
  33.3 6.6 %collective-permute-start.12 = (bf16[80,512]{1,0:T(8,128)(2,1)S(1)}, bf16[80,512]{1,0:T(8,128)(2,1)S(1)}, u32[]{:S(2)}, u32[]{:S(2)}) collective-permute-start(bf16[80,512]{1,0:T(8,128)(2,1)S(1)} %get-tuple-element.80), channel_id=1, source_target_pairs={{0,56},{8,48},{16,40},{24,32},{32,24},{40,16},{48,8},{56,0},{64,12... | collective-permute-start | bytes 245768 | tf_op jit(solution)/shard_map/sum_over_rows/ppermute | solution.py:29
  41.3 22.2 %copy-start.2 = (f32[512,16]{0,1:T(8,128)S(1)}, f32[512,16]{0,1:T(8,128)}, u32[]{:S(2)}) copy-start(f32[512,16]{0,1:T(8,128)} %param.5) | copy-start | bytes 98308
  41.3 1.5 %collective-permute-start.13 = (f32[16,2048]{1,0:T(8,128)S(1)}, f32[16,2048]{1,0:T(8,128)S(1)}, u32[]{:S(2)}, u32[]{:S(2)}) collective-permute-start(f32[16,2048]{1,0:T(8,128)S(1)} %second_product.2), channel_id=1, source_target_pairs={{0,4},{4,0},{1,5},{5,1},{2,6},{6,2},{3,7},{7,3},{8,12},{12,8},{9,1... | collective-permute-start | bytes 393224 | tf_op jit(solution)/shard_map/sum_over_columns/ppermute | solution.py:38
  42.8 5.2 %collective-permute-start.14 = (f32[16,512]{1,0:T(8,128)S(1)}, f32[16,512]{1,0:T(8,128)S(1)}, u32[]{:S(2)}, u32[]{:S(2)}) collective-permute-start(f32[16,512]{1,0:T(8,128)S(1)} %get-tuple-element.95), channel_id=1, source_target_pairs={{0,96},{8,104},{16,112},{24,120},{32,64},{40,72},{48,80},{56,88},{... | collective-permute-start | bytes 98312 | tf_op jit(solution)/shard_map/sum_over_columns/ppermute | solution.py:29
  45.1 3.9 %collective-permute-start.15 = (f32[16,512]{1,0:T(8,128)S(1)}, f32[16,512]{1,0:T(8,128)S(1)}, u32[]{:S(2)}, u32[]{:S(2)}) collective-permute-start(f32[16,512]{1,0:T(8,128)S(1)} %get-tuple-element.96), channel_id=1, source_target_pairs={{0,8},{8,0},{16,24},{24,16},{32,40},{40,32},{48,56},{56,48},{64,72... | collective-permute-start | bytes 98312 | tf_op jit(solution)/shard_map/sum_over_columns/ppermute | solution.py:29
  45.1 6.0 %collective-permute-start.16 = (f32[16,512]{1,0:T(8,128)S(1)}, f32[16,512]{1,0:T(8,128)S(1)}, u32[]{:S(2)}, u32[]{:S(2)}) collective-permute-start(f32[16,512]{1,0:T(8,128)S(1)} %get-tuple-element.97), channel_id=1, source_target_pairs={{0,104},{8,96},{16,120},{24,112},{32,72},{40,64},{48,88},{56,80},{... | collective-permute-start | bytes 98312 | tf_op jit(solution)/shard_map/sum_over_columns/ppermute | solution.py:29

commit v23 on v20

--- a/solution.py
+++ b/solution.py
@@ -10,6 +10,7 @@
 
 NY, NZ, NC, NX = 4, 4, 2, 4
 LANES = 128
+ALIGN = 16
 CHUNK = 256
 HERE = (0, 0)
 ROWS = (HERE, (1, 0), (0, 1), (1, 1))
@@ -45,11 +46,23 @@
     return high, middle, (rest - middle.astype(jnp.float32)).astype(jnp.bfloat16)
 
 
-def pack_kernel(points_ref, side_ref, out_ref):
+def front_kernel(offset_ref, states_ref, side_from, points_ref, out_ref, window_ref, side_ref, sems):
     own, width = points_ref.shape
     probes = side_ref.shape[0]
-    out_ref[:own, :] = points_ref[...]
-    high, middle, _ = split(points_ref[...].astype(jnp.float32) ** 2)
+    side_copy = pltpu.make_async_copy(side_from, side_ref, sems.at[0])
+    side_copy.start()
+    size = own + ALIGN
+    offset = offset_ref[0]
+    start = jnp.minimum(lax.div(offset, ALIGN) * ALIGN, states_ref.shape[0] - size)
+    window_from = states_ref.at[pl.ds(pl.multiple_of(start, ALIGN), size), :]
+    window_copy = pltpu.make_async_copy(window_from, window_ref, sems.at[1])
+    window_copy.start()
+    side_copy.wait()
+    window_copy.wait()
+    points = pltpu.roll(window_ref[...].astype(jnp.float32), lax.rem(size - (offset - start), size), 0)[:own]
+    points_ref[...] = points.astype(jnp.bfloat16)
+    out_ref[:own, :] = points.astype(jnp.bfloat16)
+    high, middle, _ = split(points**2)
     ones = jnp.ones((probes, width), jnp.bfloat16)
     norms = 0.0
     for term in (high, middle):
@@ -58,21 +71,35 @@
     row = lax.broadcasted_iota(jnp.int32, norms.shape, 0)
     norms = jnp.where(row == 0, high.astype(jnp.float32), jnp.where(row == 1, middle.astype(jnp.float32), low.astype(jnp.float32)))
     at = own
-    for part in (side_ref[...], norms.astype(jnp.bfloat16)):
+    for part in (side_ref[...].astype(jnp.bfloat16), norms.astype(jnp.bfloat16)):
         for j in range(own // width):
             out_ref[at : at + probes, :] = part[:, j * width : (j + 1) * width]
             at += probes
 
 
-def pack(points, side):
-    own, width = points.shape
-    extra = side.shape[0] * 2 * own // width
-    return pl.pallas_call(
-        pack_kernel,
-        out_shape=jax.ShapeDtypeStruct((own + extra, width), jnp.bfloat16),
+def front(states, offsets, side):
+    width = states.shape[1]
+    probes, own = side.shape
+    extra = probes * 2 * own // width
+    return pl.pallas_call(
+        front_kernel,
+        in_specs=[
+            pl.BlockSpec(memory_space=pltpu.SMEM),
+            pl.BlockSpec(memory_space=pltpu.HBM),
+            pl.BlockSpec(memory_space=pltpu.HBM),
+        ],
+        out_shape=[
+            jax.ShapeDtypeStruct((own, width), jnp.bfloat16),
+            jax.ShapeDtypeStruct((own + extra, width), jnp.bfloat16),
+        ],
+        scratch_shapes=[
+            pltpu.VMEM((own + ALIGN, width), jnp.bfloat16),
+            pltpu.VMEM((probes, own), jnp.float32),
+            pltpu.SemaphoreType.DMA((2,)),
+        ],
         compiler_params=pltpu.CompilerParams(vmem_limit_bytes=8 << 20),
-        name="pack",
-    )(points, side)
+        name="front",
+    )(offsets, states, side)
 
 
 def unpack_rows(message, probes, own, term):
@@ -313,9 +340,8 @@
 def on_device(states, offsets, right_side):
     own, probes = right_side.shape
     side = right_side.T
-    points = lax.dynamic_slice_in_dim(states, offsets[0], own, 0)
+    points, message = front(states, offsets, side)
     with jax.named_scope("fetch_points"):
-        message = pack(points, side.astype(jnp.bfloat16))
         rows = [points] + [swap(points, offset) for offset in ROWS[1:3]]
         cols = [message] + [swap(message, offset) for offset in SQUARE[1:]]
         first = [message, swap_core(message)]

time: 64.5 us -> 65.8 us (1.020)
  local copies, waits for them, and re-layouts: 0.85 us -> 1.81 us
  waiting for transfers between devices: 10.3 us -> 11.1 us
  other arithmetic: 0.76 us -> 0 us
    unnamed x6, local copies, waits for them, and re-layouts: 0.77 us -> 1.8 us
    convert_element_type x1 -> x0, other arithmetic: 0.76 us -> none  [on_device(): message = pack(points, side.astype(jnp.bfloat16))]
    ppermute x12, waiting for transfers between devices: 10.1 us -> 10.8 us  [swap(): return lax.ppermute(value, ('y', 'z'), pairs)]
where the time goes in v23:
time: 65.8 us; the launch traced here: 64.7 us
  starting transfers between devices  22.2 us (34%)
  Pallas kernels  16.2 us (25%)
  blocking collectives  12.1 us (18%)
  waiting for transfers between devices  11.1 us (17%)
  local copies, waits for them, and re-layouts  1.81 us (3%)
  between operations  1.36 us (2%)
    ppermute x12, starting transfers between devices, swap(): return lax.ppermute(value, ('y', 'z'), pairs)  21.3 us
    all_to_all x1, blocking collectives, on_device(): sums = lax.all_to_all(sums, ('y', 'z', 'c'), 0, 0, tiled=True)  12.1 us
    pallas_call x9, Pallas kernels, build(): pl.pallas_call(functools.partial(tile_kernel, counts, probes), out_shape=...  11.3 us
    ppermute x12, waiting for transfers between devices, swap(): return lax.ppermute(value, ('y', 'z'), pairs)  10.8 us
    pallas_call x2, Pallas kernels, second_product(): pl.pallas_call(functools.partial(second_kernel, own, half, places), in_sp...  2.87 us
    unnamed x6, local copies, waits for them, and re-layouts  1.8 us
  transfers between devices with their start and end apart: 17, of which 7 were waited for; matrix products, arithmetic and copies ran while one was open for 0% of the time, Pallas kernels for 18%

profile of v23, /device:TPU:0, one launch (start us, length us, event | category | flops | bytes accessed | tf_op | source)
XLA Modules:
  0.0 64.7 jit_solution(14815587558053271949)
XLA Ops:
  1.3 0.7 %copy-done = f32[512,16]{0,1:T(8,128)S(1)} copy-done((f32[512,16]{0,1:T(8,128)S(1)}, f32[512,16]{0,1:T(8,128)}, u32[]{:S(2)}) %copy-start) | copy-done | bytes 32792
  2.0 1.0 %copy-done.2 = bf16[1024,256]{1,0:T(8,128)(2,1)S(1)} copy-done((bf16[1024,256]{1,0:T(8,128)(2,1)S(1)}, bf16[1024,256]{1,0:T(8,128)(2,1)}, u32[]{:S(2)}) %copy-start.2) | copy-done | bytes 524312
  3.1 0.6 front.1
  3.8 4.2 %collective-permute-start.5 = (bf16[576,256]{1,0:T(8,128)(2,1)S(1)}, bf16[576,256]{1,0:T(8,128)(2,1)S(1)}, u32[]{:S(2)}, u32[]{:S(2)}) collective-permute-start(bf16[576,256]{1,0:T(8,128)(2,1)S(1)} %get-tuple-element.55.refs_1_.refs_2_), channel_id=1, source_target_pairs={{0,24},{8,16},{16,8},{24,0},{32,56},{40,48},{48,40},{56,32},{64,88... | collective-permute-start | bytes 884744 | tf_op jit(solution)/shard_map/fetch_points/ppermute | solution.py:30
  8.0 1.6 %collective-permute-start = (bf16[512,256]{1,0:T(8,128)(2,1)S(1)}, bf16[512,256]{1,0:T(8,128)(2,1)S(1)}, u32[]{:S(2)}, u32[]{:S(2)}) collective-permute-start(bf16[512,256]{1,0:T(8,128)(2,1)S(1)} %get-tuple-element.59.refs_0_), channel_id=1, source_target_pairs={{0,32},{8,40},{16,48},{24,56},{32,0},{40,8},{48,16},{56,24},{64,96... | collective-permute-start | bytes 786440 | tf_op jit(solution)/shard_map/fetch_points/ppermute | solution.py:30
  9.6 2.2 %collective-permute-start.4 = (bf16[576,256]{1,0:T(8,128)(2,1)S(1)}, bf16[576,256]{1,0:T(8,128)(2,1)S(1)}, u32[]{:S(2)}, u32[]{:S(2)}) collective-permute-start(bf16[576,256]{1,0:T(8,128)(2,1)S(1)} %get-tuple-element.55.refs_1_.refs_2_), channel_id=1, source_target_pairs={{0,96},{8,104},{16,112},{24,120},{32,64},{40,72},{48,80},{56,88},{... | collective-permute-start | bytes 884744 | tf_op jit(solution)/shard_map/fetch_points/ppermute | solution.py:30
  11.7 1.0 %collective-permute-start.8 = (bf16[576,256]{1,0:T(8,128)(2,1)S(1)}, bf16[576,256]{1,0:T(8,128)(2,1)S(1)}, u32[]{:S(2)}, u32[]{:S(2)}) collective-permute-start(bf16[576,256]{1,0:T(8,128)(2,1)S(1)} %get-tuple-element.55.refs_1_.refs_2_), channel_id=1, source_target_pairs={{0,120},{8,112},{16,104},{24,96},{32,88},{40,80},{48,72},{56,64},{... | collective-permute-start | bytes 884744 | tf_op jit(solution)/shard_map/fetch_points/ppermute | solution.py:30
  12.7 0.8 %build_tile.9 = (bf16[512,1024]{1,0:T(8,128)(2,1)S(1)}, f32[16,512]{1,0:T(8,128)S(1)}, f32[512,1]{1,0:T(8,128)S(1)}) custom-call(bf16[512,256]{1,0:T(8,128)(2,1)S(1)} %get-tuple-element.59.refs_0_, bf16[576,256]{1,0:T(8,128)(2,1)S(1)} %get-tuple-element.55.refs_1_.refs_2_, bf16[576,256]{1,0:T(8,128)(2,1)S(1)} %collective-permute-done.2.refs_2_.refs_3_, ...), custom_call_target="tpu_custom_call" | custom-call | flops 16777216 | bytes 1024 | tf_op jit(solution)/shard_map/fetch_points/build_tile/pallas_call | solution.py:172
  13.6 2.8 %collective-permute-done.1.refs_1_.refs_2_ = bf16[512,256]{1,0:T(8,128)(2,1)S(1)} collective-permute-done((bf16[512,256]{1,0:T(8,128)(2,1)S(1)}, bf16[512,256]{1,0:T(8,128)(2,1)S(1)}, u32[]{:S(2)}, u32[]{:S(2)}) %collective-permute-start.1) | collective-permute-done | bytes 262176 | tf_op jit(solution)/shard_map/fetch_points/ppermute | solution.py:30
  16.3 2.8 %collective-permute-start.3 = (bf16[512,256]{1,0:T(8,128)(2,1)S(1)}, bf16[512,256]{1,0:T(8,128)(2,1)S(1)}, u32[]{:S(2)}, u32[]{:S(2)}) collective-permute-start(bf16[512,256]{1,0:T(8,128)(2,1)S(1)} %get-tuple-element.59.refs_0_), channel_id=1, source_target_pairs={{0,40},{8,32},{16,56},{24,48},{32,8},{40,0},{48,24},{56,16},{64,10... | collective-permute-start | bytes 786440 | tf_op jit(solution)/shard_map/fetch_points/ppermute | solution.py:30
  19.1 1.4 %build_tile.10 = (bf16[1024,1024]{1,0:T(8,128)(2,1)S(1)}, f32[16,1024]{1,0:T(8,128)S(1)}, f32[1024,1]{1,0:T(8,128)S(1)}) custom-call(bf16[512,256]{1,0:T(8,128)(2,1)S(1)} %collective-permute-done.refs_0_.refs_1_, bf16[512,256]{1,0:T(8,128)(2,1)S(1)} %collective-permute-done.1.refs_1_.refs_2_, bf16[576,256]{1,0:T(8,128)(2,1)S(1)} %get-tuple-element.55.refs_1_.refs_2_, ...), custom_call_target="tpu_custom_call" | custom-call | flops 33554432 | bytes 1024 | tf_op jit(solution)/shard_map/fetch_points/build_tile/pallas_call | solution.py:172
  20.6 1.1 %build_tile.11 = (bf16[1536,512]{1,0:T(8,128)(2,1)S(1)}, f32[16,1536]{1,0:T(8,128)S(1)}) custom-call(bf16[512,256]{1,0:T(8,128)(2,1)S(1)} %get-tuple-element.59.refs_0_, bf16[512,256]{1,0:T(8,128)(2,1)S(1)} %collective-permute-done.refs_0_.refs_1_, bf16[512,256]{1,0:T(8,128)(2,1)S(1)} %collective-permute-done.1.refs_1_.refs_2_, ...), custom_call_target="tpu_custom_call" | custom-call | flops 1610612736 | bytes 1024 | tf_op jit(solution)/shard_map/build_tiles/build_tile/pallas_call | solution.py:172
  22.2 1.1 %build_tile.12 = (bf16[1536,512]{1,0:T(8,128)(2,1)S(1)}, f32[16,1536]{1,0:T(8,128)S(1)}) custom-call(bf16[512,256]{1,0:T(8,128)(2,1)S(1)} %get-tuple-element.59.refs_0_, bf16[512,256]{1,0:T(8,128)(2,1)S(1)} %collective-permute-done.refs_0_.refs_1_, bf16[512,256]{1,0:T(8,128)(2,1)S(1)} %collective-permute-done.1.refs_1_.refs_2_, ...), custom_call_target="tpu_custom_call" | custom-call | flops 1610612736 | bytes 1024 | tf_op jit(solution)/shard_map/build_tiles/build_tile/pallas_call | solution.py:172
  23.3 1.1 %build_tile.13 = (bf16[1536,512]{1,0:T(8,128)(2,1)S(1)}, f32[16,1536]{1,0:T(8,128)S(1)}) custom-call(bf16[512,256]{1,0:T(8,128)(2,1)S(1)} %get-tuple-element.59.refs_0_, bf16[512,256]{1,0:T(8,128)(2,1)S(1)} %collective-permute-done.refs_0_.refs_1_, bf16[512,256]{1,0:T(8,128)(2,1)S(1)} %collective-permute-done.1.refs_1_.refs_2_, ...), custom_call_target="tpu_custom_call" | custom-call | flops 1610612736 | bytes 1024 | tf_op jit(solution)/shard_map/build_tiles/build_tile/pallas_call | solution.py:172
  24.4 1.1 %build_tile.14 = (bf16[1536,512]{1,0:T(8,128)(2,1)S(1)}, f32[16,1536]{1,0:T(8,128)S(1)}) custom-call(bf16[512,256]{1,0:T(8,128)(2,1)S(1)} %get-tuple-element.59.refs_0_, bf16[512,256]{1,0:T(8,128)(2,1)S(1)} %collective-permute-done.refs_0_.refs_1_, bf16[512,256]{1,0:T(8,128)(2,1)S(1)} %collective-permute-done.1.refs_1_.refs_2_, ...), custom_call_target="tpu_custom_call" | custom-call | flops 1610612736 | bytes 1024 | tf_op jit(solution)/shard_map/build_tiles/build_tile/pallas_call | solution.py:172
  25.5 2.1 %build_tile.15 = (bf16[512,3072]{1,0:T(8,128)(2,1)S(1)}, f32[16,512]{1,0:T(8,128)S(1)}, f32[512,1]{1,0:T(8,128)S(1)}) custom-call(bf16[512,256]{1,0:T(8,128)(2,1)S(1)} %collective-permute-done.3.refs_0_.refs_3_, bf16[576,256]{1,0:T(8,128)(2,1)S(1)} %get-tuple-element.55.refs_1_.refs_2_, bf16[576,256]{1,0:T(8,128)(2,1)S(1)} %collective-permute-done.2.refs_2_.refs_3_, ...), custom_call_target="tpu_custom_call" | custom-call | flops 3221225472 | bytes 1024 | tf_op jit(solution)/shard_map/build_tiles/build_tile/pallas_call | solution.py:172
  27.8 1.3 %build_tile.16 = (bf16[2048,512]{1,0:T(8,128)(2,1)S(1)}, f32[16,2048]{1,0:T(8,128)S(1)}) custom-call(bf16[512,256]{1,0:T(8,128)(2,1)S(1)} %get-tuple-element.59.refs_0_, bf16[512,256]{1,0:T(8,128)(2,1)S(1)} %collective-permute-done.refs_0_.refs_1_, bf16[512,256]{1,0:T(8,128)(2,1)S(1)} %collective-permute-done.1.refs_1_.refs_2_, ...), custom_call_target="tpu_custom_call" | custom-call | flops 2147483648 | bytes 1024 | tf_op jit(solution)/shard_map/build_tiles/build_tile/pallas_call | solution.py:172
  29.4 1.3 %build_tile.17 = (bf16[2048,512]{1,0:T(8,128)(2,1)S(1)}, f32[16,2048]{1,0:T(8,128)S(1)}) custom-call(bf16[512,256]{1,0:T(8,128)(2,1)S(1)} %get-tuple-element.59.refs_0_, bf16[512,256]{1,0:T(8,128)(2,1)S(1)} %collective-permute-done.refs_0_.refs_1_, bf16[512,256]{1,0:T(8,128)(2,1)S(1)} %collective-permute-done.1.refs_1_.refs_2_, ...), custom_call_target="tpu_custom_call" | custom-call | flops 2147483648 | bytes 1024 | tf_op jit(solution)/shard_map/build_tiles/build_tile/pallas_call | solution.py:172
  30.8 0.9 %collective-permute-start.10 = (bf16[80,512]{1,0:T(8,128)(2,1)S(1)}, bf16[80,512]{1,0:T(8,128)(2,1)S(1)}, u32[]{:S(2)}, u32[]{:S(2)}) collective-permute-start(bf16[80,512]{1,0:T(8,128)(2,1)S(1)} %get-tuple-element.82), channel_id=1, source_target_pairs={{0,32},{8,40},{16,48},{24,56},{32,0},{40,8},{48,16},{56,24},{64,96... | collective-permute-start | bytes 245768 | tf_op jit(solution)/shard_map/sum_over_rows/ppermute | solution.py:30
  31.7 1.4 %collective-permute-start.11 = (bf16[80,512]{1,0:T(8,128)(2,1)S(1)}, bf16[80,512]{1,0:T(8,128)(2,1)S(1)}, u32[]{:S(2)}, u32[]{:S(2)}) collective-permute-start(bf16[80,512]{1,0:T(8,128)(2,1)S(1)} %get-tuple-element.83), channel_id=1, source_target_pairs={{0,8},{8,0},{16,24},{24,16},{32,40},{40,32},{48,56},{56,48},{64,72... | collective-permute-start | bytes 245768 | tf_op jit(solution)/shard_map/sum_over_rows/ppermute | solution.py:30
  33.1 1.2 %collective-permute-start.12 = (bf16[80,512]{1,0:T(8,128)(2,1)S(1)}, bf16[80,512]{1,0:T(8,128)(2,1)S(1)}, u32[]{:S(2)}, u32[]{:S(2)}) collective-permute-start(bf16[80,512]{1,0:T(8,128)(2,1)S(1)} %get-tuple-element.84), channel_id=1, source_target_pairs={{0,40},{8,32},{16,56},{24,48},{32,8},{40,0},{48,24},{56,16},{64,10... | collective-permute-start | bytes 245768 | tf_op jit(solution)/shard_map/sum_over_rows/ppermute | solution.py:30
  34.3 1.2 %collective-permute-done.10.refs_1_ = bf16[80,512]{1,0:T(8,128)(2,1)S(1)} collective-permute-done((bf16[80,512]{1,0:T(8,128)(2,1)S(1)}, bf16[80,512]{1,0:T(8,128)(2,1)S(1)}, u32[]{:S(2)}, u32[]{:S(2)}) %collective-permute-start.10) | collective-permute-done | bytes 81952 | tf_op jit(solution)/shard_map/sum_over_rows/ppermute | solution.py:30
  35.5 1.3 %collective-permute-done.11.refs_2_ = bf16[80,512]{1,0:T(8,128)(2,1)S(1)} collective-permute-done((bf16[80,512]{1,0:T(8,128)(2,1)S(1)}, bf16[80,512]{1,0:T(8,128)(2,1)S(1)}, u32[]{:S(2)}, u32[]{:S(2)}) %collective-permute-start.11) | collective-permute-done | bytes 81952 | tf_op jit(solution)/shard_map/sum_over_rows/ppermute | solution.py:30
  36.8 1.6 %collective-permute-done.12.refs_3_ = bf16[80,512]{1,0:T(8,128)(2,1)S(1)} collective-permute-done((bf16[80,512]{1,0:T(8,128)(2,1)S(1)}, bf16[80,512]{1,0:T(8,128)(2,1)S(1)}, u32[]{:S(2)}, u32[]{:S(2)}) %collective-permute-start.12) | collective-permute-done | bytes 81952 | tf_op jit(solution)/shard_map/sum_over_rows/ppermute | solution.py:30
  38.5 1.4 %second_product.2 = f32[16,2048]{1,0:T(8,128)S(1)} custom-call(bf16[32,2048]{1,0:T(8,128)(2,1)S(1)} %get-tuple-element.96.narrow_ref, bf16[512,1024]{1,0:T(8,128)(2,1)S(1)} %get-tuple-element.87.refs_0_, bf16[1024,1024]{1,0:T(8,128)(2,1)S(1)} %get-tuple-element.88.refs_1_, bf16[1536,512]{1,0:T(8,128)(2,1)S(1)} %get-tuple-element.89.refs_2_, ...), custom_call_target="tpu_custom_call" | custom-call | flops 134217728 | bytes 1024 | tf_op jit(solution)/shard_map/second_product/pallas_call | solution.py:258
  39.9 1.4 %second_product.3.mine_ref = f32[16,2048]{1,0:T(8,128)S(1)} custom-call(bf16[32,2048]{1,0:T(8,128)(2,1)S(1)} %get-tuple-element.96.narrow_ref, bf16[512,1024]{1,0:T(8,128)(2,1)S(1)} %get-tuple-element.87.refs_0_, bf16[1024,1024]{1,0:T(8,128)(2,1)S(1)} %get-tuple-element.88.refs_1_, bf16[1536,512]{1,0:T(8,128)(2,1)S(1)} %get-tuple-element.89.refs_2_, ...), custom_call_target="tpu_custom_call" | custom-call | flops 134217728 | bytes 1024 | tf_op jit(solution)/shard_map/second_product/pallas_call | solution.py:258
  41.4 2.3 %collective-permute-start.14 = (f32[16,512]{1,0:T(8,128)S(1)}, f32[16,512]{1,0:T(8,128)S(1)}, u32[]{:S(2)}, u32[]{:S(2)}) collective-permute-start(f32[16,512]{1,0:T(8,128)S(1)} %get-tuple-element.99), channel_id=1, source_target_pairs={{0,96},{8,104},{16,112},{24,120},{32,64},{40,72},{48,80},{56,88},{... | collective-permute-start | bytes 98312 | tf_op jit(solution)/shard_map/sum_over_columns/ppermute | solution.py:30
  44.1 3.3 %collective-permute-start.16 = (f32[16,512]{1,0:T(8,128)S(1)}, f32[16,512]{1,0:T(8,128)S(1)}, u32[]{:S(2)}, u32[]{:S(2)}) collective-permute-start(f32[16,512]{1,0:T(8,128)S(1)} %get-tuple-element.101), channel_id=1, source_target_pairs={{0,120},{8,112},{16,104},{24,96},{32,88},{40,80},{48,72},{56,64},{... | collective-permute-start | bytes 98312 | tf_op jit(solution)/shard_map/sum_over_columns/ppermute | solution.py:30
  47.4 1.4 %collective-permute-done.15.refs_2_ = f32[16,512]{1,0:T(8,128)S(1)} collective-permute-done((f32[16,512]{1,0:T(8,128)S(1)}, f32[16,512]{1,0:T(8,128)S(1)}, u32[]{:S(2)}, u32[]{:S(2)}) %collective-permute-start.15) | collective-permute-done | bytes 32800 | tf_op jit(solution)/shard_map/sum_over_columns/ppermute | solution.py:30
  48.8 2.6 %collective-permute-done.16.refs_3_ = f32[16,512]{1,0:T(8,128)S(1)} collective-permute-done((f32[16,512]{1,0:T(8,128)S(1)}, f32[16,512]{1,0:T(8,128)S(1)}, u32[]{:S(2)}, u32[]{:S(2)}) %collective-permute-start.16) | collective-permute-done | bytes 32800 | tf_op jit(solution)/shard_map/sum_over_columns/ppermute | solution.py:30
  51.6 12.1 %all_to_all.8 = f32[32,1,128]{2,1,0:T(1,128)S(1)} all-to-all(f32[32,1,128]{2,1,0:T(1,128)S(1)} %broadcast_in_dim.2), channel_id=1, replica_groups=mesh['y'=4,'z'=4,'c'=2,'x'=4] {'y','z','c'}, dimensions={0} | all-to-all | bytes 32768 | tf_op jit(solution)/shard_map/final_sums/all_to_all | solution.py:399
  63.7 1.0 %finish.1 = (f32[16,512]{1,0:T(8,128)}, f32[16,512]{1,0:T(8,128)}) custom-call(f32[16,512]{1,0:T(8,128)S(1)} %bitcast.8, f32[16,512]{1,0:T(8,128)S(1)} %get-tuple-element.85.rho_ref, f32[16,512]{1,0:T(8,128)S(1)} %get-tuple-element.102.image_ref, f32[32,128]{1,0:T(8,128)S(1)} %bitcast.9), custom_call_target="tpu_custom_call" | custom-call | tf_op jit(solution)/shard_map/finish/pallas_call | solution.py:332
  (27 shorter events, 2.1 us)
Async XLA Ops:
  1.3 0.8 %copy-start = (f32[512,16]{0,1:T(8,128)S(1)}, f32[512,16]{0,1:T(8,128)}, u32[]{:S(2)}) copy-start(f32[512,16]{0,1:T(8,128)} %param.5) | copy-start | bytes 98308
  2.0 1.0 %copy-start.2 = (bf16[1024,256]{1,0:T(8,128)(2,1)S(1)}, bf16[1024,256]{1,0:T(8,128)(2,1)}, u32[]{:S(2)}) copy-start(bf16[1024,256]{1,0:T(8,128)(2,1)} %states_ref.1) | copy-start | bytes 1572868
  3.7 8.1 %collective-permute-start.2 = (bf16[576,256]{1,0:T(8,128)(2,1)S(1)}, bf16[576,256]{1,0:T(8,128)(2,1)S(1)}, u32[]{:S(2)}, u32[]{:S(2)}) collective-permute-start(bf16[576,256]{1,0:T(8,128)(2,1)S(1)} %get-tuple-element.55.refs_1_.refs_2_), channel_id=1, source_target_pairs={{0,4},{4,0},{1,5},{5,1},{2,6},{6,2},{3,7},{7,3},{8,12},{12,8},{9,1... | collective-permute-start | bytes 884744 | tf_op jit(solution)/shard_map/fetch_points/ppermute | solution.py:39
  3.8 16.8 %collective-permute-start.5 = (bf16[576,256]{1,0:T(8,128)(2,1)S(1)}, bf16[576,256]{1,0:T(8,128)(2,1)S(1)}, u32[]{:S(2)}, u32[]{:S(2)}) collective-permute-start(bf16[576,256]{1,0:T(8,128)(2,1)S(1)} %get-tuple-element.55.refs_1_.refs_2_), channel_id=1, source_target_pairs={{0,24},{8,16},{16,8},{24,0},{32,56},{40,48},{48,40},{56,32},{64,88... | collective-permute-start | bytes 884744 | tf_op jit(solution)/shard_map/fetch_points/ppermute | solution.py:30
  8.0 8.4 %collective-permute-start.1 = (bf16[512,256]{1,0:T(8,128)(2,1)S(1)}, bf16[512,256]{1,0:T(8,128)(2,1)S(1)}, u32[]{:S(2)}, u32[]{:S(2)}) collective-permute-start(bf16[512,256]{1,0:T(8,128)(2,1)S(1)} %get-tuple-element.59.refs_0_), channel_id=1, source_target_pairs={{0,8},{8,0},{16,24},{24,16},{32,40},{40,32},{48,56},{56,48},{64,72... | collective-permute-start | bytes 786440 | tf_op jit(solution)/shard_map/fetch_points/ppermute | solution.py:30
  8.0 8.4 %collective-permute-start = (bf16[512,256]{1,0:T(8,128)(2,1)S(1)}, bf16[512,256]{1,0:T(8,128)(2,1)S(1)}, u32[]{:S(2)}, u32[]{:S(2)}) collective-permute-start(bf16[512,256]{1,0:T(8,128)(2,1)S(1)} %get-tuple-element.59.refs_0_), channel_id=1, source_target_pairs={{0,32},{8,40},{16,48},{24,56},{32,0},{40,8},{48,16},{56,24},{64,96... | collective-permute-start | bytes 786440 | tf_op jit(solution)/shard_map/fetch_points/ppermute | solution.py:30
  9.6 12.1 %collective-permute-start.4 = (bf16[576,256]{1,0:T(8,128)(2,1)S(1)}, bf16[576,256]{1,0:T(8,128)(2,1)S(1)}, u32[]{:S(2)}, u32[]{:S(2)}) collective-permute-start(bf16[576,256]{1,0:T(8,128)(2,1)S(1)} %get-tuple-element.55.refs_1_.refs_2_), channel_id=1, source_target_pairs={{0,96},{8,104},{16,112},{24,120},{32,64},{40,72},{48,80},{56,88},{... | collective-permute-start | bytes 884744 | tf_op jit(solution)/shard_map/fetch_points/ppermute | solution.py:30
  11.7 15.8 %collective-permute-start.8 = (bf16[576,256]{1,0:T(8,128)(2,1)S(1)}, bf16[576,256]{1,0:T(8,128)(2,1)S(1)}, u32[]{:S(2)}, u32[]{:S(2)}) collective-permute-start(bf16[576,256]{1,0:T(8,128)(2,1)S(1)} %get-tuple-element.55.refs_1_.refs_2_), channel_id=1, source_target_pairs={{0,120},{8,112},{16,104},{24,96},{32,88},{40,80},{48,72},{56,64},{... | collective-permute-start | bytes 884744 | tf_op jit(solution)/shard_map/fetch_points/ppermute | solution.py:30
  16.3 9.1 %collective-permute-start.3 = (bf16[512,256]{1,0:T(8,128)(2,1)S(1)}, bf16[512,256]{1,0:T(8,128)(2,1)S(1)}, u32[]{:S(2)}, u32[]{:S(2)}) collective-permute-start(bf16[512,256]{1,0:T(8,128)(2,1)S(1)} %get-tuple-element.59.refs_0_), channel_id=1, source_target_pairs={{0,40},{8,32},{16,56},{24,48},{32,8},{40,0},{48,24},{56,16},{64,10... | collective-permute-start | bytes 786440 | tf_op jit(solution)/shard_map/fetch_points/ppermute | solution.py:30
  20.5 2.7 %collective-permute-start.7 = (bf16[576,256]{1,0:T(8,128)(2,1)S(1)}, bf16[576,256]{1,0:T(8,128)(2,1)S(1)}, u32[]{:S(2)}, u32[]{:S(2)}) collective-permute-start(bf16[576,256]{1,0:T(8,128)(2,1)S(1)} %collective-permute-done.5.refs_3_.refs_4_), channel_id=1, source_target_pairs={{0,4},{4,0},{1,5},{5,1},{2,6},{6,2},{3,7},{7,3},{8,12},{12,8},{9,1... | collective-permute-start | bytes 884744 | tf_op jit(solution)/shard_map/build_tiles/ppermute | solution.py:39
  21.6 2.7 %collective-permute-start.6 = (bf16[576,256]{1,0:T(8,128)(2,1)S(1)}, bf16[576,256]{1,0:T(8,128)(2,1)S(1)}, u32[]{:S(2)}, u32[]{:S(2)}) collective-permute-start(bf16[576,256]{1,0:T(8,128)(2,1)S(1)} %collective-permute-done.4.refs_3_), channel_id=1, source_target_pairs={{0,4},{4,0},{1,5},{5,1},{2,6},{6,2},{3,7},{7,3},{8,12},{12,8},{9,1... | collective-permute-start | bytes 884744 | tf_op jit(solution)/shard_map/build_tiles/ppermute | solution.py:39
  27.6 1.8 %collective-permute-start.9 = (bf16[576,256]{1,0:T(8,128)(2,1)S(1)}, bf16[576,256]{1,0:T(8,128)(2,1)S(1)}, u32[]{:S(2)}, u32[]{:S(2)}) collective-permute-start(bf16[576,256]{1,0:T(8,128)(2,1)S(1)} %collective-permute-done.8.refs_4_), channel_id=1, source_target_pairs={{0,4},{4,0},{1,5},{5,1},{2,6},{6,2},{3,7},{7,3},{8,12},{12,8},{9,1... | collective-permute-start | bytes 884744 | tf_op jit(solution)/shard_map/build_tiles/ppermute | solution.py:39
  30.8 4.8 %collective-permute-start.10 = (bf16[80,512]{1,0:T(8,128)(2,1)S(1)}, bf16[80,512]{1,0:T(8,128)(2,1)S(1)}, u32[]{:S(2)}, u32[]{:S(2)}) collective-permute-start(bf16[80,512]{1,0:T(8,128)(2,1)S(1)} %get-tuple-element.82), channel_id=1, source_target_pairs={{0,32},{8,40},{16,48},{24,56},{32,0},{40,8},{48,16},{56,24},{64,96... | collective-permute-start | bytes 245768 | tf_op jit(solution)/shard_map/sum_over_rows/ppermute | solution.py:30
  31.7 5.2 %collective-permute-start.11 = (bf16[80,512]{1,0:T(8,128)(2,1)S(1)}, bf16[80,512]{1,0:T(8,128)(2,1)S(1)}, u32[]{:S(2)}, u32[]{:S(2)}) collective-permute-start(bf16[80,512]{1,0:T(8,128)(2,1)S(1)} %get-tuple-element.83), channel_id=1, source_target_pairs={{0,8},{8,0},{16,24},{24,16},{32,40},{40,32},{48,56},{56,48},{64,72... | collective-permute-start | bytes 245768 | tf_op jit(solution)/shard_map/sum_over_rows/ppermute | solution.py:30
  33.1 5.3 %collective-permute-start.12 = (bf16[80,512]{1,0:T(8,128)(2,1)S(1)}, bf16[80,512]{1,0:T(8,128)(2,1)S(1)}, u32[]{:S(2)}, u32[]{:S(2)}) collective-permute-start(bf16[80,512]{1,0:T(8,128)(2,1)S(1)} %get-tuple-element.84), channel_id=1, source_target_pairs={{0,40},{8,32},{16,56},{24,48},{32,8},{40,0},{48,24},{56,16},{64,10... | collective-permute-start | bytes 245768 | tf_op jit(solution)/shard_map/sum_over_rows/ppermute | solution.py:30
  39.9 11.5 %copy-start.1 = (f32[512,16]{0,1:T(8,128)S(1)}, f32[512,16]{0,1:T(8,128)}, u32[]{:S(2)}) copy-start(f32[512,16]{0,1:T(8,128)} %param.5) | copy-start | bytes 98308
  39.9 1.5 %collective-permute-start.13 = (f32[16,2048]{1,0:T(8,128)S(1)}, f32[16,2048]{1,0:T(8,128)S(1)}, u32[]{:S(2)}, u32[]{:S(2)}) collective-permute-start(f32[16,2048]{1,0:T(8,128)S(1)} %second_product.2), channel_id=1, source_target_pairs={{0,4},{4,0},{1,5},{5,1},{2,6},{6,2},{3,7},{7,3},{8,12},{12,8},{9,1... | collective-permute-start | bytes 393224 | tf_op jit(solution)/shard_map/sum_over_columns/ppermute | solution.py:39
  41.4 6.0 %collective-permute-start.14 = (f32[16,512]{1,0:T(8,128)S(1)}, f32[16,512]{1,0:T(8,128)S(1)}, u32[]{:S(2)}, u32[]{:S(2)}) collective-permute-start(f32[16,512]{1,0:T(8,128)S(1)} %get-tuple-element.99), channel_id=1, source_target_pairs={{0,96},{8,104},{16,112},{24,120},{32,64},{40,72},{48,80},{56,88},{... | collective-permute-start | bytes 98312 | tf_op jit(solution)/shard_map/sum_over_columns/ppermute | solution.py:30
  43.7 5.1 %collective-permute-start.15 = (f32[16,512]{1,0:T(8,128)S(1)}, f32[16,512]{1,0:T(8,128)S(1)}, u32[]{:S(2)}, u32[]{:S(2)}) collective-permute-start(f32[16,512]{1,0:T(8,128)S(1)} %get-tuple-element.100), channel_id=1, source_target_pairs={{0,24},{8,16},{16,8},{24,0},{32,56},{40,48},{48,40},{56,32},{64,88... | collective-permute-start | bytes 98312 | tf_op jit(solution)/shard_map/sum_over_columns/ppermute | solution.py:30
  44.1 7.2 %collective-permute-start.16 = (f32[16,512]{1,0:T(8,128)S(1)}, f32[16,512]{1,0:T(8,128)S(1)}, u32[]{:S(2)}, u32[]{:S(2)}) collective-permute-start(f32[16,512]{1,0:T(8,128)S(1)} %get-tuple-element.101), channel_id=1, source_target_pairs={{0,120},{8,112},{16,104},{24,96},{32,88},{40,80},{48,72},{56,64},{... | collective-permute-start | bytes 98312 | tf_op jit(solution)/shard_map/sum_over_columns/ppermute | solution.py:30

commit v24 on v21

--- a/solution.py
+++ b/solution.py
@@ -32,6 +32,16 @@
 def swap_each(values, offsets):
     received = [swap(value, offset) for value, offset in reversed(list(zip(values, offsets)))]
     return received[::-1]
+
+
+def hand_on(along_y, along_z, offset):
+    value = jnp.where(lax.axis_index("c") == 0, along_z, along_y)
+    pairs = []
+    for y in range(NY):
+        for z in range(NZ):
+            here = (y * NZ + z) * NC
+            pairs += [(here, ((y ^ offset[0]) * NZ + z) * NC), (here + 1, (y * NZ + (z ^ offset[1])) * NC + 1)]
+    return lax.ppermute(value, ("y", "z", "c"), pairs)
 
 
 def swap_core(value):
@@ -321,10 +331,9 @@
         first = [message, swap_core(message)]
         tile_a, image_a, half_a = build([points], first, own, probes, side=side, weight=1)
         (rows[1], rows[2]), image_a = lax.optimization_barrier(((rows[1], rows[2]), image_a))
+        rows.append(hand_on(rows[1], rows[2], ROWS[3]))
         tile_b, image_b, half_b = build(rows[1:3], first, own, probes, weight=1)
         half = [half_a, half_b]
-        again, image_b = lax.optimization_barrier((points, image_b))
-        rows.append(swap(again, ROWS[3]))
 
     with jax.named_scope("build_tiles"):
         cols[2], image_b = lax.optimization_barrier((cols[2], image_b))

time: 66 us -> 68 us (1.030)
  waiting for transfers between devices: 11.8 us -> 16.8 us
  blocking collectives: 12.1 us -> 10.3 us
  starting transfers between devices: 22.2 us -> 20.8 us
    ppermute x12 -> x11, waiting for transfers between devices: 11.6 us -> 16.7 us  [swap(): return lax.ppermute(value, ('y', 'z'), pairs)]
    ppermute x12 -> x11, starting transfers between devices: 21.3 us -> 19.1 us  [swap(): return lax.ppermute(value, ('y', 'z'), pairs)]
    all_to_all x1, blocking collectives: 12.1 us -> 10.3 us  [on_device(): sums = lax.all_to_all(sums, ('y', 'z', 'c'), 0, 0, tiled=True)]
    ppermute x0 -> x1, starting transfers between devices: none -> 0.89 us  [hand_on(): return lax.ppermute(value, ('y', 'z', 'c'), pairs)]
  transfers between devices with their start and end apart: 17 -> 17, of which waited for: 8 -> 6; matrix products, arithmetic and copies ran while one was open for 0% -> 0% of each run, Pallas kernels for 18% -> 17%
where the time goes in v24:
time: 68 us; the launch traced here: 66.9 us
  starting transfers between devices  20.8 us (31%)
  waiting for transfers between devices  16.8 us (25%)
  Pallas kernels  15.9 us (23%)
  blocking collectives  10.3 us (15%)
  between operations  1.44 us (2%)
  local copies, waits for them, and re-layouts  0.85 us (1%)
  other arithmetic  0.8 us (1%)
    ppermute x11, starting transfers between devices, swap(): return lax.ppermute(value, ('y', 'z'), pairs)  19.1 us
    ppermute x11, waiting for transfers between devices, swap(): return lax.ppermute(value, ('y', 'z'), pairs)  16.7 us
    pallas_call x9, Pallas kernels, build(): pl.pallas_call(functools.partial(tile_kernel, counts, probes), out_shape=...  11.4 us
    all_to_all x1, blocking collectives, on_device(): sums = lax.all_to_all(sums, ('y', 'z', 'c'), 0, 0, tiled=True)  10.3 us
    pallas_call x2, Pallas kernels, second_product(): pl.pallas_call(functools.partial(second_kernel, own, half, places), in_sp...  2.87 us
  transfers between devices with their start and end apart: 17, of which 6 were waited for; matrix products, arithmetic and copies ran while one was open for 0% of the time, Pallas kernels for 17%

profile of v24, /device:TPU:0, one launch (start us, length us, event | category | flops | bytes accessed | tf_op | source)
XLA Modules:
  0.0 66.9 jit_solution(2676729359553881502)
XLA Ops:
  1.3 0.8 %bitcast_convert_fusion.side_ref = bf16[16,512]{1,0:T(8,128)(2,1)S(1)} fusion(f32[512,16]{0,1:T(8,128)} %param.5), kind=kLoop, calls=%fused_computation.2 | loop fusion | flops 8192 | bytes 49152 | tf_op jit(solution)/shard_map/fetch_points/convert_element_type | solution.py:328
  2.6 2.1 %collective-permute-start.1 = (bf16[512,256]{1,0:T(8,128)(2,1)S(1)}, bf16[512,256]{1,0:T(8,128)(2,1)S(1)}, u32[]{:S(2)}, u32[]{:S(2)}) collective-permute-start(bf16[512,256]{1,0:T(8,128)(2,1)S(1)} %constant_dynamic-slice_fusion.points_ref.refs_0_), channel_id=1, source_target_pairs={{0,8},{8,0},{16,24},{24,16},{32,40},{40,32},{48,56},{56,48},{64,72... | collective-permute-start | bytes 786440 | tf_op jit(solution)/shard_map/fetch_points/ppermute | solution.py:29
  4.6 1.6 %collective-permute-start = (bf16[512,256]{1,0:T(8,128)(2,1)S(1)}, bf16[512,256]{1,0:T(8,128)(2,1)S(1)}, u32[]{:S(2)}, u32[]{:S(2)}) collective-permute-start(bf16[512,256]{1,0:T(8,128)(2,1)S(1)} %constant_dynamic-slice_fusion.points_ref.refs_0_), channel_id=1, source_target_pairs={{0,32},{8,40},{16,48},{24,56},{32,0},{40,8},{48,16},{56,24},{64,96... | collective-permute-start | bytes 786440 | tf_op jit(solution)/shard_map/fetch_points/ppermute | solution.py:29
  6.2 2.5 %collective-permute-start.5 = (bf16[576,256]{1,0:T(8,128)(2,1)S(1)}, bf16[576,256]{1,0:T(8,128)(2,1)S(1)}, u32[]{:S(2)}, u32[]{:S(2)}) collective-permute-start(bf16[576,256]{1,0:T(8,128)(2,1)S(1)} %pack.1.refs_1_.refs_2_), channel_id=1, source_target_pairs={{0,24},{8,16},{16,8},{24,0},{32,56},{40,48},{48,40},{56,32},{64,88... | collective-permute-start | bytes 884744 | tf_op jit(solution)/shard_map/fetch_points/ppermute | solution.py:29
  8.7 2.3 %collective-permute-start.8 = (bf16[576,256]{1,0:T(8,128)(2,1)S(1)}, bf16[576,256]{1,0:T(8,128)(2,1)S(1)}, u32[]{:S(2)}, u32[]{:S(2)}) collective-permute-start(bf16[576,256]{1,0:T(8,128)(2,1)S(1)} %pack.1.refs_1_.refs_2_), channel_id=1, source_target_pairs={{0,120},{8,112},{16,104},{24,96},{32,88},{40,80},{48,72},{56,64},{... | collective-permute-start | bytes 884744 | tf_op jit(solution)/shard_map/fetch_points/ppermute | solution.py:29
  11.1 1.1 %collective-permute-start.4 = (bf16[576,256]{1,0:T(8,128)(2,1)S(1)}, bf16[576,256]{1,0:T(8,128)(2,1)S(1)}, u32[]{:S(2)}, u32[]{:S(2)}) collective-permute-start(bf16[576,256]{1,0:T(8,128)(2,1)S(1)} %pack.1.refs_1_.refs_2_), channel_id=1, source_target_pairs={{0,96},{8,104},{16,112},{24,120},{32,64},{40,72},{48,80},{56,88},{... | collective-permute-start | bytes 884744 | tf_op jit(solution)/shard_map/fetch_points/ppermute | solution.py:29
  12.1 0.8 %copy-done.1 = f32[512,16]{0,1:T(8,128)S(1)} copy-done((f32[512,16]{0,1:T(8,128)S(1)}, f32[512,16]{0,1:T(8,128)}, u32[]{:S(2)}) %copy-start.1) | copy-done | bytes 32792
  12.9 0.8 %build_tile.9 = (bf16[512,1024]{1,0:T(8,128)(2,1)S(1)}, f32[16,512]{1,0:T(8,128)S(1)}, f32[512,1]{1,0:T(8,128)S(1)}) custom-call(bf16[512,256]{1,0:T(8,128)(2,1)S(1)} %constant_dynamic-slice_fusion.points_ref.refs_0_, bf16[576,256]{1,0:T(8,128)(2,1)S(1)} %pack.1.refs_1_.refs_2_, bf16[576,256]{1,0:T(8,128)(2,1)S(1)} %collective-permute-done.2.refs_2_.refs_3_, ...), custom_call_target="tpu_custom_call" | custom-call | flops 16777216 | bytes 1024 | tf_op jit(solution)/shard_map/fetch_points/build_tile/pallas_call | solution.py:155
  13.8 0.9 %collective-permute-start.3 = (bf16[512,256]{1,0:T(8,128)(2,1)S(1)}, bf16[512,256]{1,0:T(8,128)(2,1)S(1)}, u32[]{:S(2)}, u32[]{:S(2)}) collective-permute-start(bf16[512,256]{1,0:T(8,128)(2,1)S(1)} %broadcast_select_fusion), channel_id=1, source_target_pairs={{0,32},{4,12},{8,40},{12,4},{16,48},{20,28},{24,56},{28,20},{32,0}... | collective-permute-start | bytes 786440 | tf_op jit(solution)/shard_map/fetch_points/ppermute | solution.py:44
  14.7 1.4 %build_tile.10 = (bf16[1024,1024]{1,0:T(8,128)(2,1)S(1)}, f32[16,1024]{1,0:T(8,128)S(1)}, f32[1024,1]{1,0:T(8,128)S(1)}) custom-call(bf16[512,256]{1,0:T(8,128)(2,1)S(1)} %collective-permute-done.refs_0_.refs_1_, bf16[512,256]{1,0:T(8,128)(2,1)S(1)} %collective-permute-done.1.refs_1_.refs_2_, bf16[576,256]{1,0:T(8,128)(2,1)S(1)} %pack.1.refs_1_.refs_2_, ...), custom_call_target="tpu_custom_call" | custom-call | flops 33554432 | bytes 1024 | tf_op jit(solution)/shard_map/fetch_points/build_tile/pallas_call | solution.py:155
  16.1 6.4 %collective-permute-done.5.refs_3_.refs_4_ = bf16[576,256]{1,0:T(8,128)(2,1)S(1)} collective-permute-done((bf16[576,256]{1,0:T(8,128)(2,1)S(1)}, bf16[576,256]{1,0:T(8,128)(2,1)S(1)}, u32[]{:S(2)}, u32[]{:S(2)}) %collective-permute-start.5) | collective-permute-done | bytes 294944 | tf_op jit(solution)/shard_map/fetch_points/ppermute | solution.py:29
  22.5 1.1 %build_tile.11 = (bf16[1536,512]{1,0:T(8,128)(2,1)S(1)}, f32[16,1536]{1,0:T(8,128)S(1)}) custom-call(bf16[512,256]{1,0:T(8,128)(2,1)S(1)} %constant_dynamic-slice_fusion.points_ref.refs_0_, bf16[512,256]{1,0:T(8,128)(2,1)S(1)} %collective-permute-done.refs_0_.refs_1_, bf16[512,256]{1,0:T(8,128)(2,1)S(1)} %collective-permute-done.1.refs_1_.refs_2_, ...), custom_call_target="tpu_custom_call" | custom-call | flops 1610612736 | bytes 1024 | tf_op jit(solution)/shard_map/build_tiles/build_tile/pallas_call | solution.py:155
  23.6 1.4 %collective-permute-done.4.refs_3_ = bf16[576,256]{1,0:T(8,128)(2,1)S(1)} collective-permute-done((bf16[576,256]{1,0:T(8,128)(2,1)S(1)}, bf16[576,256]{1,0:T(8,128)(2,1)S(1)}, u32[]{:S(2)}, u32[]{:S(2)}) %collective-permute-start.4) | collective-permute-done | bytes 294944 | tf_op jit(solution)/shard_map/fetch_points/ppermute | solution.py:29
  25.0 1.1 %build_tile.12 = (bf16[1536,512]{1,0:T(8,128)(2,1)S(1)}, f32[16,1536]{1,0:T(8,128)S(1)}) custom-call(bf16[512,256]{1,0:T(8,128)(2,1)S(1)} %constant_dynamic-slice_fusion.points_ref.refs_0_, bf16[512,256]{1,0:T(8,128)(2,1)S(1)} %collective-permute-done.refs_0_.refs_1_, bf16[512,256]{1,0:T(8,128)(2,1)S(1)} %collective-permute-done.1.refs_1_.refs_2_, ...), custom_call_target="tpu_custom_call" | custom-call | flops 1610612736 | bytes 1024 | tf_op jit(solution)/shard_map/build_tiles/build_tile/pallas_call | solution.py:155
  26.0 1.1 %build_tile.13 = (bf16[1536,512]{1,0:T(8,128)(2,1)S(1)}, f32[16,1536]{1,0:T(8,128)S(1)}) custom-call(bf16[512,256]{1,0:T(8,128)(2,1)S(1)} %constant_dynamic-slice_fusion.points_ref.refs_0_, bf16[512,256]{1,0:T(8,128)(2,1)S(1)} %collective-permute-done.refs_0_.refs_1_, bf16[512,256]{1,0:T(8,128)(2,1)S(1)} %collective-permute-done.1.refs_1_.refs_2_, ...), custom_call_target="tpu_custom_call" | custom-call | flops 1610612736 | bytes 1024 | tf_op jit(solution)/shard_map/build_tiles/build_tile/pallas_call | solution.py:155
  27.1 1.1 %build_tile.14 = (bf16[1536,512]{1,0:T(8,128)(2,1)S(1)}, f32[16,1536]{1,0:T(8,128)S(1)}) custom-call(bf16[512,256]{1,0:T(8,128)(2,1)S(1)} %constant_dynamic-slice_fusion.points_ref.refs_0_, bf16[512,256]{1,0:T(8,128)(2,1)S(1)} %collective-permute-done.refs_0_.refs_1_, bf16[512,256]{1,0:T(8,128)(2,1)S(1)} %collective-permute-done.1.refs_1_.refs_2_, ...), custom_call_target="tpu_custom_call" | custom-call | flops 1610612736 | bytes 1024 | tf_op jit(solution)/shard_map/build_tiles/build_tile/pallas_call | solution.py:155
  28.3 2.1 %build_tile.15 = (bf16[512,3072]{1,0:T(8,128)(2,1)S(1)}, f32[16,512]{1,0:T(8,128)S(1)}, f32[512,1]{1,0:T(8,128)S(1)}) custom-call(bf16[512,256]{1,0:T(8,128)(2,1)S(1)} %collective-permute-done.3.refs_0_.refs_3_, bf16[576,256]{1,0:T(8,128)(2,1)S(1)} %pack.1.refs_1_.refs_2_, bf16[576,256]{1,0:T(8,128)(2,1)S(1)} %collective-permute-done.2.refs_2_.refs_3_, ...), custom_call_target="tpu_custom_call" | custom-call | flops 3221225472 | bytes 1024 | tf_op jit(solution)/shard_map/build_tiles/build_tile/pallas_call | solution.py:155
  31.1 1.3 %build_tile.16 = (bf16[2048,512]{1,0:T(8,128)(2,1)S(1)}, f32[16,2048]{1,0:T(8,128)S(1)}) custom-call(bf16[512,256]{1,0:T(8,128)(2,1)S(1)} %constant_dynamic-slice_fusion.points_ref.refs_0_, bf16[512,256]{1,0:T(8,128)(2,1)S(1)} %collective-permute-done.refs_0_.refs_1_, bf16[512,256]{1,0:T(8,128)(2,1)S(1)} %collective-permute-done.1.refs_1_.refs_2_, ...), custom_call_target="tpu_custom_call" | custom-call | flops 2147483648 | bytes 1024 | tf_op jit(solution)/shard_map/build_tiles/build_tile/pallas_call | solution.py:155
  32.4 1.4 %build_tile.17 = (bf16[2048,512]{1,0:T(8,128)(2,1)S(1)}, f32[16,2048]{1,0:T(8,128)S(1)}) custom-call(bf16[512,256]{1,0:T(8,128)(2,1)S(1)} %constant_dynamic-slice_fusion.points_ref.refs_0_, bf16[512,256]{1,0:T(8,128)(2,1)S(1)} %collective-permute-done.refs_0_.refs_1_, bf16[512,256]{1,0:T(8,128)(2,1)S(1)} %collective-permute-done.1.refs_1_.refs_2_, ...), custom_call_target="tpu_custom_call" | custom-call | flops 2147483648 | bytes 1024 | tf_op jit(solution)/shard_map/build_tiles/build_tile/pallas_call | solution.py:155
  33.9 0.8 %collective-permute-start.11 = (bf16[80,512]{1,0:T(8,128)(2,1)S(1)}, bf16[80,512]{1,0:T(8,128)(2,1)S(1)}, u32[]{:S(2)}, u32[]{:S(2)}) collective-permute-start(bf16[80,512]{1,0:T(8,128)(2,1)S(1)} %get-tuple-element.77), channel_id=1, source_target_pairs={{0,8},{8,0},{16,24},{24,16},{32,40},{40,32},{48,56},{56,48},{64,72... | collective-permute-start | bytes 245768 | tf_op jit(solution)/shard_map/sum_over_rows/ppermute | solution.py:29
  34.7 2.7 %collective-permute-start.12 = (bf16[80,512]{1,0:T(8,128)(2,1)S(1)}, bf16[80,512]{1,0:T(8,128)(2,1)S(1)}, u32[]{:S(2)}, u32[]{:S(2)}) collective-permute-start(bf16[80,512]{1,0:T(8,128)(2,1)S(1)} %get-tuple-element.78), channel_id=1, source_target_pairs={{0,40},{8,32},{16,56},{24,48},{32,8},{40,0},{48,24},{56,16},{64,10... | collective-permute-start | bytes 245768 | tf_op jit(solution)/shard_map/sum_over_rows/ppermute | solution.py:29
  37.4 1.6 %collective-permute-done.10.refs_1_ = bf16[80,512]{1,0:T(8,128)(2,1)S(1)} collective-permute-done((bf16[80,512]{1,0:T(8,128)(2,1)S(1)}, bf16[80,512]{1,0:T(8,128)(2,1)S(1)}, u32[]{:S(2)}, u32[]{:S(2)}) %collective-permute-start.10) | collective-permute-done | bytes 81952 | tf_op jit(solution)/shard_map/sum_over_rows/ppermute | solution.py:29
  39.0 1.3 %collective-permute-done.11.refs_2_ = bf16[80,512]{1,0:T(8,128)(2,1)S(1)} collective-permute-done((bf16[80,512]{1,0:T(8,128)(2,1)S(1)}, bf16[80,512]{1,0:T(8,128)(2,1)S(1)}, u32[]{:S(2)}, u32[]{:S(2)}) %collective-permute-start.11) | collective-permute-done | bytes 81952 | tf_op jit(solution)/shard_map/sum_over_rows/ppermute | solution.py:29
  40.4 1.4 %second_product.2 = f32[16,2048]{1,0:T(8,128)S(1)} custom-call(bf16[32,2048]{1,0:T(8,128)(2,1)S(1)} %get-tuple-element.90.narrow_ref, bf16[512,1024]{1,0:T(8,128)(2,1)S(1)} %get-tuple-element.81.refs_0_, bf16[1024,1024]{1,0:T(8,128)(2,1)S(1)} %get-tuple-element.82.refs_1_, bf16[1536,512]{1,0:T(8,128)(2,1)S(1)} %get-tuple-element.83.refs_2_, ...), custom_call_target="tpu_custom_call" | custom-call | flops 134217728 | bytes 1024 | tf_op jit(solution)/shard_map/second_product/pallas_call | solution.py:241
  41.8 1.4 %second_product.3.mine_ref = f32[16,2048]{1,0:T(8,128)S(1)} custom-call(bf16[32,2048]{1,0:T(8,128)(2,1)S(1)} %get-tuple-element.90.narrow_ref, bf16[512,1024]{1,0:T(8,128)(2,1)S(1)} %get-tuple-element.81.refs_0_, bf16[1024,1024]{1,0:T(8,128)(2,1)S(1)} %get-tuple-element.82.refs_1_, bf16[1536,512]{1,0:T(8,128)(2,1)S(1)} %get-tuple-element.83.refs_2_, ...), custom_call_target="tpu_custom_call" | custom-call | flops 134217728 | bytes 1024 | tf_op jit(solution)/shard_map/second_product/pallas_call | solution.py:241
  43.3 2.3 %collective-permute-start.14 = (f32[16,512]{1,0:T(8,128)S(1)}, f32[16,512]{1,0:T(8,128)S(1)}, u32[]{:S(2)}, u32[]{:S(2)}) collective-permute-start(f32[16,512]{1,0:T(8,128)S(1)} %get-tuple-element.93), channel_id=1, source_target_pairs={{0,96},{8,104},{16,112},{24,120},{32,64},{40,72},{48,80},{56,88},{... | collective-permute-start | bytes 98312 | tf_op jit(solution)/shard_map/sum_over_columns/ppermute | solution.py:29
  45.6 2.5 %collective-permute-start.15 = (f32[16,512]{1,0:T(8,128)S(1)}, f32[16,512]{1,0:T(8,128)S(1)}, u32[]{:S(2)}, u32[]{:S(2)}) collective-permute-start(f32[16,512]{1,0:T(8,128)S(1)} %get-tuple-element.94), channel_id=1, source_target_pairs={{0,24},{8,16},{16,8},{24,0},{32,56},{40,48},{48,40},{56,32},{64,88... | collective-permute-start | bytes 98312 | tf_op jit(solution)/shard_map/sum_over_columns/ppermute | solution.py:29
  48.1 1.2 %collective-permute-start.16 = (f32[16,512]{1,0:T(8,128)S(1)}, f32[16,512]{1,0:T(8,128)S(1)}, u32[]{:S(2)}, u32[]{:S(2)}) collective-permute-start(f32[16,512]{1,0:T(8,128)S(1)} %get-tuple-element.95), channel_id=1, source_target_pairs={{0,120},{8,112},{16,104},{24,96},{32,88},{40,80},{48,72},{56,64},{... | collective-permute-start | bytes 98312 | tf_op jit(solution)/shard_map/sum_over_columns/ppermute | solution.py:29
  49.3 1.4 %collective-permute-done.15.refs_2_ = f32[16,512]{1,0:T(8,128)S(1)} collective-permute-done((f32[16,512]{1,0:T(8,128)S(1)}, f32[16,512]{1,0:T(8,128)S(1)}, u32[]{:S(2)}, u32[]{:S(2)}) %collective-permute-start.15) | collective-permute-done | bytes 32800 | tf_op jit(solution)/shard_map/sum_over_columns/ppermute | solution.py:29
  50.7 4.6 %collective-permute-done.16.refs_3_ = f32[16,512]{1,0:T(8,128)S(1)} collective-permute-done((f32[16,512]{1,0:T(8,128)S(1)}, f32[16,512]{1,0:T(8,128)S(1)}, u32[]{:S(2)}, u32[]{:S(2)}) %collective-permute-start.16) | collective-permute-done | bytes 32800 | tf_op jit(solution)/shard_map/sum_over_columns/ppermute | solution.py:29
  55.6 10.3 %all_to_all.8 = f32[32,1,128]{2,1,0:T(1,128)S(1)} all-to-all(f32[32,1,128]{2,1,0:T(1,128)S(1)} %broadcast_in_dim.2), channel_id=1, replica_groups=mesh['y'=4,'z'=4,'c'=2,'x'=4] {'y','z','c'}, dimensions={0} | all-to-all | bytes 32768 | tf_op jit(solution)/shard_map/final_sums/all_to_all | solution.py:383
  65.9 1.0 %finish.1 = (f32[16,512]{1,0:T(8,128)}, f32[16,512]{1,0:T(8,128)}) custom-call(f32[16,512]{1,0:T(8,128)S(1)} %bitcast.12, f32[16,512]{1,0:T(8,128)S(1)} %get-tuple-element.79.rho_ref, f32[16,512]{1,0:T(8,128)S(1)} %get-tuple-element.96.image_ref, f32[32,128]{1,0:T(8,128)S(1)} %bitcast.13), custom_call_target="tpu_custom_call" | custom-call | tf_op jit(solution)/shard_map/finish/pallas_call | solution.py:315
  (30 shorter events, 1.7 us)
Async XLA Ops:
  0.6 1.5 %copy-start = (bf16[1024,256]{1,0:T(8,128)(2,1)S(1)}, bf16[1024,256]{1,0:T(8,128)(2,1)}, u32[]{:S(2)}) copy-start(bf16[1024,256]{1,0:T(8,128)(2,1)} %param.3) | copy-start | bytes 1572868
  2.5 8.6 %collective-permute-start.2 = (bf16[576,256]{1,0:T(8,128)(2,1)S(1)}, bf16[576,256]{1,0:T(8,128)(2,1)S(1)}, u32[]{:S(2)}, u32[]{:S(2)}) collective-permute-start(bf16[576,256]{1,0:T(8,128)(2,1)S(1)} %pack.1.refs_1_.refs_2_), channel_id=1, source_target_pairs={{0,4},{4,0},{1,5},{5,1},{2,6},{6,2},{3,7},{7,3},{8,12},{12,8},{9,1... | collective-permute-start | bytes 884744 | tf_op jit(solution)/shard_map/fetch_points/ppermute | solution.py:48
  2.6 11.2 %collective-permute-start.1 = (bf16[512,256]{1,0:T(8,128)(2,1)S(1)}, bf16[512,256]{1,0:T(8,128)(2,1)S(1)}, u32[]{:S(2)}, u32[]{:S(2)}) collective-permute-start(bf16[512,256]{1,0:T(8,128)(2,1)S(1)} %constant_dynamic-slice_fusion.points_ref.refs_0_), channel_id=1, source_target_pairs={{0,8},{8,0},{16,24},{24,16},{32,40},{40,32},{48,56},{56,48},{64,72... | collective-permute-start | bytes 786440 | tf_op jit(solution)/shard_map/fetch_points/ppermute | solution.py:29
  4.6 9.1 %collective-permute-start = (bf16[512,256]{1,0:T(8,128)(2,1)S(1)}, bf16[512,256]{1,0:T(8,128)(2,1)S(1)}, u32[]{:S(2)}, u32[]{:S(2)}) collective-permute-start(bf16[512,256]{1,0:T(8,128)(2,1)S(1)} %constant_dynamic-slice_fusion.points_ref.refs_0_), channel_id=1, source_target_pairs={{0,32},{8,40},{16,48},{24,56},{32,0},{40,8},{48,16},{56,24},{64,96... | collective-permute-start | bytes 786440 | tf_op jit(solution)/shard_map/fetch_points/ppermute | solution.py:29
  6.2 16.3 %collective-permute-start.5 = (bf16[576,256]{1,0:T(8,128)(2,1)S(1)}, bf16[576,256]{1,0:T(8,128)(2,1)S(1)}, u32[]{:S(2)}, u32[]{:S(2)}) collective-permute-start(bf16[576,256]{1,0:T(8,128)(2,1)S(1)} %pack.1.refs_1_.refs_2_), channel_id=1, source_target_pairs={{0,24},{8,16},{16,8},{24,0},{32,56},{40,48},{48,40},{56,32},{64,88... | collective-permute-start | bytes 884744 | tf_op jit(solution)/shard_map/fetch_points/ppermute | solution.py:29
  8.7 21.6 %collective-permute-start.8 = (bf16[576,256]{1,0:T(8,128)(2,1)S(1)}, bf16[576,256]{1,0:T(8,128)(2,1)S(1)}, u32[]{:S(2)}, u32[]{:S(2)}) collective-permute-start(bf16[576,256]{1,0:T(8,128)(2,1)S(1)} %pack.1.refs_1_.refs_2_), channel_id=1, source_target_pairs={{0,120},{8,112},{16,104},{24,96},{32,88},{40,80},{48,72},{56,64},{... | collective-permute-start | bytes 884744 | tf_op jit(solution)/shard_map/fetch_points/ppermute | solution.py:29
  11.1 13.9 %collective-permute-start.4 = (bf16[576,256]{1,0:T(8,128)(2,1)S(1)}, bf16[576,256]{1,0:T(8,128)(2,1)S(1)}, u32[]{:S(2)}, u32[]{:S(2)}) collective-permute-start(bf16[576,256]{1,0:T(8,128)(2,1)S(1)} %pack.1.refs_1_.refs_2_), channel_id=1, source_target_pairs={{0,96},{8,104},{16,112},{24,120},{32,64},{40,72},{48,80},{56,88},{... | collective-permute-start | bytes 884744 | tf_op jit(solution)/shard_map/fetch_points/ppermute | solution.py:29
  12.1 0.8 %copy-start.1 = (f32[512,16]{0,1:T(8,128)S(1)}, f32[512,16]{0,1:T(8,128)}, u32[]{:S(2)}) copy-start(f32[512,16]{0,1:T(8,128)} %param.5) | copy-start | bytes 98308
  13.8 14.4 %collective-permute-start.3 = (bf16[512,256]{1,0:T(8,128)(2,1)S(1)}, bf16[512,256]{1,0:T(8,128)(2,1)S(1)}, u32[]{:S(2)}, u32[]{:S(2)}) collective-permute-start(bf16[512,256]{1,0:T(8,128)(2,1)S(1)} %broadcast_select_fusion), channel_id=1, source_target_pairs={{0,32},{4,12},{8,40},{12,4},{16,48},{20,28},{24,56},{28,20},{32,0}... | collective-permute-start | bytes 786440 | tf_op jit(solution)/shard_map/fetch_points/ppermute | solution.py:44
  22.5 3.5 %collective-permute-start.7 = (bf16[576,256]{1,0:T(8,128)(2,1)S(1)}, bf16[576,256]{1,0:T(8,128)(2,1)S(1)}, u32[]{:S(2)}, u32[]{:S(2)}) collective-permute-start(bf16[576,256]{1,0:T(8,128)(2,1)S(1)} %collective-permute-done.5.refs_3_.refs_4_), channel_id=1, source_target_pairs={{0,4},{4,0},{1,5},{5,1},{2,6},{6,2},{3,7},{7,3},{8,12},{12,8},{9,1... | collective-permute-start | bytes 884744 | tf_op jit(solution)/shard_map/build_tiles/ppermute | solution.py:48
  25.0 2.2 %collective-permute-start.6 = (bf16[576,256]{1,0:T(8,128)(2,1)S(1)}, bf16[576,256]{1,0:T(8,128)(2,1)S(1)}, u32[]{:S(2)}, u32[]{:S(2)}) collective-permute-start(bf16[576,256]{1,0:T(8,128)(2,1)S(1)} %collective-permute-done.4.refs_3_), channel_id=1, source_target_pairs={{0,4},{4,0},{1,5},{5,1},{2,6},{6,2},{3,7},{7,3},{8,12},{12,8},{9,1... | collective-permute-start | bytes 884744 | tf_op jit(solution)/shard_map/build_tiles/ppermute | solution.py:48
  30.3 2.0 %collective-permute-start.9 = (bf16[576,256]{1,0:T(8,128)(2,1)S(1)}, bf16[576,256]{1,0:T(8,128)(2,1)S(1)}, u32[]{:S(2)}, u32[]{:S(2)}) collective-permute-start(bf16[576,256]{1,0:T(8,128)(2,1)S(1)} %collective-permute-done.8.refs_4_), channel_id=1, source_target_pairs={{0,4},{4,0},{1,5},{5,1},{2,6},{6,2},{3,7},{7,3},{8,12},{12,8},{9,1... | collective-permute-start | bytes 884744 | tf_op jit(solution)/shard_map/build_tiles/ppermute | solution.py:48
  33.8 5.2 %collective-permute-start.10 = (bf16[80,512]{1,0:T(8,128)(2,1)S(1)}, bf16[80,512]{1,0:T(8,128)(2,1)S(1)}, u32[]{:S(2)}, u32[]{:S(2)}) collective-permute-start(bf16[80,512]{1,0:T(8,128)(2,1)S(1)} %get-tuple-element.76), channel_id=1, source_target_pairs={{0,32},{8,40},{16,48},{24,56},{32,0},{40,8},{48,16},{56,24},{64,96... | collective-permute-start | bytes 245768 | tf_op jit(solution)/shard_map/sum_over_rows/ppermute | solution.py:29
  33.9 6.4 %collective-permute-start.11 = (bf16[80,512]{1,0:T(8,128)(2,1)S(1)}, bf16[80,512]{1,0:T(8,128)(2,1)S(1)}, u32[]{:S(2)}, u32[]{:S(2)}) collective-permute-start(bf16[80,512]{1,0:T(8,128)(2,1)S(1)} %get-tuple-element.77), channel_id=1, source_target_pairs={{0,8},{8,0},{16,24},{24,16},{32,40},{40,32},{48,56},{56,48},{64,72... | collective-permute-start | bytes 245768 | tf_op jit(solution)/shard_map/sum_over_rows/ppermute | solution.py:29
  34.7 5.6 %collective-permute-start.12 = (bf16[80,512]{1,0:T(8,128)(2,1)S(1)}, bf16[80,512]{1,0:T(8,128)(2,1)S(1)}, u32[]{:S(2)}, u32[]{:S(2)}) collective-permute-start(bf16[80,512]{1,0:T(8,128)(2,1)S(1)} %get-tuple-element.78), channel_id=1, source_target_pairs={{0,40},{8,32},{16,56},{24,48},{32,8},{40,0},{48,24},{56,16},{64,10... | collective-permute-start | bytes 245768 | tf_op jit(solution)/shard_map/sum_over_rows/ppermute | solution.py:29
  41.8 13.5 %copy-start.2 = (f32[512,16]{0,1:T(8,128)S(1)}, f32[512,16]{0,1:T(8,128)}, u32[]{:S(2)}) copy-start(f32[512,16]{0,1:T(8,128)} %param.5) | copy-start | bytes 98308
  41.8 1.4 %collective-permute-start.13 = (f32[16,2048]{1,0:T(8,128)S(1)}, f32[16,2048]{1,0:T(8,128)S(1)}, u32[]{:S(2)}, u32[]{:S(2)}) collective-permute-start(f32[16,2048]{1,0:T(8,128)S(1)} %second_product.2), channel_id=1, source_target_pairs={{0,4},{4,0},{1,5},{5,1},{2,6},{6,2},{3,7},{7,3},{8,12},{12,8},{9,1... | collective-permute-start | bytes 393224 | tf_op jit(solution)/shard_map/sum_over_columns/ppermute | solution.py:48
  43.3 6.0 %collective-permute-start.14 = (f32[16,512]{1,0:T(8,128)S(1)}, f32[16,512]{1,0:T(8,128)S(1)}, u32[]{:S(2)}, u32[]{:S(2)}) collective-permute-start(f32[16,512]{1,0:T(8,128)S(1)} %get-tuple-element.93), channel_id=1, source_target_pairs={{0,96},{8,104},{16,112},{24,120},{32,64},{40,72},{48,80},{56,88},{... | collective-permute-start | bytes 98312 | tf_op jit(solution)/shard_map/sum_over_columns/ppermute | solution.py:29
  45.6 5.1 %collective-permute-start.15 = (f32[16,512]{1,0:T(8,128)S(1)}, f32[16,512]{1,0:T(8,128)S(1)}, u32[]{:S(2)}, u32[]{:S(2)}) collective-permute-start(f32[16,512]{1,0:T(8,128)S(1)} %get-tuple-element.94), channel_id=1, source_target_pairs={{0,24},{8,16},{16,8},{24,0},{32,56},{40,48},{48,40},{56,32},{64,88... | collective-permute-start | bytes 98312 | tf_op jit(solution)/shard_map/sum_over_columns/ppermute | solution.py:29
  48.1 7.2 %collective-permute-start.16 = (f32[16,512]{1,0:T(8,128)S(1)}, f32[16,512]{1,0:T(8,128)S(1)}, u32[]{:S(2)}, u32[]{:S(2)}) collective-permute-start(f32[16,512]{1,0:T(8,128)S(1)} %get-tuple-element.95), channel_id=1, source_target_pairs={{0,120},{8,112},{16,104},{24,96},{32,88},{40,80},{48,72},{56,64},{... | collective-permute-start | bytes 98312 | tf_op jit(solution)/shard_map/sum_over_columns/ppermute | solution.py:29

commit v25 on v20

--- a/solution.py
+++ b/solution.py
@@ -365,7 +365,7 @@
 
     with jax.named_scope("sum_over_columns"):
         blocks = merge(mine, swap_core(other), own)
-        shares = [blocks[0]] + swap_each(blocks[1:], SQUARE[1:])
+        shares = [blocks[0]] + swap_each(blocks[:0:-1], SQUARE[:0:-1])
 
     with jax.named_scope("final_sums"):
         image, sums = local_sums(side, rho, shares)

time: 64.5 us -> 62.9 us (0.975)
  blocking collectives: 12.1 us -> 10.3 us
    all_to_all x1, blocking collectives: 12.1 us -> 10.3 us  [on_device(): sums = lax.all_to_all(sums, ('y', 'z', 'c'), 0, 0, tiled=True)]
  transfers between devices with their start and end apart: 17 -> 17, of which waited for: 7 -> 8; matrix products, arithmetic and copies ran while one was open for 0% -> 0% of each run, Pallas kernels for 18% -> 19%
where the time goes in v25:
time: 62.9 us; the launch traced here: 61.8 us
  starting transfers between devices  22.2 us (35%)
  Pallas kernels  15.9 us (25%)
  waiting for transfers between devices  10.4 us (17%)
  blocking collectives  10.3 us (16%)
  between operations  1.42 us (2%)
  local copies, waits for them, and re-layouts  0.85 us (1%)
  other arithmetic  0.76 us (1%)
    ppermute x12, starting transfers between devices, swap(): return lax.ppermute(value, ('y', 'z'), pairs)  21.3 us
    pallas_call x9, Pallas kernels, build(): pl.pallas_call(functools.partial(tile_kernel, counts, probes), out_shape=...  11.3 us
    all_to_all x1, blocking collectives, on_device(): sums = lax.all_to_all(sums, ('y', 'z', 'c'), 0, 0, tiled=True)  10.3 us
    ppermute x12, waiting for transfers between devices, swap(): return lax.ppermute(value, ('y', 'z'), pairs)  10.2 us
    pallas_call x2, Pallas kernels, second_product(): pl.pallas_call(functools.partial(second_kernel, own, half, places), in_sp...  2.87 us
  transfers between devices with their start and end apart: 17, of which 8 were waited for; matrix products, arithmetic and copies ran while one was open for 0% of the time, Pallas kernels for 19%

profile of v25, /device:TPU:0, one launch (start us, length us, event | category | flops | bytes accessed | tf_op | source)
XLA Modules:
  0.0 61.8 jit_solution(12942117524091142270)
XLA Ops:
  1.3 0.8 %bitcast_convert_fusion.side_ref = bf16[16,512]{1,0:T(8,128)(2,1)S(1)} fusion(f32[512,16]{0,1:T(8,128)} %param.5), kind=kLoop, calls=%fused_computation.1 | loop fusion | flops 8192 | bytes 49152 | tf_op jit(solution)/shard_map/fetch_points/convert_element_type | solution.py:318
  2.6 4.2 %collective-permute-start.5 = (bf16[576,256]{1,0:T(8,128)(2,1)S(1)}, bf16[576,256]{1,0:T(8,128)(2,1)S(1)}, u32[]{:S(2)}, u32[]{:S(2)}) collective-permute-start(bf16[576,256]{1,0:T(8,128)(2,1)S(1)} %pack.1.refs_1_.refs_2_), channel_id=1, source_target_pairs={{0,24},{8,16},{16,8},{24,0},{32,56},{40,48},{48,40},{56,32},{64,88... | collective-permute-start | bytes 884744 | tf_op jit(solution)/shard_map/fetch_points/ppermute | solution.py:29
  6.8 1.6 %collective-permute-start = (bf16[512,256]{1,0:T(8,128)(2,1)S(1)}, bf16[512,256]{1,0:T(8,128)(2,1)S(1)}, u32[]{:S(2)}, u32[]{:S(2)}) collective-permute-start(bf16[512,256]{1,0:T(8,128)(2,1)S(1)} %constant_dynamic-slice_fusion.points_ref.refs_0_), channel_id=1, source_target_pairs={{0,32},{8,40},{16,48},{24,56},{32,0},{40,8},{48,16},{56,24},{64,96... | collective-permute-start | bytes 786440 | tf_op jit(solution)/shard_map/fetch_points/ppermute | solution.py:29
  8.3 2.2 %collective-permute-start.4 = (bf16[576,256]{1,0:T(8,128)(2,1)S(1)}, bf16[576,256]{1,0:T(8,128)(2,1)S(1)}, u32[]{:S(2)}, u32[]{:S(2)}) collective-permute-start(bf16[576,256]{1,0:T(8,128)(2,1)S(1)} %pack.1.refs_1_.refs_2_), channel_id=1, source_target_pairs={{0,96},{8,104},{16,112},{24,120},{32,64},{40,72},{48,80},{56,88},{... | collective-permute-start | bytes 884744 | tf_op jit(solution)/shard_map/fetch_points/ppermute | solution.py:29
  10.5 1.0 %collective-permute-start.8 = (bf16[576,256]{1,0:T(8,128)(2,1)S(1)}, bf16[576,256]{1,0:T(8,128)(2,1)S(1)}, u32[]{:S(2)}, u32[]{:S(2)}) collective-permute-start(bf16[576,256]{1,0:T(8,128)(2,1)S(1)} %pack.1.refs_1_.refs_2_), channel_id=1, source_target_pairs={{0,120},{8,112},{16,104},{24,96},{32,88},{40,80},{48,72},{56,64},{... | collective-permute-start | bytes 884744 | tf_op jit(solution)/shard_map/fetch_points/ppermute | solution.py:29
  11.5 0.8 %copy-done.1 = f32[512,16]{0,1:T(8,128)S(1)} copy-done((f32[512,16]{0,1:T(8,128)S(1)}, f32[512,16]{0,1:T(8,128)}, u32[]{:S(2)}) %copy-start.1) | copy-done | bytes 32792
  12.3 0.8 %build_tile.9 = (bf16[512,1024]{1,0:T(8,128)(2,1)S(1)}, f32[16,512]{1,0:T(8,128)S(1)}, f32[512,1]{1,0:T(8,128)S(1)}) custom-call(bf16[512,256]{1,0:T(8,128)(2,1)S(1)} %constant_dynamic-slice_fusion.points_ref.refs_0_, bf16[576,256]{1,0:T(8,128)(2,1)S(1)} %pack.1.refs_1_.refs_2_, bf16[576,256]{1,0:T(8,128)(2,1)S(1)} %collective-permute-done.2.refs_2_.refs_3_, ...), custom_call_target="tpu_custom_call" | custom-call | flops 16777216 | bytes 1024 | tf_op jit(solution)/shard_map/fetch_points/build_tile/pallas_call | solution.py:145
  13.1 2.0 %collective-permute-done.1.refs_1_.refs_2_ = bf16[512,256]{1,0:T(8,128)(2,1)S(1)} collective-permute-done((bf16[512,256]{1,0:T(8,128)(2,1)S(1)}, bf16[512,256]{1,0:T(8,128)(2,1)S(1)}, u32[]{:S(2)}, u32[]{:S(2)}) %collective-permute-start.1) | collective-permute-done | bytes 262176 | tf_op jit(solution)/shard_map/fetch_points/ppermute | solution.py:29
  15.1 2.8 %collective-permute-start.3 = (bf16[512,256]{1,0:T(8,128)(2,1)S(1)}, bf16[512,256]{1,0:T(8,128)(2,1)S(1)}, u32[]{:S(2)}, u32[]{:S(2)}) collective-permute-start(bf16[512,256]{1,0:T(8,128)(2,1)S(1)} %constant_dynamic-slice_fusion.points_ref.refs_0_), channel_id=1, source_target_pairs={{0,40},{8,32},{16,56},{24,48},{32,8},{40,0},{48,24},{56,16},{64,10... | collective-permute-start | bytes 786440 | tf_op jit(solution)/shard_map/fetch_points/ppermute | solution.py:29
  17.9 1.4 %build_tile.10 = (bf16[1024,1024]{1,0:T(8,128)(2,1)S(1)}, f32[16,1024]{1,0:T(8,128)S(1)}, f32[1024,1]{1,0:T(8,128)S(1)}) custom-call(bf16[512,256]{1,0:T(8,128)(2,1)S(1)} %collective-permute-done.refs_0_.refs_1_, bf16[512,256]{1,0:T(8,128)(2,1)S(1)} %collective-permute-done.1.refs_1_.refs_2_, bf16[576,256]{1,0:T(8,128)(2,1)S(1)} %pack.1.refs_1_.refs_2_, ...), custom_call_target="tpu_custom_call" | custom-call | flops 33554432 | bytes 1024 | tf_op jit(solution)/shard_map/fetch_points/build_tile/pallas_call | solution.py:145
  19.4 1.1 %build_tile.11 = (bf16[1536,512]{1,0:T(8,128)(2,1)S(1)}, f32[16,1536]{1,0:T(8,128)S(1)}) custom-call(bf16[512,256]{1,0:T(8,128)(2,1)S(1)} %constant_dynamic-slice_fusion.points_ref.refs_0_, bf16[512,256]{1,0:T(8,128)(2,1)S(1)} %collective-permute-done.refs_0_.refs_1_, bf16[512,256]{1,0:T(8,128)(2,1)S(1)} %collective-permute-done.1.refs_1_.refs_2_, ...), custom_call_target="tpu_custom_call" | custom-call | flops 1610612736 | bytes 1024 | tf_op jit(solution)/shard_map/build_tiles/build_tile/pallas_call | solution.py:145
  21.0 1.1 %build_tile.12 = (bf16[1536,512]{1,0:T(8,128)(2,1)S(1)}, f32[16,1536]{1,0:T(8,128)S(1)}) custom-call(bf16[512,256]{1,0:T(8,128)(2,1)S(1)} %constant_dynamic-slice_fusion.points_ref.refs_0_, bf16[512,256]{1,0:T(8,128)(2,1)S(1)} %collective-permute-done.refs_0_.refs_1_, bf16[512,256]{1,0:T(8,128)(2,1)S(1)} %collective-permute-done.1.refs_1_.refs_2_, ...), custom_call_target="tpu_custom_call" | custom-call | flops 1610612736 | bytes 1024 | tf_op jit(solution)/shard_map/build_tiles/build_tile/pallas_call | solution.py:145
  22.1 1.1 %build_tile.13 = (bf16[1536,512]{1,0:T(8,128)(2,1)S(1)}, f32[16,1536]{1,0:T(8,128)S(1)}) custom-call(bf16[512,256]{1,0:T(8,128)(2,1)S(1)} %constant_dynamic-slice_fusion.points_ref.refs_0_, bf16[512,256]{1,0:T(8,128)(2,1)S(1)} %collective-permute-done.refs_0_.refs_1_, bf16[512,256]{1,0:T(8,128)(2,1)S(1)} %collective-permute-done.1.refs_1_.refs_2_, ...), custom_call_target="tpu_custom_call" | custom-call | flops 1610612736 | bytes 1024 | tf_op jit(solution)/shard_map/build_tiles/build_tile/pallas_call | solution.py:145
  23.2 1.1 %build_tile.14 = (bf16[1536,512]{1,0:T(8,128)(2,1)S(1)}, f32[16,1536]{1,0:T(8,128)S(1)}) custom-call(bf16[512,256]{1,0:T(8,128)(2,1)S(1)} %constant_dynamic-slice_fusion.points_ref.refs_0_, bf16[512,256]{1,0:T(8,128)(2,1)S(1)} %collective-permute-done.refs_0_.refs_1_, bf16[512,256]{1,0:T(8,128)(2,1)S(1)} %collective-permute-done.1.refs_1_.refs_2_, ...), custom_call_target="tpu_custom_call" | custom-call | flops 1610612736 | bytes 1024 | tf_op jit(solution)/shard_map/build_tiles/build_tile/pallas_call | solution.py:145
  24.3 2.1 %build_tile.15 = (bf16[512,3072]{1,0:T(8,128)(2,1)S(1)}, f32[16,512]{1,0:T(8,128)S(1)}, f32[512,1]{1,0:T(8,128)S(1)}) custom-call(bf16[512,256]{1,0:T(8,128)(2,1)S(1)} %collective-permute-done.3.refs_0_.refs_3_, bf16[576,256]{1,0:T(8,128)(2,1)S(1)} %pack.1.refs_1_.refs_2_, bf16[576,256]{1,0:T(8,128)(2,1)S(1)} %collective-permute-done.2.refs_2_.refs_3_, ...), custom_call_target="tpu_custom_call" | custom-call | flops 3221225472 | bytes 1024 | tf_op jit(solution)/shard_map/build_tiles/build_tile/pallas_call | solution.py:145
  26.6 1.3 %build_tile.16 = (bf16[2048,512]{1,0:T(8,128)(2,1)S(1)}, f32[16,2048]{1,0:T(8,128)S(1)}) custom-call(bf16[512,256]{1,0:T(8,128)(2,1)S(1)} %constant_dynamic-slice_fusion.points_ref.refs_0_, bf16[512,256]{1,0:T(8,128)(2,1)S(1)} %collective-permute-done.refs_0_.refs_1_, bf16[512,256]{1,0:T(8,128)(2,1)S(1)} %collective-permute-done.1.refs_1_.refs_2_, ...), custom_call_target="tpu_custom_call" | custom-call | flops 2147483648 | bytes 1024 | tf_op jit(solution)/shard_map/build_tiles/build_tile/pallas_call | solution.py:145
  28.2 1.3 %build_tile.17 = (bf16[2048,512]{1,0:T(8,128)(2,1)S(1)}, f32[16,2048]{1,0:T(8,128)S(1)}) custom-call(bf16[512,256]{1,0:T(8,128)(2,1)S(1)} %constant_dynamic-slice_fusion.points_ref.refs_0_, bf16[512,256]{1,0:T(8,128)(2,1)S(1)} %collective-permute-done.refs_0_.refs_1_, bf16[512,256]{1,0:T(8,128)(2,1)S(1)} %collective-permute-done.1.refs_1_.refs_2_, ...), custom_call_target="tpu_custom_call" | custom-call | flops 2147483648 | bytes 1024 | tf_op jit(solution)/shard_map/build_tiles/build_tile/pallas_call | solution.py:145
  29.6 0.9 %collective-permute-start.10 = (bf16[80,512]{1,0:T(8,128)(2,1)S(1)}, bf16[80,512]{1,0:T(8,128)(2,1)S(1)}, u32[]{:S(2)}, u32[]{:S(2)}) collective-permute-start(bf16[80,512]{1,0:T(8,128)(2,1)S(1)} %get-tuple-element.78), channel_id=1, source_target_pairs={{0,32},{8,40},{16,48},{24,56},{32,0},{40,8},{48,16},{56,24},{64,96... | collective-permute-start | bytes 245768 | tf_op jit(solution)/shard_map/sum_over_rows/ppermute | solution.py:29
  30.5 1.4 %collective-permute-start.11 = (bf16[80,512]{1,0:T(8,128)(2,1)S(1)}, bf16[80,512]{1,0:T(8,128)(2,1)S(1)}, u32[]{:S(2)}, u32[]{:S(2)}) collective-permute-start(bf16[80,512]{1,0:T(8,128)(2,1)S(1)} %get-tuple-element.79), channel_id=1, source_target_pairs={{0,8},{8,0},{16,24},{24,16},{32,40},{40,32},{48,56},{56,48},{64,72... | collective-permute-start | bytes 245768 | tf_op jit(solution)/shard_map/sum_over_rows/ppermute | solution.py:29
  31.9 1.2 %collective-permute-start.12 = (bf16[80,512]{1,0:T(8,128)(2,1)S(1)}, bf16[80,512]{1,0:T(8,128)(2,1)S(1)}, u32[]{:S(2)}, u32[]{:S(2)}) collective-permute-start(bf16[80,512]{1,0:T(8,128)(2,1)S(1)} %get-tuple-element.80), channel_id=1, source_target_pairs={{0,40},{8,32},{16,56},{24,48},{32,8},{40,0},{48,24},{56,16},{64,10... | collective-permute-start | bytes 245768 | tf_op jit(solution)/shard_map/sum_over_rows/ppermute | solution.py:29
  33.1 1.2 %collective-permute-done.10.refs_1_ = bf16[80,512]{1,0:T(8,128)(2,1)S(1)} collective-permute-done((bf16[80,512]{1,0:T(8,128)(2,1)S(1)}, bf16[80,512]{1,0:T(8,128)(2,1)S(1)}, u32[]{:S(2)}, u32[]{:S(2)}) %collective-permute-start.10) | collective-permute-done | bytes 81952 | tf_op jit(solution)/shard_map/sum_over_rows/ppermute | solution.py:29
  34.3 1.3 %collective-permute-done.11.refs_2_ = bf16[80,512]{1,0:T(8,128)(2,1)S(1)} collective-permute-done((bf16[80,512]{1,0:T(8,128)(2,1)S(1)}, bf16[80,512]{1,0:T(8,128)(2,1)S(1)}, u32[]{:S(2)}, u32[]{:S(2)}) %collective-permute-start.11) | collective-permute-done | bytes 81952 | tf_op jit(solution)/shard_map/sum_over_rows/ppermute | solution.py:29
  35.6 1.6 %collective-permute-done.12.refs_3_ = bf16[80,512]{1,0:T(8,128)(2,1)S(1)} collective-permute-done((bf16[80,512]{1,0:T(8,128)(2,1)S(1)}, bf16[80,512]{1,0:T(8,128)(2,1)S(1)}, u32[]{:S(2)}, u32[]{:S(2)}) %collective-permute-start.12) | collective-permute-done | bytes 81952 | tf_op jit(solution)/shard_map/sum_over_rows/ppermute | solution.py:29
  37.3 1.4 %second_product.2 = f32[16,2048]{1,0:T(8,128)S(1)} custom-call(bf16[32,2048]{1,0:T(8,128)(2,1)S(1)} %get-tuple-element.92.narrow_ref, bf16[512,1024]{1,0:T(8,128)(2,1)S(1)} %get-tuple-element.83.refs_0_, bf16[1024,1024]{1,0:T(8,128)(2,1)S(1)} %get-tuple-element.84.refs_1_, bf16[1536,512]{1,0:T(8,128)(2,1)S(1)} %get-tuple-element.85.refs_2_, ...), custom_call_target="tpu_custom_call" | custom-call | flops 134217728 | bytes 1024 | tf_op jit(solution)/shard_map/second_product/pallas_call | solution.py:231
  38.7 1.4 %second_product.3.mine_ref = f32[16,2048]{1,0:T(8,128)S(1)} custom-call(bf16[32,2048]{1,0:T(8,128)(2,1)S(1)} %get-tuple-element.92.narrow_ref, bf16[512,1024]{1,0:T(8,128)(2,1)S(1)} %get-tuple-element.83.refs_0_, bf16[1024,1024]{1,0:T(8,128)(2,1)S(1)} %get-tuple-element.84.refs_1_, bf16[1536,512]{1,0:T(8,128)(2,1)S(1)} %get-tuple-element.85.refs_2_, ...), custom_call_target="tpu_custom_call" | custom-call | flops 134217728 | bytes 1024 | tf_op jit(solution)/shard_map/second_product/pallas_call | solution.py:231
  40.2 2.2 %collective-permute-start.14 = (f32[16,512]{1,0:T(8,128)S(1)}, f32[16,512]{1,0:T(8,128)S(1)}, u32[]{:S(2)}, u32[]{:S(2)}) collective-permute-start(f32[16,512]{1,0:T(8,128)S(1)} %get-tuple-element.95), channel_id=1, source_target_pairs={{0,120},{8,112},{16,104},{24,96},{32,88},{40,80},{48,72},{56,64},{... | collective-permute-start | bytes 98312 | tf_op jit(solution)/shard_map/sum_over_columns/ppermute | solution.py:29
  42.4 2.8 %collective-permute-start.15 = (f32[16,512]{1,0:T(8,128)S(1)}, f32[16,512]{1,0:T(8,128)S(1)}, u32[]{:S(2)}, u32[]{:S(2)}) collective-permute-start(f32[16,512]{1,0:T(8,128)S(1)} %get-tuple-element.96), channel_id=1, source_target_pairs={{0,24},{8,16},{16,8},{24,0},{32,56},{40,48},{48,40},{56,32},{64,88... | collective-permute-start | bytes 98312 | tf_op jit(solution)/shard_map/sum_over_columns/ppermute | solution.py:29
  45.1 1.1 %collective-permute-start.16 = (f32[16,512]{1,0:T(8,128)S(1)}, f32[16,512]{1,0:T(8,128)S(1)}, u32[]{:S(2)}, u32[]{:S(2)}) collective-permute-start(f32[16,512]{1,0:T(8,128)S(1)} %get-tuple-element.97), channel_id=1, source_target_pairs={{0,96},{8,104},{16,112},{24,120},{32,64},{40,72},{48,80},{56,88},{... | collective-permute-start | bytes 98312 | tf_op jit(solution)/shard_map/sum_over_columns/ppermute | solution.py:29
  46.2 1.4 %collective-permute-done.14.refs_1_ = f32[16,512]{1,0:T(8,128)S(1)} collective-permute-done((f32[16,512]{1,0:T(8,128)S(1)}, f32[16,512]{1,0:T(8,128)S(1)}, u32[]{:S(2)}, u32[]{:S(2)}) %collective-permute-start.14) | collective-permute-done | bytes 32800 | tf_op jit(solution)/shard_map/sum_over_columns/ppermute | solution.py:29
  47.8 2.4 %collective-permute-done.16.refs_3_ = f32[16,512]{1,0:T(8,128)S(1)} collective-permute-done((f32[16,512]{1,0:T(8,128)S(1)}, f32[16,512]{1,0:T(8,128)S(1)}, u32[]{:S(2)}, u32[]{:S(2)}) %collective-permute-start.16) | collective-permute-done | bytes 32800 | tf_op jit(solution)/shard_map/sum_over_columns/ppermute | solution.py:29
  50.5 10.3 %all_to_all.8 = f32[32,1,128]{2,1,0:T(1,128)S(1)} all-to-all(f32[32,1,128]{2,1,0:T(1,128)S(1)} %broadcast_in_dim.2), channel_id=1, replica_groups=mesh['y'=4,'z'=4,'c'=2,'x'=4] {'y','z','c'}, dimensions={0} | all-to-all | bytes 32768 | tf_op jit(solution)/shard_map/final_sums/all_to_all | solution.py:373
  60.8 1.0 %finish.1 = (f32[16,512]{1,0:T(8,128)}, f32[16,512]{1,0:T(8,128)}) custom-call(f32[16,512]{1,0:T(8,128)S(1)} %bitcast.12, f32[16,512]{1,0:T(8,128)S(1)} %get-tuple-element.81.rho_ref, f32[16,512]{1,0:T(8,128)S(1)} %get-tuple-element.98.image_ref, f32[32,128]{1,0:T(8,128)S(1)} %bitcast.13), custom_call_target="tpu_custom_call" | custom-call | tf_op jit(solution)/shard_map/finish/pallas_call | solution.py:305
  (29 shorter events, 2.2 us)
Async XLA Ops:
  0.6 1.5 %copy-start = (bf16[1024,256]{1,0:T(8,128)(2,1)S(1)}, bf16[1024,256]{1,0:T(8,128)(2,1)}, u32[]{:S(2)}) copy-start(bf16[1024,256]{1,0:T(8,128)(2,1)} %param.3) | copy-start | bytes 1572868
  2.5 8.1 %collective-permute-start.2 = (bf16[576,256]{1,0:T(8,128)(2,1)S(1)}, bf16[576,256]{1,0:T(8,128)(2,1)S(1)}, u32[]{:S(2)}, u32[]{:S(2)}) collective-permute-start(bf16[576,256]{1,0:T(8,128)(2,1)S(1)} %pack.1.refs_1_.refs_2_), channel_id=1, source_target_pairs={{0,4},{4,0},{1,5},{5,1},{2,6},{6,2},{3,7},{7,3},{8,12},{12,8},{9,1... | collective-permute-start | bytes 884744 | tf_op jit(solution)/shard_map/fetch_points/ppermute | solution.py:38
  2.6 16.8 %collective-permute-start.5 = (bf16[576,256]{1,0:T(8,128)(2,1)S(1)}, bf16[576,256]{1,0:T(8,128)(2,1)S(1)}, u32[]{:S(2)}, u32[]{:S(2)}) collective-permute-start(bf16[576,256]{1,0:T(8,128)(2,1)S(1)} %pack.1.refs_1_.refs_2_), channel_id=1, source_target_pairs={{0,24},{8,16},{16,8},{24,0},{32,56},{40,48},{48,40},{56,32},{64,88... | collective-permute-start | bytes 884744 | tf_op jit(solution)/shard_map/fetch_points/ppermute | solution.py:29
  6.8 8.4 %collective-permute-start.1 = (bf16[512,256]{1,0:T(8,128)(2,1)S(1)}, bf16[512,256]{1,0:T(8,128)(2,1)S(1)}, u32[]{:S(2)}, u32[]{:S(2)}) collective-permute-start(bf16[512,256]{1,0:T(8,128)(2,1)S(1)} %constant_dynamic-slice_fusion.points_ref.refs_0_), channel_id=1, source_target_pairs={{0,8},{8,0},{16,24},{24,16},{32,40},{40,32},{48,56},{56,48},{64,72... | collective-permute-start | bytes 786440 | tf_op jit(solution)/shard_map/fetch_points/ppermute | solution.py:29
  6.8 8.4 %collective-permute-start = (bf16[512,256]{1,0:T(8,128)(2,1)S(1)}, bf16[512,256]{1,0:T(8,128)(2,1)S(1)}, u32[]{:S(2)}, u32[]{:S(2)}) collective-permute-start(bf16[512,256]{1,0:T(8,128)(2,1)S(1)} %constant_dynamic-slice_fusion.points_ref.refs_0_), channel_id=1, source_target_pairs={{0,32},{8,40},{16,48},{24,56},{32,0},{40,8},{48,16},{56,24},{64,96... | collective-permute-start | bytes 786440 | tf_op jit(solution)/shard_map/fetch_points/ppermute | solution.py:29
  8.3 12.1 %collective-permute-start.4 = (bf16[576,256]{1,0:T(8,128)(2,1)S(1)}, bf16[576,256]{1,0:T(8,128)(2,1)S(1)}, u32[]{:S(2)}, u32[]{:S(2)}) collective-permute-start(bf16[576,256]{1,0:T(8,128)(2,1)S(1)} %pack.1.refs_1_.refs_2_), channel_id=1, source_target_pairs={{0,96},{8,104},{16,112},{24,120},{32,64},{40,72},{48,80},{56,88},{... | collective-permute-start | bytes 884744 | tf_op jit(solution)/shard_map/fetch_points/ppermute | solution.py:29
  10.5 15.8 %collective-permute-start.8 = (bf16[576,256]{1,0:T(8,128)(2,1)S(1)}, bf16[576,256]{1,0:T(8,128)(2,1)S(1)}, u32[]{:S(2)}, u32[]{:S(2)}) collective-permute-start(bf16[576,256]{1,0:T(8,128)(2,1)S(1)} %pack.1.refs_1_.refs_2_), channel_id=1, source_target_pairs={{0,120},{8,112},{16,104},{24,96},{32,88},{40,80},{48,72},{56,64},{... | collective-permute-start | bytes 884744 | tf_op jit(solution)/shard_map/fetch_points/ppermute | solution.py:29
  11.5 0.8 %copy-start.1 = (f32[512,16]{0,1:T(8,128)S(1)}, f32[512,16]{0,1:T(8,128)}, u32[]{:S(2)}) copy-start(f32[512,16]{0,1:T(8,128)} %param.5) | copy-start | bytes 98308
  15.1 9.1 %collective-permute-start.3 = (bf16[512,256]{1,0:T(8,128)(2,1)S(1)}, bf16[512,256]{1,0:T(8,128)(2,1)S(1)}, u32[]{:S(2)}, u32[]{:S(2)}) collective-permute-start(bf16[512,256]{1,0:T(8,128)(2,1)S(1)} %constant_dynamic-slice_fusion.points_ref.refs_0_), channel_id=1, source_target_pairs={{0,40},{8,32},{16,56},{24,48},{32,8},{40,0},{48,24},{56,16},{64,10... | collective-permute-start | bytes 786440 | tf_op jit(solution)/shard_map/fetch_points/ppermute | solution.py:29
  19.3 2.7 %collective-permute-start.7 = (bf16[576,256]{1,0:T(8,128)(2,1)S(1)}, bf16[576,256]{1,0:T(8,128)(2,1)S(1)}, u32[]{:S(2)}, u32[]{:S(2)}) collective-permute-start(bf16[576,256]{1,0:T(8,128)(2,1)S(1)} %collective-permute-done.5.refs_3_.refs_4_), channel_id=1, source_target_pairs={{0,4},{4,0},{1,5},{5,1},{2,6},{6,2},{3,7},{7,3},{8,12},{12,8},{9,1... | collective-permute-start | bytes 884744 | tf_op jit(solution)/shard_map/build_tiles/ppermute | solution.py:38
  20.4 2.7 %collective-permute-start.6 = (bf16[576,256]{1,0:T(8,128)(2,1)S(1)}, bf16[576,256]{1,0:T(8,128)(2,1)S(1)}, u32[]{:S(2)}, u32[]{:S(2)}) collective-permute-start(bf16[576,256]{1,0:T(8,128)(2,1)S(1)} %collective-permute-done.4.refs_3_), channel_id=1, source_target_pairs={{0,4},{4,0},{1,5},{5,1},{2,6},{6,2},{3,7},{7,3},{8,12},{12,8},{9,1... | collective-permute-start | bytes 884744 | tf_op jit(solution)/shard_map/build_tiles/ppermute | solution.py:38
  26.4 1.8 %collective-permute-start.9 = (bf16[576,256]{1,0:T(8,128)(2,1)S(1)}, bf16[576,256]{1,0:T(8,128)(2,1)S(1)}, u32[]{:S(2)}, u32[]{:S(2)}) collective-permute-start(bf16[576,256]{1,0:T(8,128)(2,1)S(1)} %collective-permute-done.8.refs_4_), channel_id=1, source_target_pairs={{0,4},{4,0},{1,5},{5,1},{2,6},{6,2},{3,7},{7,3},{8,12},{12,8},{9,1... | collective-permute-start | bytes 884744 | tf_op jit(solution)/shard_map/build_tiles/ppermute | solution.py:38
  29.6 4.8 %collective-permute-start.10 = (bf16[80,512]{1,0:T(8,128)(2,1)S(1)}, bf16[80,512]{1,0:T(8,128)(2,1)S(1)}, u32[]{:S(2)}, u32[]{:S(2)}) collective-permute-start(bf16[80,512]{1,0:T(8,128)(2,1)S(1)} %get-tuple-element.78), channel_id=1, source_target_pairs={{0,32},{8,40},{16,48},{24,56},{32,0},{40,8},{48,16},{56,24},{64,96... | collective-permute-start | bytes 245768 | tf_op jit(solution)/shard_map/sum_over_rows/ppermute | solution.py:29
  30.5 5.2 %collective-permute-start.11 = (bf16[80,512]{1,0:T(8,128)(2,1)S(1)}, bf16[80,512]{1,0:T(8,128)(2,1)S(1)}, u32[]{:S(2)}, u32[]{:S(2)}) collective-permute-start(bf16[80,512]{1,0:T(8,128)(2,1)S(1)} %get-tuple-element.79), channel_id=1, source_target_pairs={{0,8},{8,0},{16,24},{24,16},{32,40},{40,32},{48,56},{56,48},{64,72... | collective-permute-start | bytes 245768 | tf_op jit(solution)/shard_map/sum_over_rows/ppermute | solution.py:29
  31.9 5.3 %collective-permute-start.12 = (bf16[80,512]{1,0:T(8,128)(2,1)S(1)}, bf16[80,512]{1,0:T(8,128)(2,1)S(1)}, u32[]{:S(2)}, u32[]{:S(2)}) collective-permute-start(bf16[80,512]{1,0:T(8,128)(2,1)S(1)} %get-tuple-element.80), channel_id=1, source_target_pairs={{0,40},{8,32},{16,56},{24,48},{32,8},{40,0},{48,24},{56,16},{64,10... | collective-permute-start | bytes 245768 | tf_op jit(solution)/shard_map/sum_over_rows/ppermute | solution.py:29
  38.7 22.1 %copy-start.2 = (f32[512,16]{0,1:T(8,128)S(1)}, f32[512,16]{0,1:T(8,128)}, u32[]{:S(2)}) copy-start(f32[512,16]{0,1:T(8,128)} %param.5) | copy-start | bytes 98308
  38.7 1.5 %collective-permute-start.13 = (f32[16,2048]{1,0:T(8,128)S(1)}, f32[16,2048]{1,0:T(8,128)S(1)}, u32[]{:S(2)}, u32[]{:S(2)}) collective-permute-start(f32[16,2048]{1,0:T(8,128)S(1)} %second_product.2), channel_id=1, source_target_pairs={{0,4},{4,0},{1,5},{5,1},{2,6},{6,2},{3,7},{7,3},{8,12},{12,8},{9,1... | collective-permute-start | bytes 393224 | tf_op jit(solution)/shard_map/sum_over_columns/ppermute | solution.py:38
  40.2 7.4 %collective-permute-start.14 = (f32[16,512]{1,0:T(8,128)S(1)}, f32[16,512]{1,0:T(8,128)S(1)}, u32[]{:S(2)}, u32[]{:S(2)}) collective-permute-start(f32[16,512]{1,0:T(8,128)S(1)} %get-tuple-element.95), channel_id=1, source_target_pairs={{0,120},{8,112},{16,104},{24,96},{32,88},{40,80},{48,72},{56,64},{... | collective-permute-start | bytes 98312 | tf_op jit(solution)/shard_map/sum_over_columns/ppermute | solution.py:29
  42.4 5.5 %collective-permute-start.15 = (f32[16,512]{1,0:T(8,128)S(1)}, f32[16,512]{1,0:T(8,128)S(1)}, u32[]{:S(2)}, u32[]{:S(2)}) collective-permute-start(f32[16,512]{1,0:T(8,128)S(1)} %get-tuple-element.96), channel_id=1, source_target_pairs={{0,24},{8,16},{16,8},{24,0},{32,56},{40,48},{48,40},{56,32},{64,88... | collective-permute-start | bytes 98312 | tf_op jit(solution)/shard_map/sum_over_columns/ppermute | solution.py:29
  45.1 5.1 %collective-permute-start.16 = (f32[16,512]{1,0:T(8,128)S(1)}, f32[16,512]{1,0:T(8,128)S(1)}, u32[]{:S(2)}, u32[]{:S(2)}) collective-permute-start(f32[16,512]{1,0:T(8,128)S(1)} %get-tuple-element.97), channel_id=1, source_target_pairs={{0,96},{8,104},{16,112},{24,120},{32,64},{40,72},{48,80},{56,88},{... | collective-permute-start | bytes 98312 | tf_op jit(solution)/shard_map/sum_over_columns/ppermute | solution.py:29
